TPU v7x, 32 devices: a whole 2x2x4 slice. The times are simulated.
32 devices in a mesh: ctx: 8 (over z, x), mp: 4 (over y, core).
Axes of the slice: x: 2, y: 2, z: 4, core: 2. Of those that a mesh axis runs over, the one named last changes fastest.
Arguments:
- query_rows: bfloat16 [1024, 2048], P('ctx', 'mp'), may hold values from -51 to 51
- key_rows: bfloat16 [1024, 2048], P('ctx', 'mp'), may hold values from -4 to 4
- value_rows: bfloat16 [1024, 2048], P('ctx', 'mp'), may hold values from -6 to 6
- inputs: bfloat16 [1024, 2048], P('ctx', 'mp'), may hold values from -3 to 3
- out_weight: bfloat16 [2048, 2048], P('mp'), may hold values from -0.125 to 0.125
- kernel: float32 [31, 2048], P(None, 'mp'), may hold values from -1 to 1
- cotangent: bfloat16 [1024, 2048], P('ctx', 'mp'), may hold values from -6 to 6
Outputs:
- output: bfloat16 [1024, 2048], P('ctx', 'mp')
- grad_input: bfloat16 [1024, 2048], P('ctx', 'mp')
- grad_query: bfloat16 [1024, 2048], P('ctx', 'mp')
- grad_key: bfloat16 [1024, 2048], P('ctx', 'mp')
- grad_value: bfloat16 [1024, 2048], P('ctx', 'mp')
All inputs are finite; a program needn't handle non-finite values.
Results may differ from a plain program's by a relative error of at most 0.024.
Values may be sent and summed in bfloat16 or wider, within the bound.
No kernel may reach another device: no remote copies, remote signals or barrier semaphores. Data moves between devices by JAX's collectives and lax.ppermute only.
A program may use at most 64 MiB of HBM per device.

v0:
```python
import math

import jax
import jax.numpy as jnp
from jax import lax
from jax.sharding import PartitionSpec as P

HDIM = 128
LOOK = 2


def shifted(block, axis, distance):
    devices = range(lax.axis_size(axis))
    route = [(i - distance, i) for i in devices if i - distance in devices]
    return lax.ppermute(block, axis, route)


def with_halo(block, sides, width):
    for axis, dim in sides:
        count = lax.axis_size(axis)
        forward = [(i, i + 1) for i in range(count - 1)]
        backward = [(target, source) for source, target in forward]
        low = lax.ppermute(
            lax.slice_in_dim(block, block.shape[dim] - width, None, axis=dim), axis, forward
        )
        high = lax.ppermute(lax.slice_in_dim(block, 0, width, axis=dim), axis, backward)
        block = jnp.concatenate([low, block, high], axis=dim)
    return block


def kv_move(kv_pair, offset):
    return shifted(kv_pair, "ctx", offset)


def grad_move(part_pair, offset):
    return shifted(part_pair.astype(jnp.bfloat16), "ctx", offset).astype(part_pair.dtype)


def conv_rim(field_rows, rim_width):
    return with_halo(field_rows, (("ctx", 0),), rim_width)


def relay_window(center, move_step):
    lower_list = []
    upper_list = []
    rising = center
    falling = center
    for offset in range(LOOK):
        rising = move_step(rising, 1)
        falling = move_step(falling, -1)
        lower_list.append(rising)
        upper_list.append(falling)
    return lower_list[::-1] + [center] + upper_list


def per_device(query_rows, key_rows, value_rows, inputs, out_weight, kernel, cotangent):
    frames, local_width = query_rows.shape
    local_heads = local_width // HDIM
    score_scale = 1.0 / math.sqrt(HDIM)
    window_len = (2 * LOOK + 1) * frames
    dev_index = lax.axis_index("ctx")
    dev_count = lax.axis_size("ctx")
    owners = dev_index + jnp.arange(window_len, dtype=jnp.int32) // frames - LOOK
    in_range = (owners >= 0) & (owners < dev_count)
    kv_center = jnp.stack([key_rows, value_rows])
    kv_blocks = relay_window(kv_center, kv_move)
    kv_window = jnp.concatenate(kv_blocks, axis=1)
    key_win = kv_window[0].reshape(window_len, local_heads, HDIM)
    value_win = kv_window[1].reshape(window_len, local_heads, HDIM)
    query_heads = query_rows.reshape(frames, local_heads, HDIM)
    scores = (
        jnp.einsum("qhd,khd->hqk", query_heads, key_win, preferred_element_type=jnp.float32)
        * score_scale
    )
    scores = jnp.where(in_range[None, None, :], scores, -jnp.inf)
    row_max = jnp.max(scores, axis=2)
    log_total = row_max + jnp.log(jnp.sum(jnp.exp(scores - row_max[:, :, None]), axis=2))
    attn_probs = jnp.exp(scores - log_total[:, :, None])
    probs_low = attn_probs.astype(jnp.bfloat16)
    attended = jnp.einsum(
        "hqk,khd->qhd", probs_low, value_win, preferred_element_type=jnp.float32
    ).astype(jnp.bfloat16)
    attended_flat = attended.reshape(frames, local_width)
    partial_out = jnp.dot(attended_flat, out_weight, preferred_element_type=jnp.float32)
    mixed = lax.psum_scatter(
        partial_out.astype(jnp.bfloat16), "mp", scatter_dimension=1, tiled=True
    ).astype(jnp.float32)
    hidden = (inputs.astype(jnp.float32) + mixed).astype(jnp.bfloat16)
    taps = kernel.shape[0]
    half_kernel = taps // 2
    hidden_pad = conv_rim(hidden, half_kernel).astype(jnp.float32)
    conv_out = jnp.zeros((frames, local_width), jnp.float32)
    for tap_index in range(taps):
        conv_out = (
            conv_out + kernel[tap_index][None, :] * hidden_pad[tap_index : tap_index + frames]
        )
    conv_gate = jax.nn.sigmoid(conv_out)
    output = (hidden.astype(jnp.float32) + conv_out * conv_gate).astype(jnp.bfloat16)
    grad_conv = (
        cotangent.astype(jnp.float32) * (conv_gate + conv_out * conv_gate * (1.0 - conv_gate))
    ).astype(jnp.bfloat16)
    grad_pad = conv_rim(grad_conv, half_kernel).astype(jnp.float32)
    grad_hidden = cotangent.astype(jnp.float32)
    for tap_index in range(taps):
        first_row = 2 * half_kernel - tap_index
        grad_hidden = (
            grad_hidden + kernel[tap_index][None, :] * grad_pad[first_row : first_row + frames]
        )
    grad_input = grad_hidden.astype(jnp.bfloat16)
    upstream = jnp.einsum(
        "rn,wn->rw",
        lax.all_gather(grad_input, "mp", axis=1, tiled=True),
        out_weight,
        preferred_element_type=jnp.float32,
    ).astype(jnp.bfloat16)
    up_heads = upstream.reshape(frames, local_heads, HDIM)
    row_delta = jnp.sum(up_heads.astype(jnp.float32) * attended.astype(jnp.float32), axis=2).T
    grad_dots = jnp.einsum("qhd,khd->hqk", up_heads, value_win, preferred_element_type=jnp.float32)
    grad_scores = (attn_probs * (grad_dots - row_delta[:, :, None]) * score_scale).astype(
        jnp.bfloat16
    )
    grad_query = jnp.einsum(
        "hqk,khd->qhd", grad_scores, key_win, preferred_element_type=jnp.float32
    )
    grad_query = grad_query.astype(jnp.bfloat16).reshape(frames, local_width)
    key_parts = jnp.einsum(
        "hqk,qhd->khd", grad_scores, query_heads, preferred_element_type=jnp.float32
    )
    value_parts = jnp.einsum(
        "hqk,qhd->khd", probs_low, up_heads, preferred_element_type=jnp.float32
    )
    part_stack = jnp.stack(
        [key_parts.reshape(window_len, local_width), value_parts.reshape(window_len, local_width)]
    )

    def part_block(position):
        return part_stack[:, position * frames : (position + 1) * frames]

    rising = part_block(2 * LOOK)
    offset = 1
    rising = grad_move(rising, 1) + part_block(LOOK + offset)
    rising = grad_move(rising, 1)
    falling = part_block(0)
    offset = 1
    falling = grad_move(falling, -1) + part_block(LOOK - offset)
    falling = grad_move(falling, -1)
    key_sums = part_block(LOOK) + rising + falling
    grad_key = key_sums[0].astype(jnp.bfloat16)
    grad_value = key_sums[1].astype(jnp.bfloat16)
    return (output, grad_input, grad_query, grad_key, grad_value)


def solution(mesh):
    placed = (
        P("ctx", "mp"),
        P("ctx", "mp"),
        P("ctx", "mp"),
        P("ctx", "mp"),
        P("mp", None),
        P(None, "mp"),
        P("ctx", "mp"),
    )
    return jax.shard_map(
        per_device,
        mesh=mesh,
        in_specs=placed,
        out_specs=(P("ctx", "mp"), P("ctx", "mp"), P("ctx", "mp"), P("ctx", "mp"), P("ctx", "mp")),
        check_vma=False,
    )
```

profile of v0, /device:TPU:9, one launch (start us, length us, event | category | flops | bytes accessed | tf_op | source)
XLA Modules:
  0.0 154.5 jit_solution(16516493283210176689)
XLA Ops:
  7.2 0.0 copy-start
  7.2 0.0 reduce-scatter.2.cloned.1.call-start
  7.2 1.2 copy.27
  8.4 1.0 copy.28
  9.5 3.1 %collective-permute-start = (bf16[2,128,512]{1,2,0:T(8,128)(2,1)S(1)}, bf16[2,128,512]{1,2,0:T(8,128)(2,1)S(1)}, u32[]{:S(2)}, u32[]{:S(2)}) collective-permute-start(bf16[2,128,512]{1,2,0:T(8,128)(2,1)S(1)} %pad_maximum_fusion.1), channel_id=1, source_target_pairs={{0,4},{4,8},{8,12},{12,16},{16,20},{20,24},{24,28},{1,5},{5,9},{9,... | collective-permute-start | bytes 786440 | tf_op jit(solution)/shard_map/ppermute | solution.py:15
  12.6 3.1 %collective-permute-start.2 = (bf16[2,128,512]{1,2,0:T(8,128)(2,1)S(1)}, bf16[2,128,512]{1,2,0:T(8,128)(2,1)S(1)}, u32[]{:S(2)}, u32[]{:S(2)}) collective-permute-start(bf16[2,128,512]{1,2,0:T(8,128)(2,1)S(1)} %pad_maximum_fusion.1), channel_id=1, source_target_pairs={{4,0},{8,4},{12,8},{16,12},{20,16},{24,20},{28,24},{5,1},{9,5},{13... | collective-permute-start | bytes 786440 | tf_op jit(solution)/shard_map/ppermute | solution.py:15
  15.7 3.8 %collective-permute-done = bf16[2,128,512]{1,2,0:T(8,128)(2,1)S(1)} collective-permute-done((bf16[2,128,512]{1,2,0:T(8,128)(2,1)S(1)}, bf16[2,128,512]{1,2,0:T(8,128)(2,1)S(1)}, u32[]{:S(2)}, u32[]{:S(2)}) %collective-permute-start) | collective-permute-done | bytes 262176 | tf_op jit(solution)/shard_map/ppermute | solution.py:15
  19.5 7.8 %collective-permute-start.1 = (bf16[2,128,512]{1,2,0:T(8,128)(2,1)S(1)}, bf16[2,128,512]{1,2,0:T(8,128)(2,1)S(1)}, u32[]{:S(2)}, u32[]{:S(2)}) collective-permute-start(bf16[2,128,512]{1,2,0:T(8,128)(2,1)S(1)} %collective-permute-done), channel_id=1, source_target_pairs={{0,4},{4,8},{8,12},{12,16},{16,20},{20,24},{24,28},{1,5},{5,9},{9,... | collective-permute-start | bytes 786440 | tf_op jit(solution)/shard_map/ppermute | solution.py:15
  27.3 1.0 copy.51
  28.3 0.0 copy-start.9
  28.3 1.9 %collective-permute-start.3 = (bf16[2,128,512]{1,2,0:T(8,128)(2,1)S(1)}, bf16[2,128,512]{1,2,0:T(8,128)(2,1)S(1)}, u32[]{:S(2)}, u32[]{:S(2)}) collective-permute-start(bf16[2,128,512]{1,2,0:T(8,128)(2,1)S(1)} %collective-permute-done.2), channel_id=1, source_target_pairs={{4,0},{8,4},{12,8},{16,12},{20,16},{24,20},{28,24},{5,1},{9,5},{13... | collective-permute-start | bytes 786440 | tf_op jit(solution)/shard_map/ppermute | solution.py:15
  30.3 1.4 collective-permute-done.1
  31.7 0.1 constant_dynamic-update-slice_fusion.3
  31.8 0.1 constant_dynamic-update-slice_fusion.2
  31.8 0.1 constant_dynamic-update-slice_fusion.1
  31.9 6.4 %collective-permute-done.3 = bf16[2,128,512]{1,2,0:T(8,128)(2,1)S(1)} collective-permute-done((bf16[2,128,512]{1,2,0:T(8,128)(2,1)S(1)}, bf16[2,128,512]{1,2,0:T(8,128)(2,1)S(1)}, u32[]{:S(2)}, u32[]{:S(2)}) %collective-permute-start.3) | collective-permute-done | bytes 262176 | tf_op jit(solution)/shard_map/ppermute | solution.py:15
  38.3 0.1 constant_dynamic-update-slice_fusion
  38.4 0.1 fusion.93
  38.5 0.5 fusion.98
  39.0 0.2 exponential_reduce_fusion
  39.2 0.1 copy-done.2
  39.4 0.2 copy-done.4
  39.6 0.4 convolution_convert_fusion.3
  39.9 0.0 copy-start.11
  39.9 0.6 copy-done.11
  40.6 1.3 convolution_convert_fusion
  41.9 0.0 reduce-scatter.2.cloned.1.call-update
  41.9 1.8 %fusion.96 = (f32[1,512]{1,0:T(1,128)S(1)}, f32[1,512]{1,0:T(1,128)S(1)}, f32[1,512]{1,0:T(1,128)S(1)}, f32[1,512]{1,0:T(1,128)}, f32[1,512]{1,0:T(1,128)}, /*in...) fusion(f32[31,512]{1,0:T(8,128)} %param.12), kind=kLoop, calls=%fused_computation.191 | loop fusion | bytes 77824 | tf_op jit(solution)/shard_map/slice | solution.py:95
  43.7 21.8 %reduce-scatter.2.cloned.1.call-done = bf16[128,512]{1,0:T(8,128)(2,1)} async-done(((bf16[128,2048]{1,0:T(8,128)(2,1)}), bf16[128,512]{1,0:T(8,128)(2,1)}) %reduce-scatter.2.cloned.1.call-update) | async-done | bytes 131088 | tf_op jit(solution)/shard_map/reduce_scatter | solution.py:85
  65.5 1.0 add_convert_fusion.1
  66.5 0.0 copy-start.7
  66.6 3.1 %collective-permute-start.4 = (bf16[15,512]{1,0:T(8,128)(2,1)S(1)}, bf16[15,512]{1,0:T(8,128)(2,1)S(1)}, u32[]{:S(2)}, u32[]{:S(2)}) collective-permute-start(bf16[15,512]{1,0:T(8,128)(2,1)S(1)} %get-tuple-element.27), channel_id=1, source_target_pairs={{0,4},{4,8},{8,12},{12,16},{16,20},{20,24},{24,28},{1,5},{5,9},{9,... | collective-permute-start | bytes 46088 | tf_op jit(solution)/shard_map/ppermute | solution.py:23
  69.6 3.1 %collective-permute-start.5 = (bf16[15,512]{1,0:T(8,128)(2,1)S(1)}, bf16[15,512]{1,0:T(8,128)(2,1)S(1)}, u32[]{:S(2)}, u32[]{:S(2)}) collective-permute-start(bf16[15,512]{1,0:T(8,128)(2,1)S(1)} %get-tuple-element.28), channel_id=1, source_target_pairs={{4,0},{8,4},{12,8},{16,12},{20,16},{24,20},{28,24},{5,1},{9,5},{13... | collective-permute-start | bytes 46088 | tf_op jit(solution)/shard_map/ppermute | solution.py:26
  72.7 1.0 fusion.97
  73.8 0.4 collective-permute-done.5
  74.3 2.3 %fusion.17 = (bf16[128,512]{1,0:T(8,128)(2,1)S(1)}, f32[128,512]{1,0:T(8,128)}) fusion(bf16[128,512]{1,0:T(8,128)(2,1)S(1)} %copy-done.14, f32[158,512]{1,0:T(8,128)S(1)} %maximum_convert_fusion, f32[512]{0:T(512)S(1)} %bitcast.146, f32[512]{0:T(512)S(1)} %bitcast.148, f32[512]{0:T(512)S(1)} %bitcast.90, f32[512]{0:T(512)S(1)} %bitcast.92, f32[512]{0:T(512)} %bitcast.94, ...), kind=kLoop, calls=%fused_computation.34 | loop fusion | flops 4653056 | bytes 8714240 | tf_op jit(solution)/shard_map/convert_element_type | solution.py:101
  76.6 4.0 %collective-permute-start.6 = (bf16[15,512]{1,0:T(8,128)(2,1)S(1)}, bf16[15,512]{1,0:T(8,128)(2,1)S(1)}, u32[]{:S(2)}, u32[]{:S(2)}) collective-permute-start(bf16[15,512]{1,0:T(8,128)(2,1)S(1)} %get-tuple-element.25), channel_id=1, source_target_pairs={{0,4},{4,8},{8,12},{12,16},{16,20},{20,24},{24,28},{1,5},{5,9},{9,... | collective-permute-start | bytes 46088 | tf_op jit(solution)/shard_map/ppermute | solution.py:23
  80.6 2.2 %collective-permute-start.7 = (bf16[15,512]{1,0:T(8,128)(2,1)S(1)}, bf16[15,512]{1,0:T(8,128)(2,1)S(1)}, u32[]{:S(2)}, u32[]{:S(2)}) collective-permute-start(bf16[15,512]{1,0:T(8,128)(2,1)S(1)} %get-tuple-element.26), channel_id=1, source_target_pairs={{4,0},{8,4},{12,8},{16,12},{20,16},{24,20},{28,24},{5,1},{9,5},{13... | collective-permute-start | bytes 46088 | tf_op jit(solution)/shard_map/ppermute | solution.py:26
  82.8 2.3 %collective-permute-done.7 = bf16[15,512]{1,0:T(8,128)(2,1)S(1)} collective-permute-done((bf16[15,512]{1,0:T(8,128)(2,1)S(1)}, bf16[15,512]{1,0:T(8,128)(2,1)S(1)}, u32[]{:S(2)}, u32[]{:S(2)}) %collective-permute-start.7) | collective-permute-done | bytes 15392 | tf_op jit(solution)/shard_map/ppermute | solution.py:26
  85.3 0.8 fusion.44
  86.2 9.9 %all_gather.3 = bf16[128,2048]{1,0:T(8,128)(2,1)S(1)} all-gather(bf16[128,512]{1,0:T(8,128)(2,1)S(1)} %fusion.44), channel_id=1, replica_groups=mesh['ctx'=8,'mp'=4] {'mp'}, dimensions={1}, use_global_device_ids=true | all-gather | bytes 655360 | tf_op jit(solution)/shard_map/all_gather | solution.py:112
  96.1 1.5 convolution_convert_fusion.1
  97.6 1.0 copy.32
  98.6 1.0 multiply_reduce_fusion
  99.6 1.5 fusion.80
  101.0 1.3 fusion.5
  102.4 1.7 %copy.41 = f32[1,640,512]{2,1,0:T(8,128)S(1)} copy(f32[1,640,512]{1,2,0:T(8,128)} %bitcast.76) | data formatting | bytes 2621440 | tf_op jit(solution)/shard_map/stack;reshape | solution.py:132
  104.1 2.5 %fusion.99 = f32[4,640,128]{1,2,0:T(8,128)} fusion(bf16[4,128,640]{1,2,0:T(8,128)(2,1)} %fusion.5, bf16[128,4,128]{0,2,1:T(8,128)(2,1)S(1)} %bitcast.81), kind=kOutput, calls=%fused_computation.194 | convolution fusion | flops 83886080 | bytes 2097152 | tf_op jit(solution)/shard_map/hqk,qhd->khd/dot_general | solution.py:126
  106.7 2.8 %copy.40 = f32[1,640,512]{2,1,0:T(8,128)} copy(f32[1,640,512]{1,2,0:T(8,128)} %bitcast.77) | data formatting | bytes 2621440 | tf_op jit(solution)/shard_map/stack;reshape | solution.py:132
  109.5 1.6 %fusion = bf16[2,640,512]{2,1,0:T(8,128)(2,1)S(1)} fusion(f32[1,640,512]{2,1,0:T(8,128)S(1)} %copy.41, f32[1,640,512]{2,1,0:T(8,128)} %copy.40), kind=kLoop, calls=%fused_computation.7 | loop fusion | flops 655360 | bytes 3932160 | tf_op jit(solution)/shard_map/convert.3
  111.2 3.1 %collective-permute-start.8 = (bf16[2,128,512]{2,1,0:T(8,128)(2,1)S(1)}, bf16[2,128,512]{2,1,0:T(8,128)(2,1)S(1)}, u32[]{:S(2)}, u32[]{:S(2)}) collective-permute-start(bf16[2,128,512]{2,1,0:T(8,128)(2,1)S(1)} %get-tuple-element.19), channel_id=1, source_target_pairs={{0,4},{4,8},{8,12},{12,16},{16,20},{20,24},{24,28},{1,5},{5,9},{9,... | collective-permute-start | bytes 786440 | tf_op jit(solution)/shard_map/ppermute | solution.py:15
  114.3 3.2 %collective-permute-start.10 = (bf16[2,128,512]{2,1,0:T(8,128)(2,1)S(1)}, bf16[2,128,512]{2,1,0:T(8,128)(2,1)S(1)}, u32[]{:S(2)}, u32[]{:S(2)}) collective-permute-start(bf16[2,128,512]{2,1,0:T(8,128)(2,1)S(1)} %get-tuple-element.20), channel_id=1, source_target_pairs={{4,0},{8,4},{12,8},{16,12},{20,16},{24,20},{28,24},{5,1},{9,5},{13... | collective-permute-start | bytes 786440 | tf_op jit(solution)/shard_map/ppermute | solution.py:15
  117.5 7.7 %collective-permute-done.8 = bf16[2,128,512]{2,1,0:T(8,128)(2,1)S(1)} collective-permute-done((bf16[2,128,512]{2,1,0:T(8,128)(2,1)S(1)}, bf16[2,128,512]{2,1,0:T(8,128)(2,1)S(1)}, u32[]{:S(2)}, u32[]{:S(2)}) %collective-permute-start.8) | collective-permute-done | bytes 262176 | tf_op jit(solution)/shard_map/ppermute | solution.py:15
  125.3 2.5 %collective-permute-done.10 = bf16[2,128,512]{2,1,0:T(8,128)(2,1)S(1)} collective-permute-done((bf16[2,128,512]{2,1,0:T(8,128)(2,1)S(1)}, bf16[2,128,512]{2,1,0:T(8,128)(2,1)S(1)}, u32[]{:S(2)}, u32[]{:S(2)}) %collective-permute-start.10) | collective-permute-done | bytes 262176 | tf_op jit(solution)/shard_map/ppermute | solution.py:15
  127.8 1.0 fusion.13
  128.8 1.9 %collective-permute-start.9 = (bf16[2,128,512]{2,1,0:T(8,128)(2,1)}, bf16[2,128,512]{2,1,0:T(8,128)(2,1)}, u32[]{:S(2)}, u32[]{:S(2)}) collective-permute-start(bf16[2,128,512]{2,1,0:T(8,128)(2,1)} %get-tuple-element.17), channel_id=1, source_target_pairs={{0,4},{4,8},{8,12},{12,16},{16,20},{20,24},{24,28},{1,5},{5,9},{9,... | collective-permute-start | bytes 786440 | tf_op jit(solution)/shard_map/ppermute | solution.py:15
  130.7 4.3 %collective-permute-start.11 = (bf16[2,128,512]{2,1,0:T(8,128)(2,1)}, bf16[2,128,512]{2,1,0:T(8,128)(2,1)}, u32[]{:S(2)}, u32[]{:S(2)}) collective-permute-start(bf16[2,128,512]{2,1,0:T(8,128)(2,1)} %get-tuple-element.18), channel_id=1, source_target_pairs={{4,0},{8,4},{12,8},{16,12},{20,16},{24,20},{28,24},{5,1},{9,5},{13... | collective-permute-start | bytes 786440 | tf_op jit(solution)/shard_map/ppermute | solution.py:15
  135.0 0.7 add_convert_fusion
  135.7 0.3 convolution_convert_fusion.2
  136.1 0.8 copy.42
  136.8 2.5 %collective-permute-done.9 = bf16[2,128,512]{2,1,0:T(8,128)(2,1)} collective-permute-done((bf16[2,128,512]{2,1,0:T(8,128)(2,1)}, bf16[2,128,512]{2,1,0:T(8,128)(2,1)}, u32[]{:S(2)}, u32[]{:S(2)}) %collective-permute-start.9) | collective-permute-done | bytes 262176 | tf_op jit(solution)/shard_map/ppermute | solution.py:15
  139.3 6.4 %collective-permute-done.11 = bf16[2,128,512]{2,1,0:T(8,128)(2,1)} collective-permute-done((bf16[2,128,512]{2,1,0:T(8,128)(2,1)}, bf16[2,128,512]{2,1,0:T(8,128)(2,1)}, u32[]{:S(2)}, u32[]{:S(2)}) %collective-permute-start.11) | collective-permute-done | bytes 262176 | tf_op jit(solution)/shard_map/ppermute | solution.py:15
  145.7 1.2 fusion.10
  146.9 0.7 slice_bitcast_fusion
  (67 shorter events, 0.4 us)
Async XLA Ops:
  7.2 33.4 %copy-start = (bf16[512,2048]{1,0:T(8,128)(2,1)S(1)}, bf16[512,2048]{1,0:T(8,128)(2,1)}, u32[]{:S(2)}) copy-start(bf16[512,2048]{1,0:T(8,128)(2,1)} %param.11) | copy-start | bytes 6291460
  7.2 58.3 %reduce-scatter.2.cloned.1.call-start = ((), (), s32[]{:S(2)}) async-start(), calls=%async_computation.1 | async-start | bytes 655360 | tf_op jit(solution)/shard_map/reduce_scatter | solution.py:85
  9.5 10.0 %collective-permute-start = (bf16[2,128,512]{1,2,0:T(8,128)(2,1)S(1)}, bf16[2,128,512]{1,2,0:T(8,128)(2,1)S(1)}, u32[]{:S(2)}, u32[]{:S(2)}) collective-permute-start(bf16[2,128,512]{1,2,0:T(8,128)(2,1)S(1)} %pad_maximum_fusion.1), channel_id=1, source_target_pairs={{0,4},{4,8},{8,12},{12,16},{16,20},{20,24},{24,28},{1,5},{5,9},{9,... | collective-permute-start | bytes 786440 | tf_op jit(solution)/shard_map/ppermute | solution.py:15
  12.6 15.7 %collective-permute-start.2 = (bf16[2,128,512]{1,2,0:T(8,128)(2,1)S(1)}, bf16[2,128,512]{1,2,0:T(8,128)(2,1)S(1)}, u32[]{:S(2)}, u32[]{:S(2)}) collective-permute-start(bf16[2,128,512]{1,2,0:T(8,128)(2,1)S(1)} %pad_maximum_fusion.1), channel_id=1, source_target_pairs={{4,0},{8,4},{12,8},{16,12},{20,16},{24,20},{28,24},{5,1},{9,5},{13... | collective-permute-start | bytes 786440 | tf_op jit(solution)/shard_map/ppermute | solution.py:15
  19.5 12.2 %collective-permute-start.1 = (bf16[2,128,512]{1,2,0:T(8,128)(2,1)S(1)}, bf16[2,128,512]{1,2,0:T(8,128)(2,1)S(1)}, u32[]{:S(2)}, u32[]{:S(2)}) collective-permute-start(bf16[2,128,512]{1,2,0:T(8,128)(2,1)S(1)} %collective-permute-done), channel_id=1, source_target_pairs={{0,4},{4,8},{8,12},{12,16},{16,20},{20,24},{24,28},{1,5},{5,9},{9,... | collective-permute-start | bytes 786440 | tf_op jit(solution)/shard_map/ppermute | solution.py:15
  28.3 10.2 %copy-start.9 = (bf16[128,512]{0,1:T(8,128)(2,1)}, bf16[128,512]{0,1:T(8,128)(2,1)S(1)}, u32[]{:S(2)}) copy-start(bf16[128,512]{0,1:T(8,128)(2,1)S(1)} %copy.51) | copy-start | bytes 393220
  28.3 10.0 %collective-permute-start.3 = (bf16[2,128,512]{1,2,0:T(8,128)(2,1)S(1)}, bf16[2,128,512]{1,2,0:T(8,128)(2,1)S(1)}, u32[]{:S(2)}, u32[]{:S(2)}) collective-permute-start(bf16[2,128,512]{1,2,0:T(8,128)(2,1)S(1)} %collective-permute-done.2), channel_id=1, source_target_pairs={{4,0},{8,4},{12,8},{16,12},{20,16},{24,20},{28,24},{5,1},{9,5},{13... | collective-permute-start | bytes 786440 | tf_op jit(solution)/shard_map/ppermute | solution.py:15
  38.5 0.8 copy-start.2
  38.5 1.0 copy-start.4
  39.9 0.7 copy-start.11
  41.9 32.3 %copy-start.14 = (bf16[128,512]{1,0:T(8,128)(2,1)S(1)}, bf16[128,512]{1,0:T(8,128)(2,1)}, u32[]{:S(2)}) copy-start(bf16[128,512]{1,0:T(8,128)(2,1)} %param.13) | copy-start | bytes 393220
  66.5 7.6 %copy-start.7 = (bf16[128,512]{1,0:T(8,128)(2,1)}, bf16[128,512]{1,0:T(8,128)(2,1)S(1)}, u32[]{:S(2)}) copy-start(bf16[128,512]{1,0:T(8,128)(2,1)S(1)} %add_convert_fusion.1) | copy-start | bytes 393220
  66.6 7.2 %collective-permute-start.4 = (bf16[15,512]{1,0:T(8,128)(2,1)S(1)}, bf16[15,512]{1,0:T(8,128)(2,1)S(1)}, u32[]{:S(2)}, u32[]{:S(2)}) collective-permute-start(bf16[15,512]{1,0:T(8,128)(2,1)S(1)} %get-tuple-element.27), channel_id=1, source_target_pairs={{0,4},{4,8},{8,12},{12,16},{16,20},{20,24},{24,28},{1,5},{5,9},{9,... | collective-permute-start | bytes 46088 | tf_op jit(solution)/shard_map/ppermute | solution.py:23
  69.6 4.5 %collective-permute-start.5 = (bf16[15,512]{1,0:T(8,128)(2,1)S(1)}, bf16[15,512]{1,0:T(8,128)(2,1)S(1)}, u32[]{:S(2)}, u32[]{:S(2)}) collective-permute-start(bf16[15,512]{1,0:T(8,128)(2,1)S(1)} %get-tuple-element.28), channel_id=1, source_target_pairs={{4,0},{8,4},{12,8},{16,12},{20,16},{24,20},{28,24},{5,1},{9,5},{13... | collective-permute-start | bytes 46088 | tf_op jit(solution)/shard_map/ppermute | solution.py:26
  74.2 11.0 %copy-start.15 = (f32[1,512]{1,0:T(1,128)S(1)}, f32[1,512]{1,0:T(1,128)}, u32[]{:S(2)}) copy-start(f32[1,512]{1,0:T(1,128)} %get-tuple-element.32) | copy-start | bytes 6148
  74.2 11.0 %copy-start.16 = (f32[1,512]{1,0:T(1,128)S(1)}, f32[1,512]{1,0:T(1,128)}, u32[]{:S(2)}) copy-start(f32[1,512]{1,0:T(1,128)} %get-tuple-element.33) | copy-start | bytes 6148
  74.2 11.0 %copy-start.17 = (f32[1,512]{1,0:T(1,128)S(1)}, f32[1,512]{1,0:T(1,128)}, u32[]{:S(2)}) copy-start(f32[1,512]{1,0:T(1,128)} %get-tuple-element.34) | copy-start | bytes 6148
  74.2 11.0 %copy-start.18 = (f32[1,512]{1,0:T(1,128)S(1)}, f32[1,512]{1,0:T(1,128)}, u32[]{:S(2)}) copy-start(f32[1,512]{1,0:T(1,128)} %get-tuple-element.35) | copy-start | bytes 6148
  74.2 11.0 %copy-start.19 = (f32[1,512]{1,0:T(1,128)S(1)}, f32[1,512]{1,0:T(1,128)}, u32[]{:S(2)}) copy-start(f32[1,512]{1,0:T(1,128)} %get-tuple-element.36) | copy-start | bytes 6148
  74.2 11.0 %copy-start.20 = (f32[1,512]{1,0:T(1,128)S(1)}, f32[1,512]{1,0:T(1,128)}, u32[]{:S(2)}) copy-start(f32[1,512]{1,0:T(1,128)} %get-tuple-element.37) | copy-start | bytes 6148
  74.2 11.0 %copy-start.21 = (f32[1,512]{1,0:T(1,128)S(1)}, f32[1,512]{1,0:T(1,128)}, u32[]{:S(2)}) copy-start(f32[1,512]{1,0:T(1,128)} %get-tuple-element.38) | copy-start | bytes 6148
  74.3 11.0 %copy-start.22 = (f32[1,512]{1,0:T(1,128)S(1)}, f32[1,512]{1,0:T(1,128)}, u32[]{:S(2)}) copy-start(f32[1,512]{1,0:T(1,128)} %get-tuple-element.39) | copy-start | bytes 6148
  74.3 11.0 %copy-start.23 = (f32[1,512]{1,0:T(1,128)S(1)}, f32[1,512]{1,0:T(1,128)}, u32[]{:S(2)}) copy-start(f32[1,512]{1,0:T(1,128)} %get-tuple-element.40) | copy-start | bytes 6148
  74.3 11.0 %copy-start.24 = (f32[1,512]{1,0:T(1,128)S(1)}, f32[1,512]{1,0:T(1,128)}, u32[]{:S(2)}) copy-start(f32[1,512]{1,0:T(1,128)} %get-tuple-element.41) | copy-start | bytes 6148
  74.3 11.0 %copy-start.25 = (f32[1,512]{1,0:T(1,128)S(1)}, f32[1,512]{1,0:T(1,128)}, u32[]{:S(2)}) copy-start(f32[1,512]{1,0:T(1,128)} %get-tuple-element.42) | copy-start | bytes 6148
  74.3 11.0 %copy-start.26 = (f32[1,512]{1,0:T(1,128)S(1)}, f32[1,512]{1,0:T(1,128)}, u32[]{:S(2)}) copy-start(f32[1,512]{1,0:T(1,128)} %get-tuple-element.43) | copy-start | bytes 6148
  74.3 11.0 %copy-start.27 = (f32[1,512]{1,0:T(1,128)S(1)}, f32[1,512]{1,0:T(1,128)}, u32[]{:S(2)}) copy-start(f32[1,512]{1,0:T(1,128)} %get-tuple-element.44) | copy-start | bytes 6148
  74.3 11.0 %copy-start.28 = (f32[1,512]{1,0:T(1,128)S(1)}, f32[1,512]{1,0:T(1,128)}, u32[]{:S(2)}) copy-start(f32[1,512]{1,0:T(1,128)} %get-tuple-element.45) | copy-start | bytes 6148
  74.3 11.0 %copy-start.29 = (f32[1,512]{1,0:T(1,128)S(1)}, f32[1,512]{1,0:T(1,128)}, u32[]{:S(2)}) copy-start(f32[1,512]{1,0:T(1,128)} %get-tuple-element.46) | copy-start | bytes 6148
  74.3 11.0 %copy-start.30 = (f32[1,512]{1,0:T(1,128)S(1)}, f32[1,512]{1,0:T(1,128)}, u32[]{:S(2)}) copy-start(f32[1,512]{1,0:T(1,128)} %get-tuple-element.47) | copy-start | bytes 6148
  76.6 6.2 %collective-permute-start.6 = (bf16[15,512]{1,0:T(8,128)(2,1)S(1)}, bf16[15,512]{1,0:T(8,128)(2,1)S(1)}, u32[]{:S(2)}, u32[]{:S(2)}) collective-permute-start(bf16[15,512]{1,0:T(8,128)(2,1)S(1)} %get-tuple-element.25), channel_id=1, source_target_pairs={{0,4},{4,8},{8,12},{12,16},{16,20},{20,24},{24,28},{1,5},{5,9},{9,... | collective-permute-start | bytes 46088 | tf_op jit(solution)/shard_map/ppermute | solution.py:23
  80.6 4.5 %collective-permute-start.7 = (bf16[15,512]{1,0:T(8,128)(2,1)S(1)}, bf16[15,512]{1,0:T(8,128)(2,1)S(1)}, u32[]{:S(2)}, u32[]{:S(2)}) collective-permute-start(bf16[15,512]{1,0:T(8,128)(2,1)S(1)} %get-tuple-element.26), channel_id=1, source_target_pairs={{4,0},{8,4},{12,8},{16,12},{20,16},{24,20},{28,24},{5,1},{9,5},{13... | collective-permute-start | bytes 46088 | tf_op jit(solution)/shard_map/ppermute | solution.py:26
  86.2 9.9 %copy-start.13 = (bf16[128,512]{1,0:T(8,128)(2,1)}, bf16[128,512]{1,0:T(8,128)(2,1)S(1)}, u32[]{:S(2)}) copy-start(bf16[128,512]{1,0:T(8,128)(2,1)S(1)} %fusion.44) | copy-start | bytes 393220
  99.5 1.5 copy-start.5
  102.4 1.8 %copy-start.10 = (bf16[128,512]{0,1:T(8,128)(2,1)S(1)}, bf16[128,512]{0,1:T(8,128)(2,1)}, u32[]{:S(2)}) copy-start(bf16[128,512]{0,1:T(8,128)(2,1)} %copy-done.9) | copy-start | bytes 393220
  109.5 18.3 %copy-start.1 = (f32[1,640,512]{2,1,0:T(8,128)S(1)}, f32[1,640,512]{2,1,0:T(8,128)}, u32[]{:S(2)}) copy-start(f32[1,640,512]{2,1,0:T(8,128)} %copy.40) | copy-start | bytes 3932164
  111.2 14.1 %collective-permute-start.8 = (bf16[2,128,512]{2,1,0:T(8,128)(2,1)S(1)}, bf16[2,128,512]{2,1,0:T(8,128)(2,1)S(1)}, u32[]{:S(2)}, u32[]{:S(2)}) collective-permute-start(bf16[2,128,512]{2,1,0:T(8,128)(2,1)S(1)} %get-tuple-element.19), channel_id=1, source_target_pairs={{0,4},{4,8},{8,12},{12,16},{16,20},{20,24},{24,28},{1,5},{5,9},{9,... | collective-permute-start | bytes 786440 | tf_op jit(solution)/shard_map/ppermute | solution.py:15
  114.3 20.7 %copy-start.8 = (bf16[128,512]{1,0:T(8,128)(2,1)S(1)}, bf16[128,512]{1,0:T(8,128)(2,1)}, u32[]{:S(2)}) copy-start(bf16[128,512]{1,0:T(8,128)(2,1)} %copy-done.7) | copy-start | bytes 393220
  114.3 20.7 %copy-start.12 = (f32[128,512]{1,0:T(8,128)S(1)}, f32[128,512]{1,0:T(8,128)}, u32[]{:S(2)}) copy-start(f32[128,512]{1,0:T(8,128)} %get-tuple-element.16) | copy-start | bytes 786436
  114.3 21.4 %copy-start.3 = (bf16[1,640,512]{1,2,0:T(8,128)(2,1)S(1)}, bf16[1,640,512]{1,2,0:T(8,128)(2,1)}, u32[]{:S(2)}) copy-start(bf16[1,640,512]{1,2,0:T(8,128)(2,1)} %copy-done.2) | copy-start | bytes 1966084
  114.3 21.4 %copy-start.6 = (bf16[4,128,640]{1,2,0:T(8,128)(2,1)S(1)}, bf16[4,128,640]{1,2,0:T(8,128)(2,1)}, u32[]{:S(2)}) copy-start(bf16[4,128,640]{1,2,0:T(8,128)(2,1)} %fusion.5) | copy-start | bytes 1966084
  114.3 13.5 %collective-permute-start.10 = (bf16[2,128,512]{2,1,0:T(8,128)(2,1)S(1)}, bf16[2,128,512]{2,1,0:T(8,128)(2,1)S(1)}, u32[]{:S(2)}, u32[]{:S(2)}) collective-permute-start(bf16[2,128,512]{2,1,0:T(8,128)(2,1)S(1)} %get-tuple-element.20), channel_id=1, source_target_pairs={{4,0},{8,4},{12,8},{16,12},{20,16},{24,20},{28,24},{5,1},{9,5},{13... | collective-permute-start | bytes 786440 | tf_op jit(solution)/shard_map/ppermute | solution.py:15
  128.8 10.5 %collective-permute-start.9 = (bf16[2,128,512]{2,1,0:T(8,128)(2,1)}, bf16[2,128,512]{2,1,0:T(8,128)(2,1)}, u32[]{:S(2)}, u32[]{:S(2)}) collective-permute-start(bf16[2,128,512]{2,1,0:T(8,128)(2,1)} %get-tuple-element.17), channel_id=1, source_target_pairs={{0,4},{4,8},{8,12},{12,16},{16,20},{20,24},{24,28},{1,5},{5,9},{9,... | collective-permute-start | bytes 786440 | tf_op jit(solution)/shard_map/ppermute | solution.py:15
  130.7 15.0 %collective-permute-start.11 = (bf16[2,128,512]{2,1,0:T(8,128)(2,1)}, bf16[2,128,512]{2,1,0:T(8,128)(2,1)}, u32[]{:S(2)}, u32[]{:S(2)}) collective-permute-start(bf16[2,128,512]{2,1,0:T(8,128)(2,1)} %get-tuple-element.18), channel_id=1, source_target_pairs={{4,0},{8,4},{12,8},{16,12},{20,16},{24,20},{28,24},{5,1},{9,5},{13... | collective-permute-start | bytes 786440 | tf_op jit(solution)/shard_map/ppermute | solution.py:15
Sparse Core Ops, SparseCore 0:
  42.0 23.4 reduce-scatter.1
where the time goes:
time: 155 us
  waiting for transfers between devices  55.3 us (36%)
  starting transfers between devices  40.8 us (26%)
  between operations  14.7 us (9%)
  local copies, waits for them, and re-layouts  14.6 us (9%)
  other arithmetic  10 us (6%)
  blocking collectives  9.89 us (6%)
  matrix products  9.27 us (6%)
    ppermute x8, waiting for transfers between devices, shifted(): return lax.ppermute(block, axis, route)  30.8 us
    ppermute x8, starting transfers between devices, shifted(): return lax.ppermute(block, axis, route)  28.4 us
    reduce_scatter x1, waiting for transfers between devices, per_device(): lax.psum_scatter(partial_out.astype(jnp.bfloat16), 'mp', scatter_dimensio...  21.8 us
    all_gather x1, blocking collectives, per_device(): lax.all_gather(grad_input, 'mp', axis=1, tiled=True)  9.89 us
    ppermute x2, starting transfers between devices, with_halo(): lax.ppermute(lax.slice_in_dim(block, block.shape[dim] - width, None, axis...  7.08 us
    ppermute x2, starting transfers between devices, with_halo(): lax.ppermute(lax.slice_in_dim(block, 0, width, axis=dim), axis, backward)  5.28 us
    another operation x2, local copies, waits for them, and re-layouts, per_device(): jnp.stack([key_parts.reshape(window_len, local_width), value_parts.reshap...  4.56 us
    unnamed x68, local copies, waits for them, and re-layouts  4.26 us
  transfers between devices with their start and end apart: 13, of which 10 were waited for; matrix products, arithmetic and copies ran while one was open for 4% of the time, Pallas kernels for 0%

commit v1 on v0

v1 whole, which is shorter than its diff:
```python
import functools
import math

import jax
import jax.numpy as jnp
from jax import lax
from jax.experimental import pallas as pl
from jax.experimental.pallas import tpu as pltpu
from jax.sharding import PartitionSpec as P

HDIM = 128
F32 = jnp.float32
BF16 = jnp.bfloat16
HALO = 16
NT = (((1,), (1,)), ((), ()))
NN = (((1,), (0,)), ((), ()))


def dot_nt(a, b):
    return lax.dot_general(a, b, NT, preferred_element_type=F32)


def dot_nn(a, b):
    return lax.dot_general(a, b, NN, preferred_element_type=F32)


def pair_swap(block, axis, bit):
    return lax.ppermute(block, axis, [(i, i ^ bit) for i in range(lax.axis_size(axis))])


def ring_routes(count):
    rise = [(i, i + 2) for i in range(0, count - 2, 2)] + [(count - 2, count - 1)]
    fall = [(i, i - 2) for i in range(count - 1, 2, -2)] + [(1, 0)]
    route = rise + fall
    return route, [(b, a) for a, b in route]


def ring(block, way):
    return lax.ppermute(block, "ctx", ring_routes(lax.axis_size("ctx"))[way])


def kernel_call(body, outs, args, flops, name):
    smem = pl.BlockSpec(memory_space=pltpu.SMEM)
    vmem = pl.BlockSpec(memory_space=pltpu.VMEM)
    nbytes = sum(math.prod(a.shape) * a.dtype.itemsize for a in list(args) + list(outs))
    return pl.pallas_call(
        body,
        out_shape=outs,
        in_specs=[smem] + [vmem] * (len(args) - 1),
        out_specs=tuple(vmem for _ in outs),
        compiler_params=pltpu.CompilerParams(vmem_limit_bytes=24 * 1024 * 1024),
        cost_estimate=pl.CostEstimate(flops=flops, bytes_accessed=nbytes, transcendentals=0),
        name=name,
    )(*args)


def shaped(shape, dtype):
    return jax.ShapeDtypeStruct(shape, dtype)


def off_bias(flag):
    return jnp.where(flag > 0, jnp.float32(0.0), jnp.float32(-jnp.inf))


def head_cols(h):
    return slice(h * HDIM, (h + 1) * HDIM)


def window_scores(scale, flags, q, kvs, cols):
    frames = q.shape[0]
    biases = (None, None, off_bias(flags[1]), off_bias(flags[2]), off_bias(flags[1]))
    keys = jnp.concatenate([kv[0:frames, cols] for kv in kvs], axis=0)
    scores = dot_nt(q[:, cols], keys) * scale
    parts = []
    for b, bias in enumerate(biases):
        part = scores[:, b * frames : (b + 1) * frames]
        parts.append(part if bias is None else part + bias)
    return jnp.concatenate(parts, axis=1), keys


def forward_body(scale, flags, q, own, near, first, second, relay, weight, att, lse, send, keep):
    frames, width = q.shape
    kvs = (own, near, first, second, relay)
    lane = lax.broadcasted_iota(jnp.int32, (frames, HDIM), 1)
    lse_tile = jnp.zeros((frames, HDIM), F32)
    for h in range(width // HDIM):
        cols = head_cols(h)
        scores, _ = window_scores(scale, flags, q, kvs, cols)
        row_max = jnp.max(scores, axis=1, keepdims=True)
        log_total = row_max + jnp.log(jnp.sum(jnp.exp(scores - row_max), axis=1, keepdims=True))
        probs_low = jnp.exp(scores - log_total).astype(BF16)
        values = jnp.concatenate([kv[frames : 2 * frames, cols] for kv in kvs], axis=0)
        att[:, cols] = dot_nn(probs_low, values).astype(BF16)
        lse_tile = jnp.where(lane == h, log_total, lse_tile)
    lse[...] = lse_tile
    place = flags[3]
    attended = att[...]

    def share(target):
        block = weight[:, pl.ds(pl.multiple_of(target * width, 128), width)]
        return dot_nn(attended, block).astype(BF16)

    send[:, 0:width] = share(place ^ 3)
    send[:, width : 2 * width] = share(place ^ 1)
    keep[:, 0:width] = share(place ^ 2)
    keep[:, width : 2 * width] = share(place)


def hidden_body(flags, inputs, keep, core, across, cot, hidden, rims):
    frames, width = inputs.shape
    mine = slice(width, 2 * width)
    total = inputs[...].astype(F32) + keep[:, mine].astype(F32) + core[:, mine].astype(F32)
    hidden[...] = (total + across[...].astype(F32)).astype(BF16)
    wide = 2 * HALO
    rims[0:wide, :] = hidden[0:wide, :]
    rims[wide : 2 * wide, :] = hidden[frames - wide : frames, :]
    rims[2 * wide : 2 * wide + HALO, :] = cot[0:HALO, :]
    rims[2 * wide + HALO : 3 * wide, :] = cot[frames - HALO : frames, :]


def shifted_sum(load, taps_of, rows, lanes):
    total = None
    for b in range(8):
        part = None
        reach = rows if b == 0 else rows + 8
        for a in range(4):
            tap = taps_of(8 * a + b)
            if tap is None:
                continue
            term = tap * load(8 * a, reach)
            part = term if part is None else part + term
        if b:
            part = pltpu.roll(part, reach - b, 0)[0:rows]
        total = part if total is None else total + part
    return total


def conv_body(flags, hidden, rim_near, rim_first, cot, taps, output, grad_input, padded, grads):
    frames, width = hidden.shape
    wide = 2 * HALO
    count = taps.shape[0]
    even = flags[0] > 0
    have = jnp.where(flags[1] > 0, jnp.float32(1.0), jnp.float32(0.0))
    low_ok = jnp.where(even, have, jnp.float32(1.0))
    high_ok = jnp.where(even, jnp.float32(1.0), have)

    def low_of(rows):
        return jnp.where(even, rim_first[rows, :].astype(F32), rim_near[rows, :].astype(F32)) * low_ok

    def high_of(rows):
        return jnp.where(even, rim_near[rows, :].astype(F32), rim_first[rows, :].astype(F32)) * high_ok

    padded[0:wide, :] = low_of(slice(wide, 2 * wide))
    padded[wide : wide + frames, :] = hidden[...].astype(F32)
    padded[wide + frames : 2 * wide + frames, :] = high_of(slice(0, wide))
    cot_low = low_of(slice(2 * wide + HALO, 3 * wide))
    cot_high = high_of(slice(2 * wide, 2 * wide + HALO))
    for c in range(0, width, 128):
        cols = slice(c, c + 128)

        def tap_at(j):
            return taps[j : j + 1, cols] if 0 <= j < count else None

        conv = shifted_sum(
            lambda at, rows: padded[at : at + rows, cols],
            lambda s: tap_at(s - 1),
            frames + 2 * HALO,
            cols,
        )
        gate = 1.0 / (1.0 + jnp.exp(-conv))
        mid = slice(HALO, HALO + frames)
        own = padded[wide : wide + frames, cols]
        output[:, cols] = (own + conv[mid] * gate[mid]).astype(BF16)
        slope = gate + conv * gate * (1.0 - gate)
        own_cot = cot[:, cols].astype(F32)
        cots = jnp.concatenate([cot_low[:, cols], own_cot, cot_high[:, cols]], axis=0)
        grads[0 : frames + 2 * HALO, cols] = (cots * slope).astype(BF16).astype(F32)
        back = shifted_sum(
            lambda at, rows: grads[at : at + rows, cols],
            lambda s: tap_at(count - s) if s else None,
            frames,
            cols,
        )
        grad_input[:, cols] = (own_cot + back).astype(BF16)


def term_rows(rows):
    width = rows[0].shape[1]
    at = lax.broadcasted_iota(jnp.int32, (16, width), 0)
    block = jnp.zeros((16, width), F32)
    for r, row in enumerate(rows):
        rest = row
        for k in range(3):
            term = rest.astype(BF16).astype(F32)
            rest = rest - term
            block = jnp.where(at == 3 * r + k, term, block)
    return block.astype(BF16)


def upstream_body(flags, own, core, across, cross, weight, att, lse, message, delta):
    frames, width = own.shape
    place = flags[3]
    total = None
    for flip, block in ((0, own), (1, core), (2, across), (3, cross)):
        at = pl.ds(pl.multiple_of((place ^ flip) * width, 128), width)
        part = dot_nt(block[...], weight[:, at])
        total = part if total is None else total + part
    up = total.astype(BF16)
    message[0:frames, :] = up
    lane = lax.broadcasted_iota(jnp.int32, (frames, HDIM), 1)
    tile = jnp.zeros((frames, HDIM), F32)
    for h in range(width // HDIM):
        cols = head_cols(h)
        product = up[:, cols].astype(F32) * att[:, cols].astype(F32)
        tile = jnp.where(lane == h, jnp.sum(product, axis=1, keepdims=True), tile)
    delta[...] = tile
    lse_rows = lse[...].T
    delta_rows = tile.T
    for h in range(width // HDIM):
        message[frames : frames + 16, head_cols(h)] = term_rows(
            [lse_rows[h : h + 1, :], delta_rows[h : h + 1, :]]
        )


def query_grad_body(scale, flags, q, own, near, first, second, relay, message, lse, delta, grad_query):
    frames, width = q.shape
    kvs = (own, near, first, second, relay)
    for h in range(width // HDIM):
        cols = head_cols(h)
        scores, keys = window_scores(scale, flags, q, kvs, cols)
        probs = jnp.exp(scores - lse[:, h : h + 1])
        values = jnp.concatenate([kv[frames : 2 * frames, cols] for kv in kvs], axis=0)
        dots = dot_nt(message[0:frames, cols], values)
        grads = (probs * (dots - delta[:, h : h + 1]) * scale).astype(BF16)
        grad_query[:, cols] = dot_nn(grads, keys).astype(BF16)


def key_grad_body(scale, flags, own, *refs):
    queries, messages, (grad_key, grad_value) = refs[0:5], refs[5:10], refs[10:12]
    frames, width = queries[0].shape
    biases = (None, None, off_bias(flags[1]), off_bias(flags[2]), off_bias(flags[1]))
    for h in range(width // HDIM):
        cols = head_cols(h)
        asks = jnp.concatenate([q[:, cols] for q in queries], axis=0)
        ups = jnp.concatenate([m[0:frames, cols] for m in messages], axis=0)
        scores = dot_nt(own[0:frames, cols], asks) * scale
        dots = dot_nt(own[frames : 2 * frames, cols], ups)
        probs_low, grads = [], []
        for b, bias in enumerate(biases):
            at = slice(b * frames, (b + 1) * frames)
            terms = messages[b][frames : frames + 16, cols].astype(F32)
            log_total = terms[0:1] + terms[1:2] + terms[2:3]
            row_delta = terms[3:4] + terms[4:5] + terms[5:6]
            part = scores[:, at] if bias is None else scores[:, at] + bias
            probs = jnp.exp(part - log_total)
            probs_low.append(probs.astype(BF16))
            grads.append((probs * (dots[:, at] - row_delta) * scale).astype(BF16))
        grad_value[:, cols] = dot_nn(jnp.concatenate(probs_low, axis=1), ups).astype(BF16)
        grad_key[:, cols] = dot_nn(jnp.concatenate(grads, axis=1), asks).astype(BF16)


def per_device(query_rows, key_rows, value_rows, inputs, out_weight, kernel, cotangent):
    frames, width = query_rows.shape
    whole = out_weight.shape[1]
    scale = 1.0 / math.sqrt(HDIM)
    block, count = lax.axis_index("ctx"), lax.axis_size("ctx")
    even = block % 2 == 0
    lower, upper = block >= 2, block < count - 2
    flags = jnp.stack(
        [even, jnp.where(even, lower, upper), jnp.where(even, upper, lower), lax.axis_index("mp")]
    ).astype(jnp.int32)
    tile = shaped((frames, width), BF16)
    half = shaped((frames, 2 * width), BF16)
    side = shaped((frames, HDIM), F32)

    kv = jnp.concatenate([key_rows, value_rows], axis=0)
    kv_second = ring(kv, 1)
    kv_first = ring(kv, 0)
    kv_near = pair_swap(kv, "ctx", 1)
    kv_relay = pair_swap(kv_second, "ctx", 1)
    window = (kv, kv_near, kv_first, kv_second, kv_relay)

    att, lse, send, keep = kernel_call(
        functools.partial(forward_body, scale),
        (tile, side, half, half),
        (flags, query_rows, *window, out_weight),
        2 * frames * width * (10 * frames + whole),
        "forward",
    )
    core = pair_swap(send, "mp", 1)
    outgoing = keep[:, 0:width] + core[:, 0:width]
    outgoing, query_late = lax.optimization_barrier((outgoing, query_rows))
    across = pair_swap(outgoing, "mp", 2)
    q_second = ring(query_late, 1)
    q_first = ring(query_late, 0)

    hidden, rims = kernel_call(
        hidden_body,
        (tile, shaped((6 * HALO, width), BF16)),
        (flags, inputs, keep, core, across, cotangent),
        4 * frames * width,
        "hidden",
    )
    rim_near = pair_swap(rims, "ctx", 1)
    rim_first = ring(rim_near, 0)

    output, grad_input = pl.pallas_call(
        conv_body,
        out_shape=(tile, tile),
        in_specs=[pl.BlockSpec(memory_space=pltpu.SMEM)]
        + [pl.BlockSpec(memory_space=pltpu.VMEM)] * 5,
        out_specs=(pl.BlockSpec(memory_space=pltpu.VMEM),) * 2,
        scratch_shapes=[
            pltpu.VMEM((frames + 4 * HALO, width), F32),
            pltpu.VMEM((frames + 2 * HALO, width), F32),
        ],
        compiler_params=pltpu.CompilerParams(vmem_limit_bytes=24 * 1024 * 1024),
        cost_estimate=pl.CostEstimate(
            flops=130 * frames * width, bytes_accessed=10 * frames * width, transcendentals=0
        ),
        name="conv",
    )(flags, hidden, rim_near, rim_first, cotangent, kernel)

    grad_input, query_last, second_last = lax.optimization_barrier(
        (grad_input, query_rows, q_second)
    )
    gi_across = pair_swap(grad_input, "mp", 2)
    gi_core = pair_swap(grad_input, "mp", 1)
    q_near = pair_swap(query_last, "ctx", 1)
    q_relay = pair_swap(second_last, "ctx", 1)
    gi_cross = pair_swap(gi_across, "mp", 1)

    message, delta = kernel_call(
        upstream_body,
        (shaped((frames + 16, width), BF16), side),
        (flags, grad_input, gi_core, gi_across, gi_cross, out_weight, att, lse),
        2 * frames * width * whole,
        "upstream",
    )
    m_second = ring(message, 1)
    m_first = ring(message, 0)
    m_near = pair_swap(message, "ctx", 1)
    m_relay = pair_swap(m_second, "ctx", 1)

    (grad_query,) = kernel_call(
        functools.partial(query_grad_body, scale),
        (tile,),
        (flags, query_rows, *window, message, lse, delta),
        30 * frames * frames * width,
        "query_grad",
    )
    grad_key, grad_value = kernel_call(
        functools.partial(key_grad_body, scale),
        (tile, tile),
        (flags, kv, query_rows, q_near, q_first, q_second, q_relay)
        + (message, m_near, m_first, m_second, m_relay),
        40 * frames * frames * width,
        "key_grad",
    )
    return (output, grad_input, grad_query, grad_key, grad_value)


def solution(mesh):
    rows = P("ctx", "mp")
    return jax.shard_map(
        per_device,
        mesh=mesh,
        in_specs=(rows, rows, rows, rows, P("mp", None), P(None, "mp"), rows),
        out_specs=(rows,) * 5,
        check_vma=False,
    )
```

time: 155 us -> 83.2 us (0.54)
  the two profiles are of different devices: /device:TPU:9 before, /device:TPU:0 now
where the time goes in v1:
time: 83.2 us; the launch traced here: 83 us
  waiting for transfers between devices  42.8 us (51%)
  starting transfers between devices  21.5 us (26%)
  Pallas kernels  12.6 us (15%)
  local copies, waits for them, and re-layouts  5.29 us (6%)
    ppermute x12, waiting for transfers between devices, pair_swap(): lax.ppermute(block, axis, [(i, i ^ bit) for i in range(lax.axis_size(axis...  29.7 us
    ppermute x7, waiting for transfers between devices, ring(): return lax.ppermute(block, 'ctx', ring_routes(lax.axis_size('ctx'))[way])  13.2 us
    ppermute x12, starting transfers between devices, pair_swap(): lax.ppermute(block, axis, [(i, i ^ bit) for i in range(lax.axis_size(axis...  13.1 us
    pallas_call x5, Pallas kernels, kernel_call(): pl.pallas_call(body, out_shape=outs, in_specs=[smem] + [vmem] * (len(args...  9.58 us
    ppermute x7, starting transfers between devices, ring(): return lax.ppermute(block, 'ctx', ring_routes(lax.axis_size('ctx'))[way])  8.46 us
    unnamed x17, local copies, waits for them, and re-layouts  4.34 us
    pallas_call x1, Pallas kernels, per_device(): pl.pallas_call(conv_body, out_shape=(tile, tile), in_specs=[pl.BlockSpec(...  2.98 us
  transfers between devices with their start and end apart: 19, of which 13 were waited for; matrix products, arithmetic and copies ran while one was open for 0% of the time, Pallas kernels for 6%

profile of v1, /device:TPU:0, one launch (start us, length us, event | category | flops | bytes accessed | tf_op | source)
XLA Modules:
  0.0 83.0 jit_solution(8517312169659377633)
XLA Ops:
  0.6 0.9 %constant_dynamic-update-slice_fusion.1 = bf16[256,512]{1,0:T(8,128)(2,1)S(1)} fusion(bf16[128,512]{1,0:T(8,128)(2,1)} %param.8), kind=kLoop, calls=%fused_computation.2 | loop fusion | bytes 262144
  1.5 0.0 copy-start.4
  1.6 0.0 copy-start.5
  1.6 1.0 %constant_dynamic-update-slice_fusion.own = bf16[256,512]{1,0:T(8,128)(2,1)S(1)} fusion(bf16[256,512]{1,0:T(8,128)(2,1)S(1)} %constant_dynamic-update-slice_fusion.1, bf16[128,512]{1,0:T(8,128)(2,1)} %param.9), kind=kLoop, calls=%fused_computation.1 | loop fusion | bytes 262144 | tf_op jit(solution)/shard_map/concatenate | solution.py:276
  2.5 3.0 %collective-permute-start.2 = (bf16[256,512]{1,0:T(8,128)(2,1)S(1)}, bf16[256,512]{1,0:T(8,128)(2,1)S(1)}, u32[]{:S(2)}, u32[]{:S(2)}) collective-permute-start(bf16[256,512]{1,0:T(8,128)(2,1)S(1)} %constant_dynamic-update-slice_fusion.own), channel_id=1, source_target_pairs={{8,0},{16,8},{24,16},{28,24},{20,28},{12,20},{4,12},{0,4},{9,1},{1... | collective-permute-start | bytes 786440 | tf_op jit(solution)/shard_map/ppermute | solution.py:39
  5.5 1.6 %collective-permute-start = (bf16[256,512]{1,0:T(8,128)(2,1)S(1)}, bf16[256,512]{1,0:T(8,128)(2,1)S(1)}, u32[]{:S(2)}, u32[]{:S(2)}) collective-permute-start(bf16[256,512]{1,0:T(8,128)(2,1)S(1)} %constant_dynamic-update-slice_fusion.own), channel_id=1, source_target_pairs={{0,4},{4,0},{8,12},{12,8},{16,20},{20,16},{24,28},{28,24},{1,5},{5... | collective-permute-start | bytes 786440 | tf_op jit(solution)/shard_map/ppermute | solution.py:28
  7.1 1.6 %collective-permute-start.1 = (bf16[256,512]{1,0:T(8,128)(2,1)S(1)}, bf16[256,512]{1,0:T(8,128)(2,1)S(1)}, u32[]{:S(2)}, u32[]{:S(2)}) collective-permute-start(bf16[256,512]{1,0:T(8,128)(2,1)S(1)} %constant_dynamic-update-slice_fusion.own), channel_id=1, source_target_pairs={{0,8},{8,16},{16,24},{24,28},{28,20},{20,12},{12,4},{4,0},{1,9},{9... | collective-permute-start | bytes 786440 | tf_op jit(solution)/shard_map/ppermute | solution.py:39
  8.7 3.6 %collective-permute-done.2.second = bf16[256,512]{1,0:T(8,128)(2,1)S(1)} collective-permute-done((bf16[256,512]{1,0:T(8,128)(2,1)S(1)}, bf16[256,512]{1,0:T(8,128)(2,1)S(1)}, u32[]{:S(2)}, u32[]{:S(2)}) %collective-permute-start.2) | collective-permute-done | bytes 262176 | tf_op jit(solution)/shard_map/ppermute | solution.py:39
  12.2 2.5 %collective-permute-start.3 = (bf16[256,512]{1,0:T(8,128)(2,1)S(1)}, bf16[256,512]{1,0:T(8,128)(2,1)S(1)}, u32[]{:S(2)}, u32[]{:S(2)}) collective-permute-start(bf16[256,512]{1,0:T(8,128)(2,1)S(1)} %collective-permute-done.2.second), channel_id=1, source_target_pairs={{0,4},{4,0},{8,12},{12,8},{16,20},{20,16},{24,28},{28,24},{1,5},{5... | collective-permute-start | bytes 786440 | tf_op jit(solution)/shard_map/ppermute | solution.py:28
  14.7 0.1 pad_add_fusion.flags
  14.8 3.1 %collective-permute-done.near = bf16[256,512]{1,0:T(8,128)(2,1)S(1)} collective-permute-done((bf16[256,512]{1,0:T(8,128)(2,1)S(1)}, bf16[256,512]{1,0:T(8,128)(2,1)S(1)}, u32[]{:S(2)}, u32[]{:S(2)}) %collective-permute-start) | collective-permute-done | bytes 262176 | tf_op jit(solution)/shard_map/ppermute | solution.py:28
  17.9 2.5 %collective-permute-done.1.first = bf16[256,512]{1,0:T(8,128)(2,1)S(1)} collective-permute-done((bf16[256,512]{1,0:T(8,128)(2,1)S(1)}, bf16[256,512]{1,0:T(8,128)(2,1)S(1)}, u32[]{:S(2)}, u32[]{:S(2)}) %collective-permute-start.1) | collective-permute-done | bytes 262176 | tf_op jit(solution)/shard_map/ppermute | solution.py:39
  20.4 4.2 %collective-permute-done.3.relay = bf16[256,512]{1,0:T(8,128)(2,1)S(1)} collective-permute-done((bf16[256,512]{1,0:T(8,128)(2,1)S(1)}, bf16[256,512]{1,0:T(8,128)(2,1)S(1)}, u32[]{:S(2)}, u32[]{:S(2)}) %collective-permute-start.3) | collective-permute-done | bytes 262176 | tf_op jit(solution)/shard_map/ppermute | solution.py:28
  24.5 0.0 copy-start
  24.5 1.6 %copy-done = bf16[512,2048]{1,0:T(8,128)(2,1)S(1)} copy-done((bf16[512,2048]{1,0:T(8,128)(2,1)S(1)}, bf16[512,2048]{1,0:T(8,128)(2,1)}, u32[]{:S(2)}) %copy-start) | copy-done | bytes 2097176
  26.1 0.0 copy-start.2
  26.1 0.9 %copy-done.2 = bf16[128,512]{1,0:T(8,128)(2,1)S(1)} copy-done((bf16[128,512]{1,0:T(8,128)(2,1)S(1)}, bf16[128,512]{1,0:T(8,128)(2,1)}, u32[]{:S(2)}) %copy-start.2) | copy-done | bytes 131096
  27.0 0.0 copy-start.3
  27.0 0.0 copy-start.7
  27.0 0.0 copy-start.1
  27.0 2.7 %forward.1 = (bf16[128,512]{1,0:T(8,128)(2,1)S(1)}, f32[128,128]{1,0:T(8,128)S(1)}, bf16[128,1024]{1,0:T(8,128)(2,1)S(1)}, bf16[128,1024]{1,0:T(8,128)(2,1)S(1)}) custom-call(s32[4]{0:T(128)S(1)} %pad_add_fusion.flags, bf16[128,512]{1,0:T(8,128)(2,1)S(1)} %copy-done.2, bf16[256,512]{1,0:T(8,128)(2,1)S(1)} %constant_dynamic-update-slice_fusion.own, ...), custom_call_target="tpu_custom_call" | custom-call | flops 436207616 | bytes 4259856 | tf_op jit(solution)/shard_map/forward/pallas_call | solution.py:46
  29.8 0.1 collective-permute-start.4
  29.9 1.5 %collective-permute-done.4.core = bf16[128,1024]{1,0:T(8,128)(2,1)S(1)} collective-permute-done((bf16[128,1024]{1,0:T(8,128)(2,1)S(1)}, bf16[128,1024]{1,0:T(8,128)(2,1)S(1)}, u32[]{:S(2)}, u32[]{:S(2)}) %collective-permute-start.4) | collective-permute-done | bytes 262176 | tf_op jit(solution)/shard_map/ppermute | solution.py:28
  31.4 1.6 %collective-permute-start.5 = (bf16[128,512]{1,0:T(8,128)(2,1)S(1)}, bf16[128,512]{1,0:T(8,128)(2,1)S(1)}, u32[]{:S(2)}, u32[]{:S(2)}) collective-permute-start(bf16[128,512]{1,0:T(8,128)(2,1)S(1)} %slice_add_fusion), channel_id=1, source_target_pairs={{0,2},{1,3},{2,0},{3,1},{4,6},{5,7},{6,4},{7,5},{8,10},{9,11},{10,... | collective-permute-start | bytes 393224 | tf_op jit(solution)/shard_map/ppermute | solution.py:28
  33.0 4.0 %collective-permute-done.5.across = bf16[128,512]{1,0:T(8,128)(2,1)S(1)} collective-permute-done((bf16[128,512]{1,0:T(8,128)(2,1)S(1)}, bf16[128,512]{1,0:T(8,128)(2,1)S(1)}, u32[]{:S(2)}, u32[]{:S(2)}) %collective-permute-start.5) | collective-permute-done | bytes 131104 | tf_op jit(solution)/shard_map/ppermute | solution.py:28
  37.0 0.0 copy-done.4
  37.0 0.0 copy-done.5
  37.0 0.6 hidden.1
  37.7 0.3 collective-permute-start.6
  38.0 0.0 copy-done.3
  38.0 1.7 %collective-permute-start.8 = (bf16[128,512]{1,0:T(8,128)(2,1)S(1)}, bf16[128,512]{1,0:T(8,128)(2,1)S(1)}, u32[]{:S(2)}, u32[]{:S(2)}) collective-permute-start(bf16[128,512]{1,0:T(8,128)(2,1)S(1)} %copy-done.3), channel_id=1, source_target_pairs={{8,0},{16,8},{24,16},{28,24},{20,28},{12,20},{4,12},{0,4},{9,1},{1... | collective-permute-start | bytes 393224 | tf_op jit(solution)/shard_map/ppermute | solution.py:39
  39.8 2.6 %collective-permute-done.6.rim_near = bf16[96,512]{1,0:T(8,128)(2,1)S(1)} collective-permute-done((bf16[96,512]{1,0:T(8,128)(2,1)S(1)}, bf16[96,512]{1,0:T(8,128)(2,1)S(1)}, u32[]{:S(2)}, u32[]{:S(2)}) %collective-permute-start.6) | collective-permute-done | bytes 98336 | tf_op jit(solution)/shard_map/ppermute | solution.py:28
  42.3 0.0 collective-permute-start.7
  42.3 4.6 %collective-permute-done.7.rim_first = bf16[96,512]{1,0:T(8,128)(2,1)S(1)} collective-permute-done((bf16[96,512]{1,0:T(8,128)(2,1)S(1)}, bf16[96,512]{1,0:T(8,128)(2,1)S(1)}, u32[]{:S(2)}, u32[]{:S(2)}) %collective-permute-start.7) | collective-permute-done | bytes 98336 | tf_op jit(solution)/shard_map/ppermute | solution.py:39
  47.0 0.0 copy-done.7
  47.0 3.0 %conv.1 = (bf16[128,512]{1,0:T(8,128)(2,1)}, bf16[128,512]{1,0:T(8,128)(2,1)}) custom-call(s32[4]{0:T(128)S(1)} %pad_add_fusion.flags, bf16[128,512]{1,0:T(8,128)(2,1)S(1)} %get-tuple-element.25.hidden, bf16[96,512]{1,0:T(8,128)(2,1)S(1)} %collective-permute-done.6.rim_near, bf16[96,512]{1,0:T(8,128)(2,1)S(1)} %collective-permute-done.7.rim_first, ...), custom_call_target="tpu_custom_call" | custom-call | flops 8519680 | bytes 655360 | tf_op jit(solution)/shard_map/conv/pallas_call | solution.py:307
  49.9 0.0 collective-permute-done.8.refs_3_
  49.9 1.5 %collective-permute-start.10 = (bf16[128,512]{1,0:T(8,128)(2,1)}, bf16[128,512]{1,0:T(8,128)(2,1)S(1)}, u32[]{:S(2)}, u32[]{:S(2)}) collective-permute-start(bf16[128,512]{1,0:T(8,128)(2,1)} %get-tuple-element.18.own), channel_id=1, source_target_pairs={{0,2},{1,3},{2,0},{3,1},{4,6},{5,7},{6,4},{7,5},{8,10},{9,11},{10,... | collective-permute-start | bytes 393224 | tf_op jit(solution)/shard_map/ppermute | solution.py:28
  51.5 0.0 collective-permute-start.9
  51.5 3.7 %collective-permute-done.10.across = bf16[128,512]{1,0:T(8,128)(2,1)S(1)} collective-permute-done((bf16[128,512]{1,0:T(8,128)(2,1)}, bf16[128,512]{1,0:T(8,128)(2,1)S(1)}, u32[]{:S(2)}, u32[]{:S(2)}) %collective-permute-start.10) | collective-permute-done | bytes 131104 | tf_op jit(solution)/shard_map/ppermute | solution.py:28
  55.1 0.0 collective-permute-start.11
  55.1 0.0 collective-permute-done.9.core
  55.1 1.3 %collective-permute-done.11.cross = bf16[128,512]{1,0:T(8,128)(2,1)S(1)} collective-permute-done((bf16[128,512]{1,0:T(8,128)(2,1)S(1)}, bf16[128,512]{1,0:T(8,128)(2,1)S(1)}, u32[]{:S(2)}, u32[]{:S(2)}) %collective-permute-start.11) | collective-permute-done | bytes 131104 | tf_op jit(solution)/shard_map/ppermute | solution.py:28
  56.5 0.0 copy-done.1
  56.5 0.0 copy-start.6
  56.5 0.9 %copy-done.6 = bf16[128,512]{1,0:T(8,128)(2,1)S(1)} copy-done((bf16[128,512]{1,0:T(8,128)(2,1)S(1)}, bf16[128,512]{1,0:T(8,128)(2,1)}, u32[]{:S(2)}) %copy-start.6) | copy-done | bytes 131096
  57.4 1.5 %upstream.1 = (bf16[144,512]{1,0:T(8,128)(2,1)S(1)}, f32[128,128]{1,0:T(8,128)S(1)}) custom-call(s32[4]{0:T(128)S(1)} %pad_add_fusion.flags, bf16[128,512]{1,0:T(8,128)(2,1)S(1)} %copy-done.6, bf16[128,512]{1,0:T(8,128)(2,1)S(1)} %collective-permute-done.9.core, bf16[128,512]{1,0:T(8,128)(2,1)S(1)} %collective-permute-done.10.across, ...), custom_call_target="tpu_custom_call" | custom-call | flops 268435456 | bytes 3031056 | tf_op jit(solution)/shard_map/upstream/pallas_call | solution.py:46
  58.9 1.4 %collective-permute-start.17 = (bf16[144,512]{1,0:T(8,128)(2,1)S(1)}, bf16[144,512]{1,0:T(8,128)(2,1)S(1)}, u32[]{:S(2)}, u32[]{:S(2)}) collective-permute-start(bf16[144,512]{1,0:T(8,128)(2,1)S(1)} %get-tuple-element.33.message.refs_5_), channel_id=1, source_target_pairs={{8,0},{16,8},{24,16},{28,24},{20,28},{12,20},{4,12},{0,4},{9,1},{1... | collective-permute-start | bytes 442376 | tf_op jit(solution)/shard_map/ppermute | solution.py:39
  60.3 0.7 collective-permute-start.13
  61.0 1.3 %collective-permute-start.15 = (bf16[144,512]{1,0:T(8,128)(2,1)S(1)}, bf16[144,512]{1,0:T(8,128)(2,1)S(1)}, u32[]{:S(2)}, u32[]{:S(2)}) collective-permute-start(bf16[144,512]{1,0:T(8,128)(2,1)S(1)} %get-tuple-element.33.message.refs_5_), channel_id=1, source_target_pairs={{0,4},{4,0},{8,12},{12,8},{16,20},{20,16},{24,28},{28,24},{1,5},{5... | collective-permute-start | bytes 442376 | tf_op jit(solution)/shard_map/ppermute | solution.py:28
  62.3 0.1 collective-permute-start.16
  62.4 2.5 %collective-permute-done.17.refs_8_ = bf16[144,512]{1,0:T(8,128)(2,1)S(1)} collective-permute-done((bf16[144,512]{1,0:T(8,128)(2,1)S(1)}, bf16[144,512]{1,0:T(8,128)(2,1)S(1)}, u32[]{:S(2)}, u32[]{:S(2)}) %collective-permute-start.17) | collective-permute-done | bytes 147488 | tf_op jit(solution)/shard_map/ppermute | solution.py:39
  64.9 2.1 %collective-permute-start.18 = (bf16[144,512]{1,0:T(8,128)(2,1)S(1)}, bf16[144,512]{1,0:T(8,128)(2,1)S(1)}, u32[]{:S(2)}, u32[]{:S(2)}) collective-permute-start(bf16[144,512]{1,0:T(8,128)(2,1)S(1)} %collective-permute-done.17.refs_8_), channel_id=1, source_target_pairs={{0,4},{4,0},{8,12},{12,8},{16,20},{20,16},{24,28},{28,24},{1,5},{5... | collective-permute-start | bytes 442376 | tf_op jit(solution)/shard_map/ppermute | solution.py:28
  67.0 0.0 collective-permute-start.12
  67.0 0.0 collective-permute-done.13.refs_2_
  67.0 2.0 %collective-permute-start.14 = (bf16[128,512]{1,0:T(8,128)(2,1)S(1)}, bf16[128,512]{1,0:T(8,128)(2,1)S(1)}, u32[]{:S(2)}, u32[]{:S(2)}) collective-permute-start(bf16[128,512]{1,0:T(8,128)(2,1)S(1)} %collective-permute-done.8.refs_3_), channel_id=1, source_target_pairs={{0,4},{4,0},{8,12},{12,8},{16,20},{20,16},{24,28},{28,24},{1,5},{5... | collective-permute-start | bytes 393224 | tf_op jit(solution)/shard_map/ppermute | solution.py:28
  69.0 2.3 %query_grad.1 = bf16[128,512]{1,0:T(8,128)(2,1)} custom-call(s32[4]{0:T(128)S(1)} %pad_add_fusion.flags, bf16[128,512]{1,0:T(8,128)(2,1)S(1)} %copy-done.3, bf16[256,512]{1,0:T(8,128)(2,1)S(1)} %constant_dynamic-update-slice_fusion.own, bf16[256,512]{1,0:T(8,128)(2,1)S(1)} %collective-permute-done.near, bf16[256,512]{1,0:T(8,128)(2,1)S(1)} %collective-permute-done.1.first, ...), custom_call_target="tpu_custom_call" | custom-call | flops 251658240 | bytes 1851408 | tf_op jit(solution)/shard_map/query_grad/pallas_call | solution.py:46
  71.3 7.6 %collective-permute-done.12.refs_1_ = bf16[128,512]{1,0:T(8,128)(2,1)S(1)} collective-permute-done((bf16[128,512]{1,0:T(8,128)(2,1)S(1)}, bf16[128,512]{1,0:T(8,128)(2,1)S(1)}, u32[]{:S(2)}, u32[]{:S(2)}) %collective-permute-start.12) | collective-permute-done | bytes 131104 | tf_op jit(solution)/shard_map/ppermute | solution.py:28
  79.0 1.7 %collective-permute-done.14.refs_4_ = bf16[128,512]{1,0:T(8,128)(2,1)S(1)} collective-permute-done((bf16[128,512]{1,0:T(8,128)(2,1)S(1)}, bf16[128,512]{1,0:T(8,128)(2,1)S(1)}, u32[]{:S(2)}, u32[]{:S(2)}) %collective-permute-start.14) | collective-permute-done | bytes 131104 | tf_op jit(solution)/shard_map/ppermute | solution.py:28
  80.7 0.0 collective-permute-done.15.refs_6_
  80.7 0.0 collective-permute-done.16.refs_7_
  80.7 0.0 collective-permute-done.18.refs_9_
  80.7 2.3 %key_grad.1 = (bf16[128,512]{1,0:T(8,128)(2,1)}, bf16[128,512]{1,0:T(8,128)(2,1)}) custom-call(s32[4]{0:T(128)S(1)} %pad_add_fusion.flags, bf16[256,512]{1,0:T(8,128)(2,1)S(1)} %constant_dynamic-update-slice_fusion.own, bf16[128,512]{1,0:T(8,128)(2,1)S(1)} %copy-done.3, bf16[128,512]{1,0:T(8,128)(2,1)S(1)} %collective-permute-done.12.refs_1_, ...), custom_call_target="tpu_custom_call" | custom-call | flops 335544320 | bytes 1916944 | tf_op jit(solution)/shard_map/key_grad/pallas_call | solution.py:46
  (1 shorter events, 0.0 us)
Async XLA Ops:
  1.5 35.5 %copy-start.4 = (bf16[128,512]{1,0:T(8,128)(2,1)S(1)}, bf16[128,512]{1,0:T(8,128)(2,1)}, u32[]{:S(2)}) copy-start(bf16[128,512]{1,0:T(8,128)(2,1)} %cot.3) | copy-start | bytes 393220
  1.6 35.5 %copy-start.5 = (bf16[128,512]{1,0:T(8,128)(2,1)S(1)}, bf16[128,512]{1,0:T(8,128)(2,1)}, u32[]{:S(2)}) copy-start(bf16[128,512]{1,0:T(8,128)(2,1)} %inputs.1) | copy-start | bytes 393220
  2.5 9.7 %collective-permute-start.2 = (bf16[256,512]{1,0:T(8,128)(2,1)S(1)}, bf16[256,512]{1,0:T(8,128)(2,1)S(1)}, u32[]{:S(2)}, u32[]{:S(2)}) collective-permute-start(bf16[256,512]{1,0:T(8,128)(2,1)S(1)} %constant_dynamic-update-slice_fusion.own), channel_id=1, source_target_pairs={{8,0},{16,8},{24,16},{28,24},{20,28},{12,20},{4,12},{0,4},{9,1},{1... | collective-permute-start | bytes 786440 | tf_op jit(solution)/shard_map/ppermute | solution.py:39
  5.5 12.3 %collective-permute-start = (bf16[256,512]{1,0:T(8,128)(2,1)S(1)}, bf16[256,512]{1,0:T(8,128)(2,1)S(1)}, u32[]{:S(2)}, u32[]{:S(2)}) collective-permute-start(bf16[256,512]{1,0:T(8,128)(2,1)S(1)} %constant_dynamic-update-slice_fusion.own), channel_id=1, source_target_pairs={{0,4},{4,0},{8,12},{12,8},{16,20},{20,16},{24,28},{28,24},{1,5},{5... | collective-permute-start | bytes 786440 | tf_op jit(solution)/shard_map/ppermute | solution.py:28
  7.1 13.3 %collective-permute-start.1 = (bf16[256,512]{1,0:T(8,128)(2,1)S(1)}, bf16[256,512]{1,0:T(8,128)(2,1)S(1)}, u32[]{:S(2)}, u32[]{:S(2)}) collective-permute-start(bf16[256,512]{1,0:T(8,128)(2,1)S(1)} %constant_dynamic-update-slice_fusion.own), channel_id=1, source_target_pairs={{0,8},{8,16},{16,24},{24,28},{28,20},{20,12},{12,4},{4,0},{1,9},{9... | collective-permute-start | bytes 786440 | tf_op jit(solution)/shard_map/ppermute | solution.py:39
  12.2 12.3 %collective-permute-start.3 = (bf16[256,512]{1,0:T(8,128)(2,1)S(1)}, bf16[256,512]{1,0:T(8,128)(2,1)S(1)}, u32[]{:S(2)}, u32[]{:S(2)}) collective-permute-start(bf16[256,512]{1,0:T(8,128)(2,1)S(1)} %collective-permute-done.2.second), channel_id=1, source_target_pairs={{0,4},{4,0},{8,12},{12,8},{16,20},{20,16},{24,28},{28,24},{1,5},{5... | collective-permute-start | bytes 786440 | tf_op jit(solution)/shard_map/ppermute | solution.py:28
  24.5 1.6 %copy-start = (bf16[512,2048]{1,0:T(8,128)(2,1)S(1)}, bf16[512,2048]{1,0:T(8,128)(2,1)}, u32[]{:S(2)}) copy-start(bf16[512,2048]{1,0:T(8,128)(2,1)} %weight.3) | copy-start | bytes 6291460
  26.1 0.9 %copy-start.2 = (bf16[128,512]{1,0:T(8,128)(2,1)S(1)}, bf16[128,512]{1,0:T(8,128)(2,1)}, u32[]{:S(2)}) copy-start(bf16[128,512]{1,0:T(8,128)(2,1)} %refs_0_.1) | copy-start | bytes 393220
  27.0 11.0 %copy-start.3 = (bf16[128,512]{1,0:T(8,128)(2,1)S(1)}, bf16[128,512]{1,0:T(8,128)(2,1)}, u32[]{:S(2)}) copy-start(bf16[128,512]{1,0:T(8,128)(2,1)} %refs_0_.1) | copy-start | bytes 393220
  27.0 19.9 %copy-start.7 = (f32[31,512]{1,0:T(8,128)S(1)}, f32[31,512]{1,0:T(8,128)}, u32[]{:S(2)}) copy-start(f32[31,512]{1,0:T(8,128)} %taps.1) | copy-start | bytes 190468
  27.0 29.5 %copy-start.1 = (bf16[512,2048]{1,0:T(8,128)(2,1)S(1)}, bf16[512,2048]{1,0:T(8,128)(2,1)}, u32[]{:S(2)}) copy-start(bf16[512,2048]{1,0:T(8,128)(2,1)} %weight.3) | copy-start | bytes 6291460
  29.8 1.6 %collective-permute-start.4 = (bf16[128,1024]{1,0:T(8,128)(2,1)S(1)}, bf16[128,1024]{1,0:T(8,128)(2,1)S(1)}, u32[]{:S(2)}, u32[]{:S(2)}) collective-permute-start(bf16[128,1024]{1,0:T(8,128)(2,1)S(1)} %get-tuple-element.23), channel_id=1, source_target_pairs={{0,1},{1,0},{2,3},{3,2},{4,5},{5,4},{6,7},{7,6},{8,9},{9,8},{10,11... | collective-permute-start | bytes 786440 | tf_op jit(solution)/shard_map/ppermute | solution.py:28
  31.4 5.6 %collective-permute-start.5 = (bf16[128,512]{1,0:T(8,128)(2,1)S(1)}, bf16[128,512]{1,0:T(8,128)(2,1)S(1)}, u32[]{:S(2)}, u32[]{:S(2)}) collective-permute-start(bf16[128,512]{1,0:T(8,128)(2,1)S(1)} %slice_add_fusion), channel_id=1, source_target_pairs={{0,2},{1,3},{2,0},{3,1},{4,6},{5,7},{6,4},{7,5},{8,10},{9,11},{10,... | collective-permute-start | bytes 393224 | tf_op jit(solution)/shard_map/ppermute | solution.py:28
  37.7 4.7 %collective-permute-start.6 = (bf16[96,512]{1,0:T(8,128)(2,1)S(1)}, bf16[96,512]{1,0:T(8,128)(2,1)S(1)}, u32[]{:S(2)}, u32[]{:S(2)}) collective-permute-start(bf16[96,512]{1,0:T(8,128)(2,1)S(1)} %get-tuple-element.26), channel_id=1, source_target_pairs={{0,4},{4,0},{8,12},{12,8},{16,20},{20,16},{24,28},{28,24},{1,5},{5... | collective-permute-start | bytes 294920 | tf_op jit(solution)/shard_map/ppermute | solution.py:28
  38.0 11.9 %collective-permute-start.8 = (bf16[128,512]{1,0:T(8,128)(2,1)S(1)}, bf16[128,512]{1,0:T(8,128)(2,1)S(1)}, u32[]{:S(2)}, u32[]{:S(2)}) collective-permute-start(bf16[128,512]{1,0:T(8,128)(2,1)S(1)} %copy-done.3), channel_id=1, source_target_pairs={{8,0},{16,8},{24,16},{28,24},{20,28},{12,20},{4,12},{0,4},{9,1},{1... | collective-permute-start | bytes 393224 | tf_op jit(solution)/shard_map/ppermute | solution.py:39
  42.3 4.6 %collective-permute-start.7 = (bf16[96,512]{1,0:T(8,128)(2,1)S(1)}, bf16[96,512]{1,0:T(8,128)(2,1)S(1)}, u32[]{:S(2)}, u32[]{:S(2)}) collective-permute-start(bf16[96,512]{1,0:T(8,128)(2,1)S(1)} %collective-permute-done.6.rim_near), channel_id=1, source_target_pairs={{0,8},{8,16},{16,24},{24,28},{28,20},{20,12},{12,4},{4,0},{1,9},{9... | collective-permute-start | bytes 294920 | tf_op jit(solution)/shard_map/ppermute | solution.py:39
  49.9 5.2 %collective-permute-start.10 = (bf16[128,512]{1,0:T(8,128)(2,1)}, bf16[128,512]{1,0:T(8,128)(2,1)S(1)}, u32[]{:S(2)}, u32[]{:S(2)}) collective-permute-start(bf16[128,512]{1,0:T(8,128)(2,1)} %get-tuple-element.18.own), channel_id=1, source_target_pairs={{0,2},{1,3},{2,0},{3,1},{4,6},{5,7},{6,4},{7,5},{8,10},{9,11},{10,... | collective-permute-start | bytes 393224 | tf_op jit(solution)/shard_map/ppermute | solution.py:28
  51.5 3.7 %collective-permute-start.9 = (bf16[128,512]{1,0:T(8,128)(2,1)}, bf16[128,512]{1,0:T(8,128)(2,1)S(1)}, u32[]{:S(2)}, u32[]{:S(2)}) collective-permute-start(bf16[128,512]{1,0:T(8,128)(2,1)} %get-tuple-element.18.own), channel_id=1, source_target_pairs={{0,1},{1,0},{2,3},{3,2},{4,5},{5,4},{6,7},{7,6},{8,9},{9,8},{10,11... | collective-permute-start | bytes 393224 | tf_op jit(solution)/shard_map/ppermute | solution.py:28
  55.1 1.3 %collective-permute-start.11 = (bf16[128,512]{1,0:T(8,128)(2,1)S(1)}, bf16[128,512]{1,0:T(8,128)(2,1)S(1)}, u32[]{:S(2)}, u32[]{:S(2)}) collective-permute-start(bf16[128,512]{1,0:T(8,128)(2,1)S(1)} %collective-permute-done.10.across), channel_id=1, source_target_pairs={{0,1},{1,0},{2,3},{3,2},{4,5},{5,4},{6,7},{7,6},{8,9},{9,8},{10,11... | collective-permute-start | bytes 393224 | tf_op jit(solution)/shard_map/ppermute | solution.py:28
  56.5 0.9 %copy-start.6 = (bf16[128,512]{1,0:T(8,128)(2,1)S(1)}, bf16[128,512]{1,0:T(8,128)(2,1)}, u32[]{:S(2)}) copy-start(bf16[128,512]{1,0:T(8,128)(2,1)} %get-tuple-element.18.own) | copy-start | bytes 393220
  58.9 6.0 %collective-permute-start.17 = (bf16[144,512]{1,0:T(8,128)(2,1)S(1)}, bf16[144,512]{1,0:T(8,128)(2,1)S(1)}, u32[]{:S(2)}, u32[]{:S(2)}) collective-permute-start(bf16[144,512]{1,0:T(8,128)(2,1)S(1)} %get-tuple-element.33.message.refs_5_), channel_id=1, source_target_pairs={{8,0},{16,8},{24,16},{28,24},{20,28},{12,20},{4,12},{0,4},{9,1},{1... | collective-permute-start | bytes 442376 | tf_op jit(solution)/shard_map/ppermute | solution.py:39
  60.3 6.7 %collective-permute-start.13 = (bf16[128,512]{1,0:T(8,128)(2,1)S(1)}, bf16[128,512]{1,0:T(8,128)(2,1)S(1)}, u32[]{:S(2)}, u32[]{:S(2)}) collective-permute-start(bf16[128,512]{1,0:T(8,128)(2,1)S(1)} %copy-done.3), channel_id=1, source_target_pairs={{0,8},{8,16},{16,24},{24,28},{28,20},{20,12},{12,4},{4,0},{1,9},{9... | collective-permute-start | bytes 393224 | tf_op jit(solution)/shard_map/ppermute | solution.py:39
  61.0 19.7 %collective-permute-start.15 = (bf16[144,512]{1,0:T(8,128)(2,1)S(1)}, bf16[144,512]{1,0:T(8,128)(2,1)S(1)}, u32[]{:S(2)}, u32[]{:S(2)}) collective-permute-start(bf16[144,512]{1,0:T(8,128)(2,1)S(1)} %get-tuple-element.33.message.refs_5_), channel_id=1, source_target_pairs={{0,4},{4,0},{8,12},{12,8},{16,20},{20,16},{24,28},{28,24},{1,5},{5... | collective-permute-start | bytes 442376 | tf_op jit(solution)/shard_map/ppermute | solution.py:28
  62.3 18.3 %collective-permute-start.16 = (bf16[144,512]{1,0:T(8,128)(2,1)S(1)}, bf16[144,512]{1,0:T(8,128)(2,1)S(1)}, u32[]{:S(2)}, u32[]{:S(2)}) collective-permute-start(bf16[144,512]{1,0:T(8,128)(2,1)S(1)} %get-tuple-element.33.message.refs_5_), channel_id=1, source_target_pairs={{0,8},{8,16},{16,24},{24,28},{28,20},{20,12},{12,4},{4,0},{1,9},{9... | collective-permute-start | bytes 442376 | tf_op jit(solution)/shard_map/ppermute | solution.py:39
  64.9 15.8 %collective-permute-start.18 = (bf16[144,512]{1,0:T(8,128)(2,1)S(1)}, bf16[144,512]{1,0:T(8,128)(2,1)S(1)}, u32[]{:S(2)}, u32[]{:S(2)}) collective-permute-start(bf16[144,512]{1,0:T(8,128)(2,1)S(1)} %collective-permute-done.17.refs_8_), channel_id=1, source_target_pairs={{0,4},{4,0},{8,12},{12,8},{16,20},{20,16},{24,28},{28,24},{1,5},{5... | collective-permute-start | bytes 442376 | tf_op jit(solution)/shard_map/ppermute | solution.py:28
  67.0 12.0 %collective-permute-start.12 = (bf16[128,512]{1,0:T(8,128)(2,1)S(1)}, bf16[128,512]{1,0:T(8,128)(2,1)S(1)}, u32[]{:S(2)}, u32[]{:S(2)}) collective-permute-start(bf16[128,512]{1,0:T(8,128)(2,1)S(1)} %copy-done.3), channel_id=1, source_target_pairs={{0,4},{4,0},{8,12},{12,8},{16,20},{20,16},{24,28},{28,24},{1,5},{5... | collective-permute-start | bytes 393224 | tf_op jit(solution)/shard_map/ppermute | solution.py:28
  67.0 13.6 %collective-permute-start.14 = (bf16[128,512]{1,0:T(8,128)(2,1)S(1)}, bf16[128,512]{1,0:T(8,128)(2,1)S(1)}, u32[]{:S(2)}, u32[]{:S(2)}) collective-permute-start(bf16[128,512]{1,0:T(8,128)(2,1)S(1)} %collective-permute-done.8.refs_3_), channel_id=1, source_target_pairs={{0,4},{4,0},{8,12},{12,8},{16,20},{20,16},{24,28},{28,24},{1,5},{5... | collective-permute-start | bytes 393224 | tf_op jit(solution)/shard_map/ppermute | solution.py:28

commit v2 on v1

v2 whole, which is shorter than its diff:
```python
import functools
import math

import jax
import jax.numpy as jnp
from jax import lax
from jax.experimental import pallas as pl
from jax.experimental.pallas import tpu as pltpu
from jax.sharding import PartitionSpec as P

HDIM = 128
F32 = jnp.float32
BF16 = jnp.bfloat16
HALO = 16
NT = (((1,), (1,)), ((), ()))
NN = (((1,), (0,)), ((), ()))


def dot_nt(a, b):
    return lax.dot_general(a, b, NT, preferred_element_type=F32)


def dot_nn(a, b):
    return lax.dot_general(a, b, NN, preferred_element_type=F32)


def pair_swap(block, axis, bit):
    return lax.ppermute(block, axis, [(i, i ^ bit) for i in range(lax.axis_size(axis))])


def ring_routes(count):
    rise = [(i, i + 2) for i in range(0, count - 2, 2)] + [(count - 2, count - 1)]
    fall = [(i, i - 2) for i in range(count - 1, 2, -2)] + [(1, 0)]
    route = rise + fall
    return route, [(b, a) for a, b in route]


def ring(block, way):
    return lax.ppermute(block, "ctx", ring_routes(lax.axis_size("ctx"))[way])


def inner_swap(block):
    return lax.ppermute(block, "ctx", [(i, i ^ 1) for i in range(2, lax.axis_size("ctx") - 2)])


def window_of(block):
    second = ring(block, 1)
    first = ring(block, 0)
    near = inner_swap(block)
    return near, first, second, pair_swap(second, "ctx", 1)


SMEM = pl.BlockSpec(memory_space=pltpu.SMEM)
VMEM = pl.BlockSpec(memory_space=pltpu.VMEM)
ANY = pl.BlockSpec(memory_space=pl.ANY)
HBM = pl.BlockSpec(memory_space=pltpu.HBM)


def kernel_call(body, outs, args, flops, name, spaces=None, scratch=(), mib=24, out_space=VMEM):
    nbytes = sum(math.prod(a.shape) * a.dtype.itemsize for a in list(args) + list(outs))
    return pl.pallas_call(
        body,
        out_shape=outs,
        in_specs=spaces or [SMEM] + [VMEM] * (len(args) - 1),
        out_specs=tuple(out_space for _ in outs),
        scratch_shapes=scratch,
        compiler_params=pltpu.CompilerParams(vmem_limit_bytes=mib * 1024 * 1024),
        cost_estimate=pl.CostEstimate(flops=flops, bytes_accessed=nbytes, transcendentals=0),
        name=name,
    )(*args)


def shaped(shape, dtype):
    return jax.ShapeDtypeStruct(shape, dtype)


def off_bias(flag):
    return jnp.where(flag > 0, jnp.float32(0.0), jnp.float32(-jnp.inf))


def head_cols(h):
    return slice(h * HDIM, (h + 1) * HDIM)


def pack_body(key, value, packed, sems):
    frames = key.shape[0]
    copies = [
        pltpu.make_async_copy(key, packed.at[pl.ds(0, frames)], sems.at[0]),
        pltpu.make_async_copy(value, packed.at[pl.ds(frames, frames)], sems.at[1]),
    ]
    for copy in copies:
        copy.start()
    for copy in copies:
        copy.wait()


def stacked(kvs, rows, cols):
    return jnp.concatenate([kv[rows, cols] for kv in kvs], axis=0)


def fetch_body(weight, seen, fetched, sem):
    copy = pltpu.make_async_copy(weight, fetched, sem)
    copy.start()
    copy.wait()


def forward_body(scale, flags, q, own, near, first, second, sums, tops, totals):
    frames, width = q.shape
    kvs = (near, own, first, second)
    lane = lax.broadcasted_iota(jnp.int32, (frames, HDIM), 1)
    top_tile = jnp.zeros((frames, HDIM), F32)
    total_tile = jnp.zeros((frames, HDIM), F32)
    bias = off_bias(flags[1])
    for h in range(width // HDIM):
        cols = head_cols(h)
        scores = dot_nt(q[:, cols], stacked(kvs, slice(0, frames), cols)) * scale
        scores = jnp.concatenate([scores[:, 0:frames] + bias, scores[:, frames:]], axis=1)
        top = jnp.max(scores, axis=1, keepdims=True)
        probs = jnp.exp(scores - top)
        sums[:, cols] = dot_nn(probs.astype(BF16), stacked(kvs, slice(frames, 2 * frames), cols))
        top_tile = jnp.where(lane == h, top, top_tile)
        total_tile = jnp.where(lane == h, jnp.sum(probs, axis=1, keepdims=True), total_tile)
    tops[...] = top_tile
    totals[...] = total_tile


def project_body(scale, flags, q, relay, sums, tops, totals, weight, att, lse, send, keep, q_message):
    frames, width = q.shape
    lane = lax.broadcasted_iota(jnp.int32, (frames, HDIM), 1)
    lse_tile = jnp.zeros((frames, HDIM), F32)
    bias = off_bias(flags[2])
    for h in range(width // HDIM):
        cols = head_cols(h)
        scores = dot_nt(q[:, cols], relay[0:frames, cols]) * scale + bias
        old_top = tops[:, h : h + 1]
        top = jnp.maximum(old_top, jnp.max(scores, axis=1, keepdims=True))
        shrink = jnp.exp(old_top - top)
        probs = jnp.exp(scores - top)
        total = totals[:, h : h + 1] * shrink + jnp.sum(probs, axis=1, keepdims=True)
        summed = sums[:, cols] * shrink + dot_nn(probs.astype(BF16), relay[frames : 2 * frames, cols])
        att[:, cols] = (summed / total).astype(BF16)
        lse_tile = jnp.where(lane == h, top + jnp.log(total), lse_tile)
    lse[...] = lse_tile
    place = flags[3]
    attended = att[...]

    def share(target):
        block = weight[:, pl.ds(pl.multiple_of(target * width, 128), width)]
        return dot_nn(attended, block).astype(BF16)

    send[:, 0:width] = share(place ^ 3)
    send[:, width : 2 * width] = share(place ^ 1)
    keep[:, 0:width] = share(place ^ 2)
    keep[:, width : 2 * width] = share(place)
    q_message[0:frames, :] = q[...]
    put_terms(q_message, lse_tile)


def term_rows(row):
    width = row.shape[1]
    at = lax.broadcasted_iota(jnp.int32, (16, width), 0)
    block = jnp.zeros((16, width), F32)
    rest = row
    for k in range(3):
        term = rest.astype(BF16).astype(F32)
        rest = rest - term
        block = jnp.where(at == k, term, block)
    return block.astype(BF16)


def put_terms(message, tile):
    frames = tile.shape[0]
    rows = tile.T
    for h in range(message.shape[1] // HDIM):
        message[frames : frames + 16, head_cols(h)] = term_rows(rows[h : h + 1, :])


def terms_of(message, frames, cols):
    terms = message[frames : frames + 16, cols].astype(F32)
    return terms[0:1] + terms[1:2] + terms[2:3]


def hidden_body(flags, inputs, keep, core, across, cot, seen_a, seen_b, hidden, rims):
    frames, width = inputs.shape
    mine = slice(width, 2 * width)
    total = inputs[...].astype(F32) + keep[:, mine].astype(F32) + core[:, mine].astype(F32)
    hidden[...] = (total + across[...].astype(F32)).astype(BF16)
    wide = 2 * HALO
    rims[0:wide, :] = hidden[0:wide, :]
    rims[wide : 2 * wide, :] = hidden[frames - wide : frames, :]
    rims[2 * wide : 2 * wide + HALO, :] = cot[0:HALO, :]
    rims[2 * wide + HALO : 3 * wide, :] = cot[frames - HALO : frames, :]


def shifted_sum(load, taps_of, rows):
    total = None
    for b in range(8):
        part = None
        reach = rows if b == 0 else rows + 8
        for a in range(4):
            tap = taps_of(8 * a + b)
            if tap is None:
                continue
            term = tap * load(8 * a, reach)
            part = term if part is None else part + term
        if b:
            part = pltpu.roll(part, reach - b, 0)[0:rows]
        total = part if total is None else total + part
    return total


def silu_parts(conv, cots):
    gate = 1.0 / (1.0 + jnp.exp(-conv))
    grad = cots * (gate + conv * gate * (1.0 - gate))
    return conv * gate, grad.astype(BF16).astype(F32)


def taps_forward(taps, cols):
    count = taps.shape[0]
    return lambda s: taps[s - 1 : s, cols] if 1 <= s <= count else None


def taps_backward(taps, cols):
    count = taps.shape[0]
    return lambda s: taps[count - s : count - s + 1, cols] if 1 <= s <= count else None


def conv_inner_body(hidden, cot, taps, rows_out, edge_conv, part_grad, padded, grads):
    frames, width = hidden.shape
    wide = 2 * HALO
    padded[0:wide, :] = jnp.zeros((wide, width), F32)
    padded[wide : wide + frames, :] = hidden[...].astype(F32)
    padded[wide + frames : 2 * wide + frames, :] = jnp.zeros((wide, width), F32)
    grads[0:wide, :] = jnp.zeros((wide, width), F32)
    grads[frames : frames + wide, :] = jnp.zeros((wide, width), F32)
    inner = slice(HALO, frames - HALO)
    for c in range(0, width, 128):
        cols = slice(c, c + 128)
        conv = shifted_sum(
            lambda at, rows: padded[at : at + rows, cols], taps_forward(taps, cols), frames + wide
        )
        edge_conv[0:wide, cols] = conv[0:wide]
        edge_conv[wide : 2 * wide, cols] = conv[frames : frames + wide]
        cots = cot[:, cols].astype(F32)
        silu, grad = silu_parts(conv[wide:frames], cots[inner])
        rows_out[inner, cols] = (hidden[inner, cols].astype(F32) + silu).astype(BF16)
        grads[wide:frames, cols] = grad
        back = shifted_sum(
            lambda at, rows: grads[at : at + rows, cols], taps_backward(taps, cols), frames
        )
        part_grad[:, cols] = cots + back


def conv_edge_body(
    flags, hidden, rim_near, rim_first, cot, taps, rows_in, edge_conv, part_grad,
    output, grad_input, grad_copy, padded, grads,
):
    frames, width = hidden.shape
    wide = 2 * HALO
    even = flags[0] > 0
    have = jnp.where(flags[2] > 0, jnp.float32(1.0), jnp.float32(0.0))
    low_ok = jnp.where(even, have, jnp.float32(1.0))
    high_ok = jnp.where(even, jnp.float32(1.0), have)

    def low_of(rows):
        return jnp.where(even, rim_first[rows, :].astype(F32), rim_near[rows, :].astype(F32)) * low_ok

    def high_of(rows):
        return jnp.where(even, rim_near[rows, :].astype(F32), rim_first[rows, :].astype(F32)) * high_ok

    padded[0:wide, :] = low_of(slice(wide, 2 * wide))
    padded[wide : 2 * wide, :] = jnp.zeros((wide, width), F32)
    padded[2 * wide : 3 * wide, :] = high_of(slice(0, wide))
    grads[wide : 2 * wide, :] = jnp.zeros((wide, width), F32)
    cot_low = low_of(slice(2 * wide + HALO, 3 * wide))
    cot_high = high_of(slice(2 * wide, 2 * wide + HALO))
    low, high = slice(0, HALO), slice(frames - HALO, frames)
    inner = slice(HALO, frames - HALO)
    output[inner, :] = rows_in[inner, :]
    for c in range(0, width, 128):
        cols = slice(c, c + 128)
        conv = edge_conv[:, cols] + shifted_sum(
            lambda at, rows: padded[at : at + rows, cols], taps_forward(taps, cols), 2 * wide
        )
        cots = jnp.concatenate(
            [cot_low[:, cols], cot[low, cols].astype(F32), cot[high, cols].astype(F32), cot_high[:, cols]],
            axis=0,
        )
        silu, grad = silu_parts(conv, cots)
        output[low, cols] = (hidden[low, cols].astype(F32) + silu[HALO:wide]).astype(BF16)
        output[high, cols] = (hidden[high, cols].astype(F32) + silu[wide : wide + HALO]).astype(BF16)
        grads[0:wide, cols] = grad[0:wide]
        grads[2 * wide : 3 * wide, cols] = grad[wide : 2 * wide]
        back = shifted_sum(
            lambda at, rows: grads[at : at + rows, cols], taps_backward(taps, cols), 2 * wide
        )
        part = part_grad[:, cols]
        total = jnp.concatenate(
            [part[0:wide] + back[0:wide], part[wide : frames - wide], part[frames - wide :] + back[wide:]],
            axis=0,
        ).astype(BF16)
        grad_input[:, cols] = total
        grad_copy[:, cols] = total


def upstream_body(flags, own, core, across, cross, weight, att, seen_a, seen_b, message, delta):
    frames, width = own.shape
    place = flags[3]
    total = None
    for flip, block in ((0, own), (1, core), (2, across), (3, cross)):
        at = pl.ds(pl.multiple_of((place ^ flip) * width, 128), width)
        part = dot_nt(block[...], weight[:, at])
        total = part if total is None else total + part
    up = total.astype(BF16)
    message[0:frames, :] = up
    lane = lax.broadcasted_iota(jnp.int32, (frames, HDIM), 1)
    tile = jnp.zeros((frames, HDIM), F32)
    for h in range(width // HDIM):
        cols = head_cols(h)
        product = up[:, cols].astype(F32) * att[:, cols].astype(F32)
        tile = jnp.where(lane == h, jnp.sum(product, axis=1, keepdims=True), tile)
    delta[...] = tile
    put_terms(message, tile)


def query_grad_body(scale, flags, q, own, near, first, second, relay, message, lse, delta, grad_query):
    frames, width = q.shape
    kvs = (near, relay, own, first, second)
    biases = (off_bias(flags[1]), off_bias(flags[2]))
    for h in range(width // HDIM):
        cols = head_cols(h)
        keys = stacked(kvs, slice(0, frames), cols)
        scores = dot_nt(q[:, cols], keys) * scale - lse[:, h : h + 1]
        scores = jnp.concatenate(
            [scores[:, 0:frames] + biases[0], scores[:, frames : 2 * frames] + biases[1]]
            + [scores[:, 2 * frames :]],
            axis=1,
        )
        dots = dot_nt(message[0:frames, cols], stacked(kvs, slice(frames, 2 * frames), cols))
        grads = (jnp.exp(scores) * (dots - delta[:, h : h + 1]) * scale).astype(BF16)
        grad_query[:, cols] = dot_nn(grads, keys).astype(BF16)


def key_terms(scale, own, queries, messages, biases, cols):
    frames = own.shape[0] // 2
    asks = stacked(queries, slice(0, frames), cols)
    ups = stacked(messages, slice(0, frames), cols)
    scores = dot_nt(own[0:frames, cols], asks) * scale
    dots = dot_nt(own[frames : 2 * frames, cols], ups)
    probs_low, grads = [], []
    for b, bias in enumerate(biases):
        at = slice(b * frames, (b + 1) * frames)
        part = scores[:, at] - terms_of(queries[b], frames, cols)
        probs = jnp.exp(part if bias is None else part + bias)
        probs_low.append(probs.astype(BF16))
        grads.append((probs * (dots[:, at] - terms_of(messages[b], frames, cols)) * scale).astype(BF16))
    key_part = dot_nn(jnp.concatenate(grads, axis=1), asks)
    return key_part, dot_nn(jnp.concatenate(probs_low, axis=1), ups)


def key_part_body(scale, flags, own, *refs):
    queries, messages, (key_part, value_part) = refs[0:4], refs[4:8], refs[8:10]
    biases = (None, off_bias(flags[1]), None, None)
    for h in range(own.shape[1] // HDIM):
        cols = head_cols(h)
        key_part[:, cols], value_part[:, cols] = key_terms(scale, own, queries, messages, biases, cols)


def key_grad_body(scale, flags, own, query, message, key_part, value_part, grad_key, grad_value):
    biases = (off_bias(flags[2]),)
    for h in range(own.shape[1] // HDIM):
        cols = head_cols(h)
        keys, values = key_terms(scale, own, (query,), (message,), biases, cols)
        grad_key[:, cols] = (key_part[:, cols] + keys).astype(BF16)
        grad_value[:, cols] = (value_part[:, cols] + values).astype(BF16)


def per_device(query_rows, key_rows, value_rows, inputs, out_weight, kernel, cotangent):
    frames, width = query_rows.shape
    whole = out_weight.shape[1]
    wide = 2 * HALO
    scale = 1.0 / math.sqrt(HDIM)
    block, count = lax.axis_index("ctx"), lax.axis_size("ctx")
    even = block % 2 == 0
    lower, upper = block >= 2, block < count - 2
    flags = jnp.stack(
        [even, lower & upper, jnp.where(even, lower, upper), lax.axis_index("mp")]
    ).astype(jnp.int32)
    tile = shaped((frames, width), BF16)
    tile32 = shaped((frames, width), F32)
    half = shaped((frames, 2 * width), BF16)
    side = shaped((frames, HDIM), F32)
    noted = shaped((frames + 16, width), BF16)
    square = frames * frames * width

    (kv,) = kernel_call(
        pack_body, (shaped((2 * frames, width), BF16),), (key_rows, value_rows), 0, "pack",
        [HBM] * 2, [pltpu.SemaphoreType.DMA((2,))], 60, HBM,
    )
    near, first, second, relay = window_of(kv)
    (weight,) = kernel_call(
        fetch_body, (shaped(out_weight.shape, BF16),), (out_weight, second), 0, "fetch",
        [HBM, ANY], [pltpu.SemaphoreType.DMA(())],
    )
    sums, tops, totals = kernel_call(
        functools.partial(forward_body, scale),
        (tile32, side, side),
        (flags, query_rows, kv, near, first, second),
        16 * square, "forward",
    )
    att, lse, send, keep, q_own = kernel_call(
        functools.partial(project_body, scale),
        (tile, side, half, half, noted),
        (flags, query_rows, relay, sums, tops, totals, weight),
        4 * square + 2 * frames * width * whole, "project",
    )

    core = pair_swap(send, "mp", 1)
    across = pair_swap(keep[:, 0:width] + core[:, 0:width], "mp", 2)
    q_second = ring(q_own, 1)
    q_first = ring(q_own, 0)
    hidden, rims = kernel_call(
        hidden_body,
        (tile, shaped((3 * wide, width), BF16)),
        (flags, inputs, keep, core, across, cotangent, q_second, q_first),
        4 * frames * width, "hidden", [SMEM] + [VMEM] * 5 + [ANY] * 2,
    )

    rim_near = pair_swap(rims, "ctx", 1)
    rows_out, edge_conv, part_grad = kernel_call(
        conv_inner_body,
        (tile, shaped((2 * wide, width), F32), tile32),
        (hidden, cotangent, kernel),
        140 * frames * width, "conv_inner", [VMEM] * 3,
        [pltpu.VMEM((frames + 2 * wide, width), F32), pltpu.VMEM((frames + wide, width), F32)],
    )
    rim_first = ring(rim_near, 0)
    output, grad_input, grad_copy = kernel_call(
        conv_edge_body,
        (tile, tile, tile),
        (flags, hidden, rim_near, rim_first, cotangent, kernel, rows_out, edge_conv, part_grad),
        70 * frames * width, "conv_edge", None,
        [pltpu.VMEM((3 * wide, width), F32), pltpu.VMEM((3 * wide, width), F32)],
    )

    gi_across = pair_swap(grad_copy, "mp", 2)
    gi_core = pair_swap(grad_copy, "mp", 1)
    q_near = inner_swap(q_own)
    q_relay = pair_swap(q_second, "ctx", 1)
    gi_cross = pair_swap(gi_across, "mp", 1)
    message, delta = kernel_call(
        upstream_body,
        (noted, side),
        (flags, grad_copy, gi_core, gi_across, gi_cross, weight, att, q_near, q_relay),
        2 * frames * width * whole, "upstream", [SMEM] + [VMEM] * 6 + [ANY] * 2,
    )

    m_near, m_first, m_second, m_relay = window_of(message)
    (grad_query,) = kernel_call(
        functools.partial(query_grad_body, scale),
        (tile,),
        (flags, query_rows, kv, near, first, second, relay, message, lse, delta),
        30 * square, "query_grad",
    )
    key_part, value_part = kernel_call(
        functools.partial(key_part_body, scale),
        (tile32, tile32),
        (flags, kv, q_own, q_near, q_first, q_second, message, m_near, m_first, m_second),
        32 * square, "key_part",
    )
    grad_key, grad_value = kernel_call(
        functools.partial(key_grad_body, scale),
        (tile, tile),
        (flags, kv, q_relay, m_relay, key_part, value_part),
        8 * square, "key_grad",
    )
    return (output, grad_input, grad_query, grad_key, grad_value)


def solution(mesh):
    rows = P("ctx", "mp")
    return jax.shard_map(
        per_device,
        mesh=mesh,
        in_specs=(rows, rows, rows, rows, P("mp", None), P(None, "mp"), rows),
        out_specs=(rows,) * 5,
        check_vma=False,
    )
```

time: 83.2 us -> 76 us (0.913)
  waiting for transfers between devices: 42.8 us -> 16.6 us
  Pallas kernels: 12.6 us -> 25.3 us
  starting transfers between devices: 21.5 us -> 30.9 us
  local copies, waits for them, and re-layouts: 5.29 us -> 2.09 us
    ppermute x12 -> x9, waiting for transfers between devices: 29.7 us -> 8.67 us  [pair_swap(): lax.ppermute(block, axis, [(i, i ^ bit) for i in range(lax.axis_size(axis...]
    pallas_call x6 -> x11, Pallas kernels: 12.6 us -> 25.3 us  [kernel_call(): pl.pallas_call(body, out_shape=outs, in_specs=spaces or [SMEM] + [VMEM] *...]
    ppermute x7, starting transfers between devices: 8.46 us -> 20.5 us  [ring(): return lax.ppermute(block, 'ctx', ring_routes(lax.axis_size('ctx'))[way])]
    ppermute x7, waiting for transfers between devices: 13.2 us -> 7.89 us  [ring(): return lax.ppermute(block, 'ctx', ring_routes(lax.axis_size('ctx'))[way])]
    ppermute x12 -> x9, starting transfers between devices: 13.1 us -> 8.45 us  [pair_swap(): lax.ppermute(block, axis, [(i, i ^ bit) for i in range(lax.axis_size(axis...]
    unnamed x17 -> x12, local copies, waits for them, and re-layouts: 4.34 us -> 2.09 us
    ppermute x0 -> x3, starting transfers between devices: none -> 1.98 us  [inner_swap(): lax.ppermute(block, 'ctx', [(i, i ^ 1) for i in range(2, lax.axis_size('c...]
    concatenate x1 -> x0, local copies, waits for them, and re-layouts: 0.96 us -> none  [per_device(): kv = jnp.concatenate([key_rows, value_rows], axis=0)]
  transfers between devices with their start and end apart: 19 -> 19, of which waited for: 13 -> 11; matrix products, arithmetic and copies ran while one was open for 0% -> 0% of each run, Pallas kernels for 6% -> 10%
where the time goes in v2:
time: 76 us; the launch traced here: 75.7 us
  starting transfers between devices  30.9 us (41%)
  Pallas kernels  25.3 us (33%)
  waiting for transfers between devices  16.6 us (22%)
  local copies, waits for them, and re-layouts  2.09 us (3%)
  between operations  0.77 us (1%)
    pallas_call x11, Pallas kernels, kernel_call(): pl.pallas_call(body, out_shape=outs, in_specs=spaces or [SMEM] + [VMEM] *...  25.3 us
    ppermute x7, starting transfers between devices, ring(): return lax.ppermute(block, 'ctx', ring_routes(lax.axis_size('ctx'))[way])  20.5 us
    ppermute x9, waiting for transfers between devices, pair_swap(): lax.ppermute(block, axis, [(i, i ^ bit) for i in range(lax.axis_size(axis...  8.67 us
    ppermute x9, starting transfers between devices, pair_swap(): lax.ppermute(block, axis, [(i, i ^ bit) for i in range(lax.axis_size(axis...  8.45 us
    ppermute x7, waiting for transfers between devices, ring(): return lax.ppermute(block, 'ctx', ring_routes(lax.axis_size('ctx'))[way])  7.89 us
    unnamed x12, local copies, waits for them, and re-layouts  2.09 us
    ppermute x3, starting transfers between devices, inner_swap(): lax.ppermute(block, 'ctx', [(i, i ^ 1) for i in range(2, lax.axis_size('c...  1.98 us
  transfers between devices with their start and end apart: 19, of which 11 were waited for; matrix products, arithmetic and copies ran while one was open for 0% of the time, Pallas kernels for 10%

profile of v2, /device:TPU:0, one launch (start us, length us, event | category | flops | bytes accessed | tf_op | source)
XLA Modules:
  0.0 75.7 jit_solution(2096204383446256897)
XLA Ops:
  0.6 9.1 %pack.1.own = bf16[256,512]{1,0:T(8,128)(2,1)} custom-call(bf16[128,512]{1,0:T(8,128)(2,1)} %key.1, bf16[128,512]{1,0:T(8,128)(2,1)} %value.1), custom_call_target="tpu_custom_call" | custom-call | bytes 524288 | tf_op jit(solution)/shard_map/pack/pallas_call | solution.py:61
  9.7 3.0 %collective-permute-start = (bf16[256,512]{1,0:T(8,128)(2,1)}, bf16[256,512]{1,0:T(8,128)(2,1)S(1)}, u32[]{:S(2)}, u32[]{:S(2)}) collective-permute-start(bf16[256,512]{1,0:T(8,128)(2,1)} %pack.1.own), channel_id=1, source_target_pairs={{8,0},{16,8},{24,16},{28,24},{20,28},{12,20},{4,12},{0,4},{9,1},{1... | collective-permute-start | bytes 786440 | tf_op jit(solution)/shard_map/ppermute | solution.py:39
  12.7 0.7 collective-permute-start.2
  13.4 4.4 %collective-permute-start.3 = (bf16[256,512]{1,0:T(8,128)(2,1)}, bf16[256,512]{1,0:T(8,128)(2,1)S(1)}, u32[]{:S(2)}, u32[]{:S(2)}) collective-permute-start(bf16[256,512]{1,0:T(8,128)(2,1)} %pack.1.own), channel_id=1, source_target_pairs={{0,8},{8,16},{16,24},{24,28},{28,20},{20,12},{12,4},{4,0},{1,9},{9... | collective-permute-start | bytes 786440 | tf_op jit(solution)/shard_map/ppermute | solution.py:39
  17.8 1.5 %collective-permute-done.second.seen = bf16[256,512]{1,0:T(8,128)(2,1)S(1)} collective-permute-done((bf16[256,512]{1,0:T(8,128)(2,1)}, bf16[256,512]{1,0:T(8,128)(2,1)S(1)}, u32[]{:S(2)}, u32[]{:S(2)}) %collective-permute-start) | collective-permute-done | bytes 262176 | tf_op jit(solution)/shard_map/ppermute | solution.py:39
  19.3 1.7 %collective-permute-start.1 = (bf16[256,512]{1,0:T(8,128)(2,1)S(1)}, bf16[256,512]{1,0:T(8,128)(2,1)S(1)}, u32[]{:S(2)}, u32[]{:S(2)}) collective-permute-start(bf16[256,512]{1,0:T(8,128)(2,1)S(1)} %collective-permute-done.second.seen), channel_id=1, source_target_pairs={{0,4},{4,0},{8,12},{12,8},{16,20},{20,16},{24,28},{28,24},{1,5},{5... | collective-permute-start | bytes 786440 | tf_op jit(solution)/shard_map/ppermute | solution.py:28
  20.9 0.1 pad_add_fusion.flags
  21.0 0.0 copy-start.1
  21.0 1.6 %copy-done.1 = bf16[512,2048]{1,0:T(8,128)(2,1)S(1)} copy-done((bf16[512,2048]{1,0:T(8,128)(2,1)S(1)}, bf16[512,2048]{1,0:T(8,128)(2,1)}, u32[]{:S(2)}) %copy-start.1) | copy-done | bytes 2097176
  22.6 0.0 copy-start
  22.6 0.0 copy-start.2
  22.6 0.1 fetch.1.weight
  22.8 0.0 copy-start.3
  22.8 0.0 copy-start.5
  22.8 0.0 collective-permute-done.2.near
  22.8 0.3 collective-permute-done.3.first
  23.1 0.4 copy-done
  23.6 0.0 copy-done.2
  23.6 1.7 %forward.1 = (f32[128,512]{1,0:T(8,128)S(1)}, f32[128,128]{1,0:T(8,128)S(1)}, f32[128,128]{1,0:T(8,128)S(1)}) custom-call(s32[4]{0:T(128)S(1)} %pad_add_fusion.flags, bf16[128,512]{1,0:T(8,128)(2,1)S(1)} %copy-done.2, bf16[256,512]{1,0:T(8,128)(2,1)S(1)} %copy-done, bf16[256,512]{1,0:T(8,128)(2,1)S(1)} %collective-permute-done.2.near, ...), custom_call_target="tpu_custom_call" | custom-call | flops 134217728 | bytes 1572880 | tf_op jit(solution)/shard_map/forward/pallas_call | solution.py:61
  25.3 1.7 %collective-permute-done.1.relay = bf16[256,512]{1,0:T(8,128)(2,1)S(1)} collective-permute-done((bf16[256,512]{1,0:T(8,128)(2,1)S(1)}, bf16[256,512]{1,0:T(8,128)(2,1)S(1)}, u32[]{:S(2)}, u32[]{:S(2)}) %collective-permute-start.1) | collective-permute-done | bytes 262176 | tf_op jit(solution)/shard_map/ppermute | solution.py:28
  27.0 0.0 copy-start.4
  27.0 2.5 %project.1 = (bf16[128,512]{1,0:T(8,128)(2,1)S(1)}, f32[128,128]{1,0:T(8,128)S(1)}, bf16[128,1024]{1,0:T(8,128)(2,1)S(1)}, bf16[128,1024]{1,0:T(8,128)(2,1)S(1)}, bf16[144,512]{1,0:T(8,128)(2,1)S(1)}) custom-call(s32[4]{0:T(128)S(1)} %pad_add_fusion.flags, bf16[128,512]{1,0:T(8,128)(2,1)S(1)} %copy-done.2, ...), custom_call_target="tpu_custom_call" | custom-call | flops 301989888 | bytes 3751952 | tf_op jit(solution)/shard_map/project/pallas_call | solution.py:61
  29.5 0.1 collective-permute-start.4
  29.6 1.2 %collective-permute-start.6 = (bf16[144,512]{1,0:T(8,128)(2,1)S(1)}, bf16[144,512]{1,0:T(8,128)(2,1)S(1)}, u32[]{:S(2)}, u32[]{:S(2)}) collective-permute-start(bf16[144,512]{1,0:T(8,128)(2,1)S(1)} %get-tuple-element.32.refs_0_), channel_id=1, source_target_pairs={{8,0},{16,8},{24,16},{28,24},{20,28},{12,20},{4,12},{0,4},{9,1},{1... | collective-permute-start | bytes 442376 | tf_op jit(solution)/shard_map/ppermute | solution.py:39
  30.8 1.5 %collective-permute-start.7 = (bf16[144,512]{1,0:T(8,128)(2,1)S(1)}, bf16[144,512]{1,0:T(8,128)(2,1)S(1)}, u32[]{:S(2)}, u32[]{:S(2)}) collective-permute-start(bf16[144,512]{1,0:T(8,128)(2,1)S(1)} %get-tuple-element.32.refs_0_), channel_id=1, source_target_pairs={{0,8},{8,16},{16,24},{24,28},{28,20},{20,12},{12,4},{4,0},{1,9},{9... | collective-permute-start | bytes 442376 | tf_op jit(solution)/shard_map/ppermute | solution.py:39
  32.3 0.0 collective-permute-done.4.core
  32.4 1.6 %collective-permute-start.5 = (bf16[128,512]{1,0:T(8,128)(2,1)S(1)}, bf16[128,512]{1,0:T(8,128)(2,1)S(1)}, u32[]{:S(2)}, u32[]{:S(2)}) collective-permute-start(bf16[128,512]{1,0:T(8,128)(2,1)S(1)} %slice_add_fusion), channel_id=1, source_target_pairs={{0,2},{1,3},{2,0},{3,1},{4,6},{5,7},{6,4},{7,5},{8,10},{9,11},{10,... | collective-permute-start | bytes 393224 | tf_op jit(solution)/shard_map/ppermute | solution.py:28
  34.0 2.8 %collective-permute-done.6.seen_a.refs_3_ = bf16[144,512]{1,0:T(8,128)(2,1)S(1)} collective-permute-done((bf16[144,512]{1,0:T(8,128)(2,1)S(1)}, bf16[144,512]{1,0:T(8,128)(2,1)S(1)}, u32[]{:S(2)}, u32[]{:S(2)}) %collective-permute-start.6) | collective-permute-done | bytes 147488 | tf_op jit(solution)/shard_map/ppermute | solution.py:39
  36.7 1.5 %collective-permute-done.7.seen_b.refs_2_ = bf16[144,512]{1,0:T(8,128)(2,1)S(1)} collective-permute-done((bf16[144,512]{1,0:T(8,128)(2,1)S(1)}, bf16[144,512]{1,0:T(8,128)(2,1)S(1)}, u32[]{:S(2)}, u32[]{:S(2)}) %collective-permute-start.7) | collective-permute-done | bytes 147488 | tf_op jit(solution)/shard_map/ppermute | solution.py:39
  38.2 0.0 collective-permute-done.5.across
  38.2 0.0 copy-done.3
  38.2 0.0 copy-done.5
  38.2 0.6 hidden.1
  38.8 1.8 %collective-permute-start.8 = (bf16[96,512]{1,0:T(8,128)(2,1)S(1)}, bf16[96,512]{1,0:T(8,128)(2,1)S(1)}, u32[]{:S(2)}, u32[]{:S(2)}) collective-permute-start(bf16[96,512]{1,0:T(8,128)(2,1)S(1)} %get-tuple-element.34), channel_id=1, source_target_pairs={{0,4},{4,0},{8,12},{12,8},{16,20},{20,16},{24,28},{28,24},{1,5},{5... | collective-permute-start | bytes 294920 | tf_op jit(solution)/shard_map/ppermute | solution.py:28
  40.6 2.9 %collective-permute-done.8.rim_near = bf16[96,512]{1,0:T(8,128)(2,1)S(1)} collective-permute-done((bf16[96,512]{1,0:T(8,128)(2,1)S(1)}, bf16[96,512]{1,0:T(8,128)(2,1)S(1)}, u32[]{:S(2)}, u32[]{:S(2)}) %collective-permute-start.8) | collective-permute-done | bytes 98336 | tf_op jit(solution)/shard_map/ppermute | solution.py:28
  43.5 1.5 %collective-permute-start.9 = (bf16[96,512]{1,0:T(8,128)(2,1)S(1)}, bf16[96,512]{1,0:T(8,128)(2,1)S(1)}, u32[]{:S(2)}, u32[]{:S(2)}) collective-permute-start(bf16[96,512]{1,0:T(8,128)(2,1)S(1)} %collective-permute-done.8.rim_near), channel_id=1, source_target_pairs={{0,8},{8,16},{16,24},{24,28},{28,20},{20,12},{12,4},{4,0},{1,9},{9... | collective-permute-start | bytes 294920 | tf_op jit(solution)/shard_map/ppermute | solution.py:39
  45.0 0.0 copy-done.4
  45.0 1.6 %conv_inner.1 = (bf16[128,512]{1,0:T(8,128)(2,1)S(1)}, f32[64,512]{1,0:T(8,128)S(1)}, f32[128,512]{1,0:T(8,128)S(1)}) custom-call(bf16[128,512]{1,0:T(8,128)(2,1)S(1)} %get-tuple-element.33.hidden, bf16[128,512]{1,0:T(8,128)(2,1)S(1)} %copy-done.3, f32[31,512]{1,0:T(8,128)S(1)} %copy-done.4), custom_call_target="tpu_custom_call" | custom-call | flops 9175040 | bytes 849920 | tf_op jit(solution)/shard_map/conv_inner/pallas_call | solution.py:61
  46.6 1.5 %collective-permute-done.9.rim_first = bf16[96,512]{1,0:T(8,128)(2,1)S(1)} collective-permute-done((bf16[96,512]{1,0:T(8,128)(2,1)S(1)}, bf16[96,512]{1,0:T(8,128)(2,1)S(1)}, u32[]{:S(2)}, u32[]{:S(2)}) %collective-permute-start.9) | collective-permute-done | bytes 98336 | tf_op jit(solution)/shard_map/ppermute | solution.py:39
  48.1 1.9 %conv_edge.1 = (bf16[128,512]{1,0:T(8,128)(2,1)}, bf16[128,512]{1,0:T(8,128)(2,1)}, bf16[128,512]{1,0:T(8,128)(2,1)S(1)}) custom-call(s32[4]{0:T(128)S(1)} %pad_add_fusion.flags, bf16[128,512]{1,0:T(8,128)(2,1)S(1)} %get-tuple-element.33.hidden, bf16[96,512]{1,0:T(8,128)(2,1)S(1)} %collective-permute-done.8.rim_near, ...), custom_call_target="tpu_custom_call" | custom-call | flops 4587520 | bytes 1439760 | tf_op jit(solution)/shard_map/conv_edge/pallas_call | solution.py:61
  50.1 1.5 %collective-permute-start.11 = (bf16[128,512]{1,0:T(8,128)(2,1)S(1)}, bf16[128,512]{1,0:T(8,128)(2,1)S(1)}, u32[]{:S(2)}, u32[]{:S(2)}) collective-permute-start(bf16[128,512]{1,0:T(8,128)(2,1)S(1)} %get-tuple-element.40.own), channel_id=1, source_target_pairs={{0,2},{1,3},{2,0},{3,1},{4,6},{5,7},{6,4},{7,5},{8,10},{9,11},{10,... | collective-permute-start | bytes 393224 | tf_op jit(solution)/shard_map/ppermute | solution.py:28
  51.6 0.7 collective-permute-start.13
  52.2 1.8 %collective-permute-start.14 = (bf16[144,512]{1,0:T(8,128)(2,1)S(1)}, bf16[144,512]{1,0:T(8,128)(2,1)S(1)}, u32[]{:S(2)}, u32[]{:S(2)}) collective-permute-start(bf16[144,512]{1,0:T(8,128)(2,1)S(1)} %collective-permute-done.6.seen_a.refs_3_), channel_id=1, source_target_pairs={{0,4},{4,0},{8,12},{12,8},{16,20},{20,16},{24,28},{28,24},{1,5},{5... | collective-permute-start | bytes 442376 | tf_op jit(solution)/shard_map/ppermute | solution.py:28
  54.1 0.0 collective-permute-start.10
  54.1 1.0 %collective-permute-done.11.across = bf16[128,512]{1,0:T(8,128)(2,1)S(1)} collective-permute-done((bf16[128,512]{1,0:T(8,128)(2,1)S(1)}, bf16[128,512]{1,0:T(8,128)(2,1)S(1)}, u32[]{:S(2)}, u32[]{:S(2)}) %collective-permute-start.11) | collective-permute-done | bytes 131104 | tf_op jit(solution)/shard_map/ppermute | solution.py:28
  55.0 0.0 collective-permute-start.12
  55.0 0.0 collective-permute-done.13.seen_a.refs_1_
  55.0 2.4 %collective-permute-done.14.seen_b.query = bf16[144,512]{1,0:T(8,128)(2,1)S(1)} collective-permute-done((bf16[144,512]{1,0:T(8,128)(2,1)S(1)}, bf16[144,512]{1,0:T(8,128)(2,1)S(1)}, u32[]{:S(2)}, u32[]{:S(2)}) %collective-permute-start.14) | collective-permute-done | bytes 147488 | tf_op jit(solution)/shard_map/ppermute | solution.py:28
  57.5 0.0 collective-permute-done.10.core
  57.5 0.0 collective-permute-done.12.cross
  57.5 1.5 %upstream.1 = (bf16[144,512]{1,0:T(8,128)(2,1)S(1)}, f32[128,128]{1,0:T(8,128)S(1)}) custom-call(s32[4]{0:T(128)S(1)} %pad_add_fusion.flags, bf16[128,512]{1,0:T(8,128)(2,1)S(1)} %get-tuple-element.40.own, bf16[128,512]{1,0:T(8,128)(2,1)S(1)} %collective-permute-done.10.core, bf16[128,512]{1,0:T(8,128)(2,1)S(1)} %collective-permute-done.11.across, ...), custom_call_target="tpu_custom_call" | custom-call | flops 268435456 | bytes 3260432 | tf_op jit(solution)/shard_map/upstream/pallas_call | solution.py:61
  59.0 1.8 %collective-permute-start.15 = (bf16[144,512]{1,0:T(8,128)(2,1)S(1)}, bf16[144,512]{1,0:T(8,128)(2,1)S(1)}, u32[]{:S(2)}, u32[]{:S(2)}) collective-permute-start(bf16[144,512]{1,0:T(8,128)(2,1)S(1)} %get-tuple-element.42.message.refs_4_), channel_id=1, source_target_pairs={{8,0},{16,8},{24,16},{28,24},{20,28},{12,20},{4,12},{0,4},{9,1},{1... | collective-permute-start | bytes 442376 | tf_op jit(solution)/shard_map/ppermute | solution.py:39
  60.8 0.7 collective-permute-start.17
  61.5 7.1 %collective-permute-start.18 = (bf16[144,512]{1,0:T(8,128)(2,1)S(1)}, bf16[144,512]{1,0:T(8,128)(2,1)S(1)}, u32[]{:S(2)}, u32[]{:S(2)}) collective-permute-start(bf16[144,512]{1,0:T(8,128)(2,1)S(1)} %get-tuple-element.42.message.refs_4_), channel_id=1, source_target_pairs={{0,8},{8,16},{16,24},{24,28},{28,20},{20,12},{12,4},{4,0},{1,9},{9... | collective-permute-start | bytes 442376 | tf_op jit(solution)/shard_map/ppermute | solution.py:39
  68.5 0.0 collective-permute-done.15.refs_7_
  68.5 0.0 collective-permute-start.16
  68.5 2.3 %query_grad.1 = bf16[128,512]{1,0:T(8,128)(2,1)} custom-call(s32[4]{0:T(128)S(1)} %pad_add_fusion.flags, bf16[128,512]{1,0:T(8,128)(2,1)S(1)} %copy-done.2, bf16[256,512]{1,0:T(8,128)(2,1)S(1)} %copy-done, bf16[256,512]{1,0:T(8,128)(2,1)S(1)} %collective-permute-done.2.near, bf16[256,512]{1,0:T(8,128)(2,1)S(1)} %collective-permute-done.3.first, ...), custom_call_target="tpu_custom_call" | custom-call | flops 251658240 | bytes 1851408 | tf_op jit(solution)/shard_map/query_grad/pallas_call | solution.py:61
  70.9 0.0 collective-permute-done.17.refs_5_
  70.9 0.3 collective-permute-done.18.refs_6_
  71.2 1.7 %key_part.1 = (f32[128,512]{1,0:T(8,128)S(1)}, f32[128,512]{1,0:T(8,128)S(1)}) custom-call(s32[4]{0:T(128)S(1)} %pad_add_fusion.flags, bf16[256,512]{1,0:T(8,128)(2,1)S(1)} %copy-done, bf16[144,512]{1,0:T(8,128)(2,1)S(1)} %get-tuple-element.32.refs_0_, bf16[144,512]{1,0:T(8,128)(2,1)S(1)} %collective-permute-done.13.seen_a.refs_1_, ...), custom_call_target="tpu_custom_call" | custom-call | flops 268435456 | bytes 1966096 | tf_op jit(solution)/shard_map/key_part/pallas_call | solution.py:61
  72.9 0.7 collective-permute-done.16.message
  73.7 2.1 %key_grad.1 = (bf16[128,512]{1,0:T(8,128)(2,1)}, bf16[128,512]{1,0:T(8,128)(2,1)}) custom-call(s32[4]{0:T(128)S(1)} %pad_add_fusion.flags, bf16[256,512]{1,0:T(8,128)(2,1)S(1)} %copy-done, bf16[144,512]{1,0:T(8,128)(2,1)S(1)} %collective-permute-done.14.seen_b.query, bf16[144,512]{1,0:T(8,128)(2,1)S(1)} %collective-permute-done.16.message, ...), custom_call_target="tpu_custom_call" | custom-call | flops 67108864 | bytes 1343504 | tf_op jit(solution)/shard_map/key_grad/pallas_call | solution.py:61
  (1 shorter events, 0.0 us)
Async XLA Ops:
  9.7 9.6 %collective-permute-start = (bf16[256,512]{1,0:T(8,128)(2,1)}, bf16[256,512]{1,0:T(8,128)(2,1)S(1)}, u32[]{:S(2)}, u32[]{:S(2)}) collective-permute-start(bf16[256,512]{1,0:T(8,128)(2,1)} %pack.1.own), channel_id=1, source_target_pairs={{8,0},{16,8},{24,16},{28,24},{20,28},{12,20},{4,12},{0,4},{9,1},{1... | collective-permute-start | bytes 786440 | tf_op jit(solution)/shard_map/ppermute | solution.py:39
  12.7 10.1 %collective-permute-start.2 = (bf16[256,512]{1,0:T(8,128)(2,1)}, bf16[256,512]{1,0:T(8,128)(2,1)S(1)}, u32[]{:S(2)}, u32[]{:S(2)}) collective-permute-start(bf16[256,512]{1,0:T(8,128)(2,1)} %pack.1.own), channel_id=1, source_target_pairs={{8,12},{12,8},{16,20},{20,16},{9,13},{13,9},{17,21},{21,17},{10,14... | collective-permute-start | bytes 786440 | tf_op jit(solution)/shard_map/ppermute | solution.py:43
  13.4 9.8 %collective-permute-start.3 = (bf16[256,512]{1,0:T(8,128)(2,1)}, bf16[256,512]{1,0:T(8,128)(2,1)S(1)}, u32[]{:S(2)}, u32[]{:S(2)}) collective-permute-start(bf16[256,512]{1,0:T(8,128)(2,1)} %pack.1.own), channel_id=1, source_target_pairs={{0,8},{8,16},{16,24},{24,28},{28,20},{20,12},{12,4},{4,0},{1,9},{9... | collective-permute-start | bytes 786440 | tf_op jit(solution)/shard_map/ppermute | solution.py:39
  19.3 7.7 %collective-permute-start.1 = (bf16[256,512]{1,0:T(8,128)(2,1)S(1)}, bf16[256,512]{1,0:T(8,128)(2,1)S(1)}, u32[]{:S(2)}, u32[]{:S(2)}) collective-permute-start(bf16[256,512]{1,0:T(8,128)(2,1)S(1)} %collective-permute-done.second.seen), channel_id=1, source_target_pairs={{0,4},{4,0},{8,12},{12,8},{16,20},{20,16},{24,28},{28,24},{1,5},{5... | collective-permute-start | bytes 786440 | tf_op jit(solution)/shard_map/ppermute | solution.py:28
  21.0 1.6 %copy-start.1 = (bf16[512,2048]{1,0:T(8,128)(2,1)S(1)}, bf16[512,2048]{1,0:T(8,128)(2,1)}, u32[]{:S(2)}) copy-start(bf16[512,2048]{1,0:T(8,128)(2,1)} %weight.1) | copy-start | bytes 6291460
  22.6 0.9 %copy-start = (bf16[256,512]{1,0:T(8,128)(2,1)S(1)}, bf16[256,512]{1,0:T(8,128)(2,1)}, u32[]{:S(2)}) copy-start(bf16[256,512]{1,0:T(8,128)(2,1)} %pack.1.own) | copy-start | bytes 786436
  22.6 1.0 %copy-start.2 = (bf16[128,512]{1,0:T(8,128)(2,1)S(1)}, bf16[128,512]{1,0:T(8,128)(2,1)}, u32[]{:S(2)}) copy-start(bf16[128,512]{1,0:T(8,128)(2,1)} %q.5) | copy-start | bytes 393220
  22.8 15.4 %copy-start.3 = (bf16[128,512]{1,0:T(8,128)(2,1)S(1)}, bf16[128,512]{1,0:T(8,128)(2,1)}, u32[]{:S(2)}) copy-start(bf16[128,512]{1,0:T(8,128)(2,1)} %cot.5) | copy-start | bytes 393220
  22.8 15.4 %copy-start.5 = (bf16[128,512]{1,0:T(8,128)(2,1)S(1)}, bf16[128,512]{1,0:T(8,128)(2,1)}, u32[]{:S(2)}) copy-start(bf16[128,512]{1,0:T(8,128)(2,1)} %inputs.1) | copy-start | bytes 393220
  27.0 18.0 %copy-start.4 = (f32[31,512]{1,0:T(8,128)S(1)}, f32[31,512]{1,0:T(8,128)}, u32[]{:S(2)}) copy-start(f32[31,512]{1,0:T(8,128)} %taps.3) | copy-start | bytes 190468
  29.5 2.8 %collective-permute-start.4 = (bf16[128,1024]{1,0:T(8,128)(2,1)S(1)}, bf16[128,1024]{1,0:T(8,128)(2,1)S(1)}, u32[]{:S(2)}, u32[]{:S(2)}) collective-permute-start(bf16[128,1024]{1,0:T(8,128)(2,1)S(1)} %get-tuple-element.31), channel_id=1, source_target_pairs={{0,1},{1,0},{2,3},{3,2},{4,5},{5,4},{6,7},{7,6},{8,9},{9,8},{10,11... | collective-permute-start | bytes 786440 | tf_op jit(solution)/shard_map/ppermute | solution.py:28
  29.6 7.1 %collective-permute-start.6 = (bf16[144,512]{1,0:T(8,128)(2,1)S(1)}, bf16[144,512]{1,0:T(8,128)(2,1)S(1)}, u32[]{:S(2)}, u32[]{:S(2)}) collective-permute-start(bf16[144,512]{1,0:T(8,128)(2,1)S(1)} %get-tuple-element.32.refs_0_), channel_id=1, source_target_pairs={{8,0},{16,8},{24,16},{28,24},{20,28},{12,20},{4,12},{0,4},{9,1},{1... | collective-permute-start | bytes 442376 | tf_op jit(solution)/shard_map/ppermute | solution.py:39
  30.8 7.4 %collective-permute-start.7 = (bf16[144,512]{1,0:T(8,128)(2,1)S(1)}, bf16[144,512]{1,0:T(8,128)(2,1)S(1)}, u32[]{:S(2)}, u32[]{:S(2)}) collective-permute-start(bf16[144,512]{1,0:T(8,128)(2,1)S(1)} %get-tuple-element.32.refs_0_), channel_id=1, source_target_pairs={{0,8},{8,16},{16,24},{24,28},{28,20},{20,12},{12,4},{4,0},{1,9},{9... | collective-permute-start | bytes 442376 | tf_op jit(solution)/shard_map/ppermute | solution.py:39
  32.4 5.8 %collective-permute-start.5 = (bf16[128,512]{1,0:T(8,128)(2,1)S(1)}, bf16[128,512]{1,0:T(8,128)(2,1)S(1)}, u32[]{:S(2)}, u32[]{:S(2)}) collective-permute-start(bf16[128,512]{1,0:T(8,128)(2,1)S(1)} %slice_add_fusion), channel_id=1, source_target_pairs={{0,2},{1,3},{2,0},{3,1},{4,6},{5,7},{6,4},{7,5},{8,10},{9,11},{10,... | collective-permute-start | bytes 393224 | tf_op jit(solution)/shard_map/ppermute | solution.py:28
  38.8 4.7 %collective-permute-start.8 = (bf16[96,512]{1,0:T(8,128)(2,1)S(1)}, bf16[96,512]{1,0:T(8,128)(2,1)S(1)}, u32[]{:S(2)}, u32[]{:S(2)}) collective-permute-start(bf16[96,512]{1,0:T(8,128)(2,1)S(1)} %get-tuple-element.34), channel_id=1, source_target_pairs={{0,4},{4,0},{8,12},{12,8},{16,20},{20,16},{24,28},{28,24},{1,5},{5... | collective-permute-start | bytes 294920 | tf_op jit(solution)/shard_map/ppermute | solution.py:28
  43.5 4.6 %collective-permute-start.9 = (bf16[96,512]{1,0:T(8,128)(2,1)S(1)}, bf16[96,512]{1,0:T(8,128)(2,1)S(1)}, u32[]{:S(2)}, u32[]{:S(2)}) collective-permute-start(bf16[96,512]{1,0:T(8,128)(2,1)S(1)} %collective-permute-done.8.rim_near), channel_id=1, source_target_pairs={{0,8},{8,16},{16,24},{24,28},{28,20},{20,12},{12,4},{4,0},{1,9},{9... | collective-permute-start | bytes 294920 | tf_op jit(solution)/shard_map/ppermute | solution.py:39
  50.1 5.0 %collective-permute-start.11 = (bf16[128,512]{1,0:T(8,128)(2,1)S(1)}, bf16[128,512]{1,0:T(8,128)(2,1)S(1)}, u32[]{:S(2)}, u32[]{:S(2)}) collective-permute-start(bf16[128,512]{1,0:T(8,128)(2,1)S(1)} %get-tuple-element.40.own), channel_id=1, source_target_pairs={{0,2},{1,3},{2,0},{3,1},{4,6},{5,7},{6,4},{7,5},{8,10},{9,11},{10,... | collective-permute-start | bytes 393224 | tf_op jit(solution)/shard_map/ppermute | solution.py:28
  51.6 3.5 %collective-permute-start.13 = (bf16[144,512]{1,0:T(8,128)(2,1)S(1)}, bf16[144,512]{1,0:T(8,128)(2,1)S(1)}, u32[]{:S(2)}, u32[]{:S(2)}) collective-permute-start(bf16[144,512]{1,0:T(8,128)(2,1)S(1)} %get-tuple-element.32.refs_0_), channel_id=1, source_target_pairs={{8,12},{12,8},{16,20},{20,16},{9,13},{13,9},{17,21},{21,17},{10,14... | collective-permute-start | bytes 442376 | tf_op jit(solution)/shard_map/ppermute | solution.py:43
  52.2 5.2 %collective-permute-start.14 = (bf16[144,512]{1,0:T(8,128)(2,1)S(1)}, bf16[144,512]{1,0:T(8,128)(2,1)S(1)}, u32[]{:S(2)}, u32[]{:S(2)}) collective-permute-start(bf16[144,512]{1,0:T(8,128)(2,1)S(1)} %collective-permute-done.6.seen_a.refs_3_), channel_id=1, source_target_pairs={{0,4},{4,0},{8,12},{12,8},{16,20},{20,16},{24,28},{28,24},{1,5},{5... | collective-permute-start | bytes 442376 | tf_op jit(solution)/shard_map/ppermute | solution.py:28
  54.1 3.4 %collective-permute-start.10 = (bf16[128,512]{1,0:T(8,128)(2,1)S(1)}, bf16[128,512]{1,0:T(8,128)(2,1)S(1)}, u32[]{:S(2)}, u32[]{:S(2)}) collective-permute-start(bf16[128,512]{1,0:T(8,128)(2,1)S(1)} %get-tuple-element.40.own), channel_id=1, source_target_pairs={{0,1},{1,0},{2,3},{3,2},{4,5},{5,4},{6,7},{7,6},{8,9},{9,8},{10,11... | collective-permute-start | bytes 393224 | tf_op jit(solution)/shard_map/ppermute | solution.py:28
  55.0 2.4 %collective-permute-start.12 = (bf16[128,512]{1,0:T(8,128)(2,1)S(1)}, bf16[128,512]{1,0:T(8,128)(2,1)S(1)}, u32[]{:S(2)}, u32[]{:S(2)}) collective-permute-start(bf16[128,512]{1,0:T(8,128)(2,1)S(1)} %collective-permute-done.11.across), channel_id=1, source_target_pairs={{0,1},{1,0},{2,3},{3,2},{4,5},{5,4},{6,7},{7,6},{8,9},{9,8},{10,11... | collective-permute-start | bytes 393224 | tf_op jit(solution)/shard_map/ppermute | solution.py:28
  59.0 9.5 %collective-permute-start.15 = (bf16[144,512]{1,0:T(8,128)(2,1)S(1)}, bf16[144,512]{1,0:T(8,128)(2,1)S(1)}, u32[]{:S(2)}, u32[]{:S(2)}) collective-permute-start(bf16[144,512]{1,0:T(8,128)(2,1)S(1)} %get-tuple-element.42.message.refs_4_), channel_id=1, source_target_pairs={{8,0},{16,8},{24,16},{28,24},{20,28},{12,20},{4,12},{0,4},{9,1},{1... | collective-permute-start | bytes 442376 | tf_op jit(solution)/shard_map/ppermute | solution.py:39
  60.8 10.1 %collective-permute-start.17 = (bf16[144,512]{1,0:T(8,128)(2,1)S(1)}, bf16[144,512]{1,0:T(8,128)(2,1)S(1)}, u32[]{:S(2)}, u32[]{:S(2)}) collective-permute-start(bf16[144,512]{1,0:T(8,128)(2,1)S(1)} %get-tuple-element.42.message.refs_4_), channel_id=1, source_target_pairs={{8,12},{12,8},{16,20},{20,16},{9,13},{13,9},{17,21},{21,17},{10,14... | collective-permute-start | bytes 442376 | tf_op jit(solution)/shard_map/ppermute | solution.py:43
  61.5 9.7 %collective-permute-start.18 = (bf16[144,512]{1,0:T(8,128)(2,1)S(1)}, bf16[144,512]{1,0:T(8,128)(2,1)S(1)}, u32[]{:S(2)}, u32[]{:S(2)}) collective-permute-start(bf16[144,512]{1,0:T(8,128)(2,1)S(1)} %get-tuple-element.42.message.refs_4_), channel_id=1, source_target_pairs={{0,8},{8,16},{16,24},{24,28},{28,20},{20,12},{12,4},{4,0},{1,9},{9... | collective-permute-start | bytes 442376 | tf_op jit(solution)/shard_map/ppermute | solution.py:39
  68.5 5.1 %collective-permute-start.16 = (bf16[144,512]{1,0:T(8,128)(2,1)S(1)}, bf16[144,512]{1,0:T(8,128)(2,1)S(1)}, u32[]{:S(2)}, u32[]{:S(2)}) collective-permute-start(bf16[144,512]{1,0:T(8,128)(2,1)S(1)} %collective-permute-done.15.refs_7_), channel_id=1, source_target_pairs={{0,4},{4,0},{8,12},{12,8},{16,20},{20,16},{24,28},{28,24},{1,5},{5... | collective-permute-start | bytes 442376 | tf_op jit(solution)/shard_map/ppermute | solution.py:28

commit v3 on v2

--- a/solution.py
+++ b/solution.py
@@ -39,8 +39,23 @@
     return lax.ppermute(block, "ctx", ring_routes(lax.axis_size("ctx"))[way])
 
 
+def total_swap(block, partner_of):
+    count, places = lax.axis_size("ctx"), lax.axis_size("mp")
+    route = []
+    for i in range(count):
+        other = partner_of(i, count)
+        for m in range(places):
+            target = i * places + (m ^ 1) if other is None else other * places + m
+            route.append((i * places + m, target))
+    return lax.ppermute(block, ("ctx", "mp"), route)
+
+
 def inner_swap(block):
-    return lax.ppermute(block, "ctx", [(i, i ^ 1) for i in range(2, lax.axis_size("ctx") - 2)])
+    return total_swap(block, lambda i, count: i ^ 1 if 2 <= i < count - 2 else None)
+
+
+def outer_swap(block):
+    return total_swap(block, lambda i, count: ((i + 1) ^ 1) - 1 if 0 < i < count - 1 else None)
 
 
 def window_of(block):
@@ -80,18 +95,6 @@
 
 def head_cols(h):
     return slice(h * HDIM, (h + 1) * HDIM)
-
-
-def pack_body(key, value, packed, sems):
-    frames = key.shape[0]
-    copies = [
-        pltpu.make_async_copy(key, packed.at[pl.ds(0, frames)], sems.at[0]),
-        pltpu.make_async_copy(value, packed.at[pl.ds(frames, frames)], sems.at[1]),
-    ]
-    for copy in copies:
-        copy.start()
-    for copy in copies:
-        copy.wait()
 
 
 def stacked(kvs, rows, cols):
@@ -180,16 +183,21 @@
     return terms[0:1] + terms[1:2] + terms[2:3]
 
 
-def hidden_body(flags, inputs, keep, core, across, cot, seen_a, seen_b, hidden, rims):
+def hidden_body(flags, inputs, keep, core, across, cot, seen_a, seen_b, hidden, rim_near, rim_far):
     frames, width = inputs.shape
+    wide = 2 * HALO
     mine = slice(width, 2 * width)
     total = inputs[...].astype(F32) + keep[:, mine].astype(F32) + core[:, mine].astype(F32)
-    hidden[...] = (total + across[...].astype(F32)).astype(BF16)
-    wide = 2 * HALO
-    rims[0:wide, :] = hidden[0:wide, :]
-    rims[wide : 2 * wide, :] = hidden[frames - wide : frames, :]
-    rims[2 * wide : 2 * wide + HALO, :] = cot[0:HALO, :]
-    rims[2 * wide + HALO : 3 * wide, :] = cot[frames - HALO : frames, :]
+    total = (total + across[...].astype(F32)).astype(BF16)
+    hidden[...] = total
+    even = flags[0] > 0
+    for at, first, last in (
+        (slice(0, wide), total[0:wide], total[frames - wide :]),
+        (slice(wide, wide + HALO), cot[0:HALO, :], cot[frames - HALO : frames, :]),
+    ):
+        first, last = first.astype(F32), last.astype(F32)
+        rim_near[at, :] = jnp.where(even, last, first).astype(BF16)
+        rim_far[at, :] = jnp.where(even, first, last).astype(BF16)
 
 
 def shifted_sum(load, taps_of, rows):
@@ -252,8 +260,8 @@
 
 
 def conv_edge_body(
-    flags, hidden, rim_near, rim_first, cot, taps, rows_in, edge_conv, part_grad,
-    output, grad_input, grad_copy, padded, grads,
+    flags, hidden, rim_near, rim_far, cot, taps, rows_in, edge_conv, part_grad,
+    output, grad_input, padded, grads,
 ):
     frames, width = hidden.shape
     wide = 2 * HALO
@@ -261,19 +269,19 @@
     have = jnp.where(flags[2] > 0, jnp.float32(1.0), jnp.float32(0.0))
     low_ok = jnp.where(even, have, jnp.float32(1.0))
     high_ok = jnp.where(even, jnp.float32(1.0), have)
+    rims, cots_of = slice(0, wide), slice(wide, wide + HALO)
 
     def low_of(rows):
-        return jnp.where(even, rim_first[rows, :].astype(F32), rim_near[rows, :].astype(F32)) * low_ok
+        return jnp.where(even, rim_far[rows, :].astype(F32), rim_near[rows, :].astype(F32)) * low_ok
 
     def high_of(rows):
-        return jnp.where(even, rim_near[rows, :].astype(F32), rim_first[rows, :].astype(F32)) * high_ok
-
-    padded[0:wide, :] = low_of(slice(wide, 2 * wide))
+        return jnp.where(even, rim_near[rows, :].astype(F32), rim_far[rows, :].astype(F32)) * high_ok
+
+    padded[0:wide, :] = low_of(rims)
     padded[wide : 2 * wide, :] = jnp.zeros((wide, width), F32)
-    padded[2 * wide : 3 * wide, :] = high_of(slice(0, wide))
+    padded[2 * wide : 3 * wide, :] = high_of(rims)
     grads[wide : 2 * wide, :] = jnp.zeros((wide, width), F32)
-    cot_low = low_of(slice(2 * wide + HALO, 3 * wide))
-    cot_high = high_of(slice(2 * wide, 2 * wide + HALO))
+    cot_low, cot_high = low_of(cots_of), high_of(cots_of)
     low, high = slice(0, HALO), slice(frames - HALO, frames)
     inner = slice(HALO, frames - HALO)
     output[inner, :] = rows_in[inner, :]
@@ -295,22 +303,29 @@
             lambda at, rows: grads[at : at + rows, cols], taps_backward(taps, cols), 2 * wide
         )
         part = part_grad[:, cols]
-        total = jnp.concatenate(
+        grad_input[:, cols] = jnp.concatenate(
             [part[0:wide] + back[0:wide], part[wide : frames - wide], part[frames - wide :] + back[wide:]],
             axis=0,
         ).astype(BF16)
-        grad_input[:, cols] = total
-        grad_copy[:, cols] = total
-
-
-def upstream_body(flags, own, core, across, cross, weight, att, seen_a, seen_b, message, delta):
-    frames, width = own.shape
-    place = flags[3]
+
+
+def upstream_part(flags, weight, pieces):
+    width = weight.shape[0]
     total = None
-    for flip, block in ((0, own), (1, core), (2, across), (3, cross)):
-        at = pl.ds(pl.multiple_of((place ^ flip) * width, 128), width)
+    for flip, block in pieces:
+        at = pl.ds(pl.multiple_of((flags[3] ^ flip) * width, 128), width)
         part = dot_nt(block[...], weight[:, at])
         total = part if total is None else total + part
+    return total
+
+
+def upstream_chip_body(flags, own, core, weight, partial):
+    partial[...] = upstream_part(flags, weight, ((0, own), (1, core)))
+
+
+def upstream_body(flags, across, cross, weight, att, partial, seen_a, seen_b, message, delta):
+    frames, width = across.shape
+    total = partial[...] + upstream_part(flags, weight, ((2, across), (3, cross)))
     up = total.astype(BF16)
     message[0:frames, :] = up
     lane = lax.broadcasted_iota(jnp.int32, (frames, HDIM), 1)
@@ -323,7 +338,16 @@
     put_terms(message, tile)
 
 
-def query_grad_body(scale, flags, q, own, near, first, second, relay, message, lse, delta, grad_query):
+def query_grad_body(
+    scale, flags, q, own, near, first, second, relay, message, lse, delta, output_here, grad_here,
+    output, grad_input, grad_query, held, sems,
+):
+    writes = [
+        pltpu.make_async_copy(output_here, output, sems.at[0]),
+        pltpu.make_async_copy(grad_here, grad_input, sems.at[1]),
+    ]
+    for write in writes:
+        write.start()
     frames, width = q.shape
     kvs = (near, relay, own, first, second)
     biases = (off_bias(flags[1]), off_bias(flags[2]))
@@ -338,41 +362,62 @@
         )
         dots = dot_nt(message[0:frames, cols], stacked(kvs, slice(frames, 2 * frames), cols))
         grads = (jnp.exp(scores) * (dots - delta[:, h : h + 1]) * scale).astype(BF16)
-        grad_query[:, cols] = dot_nn(grads, keys).astype(BF16)
-
-
-def key_terms(scale, own, queries, messages, biases, cols):
+        held[:, cols] = dot_nn(grads, keys).astype(BF16)
+    writes.append(pltpu.make_async_copy(held, grad_query, sems.at[2]))
+    writes[2].start()
+    for write in writes:
+        write.wait()
+
+
+def key_probs(scale, own, queries, biases, cols):
     frames = own.shape[0] // 2
-    asks = stacked(queries, slice(0, frames), cols)
-    ups = stacked(messages, slice(0, frames), cols)
-    scores = dot_nt(own[0:frames, cols], asks) * scale
-    dots = dot_nt(own[frames : 2 * frames, cols], ups)
-    probs_low, grads = [], []
+    scores = dot_nt(own[0:frames, cols], stacked(queries, slice(0, frames), cols)) * scale
+    parts = []
     for b, bias in enumerate(biases):
-        at = slice(b * frames, (b + 1) * frames)
-        part = scores[:, at] - terms_of(queries[b], frames, cols)
-        probs = jnp.exp(part if bias is None else part + bias)
-        probs_low.append(probs.astype(BF16))
-        grads.append((probs * (dots[:, at] - terms_of(messages[b], frames, cols)) * scale).astype(BF16))
-    key_part = dot_nn(jnp.concatenate(grads, axis=1), asks)
-    return key_part, dot_nn(jnp.concatenate(probs_low, axis=1), ups)
+        part = scores[:, b * frames : (b + 1) * frames] - terms_of(queries[b], frames, cols)
+        parts.append(jnp.exp(part if bias is None else part + bias))
+    return jnp.concatenate(parts, axis=1)
+
+
+def value_terms(probs, messages, cols):
+    frames = probs.shape[0]
+    return dot_nn(probs.astype(BF16), stacked(messages, slice(0, frames), cols))
+
+
+def key_terms(scale, own, probs, queries, messages, cols):
+    frames = own.shape[0] // 2
+    dots = dot_nt(own[frames : 2 * frames, cols], stacked(messages, slice(0, frames), cols))
+    deltas = jnp.concatenate([terms_of(m, frames, cols) for m in messages], axis=1)
+    grads = (probs * (dots - deltas) * scale).astype(BF16)
+    return dot_nn(grads, stacked(queries, slice(0, frames), cols))
 
 
 def key_part_body(scale, flags, own, *refs):
-    queries, messages, (key_part, value_part) = refs[0:4], refs[4:8], refs[8:10]
+    queries, late_query, messages, (key_part, value_part, late) = refs[0:4], refs[4], refs[5:9], refs[9:12]
     biases = (None, off_bias(flags[1]), None, None)
     for h in range(own.shape[1] // HDIM):
         cols = head_cols(h)
-        key_part[:, cols], value_part[:, cols] = key_terms(scale, own, queries, messages, biases, cols)
-
-
-def key_grad_body(scale, flags, own, query, message, key_part, value_part, grad_key, grad_value):
-    biases = (off_bias(flags[2]),)
-    for h in range(own.shape[1] // HDIM):
-        cols = head_cols(h)
-        keys, values = key_terms(scale, own, (query,), (message,), biases, cols)
-        grad_key[:, cols] = (key_part[:, cols] + keys).astype(BF16)
-        grad_value[:, cols] = (value_part[:, cols] + values).astype(BF16)
+        probs = key_probs(scale, own, queries, biases, cols)
+        value_part[:, cols] = value_terms(probs, messages, cols)
+        key_part[:, cols] = key_terms(scale, own, probs, queries, messages, cols)
+        late[:, cols] = key_probs(scale, own, (late_query,), (off_bias(flags[2]),), cols)
+
+
+def key_grad_body(
+    scale, own, query, message, late, key_part, value_part, grad_key, grad_value, held_key, held_value, sems
+):
+    heads = [head_cols(h) for h in range(own.shape[1] // HDIM)]
+    for cols in heads:
+        held_value[:, cols] = (value_part[:, cols] + value_terms(late[:, cols], (message,), cols)).astype(BF16)
+    value_write = pltpu.make_async_copy(held_value, grad_value, sems.at[0])
+    value_write.start()
+    for cols in heads:
+        keys = key_terms(scale, own, late[:, cols], (query,), (message,), cols)
+        held_key[:, cols] = (key_part[:, cols] + keys).astype(BF16)
+    key_write = pltpu.make_async_copy(held_key, grad_key, sems.at[1])
+    key_write.start()
+    value_write.wait()
+    key_write.wait()
 
 
 def per_device(query_rows, key_rows, value_rows, inputs, out_weight, kernel, cotangent):
@@ -390,12 +435,13 @@
     tile32 = shaped((frames, width), F32)
     half = shaped((frames, 2 * width), BF16)
     side = shaped((frames, HDIM), F32)
+    rim = shaped((wide + HALO, width), BF16)
     noted = shaped((frames + 16, width), BF16)
     square = frames * frames * width
 
-    (kv,) = kernel_call(
-        pack_body, (shaped((2 * frames, width), BF16),), (key_rows, value_rows), 0, "pack",
-        [HBM] * 2, [pltpu.SemaphoreType.DMA((2,))], 60, HBM,
+    zero = jnp.zeros((), BF16)
+    kv = lax.pad(key_rows, zero, ((0, frames, 0), (0, 0, 0))) + lax.pad(
+        value_rows, zero, ((frames, 0, 0), (0, 0, 0))
     )
     near, first, second, relay = window_of(kv)
     (weight,) = kernel_call(
@@ -419,14 +465,15 @@
     across = pair_swap(keep[:, 0:width] + core[:, 0:width], "mp", 2)
     q_second = ring(q_own, 1)
     q_first = ring(q_own, 0)
-    hidden, rims = kernel_call(
+    hidden, rim_up, rim_down = kernel_call(
         hidden_body,
-        (tile, shaped((3 * wide, width), BF16)),
+        (tile, rim, rim),
         (flags, inputs, keep, core, across, cotangent, q_second, q_first),
         4 * frames * width, "hidden", [SMEM] + [VMEM] * 5 + [ANY] * 2,
     )
 
-    rim_near = pair_swap(rims, "ctx", 1)
+    rim_far = outer_swap(rim_down)
+    rim_near = pair_swap(rim_up, "ctx", 1)
     rows_out, edge_conv, part_grad = kernel_call(
         conv_inner_body,
         (tile, shaped((2 * wide, width), F32), tile32),
@@ -434,45 +481,51 @@
         140 * frames * width, "conv_inner", [VMEM] * 3,
         [pltpu.VMEM((frames + 2 * wide, width), F32), pltpu.VMEM((frames + wide, width), F32)],
     )
-    rim_first = ring(rim_near, 0)
-    output, grad_input, grad_copy = kernel_call(
+    output_here, grad_here = kernel_call(
         conv_edge_body,
-        (tile, tile, tile),
-        (flags, hidden, rim_near, rim_first, cotangent, kernel, rows_out, edge_conv, part_grad),
+        (tile, tile),
+        (flags, hidden, rim_near, rim_far, cotangent, kernel, rows_out, edge_conv, part_grad),
         70 * frames * width, "conv_edge", None,
         [pltpu.VMEM((3 * wide, width), F32), pltpu.VMEM((3 * wide, width), F32)],
     )
 
-    gi_across = pair_swap(grad_copy, "mp", 2)
-    gi_core = pair_swap(grad_copy, "mp", 1)
+    gi_across = pair_swap(grad_here, "mp", 2)
+    gi_core = pair_swap(grad_here, "mp", 1)
     q_near = inner_swap(q_own)
     q_relay = pair_swap(q_second, "ctx", 1)
     gi_cross = pair_swap(gi_across, "mp", 1)
+    (partial,) = kernel_call(
+        upstream_chip_body, (tile32,), (flags, grad_here, gi_core, weight),
+        frames * width * whole, "upstream_chip",
+    )
     message, delta = kernel_call(
         upstream_body,
         (noted, side),
-        (flags, grad_copy, gi_core, gi_across, gi_cross, weight, att, q_near, q_relay),
-        2 * frames * width * whole, "upstream", [SMEM] + [VMEM] * 6 + [ANY] * 2,
+        (flags, gi_across, gi_cross, weight, att, partial, q_near, q_relay),
+        frames * width * whole, "upstream", [SMEM] + [VMEM] * 5 + [ANY] * 2,
     )
 
     m_near, m_first, m_second, m_relay = window_of(message)
-    (grad_query,) = kernel_call(
+    output, grad_input, grad_query = kernel_call(
         functools.partial(query_grad_body, scale),
-        (tile,),
-        (flags, query_rows, kv, near, first, second, relay, message, lse, delta),
-        30 * square, "query_grad",
-    )
-    key_part, value_part = kernel_call(
+        (tile, tile, tile),
+        (flags, query_rows, kv, near, first, second, relay, message, lse, delta)
+        + (output_here, grad_here),
+        30 * square, "query_grad", None,
+        [pltpu.VMEM((frames, width), BF16), pltpu.SemaphoreType.DMA((3,))], 24, HBM,
+    )
+    key_part, value_part, late = kernel_call(
         functools.partial(key_part_body, scale),
-        (tile32, tile32),
-        (flags, kv, q_own, q_near, q_first, q_second, message, m_near, m_first, m_second),
-        32 * square, "key_part",
+        (tile32, tile32, tile32),
+        (flags, kv, q_own, q_near, q_first, q_second, q_relay, message, m_near, m_first, m_second),
+        34 * square, "key_part",
     )
     grad_key, grad_value = kernel_call(
         functools.partial(key_grad_body, scale),
         (tile, tile),
-        (flags, kv, q_relay, m_relay, key_part, value_part),
-        8 * square, "key_grad",
+        (kv, q_relay, m_relay, late, key_part, value_part),
+        6 * square, "key_grad", [VMEM] * 6,
+        [pltpu.VMEM((frames, width), BF16)] * 2 + [pltpu.SemaphoreType.DMA((2,))], 24, HBM,
     )
     return (output, grad_input, grad_query, grad_key, grad_value)
 

time: 76 us -> 58.8 us (0.77)
  Pallas kernels: 25.3 us -> 16.1 us
  starting transfers between devices: 30.9 us -> 23.5 us
  waiting for transfers between devices: 16.6 us -> 14.8 us
  other arithmetic: 0.1 us -> 1.08 us
    pallas_call x11, Pallas kernels: 25.3 us -> 16.1 us  [kernel_call(): pl.pallas_call(body, out_shape=outs, in_specs=spaces or [SMEM] + [VMEM] *...]
    ppermute x7 -> x6, starting transfers between devices: 20.5 us -> 13 us  [ring(): return lax.ppermute(block, 'ctx', ring_routes(lax.axis_size('ctx'))[way])]
    ppermute x9, starting transfers between devices: 8.45 us -> 10.5 us  [pair_swap(): lax.ppermute(block, axis, [(i, i ^ bit) for i in range(lax.axis_size(axis...]
    ppermute x3 -> x4, starting transfers between devices: 1.98 us -> 0.01 us  [total_swap(): return lax.ppermute(block, ('ctx', 'mp'), route)]
    ppermute x9, waiting for transfers between devices: 8.67 us -> 7.33 us  [pair_swap(): lax.ppermute(block, axis, [(i, i ^ bit) for i in range(lax.axis_size(axis...]
    add x0 -> x1, other arithmetic: none -> 0.99 us  [per_device(): lax.pad(key_rows, zero, ((0, frames, 0), (0, 0, 0)))]
    ppermute x7 -> x6, waiting for transfers between devices: 7.89 us -> 7.5 us  [ring(): return lax.ppermute(block, 'ctx', ring_routes(lax.axis_size('ctx'))[way])]
    unnamed x12 -> x10, local copies, waits for them, and re-layouts: 2.09 us -> 2.31 us
  transfers between devices with their start and end apart: 19 -> 19, of which waited for: 11 -> 10; matrix products, arithmetic and copies ran while one was open for 0% -> 0% of each run, Pallas kernels for 10% -> 15%
where the time goes in v3:
time: 58.8 us; the launch traced here: 58.6 us
  starting transfers between devices  23.5 us (40%)
  Pallas kernels  16.1 us (27%)
  waiting for transfers between devices  14.8 us (25%)
  local copies, waits for them, and re-layouts  2.31 us (4%)
  other arithmetic  1.08 us (2%)
  between operations  0.79 us (1%)
    pallas_call x11, Pallas kernels, kernel_call(): pl.pallas_call(body, out_shape=outs, in_specs=spaces or [SMEM] + [VMEM] *...  16.1 us
    ppermute x6, starting transfers between devices, ring(): return lax.ppermute(block, 'ctx', ring_routes(lax.axis_size('ctx'))[way])  13 us
    ppermute x9, starting transfers between devices, pair_swap(): lax.ppermute(block, axis, [(i, i ^ bit) for i in range(lax.axis_size(axis...  10.5 us
    ppermute x6, waiting for transfers between devices, ring(): return lax.ppermute(block, 'ctx', ring_routes(lax.axis_size('ctx'))[way])  7.5 us
    ppermute x9, waiting for transfers between devices, pair_swap(): lax.ppermute(block, axis, [(i, i ^ bit) for i in range(lax.axis_size(axis...  7.33 us
    unnamed x10, local copies, waits for them, and re-layouts  2.31 us
  transfers between devices with their start and end apart: 19, of which 10 were waited for; matrix products, arithmetic and copies ran while one was open for 0% of the time, Pallas kernels for 15%

profile of v3, /device:TPU:0, one launch (start us, length us, event | category | flops | bytes accessed | tf_op | source)
XLA Modules:
  0.0 58.6 jit_solution(178120285563805897)
XLA Ops:
  0.6 1.0 %pad_add_fusion.own = bf16[256,512]{1,0:T(8,128)(2,1)S(1)} fusion(bf16[128,512]{1,0:T(8,128)(2,1)} %param.9, bf16[128,512]{1,0:T(8,128)(2,1)} %param.8), kind=kLoop, calls=%fused_computation | loop fusion | flops 524288 | bytes 524288 | tf_op jit(solution)/shard_map/add | solution.py:443
  1.6 3.0 %collective-permute-start.2 = (bf16[256,512]{1,0:T(8,128)(2,1)S(1)}, bf16[256,512]{1,0:T(8,128)(2,1)S(1)}, u32[]{:S(2)}, u32[]{:S(2)}) collective-permute-start(bf16[256,512]{1,0:T(8,128)(2,1)S(1)} %pad_add_fusion.own), channel_id=1, source_target_pairs={{8,0},{16,8},{24,16},{28,24},{20,28},{12,20},{4,12},{0,4},{9,1},{1... | collective-permute-start | bytes 786440 | tf_op jit(solution)/shard_map/ppermute | solution.py:39
  4.6 0.0 collective-permute-start
  4.6 3.2 %collective-permute-start.1 = (bf16[256,512]{1,0:T(8,128)(2,1)S(1)}, bf16[256,512]{1,0:T(8,128)(2,1)S(1)}, u32[]{:S(2)}, u32[]{:S(2)}) collective-permute-start(bf16[256,512]{1,0:T(8,128)(2,1)S(1)} %pad_add_fusion.own), channel_id=1, source_target_pairs={{0,8},{8,16},{16,24},{24,28},{28,20},{20,12},{12,4},{4,0},{1,9},{9... | collective-permute-start | bytes 786440 | tf_op jit(solution)/shard_map/ppermute | solution.py:39
  7.8 3.2 %collective-permute-done.2.second.seen = bf16[256,512]{1,0:T(8,128)(2,1)S(1)} collective-permute-done((bf16[256,512]{1,0:T(8,128)(2,1)S(1)}, bf16[256,512]{1,0:T(8,128)(2,1)S(1)}, u32[]{:S(2)}, u32[]{:S(2)}) %collective-permute-start.2) | collective-permute-done | bytes 262176 | tf_op jit(solution)/shard_map/ppermute | solution.py:39
  11.0 1.7 %collective-permute-start.3 = (bf16[256,512]{1,0:T(8,128)(2,1)S(1)}, bf16[256,512]{1,0:T(8,128)(2,1)S(1)}, u32[]{:S(2)}, u32[]{:S(2)}) collective-permute-start(bf16[256,512]{1,0:T(8,128)(2,1)S(1)} %collective-permute-done.2.second.seen), channel_id=1, source_target_pairs={{0,4},{4,0},{8,12},{12,8},{16,20},{20,16},{24,28},{28,24},{1,5},{5... | collective-permute-start | bytes 786440 | tf_op jit(solution)/shard_map/ppermute | solution.py:28
  12.7 0.1 pad_add_fusion.1.flags
  12.7 0.0 copy-start
  12.7 1.6 %copy-done = bf16[512,2048]{1,0:T(8,128)(2,1)S(1)} copy-done((bf16[512,2048]{1,0:T(8,128)(2,1)S(1)}, bf16[512,2048]{1,0:T(8,128)(2,1)}, u32[]{:S(2)}) %copy-start) | copy-done | bytes 2097176
  14.3 0.0 copy-start.1
  14.3 0.1 fetch.1.weight
  14.5 0.0 copy-start.2
  14.5 0.0 copy-start.4
  14.5 0.0 collective-permute-done.near
  14.5 0.0 collective-permute-done.1.first
  14.5 0.7 %copy-done.1 = bf16[128,512]{1,0:T(8,128)(2,1)S(1)} copy-done((bf16[128,512]{1,0:T(8,128)(2,1)S(1)}, bf16[128,512]{1,0:T(8,128)(2,1)}, u32[]{:S(2)}) %copy-start.1) | copy-done | bytes 131096
  15.2 1.7 %forward.1 = (f32[128,512]{1,0:T(8,128)S(1)}, f32[128,128]{1,0:T(8,128)S(1)}, f32[128,128]{1,0:T(8,128)S(1)}) custom-call(s32[4]{0:T(128)S(1)} %pad_add_fusion.1.flags, bf16[128,512]{1,0:T(8,128)(2,1)S(1)} %copy-done.1, bf16[256,512]{1,0:T(8,128)(2,1)S(1)} %pad_add_fusion.own, bf16[256,512]{1,0:T(8,128)(2,1)S(1)} %collective-permute-done.near, ...), custom_call_target="tpu_custom_call" | custom-call | flops 134217728 | bytes 1572880 | tf_op jit(solution)/shard_map/forward/pallas_call | solution.py:76
  17.0 2.0 %collective-permute-done.3.relay = bf16[256,512]{1,0:T(8,128)(2,1)S(1)} collective-permute-done((bf16[256,512]{1,0:T(8,128)(2,1)S(1)}, bf16[256,512]{1,0:T(8,128)(2,1)S(1)}, u32[]{:S(2)}, u32[]{:S(2)}) %collective-permute-start.3) | collective-permute-done | bytes 262176 | tf_op jit(solution)/shard_map/ppermute | solution.py:28
  19.0 0.0 copy-start.3
  19.0 2.5 %project.1 = (bf16[128,512]{1,0:T(8,128)(2,1)S(1)}, f32[128,128]{1,0:T(8,128)S(1)}, bf16[128,1024]{1,0:T(8,128)(2,1)S(1)}, bf16[128,1024]{1,0:T(8,128)(2,1)S(1)}, bf16[144,512]{1,0:T(8,128)(2,1)S(1)}) custom-call(s32[4]{0:T(128)S(1)} %pad_add_fusion.1.flags, bf16[128,512]{1,0:T(8,128)(2,1)S(1)} %copy-done.1, ...), custom_call_target="tpu_custom_call" | custom-call | flops 301989888 | bytes 3751952 | tf_op jit(solution)/shard_map/project/pallas_call | solution.py:76
  21.5 0.1 collective-permute-start.4
  21.6 0.9 %collective-permute-start.6 = (bf16[144,512]{1,0:T(8,128)(2,1)S(1)}, bf16[144,512]{1,0:T(8,128)(2,1)S(1)}, u32[]{:S(2)}, u32[]{:S(2)}) collective-permute-start(bf16[144,512]{1,0:T(8,128)(2,1)S(1)} %get-tuple-element.36.refs_0_), channel_id=1, source_target_pairs={{8,0},{16,8},{24,16},{28,24},{20,28},{12,20},{4,12},{0,4},{9,1},{1... | collective-permute-start | bytes 442376 | tf_op jit(solution)/shard_map/ppermute | solution.py:39
  22.5 1.1 %collective-permute-start.7 = (bf16[144,512]{1,0:T(8,128)(2,1)S(1)}, bf16[144,512]{1,0:T(8,128)(2,1)S(1)}, u32[]{:S(2)}, u32[]{:S(2)}) collective-permute-start(bf16[144,512]{1,0:T(8,128)(2,1)S(1)} %get-tuple-element.36.refs_0_), channel_id=1, source_target_pairs={{0,8},{8,16},{16,24},{24,28},{28,20},{20,12},{12,4},{4,0},{1,9},{9... | collective-permute-start | bytes 442376 | tf_op jit(solution)/shard_map/ppermute | solution.py:39
  23.7 0.0 collective-permute-done.4.core
  23.7 1.6 %collective-permute-start.5 = (bf16[128,512]{1,0:T(8,128)(2,1)S(1)}, bf16[128,512]{1,0:T(8,128)(2,1)S(1)}, u32[]{:S(2)}, u32[]{:S(2)}) collective-permute-start(bf16[128,512]{1,0:T(8,128)(2,1)S(1)} %slice_add_fusion), channel_id=1, source_target_pairs={{0,2},{1,3},{2,0},{3,1},{4,6},{5,7},{6,4},{7,5},{8,10},{9,11},{10,... | collective-permute-start | bytes 393224 | tf_op jit(solution)/shard_map/ppermute | solution.py:28
  25.3 2.6 %collective-permute-done.6.seen_a.refs_3_ = bf16[144,512]{1,0:T(8,128)(2,1)S(1)} collective-permute-done((bf16[144,512]{1,0:T(8,128)(2,1)S(1)}, bf16[144,512]{1,0:T(8,128)(2,1)S(1)}, u32[]{:S(2)}, u32[]{:S(2)}) %collective-permute-start.6) | collective-permute-done | bytes 147488 | tf_op jit(solution)/shard_map/ppermute | solution.py:39
  27.8 0.6 %collective-permute-done.7.seen_b.refs_2_ = bf16[144,512]{1,0:T(8,128)(2,1)S(1)} collective-permute-done((bf16[144,512]{1,0:T(8,128)(2,1)S(1)}, bf16[144,512]{1,0:T(8,128)(2,1)S(1)}, u32[]{:S(2)}, u32[]{:S(2)}) %collective-permute-start.7) | collective-permute-done | bytes 147488 | tf_op jit(solution)/shard_map/ppermute | solution.py:39
  28.4 0.6 %collective-permute-done.5.across = bf16[128,512]{1,0:T(8,128)(2,1)S(1)} collective-permute-done((bf16[128,512]{1,0:T(8,128)(2,1)S(1)}, bf16[128,512]{1,0:T(8,128)(2,1)S(1)}, u32[]{:S(2)}, u32[]{:S(2)}) %collective-permute-start.5) | collective-permute-done | bytes 131104 | tf_op jit(solution)/shard_map/ppermute | solution.py:28
  29.0 0.0 copy-done.2
  29.0 0.0 copy-done.4
  29.0 0.6 %hidden.1 = (bf16[128,512]{1,0:T(8,128)(2,1)S(1)}, bf16[48,512]{1,0:T(8,128)(2,1)S(1)}, bf16[48,512]{1,0:T(8,128)(2,1)S(1)}) custom-call(s32[4]{0:T(128)S(1)} %pad_add_fusion.1.flags, bf16[128,512]{1,0:T(8,128)(2,1)S(1)} %copy-done.4, bf16[128,1024]{1,0:T(8,128)(2,1)S(1)} %get-tuple-element.34.keep, bf16[128,1024]{1,0:T(8,128)(2,1)S(1)} %collective-permute-done.4.core, ...), custom_call_target="tpu_custom_call" | custom-call | flops 262144 | bytes 1441808 | tf_op jit(solution)/shard_map/hidden/pallas_call | solution.py:76
  29.7 1.0 %collective-permute-start.8 = (bf16[48,512]{1,0:T(8,128)(2,1)S(1)}, bf16[48,512]{1,0:T(8,128)(2,1)S(1)}, u32[]{:S(2)}, u32[]{:S(2)}) collective-permute-start(bf16[48,512]{1,0:T(8,128)(2,1)S(1)} %get-tuple-element.38), channel_id=1, source_target_pairs={{0,4},{4,0},{8,12},{12,8},{16,20},{20,16},{24,28},{28,24},{1,5},{5... | collective-permute-start | bytes 147464 | tf_op jit(solution)/shard_map/ppermute | solution.py:28
  30.7 0.0 collective-permute-start.9
  30.7 0.0 copy-done.3
  30.7 1.6 %conv_inner.1 = (bf16[128,512]{1,0:T(8,128)(2,1)S(1)}, f32[64,512]{1,0:T(8,128)S(1)}, f32[128,512]{1,0:T(8,128)S(1)}) custom-call(bf16[128,512]{1,0:T(8,128)(2,1)S(1)} %get-tuple-element.37.hidden, bf16[128,512]{1,0:T(8,128)(2,1)S(1)} %copy-done.2, f32[31,512]{1,0:T(8,128)S(1)} %copy-done.3), custom_call_target="tpu_custom_call" | custom-call | flops 9175040 | bytes 849920 | tf_op jit(solution)/shard_map/conv_inner/pallas_call | solution.py:76
  32.3 1.5 %collective-permute-done.8.rim_near = bf16[48,512]{1,0:T(8,128)(2,1)S(1)} collective-permute-done((bf16[48,512]{1,0:T(8,128)(2,1)S(1)}, bf16[48,512]{1,0:T(8,128)(2,1)S(1)}, u32[]{:S(2)}, u32[]{:S(2)}) %collective-permute-start.8) | collective-permute-done | bytes 49184 | tf_op jit(solution)/shard_map/ppermute | solution.py:28
  33.8 0.0 collective-permute-done.9.rim_far
  33.8 1.3 %conv_edge.1 = (bf16[128,512]{1,0:T(8,128)(2,1)S(1)}, bf16[128,512]{1,0:T(8,128)(2,1)S(1)}) custom-call(s32[4]{0:T(128)S(1)} %pad_add_fusion.1.flags, bf16[128,512]{1,0:T(8,128)(2,1)S(1)} %get-tuple-element.37.hidden, bf16[48,512]{1,0:T(8,128)(2,1)S(1)} %collective-permute-done.8.rim_near, bf16[48,512]{1,0:T(8,128)(2,1)S(1)} %collective-permute-done.9.rim_far, ...), custom_call_target="tpu_custom_call" | custom-call | flops 4587520 | bytes 1210384 | tf_op jit(solution)/shard_map/conv_edge/pallas_call | solution.py:76
  35.1 1.6 %collective-permute-start.10 = (bf16[128,512]{1,0:T(8,128)(2,1)S(1)}, bf16[128,512]{1,0:T(8,128)(2,1)S(1)}, u32[]{:S(2)}, u32[]{:S(2)}) collective-permute-start(bf16[128,512]{1,0:T(8,128)(2,1)S(1)} %get-tuple-element.43.own.grad_here), channel_id=1, source_target_pairs={{0,2},{1,3},{2,0},{3,1},{4,6},{5,7},{6,4},{7,5},{8,10},{9,11},{10,... | collective-permute-start | bytes 393224 | tf_op jit(solution)/shard_map/ppermute | solution.py:28
  36.7 0.0 collective-permute-start.13
  36.7 2.9 %collective-permute-start.14 = (bf16[144,512]{1,0:T(8,128)(2,1)S(1)}, bf16[144,512]{1,0:T(8,128)(2,1)S(1)}, u32[]{:S(2)}, u32[]{:S(2)}) collective-permute-start(bf16[144,512]{1,0:T(8,128)(2,1)S(1)} %collective-permute-done.6.seen_a.refs_3_), channel_id=1, source_target_pairs={{0,4},{4,0},{8,12},{12,8},{16,20},{20,16},{24,28},{28,24},{1,5},{5... | collective-permute-start | bytes 442376 | tf_op jit(solution)/shard_map/ppermute | solution.py:28
  39.6 0.2 collective-permute-start.12
  39.8 0.3 collective-permute-done.10.across
  40.1 0.0 collective-permute-start.11
  40.1 0.8 %collective-permute-done.12.core = bf16[128,512]{1,0:T(8,128)(2,1)S(1)} collective-permute-done((bf16[128,512]{1,0:T(8,128)(2,1)S(1)}, bf16[128,512]{1,0:T(8,128)(2,1)S(1)}, u32[]{:S(2)}, u32[]{:S(2)}) %collective-permute-start.12) | collective-permute-done | bytes 131104 | tf_op jit(solution)/shard_map/ppermute | solution.py:28
  41.0 1.0 %upstream_chip.1.partial = f32[128,512]{1,0:T(8,128)S(1)} custom-call(s32[4]{0:T(128)S(1)} %pad_add_fusion.1.flags, bf16[128,512]{1,0:T(8,128)(2,1)S(1)} %get-tuple-element.43.own.grad_here, bf16[128,512]{1,0:T(8,128)(2,1)S(1)} %collective-permute-done.12.core, bf16[512,2048]{1,0:T(8,128)(2,1)S(1)} %fetch.1.weight), custom_call_target="tpu_custom_call" | custom-call | flops 134217728 | bytes 2621456 | tf_op jit(solution)/shard_map/upstream_chip/pallas_call | solution.py:76
  42.0 0.0 collective-permute-done.13.seen_a.refs_1_
  42.0 2.1 %collective-permute-done.14.seen_b.refs_4_.query = bf16[144,512]{1,0:T(8,128)(2,1)S(1)} collective-permute-done((bf16[144,512]{1,0:T(8,128)(2,1)S(1)}, bf16[144,512]{1,0:T(8,128)(2,1)S(1)}, u32[]{:S(2)}, u32[]{:S(2)}) %collective-permute-start.14) | collective-permute-done | bytes 147488 | tf_op jit(solution)/shard_map/ppermute | solution.py:28
  44.1 0.0 collective-permute-done.11.cross
  44.1 1.2 %upstream.1 = (bf16[144,512]{1,0:T(8,128)(2,1)S(1)}, f32[128,128]{1,0:T(8,128)S(1)}) custom-call(s32[4]{0:T(128)S(1)} %pad_add_fusion.1.flags, bf16[128,512]{1,0:T(8,128)(2,1)S(1)} %collective-permute-done.10.across, bf16[128,512]{1,0:T(8,128)(2,1)S(1)} %collective-permute-done.11.cross, bf16[512,2048]{1,0:T(8,128)(2,1)S(1)} %fetch.1.weight, ...), custom_call_target="tpu_custom_call" | custom-call | flops 134217728 | bytes 3260432 | tf_op jit(solution)/shard_map/upstream/pallas_call | solution.py:76
  45.3 1.8 %collective-permute-start.15 = (bf16[144,512]{1,0:T(8,128)(2,1)S(1)}, bf16[144,512]{1,0:T(8,128)(2,1)S(1)}, u32[]{:S(2)}, u32[]{:S(2)}) collective-permute-start(bf16[144,512]{1,0:T(8,128)(2,1)S(1)} %get-tuple-element.45.message.refs_5_), channel_id=1, source_target_pairs={{8,0},{16,8},{24,16},{28,24},{20,28},{12,20},{4,12},{0,4},{9,1},{1... | collective-permute-start | bytes 442376 | tf_op jit(solution)/shard_map/ppermute | solution.py:39
  47.1 0.0 collective-permute-start.17
  47.1 3.0 %collective-permute-start.18 = (bf16[144,512]{1,0:T(8,128)(2,1)S(1)}, bf16[144,512]{1,0:T(8,128)(2,1)S(1)}, u32[]{:S(2)}, u32[]{:S(2)}) collective-permute-start(bf16[144,512]{1,0:T(8,128)(2,1)S(1)} %get-tuple-element.45.message.refs_5_), channel_id=1, source_target_pairs={{0,8},{8,16},{16,24},{24,28},{28,20},{20,12},{12,4},{4,0},{1,9},{9... | collective-permute-start | bytes 442376 | tf_op jit(solution)/shard_map/ppermute | solution.py:39
  50.1 1.1 %collective-permute-done.15.refs_8_ = bf16[144,512]{1,0:T(8,128)(2,1)S(1)} collective-permute-done((bf16[144,512]{1,0:T(8,128)(2,1)S(1)}, bf16[144,512]{1,0:T(8,128)(2,1)S(1)}, u32[]{:S(2)}, u32[]{:S(2)}) %collective-permute-start.15) | collective-permute-done | bytes 147488 | tf_op jit(solution)/shard_map/ppermute | solution.py:39
  51.2 1.4 %collective-permute-start.16 = (bf16[144,512]{1,0:T(8,128)(2,1)S(1)}, bf16[144,512]{1,0:T(8,128)(2,1)S(1)}, u32[]{:S(2)}, u32[]{:S(2)}) collective-permute-start(bf16[144,512]{1,0:T(8,128)(2,1)S(1)} %collective-permute-done.15.refs_8_), channel_id=1, source_target_pairs={{0,4},{4,0},{8,12},{12,8},{16,20},{20,16},{24,28},{28,24},{1,5},{5... | collective-permute-start | bytes 442376 | tf_op jit(solution)/shard_map/ppermute | solution.py:28
  52.6 2.4 %query_grad.1 = (bf16[128,512]{1,0:T(8,128)(2,1)}, bf16[128,512]{1,0:T(8,128)(2,1)}, bf16[128,512]{1,0:T(8,128)(2,1)}) custom-call(s32[4]{0:T(128)S(1)} %pad_add_fusion.1.flags, bf16[128,512]{1,0:T(8,128)(2,1)S(1)} %copy-done.1, bf16[256,512]{1,0:T(8,128)(2,1)S(1)} %pad_add_fusion.own, bf16[256,512]{1,0:T(8,128)(2,1)S(1)} %collective-permute-done.near, ...), custom_call_target="tpu_custom_call" | custom-call | flops 251658240 | bytes 2375696 | tf_op jit(solution)/shard_map/query_grad/pallas_call | solution.py:76
  55.0 0.0 collective-permute-done.17.refs_6_
  55.0 0.0 collective-permute-done.18.refs_7_
  55.0 2.2 %key_part.1 = (f32[128,512]{1,0:T(8,128)S(1)}, f32[128,512]{1,0:T(8,128)S(1)}, f32[128,512]{1,0:T(8,128)S(1)}) custom-call(s32[4]{0:T(128)S(1)} %pad_add_fusion.1.flags, bf16[256,512]{1,0:T(8,128)(2,1)S(1)} %pad_add_fusion.own, bf16[144,512]{1,0:T(8,128)(2,1)S(1)} %get-tuple-element.36.refs_0_, bf16[144,512]{1,0:T(8,128)(2,1)S(1)} %collective-permute-done.13.seen_a.refs_1_, ...), custom_call_target="tpu_custom_call" | custom-call | flops 285212672 | bytes 2375696 | tf_op jit(solution)/shard_map/key_part/pallas_call | solution.py:76
  57.2 0.0 collective-permute-done.16.message
  57.2 1.5 %key_grad.1 = (bf16[128,512]{1,0:T(8,128)(2,1)}, bf16[128,512]{1,0:T(8,128)(2,1)}) custom-call(bf16[256,512]{1,0:T(8,128)(2,1)S(1)} %pad_add_fusion.own, bf16[144,512]{1,0:T(8,128)(2,1)S(1)} %collective-permute-done.14.seen_b.refs_4_.query, bf16[144,512]{1,0:T(8,128)(2,1)S(1)} %collective-permute-done.16.message, f32[128,512]{1,0:T(8,128)S(1)} %get-tuple-element.52.late, ...), custom_call_target="tpu_custom_call" | custom-call | flops 50331648 | bytes 1605632 | tf_op jit(solution)/shard_map/key_grad/pallas_call | solution.py:76
  (1 shorter events, 0.0 us)
Async XLA Ops:
  1.6 9.4 %collective-permute-start.2 = (bf16[256,512]{1,0:T(8,128)(2,1)S(1)}, bf16[256,512]{1,0:T(8,128)(2,1)S(1)}, u32[]{:S(2)}, u32[]{:S(2)}) collective-permute-start(bf16[256,512]{1,0:T(8,128)(2,1)S(1)} %pad_add_fusion.own), channel_id=1, source_target_pairs={{8,0},{16,8},{24,16},{28,24},{20,28},{12,20},{4,12},{0,4},{9,1},{1... | collective-permute-start | bytes 786440 | tf_op jit(solution)/shard_map/ppermute | solution.py:39
  4.6 9.9 %collective-permute-start = (bf16[256,512]{1,0:T(8,128)(2,1)S(1)}, bf16[256,512]{1,0:T(8,128)(2,1)S(1)}, u32[]{:S(2)}, u32[]{:S(2)}) collective-permute-start(bf16[256,512]{1,0:T(8,128)(2,1)S(1)} %pad_add_fusion.own), channel_id=1, source_target_pairs={{0,1},{1,0},{2,3},{3,2},{4,5},{5,4},{6,7},{7,6},{8,12},{9,13},{10,... | collective-permute-start | bytes 786440 | tf_op jit(solution)/shard_map/ppermute | solution.py:50
  4.6 9.9 %collective-permute-start.1 = (bf16[256,512]{1,0:T(8,128)(2,1)S(1)}, bf16[256,512]{1,0:T(8,128)(2,1)S(1)}, u32[]{:S(2)}, u32[]{:S(2)}) collective-permute-start(bf16[256,512]{1,0:T(8,128)(2,1)S(1)} %pad_add_fusion.own), channel_id=1, source_target_pairs={{0,8},{8,16},{16,24},{24,28},{28,20},{20,12},{12,4},{4,0},{1,9},{9... | collective-permute-start | bytes 786440 | tf_op jit(solution)/shard_map/ppermute | solution.py:39
  11.0 7.9 %collective-permute-start.3 = (bf16[256,512]{1,0:T(8,128)(2,1)S(1)}, bf16[256,512]{1,0:T(8,128)(2,1)S(1)}, u32[]{:S(2)}, u32[]{:S(2)}) collective-permute-start(bf16[256,512]{1,0:T(8,128)(2,1)S(1)} %collective-permute-done.2.second.seen), channel_id=1, source_target_pairs={{0,4},{4,0},{8,12},{12,8},{16,20},{20,16},{24,28},{28,24},{1,5},{5... | collective-permute-start | bytes 786440 | tf_op jit(solution)/shard_map/ppermute | solution.py:28
  12.7 1.6 %copy-start = (bf16[512,2048]{1,0:T(8,128)(2,1)S(1)}, bf16[512,2048]{1,0:T(8,128)(2,1)}, u32[]{:S(2)}) copy-start(bf16[512,2048]{1,0:T(8,128)(2,1)} %weight.1) | copy-start | bytes 6291460
  14.3 0.9 %copy-start.1 = (bf16[128,512]{1,0:T(8,128)(2,1)S(1)}, bf16[128,512]{1,0:T(8,128)(2,1)}, u32[]{:S(2)}) copy-start(bf16[128,512]{1,0:T(8,128)(2,1)} %q.5) | copy-start | bytes 393220
  14.5 14.5 %copy-start.2 = (bf16[128,512]{1,0:T(8,128)(2,1)S(1)}, bf16[128,512]{1,0:T(8,128)(2,1)}, u32[]{:S(2)}) copy-start(bf16[128,512]{1,0:T(8,128)(2,1)} %cot.5) | copy-start | bytes 393220
  14.5 14.5 %copy-start.4 = (bf16[128,512]{1,0:T(8,128)(2,1)S(1)}, bf16[128,512]{1,0:T(8,128)(2,1)}, u32[]{:S(2)}) copy-start(bf16[128,512]{1,0:T(8,128)(2,1)} %inputs.1) | copy-start | bytes 393220
  19.0 11.8 %copy-start.3 = (f32[31,512]{1,0:T(8,128)S(1)}, f32[31,512]{1,0:T(8,128)}, u32[]{:S(2)}) copy-start(f32[31,512]{1,0:T(8,128)} %taps.3) | copy-start | bytes 190468
  21.5 2.2 %collective-permute-start.4 = (bf16[128,1024]{1,0:T(8,128)(2,1)S(1)}, bf16[128,1024]{1,0:T(8,128)(2,1)S(1)}, u32[]{:S(2)}, u32[]{:S(2)}) collective-permute-start(bf16[128,1024]{1,0:T(8,128)(2,1)S(1)} %get-tuple-element.35), channel_id=1, source_target_pairs={{0,1},{1,0},{2,3},{3,2},{4,5},{5,4},{6,7},{7,6},{8,9},{9,8},{10,11... | collective-permute-start | bytes 786440 | tf_op jit(solution)/shard_map/ppermute | solution.py:28
  21.6 6.2 %collective-permute-start.6 = (bf16[144,512]{1,0:T(8,128)(2,1)S(1)}, bf16[144,512]{1,0:T(8,128)(2,1)S(1)}, u32[]{:S(2)}, u32[]{:S(2)}) collective-permute-start(bf16[144,512]{1,0:T(8,128)(2,1)S(1)} %get-tuple-element.36.refs_0_), channel_id=1, source_target_pairs={{8,0},{16,8},{24,16},{28,24},{20,28},{12,20},{4,12},{0,4},{9,1},{1... | collective-permute-start | bytes 442376 | tf_op jit(solution)/shard_map/ppermute | solution.py:39
  22.5 5.9 %collective-permute-start.7 = (bf16[144,512]{1,0:T(8,128)(2,1)S(1)}, bf16[144,512]{1,0:T(8,128)(2,1)S(1)}, u32[]{:S(2)}, u32[]{:S(2)}) collective-permute-start(bf16[144,512]{1,0:T(8,128)(2,1)S(1)} %get-tuple-element.36.refs_0_), channel_id=1, source_target_pairs={{0,8},{8,16},{16,24},{24,28},{28,20},{20,12},{12,4},{4,0},{1,9},{9... | collective-permute-start | bytes 442376 | tf_op jit(solution)/shard_map/ppermute | solution.py:39
  23.7 5.4 %collective-permute-start.5 = (bf16[128,512]{1,0:T(8,128)(2,1)S(1)}, bf16[128,512]{1,0:T(8,128)(2,1)S(1)}, u32[]{:S(2)}, u32[]{:S(2)}) collective-permute-start(bf16[128,512]{1,0:T(8,128)(2,1)S(1)} %slice_add_fusion), channel_id=1, source_target_pairs={{0,2},{1,3},{2,0},{3,1},{4,6},{5,7},{6,4},{7,5},{8,10},{9,11},{10,... | collective-permute-start | bytes 393224 | tf_op jit(solution)/shard_map/ppermute | solution.py:28
  29.7 4.2 %collective-permute-start.8 = (bf16[48,512]{1,0:T(8,128)(2,1)S(1)}, bf16[48,512]{1,0:T(8,128)(2,1)S(1)}, u32[]{:S(2)}, u32[]{:S(2)}) collective-permute-start(bf16[48,512]{1,0:T(8,128)(2,1)S(1)} %get-tuple-element.38), channel_id=1, source_target_pairs={{0,4},{4,0},{8,12},{12,8},{16,20},{20,16},{24,28},{28,24},{1,5},{5... | collective-permute-start | bytes 147464 | tf_op jit(solution)/shard_map/ppermute | solution.py:28
  30.7 3.1 %collective-permute-start.9 = (bf16[48,512]{1,0:T(8,128)(2,1)S(1)}, bf16[48,512]{1,0:T(8,128)(2,1)S(1)}, u32[]{:S(2)}, u32[]{:S(2)}) collective-permute-start(bf16[48,512]{1,0:T(8,128)(2,1)S(1)} %get-tuple-element.39), channel_id=1, source_target_pairs={{0,1},{1,0},{2,3},{3,2},{4,8},{5,9},{6,10},{7,11},{8,4},{9,5},{10,... | collective-permute-start | bytes 147464 | tf_op jit(solution)/shard_map/ppermute | solution.py:50
  35.1 5.0 %collective-permute-start.10 = (bf16[128,512]{1,0:T(8,128)(2,1)S(1)}, bf16[128,512]{1,0:T(8,128)(2,1)S(1)}, u32[]{:S(2)}, u32[]{:S(2)}) collective-permute-start(bf16[128,512]{1,0:T(8,128)(2,1)S(1)} %get-tuple-element.43.own.grad_here), channel_id=1, source_target_pairs={{0,2},{1,3},{2,0},{3,1},{4,6},{5,7},{6,4},{7,5},{8,10},{9,11},{10,... | collective-permute-start | bytes 393224 | tf_op jit(solution)/shard_map/ppermute | solution.py:28
  36.7 5.3 %collective-permute-start.13 = (bf16[144,512]{1,0:T(8,128)(2,1)S(1)}, bf16[144,512]{1,0:T(8,128)(2,1)S(1)}, u32[]{:S(2)}, u32[]{:S(2)}) collective-permute-start(bf16[144,512]{1,0:T(8,128)(2,1)S(1)} %get-tuple-element.36.refs_0_), channel_id=1, source_target_pairs={{0,1},{1,0},{2,3},{3,2},{4,5},{5,4},{6,7},{7,6},{8,12},{9,13},{10,... | collective-permute-start | bytes 442376 | tf_op jit(solution)/shard_map/ppermute | solution.py:50
  36.7 7.4 %collective-permute-start.14 = (bf16[144,512]{1,0:T(8,128)(2,1)S(1)}, bf16[144,512]{1,0:T(8,128)(2,1)S(1)}, u32[]{:S(2)}, u32[]{:S(2)}) collective-permute-start(bf16[144,512]{1,0:T(8,128)(2,1)S(1)} %collective-permute-done.6.seen_a.refs_3_), channel_id=1, source_target_pairs={{0,4},{4,0},{8,12},{12,8},{16,20},{20,16},{24,28},{28,24},{1,5},{5... | collective-permute-start | bytes 442376 | tf_op jit(solution)/shard_map/ppermute | solution.py:28
  39.6 1.3 %collective-permute-start.12 = (bf16[128,512]{1,0:T(8,128)(2,1)S(1)}, bf16[128,512]{1,0:T(8,128)(2,1)S(1)}, u32[]{:S(2)}, u32[]{:S(2)}) collective-permute-start(bf16[128,512]{1,0:T(8,128)(2,1)S(1)} %get-tuple-element.43.own.grad_here), channel_id=1, source_target_pairs={{0,1},{1,0},{2,3},{3,2},{4,5},{5,4},{6,7},{7,6},{8,9},{9,8},{10,11... | collective-permute-start | bytes 393224 | tf_op jit(solution)/shard_map/ppermute | solution.py:28
  40.1 4.0 %collective-permute-start.11 = (bf16[128,512]{1,0:T(8,128)(2,1)S(1)}, bf16[128,512]{1,0:T(8,128)(2,1)S(1)}, u32[]{:S(2)}, u32[]{:S(2)}) collective-permute-start(bf16[128,512]{1,0:T(8,128)(2,1)S(1)} %collective-permute-done.10.across), channel_id=1, source_target_pairs={{0,1},{1,0},{2,3},{3,2},{4,5},{5,4},{6,7},{7,6},{8,9},{9,8},{10,11... | collective-permute-start | bytes 393224 | tf_op jit(solution)/shard_map/ppermute | solution.py:28
  45.3 5.9 %collective-permute-start.15 = (bf16[144,512]{1,0:T(8,128)(2,1)S(1)}, bf16[144,512]{1,0:T(8,128)(2,1)S(1)}, u32[]{:S(2)}, u32[]{:S(2)}) collective-permute-start(bf16[144,512]{1,0:T(8,128)(2,1)S(1)} %get-tuple-element.45.message.refs_5_), channel_id=1, source_target_pairs={{8,0},{16,8},{24,16},{28,24},{20,28},{12,20},{4,12},{0,4},{9,1},{1... | collective-permute-start | bytes 442376 | tf_op jit(solution)/shard_map/ppermute | solution.py:39
  47.1 7.9 %collective-permute-start.17 = (bf16[144,512]{1,0:T(8,128)(2,1)S(1)}, bf16[144,512]{1,0:T(8,128)(2,1)S(1)}, u32[]{:S(2)}, u32[]{:S(2)}) collective-permute-start(bf16[144,512]{1,0:T(8,128)(2,1)S(1)} %get-tuple-element.45.message.refs_5_), channel_id=1, source_target_pairs={{0,1},{1,0},{2,3},{3,2},{4,5},{5,4},{6,7},{7,6},{8,12},{9,13},{10,... | collective-permute-start | bytes 442376 | tf_op jit(solution)/shard_map/ppermute | solution.py:50
  47.1 7.9 %collective-permute-start.18 = (bf16[144,512]{1,0:T(8,128)(2,1)S(1)}, bf16[144,512]{1,0:T(8,128)(2,1)S(1)}, u32[]{:S(2)}, u32[]{:S(2)}) collective-permute-start(bf16[144,512]{1,0:T(8,128)(2,1)S(1)} %get-tuple-element.45.message.refs_5_), channel_id=1, source_target_pairs={{0,8},{8,16},{16,24},{24,28},{28,20},{20,12},{12,4},{4,0},{1,9},{9... | collective-permute-start | bytes 442376 | tf_op jit(solution)/shard_map/ppermute | solution.py:39
  51.2 5.9 %collective-permute-start.16 = (bf16[144,512]{1,0:T(8,128)(2,1)S(1)}, bf16[144,512]{1,0:T(8,128)(2,1)S(1)}, u32[]{:S(2)}, u32[]{:S(2)}) collective-permute-start(bf16[144,512]{1,0:T(8,128)(2,1)S(1)} %collective-permute-done.15.refs_8_), channel_id=1, source_target_pairs={{0,4},{4,0},{8,12},{12,8},{16,20},{20,16},{24,28},{28,24},{1,5},{5... | collective-permute-start | bytes 442376 | tf_op jit(solution)/shard_map/ppermute | solution.py:28

commit v4 on v3

--- a/solution.py
+++ b/solution.py
@@ -71,8 +71,7 @@
 HBM = pl.BlockSpec(memory_space=pltpu.HBM)
 
 
-def kernel_call(body, outs, args, flops, name, spaces=None, scratch=(), mib=24, out_space=VMEM):
-    nbytes = sum(math.prod(a.shape) * a.dtype.itemsize for a in list(args) + list(outs))
+def kernel_call(body, outs, args, micros, name, spaces=None, scratch=(), mib=24, out_space=VMEM):
     return pl.pallas_call(
         body,
         out_shape=outs,
@@ -80,7 +79,9 @@
         out_specs=tuple(out_space for _ in outs),
         scratch_shapes=scratch,
         compiler_params=pltpu.CompilerParams(vmem_limit_bytes=mib * 1024 * 1024),
-        cost_estimate=pl.CostEstimate(flops=flops, bytes_accessed=nbytes, transcendentals=0),
+        cost_estimate=pl.CostEstimate(
+            flops=0, bytes_accessed=int(micros * 3.69e6), transcendentals=0
+        ),
         name=name,
     )(*args)
 
@@ -97,37 +98,43 @@
     return slice(h * HDIM, (h + 1) * HDIM)
 
 
-def stacked(kvs, rows, cols):
-    return jnp.concatenate([kv[rows, cols] for kv in kvs], axis=0)
-
-
-def fetch_body(weight, seen, fetched, sem):
-    copy = pltpu.make_async_copy(weight, fetched, sem)
-    copy.start()
-    copy.wait()
+def stacked(blocks, rows, cols):
+    return jnp.concatenate([block[rows, cols] for block in blocks], axis=0)
+
+
+def hold_body(block, seen, held):
+    held[...] = block[...]
 
 
 def forward_body(scale, flags, q, own, near, first, second, sums, tops, totals):
     frames, width = q.shape
-    kvs = (near, own, first, second)
     lane = lax.broadcasted_iota(jnp.int32, (frames, HDIM), 1)
     top_tile = jnp.zeros((frames, HDIM), F32)
     total_tile = jnp.zeros((frames, HDIM), F32)
     bias = off_bias(flags[1])
+    blocks = (near, own, first, second)
     for h in range(width // HDIM):
         cols = head_cols(h)
-        scores = dot_nt(q[:, cols], stacked(kvs, slice(0, frames), cols)) * scale
+        scores = dot_nt(q[:, cols], stacked(blocks, slice(0, frames), cols)) * scale
         scores = jnp.concatenate([scores[:, 0:frames] + bias, scores[:, frames:]], axis=1)
         top = jnp.max(scores, axis=1, keepdims=True)
         probs = jnp.exp(scores - top)
-        sums[:, cols] = dot_nn(probs.astype(BF16), stacked(kvs, slice(frames, 2 * frames), cols))
+        sums[:, cols] = dot_nn(probs.astype(BF16), stacked(blocks, slice(frames, 2 * frames), cols))
         top_tile = jnp.where(lane == h, top, top_tile)
         total_tile = jnp.where(lane == h, jnp.sum(probs, axis=1, keepdims=True), total_tile)
     tops[...] = top_tile
     totals[...] = total_tile
 
 
-def project_body(scale, flags, q, relay, sums, tops, totals, weight, att, lse, send, keep, q_message):
+def share_of(attended, weight, target):
+    width = weight.shape[0]
+    block = weight[:, pl.ds(pl.multiple_of(target * width, 128), width)]
+    return dot_nn(attended, block).astype(BF16)
+
+
+def project_body(
+    scale, flags, q, relay, sums, tops, totals, weight, att, lse, send, keep
+):
     frames, width = q.shape
     lane = lax.broadcasted_iota(jnp.int32, (frames, HDIM), 1)
     lse_tile = jnp.zeros((frames, HDIM), F32)
@@ -144,50 +151,51 @@
         att[:, cols] = (summed / total).astype(BF16)
         lse_tile = jnp.where(lane == h, top + jnp.log(total), lse_tile)
     lse[...] = lse_tile
-    place = flags[3]
     attended = att[...]
-
-    def share(target):
-        block = weight[:, pl.ds(pl.multiple_of(target * width, 128), width)]
-        return dot_nn(attended, block).astype(BF16)
-
-    send[:, 0:width] = share(place ^ 3)
-    send[:, width : 2 * width] = share(place ^ 1)
-    keep[:, 0:width] = share(place ^ 2)
-    keep[:, width : 2 * width] = share(place)
-    q_message[0:frames, :] = q[...]
-    put_terms(q_message, lse_tile)
-
-
-def term_rows(row):
-    width = row.shape[1]
+    send[...] = share_of(attended, weight, flags[3] ^ 3)
+    keep[...] = share_of(attended, weight, flags[3] ^ 2)
+
+
+def join_body(keep, core, q, q_second, outgoing, q_copy, second_copy):
+    outgoing[...] = (keep[...].astype(F32) + core[...].astype(F32)).astype(BF16)
+    q_copy[...] = q[...]
+    second_copy[...] = q_second[...]
+
+
+def project_own_body(flags, att, weight, seen_a, seen_b, send, keep):
+    attended = att[...]
+    send[...] = share_of(attended, weight, flags[3] ^ 1)
+    keep[...] = share_of(attended, weight, flags[3])
+
+
+def term_rows(rows):
+    width = rows[0].shape[1]
     at = lax.broadcasted_iota(jnp.int32, (16, width), 0)
     block = jnp.zeros((16, width), F32)
-    rest = row
-    for k in range(3):
-        term = rest.astype(BF16).astype(F32)
-        rest = rest - term
-        block = jnp.where(at == k, term, block)
+    for r, rest in enumerate(rows):
+        for k in range(3):
+            term = rest.astype(BF16).astype(F32)
+            rest = rest - term
+            block = jnp.where(at == 3 * r + k, term, block)
     return block.astype(BF16)
 
 
-def put_terms(message, tile):
-    frames = tile.shape[0]
-    rows = tile.T
+def put_terms(message, tiles):
+    frames = tiles[0].shape[0]
+    turned = [tile.T for tile in tiles]
     for h in range(message.shape[1] // HDIM):
-        message[frames : frames + 16, head_cols(h)] = term_rows(rows[h : h + 1, :])
-
-
-def terms_of(message, frames, cols):
+        message[frames : frames + 16, head_cols(h)] = term_rows([t[h : h + 1, :] for t in turned])
+
+
+def terms_of(message, frames, which, cols):
     terms = message[frames : frames + 16, cols].astype(F32)
-    return terms[0:1] + terms[1:2] + terms[2:3]
+    return terms[3 * which : 3 * which + 1] + terms[3 * which + 1 : 3 * which + 2] + terms[3 * which + 2 : 3 * which + 3]
 
 
 def hidden_body(flags, inputs, keep, core, across, cot, seen_a, seen_b, hidden, rim_near, rim_far):
     frames, width = inputs.shape
     wide = 2 * HALO
-    mine = slice(width, 2 * width)
-    total = inputs[...].astype(F32) + keep[:, mine].astype(F32) + core[:, mine].astype(F32)
+    total = inputs[...].astype(F32) + keep[...].astype(F32) + core[...].astype(F32)
     total = (total + across[...].astype(F32)).astype(BF16)
     hidden[...] = total
     even = flags[0] > 0
@@ -323,9 +331,13 @@
     partial[...] = upstream_part(flags, weight, ((0, own), (1, core)))
 
 
-def upstream_body(flags, across, cross, weight, att, partial, seen_a, seen_b, message, delta):
-    frames, width = across.shape
-    total = partial[...] + upstream_part(flags, weight, ((2, across), (3, cross)))
+def upstream_across_body(flags, across, weight, before, partial):
+    partial[...] = before[...] + upstream_part(flags, weight, ((2, across),))
+
+
+def upstream_body(flags, cross, weight, att, lse, partial, message, delta):
+    frames, width = cross.shape
+    total = partial[...] + upstream_part(flags, weight, ((3, cross),))
     up = total.astype(BF16)
     message[0:frames, :] = up
     lane = lax.broadcasted_iota(jnp.int32, (frames, HDIM), 1)
@@ -335,7 +347,7 @@
         product = up[:, cols].astype(F32) * att[:, cols].astype(F32)
         tile = jnp.where(lane == h, jnp.sum(product, axis=1, keepdims=True), tile)
     delta[...] = tile
-    put_terms(message, tile)
+    put_terms(message, [lse[...], tile])
 
 
 def query_grad_body(
@@ -349,18 +361,18 @@
     for write in writes:
         write.start()
     frames, width = q.shape
-    kvs = (near, relay, own, first, second)
-    biases = (off_bias(flags[1]), off_bias(flags[2]))
+    near_bias, relay_bias = off_bias(flags[1]), off_bias(flags[2])
+    blocks = (near, own, first, second, relay)
     for h in range(width // HDIM):
         cols = head_cols(h)
-        keys = stacked(kvs, slice(0, frames), cols)
+        keys = stacked(blocks, slice(0, frames), cols)
         scores = dot_nt(q[:, cols], keys) * scale - lse[:, h : h + 1]
         scores = jnp.concatenate(
-            [scores[:, 0:frames] + biases[0], scores[:, frames : 2 * frames] + biases[1]]
-            + [scores[:, 2 * frames :]],
+            [scores[:, 0:frames] + near_bias, scores[:, frames : 4 * frames]]
+            + [scores[:, 4 * frames :] + relay_bias],
             axis=1,
         )
-        dots = dot_nt(message[0:frames, cols], stacked(kvs, slice(frames, 2 * frames), cols))
+        dots = dot_nt(message[0:frames, cols], stacked(blocks, slice(frames, 2 * frames), cols))
         grads = (jnp.exp(scores) * (dots - delta[:, h : h + 1]) * scale).astype(BF16)
         held[:, cols] = dot_nn(grads, keys).astype(BF16)
     writes.append(pltpu.make_async_copy(held, grad_query, sems.at[2]))
@@ -369,12 +381,12 @@
         write.wait()
 
 
-def key_probs(scale, own, queries, biases, cols):
+def key_probs(scale, own, queries, messages, biases, cols):
     frames = own.shape[0] // 2
     scores = dot_nt(own[0:frames, cols], stacked(queries, slice(0, frames), cols)) * scale
     parts = []
     for b, bias in enumerate(biases):
-        part = scores[:, b * frames : (b + 1) * frames] - terms_of(queries[b], frames, cols)
+        part = scores[:, b * frames : (b + 1) * frames] - terms_of(messages[b], frames, 0, cols)
         parts.append(jnp.exp(part if bias is None else part + bias))
     return jnp.concatenate(parts, axis=1)
 
@@ -387,32 +399,36 @@
 def key_terms(scale, own, probs, queries, messages, cols):
     frames = own.shape[0] // 2
     dots = dot_nt(own[frames : 2 * frames, cols], stacked(messages, slice(0, frames), cols))
-    deltas = jnp.concatenate([terms_of(m, frames, cols) for m in messages], axis=1)
+    deltas = jnp.concatenate([terms_of(m, frames, 1, cols) for m in messages], axis=1)
     grads = (probs * (dots - deltas) * scale).astype(BF16)
     return dot_nn(grads, stacked(queries, slice(0, frames), cols))
 
 
 def key_part_body(scale, flags, own, *refs):
     queries, late_query, messages, (key_part, value_part, late) = refs[0:4], refs[4], refs[5:9], refs[9:12]
+    frames = own.shape[0] // 2
     biases = (None, off_bias(flags[1]), None, None)
+    late_bias = off_bias(flags[2])
     for h in range(own.shape[1] // HDIM):
         cols = head_cols(h)
-        probs = key_probs(scale, own, queries, biases, cols)
+        probs = key_probs(scale, own, queries, messages, biases, cols)
         value_part[:, cols] = value_terms(probs, messages, cols)
         key_part[:, cols] = key_terms(scale, own, probs, queries, messages, cols)
-        late[:, cols] = key_probs(scale, own, (late_query,), (off_bias(flags[2]),), cols)
+        late[:, cols] = dot_nt(own[0:frames, cols], late_query[:, cols]) * scale + late_bias
 
 
 def key_grad_body(
     scale, own, query, message, late, key_part, value_part, grad_key, grad_value, held_key, held_value, sems
 ):
+    frames = own.shape[0] // 2
     heads = [head_cols(h) for h in range(own.shape[1] // HDIM)]
-    for cols in heads:
-        held_value[:, cols] = (value_part[:, cols] + value_terms(late[:, cols], (message,), cols)).astype(BF16)
+    probs = [jnp.exp(late[:, cols] - terms_of(message, frames, 0, cols)) for cols in heads]
+    for cols, prob in zip(heads, probs):
+        held_value[:, cols] = (value_part[:, cols] + value_terms(prob, (message,), cols)).astype(BF16)
     value_write = pltpu.make_async_copy(held_value, grad_value, sems.at[0])
     value_write.start()
-    for cols in heads:
-        keys = key_terms(scale, own, late[:, cols], (query,), (message,), cols)
+    for cols, prob in zip(heads, probs):
+        keys = key_terms(scale, own, prob, (query,), (message,), cols)
         held_key[:, cols] = (key_part[:, cols] + keys).astype(BF16)
     key_write = pltpu.make_async_copy(held_key, grad_key, sems.at[1])
     key_write.start()
@@ -422,7 +438,6 @@
 
 def per_device(query_rows, key_rows, value_rows, inputs, out_weight, kernel, cotangent):
     frames, width = query_rows.shape
-    whole = out_weight.shape[1]
     wide = 2 * HALO
     scale = 1.0 / math.sqrt(HDIM)
     block, count = lax.axis_index("ctx"), lax.axis_size("ctx")
@@ -433,43 +448,48 @@
     ).astype(jnp.int32)
     tile = shaped((frames, width), BF16)
     tile32 = shaped((frames, width), F32)
-    half = shaped((frames, 2 * width), BF16)
     side = shaped((frames, HDIM), F32)
     rim = shaped((wide + HALO, width), BF16)
     noted = shaped((frames + 16, width), BF16)
-    square = frames * frames * width
 
     zero = jnp.zeros((), BF16)
     kv = lax.pad(key_rows, zero, ((0, frames, 0), (0, 0, 0))) + lax.pad(
         value_rows, zero, ((frames, 0, 0), (0, 0, 0))
     )
     near, first, second, relay = window_of(kv)
-    (weight,) = kernel_call(
-        fetch_body, (shaped(out_weight.shape, BF16),), (out_weight, second), 0, "fetch",
-        [HBM, ANY], [pltpu.SemaphoreType.DMA(())],
-    )
+    (q_early,) = kernel_call(hold_body, (tile,), (query_rows, second), 0.3, "hold", [VMEM, ANY])
+    q_second = ring(q_early, 1)
+    q_first = ring(q_early, 0)
     sums, tops, totals = kernel_call(
         functools.partial(forward_body, scale),
         (tile32, side, side),
-        (flags, query_rows, kv, near, first, second),
-        16 * square, "forward",
-    )
-    att, lse, send, keep, q_own = kernel_call(
+        (flags, q_early, kv, near, first, second),
+        1.7, "forward",
+    )
+    att, lse, send, keep = kernel_call(
         functools.partial(project_body, scale),
-        (tile, side, half, half, noted),
-        (flags, query_rows, relay, sums, tops, totals, weight),
-        4 * square + 2 * frames * width * whole, "project",
+        (tile, side, tile, tile),
+        (flags, q_early, relay, sums, tops, totals, out_weight),
+        1.8, "project",
     )
 
     core = pair_swap(send, "mp", 1)
-    across = pair_swap(keep[:, 0:width] + core[:, 0:width], "mp", 2)
-    q_second = ring(q_own, 1)
-    q_first = ring(q_own, 0)
+    own_send, own_keep = kernel_call(
+        project_own_body, (tile, tile), (flags, att, out_weight, q_second, q_first), 0.9,
+        "project_own", [SMEM] + [VMEM] * 2 + [ANY] * 2,
+    )
+    outgoing, q_own, q_handed = kernel_call(
+        join_body, (tile, tile, tile), (keep, core, q_early, q_second), 0.3, "join", [VMEM] * 4
+    )
+    across = pair_swap(outgoing, "mp", 2)
+    own_core = pair_swap(own_send, "mp", 1)
+    q_near = inner_swap(q_own)
+    q_relay = pair_swap(q_handed, "ctx", 1)
     hidden, rim_up, rim_down = kernel_call(
         hidden_body,
         (tile, rim, rim),
-        (flags, inputs, keep, core, across, cotangent, q_second, q_first),
-        4 * frames * width, "hidden", [SMEM] + [VMEM] * 5 + [ANY] * 2,
+        (flags, inputs, own_keep, own_core, across, cotangent, q_near, q_relay),
+        0.6, "hidden", [SMEM] + [VMEM] * 5 + [ANY] * 2,
     )
 
     rim_far = outer_swap(rim_down)
@@ -478,53 +498,53 @@
         conv_inner_body,
         (tile, shaped((2 * wide, width), F32), tile32),
         (hidden, cotangent, kernel),
-        140 * frames * width, "conv_inner", [VMEM] * 3,
+        1.6, "conv_inner", [VMEM] * 3,
         [pltpu.VMEM((frames + 2 * wide, width), F32), pltpu.VMEM((frames + wide, width), F32)],
     )
     output_here, grad_here = kernel_call(
         conv_edge_body,
         (tile, tile),
         (flags, hidden, rim_near, rim_far, cotangent, kernel, rows_out, edge_conv, part_grad),
-        70 * frames * width, "conv_edge", None,
+        1.3, "conv_edge", None,
         [pltpu.VMEM((3 * wide, width), F32), pltpu.VMEM((3 * wide, width), F32)],
     )
 
     gi_across = pair_swap(grad_here, "mp", 2)
     gi_core = pair_swap(grad_here, "mp", 1)
-    q_near = inner_swap(q_own)
-    q_relay = pair_swap(q_second, "ctx", 1)
     gi_cross = pair_swap(gi_across, "mp", 1)
     (partial,) = kernel_call(
-        upstream_chip_body, (tile32,), (flags, grad_here, gi_core, weight),
-        frames * width * whole, "upstream_chip",
+        upstream_chip_body, (tile32,), (flags, grad_here, gi_core, out_weight), 1.0, "upstream_chip"
+    )
+    (partial,) = kernel_call(
+        upstream_across_body, (tile32,), (flags, gi_across, out_weight, partial), 0.6, "upstream_across"
     )
     message, delta = kernel_call(
         upstream_body,
         (noted, side),
-        (flags, gi_across, gi_cross, weight, att, partial, q_near, q_relay),
-        frames * width * whole, "upstream", [SMEM] + [VMEM] * 5 + [ANY] * 2,
+        (flags, gi_cross, out_weight, att, lse, partial),
+        0.9, "upstream",
     )
 
     m_near, m_first, m_second, m_relay = window_of(message)
     output, grad_input, grad_query = kernel_call(
         functools.partial(query_grad_body, scale),
         (tile, tile, tile),
-        (flags, query_rows, kv, near, first, second, relay, message, lse, delta)
-        + (output_here, grad_here),
-        30 * square, "query_grad", None,
+        (flags, q_own, kv, near, first, second, relay)
+        + (message, lse, delta, output_here, grad_here),
+        2.3, "query_grad", None,
         [pltpu.VMEM((frames, width), BF16), pltpu.SemaphoreType.DMA((3,))], 24, HBM,
     )
     key_part, value_part, late = kernel_call(
         functools.partial(key_part_body, scale),
         (tile32, tile32, tile32),
         (flags, kv, q_own, q_near, q_first, q_second, q_relay, message, m_near, m_first, m_second),
-        34 * square, "key_part",
+        2.2, "key_part",
     )
     grad_key, grad_value = kernel_call(
         functools.partial(key_grad_body, scale),
         (tile, tile),
         (kv, q_relay, m_relay, late, key_part, value_part),
-        6 * square, "key_grad", [VMEM] * 6,
+        1.5, "key_grad", [VMEM] * 6,
         [pltpu.VMEM((frames, width), BF16)] * 2 + [pltpu.SemaphoreType.DMA((2,))], 24, HBM,
     )
     return (output, grad_input, grad_query, grad_key, grad_value)

time: 58.8 us -> 61.9 us (1.053)
  waiting for transfers between devices: 14.8 us -> 22.7 us
  starting transfers between devices: 23.5 us -> 18.7 us
  local copies, waits for them, and re-layouts: 2.31 us -> 0.93 us
  Pallas kernels: 16.1 us -> 17.4 us
    ppermute x9 -> x10, waiting for transfers between devices: 7.33 us -> 12.2 us  [pair_swap(): lax.ppermute(block, axis, [(i, i ^ bit) for i in range(lax.axis_size(axis...]
    ppermute x6, waiting for transfers between devices: 7.5 us -> 10.5 us  [ring(): return lax.ppermute(block, 'ctx', ring_routes(lax.axis_size('ctx'))[way])]
    ppermute x9 -> x10, starting transfers between devices: 10.5 us -> 7.76 us  [pair_swap(): lax.ppermute(block, axis, [(i, i ^ bit) for i in range(lax.axis_size(axis...]
    ppermute x6, starting transfers between devices: 13 us -> 10.7 us  [ring(): return lax.ppermute(block, 'ctx', ring_routes(lax.axis_size('ctx'))[way])]
    unnamed x10, local copies, waits for them, and re-layouts: 2.31 us -> 0.93 us
    pallas_call x11 -> x14, Pallas kernels: 16.1 us -> 17.4 us  [kernel_call(): pl.pallas_call(body, out_shape=outs, in_specs=spaces or [SMEM] + [VMEM] *...]
  transfers between devices with their start and end apart: 19 -> 20, of which waited for: 10 -> 8; matrix products, arithmetic and copies ran while one was open for 0% -> 0% of each run, Pallas kernels for 15% -> 21%
where the time goes in v4:
time: 61.9 us; the launch traced here: 61.7 us
  waiting for transfers between devices  22.7 us (37%)
  starting transfers between devices  18.7 us (30%)
  Pallas kernels  17.4 us (28%)
  other arithmetic  1.21 us (2%)
  local copies, waits for them, and re-layouts  0.93 us (2%)
  between operations  0.82 us (1%)
    pallas_call x14, Pallas kernels, kernel_call(): pl.pallas_call(body, out_shape=outs, in_specs=spaces or [SMEM] + [VMEM] *...  17.4 us
    ppermute x10, waiting for transfers between devices, pair_swap(): lax.ppermute(block, axis, [(i, i ^ bit) for i in range(lax.axis_size(axis...  12.2 us
    ppermute x6, starting transfers between devices, ring(): return lax.ppermute(block, 'ctx', ring_routes(lax.axis_size('ctx'))[way])  10.7 us
    ppermute x6, waiting for transfers between devices, ring(): return lax.ppermute(block, 'ctx', ring_routes(lax.axis_size('ctx'))[way])  10.5 us
    ppermute x10, starting transfers between devices, pair_swap(): lax.ppermute(block, axis, [(i, i ^ bit) for i in range(lax.axis_size(axis...  7.76 us
  transfers between devices with their start and end apart: 20, of which 8 were waited for; matrix products, arithmetic and copies ran while one was open for 0% of the time, Pallas kernels for 21%

profile of v4, /device:TPU:0, one launch (start us, length us, event | category | flops | bytes accessed | tf_op | source)
XLA Modules:
  0.0 61.7 jit_solution(14878416656335919846)
XLA Ops:
  0.6 0.0 copy-start
  0.6 1.1 %pad_add_fusion.own = bf16[256,512]{1,0:T(8,128)(2,1)S(1)} fusion(bf16[128,512]{1,0:T(8,128)(2,1)} %param.9, bf16[128,512]{1,0:T(8,128)(2,1)} %param.8), kind=kLoop, calls=%fused_computation | loop fusion | flops 524288 | bytes 524288 | tf_op jit(solution)/shard_map/add | solution.py:456
  1.8 3.0 %collective-permute-start = (bf16[256,512]{1,0:T(8,128)(2,1)S(1)}, bf16[256,512]{1,0:T(8,128)(2,1)S(1)}, u32[]{:S(2)}, u32[]{:S(2)}) collective-permute-start(bf16[256,512]{1,0:T(8,128)(2,1)S(1)} %pad_add_fusion.own), channel_id=1, source_target_pairs={{8,0},{16,8},{24,16},{28,24},{20,28},{12,20},{4,12},{0,4},{9,1},{1... | collective-permute-start | bytes 786440 | tf_op jit(solution)/shard_map/ppermute | solution.py:39
  4.8 0.2 collective-permute-start.3
  4.9 0.0 collective-permute-start.2
  4.9 6.2 %collective-permute-done.seen.second = bf16[256,512]{1,0:T(8,128)(2,1)S(1)} collective-permute-done((bf16[256,512]{1,0:T(8,128)(2,1)S(1)}, bf16[256,512]{1,0:T(8,128)(2,1)S(1)}, u32[]{:S(2)}, u32[]{:S(2)}) %collective-permute-start) | collective-permute-done | bytes 262176 | tf_op jit(solution)/shard_map/ppermute | solution.py:39
  11.2 1.7 %collective-permute-start.1 = (bf16[256,512]{1,0:T(8,128)(2,1)S(1)}, bf16[256,512]{1,0:T(8,128)(2,1)S(1)}, u32[]{:S(2)}, u32[]{:S(2)}) collective-permute-start(bf16[256,512]{1,0:T(8,128)(2,1)S(1)} %collective-permute-done.seen.second), channel_id=1, source_target_pairs={{0,4},{4,0},{8,12},{12,8},{16,20},{20,16},{24,28},{28,24},{1,5},{5... | collective-permute-start | bytes 786440 | tf_op jit(solution)/shard_map/ppermute | solution.py:28
  12.8 0.1 pad_add_fusion.1.flags
  12.9 0.0 copy-start.4
  12.9 0.9 %copy-done.4 = bf16[128,512]{1,0:T(8,128)(2,1)S(1)} copy-done((bf16[128,512]{1,0:T(8,128)(2,1)S(1)}, bf16[128,512]{1,0:T(8,128)(2,1)}, u32[]{:S(2)}) %copy-start.4) | copy-done | bytes 131096
  13.8 1.6 %collective-permute-start.6 = (bf16[128,512]{1,0:T(8,128)(2,1)S(1)}, bf16[128,512]{1,0:T(8,128)(2,1)S(1)}, u32[]{:S(2)}, u32[]{:S(2)}) collective-permute-start(bf16[128,512]{1,0:T(8,128)(2,1)S(1)} %hold.1.q), channel_id=1, source_target_pairs={{0,8},{8,16},{16,24},{24,28},{28,20},{20,12},{12,4},{4,0},{1,9},{9... | collective-permute-start | bytes 393224 | tf_op jit(solution)/shard_map/ppermute | solution.py:39
  15.4 0.4 collective-permute-start.5
  15.9 0.0 collective-permute-done.3.first
  15.9 0.0 collective-permute-done.2.near
  15.9 1.7 %forward.1 = (f32[128,512]{1,0:T(8,128)S(1)}, f32[128,128]{1,0:T(8,128)S(1)}, f32[128,128]{1,0:T(8,128)S(1)}) custom-call(s32[4]{0:T(128)S(1)} %pad_add_fusion.1.flags, bf16[128,512]{1,0:T(8,128)(2,1)S(1)} %hold.1.q, bf16[256,512]{1,0:T(8,128)(2,1)S(1)} %pad_add_fusion.own, bf16[256,512]{1,0:T(8,128)(2,1)S(1)} %collective-permute-done.2.near, ...), custom_call_target="tpu_custom_call" | custom-call | bytes 6273000 | tf_op jit(solution)/shard_map/forward/pallas_call | solution.py:75
  17.6 2.4 %collective-permute-done.1.relay = bf16[256,512]{1,0:T(8,128)(2,1)S(1)} collective-permute-done((bf16[256,512]{1,0:T(8,128)(2,1)S(1)}, bf16[256,512]{1,0:T(8,128)(2,1)S(1)}, u32[]{:S(2)}, u32[]{:S(2)}) %collective-permute-start.1) | collective-permute-done | bytes 262176 | tf_op jit(solution)/shard_map/ppermute | solution.py:28
  20.1 0.0 copy-done
  20.1 2.3 %project.1 = (bf16[128,512]{1,0:T(8,128)(2,1)S(1)}, f32[128,128]{1,0:T(8,128)S(1)}, bf16[128,512]{1,0:T(8,128)(2,1)S(1)}, bf16[128,512]{1,0:T(8,128)(2,1)S(1)}) custom-call(s32[4]{0:T(128)S(1)} %pad_add_fusion.1.flags, bf16[128,512]{1,0:T(8,128)(2,1)S(1)} %hold.1.q, bf16[256,512]{1,0:T(8,128)(2,1)S(1)} %collective-permute-done.1.relay, ...), custom_call_target="tpu_custom_call" | custom-call | bytes 6642000 | tf_op jit(solution)/shard_map/project/pallas_call | solution.py:75
  22.4 0.0 copy-start.1
  22.4 0.0 copy-start.3
  22.4 0.0 copy-start.2
  22.4 0.1 collective-permute-start.4
  22.5 0.0 collective-permute-done.6.seen_b.refs_2_
  22.5 0.0 collective-permute-done.5.q_second.seen_a.refs_3_
  22.5 0.9 %project_own.1 = (bf16[128,512]{1,0:T(8,128)(2,1)S(1)}, bf16[128,512]{1,0:T(8,128)(2,1)S(1)}) custom-call(s32[4]{0:T(128)S(1)} %pad_add_fusion.1.flags, bf16[128,512]{1,0:T(8,128)(2,1)S(1)} %get-tuple-element.41.att, bf16[512,2048]{1,0:T(8,128)(2,1)S(1)} %copy-done, bf16[128,512]{1,0:T(8,128)(2,1)S(1)} %collective-permute-done.5.q_second.seen_a.refs_3_, ...), custom_call_target="tpu_custom_call" | custom-call | bytes 3321000 | tf_op jit(solution)/shard_map/project_own/pallas_call | solution.py:75
  23.4 0.5 collective-permute-start.7
  24.0 0.0 collective-permute-done.4.core
  24.0 1.4 %collective-permute-start.8 = (bf16[128,512]{1,0:T(8,128)(2,1)S(1)}, bf16[128,512]{1,0:T(8,128)(2,1)S(1)}, u32[]{:S(2)}, u32[]{:S(2)}) collective-permute-start(bf16[128,512]{1,0:T(8,128)(2,1)S(1)} %get-tuple-element.44), channel_id=1, source_target_pairs={{0,2},{1,3},{2,0},{3,1},{4,6},{5,7},{6,4},{7,5},{8,10},{9,11},{10,... | collective-permute-start | bytes 393224 | tf_op jit(solution)/shard_map/ppermute | solution.py:28
  25.5 1.5 %collective-permute-start.10 = (bf16[128,512]{1,0:T(8,128)(2,1)S(1)}, bf16[128,512]{1,0:T(8,128)(2,1)S(1)}, u32[]{:S(2)}, u32[]{:S(2)}) collective-permute-start(bf16[128,512]{1,0:T(8,128)(2,1)S(1)} %get-tuple-element.45), channel_id=1, source_target_pairs={{0,4},{4,0},{8,12},{12,8},{16,20},{20,16},{24,28},{28,24},{1,5},{5... | collective-permute-start | bytes 393224 | tf_op jit(solution)/shard_map/ppermute | solution.py:28
  26.9 0.0 collective-permute-start.9
  26.9 0.0 collective-permute-done.7.core
  26.9 2.6 %collective-permute-done.8.across = bf16[128,512]{1,0:T(8,128)(2,1)S(1)} collective-permute-done((bf16[128,512]{1,0:T(8,128)(2,1)S(1)}, bf16[128,512]{1,0:T(8,128)(2,1)S(1)}, u32[]{:S(2)}, u32[]{:S(2)}) %collective-permute-start.8) | collective-permute-done | bytes 131104 | tf_op jit(solution)/shard_map/ppermute | solution.py:28
  29.5 1.1 %collective-permute-done.10.seen_b.refs_4_.query = bf16[128,512]{1,0:T(8,128)(2,1)S(1)} collective-permute-done((bf16[128,512]{1,0:T(8,128)(2,1)S(1)}, bf16[128,512]{1,0:T(8,128)(2,1)S(1)}, u32[]{:S(2)}, u32[]{:S(2)}) %collective-permute-start.10) | collective-permute-done | bytes 131104 | tf_op jit(solution)/shard_map/ppermute | solution.py:28
  30.6 0.0 collective-permute-done.9.seen_a.refs_1_
  30.6 0.0 copy-done.1
  30.6 0.0 copy-done.3
  30.6 0.6 %hidden.1 = (bf16[128,512]{1,0:T(8,128)(2,1)S(1)}, bf16[48,512]{1,0:T(8,128)(2,1)S(1)}, bf16[48,512]{1,0:T(8,128)(2,1)S(1)}) custom-call(s32[4]{0:T(128)S(1)} %pad_add_fusion.1.flags, bf16[128,512]{1,0:T(8,128)(2,1)S(1)} %copy-done.3, bf16[128,512]{1,0:T(8,128)(2,1)S(1)} %get-tuple-element.42.keep, bf16[128,512]{1,0:T(8,128)(2,1)S(1)} %collective-permute-done.7.core, ...), custom_call_target="tpu_custom_call" | custom-call | bytes 2214000 | tf_op jit(solution)/shard_map/hidden/pallas_call | solution.py:75
  31.3 1.6 %collective-permute-start.11 = (bf16[48,512]{1,0:T(8,128)(2,1)S(1)}, bf16[48,512]{1,0:T(8,128)(2,1)S(1)}, u32[]{:S(2)}, u32[]{:S(2)}) collective-permute-start(bf16[48,512]{1,0:T(8,128)(2,1)S(1)} %get-tuple-element.47), channel_id=1, source_target_pairs={{0,4},{4,0},{8,12},{12,8},{16,20},{20,16},{24,28},{28,24},{1,5},{5... | collective-permute-start | bytes 147464 | tf_op jit(solution)/shard_map/ppermute | solution.py:28
  32.8 0.0 collective-permute-start.12
  32.8 0.0 copy-done.2
  32.8 1.6 %conv_inner.1 = (bf16[128,512]{1,0:T(8,128)(2,1)S(1)}, f32[64,512]{1,0:T(8,128)S(1)}, f32[128,512]{1,0:T(8,128)S(1)}) custom-call(bf16[128,512]{1,0:T(8,128)(2,1)S(1)} %get-tuple-element.46.hidden, bf16[128,512]{1,0:T(8,128)(2,1)S(1)} %copy-done.1, f32[31,512]{1,0:T(8,128)S(1)} %copy-done.2), custom_call_target="tpu_custom_call" | custom-call | bytes 5904000 | tf_op jit(solution)/shard_map/conv_inner/pallas_call | solution.py:75
  34.4 1.0 %collective-permute-done.11.rim_near = bf16[48,512]{1,0:T(8,128)(2,1)S(1)} collective-permute-done((bf16[48,512]{1,0:T(8,128)(2,1)S(1)}, bf16[48,512]{1,0:T(8,128)(2,1)S(1)}, u32[]{:S(2)}, u32[]{:S(2)}) %collective-permute-start.11) | collective-permute-done | bytes 49184 | tf_op jit(solution)/shard_map/ppermute | solution.py:28
  35.4 0.0 collective-permute-done.12.rim_far
  35.4 1.3 %conv_edge.1 = (bf16[128,512]{1,0:T(8,128)(2,1)S(1)}, bf16[128,512]{1,0:T(8,128)(2,1)S(1)}) custom-call(s32[4]{0:T(128)S(1)} %pad_add_fusion.1.flags, bf16[128,512]{1,0:T(8,128)(2,1)S(1)} %get-tuple-element.46.hidden, bf16[48,512]{1,0:T(8,128)(2,1)S(1)} %collective-permute-done.11.rim_near, bf16[48,512]{1,0:T(8,128)(2,1)S(1)} %collective-permute-done.12.rim_far, ...), custom_call_target="tpu_custom_call" | custom-call | bytes 4797000 | tf_op jit(solution)/shard_map/conv_edge/pallas_call | solution.py:75
  36.7 0.7 %collective-permute-start.13 = (bf16[128,512]{1,0:T(8,128)(2,1)S(1)}, bf16[128,512]{1,0:T(8,128)(2,1)S(1)}, u32[]{:S(2)}, u32[]{:S(2)}) collective-permute-start(bf16[128,512]{1,0:T(8,128)(2,1)S(1)} %get-tuple-element.52.own.grad_here), channel_id=1, source_target_pairs={{0,2},{1,3},{2,0},{3,1},{4,6},{5,7},{6,4},{7,5},{8,10},{9,11},{10,... | collective-permute-start | bytes 393224 | tf_op jit(solution)/shard_map/ppermute | solution.py:28
  37.4 0.0 collective-permute-start.15
  37.4 4.3 %collective-permute-done.13.across = bf16[128,512]{1,0:T(8,128)(2,1)S(1)} collective-permute-done((bf16[128,512]{1,0:T(8,128)(2,1)S(1)}, bf16[128,512]{1,0:T(8,128)(2,1)S(1)}, u32[]{:S(2)}, u32[]{:S(2)}) %collective-permute-start.13) | collective-permute-done | bytes 131104 | tf_op jit(solution)/shard_map/ppermute | solution.py:28
  41.7 0.0 collective-permute-start.14
  41.7 0.0 collective-permute-done.15.core
  41.7 1.0 %upstream_chip.1.before = f32[128,512]{1,0:T(8,128)S(1)} custom-call(s32[4]{0:T(128)S(1)} %pad_add_fusion.1.flags, bf16[128,512]{1,0:T(8,128)(2,1)S(1)} %get-tuple-element.52.own.grad_here, bf16[128,512]{1,0:T(8,128)(2,1)S(1)} %collective-permute-done.15.core, bf16[512,2048]{1,0:T(8,128)(2,1)S(1)} %copy-done), custom_call_target="tpu_custom_call" | custom-call | bytes 3690000 | tf_op jit(solution)/shard_map/upstream_chip/pallas_call | solution.py:75
  42.8 0.9 %upstream_across.1.partial = f32[128,512]{1,0:T(8,128)S(1)} custom-call(s32[4]{0:T(128)S(1)} %pad_add_fusion.1.flags, bf16[128,512]{1,0:T(8,128)(2,1)S(1)} %collective-permute-done.13.across, bf16[512,2048]{1,0:T(8,128)(2,1)S(1)} %copy-done, f32[128,512]{1,0:T(8,128)S(1)} %upstream_chip.1.before), custom_call_target="tpu_custom_call" | custom-call | bytes 2214000 | tf_op jit(solution)/shard_map/upstream_across/pallas_call | solution.py:75
  43.6 0.0 collective-permute-done.14.cross
  43.6 1.0 %upstream.1 = (bf16[144,512]{1,0:T(8,128)(2,1)S(1)}, f32[128,128]{1,0:T(8,128)S(1)}) custom-call(s32[4]{0:T(128)S(1)} %pad_add_fusion.1.flags, bf16[128,512]{1,0:T(8,128)(2,1)S(1)} %collective-permute-done.14.cross, bf16[512,2048]{1,0:T(8,128)(2,1)S(1)} %copy-done, bf16[128,512]{1,0:T(8,128)(2,1)S(1)} %get-tuple-element.41.att, ...), custom_call_target="tpu_custom_call" | custom-call | bytes 3321000 | tf_op jit(solution)/shard_map/upstream/pallas_call | solution.py:75
  44.7 3.9 %collective-permute-start.16 = (bf16[144,512]{1,0:T(8,128)(2,1)S(1)}, bf16[144,512]{1,0:T(8,128)(2,1)S(1)}, u32[]{:S(2)}, u32[]{:S(2)}) collective-permute-start(bf16[144,512]{1,0:T(8,128)(2,1)S(1)} %get-tuple-element.54.message.refs_5_), channel_id=1, source_target_pairs={{8,0},{16,8},{24,16},{28,24},{20,28},{12,20},{4,12},{0,4},{9,1},{1... | collective-permute-start | bytes 442376 | tf_op jit(solution)/shard_map/ppermute | solution.py:39
  48.6 1.5 %collective-permute-start.19 = (bf16[144,512]{1,0:T(8,128)(2,1)S(1)}, bf16[144,512]{1,0:T(8,128)(2,1)S(1)}, u32[]{:S(2)}, u32[]{:S(2)}) collective-permute-start(bf16[144,512]{1,0:T(8,128)(2,1)S(1)} %get-tuple-element.54.message.refs_5_), channel_id=1, source_target_pairs={{0,8},{8,16},{16,24},{24,28},{28,20},{20,12},{12,4},{4,0},{1,9},{9... | collective-permute-start | bytes 442376 | tf_op jit(solution)/shard_map/ppermute | solution.py:39
  50.1 0.2 collective-permute-start.18
  50.4 4.2 %collective-permute-done.16.refs_8_ = bf16[144,512]{1,0:T(8,128)(2,1)S(1)} collective-permute-done((bf16[144,512]{1,0:T(8,128)(2,1)S(1)}, bf16[144,512]{1,0:T(8,128)(2,1)S(1)}, u32[]{:S(2)}, u32[]{:S(2)}) %collective-permute-start.16) | collective-permute-done | bytes 147488 | tf_op jit(solution)/shard_map/ppermute | solution.py:39
  54.6 0.3 collective-permute-start.17
  54.9 2.4 %query_grad.1 = (bf16[128,512]{1,0:T(8,128)(2,1)}, bf16[128,512]{1,0:T(8,128)(2,1)}, bf16[128,512]{1,0:T(8,128)(2,1)}) custom-call(s32[4]{0:T(128)S(1)} %pad_add_fusion.1.flags, bf16[128,512]{1,0:T(8,128)(2,1)S(1)} %get-tuple-element.40.q.refs_0_, bf16[256,512]{1,0:T(8,128)(2,1)S(1)} %pad_add_fusion.own, bf16[256,512]{1,0:T(8,128)(2,1)S(1)} %collective-permute-done.2.near, ...), custom_call_target="tpu_custom_call" | custom-call | bytes 8487000 | tf_op jit(solution)/shard_map/query_grad/pallas_call | solution.py:75
  57.2 0.0 collective-permute-done.19.refs_7_
  57.3 0.0 collective-permute-done.18.refs_6_
  57.3 2.1 %key_part.1 = (f32[128,512]{1,0:T(8,128)S(1)}, f32[128,512]{1,0:T(8,128)S(1)}, f32[128,512]{1,0:T(8,128)S(1)}) custom-call(s32[4]{0:T(128)S(1)} %pad_add_fusion.1.flags, bf16[256,512]{1,0:T(8,128)(2,1)S(1)} %pad_add_fusion.own, bf16[128,512]{1,0:T(8,128)(2,1)S(1)} %get-tuple-element.40.q.refs_0_, bf16[128,512]{1,0:T(8,128)(2,1)S(1)} %collective-permute-done.9.seen_a.refs_1_, ...), custom_call_target="tpu_custom_call" | custom-call | bytes 8118000 | tf_op jit(solution)/shard_map/key_part/pallas_call | solution.py:75
  59.4 0.8 %collective-permute-done.17.message = bf16[144,512]{1,0:T(8,128)(2,1)S(1)} collective-permute-done((bf16[144,512]{1,0:T(8,128)(2,1)S(1)}, bf16[144,512]{1,0:T(8,128)(2,1)S(1)}, u32[]{:S(2)}, u32[]{:S(2)}) %collective-permute-start.17) | collective-permute-done | bytes 147488 | tf_op jit(solution)/shard_map/ppermute | solution.py:28
  60.3 1.5 %key_grad.1 = (bf16[128,512]{1,0:T(8,128)(2,1)}, bf16[128,512]{1,0:T(8,128)(2,1)}) custom-call(bf16[256,512]{1,0:T(8,128)(2,1)S(1)} %pad_add_fusion.own, bf16[128,512]{1,0:T(8,128)(2,1)S(1)} %collective-permute-done.10.seen_b.refs_4_.query, bf16[144,512]{1,0:T(8,128)(2,1)S(1)} %collective-permute-done.17.message, f32[128,512]{1,0:T(8,128)S(1)} %get-tuple-element.60.late, ...), custom_call_target="tpu_custom_call" | custom-call | bytes 5535000 | tf_op jit(solution)/shard_map/key_grad/pallas_call | solution.py:75
  (2 shorter events, 0.0 us)
Async XLA Ops:
  0.6 19.4 %copy-start = (bf16[512,2048]{1,0:T(8,128)(2,1)S(1)}, bf16[512,2048]{1,0:T(8,128)(2,1)}, u32[]{:S(2)}) copy-start(bf16[512,2048]{1,0:T(8,128)(2,1)} %weight.9) | copy-start | bytes 6291460
  1.8 9.4 %collective-permute-start = (bf16[256,512]{1,0:T(8,128)(2,1)S(1)}, bf16[256,512]{1,0:T(8,128)(2,1)S(1)}, u32[]{:S(2)}, u32[]{:S(2)}) collective-permute-start(bf16[256,512]{1,0:T(8,128)(2,1)S(1)} %pad_add_fusion.own), channel_id=1, source_target_pairs={{8,0},{16,8},{24,16},{28,24},{20,28},{12,20},{4,12},{0,4},{9,1},{1... | collective-permute-start | bytes 786440 | tf_op jit(solution)/shard_map/ppermute | solution.py:39
  4.8 11.1 %collective-permute-start.3 = (bf16[256,512]{1,0:T(8,128)(2,1)S(1)}, bf16[256,512]{1,0:T(8,128)(2,1)S(1)}, u32[]{:S(2)}, u32[]{:S(2)}) collective-permute-start(bf16[256,512]{1,0:T(8,128)(2,1)S(1)} %pad_add_fusion.own), channel_id=1, source_target_pairs={{0,8},{8,16},{16,24},{24,28},{28,20},{20,12},{12,4},{4,0},{1,9},{9... | collective-permute-start | bytes 786440 | tf_op jit(solution)/shard_map/ppermute | solution.py:39
  4.9 11.0 %collective-permute-start.2 = (bf16[256,512]{1,0:T(8,128)(2,1)S(1)}, bf16[256,512]{1,0:T(8,128)(2,1)S(1)}, u32[]{:S(2)}, u32[]{:S(2)}) collective-permute-start(bf16[256,512]{1,0:T(8,128)(2,1)S(1)} %pad_add_fusion.own), channel_id=1, source_target_pairs={{0,1},{1,0},{2,3},{3,2},{4,5},{5,4},{6,7},{7,6},{8,12},{9,13},{10,... | collective-permute-start | bytes 786440 | tf_op jit(solution)/shard_map/ppermute | solution.py:50
  11.2 8.9 %collective-permute-start.1 = (bf16[256,512]{1,0:T(8,128)(2,1)S(1)}, bf16[256,512]{1,0:T(8,128)(2,1)S(1)}, u32[]{:S(2)}, u32[]{:S(2)}) collective-permute-start(bf16[256,512]{1,0:T(8,128)(2,1)S(1)} %collective-permute-done.seen.second), channel_id=1, source_target_pairs={{0,4},{4,0},{8,12},{12,8},{16,20},{20,16},{24,28},{28,24},{1,5},{5... | collective-permute-start | bytes 786440 | tf_op jit(solution)/shard_map/ppermute | solution.py:28
  12.9 0.9 %copy-start.4 = (bf16[128,512]{1,0:T(8,128)(2,1)S(1)}, bf16[128,512]{1,0:T(8,128)(2,1)}, u32[]{:S(2)}) copy-start(bf16[128,512]{1,0:T(8,128)(2,1)} %block.1) | copy-start | bytes 393220
  13.8 8.7 %collective-permute-start.6 = (bf16[128,512]{1,0:T(8,128)(2,1)S(1)}, bf16[128,512]{1,0:T(8,128)(2,1)S(1)}, u32[]{:S(2)}, u32[]{:S(2)}) collective-permute-start(bf16[128,512]{1,0:T(8,128)(2,1)S(1)} %hold.1.q), channel_id=1, source_target_pairs={{0,8},{8,16},{16,24},{24,28},{28,20},{20,12},{12,4},{4,0},{1,9},{9... | collective-permute-start | bytes 393224 | tf_op jit(solution)/shard_map/ppermute | solution.py:39
  15.4 7.1 %collective-permute-start.5 = (bf16[128,512]{1,0:T(8,128)(2,1)S(1)}, bf16[128,512]{1,0:T(8,128)(2,1)S(1)}, u32[]{:S(2)}, u32[]{:S(2)}) collective-permute-start(bf16[128,512]{1,0:T(8,128)(2,1)S(1)} %hold.1.q), channel_id=1, source_target_pairs={{8,0},{16,8},{24,16},{28,24},{20,28},{12,20},{4,12},{0,4},{9,1},{1... | collective-permute-start | bytes 393224 | tf_op jit(solution)/shard_map/ppermute | solution.py:39
  22.4 8.2 %copy-start.1 = (bf16[128,512]{1,0:T(8,128)(2,1)S(1)}, bf16[128,512]{1,0:T(8,128)(2,1)}, u32[]{:S(2)}) copy-start(bf16[128,512]{1,0:T(8,128)(2,1)} %cot.5) | copy-start | bytes 393220
  22.4 8.2 %copy-start.3 = (bf16[128,512]{1,0:T(8,128)(2,1)S(1)}, bf16[128,512]{1,0:T(8,128)(2,1)}, u32[]{:S(2)}) copy-start(bf16[128,512]{1,0:T(8,128)(2,1)} %inputs.1) | copy-start | bytes 393220
  22.4 10.4 %copy-start.2 = (f32[31,512]{1,0:T(8,128)S(1)}, f32[31,512]{1,0:T(8,128)}, u32[]{:S(2)}) copy-start(f32[31,512]{1,0:T(8,128)} %taps.3) | copy-start | bytes 190468
  22.4 1.5 %collective-permute-start.4 = (bf16[128,512]{1,0:T(8,128)(2,1)S(1)}, bf16[128,512]{1,0:T(8,128)(2,1)S(1)}, u32[]{:S(2)}, u32[]{:S(2)}) collective-permute-start(bf16[128,512]{1,0:T(8,128)(2,1)S(1)} %get-tuple-element.39), channel_id=1, source_target_pairs={{0,1},{1,0},{2,3},{3,2},{4,5},{5,4},{6,7},{7,6},{8,9},{9,8},{10,11... | collective-permute-start | bytes 393224 | tf_op jit(solution)/shard_map/ppermute | solution.py:28
  23.4 3.5 %collective-permute-start.7 = (bf16[128,512]{1,0:T(8,128)(2,1)S(1)}, bf16[128,512]{1,0:T(8,128)(2,1)S(1)}, u32[]{:S(2)}, u32[]{:S(2)}) collective-permute-start(bf16[128,512]{1,0:T(8,128)(2,1)S(1)} %get-tuple-element.43), channel_id=1, source_target_pairs={{0,1},{1,0},{2,3},{3,2},{4,5},{5,4},{6,7},{7,6},{8,9},{9,8},{10,11... | collective-permute-start | bytes 393224 | tf_op jit(solution)/shard_map/ppermute | solution.py:28
  24.0 5.5 %collective-permute-start.8 = (bf16[128,512]{1,0:T(8,128)(2,1)S(1)}, bf16[128,512]{1,0:T(8,128)(2,1)S(1)}, u32[]{:S(2)}, u32[]{:S(2)}) collective-permute-start(bf16[128,512]{1,0:T(8,128)(2,1)S(1)} %get-tuple-element.44), channel_id=1, source_target_pairs={{0,2},{1,3},{2,0},{3,1},{4,6},{5,7},{6,4},{7,5},{8,10},{9,11},{10,... | collective-permute-start | bytes 393224 | tf_op jit(solution)/shard_map/ppermute | solution.py:28
  25.5 5.2 %collective-permute-start.10 = (bf16[128,512]{1,0:T(8,128)(2,1)S(1)}, bf16[128,512]{1,0:T(8,128)(2,1)S(1)}, u32[]{:S(2)}, u32[]{:S(2)}) collective-permute-start(bf16[128,512]{1,0:T(8,128)(2,1)S(1)} %get-tuple-element.45), channel_id=1, source_target_pairs={{0,4},{4,0},{8,12},{12,8},{16,20},{20,16},{24,28},{28,24},{1,5},{5... | collective-permute-start | bytes 393224 | tf_op jit(solution)/shard_map/ppermute | solution.py:28
  26.9 3.7 %collective-permute-start.9 = (bf16[128,512]{1,0:T(8,128)(2,1)S(1)}, bf16[128,512]{1,0:T(8,128)(2,1)S(1)}, u32[]{:S(2)}, u32[]{:S(2)}) collective-permute-start(bf16[128,512]{1,0:T(8,128)(2,1)S(1)} %get-tuple-element.40.q.refs_0_), channel_id=1, source_target_pairs={{0,1},{1,0},{2,3},{3,2},{4,5},{5,4},{6,7},{7,6},{8,12},{9,13},{10,... | collective-permute-start | bytes 393224 | tf_op jit(solution)/shard_map/ppermute | solution.py:50
  31.3 4.2 %collective-permute-start.11 = (bf16[48,512]{1,0:T(8,128)(2,1)S(1)}, bf16[48,512]{1,0:T(8,128)(2,1)S(1)}, u32[]{:S(2)}, u32[]{:S(2)}) collective-permute-start(bf16[48,512]{1,0:T(8,128)(2,1)S(1)} %get-tuple-element.47), channel_id=1, source_target_pairs={{0,4},{4,0},{8,12},{12,8},{16,20},{20,16},{24,28},{28,24},{1,5},{5... | collective-permute-start | bytes 147464 | tf_op jit(solution)/shard_map/ppermute | solution.py:28
  32.8 2.6 %collective-permute-start.12 = (bf16[48,512]{1,0:T(8,128)(2,1)S(1)}, bf16[48,512]{1,0:T(8,128)(2,1)S(1)}, u32[]{:S(2)}, u32[]{:S(2)}) collective-permute-start(bf16[48,512]{1,0:T(8,128)(2,1)S(1)} %get-tuple-element.48), channel_id=1, source_target_pairs={{0,1},{1,0},{2,3},{3,2},{4,8},{5,9},{6,10},{7,11},{8,4},{9,5},{10,... | collective-permute-start | bytes 147464 | tf_op jit(solution)/shard_map/ppermute | solution.py:50
  36.7 5.0 %collective-permute-start.13 = (bf16[128,512]{1,0:T(8,128)(2,1)S(1)}, bf16[128,512]{1,0:T(8,128)(2,1)S(1)}, u32[]{:S(2)}, u32[]{:S(2)}) collective-permute-start(bf16[128,512]{1,0:T(8,128)(2,1)S(1)} %get-tuple-element.52.own.grad_here), channel_id=1, source_target_pairs={{0,2},{1,3},{2,0},{3,1},{4,6},{5,7},{6,4},{7,5},{8,10},{9,11},{10,... | collective-permute-start | bytes 393224 | tf_op jit(solution)/shard_map/ppermute | solution.py:28
  37.4 4.3 %collective-permute-start.15 = (bf16[128,512]{1,0:T(8,128)(2,1)S(1)}, bf16[128,512]{1,0:T(8,128)(2,1)S(1)}, u32[]{:S(2)}, u32[]{:S(2)}) collective-permute-start(bf16[128,512]{1,0:T(8,128)(2,1)S(1)} %get-tuple-element.52.own.grad_here), channel_id=1, source_target_pairs={{0,1},{1,0},{2,3},{3,2},{4,5},{5,4},{6,7},{7,6},{8,9},{9,8},{10,11... | collective-permute-start | bytes 393224 | tf_op jit(solution)/shard_map/ppermute | solution.py:28
  41.7 1.9 %collective-permute-start.14 = (bf16[128,512]{1,0:T(8,128)(2,1)S(1)}, bf16[128,512]{1,0:T(8,128)(2,1)S(1)}, u32[]{:S(2)}, u32[]{:S(2)}) collective-permute-start(bf16[128,512]{1,0:T(8,128)(2,1)S(1)} %collective-permute-done.13.across), channel_id=1, source_target_pairs={{0,1},{1,0},{2,3},{3,2},{4,5},{5,4},{6,7},{7,6},{8,9},{9,8},{10,11... | collective-permute-start | bytes 393224 | tf_op jit(solution)/shard_map/ppermute | solution.py:28
  44.7 9.9 %collective-permute-start.16 = (bf16[144,512]{1,0:T(8,128)(2,1)S(1)}, bf16[144,512]{1,0:T(8,128)(2,1)S(1)}, u32[]{:S(2)}, u32[]{:S(2)}) collective-permute-start(bf16[144,512]{1,0:T(8,128)(2,1)S(1)} %get-tuple-element.54.message.refs_5_), channel_id=1, source_target_pairs={{8,0},{16,8},{24,16},{28,24},{20,28},{12,20},{4,12},{0,4},{9,1},{1... | collective-permute-start | bytes 442376 | tf_op jit(solution)/shard_map/ppermute | solution.py:39
  48.6 8.6 %collective-permute-start.19 = (bf16[144,512]{1,0:T(8,128)(2,1)S(1)}, bf16[144,512]{1,0:T(8,128)(2,1)S(1)}, u32[]{:S(2)}, u32[]{:S(2)}) collective-permute-start(bf16[144,512]{1,0:T(8,128)(2,1)S(1)} %get-tuple-element.54.message.refs_5_), channel_id=1, source_target_pairs={{0,8},{8,16},{16,24},{24,28},{28,20},{20,12},{12,4},{4,0},{1,9},{9... | collective-permute-start | bytes 442376 | tf_op jit(solution)/shard_map/ppermute | solution.py:39
  50.1 7.1 %collective-permute-start.18 = (bf16[144,512]{1,0:T(8,128)(2,1)S(1)}, bf16[144,512]{1,0:T(8,128)(2,1)S(1)}, u32[]{:S(2)}, u32[]{:S(2)}) collective-permute-start(bf16[144,512]{1,0:T(8,128)(2,1)S(1)} %get-tuple-element.54.message.refs_5_), channel_id=1, source_target_pairs={{0,1},{1,0},{2,3},{3,2},{4,5},{5,4},{6,7},{7,6},{8,12},{9,13},{10,... | collective-permute-start | bytes 442376 | tf_op jit(solution)/shard_map/ppermute | solution.py:50
  54.6 5.7 %collective-permute-start.17 = (bf16[144,512]{1,0:T(8,128)(2,1)S(1)}, bf16[144,512]{1,0:T(8,128)(2,1)S(1)}, u32[]{:S(2)}, u32[]{:S(2)}) collective-permute-start(bf16[144,512]{1,0:T(8,128)(2,1)S(1)} %collective-permute-done.16.refs_8_), channel_id=1, source_target_pairs={{0,4},{4,0},{8,12},{12,8},{16,20},{20,16},{24,28},{28,24},{1,5},{5... | collective-permute-start | bytes 442376 | tf_op jit(solution)/shard_map/ppermute | solution.py:28

commit v5 on v4

v5 whole, which is shorter than its diff:
```python
import functools
import math

import jax
import jax.numpy as jnp
from jax import lax
from jax.experimental import pallas as pl
from jax.experimental.pallas import tpu as pltpu
from jax.sharding import PartitionSpec as P

HDIM = 128
F32 = jnp.float32
BF16 = jnp.bfloat16
HALO = 16
NT = (((1,), (1,)), ((), ()))
NN = (((1,), (0,)), ((), ()))


def dot_nt(a, b):
    return lax.dot_general(a, b, NT, preferred_element_type=F32)


def dot_nn(a, b):
    return lax.dot_general(a, b, NN, preferred_element_type=F32)


def pair_swap(block, axis, bit):
    return lax.ppermute(block, axis, [(i, i ^ bit) for i in range(lax.axis_size(axis))])


def ring_routes(count):
    rise = [(i, i + 2) for i in range(0, count - 2, 2)] + [(count - 2, count - 1)]
    fall = [(i, i - 2) for i in range(count - 1, 2, -2)] + [(1, 0)]
    route = rise + fall
    return route, [(b, a) for a, b in route]


def ring(block, way):
    return lax.ppermute(block, "ctx", ring_routes(lax.axis_size("ctx"))[way])


def total_swap(block, partner_of):
    count, places = lax.axis_size("ctx"), lax.axis_size("mp")
    route = []
    for i in range(count):
        other = partner_of(i, count)
        for m in range(places):
            target = i * places + (m ^ 1) if other is None else other * places + m
            route.append((i * places + m, target))
    return lax.ppermute(block, ("ctx", "mp"), route)


def inner_swap(block):
    return total_swap(block, lambda i, count: i ^ 1 if 2 <= i < count - 2 else None)


def outer_swap(block):
    return total_swap(block, lambda i, count: ((i + 1) ^ 1) - 1 if 0 < i < count - 1 else None)


def window_of(block):
    second = ring(block, 1)
    first = ring(block, 0)
    near = inner_swap(block)
    return near, first, second, pair_swap(second, "ctx", 1)


VMEM = pl.BlockSpec(memory_space=pltpu.VMEM)
ANY = pl.BlockSpec(memory_space=pl.ANY)
HBM = pl.BlockSpec(memory_space=pltpu.HBM)


def kernel_call(body, outs, args, micros, name, unread=0, scratch=(), out_space=VMEM):
    return pl.pallas_call(
        body,
        out_shape=outs,
        in_specs=[VMEM] * (len(args) - unread) + [ANY] * unread,
        out_specs=tuple(out_space for _ in outs),
        scratch_shapes=scratch,
        compiler_params=pltpu.CompilerParams(vmem_limit_bytes=24 * 1024 * 1024),
        cost_estimate=pl.CostEstimate(
            flops=0, bytes_accessed=int(micros * 3.69e6), transcendentals=0
        ),
        name=name,
    )(*args)


def shaped(shape, dtype):
    return jax.ShapeDtypeStruct(shape, dtype)


def is_even():
    return lax.axis_index("ctx") % 2 == 0


def near_swapped():
    block = lax.axis_index("ctx")
    return (block >= 2) & (block < lax.axis_size("ctx") - 2)


def far_there():
    block = lax.axis_index("ctx")
    return jnp.where(is_even(), block >= 2, block < lax.axis_size("ctx") - 2)


def bias_of(there):
    return jnp.where(there, jnp.float32(0.0), jnp.float32(-jnp.inf))


def columns(width):
    return [slice(c, c + HDIM) for c in range(0, width, HDIM)]


def stacked(blocks, rows, cols):
    return jnp.concatenate([block[rows, cols] for block in blocks], axis=0)


def with_ones(values):
    return jnp.concatenate([values, jnp.ones_like(values)], axis=1)


def by_block(scores, biases, stats=None):
    parts = []
    for b, bias in enumerate(biases):
        part = scores[:, b * HDIM : (b + 1) * HDIM]
        if stats is not None:
            part = part - stats[b]
        parts.append(part if bias is None else part + bias)
    return jnp.concatenate(parts, axis=1)


def tile_of(wide):
    lane = lax.broadcasted_iota(jnp.int32, (wide[0].shape[0], HDIM), 1)
    tile = jnp.zeros((wide[0].shape[0], HDIM), F32)
    for h, part in enumerate(wide):
        tile = jnp.where(lane == h, part, tile)
    return tile


def term_rows(rows):
    at = lax.broadcasted_iota(jnp.int32, (16, rows[0].shape[1]), 0)
    block = jnp.zeros((16, rows[0].shape[1]), F32)
    for r, rest in enumerate(rows):
        for k in range(3):
            term = rest.astype(BF16).astype(F32)
            rest = rest - term
            block = jnp.where(at == 3 * r + k, term, block)
    return block.astype(BF16)


def stat_rows(message, frames, which, cols):
    terms = message[frames : frames + 16, cols].astype(F32)
    at = 3 * which
    return terms[at : at + 1] + terms[at + 1 : at + 2] + terms[at + 2 : at + 3]


def weight_columns(weight, flip):
    width = weight.shape[0]
    at = (lax.axis_index("mp") ^ flip) * width
    return weight[:, pl.ds(pl.multiple_of(at, 128), width)]


def hold_body(block, seen, held):
    held[...] = block[...]


def forward_body(scale, q, own, near, first, second, sums, tops, totals):
    frames, width = q.shape
    heads = columns(width)
    blocks = (near, own, first, second)
    biases = (bias_of(near_swapped()), None, None, None)
    keys, values = slice(0, frames), slice(frames, 2 * frames)
    scores = [dot_nt(q[:, c], stacked(blocks, keys, c)) * scale for c in heads]
    scores = [by_block(s, biases) for s in scores]
    top = [jnp.max(s, axis=1, keepdims=True) for s in scores]
    probs = [jnp.exp(s - t).astype(BF16) for s, t in zip(scores, top)]
    summed = [dot_nn(p, with_ones(stacked(blocks, values, c))) for p, c in zip(probs, heads)]
    for c, t, s in zip(heads, top, summed):
        tops[:, c] = jnp.broadcast_to(t, (frames, HDIM))
        sums[:, c] = s[:, 0:HDIM]
        totals[:, c] = s[:, HDIM:]


def project_body(scale, q, relay, sums, tops, totals, weight, att, lse, send, keep):
    frames, width = q.shape
    heads = columns(width)
    bias = bias_of(far_there())
    scores = [dot_nt(q[:, c], relay[0:frames, c]) * scale + bias for c in heads]
    before = [tops[:, c] for c in heads]
    top = [jnp.maximum(b, jnp.max(s, axis=1, keepdims=True)) for b, s in zip(before, scores)]
    shrink = [jnp.exp(b - t) for b, t in zip(before, top)]
    probs = [jnp.exp(s - t).astype(BF16) for s, t in zip(scores, top)]
    late = [dot_nn(p, with_ones(relay[frames : 2 * frames, c])) for p, c in zip(probs, heads)]
    total = [totals[:, c] * k + s[:, HDIM:] for c, k, s in zip(heads, shrink, late)]
    summed = [sums[:, c] * k + s[:, 0:HDIM] for c, k, s in zip(heads, shrink, late)]
    attended = jnp.concatenate([(s * (1.0 / t)).astype(BF16) for s, t in zip(summed, total)], axis=1)
    sent = dot_nn(attended, weight_columns(weight, 3)).astype(BF16)
    kept = dot_nn(attended, weight_columns(weight, 2)).astype(BF16)
    logs = [t + jnp.log(n) for t, n in zip(top, total)]
    att[...] = attended
    send[...] = sent
    keep[...] = kept
    for c, part in zip(heads, logs):
        lse[:, c] = part


def project_own_body(att, weight, seen_a, seen_b, send, keep):
    sent = dot_nn(att[...], weight_columns(weight, 1)).astype(BF16)
    kept = dot_nn(att[...], weight_columns(weight, 0)).astype(BF16)
    send[...] = sent
    keep[...] = kept


def join_body(keep, core, q, outgoing, q_copy):
    outgoing[...] = (keep[...].astype(F32) + core[...].astype(F32)).astype(BF16)
    q_copy[...] = q[...]


def hidden_body(inputs, keep, core, across, cot, hidden, rim_near, rim_far):
    frames, width = inputs.shape
    wide = 2 * HALO
    total = inputs[...].astype(F32) + keep[...].astype(F32) + core[...].astype(F32)
    total = (total + across[...].astype(F32)).astype(BF16)
    even = is_even()
    for at, first, last in (
        (slice(0, wide), total[0:wide], total[frames - wide :]),
        (slice(wide, wide + HALO), cot[0:HALO, :], cot[frames - HALO : frames, :]),
    ):
        first, last = first.astype(F32), last.astype(F32)
        rim_near[at, :] = jnp.where(even, last, first).astype(BF16)
        rim_far[at, :] = jnp.where(even, first, last).astype(BF16)
    hidden[...] = total


def shifted_sum(rows, taps_of, count):
    total = None
    for b in range(8):
        part = None
        reach = count if b == 0 else count + 8
        for a in range(4):
            tap = taps_of(8 * a + b)
            if tap is None:
                continue
            term = tap * rows[8 * a : 8 * a + reach]
            part = term if part is None else part + term
        if b:
            part = pltpu.roll(part, reach - b, 0)[0:count]
        total = part if total is None else total + part
    return total


def silu_parts(conv, cots):
    gate = 1.0 / (1.0 + jnp.exp(-conv))
    grad = cots * (gate + conv * gate * (1.0 - gate))
    return conv * gate, grad.astype(BF16).astype(F32)


def taps_forward(taps, cols):
    count = taps.shape[0]
    return lambda s: taps[s - 1 : s, cols] if 1 <= s <= count else None


def taps_backward(taps, cols):
    count = taps.shape[0]
    return lambda s: taps[count - s : count - s + 1, cols] if 1 <= s <= count else None


def conv_inner_body(hidden, cot, taps, seen, rows_out, edge_conv, part_grad):
    frames, width = hidden.shape
    wide = 2 * HALO
    inner = slice(HALO, frames - HALO)
    none = jnp.zeros((wide, HDIM), F32)
    for cols in columns(width):
        own = hidden[:, cols].astype(F32)
        cots = cot[:, cols].astype(F32)
        conv = shifted_sum(
            jnp.concatenate([none, own, none], axis=0), taps_forward(taps, cols), frames + wide
        )
        silu, grad = silu_parts(conv[wide:frames], cots[inner])
        back = shifted_sum(
            jnp.concatenate([none, grad, none], axis=0), taps_backward(taps, cols), frames
        )
        edge_conv[0:wide, cols] = conv[0:wide]
        edge_conv[wide : 2 * wide, cols] = conv[frames : frames + wide]
        rows_out[inner, cols] = (own[inner] + silu).astype(BF16)
        part_grad[:, cols] = cots + back


def conv_edge_body(
    hidden, rim_near, rim_far, cot, taps, rows_in, edge_conv, part_grad, q_second,
    output, grad_input, second_copy,
):
    frames, width = hidden.shape
    wide = 2 * HALO
    even, far = is_even(), far_there()
    rims, cots_of = slice(0, wide), slice(wide, wide + HALO)
    low, high = slice(0, HALO), slice(frames - HALO, frames)
    inner = slice(HALO, frames - HALO)
    none = jnp.zeros((wide, HDIM), F32)

    def sides(rows, cols):
        near = rim_near[rows, cols].astype(F32)
        beyond = jnp.where(far, rim_far[rows, cols].astype(F32), 0.0)
        return jnp.where(even, beyond, near), jnp.where(even, near, beyond)

    for cols in columns(width):
        row_low, row_high = sides(rims, cols)
        cot_low, cot_high = sides(cots_of, cols)
        conv = edge_conv[:, cols] + shifted_sum(
            jnp.concatenate([row_low, none, row_high], axis=0), taps_forward(taps, cols), 2 * wide
        )
        cots = jnp.concatenate(
            [cot_low, cot[low, cols].astype(F32), cot[high, cols].astype(F32), cot_high], axis=0
        )
        silu, grad = silu_parts(conv, cots)
        back = shifted_sum(
            jnp.concatenate([grad[0:wide], none, grad[wide:]], axis=0), taps_backward(taps, cols), 2 * wide
        )
        part = part_grad[:, cols]
        grad_input[:, cols] = jnp.concatenate(
            [part[0:wide] + back[0:wide], part[wide : frames - wide], part[frames - wide :] + back[wide:]],
            axis=0,
        ).astype(BF16)
        output[low, cols] = (hidden[low, cols].astype(F32) + silu[HALO:wide]).astype(BF16)
        output[inner, cols] = rows_in[inner, cols]
        output[high, cols] = (hidden[high, cols].astype(F32) + silu[wide : wide + HALO]).astype(BF16)
    second_copy[...] = q_second[...]


def upstream_chip_body(own, core, weight, partial):
    partial[...] = dot_nt(own[...], weight_columns(weight, 0)) + dot_nt(core[...], weight_columns(weight, 1))


def upstream_across_body(across, weight, before, partial):
    partial[...] = before[...] + dot_nt(across[...], weight_columns(weight, 2))


def upstream_body(cross, weight, att, lse, partial, seen, message, delta):
    frames, width = cross.shape
    heads = columns(width)
    up = (partial[...] + dot_nt(cross[...], weight_columns(weight, 3))).astype(BF16)
    products = [up[:, c].astype(F32) * att[:, c].astype(F32) for c in heads]
    deltas = [jnp.broadcast_to(jnp.sum(p, axis=1, keepdims=True), (frames, HDIM)) for p in products]
    lse_rows = tile_of([lse[:, c] for c in heads]).T
    delta_rows = tile_of(deltas).T
    terms = [term_rows([lse_rows[h : h + 1], delta_rows[h : h + 1]]) for h in range(len(heads))]
    message[0:frames, :] = up
    message[frames : frames + 16, :] = jnp.concatenate(terms, axis=1)
    for c, part in zip(heads, deltas):
        delta[:, c] = part


def query_grad_body(
    scale, q, own, near, first, second, relay, message, lse, delta, output_here, grad_here,
    output, grad_input, grad_query, held, sems,
):
    writes = [
        pltpu.make_async_copy(output_here, output, sems.at[0]),
        pltpu.make_async_copy(grad_here, grad_input, sems.at[1]),
    ]
    for write in writes:
        write.start()
    frames, width = q.shape
    heads = columns(width)
    blocks = (near, own, first, second, relay)
    biases = (bias_of(near_swapped()), None, None, None, bias_of(far_there()))
    above, below = slice(0, frames), slice(frames, 2 * frames)
    keys = [stacked(blocks, above, c) for c in heads]
    scores = [dot_nt(q[:, c], k) * scale for c, k in zip(heads, keys)]
    dots = [dot_nt(message[0:frames, c], stacked(blocks, below, c)) for c in heads]
    probs = [jnp.exp(by_block(s, biases, [lse[:, c]] * 5)) for c, s in zip(heads, scores)]
    drops = [by_block(d, (None,) * 5, [delta[:, c]] * 5) for c, d in zip(heads, dots)]
    grads = [(p * d * scale).astype(BF16) for p, d in zip(probs, drops)]
    held[...] = jnp.concatenate([dot_nn(g, k).astype(BF16) for g, k in zip(grads, keys)], axis=1)
    writes.append(pltpu.make_async_copy(held, grad_query, sems.at[2]))
    writes[2].start()
    for write in writes:
        write.wait()


def key_part_body(scale, own, *refs):
    queries, late_query, messages, (key_part, value_part, late) = refs[0:4], refs[4], refs[5:9], refs[9:12]
    frames = own.shape[0] // 2
    heads = columns(own.shape[1])
    above, below = slice(0, frames), slice(frames, 2 * frames)
    biases = (None, bias_of(near_swapped()), None, None)
    asks = [stacked(queries, above, c) for c in heads]
    ups = [stacked(messages, above, c) for c in heads]
    scores = [dot_nt(own[above, c], a) * scale for c, a in zip(heads, asks)]
    dots = [dot_nt(own[below, c], u) for c, u in zip(heads, ups)]
    last = [dot_nt(own[above, c], late_query[:, c]) * scale + bias_of(far_there()) for c in heads]
    logs = [[stat_rows(m, frames, 0, c) for m in messages] for c in heads]
    deltas = [[stat_rows(m, frames, 1, c) for m in messages] for c in heads]
    probs = [jnp.exp(by_block(s, biases, n)) for s, n in zip(scores, logs)]
    drops = [by_block(d, (None,) * 4, n) for d, n in zip(dots, deltas)]
    grads = [(p * d * scale).astype(BF16) for p, d in zip(probs, drops)]
    value_sums = [dot_nn(p.astype(BF16), u) for p, u in zip(probs, ups)]
    key_sums = [dot_nn(g, a) for g, a in zip(grads, asks)]
    for c, k, v, s in zip(heads, key_sums, value_sums, last):
        key_part[:, c] = k
        value_part[:, c] = v
        late[:, c] = s


def key_grad_body(
    scale, own, query, message, late, key_part, value_part, grad_key, grad_value, held_key, held_value, sems
):
    frames = own.shape[0] // 2
    heads = columns(own.shape[1])
    above, below = slice(0, frames), slice(frames, 2 * frames)
    ups = [message[above, c] for c in heads]
    probs = [jnp.exp(late[:, c] - stat_rows(message, frames, 0, c)) for c in heads]
    dots = [dot_nt(own[below, c], u) for c, u in zip(heads, ups)]
    values = [value_part[:, c] + dot_nn(p.astype(BF16), u) for c, p, u in zip(heads, probs, ups)]
    held_value[...] = jnp.concatenate([v.astype(BF16) for v in values], axis=1)
    value_write = pltpu.make_async_copy(held_value, grad_value, sems.at[0])
    value_write.start()
    drops = [d - stat_rows(message, frames, 1, c) for c, d in zip(heads, dots)]
    grads = [(p * d * scale).astype(BF16) for p, d in zip(probs, drops)]
    keys = [key_part[:, c] + dot_nn(g, query[:, c]) for c, g in zip(heads, grads)]
    held_key[...] = jnp.concatenate([k.astype(BF16) for k in keys], axis=1)
    key_write = pltpu.make_async_copy(held_key, grad_key, sems.at[1])
    key_write.start()
    value_write.wait()
    key_write.wait()


def per_device(query_rows, key_rows, value_rows, inputs, out_weight, kernel, cotangent):
    frames, width = query_rows.shape
    wide = 2 * HALO
    scale = 1.0 / math.sqrt(HDIM)
    tile = shaped((frames, width), BF16)
    tile32 = shaped((frames, width), F32)
    rim = shaped((wide + HALO, width), BF16)
    noted = shaped((frames + 16, width), BF16)

    zero = jnp.zeros((), BF16)
    kv = lax.pad(key_rows, zero, ((0, frames, 0), (0, 0, 0))) + lax.pad(
        value_rows, zero, ((frames, 0, 0), (0, 0, 0))
    )
    near, first, second, relay = window_of(kv)
    (q_early,) = kernel_call(hold_body, (tile,), (query_rows, second), 0.1, "hold", 1)
    q_second = ring(q_early, 1)
    q_first = ring(q_early, 0)
    sums, tops, totals = kernel_call(
        functools.partial(forward_body, scale),
        (tile32, tile32, tile32),
        (q_early, kv, near, first, second),
        1.0, "forward",
    )
    att, lse, send, keep = kernel_call(
        functools.partial(project_body, scale),
        (tile, tile32, tile, tile),
        (q_early, relay, sums, tops, totals, out_weight),
        1.0, "project",
    )

    core = pair_swap(send, "mp", 1)
    own_send, own_keep = kernel_call(
        project_own_body, (tile, tile), (att, out_weight, q_second, q_first), 0.4, "project_own", 2
    )
    outgoing, q_own = kernel_call(join_body, (tile, tile), (keep, core, q_early), 0.1, "join")
    across = pair_swap(outgoing, "mp", 2)
    own_core = pair_swap(own_send, "mp", 1)
    q_near = inner_swap(q_own)
    hidden, rim_up, rim_down = kernel_call(
        hidden_body,
        (tile, rim, rim),
        (inputs, own_keep, own_core, across, cotangent),
        0.2, "hidden",
    )

    rim_far = outer_swap(rim_down)
    rim_near = pair_swap(rim_up, "ctx", 1)
    rows_out, edge_conv, part_grad = kernel_call(
        conv_inner_body,
        (tile, shaped((2 * wide, width), F32), tile32),
        (hidden, cotangent, kernel, q_near),
        1.6, "conv_inner", 1,
    )
    output_here, grad_here, q_handed = kernel_call(
        conv_edge_body,
        (tile, tile, tile),
        (hidden, rim_near, rim_far, cotangent, kernel, rows_out, edge_conv, part_grad, q_second),
        0.8, "conv_edge",
    )

    gi_across = pair_swap(grad_here, "mp", 2)
    gi_core = pair_swap(grad_here, "mp", 1)
    q_relay = pair_swap(q_handed, "ctx", 1)
    (partial,) = kernel_call(
        upstream_chip_body, (tile32,), (grad_here, gi_core, out_weight), 0.5, "upstream_chip"
    )
    (turned,) = kernel_call(hold_body, (tile,), (gi_across, partial), 0.1, "turn", 1)
    gi_cross = pair_swap(turned, "mp", 1)
    (partial,) = kernel_call(
        upstream_across_body, (tile32,), (turned, out_weight, partial), 0.4, "upstream_across"
    )
    message, delta = kernel_call(
        upstream_body,
        (noted, tile32),
        (gi_cross, out_weight, att, lse, partial, q_relay),
        0.5, "upstream", 1,
    )

    m_near, m_first, m_second, m_relay = window_of(message)
    output, grad_input, grad_query = kernel_call(
        functools.partial(query_grad_body, scale),
        (tile, tile, tile),
        (q_own, kv, near, first, second, relay, message, lse, delta, output_here, grad_here),
        1.8, "query_grad", 0,
        [pltpu.VMEM((frames, width), BF16), pltpu.SemaphoreType.DMA((3,))], HBM,
    )
    key_part, value_part, late = kernel_call(
        functools.partial(key_part_body, scale),
        (tile32, tile32, tile32),
        (kv, q_own, q_near, q_first, q_second, q_relay, message, m_near, m_first, m_second),
        1.5, "key_part",
    )
    grad_key, grad_value = kernel_call(
        functools.partial(key_grad_body, scale),
        (tile, tile),
        (kv, q_relay, m_relay, late, key_part, value_part),
        1.0, "key_grad", 0,
        [pltpu.VMEM((frames, width), BF16)] * 2 + [pltpu.SemaphoreType.DMA((2,))], HBM,
    )
    return (output, grad_input, grad_query, grad_key, grad_value)


def solution(mesh):
    rows = P("ctx", "mp")
    return jax.shard_map(
        per_device,
        mesh=mesh,
        in_specs=(rows, rows, rows, rows, P("mp", None), P(None, "mp"), rows),
        out_specs=(rows,) * 5,
        check_vma=False,
    )
```

time: 61.9 us -> 54.2 us (0.88)
  Pallas kernels: 17.4 us -> 8.73 us
  waiting for transfers between devices: 22.7 us -> 23.6 us
    pallas_call x14 -> x15, Pallas kernels: 17.4 us -> 8.73 us  [kernel_call(): pl.pallas_call(body, out_shape=outs, in_specs=[VMEM] * (len(args) - unrea...]
    ppermute x10, starting transfers between devices: 7.76 us -> 11.4 us  [pair_swap(): lax.ppermute(block, axis, [(i, i ^ bit) for i in range(lax.axis_size(axis...]
    ppermute x6, starting transfers between devices: 10.7 us -> 7.36 us  [ring(): return lax.ppermute(block, 'ctx', ring_routes(lax.axis_size('ctx'))[way])]
    ppermute x10, waiting for transfers between devices: 12.2 us -> 13.2 us  [pair_swap(): lax.ppermute(block, axis, [(i, i ^ bit) for i in range(lax.axis_size(axis...]
  transfers between devices with their start and end apart: 20 -> 20, of which waited for: 8 -> 10; matrix products, arithmetic and copies ran while one was open for 0% -> 0% of each run, Pallas kernels for 21% -> 12%
where the time goes in v5:
time: 54.2 us; the launch traced here: 54 us
  waiting for transfers between devices  23.6 us (44%)
  starting transfers between devices  18.7 us (35%)
  Pallas kernels  8.73 us (16%)
  other arithmetic  1.13 us (2%)
  local copies, waits for them, and re-layouts  0.93 us (2%)
  between operations  0.82 us (2%)
    ppermute x10, waiting for transfers between devices, pair_swap(): lax.ppermute(block, axis, [(i, i ^ bit) for i in range(lax.axis_size(axis...  13.2 us
    ppermute x10, starting transfers between devices, pair_swap(): lax.ppermute(block, axis, [(i, i ^ bit) for i in range(lax.axis_size(axis...  11.4 us
    ppermute x6, waiting for transfers between devices, ring(): return lax.ppermute(block, 'ctx', ring_routes(lax.axis_size('ctx'))[way])  10.4 us
    pallas_call x15, Pallas kernels, kernel_call(): pl.pallas_call(body, out_shape=outs, in_specs=[VMEM] * (len(args) - unrea...  8.73 us
    ppermute x6, starting transfers between devices, ring(): return lax.ppermute(block, 'ctx', ring_routes(lax.axis_size('ctx'))[way])  7.36 us
    add x1, other arithmetic, per_device(): lax.pad(key_rows, zero, ((0, frames, 0), (0, 0, 0)))  1.13 us
  transfers between devices with their start and end apart: 20, of which 10 were waited for; matrix products, arithmetic and copies ran while one was open for 0% of the time, Pallas kernels for 12%

profile of v5, /device:TPU:0, one launch (start us, length us, event | category | flops | bytes accessed | tf_op | source)
XLA Modules:
  0.0 54.0 jit_solution(1287821464854220538)
XLA Ops:
  0.6 0.0 copy-start
  0.6 1.1 %pad_add_fusion.own = bf16[256,512]{1,0:T(8,128)(2,1)S(1)} fusion(bf16[128,512]{1,0:T(8,128)(2,1)} %param.9, bf16[128,512]{1,0:T(8,128)(2,1)} %param.8), kind=kLoop, calls=%fused_computation | loop fusion | flops 524288 | bytes 524288 | tf_op jit(solution)/shard_map/add | solution.py:438
  1.8 3.0 %collective-permute-start = (bf16[256,512]{1,0:T(8,128)(2,1)S(1)}, bf16[256,512]{1,0:T(8,128)(2,1)S(1)}, u32[]{:S(2)}, u32[]{:S(2)}) collective-permute-start(bf16[256,512]{1,0:T(8,128)(2,1)S(1)} %pad_add_fusion.own), channel_id=1, source_target_pairs={{8,0},{16,8},{24,16},{28,24},{20,28},{12,20},{4,12},{0,4},{9,1},{1... | collective-permute-start | bytes 786440 | tf_op jit(solution)/shard_map/ppermute | solution.py:39
  4.8 0.2 collective-permute-start.3
  4.9 0.0 collective-permute-start.2
  4.9 6.2 %collective-permute-done.seen.second = bf16[256,512]{1,0:T(8,128)(2,1)S(1)} collective-permute-done((bf16[256,512]{1,0:T(8,128)(2,1)S(1)}, bf16[256,512]{1,0:T(8,128)(2,1)S(1)}, u32[]{:S(2)}, u32[]{:S(2)}) %collective-permute-start) | collective-permute-done | bytes 262176 | tf_op jit(solution)/shard_map/ppermute | solution.py:39
  11.2 1.7 %collective-permute-start.1 = (bf16[256,512]{1,0:T(8,128)(2,1)S(1)}, bf16[256,512]{1,0:T(8,128)(2,1)S(1)}, u32[]{:S(2)}, u32[]{:S(2)}) collective-permute-start(bf16[256,512]{1,0:T(8,128)(2,1)S(1)} %collective-permute-done.seen.second), channel_id=1, source_target_pairs={{0,4},{4,0},{8,12},{12,8},{16,20},{20,16},{24,28},{28,24},{1,5},{5... | collective-permute-start | bytes 786440 | tf_op jit(solution)/shard_map/ppermute | solution.py:28
  12.8 0.0 copy-start.4
  12.8 0.9 %copy-done.4 = bf16[128,512]{1,0:T(8,128)(2,1)S(1)} copy-done((bf16[128,512]{1,0:T(8,128)(2,1)S(1)}, bf16[128,512]{1,0:T(8,128)(2,1)}, u32[]{:S(2)}) %copy-start.4) | copy-done | bytes 131096
  13.7 1.6 %collective-permute-start.6 = (bf16[128,512]{1,0:T(8,128)(2,1)S(1)}, bf16[128,512]{1,0:T(8,128)(2,1)S(1)}, u32[]{:S(2)}, u32[]{:S(2)}) collective-permute-start(bf16[128,512]{1,0:T(8,128)(2,1)S(1)} %hold.1.q), channel_id=1, source_target_pairs={{0,8},{8,16},{16,24},{24,28},{28,20},{20,12},{12,4},{4,0},{1,9},{9... | collective-permute-start | bytes 393224 | tf_op jit(solution)/shard_map/ppermute | solution.py:39
  15.4 0.4 collective-permute-start.5
  15.8 0.0 collective-permute-done.3.first
  15.8 0.0 collective-permute-done.2.near
  15.8 0.6 %forward.1 = (f32[128,512]{1,0:T(8,128)S(1)}, f32[128,512]{1,0:T(8,128)S(1)}, f32[128,512]{1,0:T(8,128)S(1)}) custom-call(bf16[128,512]{1,0:T(8,128)(2,1)S(1)} %hold.1.q, bf16[256,512]{1,0:T(8,128)(2,1)S(1)} %pad_add_fusion.own, bf16[256,512]{1,0:T(8,128)(2,1)S(1)} %collective-permute-done.2.near, bf16[256,512]{1,0:T(8,128)(2,1)S(1)} %collective-permute-done.3.first, ...), custom_call_target="tpu_custom_call" | custom-call | bytes 3690000 | tf_op jit(solution)/shard_map/forward/pallas_call | solution.py:74
  16.4 3.6 %collective-permute-done.1.relay = bf16[256,512]{1,0:T(8,128)(2,1)S(1)} collective-permute-done((bf16[256,512]{1,0:T(8,128)(2,1)S(1)}, bf16[256,512]{1,0:T(8,128)(2,1)S(1)}, u32[]{:S(2)}, u32[]{:S(2)}) %collective-permute-start.1) | collective-permute-done | bytes 262176 | tf_op jit(solution)/shard_map/ppermute | solution.py:28
  20.1 0.0 copy-done
  20.1 0.7 %project.1 = (bf16[128,512]{1,0:T(8,128)(2,1)S(1)}, f32[128,512]{1,0:T(8,128)S(1)}, bf16[128,512]{1,0:T(8,128)(2,1)S(1)}, bf16[128,512]{1,0:T(8,128)(2,1)S(1)}) custom-call(bf16[128,512]{1,0:T(8,128)(2,1)S(1)} %hold.1.q, bf16[256,512]{1,0:T(8,128)(2,1)S(1)} %collective-permute-done.1.relay, f32[128,512]{1,0:T(8,128)S(1)} %get-tuple-element.35.sums, ...), custom_call_target="tpu_custom_call" | custom-call | bytes 3690000 | tf_op jit(solution)/shard_map/project/pallas_call | solution.py:74
  20.8 0.0 copy-start.1
  20.8 0.0 copy-start.3
  20.8 0.0 copy-start.2
  20.8 0.1 collective-permute-start.4
  20.9 0.6 %collective-permute-done.6.seen_b.refs_2_ = bf16[128,512]{1,0:T(8,128)(2,1)S(1)} collective-permute-done((bf16[128,512]{1,0:T(8,128)(2,1)S(1)}, bf16[128,512]{1,0:T(8,128)(2,1)S(1)}, u32[]{:S(2)}, u32[]{:S(2)}) %collective-permute-start.6) | collective-permute-done | bytes 131104 | tf_op jit(solution)/shard_map/ppermute | solution.py:39
  21.5 0.0 collective-permute-done.5.seen_a.q_second.refs_3_
  21.5 0.3 project_own.1
  21.8 0.1 collective-permute-start.7
  21.9 0.4 collective-permute-done.4.core
  22.3 1.4 %collective-permute-start.8 = (bf16[128,512]{1,0:T(8,128)(2,1)S(1)}, bf16[128,512]{1,0:T(8,128)(2,1)S(1)}, u32[]{:S(2)}, u32[]{:S(2)}) collective-permute-start(bf16[128,512]{1,0:T(8,128)(2,1)S(1)} %get-tuple-element.44), channel_id=1, source_target_pairs={{0,2},{1,3},{2,0},{3,1},{4,6},{5,7},{6,4},{7,5},{8,10},{9,11},{10,... | collective-permute-start | bytes 393224 | tf_op jit(solution)/shard_map/ppermute | solution.py:28
  23.7 0.0 collective-permute-start.11
  23.7 0.0 collective-permute-done.7.core
  23.7 4.2 %collective-permute-done.8.across = bf16[128,512]{1,0:T(8,128)(2,1)S(1)} collective-permute-done((bf16[128,512]{1,0:T(8,128)(2,1)S(1)}, bf16[128,512]{1,0:T(8,128)(2,1)S(1)}, u32[]{:S(2)}, u32[]{:S(2)}) %collective-permute-start.8) | collective-permute-done | bytes 131104 | tf_op jit(solution)/shard_map/ppermute | solution.py:28
  27.9 0.0 copy-done.1
  27.9 0.0 copy-done.3
  27.9 0.1 hidden.1
  28.0 1.4 %collective-permute-start.9 = (bf16[48,512]{1,0:T(8,128)(2,1)S(1)}, bf16[48,512]{1,0:T(8,128)(2,1)S(1)}, u32[]{:S(2)}, u32[]{:S(2)}) collective-permute-start(bf16[48,512]{1,0:T(8,128)(2,1)S(1)} %get-tuple-element.46), channel_id=1, source_target_pairs={{0,4},{4,0},{8,12},{12,8},{16,20},{20,16},{24,28},{28,24},{1,5},{5... | collective-permute-start | bytes 147464 | tf_op jit(solution)/shard_map/ppermute | solution.py:28
  29.4 0.0 collective-permute-start.10
  29.4 0.0 collective-permute-done.11.seen.refs_1_
  29.4 0.0 copy-done.2
  29.4 1.6 %conv_inner.1 = (bf16[128,512]{1,0:T(8,128)(2,1)S(1)}, f32[64,512]{1,0:T(8,128)S(1)}, f32[128,512]{1,0:T(8,128)S(1)}) custom-call(bf16[128,512]{1,0:T(8,128)(2,1)S(1)} %get-tuple-element.45.hidden, bf16[128,512]{1,0:T(8,128)(2,1)S(1)} %copy-done.1, f32[31,512]{1,0:T(8,128)S(1)} %copy-done.2, bf16[128,512]{1,0:T(8,128)(2,1)S(1)} %collective-permute-done.11.seen.refs_1_), custom_call_target="tpu_custom_call" | custom-call | bytes 5904000 | tf_op jit(solution)/shard_map/conv_inner/pallas_call | solution.py:74
  31.0 1.2 %collective-permute-done.9.rim_near = bf16[48,512]{1,0:T(8,128)(2,1)S(1)} collective-permute-done((bf16[48,512]{1,0:T(8,128)(2,1)S(1)}, bf16[48,512]{1,0:T(8,128)(2,1)S(1)}, u32[]{:S(2)}, u32[]{:S(2)}) %collective-permute-start.9) | collective-permute-done | bytes 49184 | tf_op jit(solution)/shard_map/ppermute | solution.py:28
  32.1 0.0 collective-permute-done.10.rim_far
  32.1 0.7 %conv_edge.1 = (bf16[128,512]{1,0:T(8,128)(2,1)S(1)}, bf16[128,512]{1,0:T(8,128)(2,1)S(1)}, bf16[128,512]{1,0:T(8,128)(2,1)S(1)}) custom-call(bf16[128,512]{1,0:T(8,128)(2,1)S(1)} %get-tuple-element.45.hidden, bf16[48,512]{1,0:T(8,128)(2,1)S(1)} %collective-permute-done.9.rim_near, bf16[48,512]{1,0:T(8,128)(2,1)S(1)} %collective-permute-done.10.rim_far, ...), custom_call_target="tpu_custom_call" | custom-call | bytes 2952000 | tf_op jit(solution)/shard_map/conv_edge/pallas_call | solution.py:74
  32.9 0.1 collective-permute-start.13
  33.0 1.4 %collective-permute-start.12 = (bf16[128,512]{1,0:T(8,128)(2,1)S(1)}, bf16[128,512]{1,0:T(8,128)(2,1)S(1)}, u32[]{:S(2)}, u32[]{:S(2)}) collective-permute-start(bf16[128,512]{1,0:T(8,128)(2,1)S(1)} %get-tuple-element.51.own.grad_here), channel_id=1, source_target_pairs={{0,2},{1,3},{2,0},{3,1},{4,6},{5,7},{6,4},{7,5},{8,10},{9,11},{10,... | collective-permute-start | bytes 393224 | tf_op jit(solution)/shard_map/ppermute | solution.py:28
  34.4 2.9 %collective-permute-start.15 = (bf16[128,512]{1,0:T(8,128)(2,1)S(1)}, bf16[128,512]{1,0:T(8,128)(2,1)S(1)}, u32[]{:S(2)}, u32[]{:S(2)}) collective-permute-start(bf16[128,512]{1,0:T(8,128)(2,1)S(1)} %get-tuple-element.53), channel_id=1, source_target_pairs={{0,4},{4,0},{8,12},{12,8},{16,20},{20,16},{24,28},{28,24},{1,5},{5... | collective-permute-start | bytes 393224 | tf_op jit(solution)/shard_map/ppermute | solution.py:28
  37.3 0.0 collective-permute-done.13.core
  37.3 0.5 upstream_chip.1.seen.before
  37.8 1.1 %collective-permute-done.12.block = bf16[128,512]{1,0:T(8,128)(2,1)S(1)} collective-permute-done((bf16[128,512]{1,0:T(8,128)(2,1)S(1)}, bf16[128,512]{1,0:T(8,128)(2,1)S(1)}, u32[]{:S(2)}, u32[]{:S(2)}) %collective-permute-start.12) | collective-permute-done | bytes 131104 | tf_op jit(solution)/shard_map/ppermute | solution.py:28
  38.9 0.1 collective-permute-start.14
  39.0 0.3 upstream_across.1.partial
  39.3 1.8 %collective-permute-done.15.seen.refs_4_.query = bf16[128,512]{1,0:T(8,128)(2,1)S(1)} collective-permute-done((bf16[128,512]{1,0:T(8,128)(2,1)S(1)}, bf16[128,512]{1,0:T(8,128)(2,1)S(1)}, u32[]{:S(2)}, u32[]{:S(2)}) %collective-permute-start.15) | collective-permute-done | bytes 131104 | tf_op jit(solution)/shard_map/ppermute | solution.py:28
  41.1 0.0 collective-permute-done.14.cross
  41.1 0.5 upstream.1
  41.6 2.1 %collective-permute-start.16 = (bf16[144,512]{1,0:T(8,128)(2,1)S(1)}, bf16[144,512]{1,0:T(8,128)(2,1)S(1)}, u32[]{:S(2)}, u32[]{:S(2)}) collective-permute-start(bf16[144,512]{1,0:T(8,128)(2,1)S(1)} %get-tuple-element.54.message.refs_5_), channel_id=1, source_target_pairs={{8,0},{16,8},{24,16},{28,24},{20,28},{12,20},{4,12},{0,4},{9,1},{1... | collective-permute-start | bytes 442376 | tf_op jit(solution)/shard_map/ppermute | solution.py:39
  43.7 0.0 collective-permute-start.19
  43.8 0.0 collective-permute-start.18
  43.8 3.6 %collective-permute-done.16.refs_8_ = bf16[144,512]{1,0:T(8,128)(2,1)S(1)} collective-permute-done((bf16[144,512]{1,0:T(8,128)(2,1)S(1)}, bf16[144,512]{1,0:T(8,128)(2,1)S(1)}, u32[]{:S(2)}, u32[]{:S(2)}) %collective-permute-start.16) | collective-permute-done | bytes 147488 | tf_op jit(solution)/shard_map/ppermute | solution.py:39
  47.4 2.3 %collective-permute-start.17 = (bf16[144,512]{1,0:T(8,128)(2,1)S(1)}, bf16[144,512]{1,0:T(8,128)(2,1)S(1)}, u32[]{:S(2)}, u32[]{:S(2)}) collective-permute-start(bf16[144,512]{1,0:T(8,128)(2,1)S(1)} %collective-permute-done.16.refs_8_), channel_id=1, source_target_pairs={{0,4},{4,0},{8,12},{12,8},{16,20},{20,16},{24,28},{28,24},{1,5},{5... | collective-permute-start | bytes 442376 | tf_op jit(solution)/shard_map/ppermute | solution.py:28
  49.6 1.5 %query_grad.1 = (bf16[128,512]{1,0:T(8,128)(2,1)}, bf16[128,512]{1,0:T(8,128)(2,1)}, bf16[128,512]{1,0:T(8,128)(2,1)}) custom-call(bf16[128,512]{1,0:T(8,128)(2,1)S(1)} %get-tuple-element.40.q.refs_0_, bf16[256,512]{1,0:T(8,128)(2,1)S(1)} %pad_add_fusion.own, bf16[256,512]{1,0:T(8,128)(2,1)S(1)} %collective-permute-done.2.near, ...), custom_call_target="tpu_custom_call" | custom-call | bytes 6642000 | tf_op jit(solution)/shard_map/query_grad/pallas_call | solution.py:74
  51.2 0.0 collective-permute-done.19.refs_7_
  51.2 0.0 collective-permute-done.18.refs_6_
  51.2 0.9 %key_part.1 = (f32[128,512]{1,0:T(8,128)S(1)}, f32[128,512]{1,0:T(8,128)S(1)}, f32[128,512]{1,0:T(8,128)S(1)}) custom-call(bf16[256,512]{1,0:T(8,128)(2,1)S(1)} %pad_add_fusion.own, bf16[128,512]{1,0:T(8,128)(2,1)S(1)} %get-tuple-element.40.q.refs_0_, bf16[128,512]{1,0:T(8,128)(2,1)S(1)} %collective-permute-done.11.seen.refs_1_, ...), custom_call_target="tpu_custom_call" | custom-call | bytes 5535000 | tf_op jit(solution)/shard_map/key_part/pallas_call | solution.py:74
  52.1 0.9 %collective-permute-done.17.message = bf16[144,512]{1,0:T(8,128)(2,1)S(1)} collective-permute-done((bf16[144,512]{1,0:T(8,128)(2,1)S(1)}, bf16[144,512]{1,0:T(8,128)(2,1)S(1)}, u32[]{:S(2)}, u32[]{:S(2)}) %collective-permute-start.17) | collective-permute-done | bytes 147488 | tf_op jit(solution)/shard_map/ppermute | solution.py:28
  53.0 1.0 %key_grad.1 = (bf16[128,512]{1,0:T(8,128)(2,1)}, bf16[128,512]{1,0:T(8,128)(2,1)}) custom-call(bf16[256,512]{1,0:T(8,128)(2,1)S(1)} %pad_add_fusion.own, bf16[128,512]{1,0:T(8,128)(2,1)S(1)} %collective-permute-done.15.seen.refs_4_.query, bf16[144,512]{1,0:T(8,128)(2,1)S(1)} %collective-permute-done.17.message, f32[128,512]{1,0:T(8,128)S(1)} %get-tuple-element.60.late, ...), custom_call_target="tpu_custom_call" | custom-call | bytes 3690000 | tf_op jit(solution)/shard_map/key_grad/pallas_call | solution.py:74
  (3 shorter events, 0.1 us)
Async XLA Ops:
  0.6 19.4 %copy-start = (bf16[512,2048]{1,0:T(8,128)(2,1)S(1)}, bf16[512,2048]{1,0:T(8,128)(2,1)}, u32[]{:S(2)}) copy-start(bf16[512,2048]{1,0:T(8,128)(2,1)} %weight.9) | copy-start | bytes 6291460
  1.8 9.4 %collective-permute-start = (bf16[256,512]{1,0:T(8,128)(2,1)S(1)}, bf16[256,512]{1,0:T(8,128)(2,1)S(1)}, u32[]{:S(2)}, u32[]{:S(2)}) collective-permute-start(bf16[256,512]{1,0:T(8,128)(2,1)S(1)} %pad_add_fusion.own), channel_id=1, source_target_pairs={{8,0},{16,8},{24,16},{28,24},{20,28},{12,20},{4,12},{0,4},{9,1},{1... | collective-permute-start | bytes 786440 | tf_op jit(solution)/shard_map/ppermute | solution.py:39
  4.8 11.0 %collective-permute-start.3 = (bf16[256,512]{1,0:T(8,128)(2,1)S(1)}, bf16[256,512]{1,0:T(8,128)(2,1)S(1)}, u32[]{:S(2)}, u32[]{:S(2)}) collective-permute-start(bf16[256,512]{1,0:T(8,128)(2,1)S(1)} %pad_add_fusion.own), channel_id=1, source_target_pairs={{0,8},{8,16},{16,24},{24,28},{28,20},{20,12},{12,4},{4,0},{1,9},{9... | collective-permute-start | bytes 786440 | tf_op jit(solution)/shard_map/ppermute | solution.py:39
  4.9 10.9 %collective-permute-start.2 = (bf16[256,512]{1,0:T(8,128)(2,1)S(1)}, bf16[256,512]{1,0:T(8,128)(2,1)S(1)}, u32[]{:S(2)}, u32[]{:S(2)}) collective-permute-start(bf16[256,512]{1,0:T(8,128)(2,1)S(1)} %pad_add_fusion.own), channel_id=1, source_target_pairs={{0,1},{1,0},{2,3},{3,2},{4,5},{5,4},{6,7},{7,6},{8,12},{9,13},{10,... | collective-permute-start | bytes 786440 | tf_op jit(solution)/shard_map/ppermute | solution.py:50
  11.2 8.9 %collective-permute-start.1 = (bf16[256,512]{1,0:T(8,128)(2,1)S(1)}, bf16[256,512]{1,0:T(8,128)(2,1)S(1)}, u32[]{:S(2)}, u32[]{:S(2)}) collective-permute-start(bf16[256,512]{1,0:T(8,128)(2,1)S(1)} %collective-permute-done.seen.second), channel_id=1, source_target_pairs={{0,4},{4,0},{8,12},{12,8},{16,20},{20,16},{24,28},{28,24},{1,5},{5... | collective-permute-start | bytes 786440 | tf_op jit(solution)/shard_map/ppermute | solution.py:28
  12.8 0.9 %copy-start.4 = (bf16[128,512]{1,0:T(8,128)(2,1)S(1)}, bf16[128,512]{1,0:T(8,128)(2,1)}, u32[]{:S(2)}) copy-start(bf16[128,512]{1,0:T(8,128)(2,1)} %block.1) | copy-start | bytes 393220
  13.7 7.7 %collective-permute-start.6 = (bf16[128,512]{1,0:T(8,128)(2,1)S(1)}, bf16[128,512]{1,0:T(8,128)(2,1)S(1)}, u32[]{:S(2)}, u32[]{:S(2)}) collective-permute-start(bf16[128,512]{1,0:T(8,128)(2,1)S(1)} %hold.1.q), channel_id=1, source_target_pairs={{0,8},{8,16},{16,24},{24,28},{28,20},{20,12},{12,4},{4,0},{1,9},{9... | collective-permute-start | bytes 393224 | tf_op jit(solution)/shard_map/ppermute | solution.py:39
  15.4 6.1 %collective-permute-start.5 = (bf16[128,512]{1,0:T(8,128)(2,1)S(1)}, bf16[128,512]{1,0:T(8,128)(2,1)S(1)}, u32[]{:S(2)}, u32[]{:S(2)}) collective-permute-start(bf16[128,512]{1,0:T(8,128)(2,1)S(1)} %hold.1.q), channel_id=1, source_target_pairs={{8,0},{16,8},{24,16},{28,24},{20,28},{12,20},{4,12},{0,4},{9,1},{1... | collective-permute-start | bytes 393224 | tf_op jit(solution)/shard_map/ppermute | solution.py:39
  20.8 7.1 %copy-start.1 = (bf16[128,512]{1,0:T(8,128)(2,1)S(1)}, bf16[128,512]{1,0:T(8,128)(2,1)}, u32[]{:S(2)}) copy-start(bf16[128,512]{1,0:T(8,128)(2,1)} %cot.5) | copy-start | bytes 393220
  20.8 7.1 %copy-start.3 = (bf16[128,512]{1,0:T(8,128)(2,1)S(1)}, bf16[128,512]{1,0:T(8,128)(2,1)}, u32[]{:S(2)}) copy-start(bf16[128,512]{1,0:T(8,128)(2,1)} %inputs.1) | copy-start | bytes 393220
  20.8 8.6 %copy-start.2 = (f32[31,512]{1,0:T(8,128)S(1)}, f32[31,512]{1,0:T(8,128)}, u32[]{:S(2)}) copy-start(f32[31,512]{1,0:T(8,128)} %taps.3) | copy-start | bytes 190468
  20.8 1.4 %collective-permute-start.4 = (bf16[128,512]{1,0:T(8,128)(2,1)S(1)}, bf16[128,512]{1,0:T(8,128)(2,1)S(1)}, u32[]{:S(2)}, u32[]{:S(2)}) collective-permute-start(bf16[128,512]{1,0:T(8,128)(2,1)S(1)} %get-tuple-element.39), channel_id=1, source_target_pairs={{0,1},{1,0},{2,3},{3,2},{4,5},{5,4},{6,7},{7,6},{8,9},{9,8},{10,11... | collective-permute-start | bytes 393224 | tf_op jit(solution)/shard_map/ppermute | solution.py:28
  21.8 1.9 %collective-permute-start.7 = (bf16[128,512]{1,0:T(8,128)(2,1)S(1)}, bf16[128,512]{1,0:T(8,128)(2,1)S(1)}, u32[]{:S(2)}, u32[]{:S(2)}) collective-permute-start(bf16[128,512]{1,0:T(8,128)(2,1)S(1)} %get-tuple-element.43), channel_id=1, source_target_pairs={{0,1},{1,0},{2,3},{3,2},{4,5},{5,4},{6,7},{7,6},{8,9},{9,8},{10,11... | collective-permute-start | bytes 393224 | tf_op jit(solution)/shard_map/ppermute | solution.py:28
  22.3 5.6 %collective-permute-start.8 = (bf16[128,512]{1,0:T(8,128)(2,1)S(1)}, bf16[128,512]{1,0:T(8,128)(2,1)S(1)}, u32[]{:S(2)}, u32[]{:S(2)}) collective-permute-start(bf16[128,512]{1,0:T(8,128)(2,1)S(1)} %get-tuple-element.44), channel_id=1, source_target_pairs={{0,2},{1,3},{2,0},{3,1},{4,6},{5,7},{6,4},{7,5},{8,10},{9,11},{10,... | collective-permute-start | bytes 393224 | tf_op jit(solution)/shard_map/ppermute | solution.py:28
  23.7 5.7 %collective-permute-start.11 = (bf16[128,512]{1,0:T(8,128)(2,1)S(1)}, bf16[128,512]{1,0:T(8,128)(2,1)S(1)}, u32[]{:S(2)}, u32[]{:S(2)}) collective-permute-start(bf16[128,512]{1,0:T(8,128)(2,1)S(1)} %get-tuple-element.40.q.refs_0_), channel_id=1, source_target_pairs={{0,1},{1,0},{2,3},{3,2},{4,5},{5,4},{6,7},{7,6},{8,12},{9,13},{10,... | collective-permute-start | bytes 393224 | tf_op jit(solution)/shard_map/ppermute | solution.py:50
  28.0 4.2 %collective-permute-start.9 = (bf16[48,512]{1,0:T(8,128)(2,1)S(1)}, bf16[48,512]{1,0:T(8,128)(2,1)S(1)}, u32[]{:S(2)}, u32[]{:S(2)}) collective-permute-start(bf16[48,512]{1,0:T(8,128)(2,1)S(1)} %get-tuple-element.46), channel_id=1, source_target_pairs={{0,4},{4,0},{8,12},{12,8},{16,20},{20,16},{24,28},{28,24},{1,5},{5... | collective-permute-start | bytes 147464 | tf_op jit(solution)/shard_map/ppermute | solution.py:28
  29.4 2.8 %collective-permute-start.10 = (bf16[48,512]{1,0:T(8,128)(2,1)S(1)}, bf16[48,512]{1,0:T(8,128)(2,1)S(1)}, u32[]{:S(2)}, u32[]{:S(2)}) collective-permute-start(bf16[48,512]{1,0:T(8,128)(2,1)S(1)} %get-tuple-element.47), channel_id=1, source_target_pairs={{0,1},{1,0},{2,3},{3,2},{4,8},{5,9},{6,10},{7,11},{8,4},{9,5},{10,... | collective-permute-start | bytes 147464 | tf_op jit(solution)/shard_map/ppermute | solution.py:50
  32.9 4.4 %collective-permute-start.13 = (bf16[128,512]{1,0:T(8,128)(2,1)S(1)}, bf16[128,512]{1,0:T(8,128)(2,1)S(1)}, u32[]{:S(2)}, u32[]{:S(2)}) collective-permute-start(bf16[128,512]{1,0:T(8,128)(2,1)S(1)} %get-tuple-element.51.own.grad_here), channel_id=1, source_target_pairs={{0,1},{1,0},{2,3},{3,2},{4,5},{5,4},{6,7},{7,6},{8,9},{9,8},{10,11... | collective-permute-start | bytes 393224 | tf_op jit(solution)/shard_map/ppermute | solution.py:28
  33.0 5.9 %collective-permute-start.12 = (bf16[128,512]{1,0:T(8,128)(2,1)S(1)}, bf16[128,512]{1,0:T(8,128)(2,1)S(1)}, u32[]{:S(2)}, u32[]{:S(2)}) collective-permute-start(bf16[128,512]{1,0:T(8,128)(2,1)S(1)} %get-tuple-element.51.own.grad_here), channel_id=1, source_target_pairs={{0,2},{1,3},{2,0},{3,1},{4,6},{5,7},{6,4},{7,5},{8,10},{9,11},{10,... | collective-permute-start | bytes 393224 | tf_op jit(solution)/shard_map/ppermute | solution.py:28
  34.4 6.7 %collective-permute-start.15 = (bf16[128,512]{1,0:T(8,128)(2,1)S(1)}, bf16[128,512]{1,0:T(8,128)(2,1)S(1)}, u32[]{:S(2)}, u32[]{:S(2)}) collective-permute-start(bf16[128,512]{1,0:T(8,128)(2,1)S(1)} %get-tuple-element.53), channel_id=1, source_target_pairs={{0,4},{4,0},{8,12},{12,8},{16,20},{20,16},{24,28},{28,24},{1,5},{5... | collective-permute-start | bytes 393224 | tf_op jit(solution)/shard_map/ppermute | solution.py:28
  38.9 2.2 %collective-permute-start.14 = (bf16[128,512]{1,0:T(8,128)(2,1)S(1)}, bf16[128,512]{1,0:T(8,128)(2,1)S(1)}, u32[]{:S(2)}, u32[]{:S(2)}) collective-permute-start(bf16[128,512]{1,0:T(8,128)(2,1)S(1)} %turn.1.across), channel_id=1, source_target_pairs={{0,1},{1,0},{2,3},{3,2},{4,5},{5,4},{6,7},{7,6},{8,9},{9,8},{10,11... | collective-permute-start | bytes 393224 | tf_op jit(solution)/shard_map/ppermute | solution.py:28
  41.6 5.8 %collective-permute-start.16 = (bf16[144,512]{1,0:T(8,128)(2,1)S(1)}, bf16[144,512]{1,0:T(8,128)(2,1)S(1)}, u32[]{:S(2)}, u32[]{:S(2)}) collective-permute-start(bf16[144,512]{1,0:T(8,128)(2,1)S(1)} %get-tuple-element.54.message.refs_5_), channel_id=1, source_target_pairs={{8,0},{16,8},{24,16},{28,24},{20,28},{12,20},{4,12},{0,4},{9,1},{1... | collective-permute-start | bytes 442376 | tf_op jit(solution)/shard_map/ppermute | solution.py:39
  43.7 7.4 %collective-permute-start.19 = (bf16[144,512]{1,0:T(8,128)(2,1)S(1)}, bf16[144,512]{1,0:T(8,128)(2,1)S(1)}, u32[]{:S(2)}, u32[]{:S(2)}) collective-permute-start(bf16[144,512]{1,0:T(8,128)(2,1)S(1)} %get-tuple-element.54.message.refs_5_), channel_id=1, source_target_pairs={{0,8},{8,16},{16,24},{24,28},{28,20},{20,12},{12,4},{4,0},{1,9},{9... | collective-permute-start | bytes 442376 | tf_op jit(solution)/shard_map/ppermute | solution.py:39
  43.8 7.4 %collective-permute-start.18 = (bf16[144,512]{1,0:T(8,128)(2,1)S(1)}, bf16[144,512]{1,0:T(8,128)(2,1)S(1)}, u32[]{:S(2)}, u32[]{:S(2)}) collective-permute-start(bf16[144,512]{1,0:T(8,128)(2,1)S(1)} %get-tuple-element.54.message.refs_5_), channel_id=1, source_target_pairs={{0,1},{1,0},{2,3},{3,2},{4,5},{5,4},{6,7},{7,6},{8,12},{9,13},{10,... | collective-permute-start | bytes 442376 | tf_op jit(solution)/shard_map/ppermute | solution.py:50
  47.4 5.6 %collective-permute-start.17 = (bf16[144,512]{1,0:T(8,128)(2,1)S(1)}, bf16[144,512]{1,0:T(8,128)(2,1)S(1)}, u32[]{:S(2)}, u32[]{:S(2)}) collective-permute-start(bf16[144,512]{1,0:T(8,128)(2,1)S(1)} %collective-permute-done.16.refs_8_), channel_id=1, source_target_pairs={{0,4},{4,0},{8,12},{12,8},{16,20},{20,16},{24,28},{28,24},{1,5},{5... | collective-permute-start | bytes 442376 | tf_op jit(solution)/shard_map/ppermute | solution.py:28

commit v6 on v5

--- a/solution.py
+++ b/solution.py
@@ -164,33 +164,39 @@
     held[...] = block[...]
 
 
-def forward_body(scale, q, own, near, first, second, sums, tops, totals):
+def split_body(joined, seen, *parts):
+    frames = parts[0].shape[0]
+    for k, part in enumerate(parts):
+        part[...] = joined[k * frames : (k + 1) * frames, :]
+
+
+def forward_body(scale, q, *refs):
     frames, width = q.shape
     heads = columns(width)
-    blocks = (near, own, first, second)
-    biases = (bias_of(near_swapped()), None, None, None)
-    keys, values = slice(0, frames), slice(frames, 2 * frames)
-    scores = [dot_nt(q[:, c], stacked(blocks, keys, c)) * scale for c in heads]
+    keys, values, (sums, tops, totals) = refs[0:4], refs[4:8], refs[8:11]
+    biases = (None, bias_of(near_swapped()), None, None)
+    every = slice(0, frames)
+    scores = [dot_nt(q[:, c], stacked(keys, every, c)) * scale for c in heads]
     scores = [by_block(s, biases) for s in scores]
     top = [jnp.max(s, axis=1, keepdims=True) for s in scores]
     probs = [jnp.exp(s - t).astype(BF16) for s, t in zip(scores, top)]
-    summed = [dot_nn(p, with_ones(stacked(blocks, values, c))) for p, c in zip(probs, heads)]
+    summed = [dot_nn(p, with_ones(stacked(values, every, c))) for p, c in zip(probs, heads)]
     for c, t, s in zip(heads, top, summed):
         tops[:, c] = jnp.broadcast_to(t, (frames, HDIM))
         sums[:, c] = s[:, 0:HDIM]
         totals[:, c] = s[:, HDIM:]
 
 
-def project_body(scale, q, relay, sums, tops, totals, weight, att, lse, send, keep):
+def project_body(scale, q, relay_key, relay_value, sums, tops, totals, weight, att, lse, send, keep):
     frames, width = q.shape
     heads = columns(width)
     bias = bias_of(far_there())
-    scores = [dot_nt(q[:, c], relay[0:frames, c]) * scale + bias for c in heads]
+    scores = [dot_nt(q[:, c], relay_key[:, c]) * scale + bias for c in heads]
     before = [tops[:, c] for c in heads]
     top = [jnp.maximum(b, jnp.max(s, axis=1, keepdims=True)) for b, s in zip(before, scores)]
     shrink = [jnp.exp(b - t) for b, t in zip(before, top)]
     probs = [jnp.exp(s - t).astype(BF16) for s, t in zip(scores, top)]
-    late = [dot_nn(p, with_ones(relay[frames : 2 * frames, c])) for p, c in zip(probs, heads)]
+    late = [dot_nn(p, with_ones(relay_value[:, c])) for p, c in zip(probs, heads)]
     total = [totals[:, c] * k + s[:, HDIM:] for c, k, s in zip(heads, shrink, late)]
     summed = [sums[:, c] * k + s[:, 0:HDIM] for c, k, s in zip(heads, shrink, late)]
     attended = jnp.concatenate([(s * (1.0 / t)).astype(BF16) for s, t in zip(summed, total)], axis=1)
@@ -351,9 +357,9 @@
 
 
 def query_grad_body(
-    scale, q, own, near, first, second, relay, message, lse, delta, output_here, grad_here,
-    output, grad_input, grad_query, held, sems,
+    scale, q, message, lse, delta, output_here, grad_here, *refs
 ):
+    keys_of, values_of, (output, grad_input, grad_query, held, sems) = refs[0:5], refs[5:10], refs[10:15]
     writes = [
         pltpu.make_async_copy(output_here, output, sems.at[0]),
         pltpu.make_async_copy(grad_here, grad_input, sems.at[1]),
@@ -362,12 +368,11 @@
         write.start()
     frames, width = q.shape
     heads = columns(width)
-    blocks = (near, own, first, second, relay)
-    biases = (bias_of(near_swapped()), None, None, None, bias_of(far_there()))
-    above, below = slice(0, frames), slice(frames, 2 * frames)
-    keys = [stacked(blocks, above, c) for c in heads]
+    biases = (None, bias_of(near_swapped()), None, None, bias_of(far_there()))
+    every = slice(0, frames)
+    keys = [stacked(keys_of, every, c) for c in heads]
     scores = [dot_nt(q[:, c], k) * scale for c, k in zip(heads, keys)]
-    dots = [dot_nt(message[0:frames, c], stacked(blocks, below, c)) for c in heads]
+    dots = [dot_nt(message[0:frames, c], stacked(values_of, every, c)) for c in heads]
     probs = [jnp.exp(by_block(s, biases, [lse[:, c]] * 5)) for c, s in zip(heads, scores)]
     drops = [by_block(d, (None,) * 5, [delta[:, c]] * 5) for c, d in zip(heads, dots)]
     grads = [(p * d * scale).astype(BF16) for p, d in zip(probs, drops)]
@@ -378,17 +383,17 @@
         write.wait()
 
 
-def key_part_body(scale, own, *refs):
+def key_part_body(scale, key, value, *refs):
     queries, late_query, messages, (key_part, value_part, late) = refs[0:4], refs[4], refs[5:9], refs[9:12]
-    frames = own.shape[0] // 2
-    heads = columns(own.shape[1])
-    above, below = slice(0, frames), slice(frames, 2 * frames)
+    frames, width = key.shape
+    heads = columns(width)
+    every = slice(0, frames)
     biases = (None, bias_of(near_swapped()), None, None)
-    asks = [stacked(queries, above, c) for c in heads]
-    ups = [stacked(messages, above, c) for c in heads]
-    scores = [dot_nt(own[above, c], a) * scale for c, a in zip(heads, asks)]
-    dots = [dot_nt(own[below, c], u) for c, u in zip(heads, ups)]
-    last = [dot_nt(own[above, c], late_query[:, c]) * scale + bias_of(far_there()) for c in heads]
+    asks = [stacked(queries, every, c) for c in heads]
+    ups = [stacked(messages, every, c) for c in heads]
+    scores = [dot_nt(key[:, c], a) * scale for c, a in zip(heads, asks)]
+    dots = [dot_nt(value[:, c], u) for c, u in zip(heads, ups)]
+    last = [dot_nt(key[:, c], late_query[:, c]) * scale + bias_of(far_there()) for c in heads]
     logs = [[stat_rows(m, frames, 0, c) for m in messages] for c in heads]
     deltas = [[stat_rows(m, frames, 1, c) for m in messages] for c in heads]
     probs = [jnp.exp(by_block(s, biases, n)) for s, n in zip(scores, logs)]
@@ -403,14 +408,13 @@
 
 
 def key_grad_body(
-    scale, own, query, message, late, key_part, value_part, grad_key, grad_value, held_key, held_value, sems
+    scale, value, query, message, late, key_part, value_part, grad_key, grad_value, held_key, held_value, sems
 ):
-    frames = own.shape[0] // 2
-    heads = columns(own.shape[1])
-    above, below = slice(0, frames), slice(frames, 2 * frames)
-    ups = [message[above, c] for c in heads]
+    frames, width = value.shape
+    heads = columns(width)
+    ups = [message[0:frames, c] for c in heads]
     probs = [jnp.exp(late[:, c] - stat_rows(message, frames, 0, c)) for c in heads]
-    dots = [dot_nt(own[below, c], u) for c, u in zip(heads, ups)]
+    dots = [dot_nt(value[:, c], u) for c, u in zip(heads, ups)]
     values = [value_part[:, c] + dot_nn(p.astype(BF16), u) for c, p, u in zip(heads, probs, ups)]
     held_value[...] = jnp.concatenate([v.astype(BF16) for v in values], axis=1)
     value_write = pltpu.make_async_copy(held_value, grad_value, sems.at[0])
@@ -434,24 +438,29 @@
     rim = shaped((wide + HALO, width), BF16)
     noted = shaped((frames + 16, width), BF16)
 
+    keys = (key_rows, *window_of(key_rows))
+    values = (value_rows, *window_of(value_rows))
     zero = jnp.zeros((), BF16)
-    kv = lax.pad(key_rows, zero, ((0, frames, 0), (0, 0, 0))) + lax.pad(
-        value_rows, zero, ((frames, 0, 0), (0, 0, 0))
-    )
-    near, first, second, relay = window_of(kv)
-    (q_early,) = kernel_call(hold_body, (tile,), (query_rows, second), 0.1, "hold", 1)
+    joined = sum(
+        lax.pad(rows, zero, ((k * frames, (2 - k) * frames, 0), (0, 0, 0)))
+        for k, rows in enumerate((query_rows, key_rows, value_rows))
+    )
+    q_early, key, value = kernel_call(
+        split_body, (tile, tile, tile), (joined, values[3]), 0.1, "split", 1
+    )
+    keys, values = (key, *keys[1:]), (value, *values[1:])
     q_second = ring(q_early, 1)
     q_first = ring(q_early, 0)
     sums, tops, totals = kernel_call(
         functools.partial(forward_body, scale),
         (tile32, tile32, tile32),
-        (q_early, kv, near, first, second),
+        (q_early, *keys[0:4], *values[0:4]),
         1.0, "forward",
     )
     att, lse, send, keep = kernel_call(
         functools.partial(project_body, scale),
         (tile, tile32, tile, tile),
-        (q_early, relay, sums, tops, totals, out_weight),
+        (q_early, keys[4], values[4], sums, tops, totals, out_weight),
         1.0, "project",
     )
 
@@ -507,20 +516,20 @@
     output, grad_input, grad_query = kernel_call(
         functools.partial(query_grad_body, scale),
         (tile, tile, tile),
-        (q_own, kv, near, first, second, relay, message, lse, delta, output_here, grad_here),
+        (q_own, message, lse, delta, output_here, grad_here, *keys, *values),
         1.8, "query_grad", 0,
         [pltpu.VMEM((frames, width), BF16), pltpu.SemaphoreType.DMA((3,))], HBM,
     )
     key_part, value_part, late = kernel_call(
         functools.partial(key_part_body, scale),
         (tile32, tile32, tile32),
-        (kv, q_own, q_near, q_first, q_second, q_relay, message, m_near, m_first, m_second),
+        (key, value, q_own, q_near, q_first, q_second, q_relay, message, m_near, m_first, m_second),
         1.5, "key_part",
     )
     grad_key, grad_value = kernel_call(
         functools.partial(key_grad_body, scale),
         (tile, tile),
-        (kv, q_relay, m_relay, late, key_part, value_part),
+        (value, q_relay, m_relay, late, key_part, value_part),
         1.0, "key_grad", 0,
         [pltpu.VMEM((frames, width), BF16)] * 2 + [pltpu.SemaphoreType.DMA((2,))], HBM,
     )

time: 54.2 us -> 54.6 us (level)
  starting transfers between devices: 18.7 us -> 25.1 us
  waiting for transfers between devices: 23.6 us -> 18.6 us
  local copies, waits for them, and re-layouts: 0.93 us -> 0.02 us
    ppermute x6 -> x8, starting transfers between devices: 7.36 us -> 13.6 us  [ring(): return lax.ppermute(block, 'ctx', ring_routes(lax.axis_size('ctx'))[way])]
    ppermute x6 -> x8, waiting for transfers between devices: 10.4 us -> 5.62 us  [ring(): return lax.ppermute(block, 'ctx', ring_routes(lax.axis_size('ctx'))[way])]
    unnamed x10 -> x8, local copies, waits for them, and re-layouts: 0.93 us -> 0.02 us
    ppermute x10 -> x11, waiting for transfers between devices: 13.2 us -> 13 us  [pair_swap(): lax.ppermute(block, axis, [(i, i ^ bit) for i in range(lax.axis_size(axis...]
    ppermute x10 -> x11, starting transfers between devices: 11.4 us -> 11.4 us  [pair_swap(): lax.ppermute(block, axis, [(i, i ^ bit) for i in range(lax.axis_size(axis...]
  transfers between devices with their start and end apart: 20 -> 24, of which waited for: 10 -> 8; matrix products, arithmetic and copies ran while one was open for 0% -> 2% of each run, Pallas kernels for 12% -> 12%
where the time goes in v6:
time: 54.6 us; the launch traced here: 54.5 us
  starting transfers between devices  25.1 us (46%)
  waiting for transfers between devices  18.6 us (34%)
  Pallas kernels  8.79 us (16%)
  other arithmetic  1.06 us (2%)
  between operations  0.86 us (2%)
    ppermute x8, starting transfers between devices, ring(): return lax.ppermute(block, 'ctx', ring_routes(lax.axis_size('ctx'))[way])  13.6 us
    ppermute x11, waiting for transfers between devices, pair_swap(): lax.ppermute(block, axis, [(i, i ^ bit) for i in range(lax.axis_size(axis...  13 us
    ppermute x11, starting transfers between devices, pair_swap(): lax.ppermute(block, axis, [(i, i ^ bit) for i in range(lax.axis_size(axis...  11.4 us
    pallas_call x15, Pallas kernels, kernel_call(): pl.pallas_call(body, out_shape=outs, in_specs=[VMEM] * (len(args) - unrea...  8.79 us
    ppermute x8, waiting for transfers between devices, ring(): return lax.ppermute(block, 'ctx', ring_routes(lax.axis_size('ctx'))[way])  5.62 us
  transfers between devices with their start and end apart: 24, of which 8 were waited for; matrix products, arithmetic and copies ran while one was open for 2% of the time, Pallas kernels for 12%

profile of v6, /device:TPU:0, one launch (start us, length us, event | category | flops | bytes accessed | tf_op | source)
XLA Modules:
  0.0 54.5 jit_solution(7301241549978594586)
XLA Ops:
  0.6 3.0 %collective-permute-start.1 = (bf16[128,512]{1,0:T(8,128)(2,1)}, bf16[128,512]{1,0:T(8,128)(2,1)S(1)}, u32[]{:S(2)}, u32[]{:S(2)}) collective-permute-start(bf16[128,512]{1,0:T(8,128)(2,1)} %param.8), channel_id=1, source_target_pairs={{8,0},{16,8},{24,16},{28,24},{20,28},{12,20},{4,12},{0,4},{9,1},{1... | collective-permute-start | bytes 393224 | tf_op jit(solution)/shard_map/ppermute | solution.py:39
  3.6 0.1 collective-permute-start.5
  3.8 1.9 %collective-permute-start = (bf16[128,512]{1,0:T(8,128)(2,1)}, bf16[128,512]{1,0:T(8,128)(2,1)S(1)}, u32[]{:S(2)}, u32[]{:S(2)}) collective-permute-start(bf16[128,512]{1,0:T(8,128)(2,1)} %param.9), channel_id=1, source_target_pairs={{8,0},{16,8},{24,16},{28,24},{20,28},{12,20},{4,12},{0,4},{9,1},{1... | collective-permute-start | bytes 393224 | tf_op jit(solution)/shard_map/ppermute | solution.py:39
  5.7 0.0 collective-permute-start.4
  5.7 3.2 %collective-permute-start.7 = (bf16[128,512]{1,0:T(8,128)(2,1)}, bf16[128,512]{1,0:T(8,128)(2,1)S(1)}, u32[]{:S(2)}, u32[]{:S(2)}) collective-permute-start(bf16[128,512]{1,0:T(8,128)(2,1)} %param.9), channel_id=1, source_target_pairs={{0,8},{8,16},{16,24},{24,28},{28,20},{20,12},{12,4},{4,0},{1,9},{9... | collective-permute-start | bytes 393224 | tf_op jit(solution)/shard_map/ppermute | solution.py:39
  8.8 0.0 collective-permute-done.1.refs_3_
  8.8 0.0 collective-permute-start.6
  8.8 0.0 collective-permute-done.5.refs_2_
  8.8 1.6 %collective-permute-start.2 = (bf16[128,512]{1,0:T(8,128)(2,1)S(1)}, bf16[128,512]{1,0:T(8,128)(2,1)S(1)}, u32[]{:S(2)}, u32[]{:S(2)}) collective-permute-start(bf16[128,512]{1,0:T(8,128)(2,1)S(1)} %collective-permute-done.1.refs_3_), channel_id=1, source_target_pairs={{0,4},{4,0},{8,12},{12,8},{16,20},{20,16},{24,28},{28,24},{1,5},{5... | collective-permute-start | bytes 393224 | tf_op jit(solution)/shard_map/ppermute | solution.py:28
  10.4 0.0 collective-permute-done.seen.refs_7_.refs_8_
  10.4 1.5 %collective-permute-start.3 = (bf16[128,512]{1,0:T(8,128)(2,1)S(1)}, bf16[128,512]{1,0:T(8,128)(2,1)S(1)}, u32[]{:S(2)}, u32[]{:S(2)}) collective-permute-start(bf16[128,512]{1,0:T(8,128)(2,1)S(1)} %collective-permute-done.seen.refs_7_.refs_8_), channel_id=1, source_target_pairs={{0,4},{4,0},{8,12},{12,8},{16,20},{20,16},{24,28},{28,24},{1,5},{5... | collective-permute-start | bytes 393224 | tf_op jit(solution)/shard_map/ppermute | solution.py:28
  11.9 1.1 %pad_add_fusion.joined = bf16[384,512]{1,0:T(8,128)(2,1)S(1)} fusion(bf16[128,512]{1,0:T(8,128)(2,1)} %param.9, bf16[128,512]{1,0:T(8,128)(2,1)} %param.8, bf16[128,512]{1,0:T(8,128)(2,1)} %param.7), kind=kLoop, calls=%fused_computation | loop fusion | flops 1179648 | bytes 786432 | tf_op jit(solution)/shard_map/add | solution.py:444
  13.0 0.0 collective-permute-done.4.refs_1_
  13.0 2.0 %collective-permute-start.10 = (bf16[128,512]{1,0:T(8,128)(2,1)S(1)}, bf16[128,512]{1,0:T(8,128)(2,1)S(1)}, u32[]{:S(2)}, u32[]{:S(2)}) collective-permute-start(bf16[128,512]{1,0:T(8,128)(2,1)S(1)} %get-tuple-element.38.q), channel_id=1, source_target_pairs={{0,8},{8,16},{16,24},{24,28},{28,20},{20,12},{12,4},{4,0},{1,9},{9... | collective-permute-start | bytes 393224 | tf_op jit(solution)/shard_map/ppermute | solution.py:39
  15.0 0.0 collective-permute-done.7.refs_6_.refs_7_
  15.0 0.1 collective-permute-start.9
  15.1 0.0 collective-permute-done.6.refs_5_.refs_6_
  15.1 0.6 %forward.1 = (f32[128,512]{1,0:T(8,128)S(1)}, f32[128,512]{1,0:T(8,128)S(1)}, f32[128,512]{1,0:T(8,128)S(1)}) custom-call(bf16[128,512]{1,0:T(8,128)(2,1)S(1)} %get-tuple-element.38.q, bf16[128,512]{1,0:T(8,128)(2,1)S(1)} %get-tuple-element.39.refs_0_.key, bf16[128,512]{1,0:T(8,128)(2,1)S(1)} %collective-permute-done.4.refs_1_, ...), custom_call_target="tpu_custom_call" | custom-call | bytes 3690000 | tf_op jit(solution)/shard_map/forward/pallas_call | solution.py:74
  15.7 0.0 collective-permute-done.2.relay_key.refs_4_
  15.7 2.3 %collective-permute-done.3.relay_value.refs_9_ = bf16[128,512]{1,0:T(8,128)(2,1)S(1)} collective-permute-done((bf16[128,512]{1,0:T(8,128)(2,1)S(1)}, bf16[128,512]{1,0:T(8,128)(2,1)S(1)}, u32[]{:S(2)}, u32[]{:S(2)}) %collective-permute-start.3) | collective-permute-done | bytes 131104 | tf_op jit(solution)/shard_map/ppermute | solution.py:28
  18.0 0.7 %project.1 = (bf16[128,512]{1,0:T(8,128)(2,1)S(1)}, f32[128,512]{1,0:T(8,128)S(1)}, bf16[128,512]{1,0:T(8,128)(2,1)S(1)}, bf16[128,512]{1,0:T(8,128)(2,1)S(1)}) custom-call(bf16[128,512]{1,0:T(8,128)(2,1)S(1)} %get-tuple-element.38.q, bf16[128,512]{1,0:T(8,128)(2,1)S(1)} %collective-permute-done.2.relay_key.refs_4_, ...), custom_call_target="tpu_custom_call" | custom-call | bytes 3690000 | tf_op jit(solution)/shard_map/project/pallas_call | solution.py:74
  18.7 0.0 copy-start.1
  18.7 0.0 copy-start.3
  18.8 0.0 copy-start.2
  18.8 0.1 collective-permute-start.8
  18.8 1.5 %collective-permute-done.10.seen_b.refs_2_ = bf16[128,512]{1,0:T(8,128)(2,1)S(1)} collective-permute-done((bf16[128,512]{1,0:T(8,128)(2,1)S(1)}, bf16[128,512]{1,0:T(8,128)(2,1)S(1)}, u32[]{:S(2)}, u32[]{:S(2)}) %collective-permute-start.10) | collective-permute-done | bytes 131104 | tf_op jit(solution)/shard_map/ppermute | solution.py:39
  20.4 0.0 collective-permute-done.9.seen_a.q_second.refs_3_
  20.4 0.3 project_own.1
  20.7 0.1 collective-permute-start.11
  20.8 0.0 collective-permute-done.8.core
  20.8 1.6 %collective-permute-start.12 = (bf16[128,512]{1,0:T(8,128)(2,1)S(1)}, bf16[128,512]{1,0:T(8,128)(2,1)S(1)}, u32[]{:S(2)}, u32[]{:S(2)}) collective-permute-start(bf16[128,512]{1,0:T(8,128)(2,1)S(1)} %get-tuple-element.50), channel_id=1, source_target_pairs={{0,2},{1,3},{2,0},{3,1},{4,6},{5,7},{6,4},{7,5},{8,10},{9,11},{10,... | collective-permute-start | bytes 393224 | tf_op jit(solution)/shard_map/ppermute | solution.py:28
  22.4 0.2 collective-permute-start.15
  22.6 0.0 collective-permute-done.11.core
  22.6 4.2 %collective-permute-done.12.across = bf16[128,512]{1,0:T(8,128)(2,1)S(1)} collective-permute-done((bf16[128,512]{1,0:T(8,128)(2,1)S(1)}, bf16[128,512]{1,0:T(8,128)(2,1)S(1)}, u32[]{:S(2)}, u32[]{:S(2)}) %collective-permute-start.12) | collective-permute-done | bytes 131104 | tf_op jit(solution)/shard_map/ppermute | solution.py:28
  26.8 0.1 hidden.1
  26.8 1.5 %collective-permute-start.13 = (bf16[48,512]{1,0:T(8,128)(2,1)S(1)}, bf16[48,512]{1,0:T(8,128)(2,1)S(1)}, u32[]{:S(2)}, u32[]{:S(2)}) collective-permute-start(bf16[48,512]{1,0:T(8,128)(2,1)S(1)} %get-tuple-element.52), channel_id=1, source_target_pairs={{0,4},{4,0},{8,12},{12,8},{16,20},{20,16},{24,28},{28,24},{1,5},{5... | collective-permute-start | bytes 147464 | tf_op jit(solution)/shard_map/ppermute | solution.py:28
  28.3 0.0 collective-permute-start.14
  28.3 0.0 collective-permute-done.15.seen.refs_1_
  28.3 1.6 %conv_inner.1 = (bf16[128,512]{1,0:T(8,128)(2,1)S(1)}, f32[64,512]{1,0:T(8,128)S(1)}, f32[128,512]{1,0:T(8,128)S(1)}) custom-call(bf16[128,512]{1,0:T(8,128)(2,1)S(1)} %get-tuple-element.51.hidden, bf16[128,512]{1,0:T(8,128)(2,1)S(1)} %copy-done.1, f32[31,512]{1,0:T(8,128)S(1)} %copy-done.2, bf16[128,512]{1,0:T(8,128)(2,1)S(1)} %collective-permute-done.15.seen.refs_1_), custom_call_target="tpu_custom_call" | custom-call | bytes 5904000 | tf_op jit(solution)/shard_map/conv_inner/pallas_call | solution.py:74
  29.9 1.1 %collective-permute-done.13.rim_near = bf16[48,512]{1,0:T(8,128)(2,1)S(1)} collective-permute-done((bf16[48,512]{1,0:T(8,128)(2,1)S(1)}, bf16[48,512]{1,0:T(8,128)(2,1)S(1)}, u32[]{:S(2)}, u32[]{:S(2)}) %collective-permute-start.13) | collective-permute-done | bytes 49184 | tf_op jit(solution)/shard_map/ppermute | solution.py:28
  31.0 0.0 collective-permute-done.14.rim_far
  31.0 0.7 %conv_edge.1 = (bf16[128,512]{1,0:T(8,128)(2,1)S(1)}, bf16[128,512]{1,0:T(8,128)(2,1)S(1)}, bf16[128,512]{1,0:T(8,128)(2,1)S(1)}) custom-call(bf16[128,512]{1,0:T(8,128)(2,1)S(1)} %get-tuple-element.51.hidden, bf16[48,512]{1,0:T(8,128)(2,1)S(1)} %collective-permute-done.13.rim_near, bf16[48,512]{1,0:T(8,128)(2,1)S(1)} %collective-permute-done.14.rim_far, ...), custom_call_target="tpu_custom_call" | custom-call | bytes 2952000 | tf_op jit(solution)/shard_map/conv_edge/pallas_call | solution.py:74
  31.7 0.1 collective-permute-start.17
  31.8 1.6 %collective-permute-start.16 = (bf16[128,512]{1,0:T(8,128)(2,1)S(1)}, bf16[128,512]{1,0:T(8,128)(2,1)S(1)}, u32[]{:S(2)}, u32[]{:S(2)}) collective-permute-start(bf16[128,512]{1,0:T(8,128)(2,1)S(1)} %get-tuple-element.57.own.grad_here), channel_id=1, source_target_pairs={{0,2},{1,3},{2,0},{3,1},{4,6},{5,7},{6,4},{7,5},{8,10},{9,11},{10,... | collective-permute-start | bytes 393224 | tf_op jit(solution)/shard_map/ppermute | solution.py:28
  33.4 2.9 %collective-permute-start.19 = (bf16[128,512]{1,0:T(8,128)(2,1)S(1)}, bf16[128,512]{1,0:T(8,128)(2,1)S(1)}, u32[]{:S(2)}, u32[]{:S(2)}) collective-permute-start(bf16[128,512]{1,0:T(8,128)(2,1)S(1)} %get-tuple-element.59), channel_id=1, source_target_pairs={{0,4},{4,0},{8,12},{12,8},{16,20},{20,16},{24,28},{28,24},{1,5},{5... | collective-permute-start | bytes 393224 | tf_op jit(solution)/shard_map/ppermute | solution.py:28
  36.3 0.0 collective-permute-done.17.core
  36.3 0.5 upstream_chip.1.seen.before
  36.8 0.9 %collective-permute-done.16.block = bf16[128,512]{1,0:T(8,128)(2,1)S(1)} collective-permute-done((bf16[128,512]{1,0:T(8,128)(2,1)S(1)}, bf16[128,512]{1,0:T(8,128)(2,1)S(1)}, u32[]{:S(2)}, u32[]{:S(2)}) %collective-permute-start.16) | collective-permute-done | bytes 131104 | tf_op jit(solution)/shard_map/ppermute | solution.py:28
  37.8 0.1 collective-permute-start.18
  37.8 0.3 upstream_across.1.partial
  38.2 2.0 %collective-permute-done.19.seen.refs_4_.query = bf16[128,512]{1,0:T(8,128)(2,1)S(1)} collective-permute-done((bf16[128,512]{1,0:T(8,128)(2,1)S(1)}, bf16[128,512]{1,0:T(8,128)(2,1)S(1)}, u32[]{:S(2)}, u32[]{:S(2)}) %collective-permute-start.19) | collective-permute-done | bytes 131104 | tf_op jit(solution)/shard_map/ppermute | solution.py:28
  40.2 0.0 collective-permute-done.18.cross
  40.2 0.5 upstream.1
  40.6 2.0 %collective-permute-start.20 = (bf16[144,512]{1,0:T(8,128)(2,1)S(1)}, bf16[144,512]{1,0:T(8,128)(2,1)S(1)}, u32[]{:S(2)}, u32[]{:S(2)}) collective-permute-start(bf16[144,512]{1,0:T(8,128)(2,1)S(1)} %get-tuple-element.60.message.refs_5_), channel_id=1, source_target_pairs={{8,0},{16,8},{24,16},{28,24},{20,28},{12,20},{4,12},{0,4},{9,1},{1... | collective-permute-start | bytes 442376 | tf_op jit(solution)/shard_map/ppermute | solution.py:39
  42.6 1.4 %collective-permute-start.23 = (bf16[144,512]{1,0:T(8,128)(2,1)S(1)}, bf16[144,512]{1,0:T(8,128)(2,1)S(1)}, u32[]{:S(2)}, u32[]{:S(2)}) collective-permute-start(bf16[144,512]{1,0:T(8,128)(2,1)S(1)} %get-tuple-element.60.message.refs_5_), channel_id=1, source_target_pairs={{0,8},{8,16},{16,24},{24,28},{28,20},{20,12},{12,4},{4,0},{1,9},{9... | collective-permute-start | bytes 442376 | tf_op jit(solution)/shard_map/ppermute | solution.py:39
  44.0 0.0 collective-permute-start.22
  44.0 4.1 %collective-permute-done.20.refs_8_ = bf16[144,512]{1,0:T(8,128)(2,1)S(1)} collective-permute-done((bf16[144,512]{1,0:T(8,128)(2,1)S(1)}, bf16[144,512]{1,0:T(8,128)(2,1)S(1)}, u32[]{:S(2)}, u32[]{:S(2)}) %collective-permute-start.20) | collective-permute-done | bytes 147488 | tf_op jit(solution)/shard_map/ppermute | solution.py:39
  48.1 0.5 collective-permute-start.21
  48.5 1.6 %query_grad.1 = (bf16[128,512]{1,0:T(8,128)(2,1)}, bf16[128,512]{1,0:T(8,128)(2,1)}, bf16[128,512]{1,0:T(8,128)(2,1)}) custom-call(bf16[128,512]{1,0:T(8,128)(2,1)S(1)} %get-tuple-element.46.q.refs_0_, bf16[144,512]{1,0:T(8,128)(2,1)S(1)} %get-tuple-element.60.message.refs_5_, f32[128,512]{1,0:T(8,128)S(1)} %get-tuple-element.58.lse, ...), custom_call_target="tpu_custom_call" | custom-call | bytes 6642000 | tf_op jit(solution)/shard_map/query_grad/pallas_call | solution.py:74
  50.1 0.0 collective-permute-done.23.refs_7_
  50.1 0.0 collective-permute-done.22.refs_6_
  50.1 0.9 %key_part.1 = (f32[128,512]{1,0:T(8,128)S(1)}, f32[128,512]{1,0:T(8,128)S(1)}, f32[128,512]{1,0:T(8,128)S(1)}) custom-call(bf16[128,512]{1,0:T(8,128)(2,1)S(1)} %get-tuple-element.39.refs_0_.key, bf16[128,512]{1,0:T(8,128)(2,1)S(1)} %get-tuple-element.40.refs_4_.refs_5_.value, bf16[128,512]{1,0:T(8,128)(2,1)S(1)} %get-tuple-element.46.q.refs_0_, ...), custom_call_target="tpu_custom_call" | custom-call | bytes 5535000 | tf_op jit(solution)/shard_map/key_part/pallas_call | solution.py:74
  51.0 2.5 %collective-permute-done.21.message = bf16[144,512]{1,0:T(8,128)(2,1)S(1)} collective-permute-done((bf16[144,512]{1,0:T(8,128)(2,1)S(1)}, bf16[144,512]{1,0:T(8,128)(2,1)S(1)}, u32[]{:S(2)}, u32[]{:S(2)}) %collective-permute-start.21) | collective-permute-done | bytes 147488 | tf_op jit(solution)/shard_map/ppermute | solution.py:28
  53.5 1.0 %key_grad.1 = (bf16[128,512]{1,0:T(8,128)(2,1)}, bf16[128,512]{1,0:T(8,128)(2,1)}) custom-call(bf16[128,512]{1,0:T(8,128)(2,1)S(1)} %get-tuple-element.40.refs_4_.refs_5_.value, bf16[128,512]{1,0:T(8,128)(2,1)S(1)} %collective-permute-done.19.seen.refs_4_.query, bf16[144,512]{1,0:T(8,128)(2,1)S(1)} %collective-permute-done.21.message, ...), custom_call_target="tpu_custom_call" | custom-call | bytes 3690000 | tf_op jit(solution)/shard_map/key_grad/pallas_call | solution.py:74
  (8 shorter events, 0.1 us)
Async XLA Ops:
  0.6 17.4 %copy-start = (bf16[512,2048]{1,0:T(8,128)(2,1)S(1)}, bf16[512,2048]{1,0:T(8,128)(2,1)}, u32[]{:S(2)}) copy-start(bf16[512,2048]{1,0:T(8,128)(2,1)} %weight.9) | copy-start | bytes 6291460
  0.6 8.2 %collective-permute-start.1 = (bf16[128,512]{1,0:T(8,128)(2,1)}, bf16[128,512]{1,0:T(8,128)(2,1)S(1)}, u32[]{:S(2)}, u32[]{:S(2)}) collective-permute-start(bf16[128,512]{1,0:T(8,128)(2,1)} %param.8), channel_id=1, source_target_pairs={{8,0},{16,8},{24,16},{28,24},{20,28},{12,20},{4,12},{0,4},{9,1},{1... | collective-permute-start | bytes 393224 | tf_op jit(solution)/shard_map/ppermute | solution.py:39
  3.6 5.2 %collective-permute-start.5 = (bf16[128,512]{1,0:T(8,128)(2,1)}, bf16[128,512]{1,0:T(8,128)(2,1)S(1)}, u32[]{:S(2)}, u32[]{:S(2)}) collective-permute-start(bf16[128,512]{1,0:T(8,128)(2,1)} %param.8), channel_id=1, source_target_pairs={{0,8},{8,16},{16,24},{24,28},{28,20},{20,12},{12,4},{4,0},{1,9},{9... | collective-permute-start | bytes 393224 | tf_op jit(solution)/shard_map/ppermute | solution.py:39
  3.8 6.6 %collective-permute-start = (bf16[128,512]{1,0:T(8,128)(2,1)}, bf16[128,512]{1,0:T(8,128)(2,1)S(1)}, u32[]{:S(2)}, u32[]{:S(2)}) collective-permute-start(bf16[128,512]{1,0:T(8,128)(2,1)} %param.9), channel_id=1, source_target_pairs={{8,0},{16,8},{24,16},{28,24},{20,28},{12,20},{4,12},{0,4},{9,1},{1... | collective-permute-start | bytes 393224 | tf_op jit(solution)/shard_map/ppermute | solution.py:39
  5.7 7.3 %collective-permute-start.4 = (bf16[128,512]{1,0:T(8,128)(2,1)}, bf16[128,512]{1,0:T(8,128)(2,1)S(1)}, u32[]{:S(2)}, u32[]{:S(2)}) collective-permute-start(bf16[128,512]{1,0:T(8,128)(2,1)} %param.8), channel_id=1, source_target_pairs={{0,1},{1,0},{2,3},{3,2},{4,5},{5,4},{6,7},{7,6},{8,12},{9,13},{10,... | collective-permute-start | bytes 393224 | tf_op jit(solution)/shard_map/ppermute | solution.py:50
  5.7 9.3 %collective-permute-start.7 = (bf16[128,512]{1,0:T(8,128)(2,1)}, bf16[128,512]{1,0:T(8,128)(2,1)S(1)}, u32[]{:S(2)}, u32[]{:S(2)}) collective-permute-start(bf16[128,512]{1,0:T(8,128)(2,1)} %param.9), channel_id=1, source_target_pairs={{0,8},{8,16},{16,24},{24,28},{28,20},{20,12},{12,4},{4,0},{1,9},{9... | collective-permute-start | bytes 393224 | tf_op jit(solution)/shard_map/ppermute | solution.py:39
  8.8 6.3 %collective-permute-start.6 = (bf16[128,512]{1,0:T(8,128)(2,1)}, bf16[128,512]{1,0:T(8,128)(2,1)S(1)}, u32[]{:S(2)}, u32[]{:S(2)}) collective-permute-start(bf16[128,512]{1,0:T(8,128)(2,1)} %param.9), channel_id=1, source_target_pairs={{0,1},{1,0},{2,3},{3,2},{4,5},{5,4},{6,7},{7,6},{8,12},{9,13},{10,... | collective-permute-start | bytes 393224 | tf_op jit(solution)/shard_map/ppermute | solution.py:50
  8.8 6.9 %collective-permute-start.2 = (bf16[128,512]{1,0:T(8,128)(2,1)S(1)}, bf16[128,512]{1,0:T(8,128)(2,1)S(1)}, u32[]{:S(2)}, u32[]{:S(2)}) collective-permute-start(bf16[128,512]{1,0:T(8,128)(2,1)S(1)} %collective-permute-done.1.refs_3_), channel_id=1, source_target_pairs={{0,4},{4,0},{8,12},{12,8},{16,20},{20,16},{24,28},{28,24},{1,5},{5... | collective-permute-start | bytes 393224 | tf_op jit(solution)/shard_map/ppermute | solution.py:28
  10.4 7.6 %collective-permute-start.3 = (bf16[128,512]{1,0:T(8,128)(2,1)S(1)}, bf16[128,512]{1,0:T(8,128)(2,1)S(1)}, u32[]{:S(2)}, u32[]{:S(2)}) collective-permute-start(bf16[128,512]{1,0:T(8,128)(2,1)S(1)} %collective-permute-done.seen.refs_7_.refs_8_), channel_id=1, source_target_pairs={{0,4},{4,0},{8,12},{12,8},{16,20},{20,16},{24,28},{28,24},{1,5},{5... | collective-permute-start | bytes 393224 | tf_op jit(solution)/shard_map/ppermute | solution.py:28
  13.0 7.4 %collective-permute-start.10 = (bf16[128,512]{1,0:T(8,128)(2,1)S(1)}, bf16[128,512]{1,0:T(8,128)(2,1)S(1)}, u32[]{:S(2)}, u32[]{:S(2)}) collective-permute-start(bf16[128,512]{1,0:T(8,128)(2,1)S(1)} %get-tuple-element.38.q), channel_id=1, source_target_pairs={{0,8},{8,16},{16,24},{24,28},{28,20},{20,12},{12,4},{4,0},{1,9},{9... | collective-permute-start | bytes 393224 | tf_op jit(solution)/shard_map/ppermute | solution.py:39
  15.0 5.4 %collective-permute-start.9 = (bf16[128,512]{1,0:T(8,128)(2,1)S(1)}, bf16[128,512]{1,0:T(8,128)(2,1)S(1)}, u32[]{:S(2)}, u32[]{:S(2)}) collective-permute-start(bf16[128,512]{1,0:T(8,128)(2,1)S(1)} %get-tuple-element.38.q), channel_id=1, source_target_pairs={{8,0},{16,8},{24,16},{28,24},{20,28},{12,20},{4,12},{0,4},{9,1},{1... | collective-permute-start | bytes 393224 | tf_op jit(solution)/shard_map/ppermute | solution.py:39
  18.7 8.0 %copy-start.1 = (bf16[128,512]{1,0:T(8,128)(2,1)S(1)}, bf16[128,512]{1,0:T(8,128)(2,1)}, u32[]{:S(2)}) copy-start(bf16[128,512]{1,0:T(8,128)(2,1)} %cot.5) | copy-start | bytes 393220
  18.7 8.0 %copy-start.3 = (bf16[128,512]{1,0:T(8,128)(2,1)S(1)}, bf16[128,512]{1,0:T(8,128)(2,1)}, u32[]{:S(2)}) copy-start(bf16[128,512]{1,0:T(8,128)(2,1)} %inputs.1) | copy-start | bytes 393220
  18.8 9.6 %copy-start.2 = (f32[31,512]{1,0:T(8,128)S(1)}, f32[31,512]{1,0:T(8,128)}, u32[]{:S(2)}) copy-start(f32[31,512]{1,0:T(8,128)} %taps.3) | copy-start | bytes 190468
  18.8 2.0 %collective-permute-start.8 = (bf16[128,512]{1,0:T(8,128)(2,1)S(1)}, bf16[128,512]{1,0:T(8,128)(2,1)S(1)}, u32[]{:S(2)}, u32[]{:S(2)}) collective-permute-start(bf16[128,512]{1,0:T(8,128)(2,1)S(1)} %get-tuple-element.45), channel_id=1, source_target_pairs={{0,1},{1,0},{2,3},{3,2},{4,5},{5,4},{6,7},{7,6},{8,9},{9,8},{10,11... | collective-permute-start | bytes 393224 | tf_op jit(solution)/shard_map/ppermute | solution.py:28
  20.7 1.9 %collective-permute-start.11 = (bf16[128,512]{1,0:T(8,128)(2,1)S(1)}, bf16[128,512]{1,0:T(8,128)(2,1)S(1)}, u32[]{:S(2)}, u32[]{:S(2)}) collective-permute-start(bf16[128,512]{1,0:T(8,128)(2,1)S(1)} %get-tuple-element.49), channel_id=1, source_target_pairs={{0,1},{1,0},{2,3},{3,2},{4,5},{5,4},{6,7},{7,6},{8,9},{9,8},{10,11... | collective-permute-start | bytes 393224 | tf_op jit(solution)/shard_map/ppermute | solution.py:28
  20.8 6.0 %collective-permute-start.12 = (bf16[128,512]{1,0:T(8,128)(2,1)S(1)}, bf16[128,512]{1,0:T(8,128)(2,1)S(1)}, u32[]{:S(2)}, u32[]{:S(2)}) collective-permute-start(bf16[128,512]{1,0:T(8,128)(2,1)S(1)} %get-tuple-element.50), channel_id=1, source_target_pairs={{0,2},{1,3},{2,0},{3,1},{4,6},{5,7},{6,4},{7,5},{8,10},{9,11},{10,... | collective-permute-start | bytes 393224 | tf_op jit(solution)/shard_map/ppermute | solution.py:28
  22.4 5.9 %collective-permute-start.15 = (bf16[128,512]{1,0:T(8,128)(2,1)S(1)}, bf16[128,512]{1,0:T(8,128)(2,1)S(1)}, u32[]{:S(2)}, u32[]{:S(2)}) collective-permute-start(bf16[128,512]{1,0:T(8,128)(2,1)S(1)} %get-tuple-element.46.q.refs_0_), channel_id=1, source_target_pairs={{0,1},{1,0},{2,3},{3,2},{4,5},{5,4},{6,7},{7,6},{8,12},{9,13},{10,... | collective-permute-start | bytes 393224 | tf_op jit(solution)/shard_map/ppermute | solution.py:50
  26.8 4.2 %collective-permute-start.13 = (bf16[48,512]{1,0:T(8,128)(2,1)S(1)}, bf16[48,512]{1,0:T(8,128)(2,1)S(1)}, u32[]{:S(2)}, u32[]{:S(2)}) collective-permute-start(bf16[48,512]{1,0:T(8,128)(2,1)S(1)} %get-tuple-element.52), channel_id=1, source_target_pairs={{0,4},{4,0},{8,12},{12,8},{16,20},{20,16},{24,28},{28,24},{1,5},{5... | collective-permute-start | bytes 147464 | tf_op jit(solution)/shard_map/ppermute | solution.py:28
  28.3 2.7 %collective-permute-start.14 = (bf16[48,512]{1,0:T(8,128)(2,1)S(1)}, bf16[48,512]{1,0:T(8,128)(2,1)S(1)}, u32[]{:S(2)}, u32[]{:S(2)}) collective-permute-start(bf16[48,512]{1,0:T(8,128)(2,1)S(1)} %get-tuple-element.53), channel_id=1, source_target_pairs={{0,1},{1,0},{2,3},{3,2},{4,8},{5,9},{6,10},{7,11},{8,4},{9,5},{10,... | collective-permute-start | bytes 147464 | tf_op jit(solution)/shard_map/ppermute | solution.py:50
  31.7 4.6 %collective-permute-start.17 = (bf16[128,512]{1,0:T(8,128)(2,1)S(1)}, bf16[128,512]{1,0:T(8,128)(2,1)S(1)}, u32[]{:S(2)}, u32[]{:S(2)}) collective-permute-start(bf16[128,512]{1,0:T(8,128)(2,1)S(1)} %get-tuple-element.57.own.grad_here), channel_id=1, source_target_pairs={{0,1},{1,0},{2,3},{3,2},{4,5},{5,4},{6,7},{7,6},{8,9},{9,8},{10,11... | collective-permute-start | bytes 393224 | tf_op jit(solution)/shard_map/ppermute | solution.py:28
  31.8 5.9 %collective-permute-start.16 = (bf16[128,512]{1,0:T(8,128)(2,1)S(1)}, bf16[128,512]{1,0:T(8,128)(2,1)S(1)}, u32[]{:S(2)}, u32[]{:S(2)}) collective-permute-start(bf16[128,512]{1,0:T(8,128)(2,1)S(1)} %get-tuple-element.57.own.grad_here), channel_id=1, source_target_pairs={{0,2},{1,3},{2,0},{3,1},{4,6},{5,7},{6,4},{7,5},{8,10},{9,11},{10,... | collective-permute-start | bytes 393224 | tf_op jit(solution)/shard_map/ppermute | solution.py:28
  33.4 6.7 %collective-permute-start.19 = (bf16[128,512]{1,0:T(8,128)(2,1)S(1)}, bf16[128,512]{1,0:T(8,128)(2,1)S(1)}, u32[]{:S(2)}, u32[]{:S(2)}) collective-permute-start(bf16[128,512]{1,0:T(8,128)(2,1)S(1)} %get-tuple-element.59), channel_id=1, source_target_pairs={{0,4},{4,0},{8,12},{12,8},{16,20},{20,16},{24,28},{28,24},{1,5},{5... | collective-permute-start | bytes 393224 | tf_op jit(solution)/shard_map/ppermute | solution.py:28
  37.8 2.4 %collective-permute-start.18 = (bf16[128,512]{1,0:T(8,128)(2,1)S(1)}, bf16[128,512]{1,0:T(8,128)(2,1)S(1)}, u32[]{:S(2)}, u32[]{:S(2)}) collective-permute-start(bf16[128,512]{1,0:T(8,128)(2,1)S(1)} %turn.1.across), channel_id=1, source_target_pairs={{0,1},{1,0},{2,3},{3,2},{4,5},{5,4},{6,7},{7,6},{8,9},{9,8},{10,11... | collective-permute-start | bytes 393224 | tf_op jit(solution)/shard_map/ppermute | solution.py:28
  40.6 7.4 %collective-permute-start.20 = (bf16[144,512]{1,0:T(8,128)(2,1)S(1)}, bf16[144,512]{1,0:T(8,128)(2,1)S(1)}, u32[]{:S(2)}, u32[]{:S(2)}) collective-permute-start(bf16[144,512]{1,0:T(8,128)(2,1)S(1)} %get-tuple-element.60.message.refs_5_), channel_id=1, source_target_pairs={{8,0},{16,8},{24,16},{28,24},{20,28},{12,20},{4,12},{0,4},{9,1},{1... | collective-permute-start | bytes 442376 | tf_op jit(solution)/shard_map/ppermute | solution.py:39
  42.6 7.5 %collective-permute-start.23 = (bf16[144,512]{1,0:T(8,128)(2,1)S(1)}, bf16[144,512]{1,0:T(8,128)(2,1)S(1)}, u32[]{:S(2)}, u32[]{:S(2)}) collective-permute-start(bf16[144,512]{1,0:T(8,128)(2,1)S(1)} %get-tuple-element.60.message.refs_5_), channel_id=1, source_target_pairs={{0,8},{8,16},{16,24},{24,28},{28,20},{20,12},{12,4},{4,0},{1,9},{9... | collective-permute-start | bytes 442376 | tf_op jit(solution)/shard_map/ppermute | solution.py:39
  44.0 6.1 %collective-permute-start.22 = (bf16[144,512]{1,0:T(8,128)(2,1)S(1)}, bf16[144,512]{1,0:T(8,128)(2,1)S(1)}, u32[]{:S(2)}, u32[]{:S(2)}) collective-permute-start(bf16[144,512]{1,0:T(8,128)(2,1)S(1)} %get-tuple-element.60.message.refs_5_), channel_id=1, source_target_pairs={{0,1},{1,0},{2,3},{3,2},{4,5},{5,4},{6,7},{7,6},{8,12},{9,13},{10,... | collective-permute-start | bytes 442376 | tf_op jit(solution)/shard_map/ppermute | solution.py:50
  48.1 5.4 %collective-permute-start.21 = (bf16[144,512]{1,0:T(8,128)(2,1)S(1)}, bf16[144,512]{1,0:T(8,128)(2,1)S(1)}, u32[]{:S(2)}, u32[]{:S(2)}) collective-permute-start(bf16[144,512]{1,0:T(8,128)(2,1)S(1)} %collective-permute-done.20.refs_8_), channel_id=1, source_target_pairs={{0,4},{4,0},{8,12},{12,8},{16,20},{20,16},{24,28},{28,24},{1,5},{5... | collective-permute-start | bytes 442376 | tf_op jit(solution)/shard_map/ppermute | solution.py:28

commit v7 on v5

--- a/solution.py
+++ b/solution.py
@@ -160,8 +160,24 @@
     return weight[:, pl.ds(pl.multiple_of(at, 128), width)]
 
 
-def hold_body(block, seen, held):
-    held[...] = block[...]
+def split_body(joined, taps, seen, query, given):
+    frames = query.shape[0]
+    query[...] = joined[0:frames, :]
+    given[0 : 2 * frames, :] = joined[frames : 3 * frames, :]
+    rows, at = pad_rows(taps), 2 * frames
+    for k in range(3):
+        term = rows.astype(BF16)
+        rows = rows - term.astype(F32)
+        given[at + k * 2 * HALO : at + (k + 1) * 2 * HALO, :] = term
+
+
+def pad_rows(taps):
+    return jnp.concatenate([taps[...], jnp.zeros((2 * HALO - taps.shape[0], taps.shape[1]), F32)], axis=0)
+
+
+def taps_of(other, frames):
+    rows = other[2 * frames :, :].astype(F32)
+    return rows[0 : 2 * HALO] + rows[2 * HALO : 4 * HALO] + rows[4 * HALO :]
 
 
 def forward_body(scale, q, own, near, first, second, sums, tops, totals):
@@ -194,42 +210,48 @@
     total = [totals[:, c] * k + s[:, HDIM:] for c, k, s in zip(heads, shrink, late)]
     summed = [sums[:, c] * k + s[:, 0:HDIM] for c, k, s in zip(heads, shrink, late)]
     attended = jnp.concatenate([(s * (1.0 / t)).astype(BF16) for s, t in zip(summed, total)], axis=1)
-    sent = dot_nn(attended, weight_columns(weight, 3)).astype(BF16)
-    kept = dot_nn(attended, weight_columns(weight, 2)).astype(BF16)
+    sent = [dot_nn(attended, weight_columns(weight, flip)).astype(BF16) for flip in (1, 3)]
+    kept = [dot_nn(attended, weight_columns(weight, flip)).astype(BF16) for flip in (0, 2)]
     logs = [t + jnp.log(n) for t, n in zip(top, total)]
     att[...] = attended
-    send[...] = sent
-    keep[...] = kept
+    send[...] = jnp.concatenate(sent, axis=1)
+    keep[...] = jnp.concatenate(kept, axis=1)
     for c, part in zip(heads, logs):
         lse[:, c] = part
 
 
-def project_own_body(att, weight, seen_a, seen_b, send, keep):
-    sent = dot_nn(att[...], weight_columns(weight, 1)).astype(BF16)
-    kept = dot_nn(att[...], weight_columns(weight, 0)).astype(BF16)
-    send[...] = sent
-    keep[...] = kept
-
-
-def join_body(keep, core, q, outgoing, q_copy):
-    outgoing[...] = (keep[...].astype(F32) + core[...].astype(F32)).astype(BF16)
+def pass_body(send, q, q_second, seen, send_copy, q_copy, second_copy):
+    send_copy[...] = send[...]
     q_copy[...] = q[...]
-
-
-def hidden_body(inputs, keep, core, across, cot, hidden, rim_near, rim_far):
+    second_copy[...] = q_second[...]
+
+
+def join_body(keep, core, q, q_second, seen, chip, q_copy, second_copy):
+    chip[...] = (keep[...].astype(F32) + core[...].astype(F32)).astype(BF16)
+    q_copy[...] = q[...]
+    second_copy[...] = q_second[...]
+
+
+def hidden_body(chip, across, inputs, cot, other, hidden, rim_near, rim_far):
     frames, width = inputs.shape
     wide = 2 * HALO
-    total = inputs[...].astype(F32) + keep[...].astype(F32) + core[...].astype(F32)
-    total = (total + across[...].astype(F32)).astype(BF16)
     even = is_even()
-    for at, first, last in (
-        (slice(0, wide), total[0:wide], total[frames - wide :]),
-        (slice(wide, wide + HALO), cot[0:HALO, :], cot[frames - HALO : frames, :]),
+    mine, its = slice(0, width), slice(width, 2 * width)
+    every = slice(0, frames)
+    for cols, back, rows, cots in (
+        (mine, its, inputs[...], cot[...]),
+        (its, mine, other[every, :], other[frames : 2 * frames, :]),
     ):
-        first, last = first.astype(F32), last.astype(F32)
-        rim_near[at, :] = jnp.where(even, last, first).astype(BF16)
-        rim_far[at, :] = jnp.where(even, first, last).astype(BF16)
-    hidden[...] = total
+        mixed = chip[:, cols].astype(F32) + across[:, back].astype(F32)
+        total = (rows.astype(F32) + mixed).astype(BF16)
+        for at, first, last in (
+            (slice(0, wide), total[0:wide], total[frames - wide :]),
+            (slice(wide, wide + HALO), cots[0:HALO], cots[frames - HALO :]),
+        ):
+            first, last = first.astype(F32), last.astype(F32)
+            rim_near[at, cols] = jnp.where(even, last, first).astype(BF16)
+            rim_far[at, cols] = jnp.where(even, first, last).astype(BF16)
+        hidden[:, cols] = total
 
 
 def shifted_sum(rows, taps_of, count):
@@ -255,43 +277,49 @@
     return conv * gate, grad.astype(BF16).astype(F32)
 
 
-def taps_forward(taps, cols):
-    count = taps.shape[0]
+def taps_forward(taps, count, cols):
     return lambda s: taps[s - 1 : s, cols] if 1 <= s <= count else None
 
 
-def taps_backward(taps, cols):
-    count = taps.shape[0]
+def taps_backward(taps, count, cols):
     return lambda s: taps[count - s : count - s + 1, cols] if 1 <= s <= count else None
 
 
-def conv_inner_body(hidden, cot, taps, seen, rows_out, edge_conv, part_grad):
-    frames, width = hidden.shape
-    wide = 2 * HALO
+def conv_chunks(frames, width, cot, other, taps):
+    taps_other = taps_of(other, frames)
+    for k, cols in enumerate(columns(2 * width)):
+        own = k * HDIM < width
+        local = cols if own else slice(cols.start - width, cols.stop - width)
+        yield own, cols, local, 0 if own else frames, cot if own else other, taps if own else taps_other
+
+
+def conv_inner_body(hidden, cot, other, taps, seen_a, seen_b, rows_out, edge_conv, part_grad):
+    frames, width = cot.shape
+    wide, count = 2 * HALO, taps.shape[0]
     inner = slice(HALO, frames - HALO)
     none = jnp.zeros((wide, HDIM), F32)
-    for cols in columns(width):
-        own = hidden[:, cols].astype(F32)
-        cots = cot[:, cols].astype(F32)
+    for own, cols, local, at, cots_of, tap in conv_chunks(frames, width, cot, other, taps):
+        rows = hidden[:, cols].astype(F32)
+        cots = cots_of[at : at + frames, local].astype(F32)
         conv = shifted_sum(
-            jnp.concatenate([none, own, none], axis=0), taps_forward(taps, cols), frames + wide
+            jnp.concatenate([none, rows, none], axis=0), taps_forward(tap, count, local), frames + wide
         )
         silu, grad = silu_parts(conv[wide:frames], cots[inner])
         back = shifted_sum(
-            jnp.concatenate([none, grad, none], axis=0), taps_backward(taps, cols), frames
+            jnp.concatenate([none, grad, none], axis=0), taps_backward(tap, count, local), frames
         )
         edge_conv[0:wide, cols] = conv[0:wide]
         edge_conv[wide : 2 * wide, cols] = conv[frames : frames + wide]
-        rows_out[inner, cols] = (own[inner] + silu).astype(BF16)
+        if own:
+            rows_out[inner, cols] = (rows[inner] + silu).astype(BF16)
         part_grad[:, cols] = cots + back
 
 
 def conv_edge_body(
-    hidden, rim_near, rim_far, cot, taps, rows_in, edge_conv, part_grad, q_second,
-    output, grad_input, second_copy,
+    hidden, rim_near, rim_far, cot, other, taps, rows_in, edge_conv, part_grad, output, grad_input,
 ):
-    frames, width = hidden.shape
-    wide = 2 * HALO
+    frames, width = cot.shape
+    wide, count = 2 * HALO, taps.shape[0]
     even, far = is_even(), far_there()
     rims, cots_of = slice(0, wide), slice(wide, wide + HALO)
     low, high = slice(0, HALO), slice(frames - HALO, frames)
@@ -303,42 +331,46 @@
         beyond = jnp.where(far, rim_far[rows, cols].astype(F32), 0.0)
         return jnp.where(even, beyond, near), jnp.where(even, near, beyond)
 
-    for cols in columns(width):
+    for own, cols, local, at, block, tap in conv_chunks(frames, width, cot, other, taps):
         row_low, row_high = sides(rims, cols)
         cot_low, cot_high = sides(cots_of, cols)
         conv = edge_conv[:, cols] + shifted_sum(
-            jnp.concatenate([row_low, none, row_high], axis=0), taps_forward(taps, cols), 2 * wide
+            jnp.concatenate([row_low, none, row_high], axis=0), taps_forward(tap, count, local), 2 * wide
         )
-        cots = jnp.concatenate(
-            [cot_low, cot[low, cols].astype(F32), cot[high, cols].astype(F32), cot_high], axis=0
-        )
+        first = block[at : at + HALO, local].astype(F32)
+        last = block[at + frames - HALO : at + frames, local].astype(F32)
+        cots = jnp.concatenate([cot_low, first, last, cot_high], axis=0)
         silu, grad = silu_parts(conv, cots)
         back = shifted_sum(
-            jnp.concatenate([grad[0:wide], none, grad[wide:]], axis=0), taps_backward(taps, cols), 2 * wide
+            jnp.concatenate([grad[0:wide], none, grad[wide:]], axis=0), taps_backward(tap, count, local), 2 * wide
         )
         part = part_grad[:, cols]
         grad_input[:, cols] = jnp.concatenate(
             [part[0:wide] + back[0:wide], part[wide : frames - wide], part[frames - wide :] + back[wide:]],
             axis=0,
         ).astype(BF16)
-        output[low, cols] = (hidden[low, cols].astype(F32) + silu[HALO:wide]).astype(BF16)
-        output[inner, cols] = rows_in[inner, cols]
-        output[high, cols] = (hidden[high, cols].astype(F32) + silu[wide : wide + HALO]).astype(BF16)
-    second_copy[...] = q_second[...]
-
-
-def upstream_chip_body(own, core, weight, partial):
-    partial[...] = dot_nt(own[...], weight_columns(weight, 0)) + dot_nt(core[...], weight_columns(weight, 1))
-
-
-def upstream_across_body(across, weight, before, partial):
-    partial[...] = before[...] + dot_nt(across[...], weight_columns(weight, 2))
-
-
-def upstream_body(cross, weight, att, lse, partial, seen, message, delta):
-    frames, width = cross.shape
+        if own:
+            output[low, cols] = (hidden[low, cols].astype(F32) + silu[HALO:wide]).astype(BF16)
+            output[inner, cols] = rows_in[inner, cols]
+            output[high, cols] = (hidden[high, cols].astype(F32) + silu[wide : wide + HALO]).astype(BF16)
+
+
+def upstream_part(grads, weight, flips):
+    width = weight.shape[0]
+    return sum(
+        dot_nt(grads[:, k * width : (k + 1) * width], weight_columns(weight, flip))
+        for k, flip in enumerate(flips)
+    )
+
+
+def upstream_own_body(own, weight, partial):
+    partial[...] = upstream_part(own, weight, (0, 2))
+
+
+def upstream_body(core, weight, att, lse, partial, message, delta):
+    frames, width = att.shape
     heads = columns(width)
-    up = (partial[...] + dot_nt(cross[...], weight_columns(weight, 3))).astype(BF16)
+    up = (partial[...] + upstream_part(core, weight, (1, 3))).astype(BF16)
     products = [up[:, c].astype(F32) * att[:, c].astype(F32) for c in heads]
     deltas = [jnp.broadcast_to(jnp.sum(p, axis=1, keepdims=True), (frames, HDIM)) for p in products]
     lse_rows = tile_of([lse[:, c] for c in heads]).T
@@ -356,7 +388,7 @@
 ):
     writes = [
         pltpu.make_async_copy(output_here, output, sems.at[0]),
-        pltpu.make_async_copy(grad_here, grad_input, sems.at[1]),
+        pltpu.make_async_copy(grad_here.at[:, pl.ds(0, q.shape[1])], grad_input, sems.at[1]),
     ]
     for write in writes:
         write.start()
@@ -431,7 +463,8 @@
     scale = 1.0 / math.sqrt(HDIM)
     tile = shaped((frames, width), BF16)
     tile32 = shaped((frames, width), F32)
-    rim = shaped((wide + HALO, width), BF16)
+    rim = shaped((wide + HALO, 2 * width), BF16)
+    both = shaped((frames, 2 * width), BF16)
     noted = shaped((frames + 16, width), BF16)
 
     zero = jnp.zeros((), BF16)
@@ -439,7 +472,15 @@
         value_rows, zero, ((frames, 0, 0), (0, 0, 0))
     )
     near, first, second, relay = window_of(kv)
-    (q_early,) = kernel_call(hold_body, (tile,), (query_rows, second), 0.1, "hold", 1)
+    joined = sum(
+        lax.pad(rows, zero, ((k * frames, (2 - k) * frames, 0), (0, 0, 0)))
+        for k, rows in enumerate((query_rows, inputs, cotangent))
+    )
+    q_early, given = kernel_call(
+        split_body, (tile, shaped((2 * frames + 3 * wide, width), BF16)), (joined, kernel, second),
+        0.02, "split", 1,
+    )
+    other = pair_swap(given, "mp", 2)
     q_second = ring(q_early, 1)
     q_first = ring(q_early, 0)
     sums, tops, totals = kernel_call(
@@ -450,23 +491,25 @@
     )
     att, lse, send, keep = kernel_call(
         functools.partial(project_body, scale),
-        (tile, tile32, tile, tile),
+        (tile, tile32, both, both),
         (q_early, relay, sums, tops, totals, out_weight),
         1.0, "project",
     )
 
+    send, q_own, q_handed = kernel_call(
+        pass_body, (both, tile, tile), (send, q_early, q_second, q_first), 0.1, "pass", 1
+    )
     core = pair_swap(send, "mp", 1)
-    own_send, own_keep = kernel_call(
-        project_own_body, (tile, tile), (att, out_weight, q_second, q_first), 0.4, "project_own", 2
-    )
-    outgoing, q_own = kernel_call(join_body, (tile, tile), (keep, core, q_early), 0.1, "join")
-    across = pair_swap(outgoing, "mp", 2)
-    own_core = pair_swap(own_send, "mp", 1)
+    chip, q_own, q_handed = kernel_call(
+        join_body, (both, tile, tile), (keep, core, q_own, q_handed, other), 0.02, "join", 1
+    )
+    across = pair_swap(chip, "mp", 2)
     q_near = inner_swap(q_own)
+    q_relay = pair_swap(q_handed, "ctx", 1)
     hidden, rim_up, rim_down = kernel_call(
         hidden_body,
-        (tile, rim, rim),
-        (inputs, own_keep, own_core, across, cotangent),
+        (both, rim, rim),
+        (chip, across, inputs, cotangent, other),
         0.2, "hidden",
     )
 
@@ -474,33 +517,21 @@
     rim_near = pair_swap(rim_up, "ctx", 1)
     rows_out, edge_conv, part_grad = kernel_call(
         conv_inner_body,
-        (tile, shaped((2 * wide, width), F32), tile32),
-        (hidden, cotangent, kernel, q_near),
-        1.6, "conv_inner", 1,
-    )
-    output_here, grad_here, q_handed = kernel_call(
+        (tile, shaped((2 * wide, 2 * width), F32), shaped((frames, 2 * width), F32)),
+        (hidden, cotangent, other, kernel, q_near, q_relay),
+        3.1, "conv_inner", 2,
+    )
+    output_here, grad_here = kernel_call(
         conv_edge_body,
-        (tile, tile, tile),
-        (hidden, rim_near, rim_far, cotangent, kernel, rows_out, edge_conv, part_grad, q_second),
-        0.8, "conv_edge",
-    )
-
-    gi_across = pair_swap(grad_here, "mp", 2)
+        (tile, both),
+        (hidden, rim_near, rim_far, cotangent, other, kernel, rows_out, edge_conv, part_grad),
+        1.4, "conv_edge",
+    )
+
     gi_core = pair_swap(grad_here, "mp", 1)
-    q_relay = pair_swap(q_handed, "ctx", 1)
-    (partial,) = kernel_call(
-        upstream_chip_body, (tile32,), (grad_here, gi_core, out_weight), 0.5, "upstream_chip"
-    )
-    (turned,) = kernel_call(hold_body, (tile,), (gi_across, partial), 0.1, "turn", 1)
-    gi_cross = pair_swap(turned, "mp", 1)
-    (partial,) = kernel_call(
-        upstream_across_body, (tile32,), (turned, out_weight, partial), 0.4, "upstream_across"
-    )
+    (partial,) = kernel_call(upstream_own_body, (tile32,), (grad_here, out_weight), 0.5, "upstream_own")
     message, delta = kernel_call(
-        upstream_body,
-        (noted, tile32),
-        (gi_cross, out_weight, att, lse, partial, q_relay),
-        0.5, "upstream", 1,
+        upstream_body, (noted, tile32), (gi_core, out_weight, att, lse, partial), 0.6, "upstream"
     )
 
     m_near, m_first, m_second, m_relay = window_of(message)

time: 54.2 us -> 54.7 us (level)
  Pallas kernels: 8.73 us -> 10.9 us
  starting transfers between devices: 18.7 us -> 16.8 us
  other arithmetic: 1.13 us -> 2.19 us
  waiting for transfers between devices: 23.6 us -> 23 us
    ppermute x10 -> x8, starting transfers between devices: 11.4 us -> 7.91 us  [pair_swap(): lax.ppermute(block, axis, [(i, i ^ bit) for i in range(lax.axis_size(axis...]
    pallas_call x15 -> x13, Pallas kernels: 8.73 us -> 10.9 us  [kernel_call(): pl.pallas_call(body, out_shape=outs, in_specs=[VMEM] * (len(args) - unrea...]
    ppermute x6, starting transfers between devices: 7.36 us -> 8.89 us  [ring(): return lax.ppermute(block, 'ctx', ring_routes(lax.axis_size('ctx'))[way])]
    add x0 -> x1, other arithmetic: none -> 1.06 us  [per_device(): sum((lax.pad(rows, zero, ((k * frames, (2 - k) * frames, 0), (0, 0, 0)))...]
    ppermute x10 -> x8, waiting for transfers between devices: 13.2 us -> 12.1 us  [pair_swap(): lax.ppermute(block, axis, [(i, i ^ bit) for i in range(lax.axis_size(axis...]
  transfers between devices with their start and end apart: 20 -> 18, of which waited for: 10 -> 9; matrix products, arithmetic and copies ran while one was open for 0% -> 2% of each run, Pallas kernels for 12% -> 14%
where the time goes in v7:
time: 54.7 us; the launch traced here: 54.5 us
  waiting for transfers between devices  23 us (42%)
  starting transfers between devices  16.8 us (31%)
  Pallas kernels  10.9 us (20%)
  other arithmetic  2.19 us (4%)
  local copies, waits for them, and re-layouts  0.85 us (2%)
  between operations  0.79 us (1%)
    ppermute x8, waiting for transfers between devices, pair_swap(): lax.ppermute(block, axis, [(i, i ^ bit) for i in range(lax.axis_size(axis...  12.1 us
    pallas_call x13, Pallas kernels, kernel_call(): pl.pallas_call(body, out_shape=outs, in_specs=[VMEM] * (len(args) - unrea...  10.9 us
    ppermute x6, waiting for transfers between devices, ring(): return lax.ppermute(block, 'ctx', ring_routes(lax.axis_size('ctx'))[way])  10.8 us
    ppermute x6, starting transfers between devices, ring(): return lax.ppermute(block, 'ctx', ring_routes(lax.axis_size('ctx'))[way])  8.89 us
    ppermute x8, starting transfers between devices, pair_swap(): lax.ppermute(block, axis, [(i, i ^ bit) for i in range(lax.axis_size(axis...  7.91 us
    add x1, other arithmetic, per_device(): lax.pad(key_rows, zero, ((0, frames, 0), (0, 0, 0)))  1.13 us
  transfers between devices with their start and end apart: 18, of which 9 were waited for; matrix products, arithmetic and copies ran while one was open for 2% of the time, Pallas kernels for 14%

profile of v7, /device:TPU:0, one launch (start us, length us, event | category | flops | bytes accessed | tf_op | source)
XLA Modules:
  0.0 54.5 jit_solution(17224250624711442517)
XLA Ops:
  0.6 0.0 copy-start
  0.6 1.1 %pad_add_fusion.1.own = bf16[256,512]{1,0:T(8,128)(2,1)S(1)} fusion(bf16[128,512]{1,0:T(8,128)(2,1)} %param.9, bf16[128,512]{1,0:T(8,128)(2,1)} %param.8), kind=kLoop, calls=%fused_computation.1 | loop fusion | flops 524288 | bytes 524288 | tf_op jit(solution)/shard_map/add | solution.py:471
  1.8 3.0 %collective-permute-start = (bf16[256,512]{1,0:T(8,128)(2,1)S(1)}, bf16[256,512]{1,0:T(8,128)(2,1)S(1)}, u32[]{:S(2)}, u32[]{:S(2)}) collective-permute-start(bf16[256,512]{1,0:T(8,128)(2,1)S(1)} %pad_add_fusion.1.own), channel_id=1, source_target_pairs={{8,0},{16,8},{24,16},{28,24},{20,28},{12,20},{4,12},{0,4},{9,1},{1... | collective-permute-start | bytes 786440 | tf_op jit(solution)/shard_map/ppermute | solution.py:39
  4.8 0.2 collective-permute-start.3
  4.9 0.0 collective-permute-start.2
  4.9 6.2 %collective-permute-done.seen.second = bf16[256,512]{1,0:T(8,128)(2,1)S(1)} collective-permute-done((bf16[256,512]{1,0:T(8,128)(2,1)S(1)}, bf16[256,512]{1,0:T(8,128)(2,1)S(1)}, u32[]{:S(2)}, u32[]{:S(2)}) %collective-permute-start) | collective-permute-done | bytes 262176 | tf_op jit(solution)/shard_map/ppermute | solution.py:39
  11.2 1.7 %collective-permute-start.1 = (bf16[256,512]{1,0:T(8,128)(2,1)S(1)}, bf16[256,512]{1,0:T(8,128)(2,1)S(1)}, u32[]{:S(2)}, u32[]{:S(2)}) collective-permute-start(bf16[256,512]{1,0:T(8,128)(2,1)S(1)} %collective-permute-done.seen.second), channel_id=1, source_target_pairs={{0,4},{4,0},{8,12},{12,8},{16,20},{20,16},{24,28},{28,24},{1,5},{5... | collective-permute-start | bytes 786440 | tf_op jit(solution)/shard_map/ppermute | solution.py:28
  12.8 1.1 %pad_add_fusion.joined = bf16[384,512]{1,0:T(8,128)(2,1)S(1)} fusion(bf16[128,512]{1,0:T(8,128)(2,1)} %cot.5, bf16[128,512]{1,0:T(8,128)(2,1)} %inputs.1, bf16[128,512]{1,0:T(8,128)(2,1)} %param.7), kind=kLoop, calls=%fused_computation | loop fusion | flops 1179648 | bytes 786432 | tf_op jit(solution)/shard_map/add | solution.py:475
  13.9 0.0 copy-start.2
  13.9 0.8 %copy-done.2 = f32[31,512]{1,0:T(8,128)S(1)} copy-done((f32[31,512]{1,0:T(8,128)S(1)}, f32[31,512]{1,0:T(8,128)}, u32[]{:S(2)}) %copy-start.2) | copy-done | bytes 63512
  14.8 1.6 %collective-permute-start.5 = (bf16[128,512]{1,0:T(8,128)(2,1)S(1)}, bf16[128,512]{1,0:T(8,128)(2,1)S(1)}, u32[]{:S(2)}, u32[]{:S(2)}) collective-permute-start(bf16[128,512]{1,0:T(8,128)(2,1)S(1)} %get-tuple-element.38.q), channel_id=1, source_target_pairs={{0,8},{8,16},{16,24},{24,28},{28,20},{20,12},{12,4},{4,0},{1,9},{9... | collective-permute-start | bytes 393224 | tf_op jit(solution)/shard_map/ppermute | solution.py:39
  16.4 0.4 collective-permute-start.4
  16.8 0.0 collective-permute-done.3.first
  16.8 1.5 %collective-permute-start.7 = (bf16[352,512]{1,0:T(8,128)(2,1)S(1)}, bf16[352,512]{1,0:T(8,128)(2,1)S(1)}, u32[]{:S(2)}, u32[]{:S(2)}) collective-permute-start(bf16[352,512]{1,0:T(8,128)(2,1)S(1)} %get-tuple-element.47), channel_id=1, source_target_pairs={{0,2},{1,3},{2,0},{3,1},{4,6},{5,7},{6,4},{7,5},{8,10},{9,11},{10,... | collective-permute-start | bytes 1081352 | tf_op jit(solution)/shard_map/ppermute | solution.py:28
  18.4 0.0 collective-permute-done.2.near
  18.4 0.6 %forward.1 = (f32[128,512]{1,0:T(8,128)S(1)}, f32[128,512]{1,0:T(8,128)S(1)}, f32[128,512]{1,0:T(8,128)S(1)}) custom-call(bf16[128,512]{1,0:T(8,128)(2,1)S(1)} %get-tuple-element.38.q, bf16[256,512]{1,0:T(8,128)(2,1)S(1)} %pad_add_fusion.1.own, bf16[256,512]{1,0:T(8,128)(2,1)S(1)} %collective-permute-done.2.near, ...), custom_call_target="tpu_custom_call" | custom-call | bytes 3690000 | tf_op jit(solution)/shard_map/forward/pallas_call | solution.py:74
  19.0 1.1 %collective-permute-done.1.relay = bf16[256,512]{1,0:T(8,128)(2,1)S(1)} collective-permute-done((bf16[256,512]{1,0:T(8,128)(2,1)S(1)}, bf16[256,512]{1,0:T(8,128)(2,1)S(1)}, u32[]{:S(2)}, u32[]{:S(2)}) %collective-permute-start.1) | collective-permute-done | bytes 262176 | tf_op jit(solution)/shard_map/ppermute | solution.py:28
  20.1 0.0 copy-done
  20.1 0.0 copy-start.1
  20.1 0.0 copy-start.4
  20.1 0.9 %project.1 = (bf16[128,512]{1,0:T(8,128)(2,1)S(1)}, f32[128,512]{1,0:T(8,128)S(1)}, bf16[128,1024]{1,0:T(8,128)(2,1)S(1)}, bf16[128,1024]{1,0:T(8,128)(2,1)S(1)}) custom-call(bf16[128,512]{1,0:T(8,128)(2,1)S(1)} %get-tuple-element.38.q, bf16[256,512]{1,0:T(8,128)(2,1)S(1)} %collective-permute-done.1.relay, f32[128,512]{1,0:T(8,128)S(1)} %get-tuple-element.39.sums, ...), custom_call_target="tpu_custom_call" | custom-call | bytes 3690000 | tf_op jit(solution)/shard_map/project/pallas_call | solution.py:74
  20.9 0.0 copy-start.3
  20.9 0.5 collective-permute-done.5.seen.refs_2_
  21.5 0.0 collective-permute-done.4.q_second.refs_3_
  21.5 0.1 collective-permute-start.6
  21.6 3.7 %collective-permute-done.7.seen.other = bf16[352,512]{1,0:T(8,128)(2,1)S(1)} collective-permute-done((bf16[352,512]{1,0:T(8,128)(2,1)S(1)}, bf16[352,512]{1,0:T(8,128)(2,1)S(1)}, u32[]{:S(2)}, u32[]{:S(2)}) %collective-permute-start.7) | collective-permute-done | bytes 360480 | tf_op jit(solution)/shard_map/ppermute | solution.py:28
  25.3 0.0 collective-permute-done.6.core
  25.3 0.1 join.1
  25.4 1.6 %collective-permute-start.8 = (bf16[128,1024]{1,0:T(8,128)(2,1)S(1)}, bf16[128,1024]{1,0:T(8,128)(2,1)S(1)}, u32[]{:S(2)}, u32[]{:S(2)}) collective-permute-start(bf16[128,1024]{1,0:T(8,128)(2,1)S(1)} %get-tuple-element.49.chip), channel_id=1, source_target_pairs={{0,2},{1,3},{2,0},{3,1},{4,6},{5,7},{6,4},{7,5},{8,10},{9,11},{10,... | collective-permute-start | bytes 786440 | tf_op jit(solution)/shard_map/ppermute | solution.py:28
  26.9 0.5 collective-permute-start.12
  27.5 0.0 collective-permute-start.11
  27.5 4.3 %collective-permute-done.8.across = bf16[128,1024]{1,0:T(8,128)(2,1)S(1)} collective-permute-done((bf16[128,1024]{1,0:T(8,128)(2,1)S(1)}, bf16[128,1024]{1,0:T(8,128)(2,1)S(1)}, u32[]{:S(2)}, u32[]{:S(2)}) %collective-permute-start.8) | collective-permute-done | bytes 262176 | tf_op jit(solution)/shard_map/ppermute | solution.py:28
  31.8 0.0 copy-done.1
  31.8 0.0 copy-done.4
  31.8 0.1 hidden.1
  31.9 1.2 %collective-permute-start.9 = (bf16[48,1024]{1,0:T(8,128)(2,1)S(1)}, bf16[48,1024]{1,0:T(8,128)(2,1)S(1)}, u32[]{:S(2)}, u32[]{:S(2)}) collective-permute-start(bf16[48,1024]{1,0:T(8,128)(2,1)S(1)} %get-tuple-element.51), channel_id=1, source_target_pairs={{0,4},{4,0},{8,12},{12,8},{16,20},{20,16},{24,28},{28,24},{1,5},{5... | collective-permute-start | bytes 294920 | tf_op jit(solution)/shard_map/ppermute | solution.py:28
  33.1 0.0 collective-permute-start.10
  33.1 0.0 collective-permute-done.12.seen_b.refs_4_.query
  33.1 0.0 collective-permute-done.11.seen_a.refs_1_
  33.1 0.0 copy-done.3
  33.1 3.1 %conv_inner.1 = (bf16[128,512]{1,0:T(8,128)(2,1)S(1)}, f32[64,1024]{1,0:T(8,128)S(1)}, f32[128,1024]{1,0:T(8,128)S(1)}) custom-call(bf16[128,1024]{1,0:T(8,128)(2,1)S(1)} %get-tuple-element.50.hidden, bf16[128,512]{1,0:T(8,128)(2,1)S(1)} %copy-done.1, bf16[352,512]{1,0:T(8,128)(2,1)S(1)} %collective-permute-done.7.seen.other, f32[31,512]{1,0:T(8,128)S(1)} %copy-done.3, ...), custom_call_target="tpu_custom_call" | custom-call | bytes 11439000 | tf_op jit(solution)/shard_map/conv_inner/pallas_call | solution.py:74
  36.3 0.3 collective-permute-done.9.rim_near
  36.6 0.0 collective-permute-done.10.rim_far
  36.6 1.5 %conv_edge.1 = (bf16[128,512]{1,0:T(8,128)(2,1)S(1)}, bf16[128,1024]{1,0:T(8,128)(2,1)S(1)}) custom-call(bf16[128,1024]{1,0:T(8,128)(2,1)S(1)} %get-tuple-element.50.hidden, bf16[48,1024]{1,0:T(8,128)(2,1)S(1)} %collective-permute-done.9.rim_near, bf16[48,1024]{1,0:T(8,128)(2,1)S(1)} %collective-permute-done.10.rim_far, bf16[128,512]{1,0:T(8,128)(2,1)S(1)} %copy-done.1, ...), custom_call_target="tpu_custom_call" | custom-call | bytes 5166000 | tf_op jit(solution)/shard_map/conv_edge/pallas_call | solution.py:74
  38.1 0.3 collective-permute-start.13
  38.4 0.5 upstream_own.1.partial
  38.8 0.9 %collective-permute-done.13.core = bf16[128,1024]{1,0:T(8,128)(2,1)S(1)} collective-permute-done((bf16[128,1024]{1,0:T(8,128)(2,1)S(1)}, bf16[128,1024]{1,0:T(8,128)(2,1)S(1)}, u32[]{:S(2)}, u32[]{:S(2)}) %collective-permute-start.13) | collective-permute-done | bytes 262176 | tf_op jit(solution)/shard_map/ppermute | solution.py:28
  39.7 0.7 %upstream.1 = (bf16[144,512]{1,0:T(8,128)(2,1)S(1)}, f32[128,512]{1,0:T(8,128)S(1)}) custom-call(bf16[128,1024]{1,0:T(8,128)(2,1)S(1)} %collective-permute-done.13.core, bf16[512,2048]{1,0:T(8,128)(2,1)S(1)} %copy-done, bf16[128,512]{1,0:T(8,128)(2,1)S(1)} %get-tuple-element.58.att, f32[128,512]{1,0:T(8,128)S(1)} %get-tuple-element.59.lse, ...), custom_call_target="tpu_custom_call" | custom-call | bytes 2214000 | tf_op jit(solution)/shard_map/upstream/pallas_call | solution.py:74
  40.4 3.0 %collective-permute-start.14 = (bf16[144,512]{1,0:T(8,128)(2,1)S(1)}, bf16[144,512]{1,0:T(8,128)(2,1)S(1)}, u32[]{:S(2)}, u32[]{:S(2)}) collective-permute-start(bf16[144,512]{1,0:T(8,128)(2,1)S(1)} %get-tuple-element.60.message.refs_5_), channel_id=1, source_target_pairs={{8,0},{16,8},{24,16},{28,24},{20,28},{12,20},{4,12},{0,4},{9,1},{1... | collective-permute-start | bytes 442376 | tf_op jit(solution)/shard_map/ppermute | solution.py:39
  43.3 0.7 %collective-permute-start.17 = (bf16[144,512]{1,0:T(8,128)(2,1)S(1)}, bf16[144,512]{1,0:T(8,128)(2,1)S(1)}, u32[]{:S(2)}, u32[]{:S(2)}) collective-permute-start(bf16[144,512]{1,0:T(8,128)(2,1)S(1)} %get-tuple-element.60.message.refs_5_), channel_id=1, source_target_pairs={{0,8},{8,16},{16,24},{24,28},{28,20},{20,12},{12,4},{4,0},{1,9},{9... | collective-permute-start | bytes 442376 | tf_op jit(solution)/shard_map/ppermute | solution.py:39
  44.0 0.0 collective-permute-start.16
  44.0 4.1 %collective-permute-done.14.refs_8_ = bf16[144,512]{1,0:T(8,128)(2,1)S(1)} collective-permute-done((bf16[144,512]{1,0:T(8,128)(2,1)S(1)}, bf16[144,512]{1,0:T(8,128)(2,1)S(1)}, u32[]{:S(2)}, u32[]{:S(2)}) %collective-permute-start.14) | collective-permute-done | bytes 147488 | tf_op jit(solution)/shard_map/ppermute | solution.py:39
  48.1 1.1 %collective-permute-start.15 = (bf16[144,512]{1,0:T(8,128)(2,1)S(1)}, bf16[144,512]{1,0:T(8,128)(2,1)S(1)}, u32[]{:S(2)}, u32[]{:S(2)}) collective-permute-start(bf16[144,512]{1,0:T(8,128)(2,1)S(1)} %collective-permute-done.14.refs_8_), channel_id=1, source_target_pairs={{0,4},{4,0},{8,12},{12,8},{16,20},{20,16},{24,28},{28,24},{1,5},{5... | collective-permute-start | bytes 442376 | tf_op jit(solution)/shard_map/ppermute | solution.py:28
  49.2 1.5 %query_grad.1 = (bf16[128,512]{1,0:T(8,128)(2,1)}, bf16[128,512]{1,0:T(8,128)(2,1)}, bf16[128,512]{1,0:T(8,128)(2,1)}) custom-call(bf16[128,512]{1,0:T(8,128)(2,1)S(1)} %get-tuple-element.48.q.refs_0_, bf16[256,512]{1,0:T(8,128)(2,1)S(1)} %pad_add_fusion.1.own, bf16[256,512]{1,0:T(8,128)(2,1)S(1)} %collective-permute-done.2.near, ...), custom_call_target="tpu_custom_call" | custom-call | bytes 6642000 | tf_op jit(solution)/shard_map/query_grad/pallas_call | solution.py:74
  50.8 0.0 collective-permute-done.17.refs_7_
  50.8 0.0 collective-permute-done.16.refs_6_
  50.8 0.9 %key_part.1 = (f32[128,512]{1,0:T(8,128)S(1)}, f32[128,512]{1,0:T(8,128)S(1)}, f32[128,512]{1,0:T(8,128)S(1)}) custom-call(bf16[256,512]{1,0:T(8,128)(2,1)S(1)} %pad_add_fusion.1.own, bf16[128,512]{1,0:T(8,128)(2,1)S(1)} %get-tuple-element.48.q.refs_0_, bf16[128,512]{1,0:T(8,128)(2,1)S(1)} %collective-permute-done.11.seen_a.refs_1_, ...), custom_call_target="tpu_custom_call" | custom-call | bytes 5535000 | tf_op jit(solution)/shard_map/key_part/pallas_call | solution.py:74
  51.6 1.8 %collective-permute-done.15.message = bf16[144,512]{1,0:T(8,128)(2,1)S(1)} collective-permute-done((bf16[144,512]{1,0:T(8,128)(2,1)S(1)}, bf16[144,512]{1,0:T(8,128)(2,1)S(1)}, u32[]{:S(2)}, u32[]{:S(2)}) %collective-permute-start.15) | collective-permute-done | bytes 147488 | tf_op jit(solution)/shard_map/ppermute | solution.py:28
  53.5 1.0 %key_grad.1 = (bf16[128,512]{1,0:T(8,128)(2,1)}, bf16[128,512]{1,0:T(8,128)(2,1)}) custom-call(bf16[256,512]{1,0:T(8,128)(2,1)S(1)} %pad_add_fusion.1.own, bf16[128,512]{1,0:T(8,128)(2,1)S(1)} %collective-permute-done.12.seen_b.refs_4_.query, bf16[144,512]{1,0:T(8,128)(2,1)S(1)} %collective-permute-done.15.message, f32[128,512]{1,0:T(8,128)S(1)} %get-tuple-element.66.late, ...), custom_call_target="tpu_custom_call" | custom-call | bytes 3690000 | tf_op jit(solution)/shard_map/key_grad/pallas_call | solution.py:74
  (2 shorter events, 0.1 us)
Async XLA Ops:
  0.6 19.4 %copy-start = (bf16[512,2048]{1,0:T(8,128)(2,1)S(1)}, bf16[512,2048]{1,0:T(8,128)(2,1)}, u32[]{:S(2)}) copy-start(bf16[512,2048]{1,0:T(8,128)(2,1)} %weight.5) | copy-start | bytes 6291460
  1.8 9.4 %collective-permute-start = (bf16[256,512]{1,0:T(8,128)(2,1)S(1)}, bf16[256,512]{1,0:T(8,128)(2,1)S(1)}, u32[]{:S(2)}, u32[]{:S(2)}) collective-permute-start(bf16[256,512]{1,0:T(8,128)(2,1)S(1)} %pad_add_fusion.1.own), channel_id=1, source_target_pairs={{8,0},{16,8},{24,16},{28,24},{20,28},{12,20},{4,12},{0,4},{9,1},{1... | collective-permute-start | bytes 786440 | tf_op jit(solution)/shard_map/ppermute | solution.py:39
  4.8 12.1 %collective-permute-start.3 = (bf16[256,512]{1,0:T(8,128)(2,1)S(1)}, bf16[256,512]{1,0:T(8,128)(2,1)S(1)}, u32[]{:S(2)}, u32[]{:S(2)}) collective-permute-start(bf16[256,512]{1,0:T(8,128)(2,1)S(1)} %pad_add_fusion.1.own), channel_id=1, source_target_pairs={{0,8},{8,16},{16,24},{24,28},{28,20},{20,12},{12,4},{4,0},{1,9},{9... | collective-permute-start | bytes 786440 | tf_op jit(solution)/shard_map/ppermute | solution.py:39
  4.9 13.4 %collective-permute-start.2 = (bf16[256,512]{1,0:T(8,128)(2,1)S(1)}, bf16[256,512]{1,0:T(8,128)(2,1)S(1)}, u32[]{:S(2)}, u32[]{:S(2)}) collective-permute-start(bf16[256,512]{1,0:T(8,128)(2,1)S(1)} %pad_add_fusion.1.own), channel_id=1, source_target_pairs={{0,1},{1,0},{2,3},{3,2},{4,5},{5,4},{6,7},{7,6},{8,12},{9,13},{10,... | collective-permute-start | bytes 786440 | tf_op jit(solution)/shard_map/ppermute | solution.py:50
  11.2 8.9 %collective-permute-start.1 = (bf16[256,512]{1,0:T(8,128)(2,1)S(1)}, bf16[256,512]{1,0:T(8,128)(2,1)S(1)}, u32[]{:S(2)}, u32[]{:S(2)}) collective-permute-start(bf16[256,512]{1,0:T(8,128)(2,1)S(1)} %collective-permute-done.seen.second), channel_id=1, source_target_pairs={{0,4},{4,0},{8,12},{12,8},{16,20},{20,16},{24,28},{28,24},{1,5},{5... | collective-permute-start | bytes 786440 | tf_op jit(solution)/shard_map/ppermute | solution.py:28
  13.9 0.8 %copy-start.2 = (f32[31,512]{1,0:T(8,128)S(1)}, f32[31,512]{1,0:T(8,128)}, u32[]{:S(2)}) copy-start(f32[31,512]{1,0:T(8,128)} %taps.5) | copy-start | bytes 190468
  14.8 6.7 %collective-permute-start.5 = (bf16[128,512]{1,0:T(8,128)(2,1)S(1)}, bf16[128,512]{1,0:T(8,128)(2,1)S(1)}, u32[]{:S(2)}, u32[]{:S(2)}) collective-permute-start(bf16[128,512]{1,0:T(8,128)(2,1)S(1)} %get-tuple-element.38.q), channel_id=1, source_target_pairs={{0,8},{8,16},{16,24},{24,28},{28,20},{20,12},{12,4},{4,0},{1,9},{9... | collective-permute-start | bytes 393224 | tf_op jit(solution)/shard_map/ppermute | solution.py:39
  16.4 5.1 %collective-permute-start.4 = (bf16[128,512]{1,0:T(8,128)(2,1)S(1)}, bf16[128,512]{1,0:T(8,128)(2,1)S(1)}, u32[]{:S(2)}, u32[]{:S(2)}) collective-permute-start(bf16[128,512]{1,0:T(8,128)(2,1)S(1)} %get-tuple-element.38.q), channel_id=1, source_target_pairs={{8,0},{16,8},{24,16},{28,24},{20,28},{12,20},{4,12},{0,4},{9,1},{1... | collective-permute-start | bytes 393224 | tf_op jit(solution)/shard_map/ppermute | solution.py:39
  16.8 8.4 %collective-permute-start.7 = (bf16[352,512]{1,0:T(8,128)(2,1)S(1)}, bf16[352,512]{1,0:T(8,128)(2,1)S(1)}, u32[]{:S(2)}, u32[]{:S(2)}) collective-permute-start(bf16[352,512]{1,0:T(8,128)(2,1)S(1)} %get-tuple-element.47), channel_id=1, source_target_pairs={{0,2},{1,3},{2,0},{3,1},{4,6},{5,7},{6,4},{7,5},{8,10},{9,11},{10,... | collective-permute-start | bytes 1081352 | tf_op jit(solution)/shard_map/ppermute | solution.py:28
  20.1 11.7 %copy-start.1 = (bf16[128,512]{1,0:T(8,128)(2,1)S(1)}, bf16[128,512]{1,0:T(8,128)(2,1)}, u32[]{:S(2)}) copy-start(bf16[128,512]{1,0:T(8,128)(2,1)} %cot.5) | copy-start | bytes 393220
  20.1 11.7 %copy-start.4 = (bf16[128,512]{1,0:T(8,128)(2,1)S(1)}, bf16[128,512]{1,0:T(8,128)(2,1)}, u32[]{:S(2)}) copy-start(bf16[128,512]{1,0:T(8,128)(2,1)} %inputs.1) | copy-start | bytes 393220
  20.9 12.2 %copy-start.3 = (f32[31,512]{1,0:T(8,128)S(1)}, f32[31,512]{1,0:T(8,128)}, u32[]{:S(2)}) copy-start(f32[31,512]{1,0:T(8,128)} %taps.5) | copy-start | bytes 190468
  21.5 3.8 %collective-permute-start.6 = (bf16[128,1024]{1,0:T(8,128)(2,1)S(1)}, bf16[128,1024]{1,0:T(8,128)(2,1)S(1)}, u32[]{:S(2)}, u32[]{:S(2)}) collective-permute-start(bf16[128,1024]{1,0:T(8,128)(2,1)S(1)} %get-tuple-element.44), channel_id=1, source_target_pairs={{0,1},{1,0},{2,3},{3,2},{4,5},{5,4},{6,7},{7,6},{8,9},{9,8},{10,11... | collective-permute-start | bytes 786440 | tf_op jit(solution)/shard_map/ppermute | solution.py:28
  25.4 6.4 %collective-permute-start.8 = (bf16[128,1024]{1,0:T(8,128)(2,1)S(1)}, bf16[128,1024]{1,0:T(8,128)(2,1)S(1)}, u32[]{:S(2)}, u32[]{:S(2)}) collective-permute-start(bf16[128,1024]{1,0:T(8,128)(2,1)S(1)} %get-tuple-element.49.chip), channel_id=1, source_target_pairs={{0,2},{1,3},{2,0},{3,1},{4,6},{5,7},{6,4},{7,5},{8,10},{9,11},{10,... | collective-permute-start | bytes 786440 | tf_op jit(solution)/shard_map/ppermute | solution.py:28
  26.9 6.2 %collective-permute-start.12 = (bf16[128,512]{1,0:T(8,128)(2,1)S(1)}, bf16[128,512]{1,0:T(8,128)(2,1)S(1)}, u32[]{:S(2)}, u32[]{:S(2)}) collective-permute-start(bf16[128,512]{1,0:T(8,128)(2,1)S(1)} %get-tuple-element.53), channel_id=1, source_target_pairs={{0,4},{4,0},{8,12},{12,8},{16,20},{20,16},{24,28},{28,24},{1,5},{5... | collective-permute-start | bytes 393224 | tf_op jit(solution)/shard_map/ppermute | solution.py:28
  27.5 5.6 %collective-permute-start.11 = (bf16[128,512]{1,0:T(8,128)(2,1)S(1)}, bf16[128,512]{1,0:T(8,128)(2,1)S(1)}, u32[]{:S(2)}, u32[]{:S(2)}) collective-permute-start(bf16[128,512]{1,0:T(8,128)(2,1)S(1)} %get-tuple-element.48.q.refs_0_), channel_id=1, source_target_pairs={{0,1},{1,0},{2,3},{3,2},{4,5},{5,4},{6,7},{7,6},{8,12},{9,13},{10,... | collective-permute-start | bytes 393224 | tf_op jit(solution)/shard_map/ppermute | solution.py:50
  31.9 4.7 %collective-permute-start.9 = (bf16[48,1024]{1,0:T(8,128)(2,1)S(1)}, bf16[48,1024]{1,0:T(8,128)(2,1)S(1)}, u32[]{:S(2)}, u32[]{:S(2)}) collective-permute-start(bf16[48,1024]{1,0:T(8,128)(2,1)S(1)} %get-tuple-element.51), channel_id=1, source_target_pairs={{0,4},{4,0},{8,12},{12,8},{16,20},{20,16},{24,28},{28,24},{1,5},{5... | collective-permute-start | bytes 294920 | tf_op jit(solution)/shard_map/ppermute | solution.py:28
  33.1 3.5 %collective-permute-start.10 = (bf16[48,1024]{1,0:T(8,128)(2,1)S(1)}, bf16[48,1024]{1,0:T(8,128)(2,1)S(1)}, u32[]{:S(2)}, u32[]{:S(2)}) collective-permute-start(bf16[48,1024]{1,0:T(8,128)(2,1)S(1)} %get-tuple-element.52), channel_id=1, source_target_pairs={{0,1},{1,0},{2,3},{3,2},{4,8},{5,9},{6,10},{7,11},{8,4},{9,5},{10,... | collective-permute-start | bytes 294920 | tf_op jit(solution)/shard_map/ppermute | solution.py:50
  38.1 1.6 %collective-permute-start.13 = (bf16[128,1024]{1,0:T(8,128)(2,1)S(1)}, bf16[128,1024]{1,0:T(8,128)(2,1)S(1)}, u32[]{:S(2)}, u32[]{:S(2)}) collective-permute-start(bf16[128,1024]{1,0:T(8,128)(2,1)S(1)} %get-tuple-element.57.own.grad_here), channel_id=1, source_target_pairs={{0,1},{1,0},{2,3},{3,2},{4,5},{5,4},{6,7},{7,6},{8,9},{9,8},{10,11... | collective-permute-start | bytes 786440 | tf_op jit(solution)/shard_map/ppermute | solution.py:28
  40.4 7.8 %collective-permute-start.14 = (bf16[144,512]{1,0:T(8,128)(2,1)S(1)}, bf16[144,512]{1,0:T(8,128)(2,1)S(1)}, u32[]{:S(2)}, u32[]{:S(2)}) collective-permute-start(bf16[144,512]{1,0:T(8,128)(2,1)S(1)} %get-tuple-element.60.message.refs_5_), channel_id=1, source_target_pairs={{8,0},{16,8},{24,16},{28,24},{20,28},{12,20},{4,12},{0,4},{9,1},{1... | collective-permute-start | bytes 442376 | tf_op jit(solution)/shard_map/ppermute | solution.py:39
  43.3 7.4 %collective-permute-start.17 = (bf16[144,512]{1,0:T(8,128)(2,1)S(1)}, bf16[144,512]{1,0:T(8,128)(2,1)S(1)}, u32[]{:S(2)}, u32[]{:S(2)}) collective-permute-start(bf16[144,512]{1,0:T(8,128)(2,1)S(1)} %get-tuple-element.60.message.refs_5_), channel_id=1, source_target_pairs={{0,8},{8,16},{16,24},{24,28},{28,20},{20,12},{12,4},{4,0},{1,9},{9... | collective-permute-start | bytes 442376 | tf_op jit(solution)/shard_map/ppermute | solution.py:39
  44.0 6.7 %collective-permute-start.16 = (bf16[144,512]{1,0:T(8,128)(2,1)S(1)}, bf16[144,512]{1,0:T(8,128)(2,1)S(1)}, u32[]{:S(2)}, u32[]{:S(2)}) collective-permute-start(bf16[144,512]{1,0:T(8,128)(2,1)S(1)} %get-tuple-element.60.message.refs_5_), channel_id=1, source_target_pairs={{0,1},{1,0},{2,3},{3,2},{4,5},{5,4},{6,7},{7,6},{8,12},{9,13},{10,... | collective-permute-start | bytes 442376 | tf_op jit(solution)/shard_map/ppermute | solution.py:50
  48.1 5.4 %collective-permute-start.15 = (bf16[144,512]{1,0:T(8,128)(2,1)S(1)}, bf16[144,512]{1,0:T(8,128)(2,1)S(1)}, u32[]{:S(2)}, u32[]{:S(2)}) collective-permute-start(bf16[144,512]{1,0:T(8,128)(2,1)S(1)} %collective-permute-done.14.refs_8_), channel_id=1, source_target_pairs={{0,4},{4,0},{8,12},{12,8},{16,20},{20,16},{24,28},{28,24},{1,5},{5... | collective-permute-start | bytes 442376 | tf_op jit(solution)/shard_map/ppermute | solution.py:28

commit v8 on v7

--- a/solution.py
+++ b/solution.py
@@ -58,10 +58,11 @@
     return total_swap(block, lambda i, count: ((i + 1) ^ 1) - 1 if 0 < i < count - 1 else None)
 
 
-def window_of(block):
+def window_of(block, before_relay=lambda second: second):
     second = ring(block, 1)
     first = ring(block, 0)
     near = inner_swap(block)
+    second = before_relay(second)
     return near, first, second, pair_swap(second, "ctx", 1)
 
 
@@ -160,27 +161,18 @@
     return weight[:, pl.ds(pl.multiple_of(at, 128), width)]
 
 
-def split_body(joined, taps, seen, query, given):
-    frames = query.shape[0]
-    query[...] = joined[0:frames, :]
-    given[0 : 2 * frames, :] = joined[frames : 3 * frames, :]
-    rows, at = pad_rows(taps), 2 * frames
-    for k in range(3):
-        term = rows.astype(BF16)
-        rows = rows - term.astype(F32)
-        given[at + k * 2 * HALO : at + (k + 1) * 2 * HALO, :] = term
-
-
-def pad_rows(taps):
-    return jnp.concatenate([taps[...], jnp.zeros((2 * HALO - taps.shape[0], taps.shape[1]), F32)], axis=0)
-
-
-def taps_of(other, frames):
-    rows = other[2 * frames :, :].astype(F32)
-    return rows[0 : 2 * HALO] + rows[2 * HALO : 4 * HALO] + rows[4 * HALO :]
-
-
-def forward_body(scale, q, own, near, first, second, sums, tops, totals):
+def hold_body(block, seen, held):
+    held[...] = block[...]
+
+
+def split_body(joined, seen, *parts):
+    frames = parts[0].shape[0]
+    for k, part in enumerate(parts):
+        part[...] = joined[k * frames : (k + 1) * frames, :]
+
+
+def forward_body(scale, q, own, near, first, second, *refs):
+    sums, tops, totals = refs[-3:]
     frames, width = q.shape
     heads = columns(width)
     blocks = (near, own, first, second)
@@ -220,27 +212,19 @@
         lse[:, c] = part
 
 
-def pass_body(send, q, q_second, seen, send_copy, q_copy, second_copy):
-    send_copy[...] = send[...]
-    q_copy[...] = q[...]
-    second_copy[...] = q_second[...]
-
-
-def join_body(keep, core, q, q_second, seen, chip, q_copy, second_copy):
+def join_body(keep, core, q, chip, q_copy):
     chip[...] = (keep[...].astype(F32) + core[...].astype(F32)).astype(BF16)
     q_copy[...] = q[...]
-    second_copy[...] = q_second[...]
-
-
-def hidden_body(chip, across, inputs, cot, other, hidden, rim_near, rim_far):
+
+
+def hidden_body(chip, across, inputs, cot, inputs_other, cot_other, hidden, rim_near, rim_far):
     frames, width = inputs.shape
     wide = 2 * HALO
     even = is_even()
     mine, its = slice(0, width), slice(width, 2 * width)
-    every = slice(0, frames)
     for cols, back, rows, cots in (
         (mine, its, inputs[...], cot[...]),
-        (its, mine, other[every, :], other[frames : 2 * frames, :]),
+        (its, mine, inputs_other[...], cot_other[...]),
     ):
         mixed = chip[:, cols].astype(F32) + across[:, back].astype(F32)
         total = (rows.astype(F32) + mixed).astype(BF16)
@@ -285,22 +269,21 @@
     return lambda s: taps[count - s : count - s + 1, cols] if 1 <= s <= count else None
 
 
-def conv_chunks(frames, width, cot, other, taps):
-    taps_other = taps_of(other, frames)
+def conv_chunks(width, cot, cot_other, taps, taps_other):
     for k, cols in enumerate(columns(2 * width)):
         own = k * HDIM < width
         local = cols if own else slice(cols.start - width, cols.stop - width)
-        yield own, cols, local, 0 if own else frames, cot if own else other, taps if own else taps_other
-
-
-def conv_inner_body(hidden, cot, other, taps, seen_a, seen_b, rows_out, edge_conv, part_grad):
+        yield own, cols, local, cot if own else cot_other, taps if own else taps_other
+
+
+def conv_inner_body(hidden, cot, cot_other, taps, taps_other, seen_a, seen_b, rows_out, edge_conv, part_grad):
     frames, width = cot.shape
     wide, count = 2 * HALO, taps.shape[0]
     inner = slice(HALO, frames - HALO)
     none = jnp.zeros((wide, HDIM), F32)
-    for own, cols, local, at, cots_of, tap in conv_chunks(frames, width, cot, other, taps):
+    for own, cols, local, cots_of, tap in conv_chunks(width, cot, cot_other, taps, taps_other):
         rows = hidden[:, cols].astype(F32)
-        cots = cots_of[at : at + frames, local].astype(F32)
+        cots = cots_of[:, local].astype(F32)
         conv = shifted_sum(
             jnp.concatenate([none, rows, none], axis=0), taps_forward(tap, count, local), frames + wide
         )
@@ -316,7 +299,8 @@
 
 
 def conv_edge_body(
-    hidden, rim_near, rim_far, cot, other, taps, rows_in, edge_conv, part_grad, output, grad_input,
+    hidden, rim_near, rim_far, cot, cot_other, taps, taps_other, rows_in, edge_conv, part_grad,
+    q_second, output, grad_input, second_copy,
 ):
     frames, width = cot.shape
     wide, count = 2 * HALO, taps.shape[0]
@@ -331,14 +315,14 @@
         beyond = jnp.where(far, rim_far[rows, cols].astype(F32), 0.0)
         return jnp.where(even, beyond, near), jnp.where(even, near, beyond)
 
-    for own, cols, local, at, block, tap in conv_chunks(frames, width, cot, other, taps):
+    for own, cols, local, block, tap in conv_chunks(width, cot, cot_other, taps, taps_other):
         row_low, row_high = sides(rims, cols)
         cot_low, cot_high = sides(cots_of, cols)
         conv = edge_conv[:, cols] + shifted_sum(
             jnp.concatenate([row_low, none, row_high], axis=0), taps_forward(tap, count, local), 2 * wide
         )
-        first = block[at : at + HALO, local].astype(F32)
-        last = block[at + frames - HALO : at + frames, local].astype(F32)
+        first = block[low, local].astype(F32)
+        last = block[high, local].astype(F32)
         cots = jnp.concatenate([cot_low, first, last, cot_high], axis=0)
         silu, grad = silu_parts(conv, cots)
         back = shifted_sum(
@@ -353,6 +337,7 @@
             output[low, cols] = (hidden[low, cols].astype(F32) + silu[HALO:wide]).astype(BF16)
             output[inner, cols] = rows_in[inner, cols]
             output[high, cols] = (hidden[high, cols].astype(F32) + silu[wide : wide + HALO]).astype(BF16)
+    second_copy[...] = q_second[...]
 
 
 def upstream_part(grads, weight, flips):
@@ -367,7 +352,7 @@
     partial[...] = upstream_part(own, weight, (0, 2))
 
 
-def upstream_body(core, weight, att, lse, partial, message, delta):
+def upstream_body(core, weight, att, lse, partial, seen, message, delta):
     frames, width = att.shape
     heads = columns(width)
     up = (partial[...] + upstream_part(core, weight, (1, 3))).astype(BF16)
@@ -471,45 +456,43 @@
     kv = lax.pad(key_rows, zero, ((0, frames, 0), (0, 0, 0))) + lax.pad(
         value_rows, zero, ((frames, 0, 0), (0, 0, 0))
     )
-    near, first, second, relay = window_of(kv)
+    other = [pair_swap(block, "mp", 2) for block in (inputs, cotangent, kernel)]
+    near, first, second, relay = window_of(
+        kv,
+        lambda second: kernel_call(
+            hold_body, (shaped(kv.shape, BF16),), (second, other[0]), 0.1, "turn", 1
+        )[0],
+    )
     joined = sum(
         lax.pad(rows, zero, ((k * frames, (2 - k) * frames, 0), (0, 0, 0)))
         for k, rows in enumerate((query_rows, inputs, cotangent))
     )
-    q_early, given = kernel_call(
-        split_body, (tile, shaped((2 * frames + 3 * wide, width), BF16)), (joined, kernel, second),
-        0.02, "split", 1,
-    )
-    other = pair_swap(given, "mp", 2)
-    q_second = ring(q_early, 1)
-    q_first = ring(q_early, 0)
+    query, inputs, cotangent = kernel_call(
+        split_body, (tile, tile, tile), (joined, second), 0.1, "split", 1
+    )
     sums, tops, totals = kernel_call(
         functools.partial(forward_body, scale),
         (tile32, tile32, tile32),
-        (q_early, kv, near, first, second),
-        1.0, "forward",
+        (query, kv, near, first, second, *other[1:]),
+        1.0, "forward", 2,
     )
     att, lse, send, keep = kernel_call(
         functools.partial(project_body, scale),
         (tile, tile32, both, both),
-        (q_early, relay, sums, tops, totals, out_weight),
+        (query, relay, sums, tops, totals, out_weight),
         1.0, "project",
     )
 
-    send, q_own, q_handed = kernel_call(
-        pass_body, (both, tile, tile), (send, q_early, q_second, q_first), 0.1, "pass", 1
-    )
     core = pair_swap(send, "mp", 1)
-    chip, q_own, q_handed = kernel_call(
-        join_body, (both, tile, tile), (keep, core, q_own, q_handed, other), 0.02, "join", 1
-    )
+    chip, q_own = kernel_call(join_body, (both, tile), (keep, core, query), 0.1, "join")
     across = pair_swap(chip, "mp", 2)
+    q_second = ring(q_own, 1)
+    q_first = ring(q_own, 0)
     q_near = inner_swap(q_own)
-    q_relay = pair_swap(q_handed, "ctx", 1)
     hidden, rim_up, rim_down = kernel_call(
         hidden_body,
         (both, rim, rim),
-        (chip, across, inputs, cotangent, other),
+        (chip, across, inputs, cotangent, *other[0:2]),
         0.2, "hidden",
     )
 
@@ -518,20 +501,23 @@
     rows_out, edge_conv, part_grad = kernel_call(
         conv_inner_body,
         (tile, shaped((2 * wide, 2 * width), F32), shaped((frames, 2 * width), F32)),
-        (hidden, cotangent, other, kernel, q_near, q_relay),
+        (hidden, cotangent, other[1], kernel, other[2], q_near, q_first),
         3.1, "conv_inner", 2,
     )
-    output_here, grad_here = kernel_call(
+    output_here, grad_here, q_handed = kernel_call(
         conv_edge_body,
-        (tile, both),
-        (hidden, rim_near, rim_far, cotangent, other, kernel, rows_out, edge_conv, part_grad),
+        (tile, both, tile),
+        (hidden, rim_near, rim_far, cotangent, other[1], kernel, other[2], rows_out, edge_conv, part_grad)
+        + (q_second,),
         1.4, "conv_edge",
     )
 
     gi_core = pair_swap(grad_here, "mp", 1)
+    q_relay = pair_swap(q_handed, "ctx", 1)
     (partial,) = kernel_call(upstream_own_body, (tile32,), (grad_here, out_weight), 0.5, "upstream_own")
     message, delta = kernel_call(
-        upstream_body, (noted, tile32), (gi_core, out_weight, att, lse, partial), 0.6, "upstream"
+        upstream_body, (noted, tile32), (gi_core, out_weight, att, lse, partial, q_relay), 0.6,
+        "upstream", 1,
     )
 
     m_near, m_first, m_second, m_relay = window_of(message)

time: 54.7 us -> 57.5 us (1.051)
  starting transfers between devices: 16.8 us -> 19.9 us
  local copies, waits for them, and re-layouts: 0.85 us -> 0.01 us
  waiting for transfers between devices: 23 us -> 23.7 us
    ppermute x8 -> x10, waiting for transfers between devices: 12.1 us -> 18.9 us  [pair_swap(): lax.ppermute(block, axis, [(i, i ^ bit) for i in range(lax.axis_size(axis...]
    ppermute x6, waiting for transfers between devices: 10.8 us -> 4.82 us  [ring(): return lax.ppermute(block, 'ctx', ring_routes(lax.axis_size('ctx'))[way])]
    ppermute x8 -> x10, starting transfers between devices: 7.91 us -> 11.5 us  [pair_swap(): lax.ppermute(block, axis, [(i, i ^ bit) for i in range(lax.axis_size(axis...]
    unnamed x10 -> x4, local copies, waits for them, and re-layouts: 0.85 us -> 0.01 us
  transfers between devices with their start and end apart: 18 -> 20, of which waited for: 9 -> 9; matrix products, arithmetic and copies ran while one was open for 2% -> 2% of each run, Pallas kernels for 14% -> 12%
where the time goes in v8:
time: 57.5 us; the launch traced here: 57.3 us
  waiting for transfers between devices  23.7 us (41%)
  starting transfers between devices  19.9 us (35%)
  Pallas kernels  10.8 us (19%)
  other arithmetic  2.19 us (4%)
  between operations  0.82 us (1%)
    ppermute x10, waiting for transfers between devices, pair_swap(): lax.ppermute(block, axis, [(i, i ^ bit) for i in range(lax.axis_size(axis...  18.9 us
    ppermute x10, starting transfers between devices, pair_swap(): lax.ppermute(block, axis, [(i, i ^ bit) for i in range(lax.axis_size(axis...  11.5 us
    pallas_call x13, Pallas kernels, kernel_call(): pl.pallas_call(body, out_shape=outs, in_specs=[VMEM] * (len(args) - unrea...  10.8 us
    ppermute x6, starting transfers between devices, ring(): return lax.ppermute(block, 'ctx', ring_routes(lax.axis_size('ctx'))[way])  8.33 us
    ppermute x6, waiting for transfers between devices, ring(): return lax.ppermute(block, 'ctx', ring_routes(lax.axis_size('ctx'))[way])  4.82 us
  transfers between devices with their start and end apart: 20, of which 9 were waited for; matrix products, arithmetic and copies ran while one was open for 2% of the time, Pallas kernels for 12%

profile of v8, /device:TPU:0, one launch (start us, length us, event | category | flops | bytes accessed | tf_op | source)
XLA Modules:
  0.0 57.3 jit_solution(14259463586010166938)
XLA Ops:
  0.6 0.0 copy-start
  0.6 1.1 %pad_add_fusion.1.own = bf16[256,512]{1,0:T(8,128)(2,1)S(1)} fusion(bf16[128,512]{1,0:T(8,128)(2,1)} %param.9, bf16[128,512]{1,0:T(8,128)(2,1)} %param.8), kind=kLoop, calls=%fused_computation.1 | loop fusion | flops 524288 | bytes 524288 | tf_op jit(solution)/shard_map/add | solution.py:456
  1.8 3.0 %collective-permute-start = (bf16[256,512]{1,0:T(8,128)(2,1)S(1)}, bf16[256,512]{1,0:T(8,128)(2,1)S(1)}, u32[]{:S(2)}, u32[]{:S(2)}) collective-permute-start(bf16[256,512]{1,0:T(8,128)(2,1)S(1)} %pad_add_fusion.1.own), channel_id=1, source_target_pairs={{8,0},{16,8},{24,16},{28,24},{20,28},{12,20},{4,12},{0,4},{9,1},{1... | collective-permute-start | bytes 786440 | tf_op jit(solution)/shard_map/ppermute | solution.py:39
  4.8 1.5 %collective-permute-start.1 = (bf16[128,512]{1,0:T(8,128)(2,1)}, bf16[128,512]{1,0:T(8,128)(2,1)S(1)}, u32[]{:S(2)}, u32[]{:S(2)}) collective-permute-start(bf16[128,512]{1,0:T(8,128)(2,1)} %param.10), channel_id=1, source_target_pairs={{0,2},{1,3},{2,0},{3,1},{4,6},{5,7},{6,4},{7,5},{8,10},{9,11},{10,... | collective-permute-start | bytes 393224 | tf_op jit(solution)/shard_map/ppermute | solution.py:28
  6.3 0.5 collective-permute-start.4
  6.8 0.0 collective-permute-start.3
  6.8 3.1 %collective-permute-done.1.seen.inputs_other = bf16[128,512]{1,0:T(8,128)(2,1)S(1)} collective-permute-done((bf16[128,512]{1,0:T(8,128)(2,1)}, bf16[128,512]{1,0:T(8,128)(2,1)S(1)}, u32[]{:S(2)}, u32[]{:S(2)}) %collective-permute-start.1) | collective-permute-done | bytes 131104 | tf_op jit(solution)/shard_map/ppermute | solution.py:28
  9.9 1.2 %collective-permute-done.block = bf16[256,512]{1,0:T(8,128)(2,1)S(1)} collective-permute-done((bf16[256,512]{1,0:T(8,128)(2,1)S(1)}, bf16[256,512]{1,0:T(8,128)(2,1)S(1)}, u32[]{:S(2)}, u32[]{:S(2)}) %collective-permute-start) | collective-permute-done | bytes 262176 | tf_op jit(solution)/shard_map/ppermute | solution.py:39
  11.2 1.7 %collective-permute-start.2 = (bf16[256,512]{1,0:T(8,128)(2,1)S(1)}, bf16[256,512]{1,0:T(8,128)(2,1)S(1)}, u32[]{:S(2)}, u32[]{:S(2)}) collective-permute-start(bf16[256,512]{1,0:T(8,128)(2,1)S(1)} %turn.1.seen.second), channel_id=1, source_target_pairs={{0,4},{4,0},{8,12},{12,8},{16,20},{20,16},{24,28},{28,24},{1,5},{5... | collective-permute-start | bytes 786440 | tf_op jit(solution)/shard_map/ppermute | solution.py:28
  12.9 1.5 %collective-permute-start.5 = (bf16[128,512]{1,0:T(8,128)(2,1)}, bf16[128,512]{1,0:T(8,128)(2,1)S(1)}, u32[]{:S(2)}, u32[]{:S(2)}) collective-permute-start(bf16[128,512]{1,0:T(8,128)(2,1)} %param.13), channel_id=1, source_target_pairs={{0,2},{1,3},{2,0},{3,1},{4,6},{5,7},{6,4},{7,5},{8,10},{9,11},{10,... | collective-permute-start | bytes 393224 | tf_op jit(solution)/shard_map/ppermute | solution.py:28
  14.4 0.5 collective-permute-start.6
  14.9 1.1 %pad_add_fusion.joined = bf16[384,512]{1,0:T(8,128)(2,1)S(1)} fusion(bf16[128,512]{1,0:T(8,128)(2,1)} %param.13, bf16[128,512]{1,0:T(8,128)(2,1)} %param.10, bf16[128,512]{1,0:T(8,128)(2,1)} %param.7), kind=kLoop, calls=%fused_computation | loop fusion | flops 1179648 | bytes 786432 | tf_op jit(solution)/shard_map/add | solution.py:466
  16.0 2.9 %collective-permute-done.6.refs_1_.taps_other = f32[31,512]{1,0:T(8,128)S(1)} collective-permute-done((f32[31,512]{1,0:T(8,128)}, f32[31,512]{1,0:T(8,128)S(1)}, u32[]{:S(2)}, u32[]{:S(2)}) %collective-permute-start.6) | collective-permute-done | bytes 63520 | tf_op jit(solution)/shard_map/ppermute | solution.py:28
  18.9 0.0 collective-permute-done.5.refs_0_.cot_other
  18.9 0.0 collective-permute-done.4.first
  18.9 0.0 collective-permute-done.3.near
  18.9 0.6 %forward.1 = (f32[128,512]{1,0:T(8,128)S(1)}, f32[128,512]{1,0:T(8,128)S(1)}, f32[128,512]{1,0:T(8,128)S(1)}) custom-call(bf16[128,512]{1,0:T(8,128)(2,1)S(1)} %get-tuple-element.36.q, bf16[256,512]{1,0:T(8,128)(2,1)S(1)} %pad_add_fusion.1.own, bf16[256,512]{1,0:T(8,128)(2,1)S(1)} %collective-permute-done.3.near, ...), custom_call_target="tpu_custom_call" | custom-call | bytes 3690000 | tf_op jit(solution)/shard_map/forward/pallas_call | solution.py:75
  19.5 0.0 collective-permute-done.2.relay
  19.5 0.0 copy-done
  19.5 0.0 copy-start.1
  19.6 0.9 %project.1 = (bf16[128,512]{1,0:T(8,128)(2,1)S(1)}, f32[128,512]{1,0:T(8,128)S(1)}, bf16[128,1024]{1,0:T(8,128)(2,1)S(1)}, bf16[128,1024]{1,0:T(8,128)(2,1)S(1)}) custom-call(bf16[128,512]{1,0:T(8,128)(2,1)S(1)} %get-tuple-element.36.q, bf16[256,512]{1,0:T(8,128)(2,1)S(1)} %collective-permute-done.2.relay, f32[128,512]{1,0:T(8,128)S(1)} %get-tuple-element.37.sums, ...), custom_call_target="tpu_custom_call" | custom-call | bytes 3690000 | tf_op jit(solution)/shard_map/project/pallas_call | solution.py:75
  20.4 0.1 collective-permute-start.7
  20.5 1.5 %collective-permute-done.7.core = bf16[128,1024]{1,0:T(8,128)(2,1)S(1)} collective-permute-done((bf16[128,1024]{1,0:T(8,128)(2,1)S(1)}, bf16[128,1024]{1,0:T(8,128)(2,1)S(1)}, u32[]{:S(2)}, u32[]{:S(2)}) %collective-permute-start.7) | collective-permute-done | bytes 262176 | tf_op jit(solution)/shard_map/ppermute | solution.py:28
  22.0 0.1 join.1
  22.1 1.5 %collective-permute-start.8 = (bf16[128,1024]{1,0:T(8,128)(2,1)S(1)}, bf16[128,1024]{1,0:T(8,128)(2,1)S(1)}, u32[]{:S(2)}, u32[]{:S(2)}) collective-permute-start(bf16[128,1024]{1,0:T(8,128)(2,1)S(1)} %get-tuple-element.43.chip), channel_id=1, source_target_pairs={{0,2},{1,3},{2,0},{3,1},{4,6},{5,7},{6,4},{7,5},{8,10},{9,11},{10,... | collective-permute-start | bytes 786440 | tf_op jit(solution)/shard_map/ppermute | solution.py:28
  23.5 1.6 %collective-permute-start.12 = (bf16[128,512]{1,0:T(8,128)(2,1)S(1)}, bf16[128,512]{1,0:T(8,128)(2,1)S(1)}, u32[]{:S(2)}, u32[]{:S(2)}) collective-permute-start(bf16[128,512]{1,0:T(8,128)(2,1)S(1)} %get-tuple-element.42.q.refs_0_), channel_id=1, source_target_pairs={{0,8},{8,16},{16,24},{24,28},{28,20},{20,12},{12,4},{4,0},{1,9},{9... | collective-permute-start | bytes 393224 | tf_op jit(solution)/shard_map/ppermute | solution.py:39
  25.1 0.0 collective-permute-start.11
  25.1 0.5 collective-permute-start.13
  25.6 4.9 %collective-permute-done.8.across = bf16[128,1024]{1,0:T(8,128)(2,1)S(1)} collective-permute-done((bf16[128,1024]{1,0:T(8,128)(2,1)S(1)}, bf16[128,1024]{1,0:T(8,128)(2,1)S(1)}, u32[]{:S(2)}, u32[]{:S(2)}) %collective-permute-start.8) | collective-permute-done | bytes 262176 | tf_op jit(solution)/shard_map/ppermute | solution.py:28
  30.5 0.1 hidden.1
  30.6 0.6 %collective-permute-start.9 = (bf16[48,1024]{1,0:T(8,128)(2,1)S(1)}, bf16[48,1024]{1,0:T(8,128)(2,1)S(1)}, u32[]{:S(2)}, u32[]{:S(2)}) collective-permute-start(bf16[48,1024]{1,0:T(8,128)(2,1)S(1)} %get-tuple-element.47), channel_id=1, source_target_pairs={{0,4},{4,0},{8,12},{12,8},{16,20},{20,16},{24,28},{28,24},{1,5},{5... | collective-permute-start | bytes 294920 | tf_op jit(solution)/shard_map/ppermute | solution.py:28
  31.2 0.0 collective-permute-start.10
  31.2 0.0 collective-permute-done.12.seen_b.refs_2_
  31.2 0.0 collective-permute-done.11.seen_a.refs_1_
  31.2 0.0 copy-done.1
  31.2 3.1 %conv_inner.1 = (bf16[128,512]{1,0:T(8,128)(2,1)S(1)}, f32[64,1024]{1,0:T(8,128)S(1)}, f32[128,1024]{1,0:T(8,128)S(1)}) custom-call(bf16[128,1024]{1,0:T(8,128)(2,1)S(1)} %get-tuple-element.46.hidden, bf16[128,512]{1,0:T(8,128)(2,1)S(1)} %get-tuple-element.45.cot, bf16[128,512]{1,0:T(8,128)(2,1)S(1)} %collective-permute-done.5.refs_0_.cot_other, ...), custom_call_target="tpu_custom_call" | custom-call | bytes 11439000 | tf_op jit(solution)/shard_map/conv_inner/pallas_call | solution.py:75
  34.3 0.0 collective-permute-done.13.q_second.refs_3_
  34.3 1.0 %collective-permute-done.9.rim_near = bf16[48,1024]{1,0:T(8,128)(2,1)S(1)} collective-permute-done((bf16[48,1024]{1,0:T(8,128)(2,1)S(1)}, bf16[48,1024]{1,0:T(8,128)(2,1)S(1)}, u32[]{:S(2)}, u32[]{:S(2)}) %collective-permute-start.9) | collective-permute-done | bytes 98336 | tf_op jit(solution)/shard_map/ppermute | solution.py:28
  35.3 0.0 collective-permute-done.10.rim_far
  35.3 1.4 %conv_edge.1 = (bf16[128,512]{1,0:T(8,128)(2,1)S(1)}, bf16[128,1024]{1,0:T(8,128)(2,1)S(1)}, bf16[128,512]{1,0:T(8,128)(2,1)S(1)}) custom-call(bf16[128,1024]{1,0:T(8,128)(2,1)S(1)} %get-tuple-element.46.hidden, bf16[48,1024]{1,0:T(8,128)(2,1)S(1)} %collective-permute-done.9.rim_near, bf16[48,1024]{1,0:T(8,128)(2,1)S(1)} %collective-permute-done.10.rim_far, ...), custom_call_target="tpu_custom_call" | custom-call | bytes 5166000 | tf_op jit(solution)/shard_map/conv_edge/pallas_call | solution.py:75
  36.8 0.1 collective-permute-start.14
  36.8 3.2 %collective-permute-start.15 = (bf16[128,512]{1,0:T(8,128)(2,1)S(1)}, bf16[128,512]{1,0:T(8,128)(2,1)S(1)}, u32[]{:S(2)}, u32[]{:S(2)}) collective-permute-start(bf16[128,512]{1,0:T(8,128)(2,1)S(1)} %get-tuple-element.55), channel_id=1, source_target_pairs={{0,4},{4,0},{8,12},{12,8},{16,20},{20,16},{24,28},{28,24},{1,5},{5... | collective-permute-start | bytes 393224 | tf_op jit(solution)/shard_map/ppermute | solution.py:28
  40.0 0.5 upstream_own.1.partial
  40.5 3.6 %collective-permute-done.15.seen.refs_4_.query = bf16[128,512]{1,0:T(8,128)(2,1)S(1)} collective-permute-done((bf16[128,512]{1,0:T(8,128)(2,1)S(1)}, bf16[128,512]{1,0:T(8,128)(2,1)S(1)}, u32[]{:S(2)}, u32[]{:S(2)}) %collective-permute-start.15) | collective-permute-done | bytes 131104 | tf_op jit(solution)/shard_map/ppermute | solution.py:28
  44.1 0.0 collective-permute-done.14.core
  44.1 0.7 %upstream.1 = (bf16[144,512]{1,0:T(8,128)(2,1)S(1)}, f32[128,512]{1,0:T(8,128)S(1)}) custom-call(bf16[128,1024]{1,0:T(8,128)(2,1)S(1)} %collective-permute-done.14.core, bf16[512,2048]{1,0:T(8,128)(2,1)S(1)} %copy-done, bf16[128,512]{1,0:T(8,128)(2,1)S(1)} %get-tuple-element.53.att, f32[128,512]{1,0:T(8,128)S(1)} %get-tuple-element.54.lse, ...), custom_call_target="tpu_custom_call" | custom-call | bytes 2214000 | tf_op jit(solution)/shard_map/upstream/pallas_call | solution.py:75
  44.8 1.8 %collective-permute-start.16 = (bf16[144,512]{1,0:T(8,128)(2,1)S(1)}, bf16[144,512]{1,0:T(8,128)(2,1)S(1)}, u32[]{:S(2)}, u32[]{:S(2)}) collective-permute-start(bf16[144,512]{1,0:T(8,128)(2,1)S(1)} %get-tuple-element.56.message.refs_5_), channel_id=1, source_target_pairs={{8,0},{16,8},{24,16},{28,24},{20,28},{12,20},{4,12},{0,4},{9,1},{1... | collective-permute-start | bytes 442376 | tf_op jit(solution)/shard_map/ppermute | solution.py:39
  46.6 1.0 %collective-permute-start.19 = (bf16[144,512]{1,0:T(8,128)(2,1)S(1)}, bf16[144,512]{1,0:T(8,128)(2,1)S(1)}, u32[]{:S(2)}, u32[]{:S(2)}) collective-permute-start(bf16[144,512]{1,0:T(8,128)(2,1)S(1)} %get-tuple-element.56.message.refs_5_), channel_id=1, source_target_pairs={{0,8},{8,16},{16,24},{24,28},{28,20},{20,12},{12,4},{4,0},{1,9},{9... | collective-permute-start | bytes 442376 | tf_op jit(solution)/shard_map/ppermute | solution.py:39
  47.6 0.0 collective-permute-start.18
  47.6 3.6 %collective-permute-done.16.refs_8_ = bf16[144,512]{1,0:T(8,128)(2,1)S(1)} collective-permute-done((bf16[144,512]{1,0:T(8,128)(2,1)S(1)}, bf16[144,512]{1,0:T(8,128)(2,1)S(1)}, u32[]{:S(2)}, u32[]{:S(2)}) %collective-permute-start.16) | collective-permute-done | bytes 147488 | tf_op jit(solution)/shard_map/ppermute | solution.py:39
  51.2 0.8 %collective-permute-start.17 = (bf16[144,512]{1,0:T(8,128)(2,1)S(1)}, bf16[144,512]{1,0:T(8,128)(2,1)S(1)}, u32[]{:S(2)}, u32[]{:S(2)}) collective-permute-start(bf16[144,512]{1,0:T(8,128)(2,1)S(1)} %collective-permute-done.16.refs_8_), channel_id=1, source_target_pairs={{0,4},{4,0},{8,12},{12,8},{16,20},{20,16},{24,28},{28,24},{1,5},{5... | collective-permute-start | bytes 442376 | tf_op jit(solution)/shard_map/ppermute | solution.py:28
  52.0 1.5 %query_grad.1 = (bf16[128,512]{1,0:T(8,128)(2,1)}, bf16[128,512]{1,0:T(8,128)(2,1)}, bf16[128,512]{1,0:T(8,128)(2,1)}) custom-call(bf16[128,512]{1,0:T(8,128)(2,1)S(1)} %get-tuple-element.42.q.refs_0_, bf16[256,512]{1,0:T(8,128)(2,1)S(1)} %pad_add_fusion.1.own, bf16[256,512]{1,0:T(8,128)(2,1)S(1)} %collective-permute-done.3.near, ...), custom_call_target="tpu_custom_call" | custom-call | bytes 6642000 | tf_op jit(solution)/shard_map/query_grad/pallas_call | solution.py:75
  53.6 0.0 collective-permute-done.19.refs_7_
  53.6 0.0 collective-permute-done.18.refs_6_
  53.6 0.9 %key_part.1 = (f32[128,512]{1,0:T(8,128)S(1)}, f32[128,512]{1,0:T(8,128)S(1)}, f32[128,512]{1,0:T(8,128)S(1)}) custom-call(bf16[256,512]{1,0:T(8,128)(2,1)S(1)} %pad_add_fusion.1.own, bf16[128,512]{1,0:T(8,128)(2,1)S(1)} %get-tuple-element.42.q.refs_0_, bf16[128,512]{1,0:T(8,128)(2,1)S(1)} %collective-permute-done.11.seen_a.refs_1_, ...), custom_call_target="tpu_custom_call" | custom-call | bytes 5535000 | tf_op jit(solution)/shard_map/key_part/pallas_call | solution.py:75
  54.5 1.9 %collective-permute-done.17.message = bf16[144,512]{1,0:T(8,128)(2,1)S(1)} collective-permute-done((bf16[144,512]{1,0:T(8,128)(2,1)S(1)}, bf16[144,512]{1,0:T(8,128)(2,1)S(1)}, u32[]{:S(2)}, u32[]{:S(2)}) %collective-permute-start.17) | collective-permute-done | bytes 147488 | tf_op jit(solution)/shard_map/ppermute | solution.py:28
  56.3 1.0 %key_grad.1 = (bf16[128,512]{1,0:T(8,128)(2,1)}, bf16[128,512]{1,0:T(8,128)(2,1)}) custom-call(bf16[256,512]{1,0:T(8,128)(2,1)S(1)} %pad_add_fusion.1.own, bf16[128,512]{1,0:T(8,128)(2,1)S(1)} %collective-permute-done.15.seen.refs_4_.query, bf16[144,512]{1,0:T(8,128)(2,1)S(1)} %collective-permute-done.17.message, f32[128,512]{1,0:T(8,128)S(1)} %get-tuple-element.62.late, ...), custom_call_target="tpu_custom_call" | custom-call | bytes 3690000 | tf_op jit(solution)/shard_map/key_grad/pallas_call | solution.py:75
  (2 shorter events, 0.0 us)
Async XLA Ops:
  0.6 18.9 %copy-start = (bf16[512,2048]{1,0:T(8,128)(2,1)S(1)}, bf16[512,2048]{1,0:T(8,128)(2,1)}, u32[]{:S(2)}) copy-start(bf16[512,2048]{1,0:T(8,128)(2,1)} %weight.5) | copy-start | bytes 6291460
  1.8 9.4 %collective-permute-start = (bf16[256,512]{1,0:T(8,128)(2,1)S(1)}, bf16[256,512]{1,0:T(8,128)(2,1)S(1)}, u32[]{:S(2)}, u32[]{:S(2)}) collective-permute-start(bf16[256,512]{1,0:T(8,128)(2,1)S(1)} %pad_add_fusion.1.own), channel_id=1, source_target_pairs={{8,0},{16,8},{24,16},{28,24},{20,28},{12,20},{4,12},{0,4},{9,1},{1... | collective-permute-start | bytes 786440 | tf_op jit(solution)/shard_map/ppermute | solution.py:39
  4.8 5.2 %collective-permute-start.1 = (bf16[128,512]{1,0:T(8,128)(2,1)}, bf16[128,512]{1,0:T(8,128)(2,1)S(1)}, u32[]{:S(2)}, u32[]{:S(2)}) collective-permute-start(bf16[128,512]{1,0:T(8,128)(2,1)} %param.10), channel_id=1, source_target_pairs={{0,2},{1,3},{2,0},{3,1},{4,6},{5,7},{6,4},{7,5},{8,10},{9,11},{10,... | collective-permute-start | bytes 393224 | tf_op jit(solution)/shard_map/ppermute | solution.py:28
  6.3 12.6 %collective-permute-start.4 = (bf16[256,512]{1,0:T(8,128)(2,1)S(1)}, bf16[256,512]{1,0:T(8,128)(2,1)S(1)}, u32[]{:S(2)}, u32[]{:S(2)}) collective-permute-start(bf16[256,512]{1,0:T(8,128)(2,1)S(1)} %pad_add_fusion.1.own), channel_id=1, source_target_pairs={{0,8},{8,16},{16,24},{24,28},{28,20},{20,12},{12,4},{4,0},{1,9},{9... | collective-permute-start | bytes 786440 | tf_op jit(solution)/shard_map/ppermute | solution.py:39
  6.8 12.1 %collective-permute-start.3 = (bf16[256,512]{1,0:T(8,128)(2,1)S(1)}, bf16[256,512]{1,0:T(8,128)(2,1)S(1)}, u32[]{:S(2)}, u32[]{:S(2)}) collective-permute-start(bf16[256,512]{1,0:T(8,128)(2,1)S(1)} %pad_add_fusion.1.own), channel_id=1, source_target_pairs={{0,1},{1,0},{2,3},{3,2},{4,5},{5,4},{6,7},{7,6},{8,12},{9,13},{10,... | collective-permute-start | bytes 786440 | tf_op jit(solution)/shard_map/ppermute | solution.py:50
  11.2 8.3 %collective-permute-start.2 = (bf16[256,512]{1,0:T(8,128)(2,1)S(1)}, bf16[256,512]{1,0:T(8,128)(2,1)S(1)}, u32[]{:S(2)}, u32[]{:S(2)}) collective-permute-start(bf16[256,512]{1,0:T(8,128)(2,1)S(1)} %turn.1.seen.second), channel_id=1, source_target_pairs={{0,4},{4,0},{8,12},{12,8},{16,20},{20,16},{24,28},{28,24},{1,5},{5... | collective-permute-start | bytes 786440 | tf_op jit(solution)/shard_map/ppermute | solution.py:28
  12.9 6.0 %collective-permute-start.5 = (bf16[128,512]{1,0:T(8,128)(2,1)}, bf16[128,512]{1,0:T(8,128)(2,1)S(1)}, u32[]{:S(2)}, u32[]{:S(2)}) collective-permute-start(bf16[128,512]{1,0:T(8,128)(2,1)} %param.13), channel_id=1, source_target_pairs={{0,2},{1,3},{2,0},{3,1},{4,6},{5,7},{6,4},{7,5},{8,10},{9,11},{10,... | collective-permute-start | bytes 393224 | tf_op jit(solution)/shard_map/ppermute | solution.py:28
  14.4 4.5 %collective-permute-start.6 = (f32[31,512]{1,0:T(8,128)}, f32[31,512]{1,0:T(8,128)S(1)}, u32[]{:S(2)}, u32[]{:S(2)}) collective-permute-start(f32[31,512]{1,0:T(8,128)} %taps.3), channel_id=1, source_target_pairs={{0,2},{1,3},{2,0},{3,1},{4,6},{5,7},{6,4},{7,5},{8,10},{9,11},{10,... | collective-permute-start | bytes 190472 | tf_op jit(solution)/shard_map/ppermute | solution.py:28
  19.5 11.7 %copy-start.1 = (f32[31,512]{1,0:T(8,128)S(1)}, f32[31,512]{1,0:T(8,128)}, u32[]{:S(2)}) copy-start(f32[31,512]{1,0:T(8,128)} %taps.3) | copy-start | bytes 190468
  20.4 1.6 %collective-permute-start.7 = (bf16[128,1024]{1,0:T(8,128)(2,1)S(1)}, bf16[128,1024]{1,0:T(8,128)(2,1)S(1)}, u32[]{:S(2)}, u32[]{:S(2)}) collective-permute-start(bf16[128,1024]{1,0:T(8,128)(2,1)S(1)} %get-tuple-element.41), channel_id=1, source_target_pairs={{0,1},{1,0},{2,3},{3,2},{4,5},{5,4},{6,7},{7,6},{8,9},{9,8},{10,11... | collective-permute-start | bytes 786440 | tf_op jit(solution)/shard_map/ppermute | solution.py:28
  22.1 8.4 %collective-permute-start.8 = (bf16[128,1024]{1,0:T(8,128)(2,1)S(1)}, bf16[128,1024]{1,0:T(8,128)(2,1)S(1)}, u32[]{:S(2)}, u32[]{:S(2)}) collective-permute-start(bf16[128,1024]{1,0:T(8,128)(2,1)S(1)} %get-tuple-element.43.chip), channel_id=1, source_target_pairs={{0,2},{1,3},{2,0},{3,1},{4,6},{5,7},{6,4},{7,5},{8,10},{9,11},{10,... | collective-permute-start | bytes 786440 | tf_op jit(solution)/shard_map/ppermute | solution.py:28
  23.5 7.7 %collective-permute-start.12 = (bf16[128,512]{1,0:T(8,128)(2,1)S(1)}, bf16[128,512]{1,0:T(8,128)(2,1)S(1)}, u32[]{:S(2)}, u32[]{:S(2)}) collective-permute-start(bf16[128,512]{1,0:T(8,128)(2,1)S(1)} %get-tuple-element.42.q.refs_0_), channel_id=1, source_target_pairs={{0,8},{8,16},{16,24},{24,28},{28,20},{20,12},{12,4},{4,0},{1,9},{9... | collective-permute-start | bytes 393224 | tf_op jit(solution)/shard_map/ppermute | solution.py:39
  25.1 6.1 %collective-permute-start.11 = (bf16[128,512]{1,0:T(8,128)(2,1)S(1)}, bf16[128,512]{1,0:T(8,128)(2,1)S(1)}, u32[]{:S(2)}, u32[]{:S(2)}) collective-permute-start(bf16[128,512]{1,0:T(8,128)(2,1)S(1)} %get-tuple-element.42.q.refs_0_), channel_id=1, source_target_pairs={{0,1},{1,0},{2,3},{3,2},{4,5},{5,4},{6,7},{7,6},{8,12},{9,13},{10,... | collective-permute-start | bytes 393224 | tf_op jit(solution)/shard_map/ppermute | solution.py:50
  25.1 9.2 %collective-permute-start.13 = (bf16[128,512]{1,0:T(8,128)(2,1)S(1)}, bf16[128,512]{1,0:T(8,128)(2,1)S(1)}, u32[]{:S(2)}, u32[]{:S(2)}) collective-permute-start(bf16[128,512]{1,0:T(8,128)(2,1)S(1)} %get-tuple-element.42.q.refs_0_), channel_id=1, source_target_pairs={{8,0},{16,8},{24,16},{28,24},{20,28},{12,20},{4,12},{0,4},{9,1},{1... | collective-permute-start | bytes 393224 | tf_op jit(solution)/shard_map/ppermute | solution.py:39
  30.6 4.7 %collective-permute-start.9 = (bf16[48,1024]{1,0:T(8,128)(2,1)S(1)}, bf16[48,1024]{1,0:T(8,128)(2,1)S(1)}, u32[]{:S(2)}, u32[]{:S(2)}) collective-permute-start(bf16[48,1024]{1,0:T(8,128)(2,1)S(1)} %get-tuple-element.47), channel_id=1, source_target_pairs={{0,4},{4,0},{8,12},{12,8},{16,20},{20,16},{24,28},{28,24},{1,5},{5... | collective-permute-start | bytes 294920 | tf_op jit(solution)/shard_map/ppermute | solution.py:28
  31.2 4.1 %collective-permute-start.10 = (bf16[48,1024]{1,0:T(8,128)(2,1)S(1)}, bf16[48,1024]{1,0:T(8,128)(2,1)S(1)}, u32[]{:S(2)}, u32[]{:S(2)}) collective-permute-start(bf16[48,1024]{1,0:T(8,128)(2,1)S(1)} %get-tuple-element.48), channel_id=1, source_target_pairs={{0,1},{1,0},{2,3},{3,2},{4,8},{5,9},{6,10},{7,11},{8,4},{9,5},{10,... | collective-permute-start | bytes 294920 | tf_op jit(solution)/shard_map/ppermute | solution.py:50
  36.8 7.4 %collective-permute-start.14 = (bf16[128,1024]{1,0:T(8,128)(2,1)S(1)}, bf16[128,1024]{1,0:T(8,128)(2,1)S(1)}, u32[]{:S(2)}, u32[]{:S(2)}) collective-permute-start(bf16[128,1024]{1,0:T(8,128)(2,1)S(1)} %get-tuple-element.52.own.grad_here), channel_id=1, source_target_pairs={{0,1},{1,0},{2,3},{3,2},{4,5},{5,4},{6,7},{7,6},{8,9},{9,8},{10,11... | collective-permute-start | bytes 786440 | tf_op jit(solution)/shard_map/ppermute | solution.py:28
  36.8 7.3 %collective-permute-start.15 = (bf16[128,512]{1,0:T(8,128)(2,1)S(1)}, bf16[128,512]{1,0:T(8,128)(2,1)S(1)}, u32[]{:S(2)}, u32[]{:S(2)}) collective-permute-start(bf16[128,512]{1,0:T(8,128)(2,1)S(1)} %get-tuple-element.55), channel_id=1, source_target_pairs={{0,4},{4,0},{8,12},{12,8},{16,20},{20,16},{24,28},{28,24},{1,5},{5... | collective-permute-start | bytes 393224 | tf_op jit(solution)/shard_map/ppermute | solution.py:28
  44.8 6.4 %collective-permute-start.16 = (bf16[144,512]{1,0:T(8,128)(2,1)S(1)}, bf16[144,512]{1,0:T(8,128)(2,1)S(1)}, u32[]{:S(2)}, u32[]{:S(2)}) collective-permute-start(bf16[144,512]{1,0:T(8,128)(2,1)S(1)} %get-tuple-element.56.message.refs_5_), channel_id=1, source_target_pairs={{8,0},{16,8},{24,16},{28,24},{20,28},{12,20},{4,12},{0,4},{9,1},{1... | collective-permute-start | bytes 442376 | tf_op jit(solution)/shard_map/ppermute | solution.py:39
  46.6 7.0 %collective-permute-start.19 = (bf16[144,512]{1,0:T(8,128)(2,1)S(1)}, bf16[144,512]{1,0:T(8,128)(2,1)S(1)}, u32[]{:S(2)}, u32[]{:S(2)}) collective-permute-start(bf16[144,512]{1,0:T(8,128)(2,1)S(1)} %get-tuple-element.56.message.refs_5_), channel_id=1, source_target_pairs={{0,8},{8,16},{16,24},{24,28},{28,20},{20,12},{12,4},{4,0},{1,9},{9... | collective-permute-start | bytes 442376 | tf_op jit(solution)/shard_map/ppermute | solution.py:39
  47.6 6.0 %collective-permute-start.18 = (bf16[144,512]{1,0:T(8,128)(2,1)S(1)}, bf16[144,512]{1,0:T(8,128)(2,1)S(1)}, u32[]{:S(2)}, u32[]{:S(2)}) collective-permute-start(bf16[144,512]{1,0:T(8,128)(2,1)S(1)} %get-tuple-element.56.message.refs_5_), channel_id=1, source_target_pairs={{0,1},{1,0},{2,3},{3,2},{4,5},{5,4},{6,7},{7,6},{8,12},{9,13},{10,... | collective-permute-start | bytes 442376 | tf_op jit(solution)/shard_map/ppermute | solution.py:50
  51.2 5.1 %collective-permute-start.17 = (bf16[144,512]{1,0:T(8,128)(2,1)S(1)}, bf16[144,512]{1,0:T(8,128)(2,1)S(1)}, u32[]{:S(2)}, u32[]{:S(2)}) collective-permute-start(bf16[144,512]{1,0:T(8,128)(2,1)S(1)} %collective-permute-done.16.refs_8_), channel_id=1, source_target_pairs={{0,4},{4,0},{8,12},{12,8},{16,20},{20,16},{24,28},{28,24},{1,5},{5... | collective-permute-start | bytes 442376 | tf_op jit(solution)/shard_map/ppermute | solution.py:28

commit v9 on v8

--- a/solution.py
+++ b/solution.py
@@ -161,7 +161,7 @@
     return weight[:, pl.ds(pl.multiple_of(at, 128), width)]
 
 
-def hold_body(block, seen, held):
+def hold_body(block, seen_a, seen_b, held):
     held[...] = block[...]
 
 
@@ -300,7 +300,7 @@
 
 def conv_edge_body(
     hidden, rim_near, rim_far, cot, cot_other, taps, taps_other, rows_in, edge_conv, part_grad,
-    q_second, output, grad_input, second_copy,
+    seen, output, grad_input,
 ):
     frames, width = cot.shape
     wide, count = 2 * HALO, taps.shape[0]
@@ -337,7 +337,6 @@
             output[low, cols] = (hidden[low, cols].astype(F32) + silu[HALO:wide]).astype(BF16)
             output[inner, cols] = rows_in[inner, cols]
             output[high, cols] = (hidden[high, cols].astype(F32) + silu[wide : wide + HALO]).astype(BF16)
-    second_copy[...] = q_second[...]
 
 
 def upstream_part(grads, weight, flips):
@@ -352,7 +351,7 @@
     partial[...] = upstream_part(own, weight, (0, 2))
 
 
-def upstream_body(core, weight, att, lse, partial, seen, message, delta):
+def upstream_body(core, weight, att, lse, partial, message, delta):
     frames, width = att.shape
     heads = columns(width)
     up = (partial[...] + upstream_part(core, weight, (1, 3))).astype(BF16)
@@ -460,7 +459,7 @@
     near, first, second, relay = window_of(
         kv,
         lambda second: kernel_call(
-            hold_body, (shaped(kv.shape, BF16),), (second, other[0]), 0.1, "turn", 1
+            hold_body, (shaped(kv.shape, BF16),), (second, other[0], other[2]), 0.1, "turn", 2
         )[0],
     )
     joined = sum(
@@ -473,8 +472,8 @@
     sums, tops, totals = kernel_call(
         functools.partial(forward_body, scale),
         (tile32, tile32, tile32),
-        (query, kv, near, first, second, *other[1:]),
-        1.0, "forward", 2,
+        (query, kv, near, first, second, other[1]),
+        1.0, "forward", 1,
     )
     att, lse, send, keep = kernel_call(
         functools.partial(project_body, scale),
@@ -489,6 +488,7 @@
     q_second = ring(q_own, 1)
     q_first = ring(q_own, 0)
     q_near = inner_swap(q_own)
+    q_relay = pair_swap(q_second, "ctx", 1)
     hidden, rim_up, rim_down = kernel_call(
         hidden_body,
         (both, rim, rim),
@@ -504,20 +504,18 @@
         (hidden, cotangent, other[1], kernel, other[2], q_near, q_first),
         3.1, "conv_inner", 2,
     )
-    output_here, grad_here, q_handed = kernel_call(
+    output_here, grad_here = kernel_call(
         conv_edge_body,
-        (tile, both, tile),
+        (tile, both),
         (hidden, rim_near, rim_far, cotangent, other[1], kernel, other[2], rows_out, edge_conv, part_grad)
-        + (q_second,),
-        1.4, "conv_edge",
+        + (q_relay,),
+        1.4, "conv_edge", 1,
     )
 
     gi_core = pair_swap(grad_here, "mp", 1)
-    q_relay = pair_swap(q_handed, "ctx", 1)
     (partial,) = kernel_call(upstream_own_body, (tile32,), (grad_here, out_weight), 0.5, "upstream_own")
     message, delta = kernel_call(
-        upstream_body, (noted, tile32), (gi_core, out_weight, att, lse, partial, q_relay), 0.6,
-        "upstream", 1,
+        upstream_body, (noted, tile32), (gi_core, out_weight, att, lse, partial), 0.6, "upstream"
     )
 
     m_near, m_first, m_second, m_relay = window_of(message)

time: 57.5 us -> 54.5 us (0.948)
  starting transfers between devices: 19.9 us -> 18.1 us
  waiting for transfers between devices: 23.7 us -> 22.5 us
    ppermute x10, waiting for transfers between devices: 18.9 us -> 15.1 us  [pair_swap(): lax.ppermute(block, axis, [(i, i ^ bit) for i in range(lax.axis_size(axis...]
    ppermute x6, waiting for transfers between devices: 4.82 us -> 7.4 us  [ring(): return lax.ppermute(block, 'ctx', ring_routes(lax.axis_size('ctx'))[way])]
    ppermute x10, starting transfers between devices: 11.5 us -> 9.02 us  [pair_swap(): lax.ppermute(block, axis, [(i, i ^ bit) for i in range(lax.axis_size(axis...]
    ppermute x6, starting transfers between devices: 8.33 us -> 9.02 us  [ring(): return lax.ppermute(block, 'ctx', ring_routes(lax.axis_size('ctx'))[way])]
  transfers between devices with their start and end apart: 20 -> 20, of which waited for: 9 -> 11; matrix products, arithmetic and copies ran while one was open for 2% -> 2% of each run, Pallas kernels for 12% -> 12%
where the time goes in v9:
time: 54.5 us; the launch traced here: 54.3 us
  waiting for transfers between devices  22.5 us (41%)
  starting transfers between devices  18.1 us (33%)
  Pallas kernels  10.8 us (20%)
  other arithmetic  2.19 us (4%)
  between operations  0.78 us (1%)
    ppermute x10, waiting for transfers between devices, pair_swap(): lax.ppermute(block, axis, [(i, i ^ bit) for i in range(lax.axis_size(axis...  15.1 us
    pallas_call x13, Pallas kernels, kernel_call(): pl.pallas_call(body, out_shape=outs, in_specs=[VMEM] * (len(args) - unrea...  10.8 us
    ppermute x6, starting transfers between devices, ring(): return lax.ppermute(block, 'ctx', ring_routes(lax.axis_size('ctx'))[way])  9.02 us
    ppermute x10, starting transfers between devices, pair_swap(): lax.ppermute(block, axis, [(i, i ^ bit) for i in range(lax.axis_size(axis...  9.02 us
    ppermute x6, waiting for transfers between devices, ring(): return lax.ppermute(block, 'ctx', ring_routes(lax.axis_size('ctx'))[way])  7.4 us
    add x1, other arithmetic, per_device(): lax.pad(key_rows, zero, ((0, frames, 0), (0, 0, 0)))  1.13 us
  transfers between devices with their start and end apart: 20, of which 11 were waited for; matrix products, arithmetic and copies ran while one was open for 2% of the time, Pallas kernels for 12%

profile of v9, /device:TPU:0, one launch (start us, length us, event | category | flops | bytes accessed | tf_op | source)
XLA Modules:
  0.0 54.3 jit_solution(55061022329258483)
XLA Ops:
  0.6 0.0 copy-start
  0.6 1.1 %pad_add_fusion.1.own = bf16[256,512]{1,0:T(8,128)(2,1)S(1)} fusion(bf16[128,512]{1,0:T(8,128)(2,1)} %param.9, bf16[128,512]{1,0:T(8,128)(2,1)} %param.8), kind=kLoop, calls=%fused_computation.1 | loop fusion | flops 524288 | bytes 524288 | tf_op jit(solution)/shard_map/add | solution.py:455
  1.8 3.0 %collective-permute-start = (bf16[256,512]{1,0:T(8,128)(2,1)S(1)}, bf16[256,512]{1,0:T(8,128)(2,1)S(1)}, u32[]{:S(2)}, u32[]{:S(2)}) collective-permute-start(bf16[256,512]{1,0:T(8,128)(2,1)S(1)} %pad_add_fusion.1.own), channel_id=1, source_target_pairs={{8,0},{16,8},{24,16},{28,24},{20,28},{12,20},{4,12},{0,4},{9,1},{1... | collective-permute-start | bytes 786440 | tf_op jit(solution)/shard_map/ppermute | solution.py:39
  4.8 1.5 %collective-permute-start.1 = (bf16[128,512]{1,0:T(8,128)(2,1)}, bf16[128,512]{1,0:T(8,128)(2,1)S(1)}, u32[]{:S(2)}, u32[]{:S(2)}) collective-permute-start(bf16[128,512]{1,0:T(8,128)(2,1)} %param.10), channel_id=1, source_target_pairs={{0,2},{1,3},{2,0},{3,1},{4,6},{5,7},{6,4},{7,5},{8,10},{9,11},{10,... | collective-permute-start | bytes 393224 | tf_op jit(solution)/shard_map/ppermute | solution.py:28
  6.3 0.5 collective-permute-start.2
  6.8 0.2 collective-permute-start.5
  7.0 0.0 collective-permute-start.4
  7.0 4.4 %collective-permute-done.2.seen_b.taps_other = f32[31,512]{1,0:T(8,128)S(1)} collective-permute-done((f32[31,512]{1,0:T(8,128)}, f32[31,512]{1,0:T(8,128)S(1)}, u32[]{:S(2)}, u32[]{:S(2)}) %collective-permute-start.2) | collective-permute-done | bytes 63520 | tf_op jit(solution)/shard_map/ppermute | solution.py:28
  11.3 0.0 collective-permute-done.1.seen_a.inputs_other
  11.3 0.0 collective-permute-done.block
  11.4 1.6 %collective-permute-start.3 = (bf16[256,512]{1,0:T(8,128)(2,1)S(1)}, bf16[256,512]{1,0:T(8,128)(2,1)S(1)}, u32[]{:S(2)}, u32[]{:S(2)}) collective-permute-start(bf16[256,512]{1,0:T(8,128)(2,1)S(1)} %turn.1.seen.second), channel_id=1, source_target_pairs={{0,4},{4,0},{8,12},{12,8},{16,20},{20,16},{24,28},{28,24},{1,5},{5... | collective-permute-start | bytes 786440 | tf_op jit(solution)/shard_map/ppermute | solution.py:28
  13.0 1.5 %collective-permute-start.6 = (bf16[128,512]{1,0:T(8,128)(2,1)}, bf16[128,512]{1,0:T(8,128)(2,1)S(1)}, u32[]{:S(2)}, u32[]{:S(2)}) collective-permute-start(bf16[128,512]{1,0:T(8,128)(2,1)} %param.13), channel_id=1, source_target_pairs={{0,2},{1,3},{2,0},{3,1},{4,6},{5,7},{6,4},{7,5},{8,10},{9,11},{10,... | collective-permute-start | bytes 393224 | tf_op jit(solution)/shard_map/ppermute | solution.py:28
  14.5 1.1 %pad_add_fusion.joined = bf16[384,512]{1,0:T(8,128)(2,1)S(1)} fusion(bf16[128,512]{1,0:T(8,128)(2,1)} %param.13, bf16[128,512]{1,0:T(8,128)(2,1)} %param.10, bf16[128,512]{1,0:T(8,128)(2,1)} %param.7), kind=kLoop, calls=%fused_computation | loop fusion | flops 1179648 | bytes 786432 | tf_op jit(solution)/shard_map/add | solution.py:465
  15.6 2.6 %collective-permute-done.6.refs_0_.cot_other = bf16[128,512]{1,0:T(8,128)(2,1)S(1)} collective-permute-done((bf16[128,512]{1,0:T(8,128)(2,1)}, bf16[128,512]{1,0:T(8,128)(2,1)S(1)}, u32[]{:S(2)}, u32[]{:S(2)}) %collective-permute-start.6) | collective-permute-done | bytes 131104 | tf_op jit(solution)/shard_map/ppermute | solution.py:28
  18.2 0.0 collective-permute-done.5.first
  18.2 0.0 collective-permute-done.4.near
  18.2 0.6 %forward.1 = (f32[128,512]{1,0:T(8,128)S(1)}, f32[128,512]{1,0:T(8,128)S(1)}, f32[128,512]{1,0:T(8,128)S(1)}) custom-call(bf16[128,512]{1,0:T(8,128)(2,1)S(1)} %get-tuple-element.35.q, bf16[256,512]{1,0:T(8,128)(2,1)S(1)} %pad_add_fusion.1.own, bf16[256,512]{1,0:T(8,128)(2,1)S(1)} %collective-permute-done.4.near, ...), custom_call_target="tpu_custom_call" | custom-call | bytes 3690000 | tf_op jit(solution)/shard_map/forward/pallas_call | solution.py:75
  18.8 0.8 %collective-permute-done.3.relay = bf16[256,512]{1,0:T(8,128)(2,1)S(1)} collective-permute-done((bf16[256,512]{1,0:T(8,128)(2,1)S(1)}, bf16[256,512]{1,0:T(8,128)(2,1)S(1)}, u32[]{:S(2)}, u32[]{:S(2)}) %collective-permute-start.3) | collective-permute-done | bytes 262176 | tf_op jit(solution)/shard_map/ppermute | solution.py:28
  19.6 0.0 copy-done
  19.6 0.0 copy-start.1
  19.6 0.9 %project.1 = (bf16[128,512]{1,0:T(8,128)(2,1)S(1)}, f32[128,512]{1,0:T(8,128)S(1)}, bf16[128,1024]{1,0:T(8,128)(2,1)S(1)}, bf16[128,1024]{1,0:T(8,128)(2,1)S(1)}) custom-call(bf16[128,512]{1,0:T(8,128)(2,1)S(1)} %get-tuple-element.35.q, bf16[256,512]{1,0:T(8,128)(2,1)S(1)} %collective-permute-done.3.relay, f32[128,512]{1,0:T(8,128)S(1)} %get-tuple-element.36.sums, ...), custom_call_target="tpu_custom_call" | custom-call | bytes 3690000 | tf_op jit(solution)/shard_map/project/pallas_call | solution.py:75
  20.5 0.1 collective-permute-start.7
  20.6 1.5 %collective-permute-done.7.core = bf16[128,1024]{1,0:T(8,128)(2,1)S(1)} collective-permute-done((bf16[128,1024]{1,0:T(8,128)(2,1)S(1)}, bf16[128,1024]{1,0:T(8,128)(2,1)S(1)}, u32[]{:S(2)}, u32[]{:S(2)}) %collective-permute-start.7) | collective-permute-done | bytes 262176 | tf_op jit(solution)/shard_map/ppermute | solution.py:28
  22.1 0.1 join.1
  22.2 1.6 %collective-permute-start.8 = (bf16[128,1024]{1,0:T(8,128)(2,1)S(1)}, bf16[128,1024]{1,0:T(8,128)(2,1)S(1)}, u32[]{:S(2)}, u32[]{:S(2)}) collective-permute-start(bf16[128,1024]{1,0:T(8,128)(2,1)S(1)} %get-tuple-element.42.chip), channel_id=1, source_target_pairs={{0,2},{1,3},{2,0},{3,1},{4,6},{5,7},{6,4},{7,5},{8,10},{9,11},{10,... | collective-permute-start | bytes 786440 | tf_op jit(solution)/shard_map/ppermute | solution.py:28
  23.7 0.5 collective-permute-start.13
  24.2 1.6 %collective-permute-start.12 = (bf16[128,512]{1,0:T(8,128)(2,1)S(1)}, bf16[128,512]{1,0:T(8,128)(2,1)S(1)}, u32[]{:S(2)}, u32[]{:S(2)}) collective-permute-start(bf16[128,512]{1,0:T(8,128)(2,1)S(1)} %get-tuple-element.41.q.refs_0_), channel_id=1, source_target_pairs={{0,8},{8,16},{16,24},{24,28},{28,20},{20,12},{12,4},{4,0},{1,9},{9... | collective-permute-start | bytes 393224 | tf_op jit(solution)/shard_map/ppermute | solution.py:39
  25.8 0.0 collective-permute-start.11
  25.8 3.3 %collective-permute-done.13.refs_3_ = bf16[128,512]{1,0:T(8,128)(2,1)S(1)} collective-permute-done((bf16[128,512]{1,0:T(8,128)(2,1)S(1)}, bf16[128,512]{1,0:T(8,128)(2,1)S(1)}, u32[]{:S(2)}, u32[]{:S(2)}) %collective-permute-start.13) | collective-permute-done | bytes 131104 | tf_op jit(solution)/shard_map/ppermute | solution.py:39
  29.1 0.8 %collective-permute-start.14 = (bf16[128,512]{1,0:T(8,128)(2,1)S(1)}, bf16[128,512]{1,0:T(8,128)(2,1)S(1)}, u32[]{:S(2)}, u32[]{:S(2)}) collective-permute-start(bf16[128,512]{1,0:T(8,128)(2,1)S(1)} %collective-permute-done.13.refs_3_), channel_id=1, source_target_pairs={{0,4},{4,0},{8,12},{12,8},{16,20},{20,16},{24,28},{28,24},{1,5},{5... | collective-permute-start | bytes 393224 | tf_op jit(solution)/shard_map/ppermute | solution.py:28
  29.8 0.7 %collective-permute-done.8.across = bf16[128,1024]{1,0:T(8,128)(2,1)S(1)} collective-permute-done((bf16[128,1024]{1,0:T(8,128)(2,1)S(1)}, bf16[128,1024]{1,0:T(8,128)(2,1)S(1)}, u32[]{:S(2)}, u32[]{:S(2)}) %collective-permute-start.8) | collective-permute-done | bytes 262176 | tf_op jit(solution)/shard_map/ppermute | solution.py:28
  30.6 0.1 hidden.1
  30.7 0.6 %collective-permute-start.9 = (bf16[48,1024]{1,0:T(8,128)(2,1)S(1)}, bf16[48,1024]{1,0:T(8,128)(2,1)S(1)}, u32[]{:S(2)}, u32[]{:S(2)}) collective-permute-start(bf16[48,1024]{1,0:T(8,128)(2,1)S(1)} %get-tuple-element.46), channel_id=1, source_target_pairs={{0,4},{4,0},{8,12},{12,8},{16,20},{20,16},{24,28},{28,24},{1,5},{5... | collective-permute-start | bytes 294920 | tf_op jit(solution)/shard_map/ppermute | solution.py:28
  31.3 0.0 collective-permute-start.10
  31.3 0.0 collective-permute-done.12.seen_b.refs_2_
  31.3 0.0 collective-permute-done.11.seen_a.refs_1_
  31.3 0.0 copy-done.1
  31.3 3.1 %conv_inner.1 = (bf16[128,512]{1,0:T(8,128)(2,1)S(1)}, f32[64,1024]{1,0:T(8,128)S(1)}, f32[128,1024]{1,0:T(8,128)S(1)}) custom-call(bf16[128,1024]{1,0:T(8,128)(2,1)S(1)} %get-tuple-element.45.hidden, bf16[128,512]{1,0:T(8,128)(2,1)S(1)} %get-tuple-element.44.cot, bf16[128,512]{1,0:T(8,128)(2,1)S(1)} %collective-permute-done.6.refs_0_.cot_other, ...), custom_call_target="tpu_custom_call" | custom-call | bytes 11439000 | tf_op jit(solution)/shard_map/conv_inner/pallas_call | solution.py:75
  34.4 0.7 %collective-permute-done.14.seen.refs_4_.query = bf16[128,512]{1,0:T(8,128)(2,1)S(1)} collective-permute-done((bf16[128,512]{1,0:T(8,128)(2,1)S(1)}, bf16[128,512]{1,0:T(8,128)(2,1)S(1)}, u32[]{:S(2)}, u32[]{:S(2)}) %collective-permute-start.14) | collective-permute-done | bytes 131104 | tf_op jit(solution)/shard_map/ppermute | solution.py:28
  35.1 1.2 %collective-permute-done.9.rim_near = bf16[48,1024]{1,0:T(8,128)(2,1)S(1)} collective-permute-done((bf16[48,1024]{1,0:T(8,128)(2,1)S(1)}, bf16[48,1024]{1,0:T(8,128)(2,1)S(1)}, u32[]{:S(2)}, u32[]{:S(2)}) %collective-permute-start.9) | collective-permute-done | bytes 98336 | tf_op jit(solution)/shard_map/ppermute | solution.py:28
  36.3 0.0 collective-permute-done.10.rim_far
  36.3 1.4 %conv_edge.1 = (bf16[128,512]{1,0:T(8,128)(2,1)S(1)}, bf16[128,1024]{1,0:T(8,128)(2,1)S(1)}) custom-call(bf16[128,1024]{1,0:T(8,128)(2,1)S(1)} %get-tuple-element.45.hidden, bf16[48,1024]{1,0:T(8,128)(2,1)S(1)} %collective-permute-done.9.rim_near, bf16[48,1024]{1,0:T(8,128)(2,1)S(1)} %collective-permute-done.10.rim_far, ...), custom_call_target="tpu_custom_call" | custom-call | bytes 5166000 | tf_op jit(solution)/shard_map/conv_edge/pallas_call | solution.py:75
  37.7 0.1 collective-permute-start.15
  37.8 0.5 upstream_own.1.partial
  38.3 1.0 %collective-permute-done.15.core = bf16[128,1024]{1,0:T(8,128)(2,1)S(1)} collective-permute-done((bf16[128,1024]{1,0:T(8,128)(2,1)S(1)}, bf16[128,1024]{1,0:T(8,128)(2,1)S(1)}, u32[]{:S(2)}, u32[]{:S(2)}) %collective-permute-start.15) | collective-permute-done | bytes 262176 | tf_op jit(solution)/shard_map/ppermute | solution.py:28
  39.3 0.7 %upstream.1 = (bf16[144,512]{1,0:T(8,128)(2,1)S(1)}, f32[128,512]{1,0:T(8,128)S(1)}) custom-call(bf16[128,1024]{1,0:T(8,128)(2,1)S(1)} %collective-permute-done.15.core, bf16[512,2048]{1,0:T(8,128)(2,1)S(1)} %copy-done, bf16[128,512]{1,0:T(8,128)(2,1)S(1)} %get-tuple-element.52.att, f32[128,512]{1,0:T(8,128)S(1)} %get-tuple-element.53.lse, ...), custom_call_target="tpu_custom_call" | custom-call | bytes 2214000 | tf_op jit(solution)/shard_map/upstream/pallas_call | solution.py:75
  40.0 2.5 %collective-permute-start.16 = (bf16[144,512]{1,0:T(8,128)(2,1)S(1)}, bf16[144,512]{1,0:T(8,128)(2,1)S(1)}, u32[]{:S(2)}, u32[]{:S(2)}) collective-permute-start(bf16[144,512]{1,0:T(8,128)(2,1)S(1)} %get-tuple-element.54.message.refs_5_), channel_id=1, source_target_pairs={{8,0},{16,8},{24,16},{28,24},{20,28},{12,20},{4,12},{0,4},{9,1},{1... | collective-permute-start | bytes 442376 | tf_op jit(solution)/shard_map/ppermute | solution.py:39
  42.5 1.3 %collective-permute-start.19 = (bf16[144,512]{1,0:T(8,128)(2,1)S(1)}, bf16[144,512]{1,0:T(8,128)(2,1)S(1)}, u32[]{:S(2)}, u32[]{:S(2)}) collective-permute-start(bf16[144,512]{1,0:T(8,128)(2,1)S(1)} %get-tuple-element.54.message.refs_5_), channel_id=1, source_target_pairs={{0,8},{8,16},{16,24},{24,28},{28,20},{20,12},{12,4},{4,0},{1,9},{9... | collective-permute-start | bytes 442376 | tf_op jit(solution)/shard_map/ppermute | solution.py:39
  43.8 0.0 collective-permute-start.18
  43.8 4.1 %collective-permute-done.16.refs_8_ = bf16[144,512]{1,0:T(8,128)(2,1)S(1)} collective-permute-done((bf16[144,512]{1,0:T(8,128)(2,1)S(1)}, bf16[144,512]{1,0:T(8,128)(2,1)S(1)}, u32[]{:S(2)}, u32[]{:S(2)}) %collective-permute-start.16) | collective-permute-done | bytes 147488 | tf_op jit(solution)/shard_map/ppermute | solution.py:39
  47.9 0.8 %collective-permute-start.17 = (bf16[144,512]{1,0:T(8,128)(2,1)S(1)}, bf16[144,512]{1,0:T(8,128)(2,1)S(1)}, u32[]{:S(2)}, u32[]{:S(2)}) collective-permute-start(bf16[144,512]{1,0:T(8,128)(2,1)S(1)} %collective-permute-done.16.refs_8_), channel_id=1, source_target_pairs={{0,4},{4,0},{8,12},{12,8},{16,20},{20,16},{24,28},{28,24},{1,5},{5... | collective-permute-start | bytes 442376 | tf_op jit(solution)/shard_map/ppermute | solution.py:28
  48.7 1.5 %query_grad.1 = (bf16[128,512]{1,0:T(8,128)(2,1)}, bf16[128,512]{1,0:T(8,128)(2,1)}, bf16[128,512]{1,0:T(8,128)(2,1)}) custom-call(bf16[128,512]{1,0:T(8,128)(2,1)S(1)} %get-tuple-element.41.q.refs_0_, bf16[256,512]{1,0:T(8,128)(2,1)S(1)} %pad_add_fusion.1.own, bf16[256,512]{1,0:T(8,128)(2,1)S(1)} %collective-permute-done.4.near, ...), custom_call_target="tpu_custom_call" | custom-call | bytes 6642000 | tf_op jit(solution)/shard_map/query_grad/pallas_call | solution.py:75
  50.2 0.0 collective-permute-done.19.refs_7_
  50.2 0.0 collective-permute-done.18.refs_6_
  50.2 0.9 %key_part.1 = (f32[128,512]{1,0:T(8,128)S(1)}, f32[128,512]{1,0:T(8,128)S(1)}, f32[128,512]{1,0:T(8,128)S(1)}) custom-call(bf16[256,512]{1,0:T(8,128)(2,1)S(1)} %pad_add_fusion.1.own, bf16[128,512]{1,0:T(8,128)(2,1)S(1)} %get-tuple-element.41.q.refs_0_, bf16[128,512]{1,0:T(8,128)(2,1)S(1)} %collective-permute-done.11.seen_a.refs_1_, ...), custom_call_target="tpu_custom_call" | custom-call | bytes 5535000 | tf_op jit(solution)/shard_map/key_part/pallas_call | solution.py:75
  51.1 2.2 %collective-permute-done.17.message = bf16[144,512]{1,0:T(8,128)(2,1)S(1)} collective-permute-done((bf16[144,512]{1,0:T(8,128)(2,1)S(1)}, bf16[144,512]{1,0:T(8,128)(2,1)S(1)}, u32[]{:S(2)}, u32[]{:S(2)}) %collective-permute-start.17) | collective-permute-done | bytes 147488 | tf_op jit(solution)/shard_map/ppermute | solution.py:28
  53.3 1.0 %key_grad.1 = (bf16[128,512]{1,0:T(8,128)(2,1)}, bf16[128,512]{1,0:T(8,128)(2,1)}) custom-call(bf16[256,512]{1,0:T(8,128)(2,1)S(1)} %pad_add_fusion.1.own, bf16[128,512]{1,0:T(8,128)(2,1)S(1)} %collective-permute-done.14.seen.refs_4_.query, bf16[144,512]{1,0:T(8,128)(2,1)S(1)} %collective-permute-done.17.message, f32[128,512]{1,0:T(8,128)S(1)} %get-tuple-element.60.late, ...), custom_call_target="tpu_custom_call" | custom-call | bytes 3690000 | tf_op jit(solution)/shard_map/key_grad/pallas_call | solution.py:75
  (2 shorter events, 0.0 us)
Async XLA Ops:
  0.6 19.0 %copy-start = (bf16[512,2048]{1,0:T(8,128)(2,1)S(1)}, bf16[512,2048]{1,0:T(8,128)(2,1)}, u32[]{:S(2)}) copy-start(bf16[512,2048]{1,0:T(8,128)(2,1)} %weight.5) | copy-start | bytes 6291460
  1.8 9.6 %collective-permute-start = (bf16[256,512]{1,0:T(8,128)(2,1)S(1)}, bf16[256,512]{1,0:T(8,128)(2,1)S(1)}, u32[]{:S(2)}, u32[]{:S(2)}) collective-permute-start(bf16[256,512]{1,0:T(8,128)(2,1)S(1)} %pad_add_fusion.1.own), channel_id=1, source_target_pairs={{8,0},{16,8},{24,16},{28,24},{20,28},{12,20},{4,12},{0,4},{9,1},{1... | collective-permute-start | bytes 786440 | tf_op jit(solution)/shard_map/ppermute | solution.py:39
  4.8 6.6 %collective-permute-start.1 = (bf16[128,512]{1,0:T(8,128)(2,1)}, bf16[128,512]{1,0:T(8,128)(2,1)S(1)}, u32[]{:S(2)}, u32[]{:S(2)}) collective-permute-start(bf16[128,512]{1,0:T(8,128)(2,1)} %param.10), channel_id=1, source_target_pairs={{0,2},{1,3},{2,0},{3,1},{4,6},{5,7},{6,4},{7,5},{8,10},{9,11},{10,... | collective-permute-start | bytes 393224 | tf_op jit(solution)/shard_map/ppermute | solution.py:28
  6.3 5.1 %collective-permute-start.2 = (f32[31,512]{1,0:T(8,128)}, f32[31,512]{1,0:T(8,128)S(1)}, u32[]{:S(2)}, u32[]{:S(2)}) collective-permute-start(f32[31,512]{1,0:T(8,128)} %taps.3), channel_id=1, source_target_pairs={{0,2},{1,3},{2,0},{3,1},{4,6},{5,7},{6,4},{7,5},{8,10},{9,11},{10,... | collective-permute-start | bytes 190472 | tf_op jit(solution)/shard_map/ppermute | solution.py:28
  6.8 11.4 %collective-permute-start.5 = (bf16[256,512]{1,0:T(8,128)(2,1)S(1)}, bf16[256,512]{1,0:T(8,128)(2,1)S(1)}, u32[]{:S(2)}, u32[]{:S(2)}) collective-permute-start(bf16[256,512]{1,0:T(8,128)(2,1)S(1)} %pad_add_fusion.1.own), channel_id=1, source_target_pairs={{0,8},{8,16},{16,24},{24,28},{28,20},{20,12},{12,4},{4,0},{1,9},{9... | collective-permute-start | bytes 786440 | tf_op jit(solution)/shard_map/ppermute | solution.py:39
  7.0 11.2 %collective-permute-start.4 = (bf16[256,512]{1,0:T(8,128)(2,1)S(1)}, bf16[256,512]{1,0:T(8,128)(2,1)S(1)}, u32[]{:S(2)}, u32[]{:S(2)}) collective-permute-start(bf16[256,512]{1,0:T(8,128)(2,1)S(1)} %pad_add_fusion.1.own), channel_id=1, source_target_pairs={{0,1},{1,0},{2,3},{3,2},{4,5},{5,4},{6,7},{7,6},{8,12},{9,13},{10,... | collective-permute-start | bytes 786440 | tf_op jit(solution)/shard_map/ppermute | solution.py:50
  11.4 8.2 %collective-permute-start.3 = (bf16[256,512]{1,0:T(8,128)(2,1)S(1)}, bf16[256,512]{1,0:T(8,128)(2,1)S(1)}, u32[]{:S(2)}, u32[]{:S(2)}) collective-permute-start(bf16[256,512]{1,0:T(8,128)(2,1)S(1)} %turn.1.seen.second), channel_id=1, source_target_pairs={{0,4},{4,0},{8,12},{12,8},{16,20},{20,16},{24,28},{28,24},{1,5},{5... | collective-permute-start | bytes 786440 | tf_op jit(solution)/shard_map/ppermute | solution.py:28
  13.0 5.2 %collective-permute-start.6 = (bf16[128,512]{1,0:T(8,128)(2,1)}, bf16[128,512]{1,0:T(8,128)(2,1)S(1)}, u32[]{:S(2)}, u32[]{:S(2)}) collective-permute-start(bf16[128,512]{1,0:T(8,128)(2,1)} %param.13), channel_id=1, source_target_pairs={{0,2},{1,3},{2,0},{3,1},{4,6},{5,7},{6,4},{7,5},{8,10},{9,11},{10,... | collective-permute-start | bytes 393224 | tf_op jit(solution)/shard_map/ppermute | solution.py:28
  19.6 11.7 %copy-start.1 = (f32[31,512]{1,0:T(8,128)S(1)}, f32[31,512]{1,0:T(8,128)}, u32[]{:S(2)}) copy-start(f32[31,512]{1,0:T(8,128)} %taps.3) | copy-start | bytes 190468
  20.5 1.6 %collective-permute-start.7 = (bf16[128,1024]{1,0:T(8,128)(2,1)S(1)}, bf16[128,1024]{1,0:T(8,128)(2,1)S(1)}, u32[]{:S(2)}, u32[]{:S(2)}) collective-permute-start(bf16[128,1024]{1,0:T(8,128)(2,1)S(1)} %get-tuple-element.40), channel_id=1, source_target_pairs={{0,1},{1,0},{2,3},{3,2},{4,5},{5,4},{6,7},{7,6},{8,9},{9,8},{10,11... | collective-permute-start | bytes 786440 | tf_op jit(solution)/shard_map/ppermute | solution.py:28
  22.2 8.4 %collective-permute-start.8 = (bf16[128,1024]{1,0:T(8,128)(2,1)S(1)}, bf16[128,1024]{1,0:T(8,128)(2,1)S(1)}, u32[]{:S(2)}, u32[]{:S(2)}) collective-permute-start(bf16[128,1024]{1,0:T(8,128)(2,1)S(1)} %get-tuple-element.42.chip), channel_id=1, source_target_pairs={{0,2},{1,3},{2,0},{3,1},{4,6},{5,7},{6,4},{7,5},{8,10},{9,11},{10,... | collective-permute-start | bytes 786440 | tf_op jit(solution)/shard_map/ppermute | solution.py:28
  23.7 5.3 %collective-permute-start.13 = (bf16[128,512]{1,0:T(8,128)(2,1)S(1)}, bf16[128,512]{1,0:T(8,128)(2,1)S(1)}, u32[]{:S(2)}, u32[]{:S(2)}) collective-permute-start(bf16[128,512]{1,0:T(8,128)(2,1)S(1)} %get-tuple-element.41.q.refs_0_), channel_id=1, source_target_pairs={{8,0},{16,8},{24,16},{28,24},{20,28},{12,20},{4,12},{0,4},{9,1},{1... | collective-permute-start | bytes 393224 | tf_op jit(solution)/shard_map/ppermute | solution.py:39
  24.2 7.1 %collective-permute-start.12 = (bf16[128,512]{1,0:T(8,128)(2,1)S(1)}, bf16[128,512]{1,0:T(8,128)(2,1)S(1)}, u32[]{:S(2)}, u32[]{:S(2)}) collective-permute-start(bf16[128,512]{1,0:T(8,128)(2,1)S(1)} %get-tuple-element.41.q.refs_0_), channel_id=1, source_target_pairs={{0,8},{8,16},{16,24},{24,28},{28,20},{20,12},{12,4},{4,0},{1,9},{9... | collective-permute-start | bytes 393224 | tf_op jit(solution)/shard_map/ppermute | solution.py:39
  25.8 5.5 %collective-permute-start.11 = (bf16[128,512]{1,0:T(8,128)(2,1)S(1)}, bf16[128,512]{1,0:T(8,128)(2,1)S(1)}, u32[]{:S(2)}, u32[]{:S(2)}) collective-permute-start(bf16[128,512]{1,0:T(8,128)(2,1)S(1)} %get-tuple-element.41.q.refs_0_), channel_id=1, source_target_pairs={{0,1},{1,0},{2,3},{3,2},{4,5},{5,4},{6,7},{7,6},{8,12},{9,13},{10,... | collective-permute-start | bytes 393224 | tf_op jit(solution)/shard_map/ppermute | solution.py:50
  29.1 6.0 %collective-permute-start.14 = (bf16[128,512]{1,0:T(8,128)(2,1)S(1)}, bf16[128,512]{1,0:T(8,128)(2,1)S(1)}, u32[]{:S(2)}, u32[]{:S(2)}) collective-permute-start(bf16[128,512]{1,0:T(8,128)(2,1)S(1)} %collective-permute-done.13.refs_3_), channel_id=1, source_target_pairs={{0,4},{4,0},{8,12},{12,8},{16,20},{20,16},{24,28},{28,24},{1,5},{5... | collective-permute-start | bytes 393224 | tf_op jit(solution)/shard_map/ppermute | solution.py:28
  30.7 5.6 %collective-permute-start.9 = (bf16[48,1024]{1,0:T(8,128)(2,1)S(1)}, bf16[48,1024]{1,0:T(8,128)(2,1)S(1)}, u32[]{:S(2)}, u32[]{:S(2)}) collective-permute-start(bf16[48,1024]{1,0:T(8,128)(2,1)S(1)} %get-tuple-element.46), channel_id=1, source_target_pairs={{0,4},{4,0},{8,12},{12,8},{16,20},{20,16},{24,28},{28,24},{1,5},{5... | collective-permute-start | bytes 294920 | tf_op jit(solution)/shard_map/ppermute | solution.py:28
  31.3 5.0 %collective-permute-start.10 = (bf16[48,1024]{1,0:T(8,128)(2,1)S(1)}, bf16[48,1024]{1,0:T(8,128)(2,1)S(1)}, u32[]{:S(2)}, u32[]{:S(2)}) collective-permute-start(bf16[48,1024]{1,0:T(8,128)(2,1)S(1)} %get-tuple-element.47), channel_id=1, source_target_pairs={{0,1},{1,0},{2,3},{3,2},{4,8},{5,9},{6,10},{7,11},{8,4},{9,5},{10,... | collective-permute-start | bytes 294920 | tf_op jit(solution)/shard_map/ppermute | solution.py:50
  37.7 1.6 %collective-permute-start.15 = (bf16[128,1024]{1,0:T(8,128)(2,1)S(1)}, bf16[128,1024]{1,0:T(8,128)(2,1)S(1)}, u32[]{:S(2)}, u32[]{:S(2)}) collective-permute-start(bf16[128,1024]{1,0:T(8,128)(2,1)S(1)} %get-tuple-element.51.own.grad_here), channel_id=1, source_target_pairs={{0,1},{1,0},{2,3},{3,2},{4,5},{5,4},{6,7},{7,6},{8,9},{9,8},{10,11... | collective-permute-start | bytes 786440 | tf_op jit(solution)/shard_map/ppermute | solution.py:28
  40.0 7.9 %collective-permute-start.16 = (bf16[144,512]{1,0:T(8,128)(2,1)S(1)}, bf16[144,512]{1,0:T(8,128)(2,1)S(1)}, u32[]{:S(2)}, u32[]{:S(2)}) collective-permute-start(bf16[144,512]{1,0:T(8,128)(2,1)S(1)} %get-tuple-element.54.message.refs_5_), channel_id=1, source_target_pairs={{8,0},{16,8},{24,16},{28,24},{20,28},{12,20},{4,12},{0,4},{9,1},{1... | collective-permute-start | bytes 442376 | tf_op jit(solution)/shard_map/ppermute | solution.py:39
  42.5 7.7 %collective-permute-start.19 = (bf16[144,512]{1,0:T(8,128)(2,1)S(1)}, bf16[144,512]{1,0:T(8,128)(2,1)S(1)}, u32[]{:S(2)}, u32[]{:S(2)}) collective-permute-start(bf16[144,512]{1,0:T(8,128)(2,1)S(1)} %get-tuple-element.54.message.refs_5_), channel_id=1, source_target_pairs={{0,8},{8,16},{16,24},{24,28},{28,20},{20,12},{12,4},{4,0},{1,9},{9... | collective-permute-start | bytes 442376 | tf_op jit(solution)/shard_map/ppermute | solution.py:39
  43.8 6.4 %collective-permute-start.18 = (bf16[144,512]{1,0:T(8,128)(2,1)S(1)}, bf16[144,512]{1,0:T(8,128)(2,1)S(1)}, u32[]{:S(2)}, u32[]{:S(2)}) collective-permute-start(bf16[144,512]{1,0:T(8,128)(2,1)S(1)} %get-tuple-element.54.message.refs_5_), channel_id=1, source_target_pairs={{0,1},{1,0},{2,3},{3,2},{4,5},{5,4},{6,7},{7,6},{8,12},{9,13},{10,... | collective-permute-start | bytes 442376 | tf_op jit(solution)/shard_map/ppermute | solution.py:50
  47.9 5.4 %collective-permute-start.17 = (bf16[144,512]{1,0:T(8,128)(2,1)S(1)}, bf16[144,512]{1,0:T(8,128)(2,1)S(1)}, u32[]{:S(2)}, u32[]{:S(2)}) collective-permute-start(bf16[144,512]{1,0:T(8,128)(2,1)S(1)} %collective-permute-done.16.refs_8_), channel_id=1, source_target_pairs={{0,4},{4,0},{8,12},{12,8},{16,20},{20,16},{24,28},{28,24},{1,5},{5... | collective-permute-start | bytes 442376 | tf_op jit(solution)/shard_map/ppermute | solution.py:28

commit v10 on v9

--- a/solution.py
+++ b/solution.py
@@ -58,11 +58,10 @@
     return total_swap(block, lambda i, count: ((i + 1) ^ 1) - 1 if 0 < i < count - 1 else None)
 
 
-def window_of(block, before_relay=lambda second: second):
+def window_of(block):
     second = ring(block, 1)
     first = ring(block, 0)
     near = inner_swap(block)
-    second = before_relay(second)
     return near, first, second, pair_swap(second, "ctx", 1)
 
 
@@ -159,10 +158,6 @@
     width = weight.shape[0]
     at = (lax.axis_index("mp") ^ flip) * width
     return weight[:, pl.ds(pl.multiple_of(at, 128), width)]
-
-
-def hold_body(block, seen_a, seen_b, held):
-    held[...] = block[...]
 
 
 def split_body(joined, seen, *parts):
@@ -189,7 +184,7 @@
         totals[:, c] = s[:, HDIM:]
 
 
-def project_body(scale, q, relay, sums, tops, totals, weight, att, lse, send, keep):
+def project_body(scale, q, relay, sums, tops, totals, weight, seen_a, seen_b, att, lse, send, keep):
     frames, width = q.shape
     heads = columns(width)
     bias = bias_of(far_there())
@@ -212,30 +207,44 @@
         lse[:, c] = part
 
 
-def join_body(keep, core, q, chip, q_copy):
-    chip[...] = (keep[...].astype(F32) + core[...].astype(F32)).astype(BF16)
-    q_copy[...] = q[...]
-
-
-def hidden_body(chip, across, inputs, cot, inputs_other, cot_other, hidden, rim_near, rim_far):
+def pass_body(send, q_second, send_copy, second_copy):
+    send_copy[...] = send[...]
+    second_copy[...] = q_second[...]
+
+
+def join_body(keep, core, inputs, cot, cot_other, q, q_second, chip, rim_near, rim_far, q_copy, second_copy):
     frames, width = inputs.shape
     wide = 2 * HALO
     even = is_even()
-    mine, its = slice(0, width), slice(width, 2 * width)
-    for cols, back, rows, cots in (
-        (mine, its, inputs[...], cot[...]),
-        (its, mine, inputs_other[...], cot_other[...]),
+    for cols, rows, cots in (
+        (slice(0, width), inputs[...].astype(F32), cot),
+        (slice(width, 2 * width), 0.0, cot_other),
     ):
-        mixed = chip[:, cols].astype(F32) + across[:, back].astype(F32)
-        total = (rows.astype(F32) + mixed).astype(BF16)
+        total = (rows + (keep[:, cols].astype(F32) + core[:, cols].astype(F32))).astype(BF16)
         for at, first, last in (
             (slice(0, wide), total[0:wide], total[frames - wide :]),
-            (slice(wide, wide + HALO), cots[0:HALO], cots[frames - HALO :]),
+            (slice(wide, wide + HALO), cots[0:HALO, :], cots[frames - HALO : frames, :]),
         ):
             first, last = first.astype(F32), last.astype(F32)
             rim_near[at, cols] = jnp.where(even, last, first).astype(BF16)
             rim_far[at, cols] = jnp.where(even, first, last).astype(BF16)
-        hidden[:, cols] = total
+        chip[:, cols] = total
+    q_copy[...] = q[...]
+    second_copy[...] = q_second[...]
+
+
+def stack_body(rim_near, rim_far, q, q_second, ends, q_copy, second_copy):
+    wide = 2 * HALO
+    ends[0:wide, :] = rim_near[0:wide, :]
+    ends[wide : 2 * wide, :] = rim_far[0:wide, :]
+    q_copy[...] = q[...]
+    second_copy[...] = q_second[...]
+
+
+def summed(share, across, rows, cols, width):
+    back = slice((cols.start + width) % (2 * width), (cols.stop - 1 + width) % (2 * width) + 1)
+    total = share[rows, cols].astype(F32) + across[rows, back].astype(F32)
+    return total.astype(BF16).astype(F32)
 
 
 def shifted_sum(rows, taps_of, count):
@@ -276,13 +285,15 @@
         yield own, cols, local, cot if own else cot_other, taps if own else taps_other
 
 
-def conv_inner_body(hidden, cot, cot_other, taps, taps_other, seen_a, seen_b, rows_out, edge_conv, part_grad):
+def conv_inner_body(
+    chip, across, cot, cot_other, taps, taps_other, rows_out, edge_rows, edge_conv, part_grad
+):
     frames, width = cot.shape
     wide, count = 2 * HALO, taps.shape[0]
     inner = slice(HALO, frames - HALO)
     none = jnp.zeros((wide, HDIM), F32)
     for own, cols, local, cots_of, tap in conv_chunks(width, cot, cot_other, taps, taps_other):
-        rows = hidden[:, cols].astype(F32)
+        rows = summed(chip, across, slice(0, frames), cols, width)
         cots = cots_of[:, local].astype(F32)
         conv = shifted_sum(
             jnp.concatenate([none, rows, none], axis=0), taps_forward(tap, count, local), frames + wide
@@ -295,29 +306,31 @@
         edge_conv[wide : 2 * wide, cols] = conv[frames : frames + wide]
         if own:
             rows_out[inner, cols] = (rows[inner] + silu).astype(BF16)
+            edge_rows[0:HALO, cols] = rows[0:HALO]
+            edge_rows[HALO:wide, cols] = rows[frames - HALO :]
         part_grad[:, cols] = cots + back
 
 
 def conv_edge_body(
-    hidden, rim_near, rim_far, cot, cot_other, taps, taps_other, rows_in, edge_conv, part_grad,
-    seen, output, grad_input,
+    ends, ends_across, rim_near, rim_far, cot, cot_other, taps, taps_other,
+    rows_in, edge_rows, edge_conv, part_grad, seen_a, seen_b, seen_c, output, grad_input,
 ):
     frames, width = cot.shape
     wide, count = 2 * HALO, taps.shape[0]
     even, far = is_even(), far_there()
-    rims, cots_of = slice(0, wide), slice(wide, wide + HALO)
     low, high = slice(0, HALO), slice(frames - HALO, frames)
     inner = slice(HALO, frames - HALO)
     none = jnp.zeros((wide, HDIM), F32)
-
-    def sides(rows, cols):
-        near = rim_near[rows, cols].astype(F32)
-        beyond = jnp.where(far, rim_far[rows, cols].astype(F32), 0.0)
+    cots_of = slice(wide, wide + HALO)
+
+    def sides(near, beyond):
+        beyond = jnp.where(far, beyond, 0.0)
         return jnp.where(even, beyond, near), jnp.where(even, near, beyond)
 
     for own, cols, local, block, tap in conv_chunks(width, cot, cot_other, taps, taps_other):
-        row_low, row_high = sides(rims, cols)
-        cot_low, cot_high = sides(cots_of, cols)
+        rows = summed(ends, ends_across, slice(0, 2 * wide), cols, width)
+        row_low, row_high = sides(rows[0:wide], rows[wide:])
+        cot_low, cot_high = sides(rim_near[cots_of, cols].astype(F32), rim_far[cots_of, cols].astype(F32))
         conv = edge_conv[:, cols] + shifted_sum(
             jnp.concatenate([row_low, none, row_high], axis=0), taps_forward(tap, count, local), 2 * wide
         )
@@ -334,9 +347,9 @@
             axis=0,
         ).astype(BF16)
         if own:
-            output[low, cols] = (hidden[low, cols].astype(F32) + silu[HALO:wide]).astype(BF16)
+            output[low, cols] = (edge_rows[0:HALO, cols] + silu[HALO:wide]).astype(BF16)
             output[inner, cols] = rows_in[inner, cols]
-            output[high, cols] = (hidden[high, cols].astype(F32) + silu[wide : wide + HALO]).astype(BF16)
+            output[high, cols] = (edge_rows[HALO:wide, cols] + silu[wide : wide + HALO]).astype(BF16)
 
 
 def upstream_part(grads, weight, flips):
@@ -455,13 +468,9 @@
     kv = lax.pad(key_rows, zero, ((0, frames, 0), (0, 0, 0))) + lax.pad(
         value_rows, zero, ((frames, 0, 0), (0, 0, 0))
     )
-    other = [pair_swap(block, "mp", 2) for block in (inputs, cotangent, kernel)]
-    near, first, second, relay = window_of(
-        kv,
-        lambda second: kernel_call(
-            hold_body, (shaped(kv.shape, BF16),), (second, other[0], other[2]), 0.1, "turn", 2
-        )[0],
-    )
+    near, first, second, relay = window_of(kv)
+    cot_other = pair_swap(cotangent, "mp", 2)
+    taps_other = pair_swap(kernel, "mp", 2)
     joined = sum(
         lax.pad(rows, zero, ((k * frames, (2 - k) * frames, 0), (0, 0, 0)))
         for k, rows in enumerate((query_rows, inputs, cotangent))
@@ -469,47 +478,58 @@
     query, inputs, cotangent = kernel_call(
         split_body, (tile, tile, tile), (joined, second), 0.1, "split", 1
     )
+    q_second = ring(query, 1)
     sums, tops, totals = kernel_call(
         functools.partial(forward_body, scale),
         (tile32, tile32, tile32),
-        (query, kv, near, first, second, other[1]),
-        1.0, "forward", 1,
+        (query, kv, near, first, second),
+        1.0, "forward",
     )
     att, lse, send, keep = kernel_call(
         functools.partial(project_body, scale),
         (tile, tile32, both, both),
-        (query, relay, sums, tops, totals, out_weight),
-        1.0, "project",
-    )
-
+        (query, relay, sums, tops, totals, out_weight, cot_other, taps_other),
+        1.0, "project", 2,
+    )
+
+    send, q_second = kernel_call(pass_body, (both, tile), (send, q_second), 0.1, "pass")
     core = pair_swap(send, "mp", 1)
-    chip, q_own = kernel_call(join_body, (both, tile), (keep, core, query), 0.1, "join")
+    chip, rim_up, rim_down, q_own, q_handed = kernel_call(
+        join_body,
+        (both, rim, rim, tile, tile),
+        (keep, core, inputs, cotangent, cot_other, query, q_second),
+        0.2, "join",
+    )
     across = pair_swap(chip, "mp", 2)
-    q_second = ring(q_own, 1)
+    rim_far = outer_swap(rim_down)
+    rim_near = pair_swap(rim_up, "ctx", 1)
+    ends, q_own, q_handed = kernel_call(
+        stack_body,
+        (shaped((2 * wide, 2 * width), BF16), tile, tile),
+        (rim_near, rim_far, q_own, q_handed),
+        0.1, "stack",
+    )
+    ends_across = pair_swap(ends, "mp", 2)
     q_first = ring(q_own, 0)
     q_near = inner_swap(q_own)
-    q_relay = pair_swap(q_second, "ctx", 1)
-    hidden, rim_up, rim_down = kernel_call(
-        hidden_body,
-        (both, rim, rim),
-        (chip, across, inputs, cotangent, *other[0:2]),
-        0.2, "hidden",
-    )
-
-    rim_far = outer_swap(rim_down)
-    rim_near = pair_swap(rim_up, "ctx", 1)
-    rows_out, edge_conv, part_grad = kernel_call(
+    q_relay = pair_swap(q_handed, "ctx", 1)
+    rows_out, edge_rows, edge_conv, part_grad = kernel_call(
         conv_inner_body,
-        (tile, shaped((2 * wide, 2 * width), F32), shaped((frames, 2 * width), F32)),
-        (hidden, cotangent, other[1], kernel, other[2], q_near, q_first),
-        3.1, "conv_inner", 2,
+        (
+            tile,
+            shaped((wide, width), F32),
+            shaped((2 * wide, 2 * width), F32),
+            shaped((frames, 2 * width), F32),
+        ),
+        (chip, across, cotangent, cot_other, kernel, taps_other),
+        3.1, "conv_inner",
     )
     output_here, grad_here = kernel_call(
         conv_edge_body,
         (tile, both),
-        (hidden, rim_near, rim_far, cotangent, other[1], kernel, other[2], rows_out, edge_conv, part_grad)
-        + (q_relay,),
-        1.4, "conv_edge", 1,
+        (ends, ends_across, rim_near, rim_far, cotangent, cot_other, kernel, taps_other)
+        + (rows_out, edge_rows, edge_conv, part_grad, q_first, q_near, q_relay),
+        1.4, "conv_edge", 3,
     )
 
     gi_core = pair_swap(grad_here, "mp", 1)

time: 54.5 us -> 56.4 us (1.035)
  starting transfers between devices: 18.1 us -> 21.2 us
  waiting for transfers between devices: 22.5 us -> 21.2 us
    ppermute x6, starting transfers between devices: 9.02 us -> 13.8 us  [ring(): return lax.ppermute(block, 'ctx', ring_routes(lax.axis_size('ctx'))[way])]
    ppermute x6, waiting for transfers between devices: 7.4 us -> 5.28 us  [ring(): return lax.ppermute(block, 'ctx', ring_routes(lax.axis_size('ctx'))[way])]
    ppermute x10, starting transfers between devices: 9.02 us -> 7.41 us  [pair_swap(): lax.ppermute(block, axis, [(i, i ^ bit) for i in range(lax.axis_size(axis...]
    ppermute x10, waiting for transfers between devices: 15.1 us -> 15.9 us  [pair_swap(): lax.ppermute(block, axis, [(i, i ^ bit) for i in range(lax.axis_size(axis...]
  transfers between devices with their start and end apart: 20 -> 20, of which waited for: 11 -> 8; matrix products, arithmetic and copies ran while one was open for 2% -> 2% of each run, Pallas kernels for 12% -> 13%
where the time goes in v10:
time: 56.4 us; the launch traced here: 56.3 us
  starting transfers between devices  21.2 us (38%)
  waiting for transfers between devices  21.2 us (38%)
  Pallas kernels  10.8 us (19%)
  other arithmetic  2.19 us (4%)
  between operations  0.83 us (1%)
    ppermute x10, waiting for transfers between devices, pair_swap(): lax.ppermute(block, axis, [(i, i ^ bit) for i in range(lax.axis_size(axis...  15.9 us
    ppermute x6, starting transfers between devices, ring(): return lax.ppermute(block, 'ctx', ring_routes(lax.axis_size('ctx'))[way])  13.8 us
    pallas_call x13, Pallas kernels, kernel_call(): pl.pallas_call(body, out_shape=outs, in_specs=[VMEM] * (len(args) - unrea...  10.8 us
    ppermute x10, starting transfers between devices, pair_swap(): lax.ppermute(block, axis, [(i, i ^ bit) for i in range(lax.axis_size(axis...  7.41 us
    ppermute x6, waiting for transfers between devices, ring(): return lax.ppermute(block, 'ctx', ring_routes(lax.axis_size('ctx'))[way])  5.28 us
    add x1, other arithmetic, per_device(): lax.pad(key_rows, zero, ((0, frames, 0), (0, 0, 0)))  1.13 us
  transfers between devices with their start and end apart: 20, of which 8 were waited for; matrix products, arithmetic and copies ran while one was open for 2% of the time, Pallas kernels for 13%

profile of v10, /device:TPU:0, one launch (start us, length us, event | category | flops | bytes accessed | tf_op | source)
XLA Modules:
  0.0 56.3 jit_solution(13590331850147436906)
XLA Ops:
  0.6 0.0 copy-start
  0.6 1.1 %pad_add_fusion.1.own = bf16[256,512]{1,0:T(8,128)(2,1)S(1)} fusion(bf16[128,512]{1,0:T(8,128)(2,1)} %param.9, bf16[128,512]{1,0:T(8,128)(2,1)} %param.8), kind=kLoop, calls=%fused_computation.1 | loop fusion | flops 524288 | bytes 524288 | tf_op jit(solution)/shard_map/add | solution.py:468
  1.8 3.0 %collective-permute-start = (bf16[256,512]{1,0:T(8,128)(2,1)S(1)}, bf16[256,512]{1,0:T(8,128)(2,1)S(1)}, u32[]{:S(2)}, u32[]{:S(2)}) collective-permute-start(bf16[256,512]{1,0:T(8,128)(2,1)S(1)} %pad_add_fusion.1.own), channel_id=1, source_target_pairs={{8,0},{16,8},{24,16},{28,24},{20,28},{12,20},{4,12},{0,4},{9,1},{1... | collective-permute-start | bytes 786440 | tf_op jit(solution)/shard_map/ppermute | solution.py:39
  4.8 0.0 collective-permute-start.2
  4.8 3.2 %collective-permute-start.3 = (bf16[256,512]{1,0:T(8,128)(2,1)S(1)}, bf16[256,512]{1,0:T(8,128)(2,1)S(1)}, u32[]{:S(2)}, u32[]{:S(2)}) collective-permute-start(bf16[256,512]{1,0:T(8,128)(2,1)S(1)} %pad_add_fusion.1.own), channel_id=1, source_target_pairs={{0,8},{8,16},{16,24},{24,28},{28,20},{20,12},{12,4},{4,0},{1,9},{9... | collective-permute-start | bytes 786440 | tf_op jit(solution)/shard_map/ppermute | solution.py:39
  7.9 3.2 %collective-permute-done.seen.second = bf16[256,512]{1,0:T(8,128)(2,1)S(1)} collective-permute-done((bf16[256,512]{1,0:T(8,128)(2,1)S(1)}, bf16[256,512]{1,0:T(8,128)(2,1)S(1)}, u32[]{:S(2)}, u32[]{:S(2)}) %collective-permute-start) | collective-permute-done | bytes 262176 | tf_op jit(solution)/shard_map/ppermute | solution.py:39
  11.2 1.7 %collective-permute-start.1 = (bf16[256,512]{1,0:T(8,128)(2,1)S(1)}, bf16[256,512]{1,0:T(8,128)(2,1)S(1)}, u32[]{:S(2)}, u32[]{:S(2)}) collective-permute-start(bf16[256,512]{1,0:T(8,128)(2,1)S(1)} %collective-permute-done.seen.second), channel_id=1, source_target_pairs={{0,4},{4,0},{8,12},{12,8},{16,20},{20,16},{24,28},{28,24},{1,5},{5... | collective-permute-start | bytes 786440 | tf_op jit(solution)/shard_map/ppermute | solution.py:28
  12.8 1.5 %collective-permute-start.4 = (bf16[128,512]{1,0:T(8,128)(2,1)}, bf16[128,512]{1,0:T(8,128)(2,1)S(1)}, u32[]{:S(2)}, u32[]{:S(2)}) collective-permute-start(bf16[128,512]{1,0:T(8,128)(2,1)} %param.13), channel_id=1, source_target_pairs={{0,2},{1,3},{2,0},{3,1},{4,6},{5,7},{6,4},{7,5},{8,10},{9,11},{10,... | collective-permute-start | bytes 393224 | tf_op jit(solution)/shard_map/ppermute | solution.py:28
  14.3 1.1 %pad_add_fusion.joined = bf16[384,512]{1,0:T(8,128)(2,1)S(1)} fusion(bf16[128,512]{1,0:T(8,128)(2,1)} %param.13, bf16[128,512]{1,0:T(8,128)(2,1)} %param.10, bf16[128,512]{1,0:T(8,128)(2,1)} %param.7), kind=kLoop, calls=%fused_computation | loop fusion | flops 1179648 | bytes 786432 | tf_op jit(solution)/shard_map/add | solution.py:474
  15.4 0.6 %collective-permute-start.6 = (bf16[128,512]{1,0:T(8,128)(2,1)S(1)}, bf16[128,512]{1,0:T(8,128)(2,1)S(1)}, u32[]{:S(2)}, u32[]{:S(2)}) collective-permute-start(bf16[128,512]{1,0:T(8,128)(2,1)S(1)} %get-tuple-element.41.q), channel_id=1, source_target_pairs={{8,0},{16,8},{24,16},{28,24},{20,28},{12,20},{4,12},{0,4},{9,1},{1... | collective-permute-start | bytes 393224 | tf_op jit(solution)/shard_map/ppermute | solution.py:39
  16.0 0.0 collective-permute-done.2.near
  16.0 0.3 collective-permute-start.5
  16.4 0.0 collective-permute-done.3.first
  16.4 0.6 %forward.1 = (f32[128,512]{1,0:T(8,128)S(1)}, f32[128,512]{1,0:T(8,128)S(1)}, f32[128,512]{1,0:T(8,128)S(1)}) custom-call(bf16[128,512]{1,0:T(8,128)(2,1)S(1)} %get-tuple-element.41.q, bf16[256,512]{1,0:T(8,128)(2,1)S(1)} %pad_add_fusion.1.own, bf16[256,512]{1,0:T(8,128)(2,1)S(1)} %collective-permute-done.2.near, ...), custom_call_target="tpu_custom_call" | custom-call | bytes 3690000 | tf_op jit(solution)/shard_map/forward/pallas_call | solution.py:74
  17.0 3.5 %collective-permute-done.5.seen_b.taps_other = f32[31,512]{1,0:T(8,128)S(1)} collective-permute-done((f32[31,512]{1,0:T(8,128)}, f32[31,512]{1,0:T(8,128)S(1)}, u32[]{:S(2)}, u32[]{:S(2)}) %collective-permute-start.5) | collective-permute-done | bytes 63520 | tf_op jit(solution)/shard_map/ppermute | solution.py:28
  20.5 0.0 collective-permute-done.4.seen_a.cot_other
  20.5 0.0 collective-permute-done.1.relay
  20.5 0.0 copy-done
  20.5 0.0 copy-start.1
  20.5 0.9 %project.1 = (bf16[128,512]{1,0:T(8,128)(2,1)S(1)}, f32[128,512]{1,0:T(8,128)S(1)}, bf16[128,1024]{1,0:T(8,128)(2,1)S(1)}, bf16[128,1024]{1,0:T(8,128)(2,1)S(1)}) custom-call(bf16[128,512]{1,0:T(8,128)(2,1)S(1)} %get-tuple-element.41.q, bf16[256,512]{1,0:T(8,128)(2,1)S(1)} %collective-permute-done.1.relay, f32[128,512]{1,0:T(8,128)S(1)} %get-tuple-element.42.sums, ...), custom_call_target="tpu_custom_call" | custom-call | bytes 3690000 | tf_op jit(solution)/shard_map/project/pallas_call | solution.py:74
  21.4 0.0 collective-permute-done.6.q_second
  21.4 0.1 collective-permute-start.7
  21.5 1.5 %collective-permute-done.7.core = bf16[128,1024]{1,0:T(8,128)(2,1)S(1)} collective-permute-done((bf16[128,1024]{1,0:T(8,128)(2,1)S(1)}, bf16[128,1024]{1,0:T(8,128)(2,1)S(1)}, u32[]{:S(2)}, u32[]{:S(2)}) %collective-permute-start.7) | collective-permute-done | bytes 262176 | tf_op jit(solution)/shard_map/ppermute | solution.py:28
  23.0 0.1 join.1
  23.2 0.5 collective-permute-start.11
  23.6 2.5 %collective-permute-start.8 = (bf16[48,1024]{1,0:T(8,128)(2,1)S(1)}, bf16[48,1024]{1,0:T(8,128)(2,1)S(1)}, u32[]{:S(2)}, u32[]{:S(2)}) collective-permute-start(bf16[48,1024]{1,0:T(8,128)(2,1)S(1)} %get-tuple-element.51), channel_id=1, source_target_pairs={{0,4},{4,0},{8,12},{12,8},{16,20},{20,16},{24,28},{28,24},{1,5},{5... | collective-permute-start | bytes 294920 | tf_op jit(solution)/shard_map/ppermute | solution.py:28
  26.1 0.0 collective-permute-start.9
  26.1 4.2 %collective-permute-done.8.rim_near = bf16[48,1024]{1,0:T(8,128)(2,1)S(1)} collective-permute-done((bf16[48,1024]{1,0:T(8,128)(2,1)S(1)}, bf16[48,1024]{1,0:T(8,128)(2,1)S(1)}, u32[]{:S(2)}, u32[]{:S(2)}) %collective-permute-start.8) | collective-permute-done | bytes 98336 | tf_op jit(solution)/shard_map/ppermute | solution.py:28
  30.3 0.0 collective-permute-done.9.rim_far
  30.3 0.8 %collective-permute-start.10 = (bf16[64,1024]{1,0:T(8,128)(2,1)S(1)}, bf16[64,1024]{1,0:T(8,128)(2,1)S(1)}, u32[]{:S(2)}, u32[]{:S(2)}) collective-permute-start(bf16[64,1024]{1,0:T(8,128)(2,1)S(1)} %get-tuple-element.56.ends), channel_id=1, source_target_pairs={{0,2},{1,3},{2,0},{3,1},{4,6},{5,7},{6,4},{7,5},{8,10},{9,11},{10,... | collective-permute-start | bytes 393224 | tf_op jit(solution)/shard_map/ppermute | solution.py:28
  31.1 2.9 %collective-permute-start.12 = (bf16[128,512]{1,0:T(8,128)(2,1)S(1)}, bf16[128,512]{1,0:T(8,128)(2,1)S(1)}, u32[]{:S(2)}, u32[]{:S(2)}) collective-permute-start(bf16[128,512]{1,0:T(8,128)(2,1)S(1)} %get-tuple-element.55.q.refs_0_), channel_id=1, source_target_pairs={{0,8},{8,16},{16,24},{24,28},{28,20},{20,12},{12,4},{4,0},{1,9},{9... | collective-permute-start | bytes 393224 | tf_op jit(solution)/shard_map/ppermute | solution.py:39
  34.0 0.0 collective-permute-start.13
  34.0 0.0 collective-permute-start.14
  34.0 0.0 collective-permute-done.11.across
  34.0 0.0 copy-done.1
  34.0 3.2 %conv_inner.1 = (bf16[128,512]{1,0:T(8,128)(2,1)S(1)}, f32[32,512]{1,0:T(8,128)S(1)}, f32[64,1024]{1,0:T(8,128)S(1)}, f32[128,1024]{1,0:T(8,128)S(1)}) custom-call(bf16[128,1024]{1,0:T(8,128)(2,1)S(1)} %get-tuple-element.57.chip, bf16[128,1024]{1,0:T(8,128)(2,1)S(1)} %collective-permute-done.11.across, bf16[128,512]{1,0:T(8,128)(2,1)S(1)} %get-tuple-element.49.cot, ...), custom_call_target="tpu_custom_call" | custom-call | bytes 11439000 | tf_op jit(solution)/shard_map/conv_inner/pallas_call | solution.py:74
  37.2 0.0 collective-permute-done.10.ends_across
  37.2 0.0 collective-permute-done.12.seen_a.refs_2_
  37.2 0.0 collective-permute-done.13.seen_b.refs_1_
  37.2 2.7 %collective-permute-done.14.seen_c.refs_4_.query = bf16[128,512]{1,0:T(8,128)(2,1)S(1)} collective-permute-done((bf16[128,512]{1,0:T(8,128)(2,1)S(1)}, bf16[128,512]{1,0:T(8,128)(2,1)S(1)}, u32[]{:S(2)}, u32[]{:S(2)}) %collective-permute-start.14) | collective-permute-done | bytes 131104 | tf_op jit(solution)/shard_map/ppermute | solution.py:28
  39.9 1.5 %conv_edge.1 = (bf16[128,512]{1,0:T(8,128)(2,1)S(1)}, bf16[128,1024]{1,0:T(8,128)(2,1)S(1)}) custom-call(bf16[64,1024]{1,0:T(8,128)(2,1)S(1)} %get-tuple-element.56.ends, bf16[64,1024]{1,0:T(8,128)(2,1)S(1)} %collective-permute-done.10.ends_across, bf16[48,1024]{1,0:T(8,128)(2,1)S(1)} %collective-permute-done.8.rim_near, ...), custom_call_target="tpu_custom_call" | custom-call | bytes 5166000 | tf_op jit(solution)/shard_map/conv_edge/pallas_call | solution.py:74
  41.4 0.1 collective-permute-start.15
  41.5 0.5 upstream_own.1.partial
  42.0 1.0 %collective-permute-done.15.core = bf16[128,1024]{1,0:T(8,128)(2,1)S(1)} collective-permute-done((bf16[128,1024]{1,0:T(8,128)(2,1)S(1)}, bf16[128,1024]{1,0:T(8,128)(2,1)S(1)}, u32[]{:S(2)}, u32[]{:S(2)}) %collective-permute-start.15) | collective-permute-done | bytes 262176 | tf_op jit(solution)/shard_map/ppermute | solution.py:28
  43.0 0.7 %upstream.1 = (bf16[144,512]{1,0:T(8,128)(2,1)S(1)}, f32[128,512]{1,0:T(8,128)S(1)}) custom-call(bf16[128,1024]{1,0:T(8,128)(2,1)S(1)} %collective-permute-done.15.core, bf16[512,2048]{1,0:T(8,128)(2,1)S(1)} %copy-done, bf16[128,512]{1,0:T(8,128)(2,1)S(1)} %get-tuple-element.64.att, f32[128,512]{1,0:T(8,128)S(1)} %get-tuple-element.65.lse, ...), custom_call_target="tpu_custom_call" | custom-call | bytes 2214000 | tf_op jit(solution)/shard_map/upstream/pallas_call | solution.py:74
  43.7 0.3 collective-permute-start.16
  44.0 0.0 collective-permute-start.18
  44.0 3.9 %collective-permute-start.19 = (bf16[144,512]{1,0:T(8,128)(2,1)S(1)}, bf16[144,512]{1,0:T(8,128)(2,1)S(1)}, u32[]{:S(2)}, u32[]{:S(2)}) collective-permute-start(bf16[144,512]{1,0:T(8,128)(2,1)S(1)} %get-tuple-element.66.message.refs_5_), channel_id=1, source_target_pairs={{0,8},{8,16},{16,24},{24,28},{28,20},{20,12},{12,4},{4,0},{1,9},{9... | collective-permute-start | bytes 442376 | tf_op jit(solution)/shard_map/ppermute | solution.py:39
  47.9 2.0 %collective-permute-done.16.refs_8_ = bf16[144,512]{1,0:T(8,128)(2,1)S(1)} collective-permute-done((bf16[144,512]{1,0:T(8,128)(2,1)S(1)}, bf16[144,512]{1,0:T(8,128)(2,1)S(1)}, u32[]{:S(2)}, u32[]{:S(2)}) %collective-permute-start.16) | collective-permute-done | bytes 147488 | tf_op jit(solution)/shard_map/ppermute | solution.py:39
  49.9 0.0 collective-permute-start.17
  49.9 1.5 %query_grad.1 = (bf16[128,512]{1,0:T(8,128)(2,1)}, bf16[128,512]{1,0:T(8,128)(2,1)}, bf16[128,512]{1,0:T(8,128)(2,1)}) custom-call(bf16[128,512]{1,0:T(8,128)(2,1)S(1)} %get-tuple-element.55.q.refs_0_, bf16[256,512]{1,0:T(8,128)(2,1)S(1)} %pad_add_fusion.1.own, bf16[256,512]{1,0:T(8,128)(2,1)S(1)} %collective-permute-done.2.near, ...), custom_call_target="tpu_custom_call" | custom-call | bytes 6642000 | tf_op jit(solution)/shard_map/query_grad/pallas_call | solution.py:74
  51.4 0.0 collective-permute-done.18.refs_6_
  51.4 0.0 collective-permute-done.19.refs_7_
  51.5 0.9 %key_part.1 = (f32[128,512]{1,0:T(8,128)S(1)}, f32[128,512]{1,0:T(8,128)S(1)}, f32[128,512]{1,0:T(8,128)S(1)}) custom-call(bf16[256,512]{1,0:T(8,128)(2,1)S(1)} %pad_add_fusion.1.own, bf16[128,512]{1,0:T(8,128)(2,1)S(1)} %get-tuple-element.55.q.refs_0_, bf16[128,512]{1,0:T(8,128)(2,1)S(1)} %collective-permute-done.13.seen_b.refs_1_, ...), custom_call_target="tpu_custom_call" | custom-call | bytes 5535000 | tf_op jit(solution)/shard_map/key_part/pallas_call | solution.py:74
  52.3 3.0 %collective-permute-done.17.message = bf16[144,512]{1,0:T(8,128)(2,1)S(1)} collective-permute-done((bf16[144,512]{1,0:T(8,128)(2,1)S(1)}, bf16[144,512]{1,0:T(8,128)(2,1)S(1)}, u32[]{:S(2)}, u32[]{:S(2)}) %collective-permute-start.17) | collective-permute-done | bytes 147488 | tf_op jit(solution)/shard_map/ppermute | solution.py:28
  55.3 1.0 %key_grad.1 = (bf16[128,512]{1,0:T(8,128)(2,1)}, bf16[128,512]{1,0:T(8,128)(2,1)}) custom-call(bf16[256,512]{1,0:T(8,128)(2,1)S(1)} %pad_add_fusion.1.own, bf16[128,512]{1,0:T(8,128)(2,1)S(1)} %collective-permute-done.14.seen_c.refs_4_.query, bf16[144,512]{1,0:T(8,128)(2,1)S(1)} %collective-permute-done.17.message, f32[128,512]{1,0:T(8,128)S(1)} %get-tuple-element.72.late, ...), custom_call_target="tpu_custom_call" | custom-call | bytes 3690000 | tf_op jit(solution)/shard_map/key_grad/pallas_call | solution.py:74
  (3 shorter events, 0.1 us)
Async XLA Ops:
  0.6 19.9 %copy-start = (bf16[512,2048]{1,0:T(8,128)(2,1)S(1)}, bf16[512,2048]{1,0:T(8,128)(2,1)}, u32[]{:S(2)}) copy-start(bf16[512,2048]{1,0:T(8,128)(2,1)} %weight.5) | copy-start | bytes 6291460
  1.8 9.4 %collective-permute-start = (bf16[256,512]{1,0:T(8,128)(2,1)S(1)}, bf16[256,512]{1,0:T(8,128)(2,1)S(1)}, u32[]{:S(2)}, u32[]{:S(2)}) collective-permute-start(bf16[256,512]{1,0:T(8,128)(2,1)S(1)} %pad_add_fusion.1.own), channel_id=1, source_target_pairs={{8,0},{16,8},{24,16},{28,24},{20,28},{12,20},{4,12},{0,4},{9,1},{1... | collective-permute-start | bytes 786440 | tf_op jit(solution)/shard_map/ppermute | solution.py:39
  4.8 11.3 %collective-permute-start.2 = (bf16[256,512]{1,0:T(8,128)(2,1)S(1)}, bf16[256,512]{1,0:T(8,128)(2,1)S(1)}, u32[]{:S(2)}, u32[]{:S(2)}) collective-permute-start(bf16[256,512]{1,0:T(8,128)(2,1)S(1)} %pad_add_fusion.1.own), channel_id=1, source_target_pairs={{0,1},{1,0},{2,3},{3,2},{4,5},{5,4},{6,7},{7,6},{8,12},{9,13},{10,... | collective-permute-start | bytes 786440 | tf_op jit(solution)/shard_map/ppermute | solution.py:50
  4.8 11.6 %collective-permute-start.3 = (bf16[256,512]{1,0:T(8,128)(2,1)S(1)}, bf16[256,512]{1,0:T(8,128)(2,1)S(1)}, u32[]{:S(2)}, u32[]{:S(2)}) collective-permute-start(bf16[256,512]{1,0:T(8,128)(2,1)S(1)} %pad_add_fusion.1.own), channel_id=1, source_target_pairs={{0,8},{8,16},{16,24},{24,28},{28,20},{20,12},{12,4},{4,0},{1,9},{9... | collective-permute-start | bytes 786440 | tf_op jit(solution)/shard_map/ppermute | solution.py:39
  11.2 9.3 %collective-permute-start.1 = (bf16[256,512]{1,0:T(8,128)(2,1)S(1)}, bf16[256,512]{1,0:T(8,128)(2,1)S(1)}, u32[]{:S(2)}, u32[]{:S(2)}) collective-permute-start(bf16[256,512]{1,0:T(8,128)(2,1)S(1)} %collective-permute-done.seen.second), channel_id=1, source_target_pairs={{0,4},{4,0},{8,12},{12,8},{16,20},{20,16},{24,28},{28,24},{1,5},{5... | collective-permute-start | bytes 786440 | tf_op jit(solution)/shard_map/ppermute | solution.py:28
  12.8 7.7 %collective-permute-start.4 = (bf16[128,512]{1,0:T(8,128)(2,1)}, bf16[128,512]{1,0:T(8,128)(2,1)S(1)}, u32[]{:S(2)}, u32[]{:S(2)}) collective-permute-start(bf16[128,512]{1,0:T(8,128)(2,1)} %param.13), channel_id=1, source_target_pairs={{0,2},{1,3},{2,0},{3,1},{4,6},{5,7},{6,4},{7,5},{8,10},{9,11},{10,... | collective-permute-start | bytes 393224 | tf_op jit(solution)/shard_map/ppermute | solution.py:28
  15.4 6.0 %collective-permute-start.6 = (bf16[128,512]{1,0:T(8,128)(2,1)S(1)}, bf16[128,512]{1,0:T(8,128)(2,1)S(1)}, u32[]{:S(2)}, u32[]{:S(2)}) collective-permute-start(bf16[128,512]{1,0:T(8,128)(2,1)S(1)} %get-tuple-element.41.q), channel_id=1, source_target_pairs={{8,0},{16,8},{24,16},{28,24},{20,28},{12,20},{4,12},{0,4},{9,1},{1... | collective-permute-start | bytes 393224 | tf_op jit(solution)/shard_map/ppermute | solution.py:39
  16.0 4.5 %collective-permute-start.5 = (f32[31,512]{1,0:T(8,128)}, f32[31,512]{1,0:T(8,128)S(1)}, u32[]{:S(2)}, u32[]{:S(2)}) collective-permute-start(f32[31,512]{1,0:T(8,128)} %taps.3), channel_id=1, source_target_pairs={{0,2},{1,3},{2,0},{3,1},{4,6},{5,7},{6,4},{7,5},{8,10},{9,11},{10,... | collective-permute-start | bytes 190472 | tf_op jit(solution)/shard_map/ppermute | solution.py:28
  20.5 13.5 %copy-start.1 = (f32[31,512]{1,0:T(8,128)S(1)}, f32[31,512]{1,0:T(8,128)}, u32[]{:S(2)}) copy-start(f32[31,512]{1,0:T(8,128)} %taps.3) | copy-start | bytes 190468
  21.4 1.6 %collective-permute-start.7 = (bf16[128,1024]{1,0:T(8,128)(2,1)S(1)}, bf16[128,1024]{1,0:T(8,128)(2,1)S(1)}, u32[]{:S(2)}, u32[]{:S(2)}) collective-permute-start(bf16[128,1024]{1,0:T(8,128)(2,1)S(1)} %get-tuple-element.47), channel_id=1, source_target_pairs={{0,1},{1,0},{2,3},{3,2},{4,5},{5,4},{6,7},{7,6},{8,9},{9,8},{10,11... | collective-permute-start | bytes 786440 | tf_op jit(solution)/shard_map/ppermute | solution.py:28
  23.2 10.9 %collective-permute-start.11 = (bf16[128,1024]{1,0:T(8,128)(2,1)S(1)}, bf16[128,1024]{1,0:T(8,128)(2,1)S(1)}, u32[]{:S(2)}, u32[]{:S(2)}) collective-permute-start(bf16[128,1024]{1,0:T(8,128)(2,1)S(1)} %get-tuple-element.57.chip), channel_id=1, source_target_pairs={{0,2},{1,3},{2,0},{3,1},{4,6},{5,7},{6,4},{7,5},{8,10},{9,11},{10,... | collective-permute-start | bytes 786440 | tf_op jit(solution)/shard_map/ppermute | solution.py:28
  23.6 6.7 %collective-permute-start.8 = (bf16[48,1024]{1,0:T(8,128)(2,1)S(1)}, bf16[48,1024]{1,0:T(8,128)(2,1)S(1)}, u32[]{:S(2)}, u32[]{:S(2)}) collective-permute-start(bf16[48,1024]{1,0:T(8,128)(2,1)S(1)} %get-tuple-element.51), channel_id=1, source_target_pairs={{0,4},{4,0},{8,12},{12,8},{16,20},{20,16},{24,28},{28,24},{1,5},{5... | collective-permute-start | bytes 294920 | tf_op jit(solution)/shard_map/ppermute | solution.py:28
  26.1 4.2 %collective-permute-start.9 = (bf16[48,1024]{1,0:T(8,128)(2,1)S(1)}, bf16[48,1024]{1,0:T(8,128)(2,1)S(1)}, u32[]{:S(2)}, u32[]{:S(2)}) collective-permute-start(bf16[48,1024]{1,0:T(8,128)(2,1)S(1)} %get-tuple-element.52), channel_id=1, source_target_pairs={{0,1},{1,0},{2,3},{3,2},{4,8},{5,9},{6,10},{7,11},{8,4},{9,5},{10,... | collective-permute-start | bytes 294920 | tf_op jit(solution)/shard_map/ppermute | solution.py:50
  30.3 6.8 %collective-permute-start.10 = (bf16[64,1024]{1,0:T(8,128)(2,1)S(1)}, bf16[64,1024]{1,0:T(8,128)(2,1)S(1)}, u32[]{:S(2)}, u32[]{:S(2)}) collective-permute-start(bf16[64,1024]{1,0:T(8,128)(2,1)S(1)} %get-tuple-element.56.ends), channel_id=1, source_target_pairs={{0,2},{1,3},{2,0},{3,1},{4,6},{5,7},{6,4},{7,5},{8,10},{9,11},{10,... | collective-permute-start | bytes 393224 | tf_op jit(solution)/shard_map/ppermute | solution.py:28
  31.1 6.1 %collective-permute-start.12 = (bf16[128,512]{1,0:T(8,128)(2,1)S(1)}, bf16[128,512]{1,0:T(8,128)(2,1)S(1)}, u32[]{:S(2)}, u32[]{:S(2)}) collective-permute-start(bf16[128,512]{1,0:T(8,128)(2,1)S(1)} %get-tuple-element.55.q.refs_0_), channel_id=1, source_target_pairs={{0,8},{8,16},{16,24},{24,28},{28,20},{20,12},{12,4},{4,0},{1,9},{9... | collective-permute-start | bytes 393224 | tf_op jit(solution)/shard_map/ppermute | solution.py:39
  34.0 3.2 %collective-permute-start.13 = (bf16[128,512]{1,0:T(8,128)(2,1)S(1)}, bf16[128,512]{1,0:T(8,128)(2,1)S(1)}, u32[]{:S(2)}, u32[]{:S(2)}) collective-permute-start(bf16[128,512]{1,0:T(8,128)(2,1)S(1)} %get-tuple-element.55.q.refs_0_), channel_id=1, source_target_pairs={{0,1},{1,0},{2,3},{3,2},{4,5},{5,4},{6,7},{7,6},{8,12},{9,13},{10,... | collective-permute-start | bytes 393224 | tf_op jit(solution)/shard_map/ppermute | solution.py:50
  34.0 5.9 %collective-permute-start.14 = (bf16[128,512]{1,0:T(8,128)(2,1)S(1)}, bf16[128,512]{1,0:T(8,128)(2,1)S(1)}, u32[]{:S(2)}, u32[]{:S(2)}) collective-permute-start(bf16[128,512]{1,0:T(8,128)(2,1)S(1)} %get-tuple-element.62), channel_id=1, source_target_pairs={{0,4},{4,0},{8,12},{12,8},{16,20},{20,16},{24,28},{28,24},{1,5},{5... | collective-permute-start | bytes 393224 | tf_op jit(solution)/shard_map/ppermute | solution.py:28
  41.4 1.6 %collective-permute-start.15 = (bf16[128,1024]{1,0:T(8,128)(2,1)S(1)}, bf16[128,1024]{1,0:T(8,128)(2,1)S(1)}, u32[]{:S(2)}, u32[]{:S(2)}) collective-permute-start(bf16[128,1024]{1,0:T(8,128)(2,1)S(1)} %get-tuple-element.63.own.grad_here), channel_id=1, source_target_pairs={{0,1},{1,0},{2,3},{3,2},{4,5},{5,4},{6,7},{7,6},{8,9},{9,8},{10,11... | collective-permute-start | bytes 786440 | tf_op jit(solution)/shard_map/ppermute | solution.py:28
  43.7 6.2 %collective-permute-start.16 = (bf16[144,512]{1,0:T(8,128)(2,1)S(1)}, bf16[144,512]{1,0:T(8,128)(2,1)S(1)}, u32[]{:S(2)}, u32[]{:S(2)}) collective-permute-start(bf16[144,512]{1,0:T(8,128)(2,1)S(1)} %get-tuple-element.66.message.refs_5_), channel_id=1, source_target_pairs={{8,0},{16,8},{24,16},{28,24},{20,28},{12,20},{4,12},{0,4},{9,1},{1... | collective-permute-start | bytes 442376 | tf_op jit(solution)/shard_map/ppermute | solution.py:39
  44.0 7.4 %collective-permute-start.18 = (bf16[144,512]{1,0:T(8,128)(2,1)S(1)}, bf16[144,512]{1,0:T(8,128)(2,1)S(1)}, u32[]{:S(2)}, u32[]{:S(2)}) collective-permute-start(bf16[144,512]{1,0:T(8,128)(2,1)S(1)} %get-tuple-element.66.message.refs_5_), channel_id=1, source_target_pairs={{0,1},{1,0},{2,3},{3,2},{4,5},{5,4},{6,7},{7,6},{8,12},{9,13},{10,... | collective-permute-start | bytes 442376 | tf_op jit(solution)/shard_map/ppermute | solution.py:50
  44.0 7.4 %collective-permute-start.19 = (bf16[144,512]{1,0:T(8,128)(2,1)S(1)}, bf16[144,512]{1,0:T(8,128)(2,1)S(1)}, u32[]{:S(2)}, u32[]{:S(2)}) collective-permute-start(bf16[144,512]{1,0:T(8,128)(2,1)S(1)} %get-tuple-element.66.message.refs_5_), channel_id=1, source_target_pairs={{0,8},{8,16},{16,24},{24,28},{28,20},{20,12},{12,4},{4,0},{1,9},{9... | collective-permute-start | bytes 442376 | tf_op jit(solution)/shard_map/ppermute | solution.py:39
  49.9 5.4 %collective-permute-start.17 = (bf16[144,512]{1,0:T(8,128)(2,1)S(1)}, bf16[144,512]{1,0:T(8,128)(2,1)S(1)}, u32[]{:S(2)}, u32[]{:S(2)}) collective-permute-start(bf16[144,512]{1,0:T(8,128)(2,1)S(1)} %collective-permute-done.16.refs_8_), channel_id=1, source_target_pairs={{0,4},{4,0},{8,12},{12,8},{16,20},{20,16},{24,28},{28,24},{1,5},{5... | collective-permute-start | bytes 442376 | tf_op jit(solution)/shard_map/ppermute | solution.py:28

commit v11 on v10

--- a/solution.py
+++ b/solution.py
@@ -184,7 +184,7 @@
         totals[:, c] = s[:, HDIM:]
 
 
-def project_body(scale, q, relay, sums, tops, totals, weight, seen_a, seen_b, att, lse, send, keep):
+def project_body(scale, q, relay, sums, tops, totals, weight, att, lse, send, keep):
     frames, width = q.shape
     heads = columns(width)
     bias = bias_of(far_there())
@@ -207,7 +207,7 @@
         lse[:, c] = part
 
 
-def pass_body(send, q_second, send_copy, second_copy):
+def pass_body(send, q_second, seen_a, seen_b, send_copy, second_copy):
     send_copy[...] = send[...]
     second_copy[...] = q_second[...]
 
@@ -233,12 +233,10 @@
     second_copy[...] = q_second[...]
 
 
-def stack_body(rim_near, rim_far, q, q_second, ends, q_copy, second_copy):
+def stack_body(rim_near, rim_far, ends):
     wide = 2 * HALO
     ends[0:wide, :] = rim_near[0:wide, :]
     ends[wide : 2 * wide, :] = rim_far[0:wide, :]
-    q_copy[...] = q[...]
-    second_copy[...] = q_second[...]
 
 
 def summed(share, across, rows, cols, width):
@@ -286,7 +284,7 @@
 
 
 def conv_inner_body(
-    chip, across, cot, cot_other, taps, taps_other, rows_out, edge_rows, edge_conv, part_grad
+    chip, across, cot, cot_other, taps, taps_other, seen_a, seen_b, rows_out, edge_rows, edge_conv, part_grad
 ):
     frames, width = cot.shape
     wide, count = 2 * HALO, taps.shape[0]
@@ -313,7 +311,7 @@
 
 def conv_edge_body(
     ends, ends_across, rim_near, rim_far, cot, cot_other, taps, taps_other,
-    rows_in, edge_rows, edge_conv, part_grad, seen_a, seen_b, seen_c, output, grad_input,
+    rows_in, edge_rows, edge_conv, part_grad, seen, output, grad_input,
 ):
     frames, width = cot.shape
     wide, count = 2 * HALO, taps.shape[0]
@@ -488,11 +486,11 @@
     att, lse, send, keep = kernel_call(
         functools.partial(project_body, scale),
         (tile, tile32, both, both),
-        (query, relay, sums, tops, totals, out_weight, cot_other, taps_other),
-        1.0, "project", 2,
-    )
-
-    send, q_second = kernel_call(pass_body, (both, tile), (send, q_second), 0.1, "pass")
+        (query, relay, sums, tops, totals, out_weight),
+        1.0, "project",
+    )
+
+    send, q_second = kernel_call(pass_body, (both, tile), (send, q_second, cot_other, taps_other), 0.1, "pass", 2)
     core = pair_swap(send, "mp", 1)
     chip, rim_up, rim_down, q_own, q_handed = kernel_call(
         join_body,
@@ -503,11 +501,8 @@
     across = pair_swap(chip, "mp", 2)
     rim_far = outer_swap(rim_down)
     rim_near = pair_swap(rim_up, "ctx", 1)
-    ends, q_own, q_handed = kernel_call(
-        stack_body,
-        (shaped((2 * wide, 2 * width), BF16), tile, tile),
-        (rim_near, rim_far, q_own, q_handed),
-        0.1, "stack",
+    (ends,) = kernel_call(
+        stack_body, (shaped((2 * wide, 2 * width), BF16),), (rim_near, rim_far), 0.1, "stack"
     )
     ends_across = pair_swap(ends, "mp", 2)
     q_first = ring(q_own, 0)
@@ -521,15 +516,15 @@
             shaped((2 * wide, 2 * width), F32),
             shaped((frames, 2 * width), F32),
         ),
-        (chip, across, cotangent, cot_other, kernel, taps_other),
-        3.1, "conv_inner",
+        (chip, across, cotangent, cot_other, kernel, taps_other, q_first, q_near),
+        3.1, "conv_inner", 2,
     )
     output_here, grad_here = kernel_call(
         conv_edge_body,
         (tile, both),
         (ends, ends_across, rim_near, rim_far, cotangent, cot_other, kernel, taps_other)
-        + (rows_out, edge_rows, edge_conv, part_grad, q_first, q_near, q_relay),
-        1.4, "conv_edge", 3,
+        + (rows_out, edge_rows, edge_conv, part_grad, q_relay),
+        1.4, "conv_edge", 1,
     )
 
     gi_core = pair_swap(grad_here, "mp", 1)

time: 56.4 us -> 53.8 us (0.954)
  waiting for transfers between devices: 21.2 us -> 17.9 us
  starting transfers between devices: 21.2 us -> 22 us
    ppermute x10, waiting for transfers between devices: 15.9 us -> 11.6 us  [pair_swap(): lax.ppermute(block, axis, [(i, i ^ bit) for i in range(lax.axis_size(axis...]
    ppermute x10, starting transfers between devices: 7.41 us -> 10.9 us  [pair_swap(): lax.ppermute(block, axis, [(i, i ^ bit) for i in range(lax.axis_size(axis...]
    ppermute x6, starting transfers between devices: 13.8 us -> 10.9 us  [ring(): return lax.ppermute(block, 'ctx', ring_routes(lax.axis_size('ctx'))[way])]
    ppermute x6, waiting for transfers between devices: 5.28 us -> 6.24 us  [ring(): return lax.ppermute(block, 'ctx', ring_routes(lax.axis_size('ctx'))[way])]
  transfers between devices with their start and end apart: 20 -> 20, of which waited for: 8 -> 9; matrix products, arithmetic and copies ran while one was open for 2% -> 2% of each run, Pallas kernels for 13% -> 14%
where the time goes in v11:
time: 53.8 us; the launch traced here: 53.7 us
  starting transfers between devices  22 us (41%)
  waiting for transfers between devices  17.9 us (33%)
  Pallas kernels  10.8 us (20%)
  other arithmetic  2.19 us (4%)
  between operations  0.8 us (1%)
    ppermute x10, waiting for transfers between devices, pair_swap(): lax.ppermute(block, axis, [(i, i ^ bit) for i in range(lax.axis_size(axis...  11.6 us
    ppermute x6, starting transfers between devices, ring(): return lax.ppermute(block, 'ctx', ring_routes(lax.axis_size('ctx'))[way])  10.9 us
    ppermute x10, starting transfers between devices, pair_swap(): lax.ppermute(block, axis, [(i, i ^ bit) for i in range(lax.axis_size(axis...  10.9 us
    pallas_call x13, Pallas kernels, kernel_call(): pl.pallas_call(body, out_shape=outs, in_specs=[VMEM] * (len(args) - unrea...  10.8 us
    ppermute x6, waiting for transfers between devices, ring(): return lax.ppermute(block, 'ctx', ring_routes(lax.axis_size('ctx'))[way])  6.24 us
    add x1, other arithmetic, per_device(): lax.pad(key_rows, zero, ((0, frames, 0), (0, 0, 0)))  1.13 us
  transfers between devices with their start and end apart: 20, of which 9 were waited for; matrix products, arithmetic and copies ran while one was open for 2% of the time, Pallas kernels for 14%

profile of v11, /device:TPU:0, one launch (start us, length us, event | category | flops | bytes accessed | tf_op | source)
XLA Modules:
  0.0 53.7 jit_solution(8051305732199711457)
XLA Ops:
  0.6 0.0 copy-start
  0.6 1.1 %pad_add_fusion.1.own = bf16[256,512]{1,0:T(8,128)(2,1)S(1)} fusion(bf16[128,512]{1,0:T(8,128)(2,1)} %param.9, bf16[128,512]{1,0:T(8,128)(2,1)} %param.8), kind=kLoop, calls=%fused_computation.1 | loop fusion | flops 524288 | bytes 524288 | tf_op jit(solution)/shard_map/add | solution.py:466
  1.8 3.0 %collective-permute-start = (bf16[256,512]{1,0:T(8,128)(2,1)S(1)}, bf16[256,512]{1,0:T(8,128)(2,1)S(1)}, u32[]{:S(2)}, u32[]{:S(2)}) collective-permute-start(bf16[256,512]{1,0:T(8,128)(2,1)S(1)} %pad_add_fusion.1.own), channel_id=1, source_target_pairs={{8,0},{16,8},{24,16},{28,24},{20,28},{12,20},{4,12},{0,4},{9,1},{1... | collective-permute-start | bytes 786440 | tf_op jit(solution)/shard_map/ppermute | solution.py:39
  4.8 0.0 collective-permute-start.2
  4.8 3.2 %collective-permute-start.3 = (bf16[256,512]{1,0:T(8,128)(2,1)S(1)}, bf16[256,512]{1,0:T(8,128)(2,1)S(1)}, u32[]{:S(2)}, u32[]{:S(2)}) collective-permute-start(bf16[256,512]{1,0:T(8,128)(2,1)S(1)} %pad_add_fusion.1.own), channel_id=1, source_target_pairs={{0,8},{8,16},{16,24},{24,28},{28,20},{20,12},{12,4},{4,0},{1,9},{9... | collective-permute-start | bytes 786440 | tf_op jit(solution)/shard_map/ppermute | solution.py:39
  7.9 3.2 %collective-permute-done.seen.second = bf16[256,512]{1,0:T(8,128)(2,1)S(1)} collective-permute-done((bf16[256,512]{1,0:T(8,128)(2,1)S(1)}, bf16[256,512]{1,0:T(8,128)(2,1)S(1)}, u32[]{:S(2)}, u32[]{:S(2)}) %collective-permute-start) | collective-permute-done | bytes 262176 | tf_op jit(solution)/shard_map/ppermute | solution.py:39
  11.2 1.7 %collective-permute-start.1 = (bf16[256,512]{1,0:T(8,128)(2,1)S(1)}, bf16[256,512]{1,0:T(8,128)(2,1)S(1)}, u32[]{:S(2)}, u32[]{:S(2)}) collective-permute-start(bf16[256,512]{1,0:T(8,128)(2,1)S(1)} %collective-permute-done.seen.second), channel_id=1, source_target_pairs={{0,4},{4,0},{8,12},{12,8},{16,20},{20,16},{24,28},{28,24},{1,5},{5... | collective-permute-start | bytes 786440 | tf_op jit(solution)/shard_map/ppermute | solution.py:28
  12.8 1.5 %collective-permute-start.5 = (bf16[128,512]{1,0:T(8,128)(2,1)}, bf16[128,512]{1,0:T(8,128)(2,1)S(1)}, u32[]{:S(2)}, u32[]{:S(2)}) collective-permute-start(bf16[128,512]{1,0:T(8,128)(2,1)} %param.13), channel_id=1, source_target_pairs={{0,2},{1,3},{2,0},{3,1},{4,6},{5,7},{6,4},{7,5},{8,10},{9,11},{10,... | collective-permute-start | bytes 393224 | tf_op jit(solution)/shard_map/ppermute | solution.py:28
  14.3 1.1 %pad_add_fusion.joined = bf16[384,512]{1,0:T(8,128)(2,1)S(1)} fusion(bf16[128,512]{1,0:T(8,128)(2,1)} %param.13, bf16[128,512]{1,0:T(8,128)(2,1)} %param.10, bf16[128,512]{1,0:T(8,128)(2,1)} %param.7), kind=kLoop, calls=%fused_computation | loop fusion | flops 1179648 | bytes 786432 | tf_op jit(solution)/shard_map/add | solution.py:472
  15.4 0.6 %collective-permute-start.4 = (bf16[128,512]{1,0:T(8,128)(2,1)S(1)}, bf16[128,512]{1,0:T(8,128)(2,1)S(1)}, u32[]{:S(2)}, u32[]{:S(2)}) collective-permute-start(bf16[128,512]{1,0:T(8,128)(2,1)S(1)} %get-tuple-element.38.q), channel_id=1, source_target_pairs={{8,0},{16,8},{24,16},{28,24},{20,28},{12,20},{4,12},{0,4},{9,1},{1... | collective-permute-start | bytes 393224 | tf_op jit(solution)/shard_map/ppermute | solution.py:39
  16.0 0.0 collective-permute-done.2.near
  16.0 0.3 collective-permute-start.6
  16.4 0.0 collective-permute-done.3.first
  16.4 0.6 %forward.1 = (f32[128,512]{1,0:T(8,128)S(1)}, f32[128,512]{1,0:T(8,128)S(1)}, f32[128,512]{1,0:T(8,128)S(1)}) custom-call(bf16[128,512]{1,0:T(8,128)(2,1)S(1)} %get-tuple-element.38.q, bf16[256,512]{1,0:T(8,128)(2,1)S(1)} %pad_add_fusion.1.own, bf16[256,512]{1,0:T(8,128)(2,1)S(1)} %collective-permute-done.2.near, ...), custom_call_target="tpu_custom_call" | custom-call | bytes 3690000 | tf_op jit(solution)/shard_map/forward/pallas_call | solution.py:74
  17.0 2.1 %collective-permute-done.1.relay = bf16[256,512]{1,0:T(8,128)(2,1)S(1)} collective-permute-done((bf16[256,512]{1,0:T(8,128)(2,1)S(1)}, bf16[256,512]{1,0:T(8,128)(2,1)S(1)}, u32[]{:S(2)}, u32[]{:S(2)}) %collective-permute-start.1) | collective-permute-done | bytes 262176 | tf_op jit(solution)/shard_map/ppermute | solution.py:28
  19.1 0.0 copy-done
  19.1 0.0 copy-start.1
  19.1 0.8 %project.1 = (bf16[128,512]{1,0:T(8,128)(2,1)S(1)}, f32[128,512]{1,0:T(8,128)S(1)}, bf16[128,1024]{1,0:T(8,128)(2,1)S(1)}, bf16[128,1024]{1,0:T(8,128)(2,1)S(1)}) custom-call(bf16[128,512]{1,0:T(8,128)(2,1)S(1)} %get-tuple-element.38.q, bf16[256,512]{1,0:T(8,128)(2,1)S(1)} %collective-permute-done.1.relay, f32[128,512]{1,0:T(8,128)S(1)} %get-tuple-element.39.sums, ...), custom_call_target="tpu_custom_call" | custom-call | bytes 3690000 | tf_op jit(solution)/shard_map/project/pallas_call | solution.py:74
  20.0 0.5 collective-permute-done.6.seen_b.taps_other
  20.5 0.0 collective-permute-done.5.seen_a.cot_other
  20.5 0.0 collective-permute-done.4.q_second
  20.5 0.1 collective-permute-start.7
  20.6 1.5 %collective-permute-done.7.core = bf16[128,1024]{1,0:T(8,128)(2,1)S(1)} collective-permute-done((bf16[128,1024]{1,0:T(8,128)(2,1)S(1)}, bf16[128,1024]{1,0:T(8,128)(2,1)S(1)}, u32[]{:S(2)}, u32[]{:S(2)}) %collective-permute-start.7) | collective-permute-done | bytes 262176 | tf_op jit(solution)/shard_map/ppermute | solution.py:28
  22.1 0.1 join.1
  22.3 1.4 %collective-permute-start.11 = (bf16[128,1024]{1,0:T(8,128)(2,1)S(1)}, bf16[128,1024]{1,0:T(8,128)(2,1)S(1)}, u32[]{:S(2)}, u32[]{:S(2)}) collective-permute-start(bf16[128,1024]{1,0:T(8,128)(2,1)S(1)} %get-tuple-element.51.chip), channel_id=1, source_target_pairs={{0,2},{1,3},{2,0},{3,1},{4,6},{5,7},{6,4},{7,5},{8,10},{9,11},{10,... | collective-permute-start | bytes 786440 | tf_op jit(solution)/shard_map/ppermute | solution.py:28
  23.6 2.5 %collective-permute-start.8 = (bf16[48,1024]{1,0:T(8,128)(2,1)S(1)}, bf16[48,1024]{1,0:T(8,128)(2,1)S(1)}, u32[]{:S(2)}, u32[]{:S(2)}) collective-permute-start(bf16[48,1024]{1,0:T(8,128)(2,1)S(1)} %get-tuple-element.49), channel_id=1, source_target_pairs={{0,4},{4,0},{8,12},{12,8},{16,20},{20,16},{24,28},{28,24},{1,5},{5... | collective-permute-start | bytes 294920 | tf_op jit(solution)/shard_map/ppermute | solution.py:28
  26.1 0.0 collective-permute-start.9
  26.1 1.5 %collective-permute-start.12 = (bf16[128,512]{1,0:T(8,128)(2,1)S(1)}, bf16[128,512]{1,0:T(8,128)(2,1)S(1)}, u32[]{:S(2)}, u32[]{:S(2)}) collective-permute-start(bf16[128,512]{1,0:T(8,128)(2,1)S(1)} %get-tuple-element.48.q.refs_0_), channel_id=1, source_target_pairs={{0,8},{8,16},{16,24},{24,28},{28,20},{20,12},{12,4},{4,0},{1,9},{9... | collective-permute-start | bytes 393224 | tf_op jit(solution)/shard_map/ppermute | solution.py:39
  27.6 0.0 collective-permute-start.13
  27.6 2.7 %collective-permute-done.8.rim_near = bf16[48,1024]{1,0:T(8,128)(2,1)S(1)} collective-permute-done((bf16[48,1024]{1,0:T(8,128)(2,1)S(1)}, bf16[48,1024]{1,0:T(8,128)(2,1)S(1)}, u32[]{:S(2)}, u32[]{:S(2)}) %collective-permute-start.8) | collective-permute-done | bytes 98336 | tf_op jit(solution)/shard_map/ppermute | solution.py:28
  30.3 2.5 %collective-permute-start.14 = (bf16[128,512]{1,0:T(8,128)(2,1)S(1)}, bf16[128,512]{1,0:T(8,128)(2,1)S(1)}, u32[]{:S(2)}, u32[]{:S(2)}) collective-permute-start(bf16[128,512]{1,0:T(8,128)(2,1)S(1)} %get-tuple-element.56), channel_id=1, source_target_pairs={{0,4},{4,0},{8,12},{12,8},{16,20},{20,16},{24,28},{28,24},{1,5},{5... | collective-permute-start | bytes 393224 | tf_op jit(solution)/shard_map/ppermute | solution.py:28
  32.8 0.0 collective-permute-done.9.rim_far
  32.8 0.6 %collective-permute-start.10 = (bf16[64,1024]{1,0:T(8,128)(2,1)S(1)}, bf16[64,1024]{1,0:T(8,128)(2,1)S(1)}, u32[]{:S(2)}, u32[]{:S(2)}) collective-permute-start(bf16[64,1024]{1,0:T(8,128)(2,1)S(1)} %stack.1.ends), channel_id=1, source_target_pairs={{0,2},{1,3},{2,0},{3,1},{4,6},{5,7},{6,4},{7,5},{8,10},{9,11},{10,... | collective-permute-start | bytes 393224 | tf_op jit(solution)/shard_map/ppermute | solution.py:28
  33.4 0.0 collective-permute-done.12.seen_a.refs_2_
  33.4 0.0 collective-permute-done.13.seen_b.refs_1_
  33.4 0.0 collective-permute-done.11.across
  33.4 0.0 copy-done.1
  33.4 3.2 %conv_inner.1 = (bf16[128,512]{1,0:T(8,128)(2,1)S(1)}, f32[32,512]{1,0:T(8,128)S(1)}, f32[64,1024]{1,0:T(8,128)S(1)}, f32[128,1024]{1,0:T(8,128)S(1)}) custom-call(bf16[128,1024]{1,0:T(8,128)(2,1)S(1)} %get-tuple-element.51.chip, bf16[128,1024]{1,0:T(8,128)(2,1)S(1)} %collective-permute-done.11.across, bf16[128,512]{1,0:T(8,128)(2,1)S(1)} %get-tuple-element.46.cot, ...), custom_call_target="tpu_custom_call" | custom-call | bytes 11439000 | tf_op jit(solution)/shard_map/conv_inner/pallas_call | solution.py:74
  36.6 0.0 collective-permute-done.14.seen.refs_4_.query
  36.6 1.3 %collective-permute-done.10.ends_across = bf16[64,1024]{1,0:T(8,128)(2,1)S(1)} collective-permute-done((bf16[64,1024]{1,0:T(8,128)(2,1)S(1)}, bf16[64,1024]{1,0:T(8,128)(2,1)S(1)}, u32[]{:S(2)}, u32[]{:S(2)}) %collective-permute-start.10) | collective-permute-done | bytes 131104 | tf_op jit(solution)/shard_map/ppermute | solution.py:28
  37.8 1.5 %conv_edge.1 = (bf16[128,512]{1,0:T(8,128)(2,1)S(1)}, bf16[128,1024]{1,0:T(8,128)(2,1)S(1)}) custom-call(bf16[64,1024]{1,0:T(8,128)(2,1)S(1)} %stack.1.ends, bf16[64,1024]{1,0:T(8,128)(2,1)S(1)} %collective-permute-done.10.ends_across, bf16[48,1024]{1,0:T(8,128)(2,1)S(1)} %collective-permute-done.8.rim_near, ...), custom_call_target="tpu_custom_call" | custom-call | bytes 5166000 | tf_op jit(solution)/shard_map/conv_edge/pallas_call | solution.py:74
  39.3 0.1 collective-permute-start.15
  39.4 0.5 upstream_own.1.partial
  39.9 1.0 %collective-permute-done.15.core = bf16[128,1024]{1,0:T(8,128)(2,1)S(1)} collective-permute-done((bf16[128,1024]{1,0:T(8,128)(2,1)S(1)}, bf16[128,1024]{1,0:T(8,128)(2,1)S(1)}, u32[]{:S(2)}, u32[]{:S(2)}) %collective-permute-start.15) | collective-permute-done | bytes 262176 | tf_op jit(solution)/shard_map/ppermute | solution.py:28
  40.9 0.7 %upstream.1 = (bf16[144,512]{1,0:T(8,128)(2,1)S(1)}, f32[128,512]{1,0:T(8,128)S(1)}) custom-call(bf16[128,1024]{1,0:T(8,128)(2,1)S(1)} %collective-permute-done.15.core, bf16[512,2048]{1,0:T(8,128)(2,1)S(1)} %copy-done, bf16[128,512]{1,0:T(8,128)(2,1)S(1)} %get-tuple-element.58.att, f32[128,512]{1,0:T(8,128)S(1)} %get-tuple-element.59.lse, ...), custom_call_target="tpu_custom_call" | custom-call | bytes 2214000 | tf_op jit(solution)/shard_map/upstream/pallas_call | solution.py:74
  41.6 0.1 collective-permute-start.16
  41.6 0.2 collective-permute-start.18
  41.8 2.7 %collective-permute-start.19 = (bf16[144,512]{1,0:T(8,128)(2,1)S(1)}, bf16[144,512]{1,0:T(8,128)(2,1)S(1)}, u32[]{:S(2)}, u32[]{:S(2)}) collective-permute-start(bf16[144,512]{1,0:T(8,128)(2,1)S(1)} %get-tuple-element.60.message.refs_5_), channel_id=1, source_target_pairs={{0,8},{8,16},{16,24},{24,28},{28,20},{20,12},{12,4},{4,0},{1,9},{9... | collective-permute-start | bytes 442376 | tf_op jit(solution)/shard_map/ppermute | solution.py:39
  44.5 3.0 %collective-permute-done.16.refs_8_ = bf16[144,512]{1,0:T(8,128)(2,1)S(1)} collective-permute-done((bf16[144,512]{1,0:T(8,128)(2,1)S(1)}, bf16[144,512]{1,0:T(8,128)(2,1)S(1)}, u32[]{:S(2)}, u32[]{:S(2)}) %collective-permute-start.16) | collective-permute-done | bytes 147488 | tf_op jit(solution)/shard_map/ppermute | solution.py:39
  47.5 0.3 collective-permute-start.17
  47.8 1.5 %query_grad.1 = (bf16[128,512]{1,0:T(8,128)(2,1)}, bf16[128,512]{1,0:T(8,128)(2,1)}, bf16[128,512]{1,0:T(8,128)(2,1)}) custom-call(bf16[128,512]{1,0:T(8,128)(2,1)S(1)} %get-tuple-element.48.q.refs_0_, bf16[256,512]{1,0:T(8,128)(2,1)S(1)} %pad_add_fusion.1.own, bf16[256,512]{1,0:T(8,128)(2,1)S(1)} %collective-permute-done.2.near, ...), custom_call_target="tpu_custom_call" | custom-call | bytes 6642000 | tf_op jit(solution)/shard_map/query_grad/pallas_call | solution.py:74
  49.3 0.0 collective-permute-done.18.refs_6_
  49.4 0.0 collective-permute-done.19.refs_7_
  49.4 0.9 %key_part.1 = (f32[128,512]{1,0:T(8,128)S(1)}, f32[128,512]{1,0:T(8,128)S(1)}, f32[128,512]{1,0:T(8,128)S(1)}) custom-call(bf16[256,512]{1,0:T(8,128)(2,1)S(1)} %pad_add_fusion.1.own, bf16[128,512]{1,0:T(8,128)(2,1)S(1)} %get-tuple-element.48.q.refs_0_, bf16[128,512]{1,0:T(8,128)(2,1)S(1)} %collective-permute-done.13.seen_b.refs_1_, ...), custom_call_target="tpu_custom_call" | custom-call | bytes 5535000 | tf_op jit(solution)/shard_map/key_part/pallas_call | solution.py:74
  50.2 2.4 %collective-permute-done.17.message = bf16[144,512]{1,0:T(8,128)(2,1)S(1)} collective-permute-done((bf16[144,512]{1,0:T(8,128)(2,1)S(1)}, bf16[144,512]{1,0:T(8,128)(2,1)S(1)}, u32[]{:S(2)}, u32[]{:S(2)}) %collective-permute-start.17) | collective-permute-done | bytes 147488 | tf_op jit(solution)/shard_map/ppermute | solution.py:28
  52.7 1.0 %key_grad.1 = (bf16[128,512]{1,0:T(8,128)(2,1)}, bf16[128,512]{1,0:T(8,128)(2,1)}) custom-call(bf16[256,512]{1,0:T(8,128)(2,1)S(1)} %pad_add_fusion.1.own, bf16[128,512]{1,0:T(8,128)(2,1)S(1)} %collective-permute-done.14.seen.refs_4_.query, bf16[144,512]{1,0:T(8,128)(2,1)S(1)} %collective-permute-done.17.message, f32[128,512]{1,0:T(8,128)S(1)} %get-tuple-element.66.late, ...), custom_call_target="tpu_custom_call" | custom-call | bytes 3690000 | tf_op jit(solution)/shard_map/key_grad/pallas_call | solution.py:74
  (3 shorter events, 0.1 us)
Async XLA Ops:
  0.6 18.5 %copy-start = (bf16[512,2048]{1,0:T(8,128)(2,1)S(1)}, bf16[512,2048]{1,0:T(8,128)(2,1)}, u32[]{:S(2)}) copy-start(bf16[512,2048]{1,0:T(8,128)(2,1)} %weight.5) | copy-start | bytes 6291460
  1.8 9.4 %collective-permute-start = (bf16[256,512]{1,0:T(8,128)(2,1)S(1)}, bf16[256,512]{1,0:T(8,128)(2,1)S(1)}, u32[]{:S(2)}, u32[]{:S(2)}) collective-permute-start(bf16[256,512]{1,0:T(8,128)(2,1)S(1)} %pad_add_fusion.1.own), channel_id=1, source_target_pairs={{8,0},{16,8},{24,16},{28,24},{20,28},{12,20},{4,12},{0,4},{9,1},{1... | collective-permute-start | bytes 786440 | tf_op jit(solution)/shard_map/ppermute | solution.py:39
  4.8 11.3 %collective-permute-start.2 = (bf16[256,512]{1,0:T(8,128)(2,1)S(1)}, bf16[256,512]{1,0:T(8,128)(2,1)S(1)}, u32[]{:S(2)}, u32[]{:S(2)}) collective-permute-start(bf16[256,512]{1,0:T(8,128)(2,1)S(1)} %pad_add_fusion.1.own), channel_id=1, source_target_pairs={{0,1},{1,0},{2,3},{3,2},{4,5},{5,4},{6,7},{7,6},{8,12},{9,13},{10,... | collective-permute-start | bytes 786440 | tf_op jit(solution)/shard_map/ppermute | solution.py:50
  4.8 11.6 %collective-permute-start.3 = (bf16[256,512]{1,0:T(8,128)(2,1)S(1)}, bf16[256,512]{1,0:T(8,128)(2,1)S(1)}, u32[]{:S(2)}, u32[]{:S(2)}) collective-permute-start(bf16[256,512]{1,0:T(8,128)(2,1)S(1)} %pad_add_fusion.1.own), channel_id=1, source_target_pairs={{0,8},{8,16},{16,24},{24,28},{28,20},{20,12},{12,4},{4,0},{1,9},{9... | collective-permute-start | bytes 786440 | tf_op jit(solution)/shard_map/ppermute | solution.py:39
  11.2 7.9 %collective-permute-start.1 = (bf16[256,512]{1,0:T(8,128)(2,1)S(1)}, bf16[256,512]{1,0:T(8,128)(2,1)S(1)}, u32[]{:S(2)}, u32[]{:S(2)}) collective-permute-start(bf16[256,512]{1,0:T(8,128)(2,1)S(1)} %collective-permute-done.seen.second), channel_id=1, source_target_pairs={{0,4},{4,0},{8,12},{12,8},{16,20},{20,16},{24,28},{28,24},{1,5},{5... | collective-permute-start | bytes 786440 | tf_op jit(solution)/shard_map/ppermute | solution.py:28
  12.8 7.7 %collective-permute-start.5 = (bf16[128,512]{1,0:T(8,128)(2,1)}, bf16[128,512]{1,0:T(8,128)(2,1)S(1)}, u32[]{:S(2)}, u32[]{:S(2)}) collective-permute-start(bf16[128,512]{1,0:T(8,128)(2,1)} %param.13), channel_id=1, source_target_pairs={{0,2},{1,3},{2,0},{3,1},{4,6},{5,7},{6,4},{7,5},{8,10},{9,11},{10,... | collective-permute-start | bytes 393224 | tf_op jit(solution)/shard_map/ppermute | solution.py:28
  15.4 5.1 %collective-permute-start.4 = (bf16[128,512]{1,0:T(8,128)(2,1)S(1)}, bf16[128,512]{1,0:T(8,128)(2,1)S(1)}, u32[]{:S(2)}, u32[]{:S(2)}) collective-permute-start(bf16[128,512]{1,0:T(8,128)(2,1)S(1)} %get-tuple-element.38.q), channel_id=1, source_target_pairs={{8,0},{16,8},{24,16},{28,24},{20,28},{12,20},{4,12},{0,4},{9,1},{1... | collective-permute-start | bytes 393224 | tf_op jit(solution)/shard_map/ppermute | solution.py:39
  16.0 4.5 %collective-permute-start.6 = (f32[31,512]{1,0:T(8,128)}, f32[31,512]{1,0:T(8,128)S(1)}, u32[]{:S(2)}, u32[]{:S(2)}) collective-permute-start(f32[31,512]{1,0:T(8,128)} %taps.3), channel_id=1, source_target_pairs={{0,2},{1,3},{2,0},{3,1},{4,6},{5,7},{6,4},{7,5},{8,10},{9,11},{10,... | collective-permute-start | bytes 190472 | tf_op jit(solution)/shard_map/ppermute | solution.py:28
  19.1 14.3 %copy-start.1 = (f32[31,512]{1,0:T(8,128)S(1)}, f32[31,512]{1,0:T(8,128)}, u32[]{:S(2)}) copy-start(f32[31,512]{1,0:T(8,128)} %taps.3) | copy-start | bytes 190468
  20.5 1.6 %collective-permute-start.7 = (bf16[128,1024]{1,0:T(8,128)(2,1)S(1)}, bf16[128,1024]{1,0:T(8,128)(2,1)S(1)}, u32[]{:S(2)}, u32[]{:S(2)}) collective-permute-start(bf16[128,1024]{1,0:T(8,128)(2,1)S(1)} %get-tuple-element.44), channel_id=1, source_target_pairs={{0,1},{1,0},{2,3},{3,2},{4,5},{5,4},{6,7},{7,6},{8,9},{9,8},{10,11... | collective-permute-start | bytes 786440 | tf_op jit(solution)/shard_map/ppermute | solution.py:28
  22.3 11.1 %collective-permute-start.11 = (bf16[128,1024]{1,0:T(8,128)(2,1)S(1)}, bf16[128,1024]{1,0:T(8,128)(2,1)S(1)}, u32[]{:S(2)}, u32[]{:S(2)}) collective-permute-start(bf16[128,1024]{1,0:T(8,128)(2,1)S(1)} %get-tuple-element.51.chip), channel_id=1, source_target_pairs={{0,2},{1,3},{2,0},{3,1},{4,6},{5,7},{6,4},{7,5},{8,10},{9,11},{10,... | collective-permute-start | bytes 786440 | tf_op jit(solution)/shard_map/ppermute | solution.py:28
  23.6 6.7 %collective-permute-start.8 = (bf16[48,1024]{1,0:T(8,128)(2,1)S(1)}, bf16[48,1024]{1,0:T(8,128)(2,1)S(1)}, u32[]{:S(2)}, u32[]{:S(2)}) collective-permute-start(bf16[48,1024]{1,0:T(8,128)(2,1)S(1)} %get-tuple-element.49), channel_id=1, source_target_pairs={{0,4},{4,0},{8,12},{12,8},{16,20},{20,16},{24,28},{28,24},{1,5},{5... | collective-permute-start | bytes 294920 | tf_op jit(solution)/shard_map/ppermute | solution.py:28
  26.1 6.7 %collective-permute-start.9 = (bf16[48,1024]{1,0:T(8,128)(2,1)S(1)}, bf16[48,1024]{1,0:T(8,128)(2,1)S(1)}, u32[]{:S(2)}, u32[]{:S(2)}) collective-permute-start(bf16[48,1024]{1,0:T(8,128)(2,1)S(1)} %get-tuple-element.50), channel_id=1, source_target_pairs={{0,1},{1,0},{2,3},{3,2},{4,8},{5,9},{6,10},{7,11},{8,4},{9,5},{10,... | collective-permute-start | bytes 294920 | tf_op jit(solution)/shard_map/ppermute | solution.py:50
  26.1 7.3 %collective-permute-start.12 = (bf16[128,512]{1,0:T(8,128)(2,1)S(1)}, bf16[128,512]{1,0:T(8,128)(2,1)S(1)}, u32[]{:S(2)}, u32[]{:S(2)}) collective-permute-start(bf16[128,512]{1,0:T(8,128)(2,1)S(1)} %get-tuple-element.48.q.refs_0_), channel_id=1, source_target_pairs={{0,8},{8,16},{16,24},{24,28},{28,20},{20,12},{12,4},{4,0},{1,9},{9... | collective-permute-start | bytes 393224 | tf_op jit(solution)/shard_map/ppermute | solution.py:39
  27.6 5.8 %collective-permute-start.13 = (bf16[128,512]{1,0:T(8,128)(2,1)S(1)}, bf16[128,512]{1,0:T(8,128)(2,1)S(1)}, u32[]{:S(2)}, u32[]{:S(2)}) collective-permute-start(bf16[128,512]{1,0:T(8,128)(2,1)S(1)} %get-tuple-element.48.q.refs_0_), channel_id=1, source_target_pairs={{0,1},{1,0},{2,3},{3,2},{4,5},{5,4},{6,7},{7,6},{8,12},{9,13},{10,... | collective-permute-start | bytes 393224 | tf_op jit(solution)/shard_map/ppermute | solution.py:50
  30.3 6.3 %collective-permute-start.14 = (bf16[128,512]{1,0:T(8,128)(2,1)S(1)}, bf16[128,512]{1,0:T(8,128)(2,1)S(1)}, u32[]{:S(2)}, u32[]{:S(2)}) collective-permute-start(bf16[128,512]{1,0:T(8,128)(2,1)S(1)} %get-tuple-element.56), channel_id=1, source_target_pairs={{0,4},{4,0},{8,12},{12,8},{16,20},{20,16},{24,28},{28,24},{1,5},{5... | collective-permute-start | bytes 393224 | tf_op jit(solution)/shard_map/ppermute | solution.py:28
  32.8 5.0 %collective-permute-start.10 = (bf16[64,1024]{1,0:T(8,128)(2,1)S(1)}, bf16[64,1024]{1,0:T(8,128)(2,1)S(1)}, u32[]{:S(2)}, u32[]{:S(2)}) collective-permute-start(bf16[64,1024]{1,0:T(8,128)(2,1)S(1)} %stack.1.ends), channel_id=1, source_target_pairs={{0,2},{1,3},{2,0},{3,1},{4,6},{5,7},{6,4},{7,5},{8,10},{9,11},{10,... | collective-permute-start | bytes 393224 | tf_op jit(solution)/shard_map/ppermute | solution.py:28
  39.3 1.6 %collective-permute-start.15 = (bf16[128,1024]{1,0:T(8,128)(2,1)S(1)}, bf16[128,1024]{1,0:T(8,128)(2,1)S(1)}, u32[]{:S(2)}, u32[]{:S(2)}) collective-permute-start(bf16[128,1024]{1,0:T(8,128)(2,1)S(1)} %get-tuple-element.57.own.grad_here), channel_id=1, source_target_pairs={{0,1},{1,0},{2,3},{3,2},{4,5},{5,4},{6,7},{7,6},{8,9},{9,8},{10,11... | collective-permute-start | bytes 786440 | tf_op jit(solution)/shard_map/ppermute | solution.py:28
  41.6 5.9 %collective-permute-start.16 = (bf16[144,512]{1,0:T(8,128)(2,1)S(1)}, bf16[144,512]{1,0:T(8,128)(2,1)S(1)}, u32[]{:S(2)}, u32[]{:S(2)}) collective-permute-start(bf16[144,512]{1,0:T(8,128)(2,1)S(1)} %get-tuple-element.60.message.refs_5_), channel_id=1, source_target_pairs={{8,0},{16,8},{24,16},{28,24},{20,28},{12,20},{4,12},{0,4},{9,1},{1... | collective-permute-start | bytes 442376 | tf_op jit(solution)/shard_map/ppermute | solution.py:39
  41.6 7.7 %collective-permute-start.18 = (bf16[144,512]{1,0:T(8,128)(2,1)S(1)}, bf16[144,512]{1,0:T(8,128)(2,1)S(1)}, u32[]{:S(2)}, u32[]{:S(2)}) collective-permute-start(bf16[144,512]{1,0:T(8,128)(2,1)S(1)} %get-tuple-element.60.message.refs_5_), channel_id=1, source_target_pairs={{0,1},{1,0},{2,3},{3,2},{4,5},{5,4},{6,7},{7,6},{8,12},{9,13},{10,... | collective-permute-start | bytes 442376 | tf_op jit(solution)/shard_map/ppermute | solution.py:50
  41.8 7.5 %collective-permute-start.19 = (bf16[144,512]{1,0:T(8,128)(2,1)S(1)}, bf16[144,512]{1,0:T(8,128)(2,1)S(1)}, u32[]{:S(2)}, u32[]{:S(2)}) collective-permute-start(bf16[144,512]{1,0:T(8,128)(2,1)S(1)} %get-tuple-element.60.message.refs_5_), channel_id=1, source_target_pairs={{0,8},{8,16},{16,24},{24,28},{28,20},{20,12},{12,4},{4,0},{1,9},{9... | collective-permute-start | bytes 442376 | tf_op jit(solution)/shard_map/ppermute | solution.py:39
  47.5 5.1 %collective-permute-start.17 = (bf16[144,512]{1,0:T(8,128)(2,1)S(1)}, bf16[144,512]{1,0:T(8,128)(2,1)S(1)}, u32[]{:S(2)}, u32[]{:S(2)}) collective-permute-start(bf16[144,512]{1,0:T(8,128)(2,1)S(1)} %collective-permute-done.16.refs_8_), channel_id=1, source_target_pairs={{0,4},{4,0},{8,12},{12,8},{16,20},{20,16},{24,28},{28,24},{1,5},{5... | collective-permute-start | bytes 442376 | tf_op jit(solution)/shard_map/ppermute | solution.py:28

commit v12 on v11

--- a/solution.py
+++ b/solution.py
@@ -11,6 +11,7 @@
 HDIM = 128
 F32 = jnp.float32
 BF16 = jnp.bfloat16
+CHUNK = 256
 HALO = 16
 NT = (((1,), (1,)), ((), ()))
 NN = (((1,), (0,)), ((), ()))
@@ -58,10 +59,11 @@
     return total_swap(block, lambda i, count: ((i + 1) ^ 1) - 1 if 0 < i < count - 1 else None)
 
 
-def window_of(block):
+def window_of(block, before_relay=lambda second: second):
     second = ring(block, 1)
     first = ring(block, 0)
     near = inner_swap(block)
+    second = before_relay(second)
     return near, first, second, pair_swap(second, "ctx", 1)
 
 
@@ -158,6 +160,10 @@
     width = weight.shape[0]
     at = (lax.axis_index("mp") ^ flip) * width
     return weight[:, pl.ds(pl.multiple_of(at, 128), width)]
+
+
+def turn_body(block, seen, copy):
+    copy[...] = block[...]
 
 
 def split_body(joined, seen, *parts):
@@ -212,7 +218,7 @@
     second_copy[...] = q_second[...]
 
 
-def join_body(keep, core, inputs, cot, cot_other, q, q_second, chip, rim_near, rim_far, q_copy, second_copy):
+def join_body(keep, core, inputs, cot, cot_other, q, chip, rim_near, rim_far, q_copy):
     frames, width = inputs.shape
     wide = 2 * HALO
     even = is_even()
@@ -230,13 +236,13 @@
             rim_far[at, cols] = jnp.where(even, first, last).astype(BF16)
         chip[:, cols] = total
     q_copy[...] = q[...]
-    second_copy[...] = q_second[...]
-
-
-def stack_body(rim_near, rim_far, ends):
+
+
+def stack_body(rim_near, rim_far, q_second, ends, second_copy):
     wide = 2 * HALO
     ends[0:wide, :] = rim_near[0:wide, :]
     ends[wide : 2 * wide, :] = rim_far[0:wide, :]
+    second_copy[...] = q_second[...]
 
 
 def summed(share, across, rows, cols, width):
@@ -245,21 +251,40 @@
     return total.astype(BF16).astype(F32)
 
 
-def shifted_sum(rows, taps_of, count):
-    total = None
+def tiles_of(rows):
+    return [rows[at : at + 8] for at in range(0, rows.shape[0], 8)]
+
+
+def shifted_sum(tiles, taps_of, count):
+    at = lax.broadcasted_iota(jnp.int32, (8, CHUNK), 0)
+    sums = [None] * (count // 8)
+
+    def add(k, term):
+        sums[k] = term if sums[k] is None else sums[k] + term
+
     for b in range(8):
-        part = None
-        reach = count if b == 0 else count + 8
-        for a in range(4):
-            tap = taps_of(8 * a + b)
-            if tap is None:
-                continue
-            term = tap * rows[8 * a : 8 * a + reach]
-            part = term if part is None else part + term
-        if b:
-            part = pltpu.roll(part, reach - b, 0)[0:count]
-        total = part if total is None else total + part
-    return total
+        parts = []
+        for k in range(count // 8 + (b > 0)):
+            part = None
+            for a in range(4):
+                tap = taps_of(8 * a + b)
+                if tap is None or tiles[k + a] is None:
+                    continue
+                term = tap * tiles[k + a]
+                part = term if part is None else part + term
+            parts.append(part if part is None or b == 0 else pltpu.roll(part, 8 - b, 0))
+        for k in range(count // 8):
+            if b == 0:
+                if parts[k] is not None:
+                    add(k, parts[k])
+            elif parts[k] is not None and parts[k + 1] is not None:
+                add(k, jnp.where(at < 8 - b, parts[k], parts[k + 1]))
+            elif parts[k] is not None:
+                add(k, jnp.where(at < 8 - b, parts[k], 0.0))
+            elif parts[k + 1] is not None:
+                add(k, jnp.where(at < 8 - b, 0.0, parts[k + 1]))
+    zero = jnp.zeros((8, CHUNK), F32)
+    return jnp.concatenate([zero if part is None else part for part in sums], axis=0)
 
 
 def silu_parts(conv, cots):
@@ -277,28 +302,28 @@
 
 
 def conv_chunks(width, cot, cot_other, taps, taps_other):
-    for k, cols in enumerate(columns(2 * width)):
-        own = k * HDIM < width
+    for c in range(0, 2 * width, CHUNK):
+        own, cols = c < width, slice(c, c + CHUNK)
         local = cols if own else slice(cols.start - width, cols.stop - width)
         yield own, cols, local, cot if own else cot_other, taps if own else taps_other
 
 
 def conv_inner_body(
-    chip, across, cot, cot_other, taps, taps_other, seen_a, seen_b, rows_out, edge_rows, edge_conv, part_grad
+    chip, across, cot, cot_other, taps, taps_other, seen, rows_out, edge_rows, edge_conv, part_grad
 ):
     frames, width = cot.shape
     wide, count = 2 * HALO, taps.shape[0]
     inner = slice(HALO, frames - HALO)
-    none = jnp.zeros((wide, HDIM), F32)
+    none = [None] * (wide // 8)
     for own, cols, local, cots_of, tap in conv_chunks(width, cot, cot_other, taps, taps_other):
         rows = summed(chip, across, slice(0, frames), cols, width)
         cots = cots_of[:, local].astype(F32)
         conv = shifted_sum(
-            jnp.concatenate([none, rows, none], axis=0), taps_forward(tap, count, local), frames + wide
+            none + tiles_of(rows) + none, taps_forward(tap, count, local), frames + wide
         )
         silu, grad = silu_parts(conv[wide:frames], cots[inner])
         back = shifted_sum(
-            jnp.concatenate([none, grad, none], axis=0), taps_backward(tap, count, local), frames
+            none + tiles_of(grad) + none, taps_backward(tap, count, local), frames
         )
         edge_conv[0:wide, cols] = conv[0:wide]
         edge_conv[wide : 2 * wide, cols] = conv[frames : frames + wide]
@@ -311,14 +336,14 @@
 
 def conv_edge_body(
     ends, ends_across, rim_near, rim_far, cot, cot_other, taps, taps_other,
-    rows_in, edge_rows, edge_conv, part_grad, seen, output, grad_input,
+    rows_in, edge_rows, edge_conv, part_grad, seen_a, seen_b, output, grad_input,
 ):
     frames, width = cot.shape
     wide, count = 2 * HALO, taps.shape[0]
     even, far = is_even(), far_there()
     low, high = slice(0, HALO), slice(frames - HALO, frames)
     inner = slice(HALO, frames - HALO)
-    none = jnp.zeros((wide, HDIM), F32)
+    none = [None] * (wide // 8)
     cots_of = slice(wide, wide + HALO)
 
     def sides(near, beyond):
@@ -330,14 +355,14 @@
         row_low, row_high = sides(rows[0:wide], rows[wide:])
         cot_low, cot_high = sides(rim_near[cots_of, cols].astype(F32), rim_far[cots_of, cols].astype(F32))
         conv = edge_conv[:, cols] + shifted_sum(
-            jnp.concatenate([row_low, none, row_high], axis=0), taps_forward(tap, count, local), 2 * wide
+            tiles_of(row_low) + none + tiles_of(row_high), taps_forward(tap, count, local), 2 * wide
         )
         first = block[low, local].astype(F32)
         last = block[high, local].astype(F32)
         cots = jnp.concatenate([cot_low, first, last, cot_high], axis=0)
         silu, grad = silu_parts(conv, cots)
         back = shifted_sum(
-            jnp.concatenate([grad[0:wide], none, grad[wide:]], axis=0), taps_backward(tap, count, local), 2 * wide
+            tiles_of(grad[0:wide]) + none + tiles_of(grad[wide:]), taps_backward(tap, count, local), 2 * wide
         )
         part = part_grad[:, cols]
         grad_input[:, cols] = jnp.concatenate(
@@ -466,13 +491,18 @@
     kv = lax.pad(key_rows, zero, ((0, frames, 0), (0, 0, 0))) + lax.pad(
         value_rows, zero, ((frames, 0, 0), (0, 0, 0))
     )
-    near, first, second, relay = window_of(kv)
-    cot_other = pair_swap(cotangent, "mp", 2)
-    taps_other = pair_swap(kernel, "mp", 2)
     joined = sum(
         lax.pad(rows, zero, ((k * frames, (2 - k) * frames, 0), (0, 0, 0)))
         for k, rows in enumerate((query_rows, inputs, cotangent))
     )
+    near, first, second, relay = window_of(
+        kv,
+        lambda second: kernel_call(
+            turn_body, (shaped(kv.shape, BF16),), (second, joined), 0.1, "turn", 1
+        )[0],
+    )
+    cot_other = pair_swap(cotangent, "mp", 2)
+    taps_other = pair_swap(kernel, "mp", 2)
     query, inputs, cotangent = kernel_call(
         split_body, (tile, tile, tile), (joined, second), 0.1, "split", 1
     )
@@ -492,17 +522,20 @@
 
     send, q_second = kernel_call(pass_body, (both, tile), (send, q_second, cot_other, taps_other), 0.1, "pass", 2)
     core = pair_swap(send, "mp", 1)
-    chip, rim_up, rim_down, q_own, q_handed = kernel_call(
+    chip, rim_up, rim_down, q_own = kernel_call(
         join_body,
-        (both, rim, rim, tile, tile),
-        (keep, core, inputs, cotangent, cot_other, query, q_second),
+        (both, rim, rim, tile),
+        (keep, core, inputs, cotangent, cot_other, query),
         0.2, "join",
     )
     across = pair_swap(chip, "mp", 2)
     rim_far = outer_swap(rim_down)
     rim_near = pair_swap(rim_up, "ctx", 1)
-    (ends,) = kernel_call(
-        stack_body, (shaped((2 * wide, 2 * width), BF16),), (rim_near, rim_far), 0.1, "stack"
+    ends, q_handed = kernel_call(
+        stack_body,
+        (shaped((2 * wide, 2 * width), BF16), tile),
+        (rim_near, rim_far, q_second),
+        0.1, "stack",
     )
     ends_across = pair_swap(ends, "mp", 2)
     q_first = ring(q_own, 0)
@@ -516,15 +549,15 @@
             shaped((2 * wide, 2 * width), F32),
             shaped((frames, 2 * width), F32),
         ),
-        (chip, across, cotangent, cot_other, kernel, taps_other, q_first, q_near),
-        3.1, "conv_inner", 2,
+        (chip, across, cotangent, cot_other, kernel, taps_other, q_first),
+        3.1, "conv_inner", 1,
     )
     output_here, grad_here = kernel_call(
         conv_edge_body,
         (tile, both),
         (ends, ends_across, rim_near, rim_far, cotangent, cot_other, kernel, taps_other)
-        + (rows_out, edge_rows, edge_conv, part_grad, q_relay),
-        1.4, "conv_edge", 1,
+        + (rows_out, edge_rows, edge_conv, part_grad, q_near, q_relay),
+        1.4, "conv_edge", 2,
     )
 
     gi_core = pair_swap(grad_here, "mp", 1)

time: 53.8 us -> 52.5 us (0.976)
  waiting for transfers between devices: 17.9 us -> 14.5 us
  starting transfers between devices: 22 us -> 24.7 us
  Pallas kernels: 10.8 us -> 10.1 us
    ppermute x10, waiting for transfers between devices: 11.6 us -> 9.59 us  [pair_swap(): lax.ppermute(block, axis, [(i, i ^ bit) for i in range(lax.axis_size(axis...]
    ppermute x10, starting transfers between devices: 10.9 us -> 12.9 us  [pair_swap(): lax.ppermute(block, axis, [(i, i ^ bit) for i in range(lax.axis_size(axis...]
    ppermute x6, waiting for transfers between devices: 6.24 us -> 4.86 us  [ring(): return lax.ppermute(block, 'ctx', ring_routes(lax.axis_size('ctx'))[way])]
    ppermute x6, starting transfers between devices: 10.9 us -> 11.9 us  [ring(): return lax.ppermute(block, 'ctx', ring_routes(lax.axis_size('ctx'))[way])]
    pallas_call x13 -> x14, Pallas kernels: 10.8 us -> 10.1 us  [kernel_call(): pl.pallas_call(body, out_shape=outs, in_specs=[VMEM] * (len(args) - unrea...]
where the time goes in v12:
time: 52.5 us; the launch traced here: 52.4 us
  starting transfers between devices  24.7 us (47%)
  waiting for transfers between devices  14.5 us (28%)
  Pallas kernels  10.1 us (19%)
  other arithmetic  2.19 us (4%)
  between operations  0.82 us (2%)
    ppermute x10, starting transfers between devices, pair_swap(): lax.ppermute(block, axis, [(i, i ^ bit) for i in range(lax.axis_size(axis...  12.9 us
    ppermute x6, starting transfers between devices, ring(): return lax.ppermute(block, 'ctx', ring_routes(lax.axis_size('ctx'))[way])  11.9 us
    pallas_call x14, Pallas kernels, kernel_call(): pl.pallas_call(body, out_shape=outs, in_specs=[VMEM] * (len(args) - unrea...  10.1 us
    ppermute x10, waiting for transfers between devices, pair_swap(): lax.ppermute(block, axis, [(i, i ^ bit) for i in range(lax.axis_size(axis...  9.59 us
    ppermute x6, waiting for transfers between devices, ring(): return lax.ppermute(block, 'ctx', ring_routes(lax.axis_size('ctx'))[way])  4.86 us
    add x1, other arithmetic, per_device(): lax.pad(key_rows, zero, ((0, frames, 0), (0, 0, 0)))  1.14 us
    add x1, other arithmetic, per_device(): sum((lax.pad(rows, zero, ((k * frames, (2 - k) * frames, 0), (0, 0, 0)))...  1.06 us
  transfers between devices with their start and end apart: 20, of which 9 were waited for; matrix products, arithmetic and copies ran while one was open for 2% of the time, Pallas kernels for 14%

profile of v12, /device:TPU:0, one launch (start us, length us, event | category | flops | bytes accessed | tf_op | source)
XLA Modules:
  0.0 52.4 jit_solution(6252896653572221240)
XLA Ops:
  0.6 0.0 copy-start.2
  0.6 0.0 copy-start.1
  0.7 0.0 copy-start
  0.7 1.1 %pad_add_fusion.1.own = bf16[256,512]{1,0:T(8,128)(2,1)S(1)} fusion(bf16[128,512]{1,0:T(8,128)(2,1)} %param.9, bf16[128,512]{1,0:T(8,128)(2,1)} %param.8), kind=kLoop, calls=%fused_computation.1 | loop fusion | flops 524288 | bytes 524288 | tf_op jit(solution)/shard_map/add | solution.py:491
  1.8 3.0 %collective-permute-start = (bf16[256,512]{1,0:T(8,128)(2,1)S(1)}, bf16[256,512]{1,0:T(8,128)(2,1)S(1)}, u32[]{:S(2)}, u32[]{:S(2)}) collective-permute-start(bf16[256,512]{1,0:T(8,128)(2,1)S(1)} %pad_add_fusion.1.own), channel_id=1, source_target_pairs={{8,0},{16,8},{24,16},{28,24},{20,28},{12,20},{4,12},{0,4},{9,1},{1... | collective-permute-start | bytes 786440 | tf_op jit(solution)/shard_map/ppermute | solution.py:40
  4.8 0.0 collective-permute-start.2
  4.8 3.2 %collective-permute-start.3 = (bf16[256,512]{1,0:T(8,128)(2,1)S(1)}, bf16[256,512]{1,0:T(8,128)(2,1)S(1)}, u32[]{:S(2)}, u32[]{:S(2)}) collective-permute-start(bf16[256,512]{1,0:T(8,128)(2,1)S(1)} %pad_add_fusion.1.own), channel_id=1, source_target_pairs={{0,8},{8,16},{16,24},{24,28},{28,20},{20,12},{12,4},{4,0},{1,9},{9... | collective-permute-start | bytes 786440 | tf_op jit(solution)/shard_map/ppermute | solution.py:40
  7.9 1.1 %pad_add_fusion.seen.joined = bf16[384,512]{1,0:T(8,128)(2,1)S(1)} fusion(bf16[128,512]{1,0:T(8,128)(2,1)} %param.13, bf16[128,512]{1,0:T(8,128)(2,1)} %param.10, bf16[128,512]{1,0:T(8,128)(2,1)} %param.7), kind=kLoop, calls=%fused_computation | loop fusion | flops 1179648 | bytes 786432 | tf_op jit(solution)/shard_map/add | solution.py:494
  9.0 2.2 %collective-permute-done.block = bf16[256,512]{1,0:T(8,128)(2,1)S(1)} collective-permute-done((bf16[256,512]{1,0:T(8,128)(2,1)S(1)}, bf16[256,512]{1,0:T(8,128)(2,1)S(1)}, u32[]{:S(2)}, u32[]{:S(2)}) %collective-permute-start) | collective-permute-done | bytes 262176 | tf_op jit(solution)/shard_map/ppermute | solution.py:40
  11.2 1.7 %collective-permute-start.1 = (bf16[256,512]{1,0:T(8,128)(2,1)S(1)}, bf16[256,512]{1,0:T(8,128)(2,1)S(1)}, u32[]{:S(2)}, u32[]{:S(2)}) collective-permute-start(bf16[256,512]{1,0:T(8,128)(2,1)S(1)} %turn.1.seen.second), channel_id=1, source_target_pairs={{0,4},{4,0},{8,12},{12,8},{16,20},{20,16},{24,28},{28,24},{1,5},{5... | collective-permute-start | bytes 786440 | tf_op jit(solution)/shard_map/ppermute | solution.py:29
  12.9 0.0 copy-done.2
  12.9 1.5 %collective-permute-start.5 = (bf16[128,512]{1,0:T(8,128)(2,1)S(1)}, bf16[128,512]{1,0:T(8,128)(2,1)S(1)}, u32[]{:S(2)}, u32[]{:S(2)}) collective-permute-start(bf16[128,512]{1,0:T(8,128)(2,1)S(1)} %copy-done.2), channel_id=1, source_target_pairs={{0,2},{1,3},{2,0},{3,1},{4,6},{5,7},{6,4},{7,5},{8,10},{9,11},{10,... | collective-permute-start | bytes 393224 | tf_op jit(solution)/shard_map/ppermute | solution.py:29
  14.5 0.6 %collective-permute-start.4 = (bf16[128,512]{1,0:T(8,128)(2,1)S(1)}, bf16[128,512]{1,0:T(8,128)(2,1)S(1)}, u32[]{:S(2)}, u32[]{:S(2)}) collective-permute-start(bf16[128,512]{1,0:T(8,128)(2,1)S(1)} %get-tuple-element.39.q), channel_id=1, source_target_pairs={{8,0},{16,8},{24,16},{28,24},{20,28},{12,20},{4,12},{0,4},{9,1},{1... | collective-permute-start | bytes 393224 | tf_op jit(solution)/shard_map/ppermute | solution.py:40
  15.1 0.0 collective-permute-done.2.near
  15.1 0.0 copy-done.1
  15.1 0.3 collective-permute-start.6
  15.4 0.0 collective-permute-done.3.first
  15.4 0.6 %forward.1 = (f32[128,512]{1,0:T(8,128)S(1)}, f32[128,512]{1,0:T(8,128)S(1)}, f32[128,512]{1,0:T(8,128)S(1)}) custom-call(bf16[128,512]{1,0:T(8,128)(2,1)S(1)} %get-tuple-element.39.q, bf16[256,512]{1,0:T(8,128)(2,1)S(1)} %pad_add_fusion.1.own, bf16[256,512]{1,0:T(8,128)(2,1)S(1)} %collective-permute-done.2.near, ...), custom_call_target="tpu_custom_call" | custom-call | bytes 3690000 | tf_op jit(solution)/shard_map/forward/pallas_call | solution.py:76
  16.0 3.1 %collective-permute-done.1.relay = bf16[256,512]{1,0:T(8,128)(2,1)S(1)} collective-permute-done((bf16[256,512]{1,0:T(8,128)(2,1)S(1)}, bf16[256,512]{1,0:T(8,128)(2,1)S(1)}, u32[]{:S(2)}, u32[]{:S(2)}) %collective-permute-start.1) | collective-permute-done | bytes 262176 | tf_op jit(solution)/shard_map/ppermute | solution.py:29
  19.1 0.0 copy-done
  19.1 0.9 %project.1 = (bf16[128,512]{1,0:T(8,128)(2,1)S(1)}, f32[128,512]{1,0:T(8,128)S(1)}, bf16[128,1024]{1,0:T(8,128)(2,1)S(1)}, bf16[128,1024]{1,0:T(8,128)(2,1)S(1)}) custom-call(bf16[128,512]{1,0:T(8,128)(2,1)S(1)} %get-tuple-element.39.q, bf16[256,512]{1,0:T(8,128)(2,1)S(1)} %collective-permute-done.1.relay, f32[128,512]{1,0:T(8,128)S(1)} %get-tuple-element.40.sums, ...), custom_call_target="tpu_custom_call" | custom-call | bytes 3690000 | tf_op jit(solution)/shard_map/project/pallas_call | solution.py:76
  20.0 0.0 collective-permute-done.6.seen_b.taps_other
  20.0 0.0 collective-permute-done.5.seen_a.cot_other
  20.0 0.4 collective-permute-done.4.q_second
  20.5 0.1 collective-permute-start.7
  20.5 1.5 %collective-permute-done.7.core = bf16[128,1024]{1,0:T(8,128)(2,1)S(1)} collective-permute-done((bf16[128,1024]{1,0:T(8,128)(2,1)S(1)}, bf16[128,1024]{1,0:T(8,128)(2,1)S(1)}, u32[]{:S(2)}, u32[]{:S(2)}) %collective-permute-start.7) | collective-permute-done | bytes 262176 | tf_op jit(solution)/shard_map/ppermute | solution.py:29
  22.1 0.1 join.1
  22.2 1.6 %collective-permute-start.11 = (bf16[128,1024]{1,0:T(8,128)(2,1)S(1)}, bf16[128,1024]{1,0:T(8,128)(2,1)S(1)}, u32[]{:S(2)}, u32[]{:S(2)}) collective-permute-start(bf16[128,1024]{1,0:T(8,128)(2,1)S(1)} %get-tuple-element.53.chip), channel_id=1, source_target_pairs={{0,2},{1,3},{2,0},{3,1},{4,6},{5,7},{6,4},{7,5},{8,10},{9,11},{10,... | collective-permute-start | bytes 786440 | tf_op jit(solution)/shard_map/ppermute | solution.py:29
  23.8 2.5 %collective-permute-start.8 = (bf16[48,1024]{1,0:T(8,128)(2,1)S(1)}, bf16[48,1024]{1,0:T(8,128)(2,1)S(1)}, u32[]{:S(2)}, u32[]{:S(2)}) collective-permute-start(bf16[48,1024]{1,0:T(8,128)(2,1)S(1)} %get-tuple-element.49), channel_id=1, source_target_pairs={{0,4},{4,0},{8,12},{12,8},{16,20},{20,16},{24,28},{28,24},{1,5},{5... | collective-permute-start | bytes 294920 | tf_op jit(solution)/shard_map/ppermute | solution.py:29
  26.2 0.0 collective-permute-start.9
  26.2 1.5 %collective-permute-start.12 = (bf16[128,512]{1,0:T(8,128)(2,1)S(1)}, bf16[128,512]{1,0:T(8,128)(2,1)S(1)}, u32[]{:S(2)}, u32[]{:S(2)}) collective-permute-start(bf16[128,512]{1,0:T(8,128)(2,1)S(1)} %get-tuple-element.48.q.refs_0_), channel_id=1, source_target_pairs={{0,8},{8,16},{16,24},{24,28},{28,20},{20,12},{12,4},{4,0},{1,9},{9... | collective-permute-start | bytes 393224 | tf_op jit(solution)/shard_map/ppermute | solution.py:40
  27.7 0.0 collective-permute-start.13
  27.7 2.7 %collective-permute-done.8.rim_near = bf16[48,1024]{1,0:T(8,128)(2,1)S(1)} collective-permute-done((bf16[48,1024]{1,0:T(8,128)(2,1)S(1)}, bf16[48,1024]{1,0:T(8,128)(2,1)S(1)}, u32[]{:S(2)}, u32[]{:S(2)}) %collective-permute-start.8) | collective-permute-done | bytes 98336 | tf_op jit(solution)/shard_map/ppermute | solution.py:29
  30.4 0.0 collective-permute-done.9.rim_far
  30.4 0.6 %collective-permute-start.10 = (bf16[64,1024]{1,0:T(8,128)(2,1)S(1)}, bf16[64,1024]{1,0:T(8,128)(2,1)S(1)}, u32[]{:S(2)}, u32[]{:S(2)}) collective-permute-start(bf16[64,1024]{1,0:T(8,128)(2,1)S(1)} %get-tuple-element.52.ends), channel_id=1, source_target_pairs={{0,2},{1,3},{2,0},{3,1},{4,6},{5,7},{6,4},{7,5},{8,10},{9,11},{10,... | collective-permute-start | bytes 393224 | tf_op jit(solution)/shard_map/ppermute | solution.py:29
  31.0 2.5 %collective-permute-start.14 = (bf16[128,512]{1,0:T(8,128)(2,1)S(1)}, bf16[128,512]{1,0:T(8,128)(2,1)S(1)}, u32[]{:S(2)}, u32[]{:S(2)}) collective-permute-start(bf16[128,512]{1,0:T(8,128)(2,1)S(1)} %get-tuple-element.58), channel_id=1, source_target_pairs={{0,4},{4,0},{8,12},{12,8},{16,20},{20,16},{24,28},{28,24},{1,5},{5... | collective-permute-start | bytes 393224 | tf_op jit(solution)/shard_map/ppermute | solution.py:29
  33.5 0.0 collective-permute-done.12.seen.refs_2_
  33.5 0.0 collective-permute-done.11.across
  33.5 2.8 %conv_inner.1 = (bf16[128,512]{1,0:T(8,128)(2,1)S(1)}, f32[32,512]{1,0:T(8,128)S(1)}, f32[64,1024]{1,0:T(8,128)S(1)}, f32[128,1024]{1,0:T(8,128)S(1)}) custom-call(bf16[128,1024]{1,0:T(8,128)(2,1)S(1)} %get-tuple-element.53.chip, bf16[128,1024]{1,0:T(8,128)(2,1)S(1)} %collective-permute-done.11.across, bf16[128,512]{1,0:T(8,128)(2,1)S(1)} %get-tuple-element.47.cot, ...), custom_call_target="tpu_custom_call" | custom-call | bytes 11439000 | tf_op jit(solution)/shard_map/conv_inner/pallas_call | solution.py:76
  36.3 0.0 collective-permute-done.13.seen_a.refs_1_
  36.3 0.0 collective-permute-done.10.ends_across
  36.4 0.1 collective-permute-done.14.seen_b.refs_4_.query
  36.4 1.1 %conv_edge.1 = (bf16[128,512]{1,0:T(8,128)(2,1)S(1)}, bf16[128,1024]{1,0:T(8,128)(2,1)S(1)}) custom-call(bf16[64,1024]{1,0:T(8,128)(2,1)S(1)} %get-tuple-element.52.ends, bf16[64,1024]{1,0:T(8,128)(2,1)S(1)} %collective-permute-done.10.ends_across, bf16[48,1024]{1,0:T(8,128)(2,1)S(1)} %collective-permute-done.8.rim_near, ...), custom_call_target="tpu_custom_call" | custom-call | bytes 5166000 | tf_op jit(solution)/shard_map/conv_edge/pallas_call | solution.py:76
  37.6 0.1 collective-permute-start.15
  37.7 0.5 upstream_own.1.partial
  38.2 1.0 %collective-permute-done.15.core = bf16[128,1024]{1,0:T(8,128)(2,1)S(1)} collective-permute-done((bf16[128,1024]{1,0:T(8,128)(2,1)S(1)}, bf16[128,1024]{1,0:T(8,128)(2,1)S(1)}, u32[]{:S(2)}, u32[]{:S(2)}) %collective-permute-start.15) | collective-permute-done | bytes 262176 | tf_op jit(solution)/shard_map/ppermute | solution.py:29
  39.2 0.7 %upstream.1 = (bf16[144,512]{1,0:T(8,128)(2,1)S(1)}, f32[128,512]{1,0:T(8,128)S(1)}) custom-call(bf16[128,1024]{1,0:T(8,128)(2,1)S(1)} %collective-permute-done.15.core, bf16[512,2048]{1,0:T(8,128)(2,1)S(1)} %copy-done, bf16[128,512]{1,0:T(8,128)(2,1)S(1)} %get-tuple-element.60.att, f32[128,512]{1,0:T(8,128)S(1)} %get-tuple-element.61.lse, ...), custom_call_target="tpu_custom_call" | custom-call | bytes 2214000 | tf_op jit(solution)/shard_map/upstream/pallas_call | solution.py:76
  39.8 2.1 %collective-permute-start.16 = (bf16[144,512]{1,0:T(8,128)(2,1)S(1)}, bf16[144,512]{1,0:T(8,128)(2,1)S(1)}, u32[]{:S(2)}, u32[]{:S(2)}) collective-permute-start(bf16[144,512]{1,0:T(8,128)(2,1)S(1)} %get-tuple-element.62.message.refs_5_), channel_id=1, source_target_pairs={{8,0},{16,8},{24,16},{28,24},{20,28},{12,20},{4,12},{0,4},{9,1},{1... | collective-permute-start | bytes 442376 | tf_op jit(solution)/shard_map/ppermute | solution.py:40
  41.9 0.0 collective-permute-start.18
  41.9 1.6 %collective-permute-start.19 = (bf16[144,512]{1,0:T(8,128)(2,1)S(1)}, bf16[144,512]{1,0:T(8,128)(2,1)S(1)}, u32[]{:S(2)}, u32[]{:S(2)}) collective-permute-start(bf16[144,512]{1,0:T(8,128)(2,1)S(1)} %get-tuple-element.62.message.refs_5_), channel_id=1, source_target_pairs={{0,8},{8,16},{16,24},{24,28},{28,20},{20,12},{12,4},{4,0},{1,9},{9... | collective-permute-start | bytes 442376 | tf_op jit(solution)/shard_map/ppermute | solution.py:40
  43.5 2.3 %collective-permute-done.16.refs_8_ = bf16[144,512]{1,0:T(8,128)(2,1)S(1)} collective-permute-done((bf16[144,512]{1,0:T(8,128)(2,1)S(1)}, bf16[144,512]{1,0:T(8,128)(2,1)S(1)}, u32[]{:S(2)}, u32[]{:S(2)}) %collective-permute-start.16) | collective-permute-done | bytes 147488 | tf_op jit(solution)/shard_map/ppermute | solution.py:40
  45.8 2.0 %collective-permute-start.17 = (bf16[144,512]{1,0:T(8,128)(2,1)S(1)}, bf16[144,512]{1,0:T(8,128)(2,1)S(1)}, u32[]{:S(2)}, u32[]{:S(2)}) collective-permute-start(bf16[144,512]{1,0:T(8,128)(2,1)S(1)} %collective-permute-done.16.refs_8_), channel_id=1, source_target_pairs={{0,4},{4,0},{8,12},{12,8},{16,20},{20,16},{24,28},{28,24},{1,5},{5... | collective-permute-start | bytes 442376 | tf_op jit(solution)/shard_map/ppermute | solution.py:29
  47.8 1.5 %query_grad.1 = (bf16[128,512]{1,0:T(8,128)(2,1)}, bf16[128,512]{1,0:T(8,128)(2,1)}, bf16[128,512]{1,0:T(8,128)(2,1)}) custom-call(bf16[128,512]{1,0:T(8,128)(2,1)S(1)} %get-tuple-element.48.q.refs_0_, bf16[256,512]{1,0:T(8,128)(2,1)S(1)} %pad_add_fusion.1.own, bf16[256,512]{1,0:T(8,128)(2,1)S(1)} %collective-permute-done.2.near, ...), custom_call_target="tpu_custom_call" | custom-call | bytes 6642000 | tf_op jit(solution)/shard_map/query_grad/pallas_call | solution.py:76
  49.3 0.0 collective-permute-done.18.refs_6_
  49.3 0.0 collective-permute-done.19.refs_7_
  49.4 0.9 %key_part.1 = (f32[128,512]{1,0:T(8,128)S(1)}, f32[128,512]{1,0:T(8,128)S(1)}, f32[128,512]{1,0:T(8,128)S(1)}) custom-call(bf16[256,512]{1,0:T(8,128)(2,1)S(1)} %pad_add_fusion.1.own, bf16[128,512]{1,0:T(8,128)(2,1)S(1)} %get-tuple-element.48.q.refs_0_, bf16[128,512]{1,0:T(8,128)(2,1)S(1)} %collective-permute-done.13.seen_a.refs_1_, ...), custom_call_target="tpu_custom_call" | custom-call | bytes 5535000 | tf_op jit(solution)/shard_map/key_part/pallas_call | solution.py:76
  50.2 1.1 %collective-permute-done.17.message = bf16[144,512]{1,0:T(8,128)(2,1)S(1)} collective-permute-done((bf16[144,512]{1,0:T(8,128)(2,1)S(1)}, bf16[144,512]{1,0:T(8,128)(2,1)S(1)}, u32[]{:S(2)}, u32[]{:S(2)}) %collective-permute-start.17) | collective-permute-done | bytes 147488 | tf_op jit(solution)/shard_map/ppermute | solution.py:29
  51.3 1.0 %key_grad.1 = (bf16[128,512]{1,0:T(8,128)(2,1)}, bf16[128,512]{1,0:T(8,128)(2,1)}) custom-call(bf16[256,512]{1,0:T(8,128)(2,1)S(1)} %pad_add_fusion.1.own, bf16[128,512]{1,0:T(8,128)(2,1)S(1)} %collective-permute-done.14.seen_b.refs_4_.query, bf16[144,512]{1,0:T(8,128)(2,1)S(1)} %collective-permute-done.17.message, f32[128,512]{1,0:T(8,128)S(1)} %get-tuple-element.68.late, ...), custom_call_target="tpu_custom_call" | custom-call | bytes 3690000 | tf_op jit(solution)/shard_map/key_grad/pallas_call | solution.py:76
  (4 shorter events, 0.1 us)
Async XLA Ops:
  0.6 12.3 %copy-start.2 = (bf16[128,512]{1,0:T(8,128)(2,1)S(1)}, bf16[128,512]{1,0:T(8,128)(2,1)}, u32[]{:S(2)}) copy-start(bf16[128,512]{1,0:T(8,128)(2,1)} %param.13) | copy-start | bytes 393220
  0.6 14.4 %copy-start.1 = (f32[31,512]{1,0:T(8,128)S(1)}, f32[31,512]{1,0:T(8,128)}, u32[]{:S(2)}) copy-start(f32[31,512]{1,0:T(8,128)} %taps.3) | copy-start | bytes 190468
  0.7 18.5 %copy-start = (bf16[512,2048]{1,0:T(8,128)(2,1)S(1)}, bf16[512,2048]{1,0:T(8,128)(2,1)}, u32[]{:S(2)}) copy-start(bf16[512,2048]{1,0:T(8,128)(2,1)} %weight.5) | copy-start | bytes 6291460
  1.8 9.4 %collective-permute-start = (bf16[256,512]{1,0:T(8,128)(2,1)S(1)}, bf16[256,512]{1,0:T(8,128)(2,1)S(1)}, u32[]{:S(2)}, u32[]{:S(2)}) collective-permute-start(bf16[256,512]{1,0:T(8,128)(2,1)S(1)} %pad_add_fusion.1.own), channel_id=1, source_target_pairs={{8,0},{16,8},{24,16},{28,24},{20,28},{12,20},{4,12},{0,4},{9,1},{1... | collective-permute-start | bytes 786440 | tf_op jit(solution)/shard_map/ppermute | solution.py:40
  4.8 10.3 %collective-permute-start.2 = (bf16[256,512]{1,0:T(8,128)(2,1)S(1)}, bf16[256,512]{1,0:T(8,128)(2,1)S(1)}, u32[]{:S(2)}, u32[]{:S(2)}) collective-permute-start(bf16[256,512]{1,0:T(8,128)(2,1)S(1)} %pad_add_fusion.1.own), channel_id=1, source_target_pairs={{0,1},{1,0},{2,3},{3,2},{4,5},{5,4},{6,7},{7,6},{8,12},{9,13},{10,... | collective-permute-start | bytes 786440 | tf_op jit(solution)/shard_map/ppermute | solution.py:51
  4.8 10.6 %collective-permute-start.3 = (bf16[256,512]{1,0:T(8,128)(2,1)S(1)}, bf16[256,512]{1,0:T(8,128)(2,1)S(1)}, u32[]{:S(2)}, u32[]{:S(2)}) collective-permute-start(bf16[256,512]{1,0:T(8,128)(2,1)S(1)} %pad_add_fusion.1.own), channel_id=1, source_target_pairs={{0,8},{8,16},{16,24},{24,28},{28,20},{20,12},{12,4},{4,0},{1,9},{9... | collective-permute-start | bytes 786440 | tf_op jit(solution)/shard_map/ppermute | solution.py:40
  11.2 7.9 %collective-permute-start.1 = (bf16[256,512]{1,0:T(8,128)(2,1)S(1)}, bf16[256,512]{1,0:T(8,128)(2,1)S(1)}, u32[]{:S(2)}, u32[]{:S(2)}) collective-permute-start(bf16[256,512]{1,0:T(8,128)(2,1)S(1)} %turn.1.seen.second), channel_id=1, source_target_pairs={{0,4},{4,0},{8,12},{12,8},{16,20},{20,16},{24,28},{28,24},{1,5},{5... | collective-permute-start | bytes 786440 | tf_op jit(solution)/shard_map/ppermute | solution.py:29
  12.9 7.1 %collective-permute-start.5 = (bf16[128,512]{1,0:T(8,128)(2,1)S(1)}, bf16[128,512]{1,0:T(8,128)(2,1)S(1)}, u32[]{:S(2)}, u32[]{:S(2)}) collective-permute-start(bf16[128,512]{1,0:T(8,128)(2,1)S(1)} %copy-done.2), channel_id=1, source_target_pairs={{0,2},{1,3},{2,0},{3,1},{4,6},{5,7},{6,4},{7,5},{8,10},{9,11},{10,... | collective-permute-start | bytes 393224 | tf_op jit(solution)/shard_map/ppermute | solution.py:29
  14.5 5.9 %collective-permute-start.4 = (bf16[128,512]{1,0:T(8,128)(2,1)S(1)}, bf16[128,512]{1,0:T(8,128)(2,1)S(1)}, u32[]{:S(2)}, u32[]{:S(2)}) collective-permute-start(bf16[128,512]{1,0:T(8,128)(2,1)S(1)} %get-tuple-element.39.q), channel_id=1, source_target_pairs={{8,0},{16,8},{24,16},{28,24},{20,28},{12,20},{4,12},{0,4},{9,1},{1... | collective-permute-start | bytes 393224 | tf_op jit(solution)/shard_map/ppermute | solution.py:40
  15.1 4.9 %collective-permute-start.6 = (f32[31,512]{1,0:T(8,128)S(1)}, f32[31,512]{1,0:T(8,128)S(1)}, u32[]{:S(2)}, u32[]{:S(2)}) collective-permute-start(f32[31,512]{1,0:T(8,128)S(1)} %copy-done.1), channel_id=1, source_target_pairs={{0,2},{1,3},{2,0},{3,1},{4,6},{5,7},{6,4},{7,5},{8,10},{9,11},{10,... | collective-permute-start | bytes 190472 | tf_op jit(solution)/shard_map/ppermute | solution.py:29
  20.5 1.6 %collective-permute-start.7 = (bf16[128,1024]{1,0:T(8,128)(2,1)S(1)}, bf16[128,1024]{1,0:T(8,128)(2,1)S(1)}, u32[]{:S(2)}, u32[]{:S(2)}) collective-permute-start(bf16[128,1024]{1,0:T(8,128)(2,1)S(1)} %get-tuple-element.45), channel_id=1, source_target_pairs={{0,1},{1,0},{2,3},{3,2},{4,5},{5,4},{6,7},{7,6},{8,9},{9,8},{10,11... | collective-permute-start | bytes 786440 | tf_op jit(solution)/shard_map/ppermute | solution.py:29
  22.2 11.3 %collective-permute-start.11 = (bf16[128,1024]{1,0:T(8,128)(2,1)S(1)}, bf16[128,1024]{1,0:T(8,128)(2,1)S(1)}, u32[]{:S(2)}, u32[]{:S(2)}) collective-permute-start(bf16[128,1024]{1,0:T(8,128)(2,1)S(1)} %get-tuple-element.53.chip), channel_id=1, source_target_pairs={{0,2},{1,3},{2,0},{3,1},{4,6},{5,7},{6,4},{7,5},{8,10},{9,11},{10,... | collective-permute-start | bytes 786440 | tf_op jit(solution)/shard_map/ppermute | solution.py:29
  23.8 6.7 %collective-permute-start.8 = (bf16[48,1024]{1,0:T(8,128)(2,1)S(1)}, bf16[48,1024]{1,0:T(8,128)(2,1)S(1)}, u32[]{:S(2)}, u32[]{:S(2)}) collective-permute-start(bf16[48,1024]{1,0:T(8,128)(2,1)S(1)} %get-tuple-element.49), channel_id=1, source_target_pairs={{0,4},{4,0},{8,12},{12,8},{16,20},{20,16},{24,28},{28,24},{1,5},{5... | collective-permute-start | bytes 294920 | tf_op jit(solution)/shard_map/ppermute | solution.py:29
  26.2 4.2 %collective-permute-start.9 = (bf16[48,1024]{1,0:T(8,128)(2,1)S(1)}, bf16[48,1024]{1,0:T(8,128)(2,1)S(1)}, u32[]{:S(2)}, u32[]{:S(2)}) collective-permute-start(bf16[48,1024]{1,0:T(8,128)(2,1)S(1)} %get-tuple-element.50), channel_id=1, source_target_pairs={{0,1},{1,0},{2,3},{3,2},{4,8},{5,9},{6,10},{7,11},{8,4},{9,5},{10,... | collective-permute-start | bytes 294920 | tf_op jit(solution)/shard_map/ppermute | solution.py:51
  26.2 7.3 %collective-permute-start.12 = (bf16[128,512]{1,0:T(8,128)(2,1)S(1)}, bf16[128,512]{1,0:T(8,128)(2,1)S(1)}, u32[]{:S(2)}, u32[]{:S(2)}) collective-permute-start(bf16[128,512]{1,0:T(8,128)(2,1)S(1)} %get-tuple-element.48.q.refs_0_), channel_id=1, source_target_pairs={{0,8},{8,16},{16,24},{24,28},{28,20},{20,12},{12,4},{4,0},{1,9},{9... | collective-permute-start | bytes 393224 | tf_op jit(solution)/shard_map/ppermute | solution.py:40
  27.7 8.6 %collective-permute-start.13 = (bf16[128,512]{1,0:T(8,128)(2,1)S(1)}, bf16[128,512]{1,0:T(8,128)(2,1)S(1)}, u32[]{:S(2)}, u32[]{:S(2)}) collective-permute-start(bf16[128,512]{1,0:T(8,128)(2,1)S(1)} %get-tuple-element.48.q.refs_0_), channel_id=1, source_target_pairs={{0,1},{1,0},{2,3},{3,2},{4,5},{5,4},{6,7},{7,6},{8,12},{9,13},{10,... | collective-permute-start | bytes 393224 | tf_op jit(solution)/shard_map/ppermute | solution.py:51
  30.4 5.9 %collective-permute-start.10 = (bf16[64,1024]{1,0:T(8,128)(2,1)S(1)}, bf16[64,1024]{1,0:T(8,128)(2,1)S(1)}, u32[]{:S(2)}, u32[]{:S(2)}) collective-permute-start(bf16[64,1024]{1,0:T(8,128)(2,1)S(1)} %get-tuple-element.52.ends), channel_id=1, source_target_pairs={{0,2},{1,3},{2,0},{3,1},{4,6},{5,7},{6,4},{7,5},{8,10},{9,11},{10,... | collective-permute-start | bytes 393224 | tf_op jit(solution)/shard_map/ppermute | solution.py:29
  31.0 5.4 %collective-permute-start.14 = (bf16[128,512]{1,0:T(8,128)(2,1)S(1)}, bf16[128,512]{1,0:T(8,128)(2,1)S(1)}, u32[]{:S(2)}, u32[]{:S(2)}) collective-permute-start(bf16[128,512]{1,0:T(8,128)(2,1)S(1)} %get-tuple-element.58), channel_id=1, source_target_pairs={{0,4},{4,0},{8,12},{12,8},{16,20},{20,16},{24,28},{28,24},{1,5},{5... | collective-permute-start | bytes 393224 | tf_op jit(solution)/shard_map/ppermute | solution.py:29
  37.6 1.6 %collective-permute-start.15 = (bf16[128,1024]{1,0:T(8,128)(2,1)S(1)}, bf16[128,1024]{1,0:T(8,128)(2,1)S(1)}, u32[]{:S(2)}, u32[]{:S(2)}) collective-permute-start(bf16[128,1024]{1,0:T(8,128)(2,1)S(1)} %get-tuple-element.59.own.grad_here), channel_id=1, source_target_pairs={{0,1},{1,0},{2,3},{3,2},{4,5},{5,4},{6,7},{7,6},{8,9},{9,8},{10,11... | collective-permute-start | bytes 786440 | tf_op jit(solution)/shard_map/ppermute | solution.py:29
  39.8 5.9 %collective-permute-start.16 = (bf16[144,512]{1,0:T(8,128)(2,1)S(1)}, bf16[144,512]{1,0:T(8,128)(2,1)S(1)}, u32[]{:S(2)}, u32[]{:S(2)}) collective-permute-start(bf16[144,512]{1,0:T(8,128)(2,1)S(1)} %get-tuple-element.62.message.refs_5_), channel_id=1, source_target_pairs={{8,0},{16,8},{24,16},{28,24},{20,28},{12,20},{4,12},{0,4},{9,1},{1... | collective-permute-start | bytes 442376 | tf_op jit(solution)/shard_map/ppermute | solution.py:40
  41.9 7.4 %collective-permute-start.18 = (bf16[144,512]{1,0:T(8,128)(2,1)S(1)}, bf16[144,512]{1,0:T(8,128)(2,1)S(1)}, u32[]{:S(2)}, u32[]{:S(2)}) collective-permute-start(bf16[144,512]{1,0:T(8,128)(2,1)S(1)} %get-tuple-element.62.message.refs_5_), channel_id=1, source_target_pairs={{0,1},{1,0},{2,3},{3,2},{4,5},{5,4},{6,7},{7,6},{8,12},{9,13},{10,... | collective-permute-start | bytes 442376 | tf_op jit(solution)/shard_map/ppermute | solution.py:51
  41.9 7.4 %collective-permute-start.19 = (bf16[144,512]{1,0:T(8,128)(2,1)S(1)}, bf16[144,512]{1,0:T(8,128)(2,1)S(1)}, u32[]{:S(2)}, u32[]{:S(2)}) collective-permute-start(bf16[144,512]{1,0:T(8,128)(2,1)S(1)} %get-tuple-element.62.message.refs_5_), channel_id=1, source_target_pairs={{0,8},{8,16},{16,24},{24,28},{28,20},{20,12},{12,4},{4,0},{1,9},{9... | collective-permute-start | bytes 442376 | tf_op jit(solution)/shard_map/ppermute | solution.py:40
  45.8 5.6 %collective-permute-start.17 = (bf16[144,512]{1,0:T(8,128)(2,1)S(1)}, bf16[144,512]{1,0:T(8,128)(2,1)S(1)}, u32[]{:S(2)}, u32[]{:S(2)}) collective-permute-start(bf16[144,512]{1,0:T(8,128)(2,1)S(1)} %collective-permute-done.16.refs_8_), channel_id=1, source_target_pairs={{0,4},{4,0},{8,12},{12,8},{16,20},{20,16},{24,28},{28,24},{1,5},{5... | collective-permute-start | bytes 442376 | tf_op jit(solution)/shard_map/ppermute | solution.py:29

commit v13 on v12

--- a/solution.py
+++ b/solution.py
@@ -59,11 +59,10 @@
     return total_swap(block, lambda i, count: ((i + 1) ^ 1) - 1 if 0 < i < count - 1 else None)
 
 
-def window_of(block, before_relay=lambda second: second):
+def window_of(block):
     second = ring(block, 1)
     first = ring(block, 0)
     near = inner_swap(block)
-    second = before_relay(second)
     return near, first, second, pair_swap(second, "ctx", 1)
 
 
@@ -117,6 +116,16 @@
     return jnp.concatenate([block[rows, cols] for block in blocks], axis=0)
 
 
+def window_keys(joined, single, frames, cols):
+    return jnp.concatenate([b[0:frames, cols] for b in joined] + [b[:, cols] for b in single], axis=0)
+
+
+def window_values(joined, single, frames, cols):
+    return jnp.concatenate(
+        [b[frames : 2 * frames, cols] for b in joined] + [b[:, cols] for b in single], axis=0
+    )
+
+
 def with_ones(values):
     return jnp.concatenate([values, jnp.ones_like(values)], axis=1)
 
@@ -172,45 +181,47 @@
         part[...] = joined[k * frames : (k + 1) * frames, :]
 
 
-def forward_body(scale, q, own, near, first, second, *refs):
+def forward_body(scale, q, own, near, first, second_key, second_value, *refs):
     sums, tops, totals = refs[-3:]
     frames, width = q.shape
     heads = columns(width)
-    blocks = (near, own, first, second)
+    blocks = (near, own, first)
     biases = (bias_of(near_swapped()), None, None, None)
-    keys, values = slice(0, frames), slice(frames, 2 * frames)
-    scores = [dot_nt(q[:, c], stacked(blocks, keys, c)) * scale for c in heads]
+    scores = [dot_nt(q[:, c], window_keys(blocks, (second_key,), frames, c)) * scale for c in heads]
     scores = [by_block(s, biases) for s in scores]
     top = [jnp.max(s, axis=1, keepdims=True) for s in scores]
     probs = [jnp.exp(s - t).astype(BF16) for s, t in zip(scores, top)]
-    summed = [dot_nn(p, with_ones(stacked(blocks, values, c))) for p, c in zip(probs, heads)]
+    summed = [dot_nn(p, with_ones(window_values(blocks, (second_value,), frames, c))) for p, c in zip(probs, heads)]
     for c, t, s in zip(heads, top, summed):
         tops[:, c] = jnp.broadcast_to(t, (frames, HDIM))
         sums[:, c] = s[:, 0:HDIM]
         totals[:, c] = s[:, HDIM:]
 
 
-def project_body(scale, q, relay, sums, tops, totals, weight, att, lse, send, keep):
+def project_body(scale, q, relay_key, relay_value, sums, tops, totals, weight, att, lse, send):
     frames, width = q.shape
     heads = columns(width)
     bias = bias_of(far_there())
-    scores = [dot_nt(q[:, c], relay[0:frames, c]) * scale + bias for c in heads]
+    scores = [dot_nt(q[:, c], relay_key[:, c]) * scale + bias for c in heads]
     before = [tops[:, c] for c in heads]
     top = [jnp.maximum(b, jnp.max(s, axis=1, keepdims=True)) for b, s in zip(before, scores)]
     shrink = [jnp.exp(b - t) for b, t in zip(before, top)]
     probs = [jnp.exp(s - t).astype(BF16) for s, t in zip(scores, top)]
-    late = [dot_nn(p, with_ones(relay[frames : 2 * frames, c])) for p, c in zip(probs, heads)]
+    late = [dot_nn(p, with_ones(relay_value[:, c])) for p, c in zip(probs, heads)]
     total = [totals[:, c] * k + s[:, HDIM:] for c, k, s in zip(heads, shrink, late)]
     summed = [sums[:, c] * k + s[:, 0:HDIM] for c, k, s in zip(heads, shrink, late)]
     attended = jnp.concatenate([(s * (1.0 / t)).astype(BF16) for s, t in zip(summed, total)], axis=1)
     sent = [dot_nn(attended, weight_columns(weight, flip)).astype(BF16) for flip in (1, 3)]
-    kept = [dot_nn(attended, weight_columns(weight, flip)).astype(BF16) for flip in (0, 2)]
     logs = [t + jnp.log(n) for t, n in zip(top, total)]
     att[...] = attended
     send[...] = jnp.concatenate(sent, axis=1)
-    keep[...] = jnp.concatenate(kept, axis=1)
     for c, part in zip(heads, logs):
         lse[:, c] = part
+
+
+def project_own_body(att, weight, keep):
+    kept = [dot_nn(att[...], weight_columns(weight, flip)).astype(BF16) for flip in (0, 2)]
+    keep[...] = jnp.concatenate(kept, axis=1)
 
 
 def pass_body(send, q_second, seen_a, seen_b, send_copy, second_copy):
@@ -403,7 +414,8 @@
 
 
 def query_grad_body(
-    scale, q, own, near, first, second, relay, message, lse, delta, output_here, grad_here,
+    scale, q, own, near, first, second_key, second_value, relay_key, relay_value, message, lse, delta,
+    output_here, grad_here,
     output, grad_input, grad_query, held, sems,
 ):
     writes = [
@@ -414,12 +426,12 @@
         write.start()
     frames, width = q.shape
     heads = columns(width)
-    blocks = (near, own, first, second, relay)
+    blocks = (near, own, first)
     biases = (bias_of(near_swapped()), None, None, None, bias_of(far_there()))
-    above, below = slice(0, frames), slice(frames, 2 * frames)
-    keys = [stacked(blocks, above, c) for c in heads]
+    keys = [window_keys(blocks, (second_key, relay_key), frames, c) for c in heads]
+    values = [window_values(blocks, (second_value, relay_value), frames, c) for c in heads]
     scores = [dot_nt(q[:, c], k) * scale for c, k in zip(heads, keys)]
-    dots = [dot_nt(message[0:frames, c], stacked(blocks, below, c)) for c in heads]
+    dots = [dot_nt(message[0:frames, c], v) for c, v in zip(heads, values)]
     probs = [jnp.exp(by_block(s, biases, [lse[:, c]] * 5)) for c, s in zip(heads, scores)]
     drops = [by_block(d, (None,) * 5, [delta[:, c]] * 5) for c, d in zip(heads, dots)]
     grads = [(p * d * scale).astype(BF16) for p, d in zip(probs, drops)]
@@ -495,33 +507,33 @@
         lax.pad(rows, zero, ((k * frames, (2 - k) * frames, 0), (0, 0, 0)))
         for k, rows in enumerate((query_rows, inputs, cotangent))
     )
-    near, first, second, relay = window_of(
-        kv,
-        lambda second: kernel_call(
-            turn_body, (shaped(kv.shape, BF16),), (second, joined), 0.1, "turn", 1
-        )[0],
-    )
+    second_key, second_value = ring(key_rows, 1), ring(value_rows, 1)
+    near, first = inner_swap(kv), ring(kv, 0)
+    (second_key,) = kernel_call(turn_body, (tile,), (second_key, joined), 0.1, "turn", 1)
+    relay_key = pair_swap(second_key, "ctx", 1)
+    relay_value = pair_swap(second_value, "ctx", 1)
     cot_other = pair_swap(cotangent, "mp", 2)
     taps_other = pair_swap(kernel, "mp", 2)
     query, inputs, cotangent = kernel_call(
-        split_body, (tile, tile, tile), (joined, second), 0.1, "split", 1
+        split_body, (tile, tile, tile), (joined, second_value), 0.1, "split", 1
     )
     q_second = ring(query, 1)
     sums, tops, totals = kernel_call(
         functools.partial(forward_body, scale),
         (tile32, tile32, tile32),
-        (query, kv, near, first, second),
+        (query, kv, near, first, second_key, second_value),
         1.0, "forward",
     )
-    att, lse, send, keep = kernel_call(
+    att, lse, send = kernel_call(
         functools.partial(project_body, scale),
-        (tile, tile32, both, both),
-        (query, relay, sums, tops, totals, out_weight),
+        (tile, tile32, both),
+        (query, relay_key, relay_value, sums, tops, totals, out_weight),
         1.0, "project",
     )
 
     send, q_second = kernel_call(pass_body, (both, tile), (send, q_second, cot_other, taps_other), 0.1, "pass", 2)
     core = pair_swap(send, "mp", 1)
+    (keep,) = kernel_call(project_own_body, (both,), (att, out_weight), 0.4, "project_own")
     chip, rim_up, rim_down, q_own = kernel_call(
         join_body,
         (both, rim, rim, tile),
@@ -529,8 +541,8 @@
         0.2, "join",
     )
     across = pair_swap(chip, "mp", 2)
+    rim_near = pair_swap(rim_up, "ctx", 1)
     rim_far = outer_swap(rim_down)
-    rim_near = pair_swap(rim_up, "ctx", 1)
     ends, q_handed = kernel_call(
         stack_body,
         (shaped((2 * wide, 2 * width), BF16), tile),
@@ -570,7 +582,8 @@
     output, grad_input, grad_query = kernel_call(
         functools.partial(query_grad_body, scale),
         (tile, tile, tile),
-        (q_own, kv, near, first, second, relay, message, lse, delta, output_here, grad_here),
+        (q_own, kv, near, first, second_key, second_value, relay_key, relay_value)
+        + (message, lse, delta, output_here, grad_here),
         1.8, "query_grad", 0,
         [pltpu.VMEM((frames, width), BF16), pltpu.SemaphoreType.DMA((3,))], HBM,
     )

time: 52.5 us -> 53.8 us (1.025)
  starting transfers between devices: 24.7 us -> 25.5 us
    ppermute x6 -> x7, starting transfers between devices: 11.9 us -> 13.7 us  [ring(): return lax.ppermute(block, 'ctx', ring_routes(lax.axis_size('ctx'))[way])]
    ppermute x10 -> x11, starting transfers between devices: 12.9 us -> 11.3 us  [pair_swap(): lax.ppermute(block, axis, [(i, i ^ bit) for i in range(lax.axis_size(axis...]
    ppermute x6 -> x7, waiting for transfers between devices: 4.86 us -> 6.4 us  [ring(): return lax.ppermute(block, 'ctx', ring_routes(lax.axis_size('ctx'))[way])]
    ppermute x10 -> x11, waiting for transfers between devices: 9.59 us -> 8.39 us  [pair_swap(): lax.ppermute(block, axis, [(i, i ^ bit) for i in range(lax.axis_size(axis...]
    pallas_call x14 -> x15, Pallas kernels: 10.1 us -> 10.3 us  [kernel_call(): pl.pallas_call(body, out_shape=outs, in_specs=[VMEM] * (len(args) - unrea...]
  transfers between devices with their start and end apart: 20 -> 22, of which waited for: 9 -> 11; matrix products, arithmetic and copies ran while one was open for 2% -> 2% of each run, Pallas kernels for 14% -> 14%
where the time goes in v13:
time: 53.8 us; the launch traced here: 53.6 us
  starting transfers between devices  25.5 us (47%)
  waiting for transfers between devices  14.8 us (28%)
  Pallas kernels  10.3 us (19%)
  other arithmetic  2.19 us (4%)
  between operations  0.82 us (2%)
    ppermute x7, starting transfers between devices, ring(): return lax.ppermute(block, 'ctx', ring_routes(lax.axis_size('ctx'))[way])  13.7 us
    ppermute x11, starting transfers between devices, pair_swap(): lax.ppermute(block, axis, [(i, i ^ bit) for i in range(lax.axis_size(axis...  11.3 us
    pallas_call x15, Pallas kernels, kernel_call(): pl.pallas_call(body, out_shape=outs, in_specs=[VMEM] * (len(args) - unrea...  10.3 us
    ppermute x11, waiting for transfers between devices, pair_swap(): lax.ppermute(block, axis, [(i, i ^ bit) for i in range(lax.axis_size(axis...  8.39 us
    ppermute x7, waiting for transfers between devices, ring(): return lax.ppermute(block, 'ctx', ring_routes(lax.axis_size('ctx'))[way])  6.4 us
    add x1, other arithmetic, per_device(): lax.pad(key_rows, zero, ((0, frames, 0), (0, 0, 0)))  1.14 us
  transfers between devices with their start and end apart: 22, of which 11 were waited for; matrix products, arithmetic and copies ran while one was open for 2% of the time, Pallas kernels for 14%

profile of v13, /device:TPU:0, one launch (start us, length us, event | category | flops | bytes accessed | tf_op | source)
XLA Modules:
  0.0 53.6 jit_solution(16525801442647398925)
XLA Ops:
  0.6 0.0 copy-start.1
  0.6 0.0 copy-start
  0.7 1.1 %pad_add_fusion.1.own = bf16[256,512]{1,0:T(8,128)(2,1)S(1)} fusion(bf16[128,512]{1,0:T(8,128)(2,1)} %param.9, bf16[128,512]{1,0:T(8,128)(2,1)} %param.8), kind=kLoop, calls=%fused_computation.1 | loop fusion | flops 524288 | bytes 524288 | tf_op jit(solution)/shard_map/add | solution.py:503
  1.8 0.5 collective-permute-start.4
  2.3 4.1 %collective-permute-start.5 = (bf16[256,512]{1,0:T(8,128)(2,1)S(1)}, bf16[256,512]{1,0:T(8,128)(2,1)S(1)}, u32[]{:S(2)}, u32[]{:S(2)}) collective-permute-start(bf16[256,512]{1,0:T(8,128)(2,1)S(1)} %pad_add_fusion.1.own), channel_id=1, source_target_pairs={{0,8},{8,16},{16,24},{24,28},{28,20},{20,12},{12,4},{4,0},{1,9},{9... | collective-permute-start | bytes 786440 | tf_op jit(solution)/shard_map/ppermute | solution.py:40
  6.4 0.0 collective-permute-start.1
  6.4 0.5 collective-permute-start
  6.9 1.1 %pad_add_fusion.joined.seen = bf16[384,512]{1,0:T(8,128)(2,1)S(1)} fusion(bf16[128,512]{1,0:T(8,128)(2,1)} %param.13, bf16[128,512]{1,0:T(8,128)(2,1)} %param.10, bf16[128,512]{1,0:T(8,128)(2,1)} %param.7), kind=kLoop, calls=%fused_computation | loop fusion | flops 1179648 | bytes 786432 | tf_op jit(solution)/shard_map/add | solution.py:506
  8.0 4.7 %collective-permute-done.1.block = bf16[128,512]{1,0:T(8,128)(2,1)S(1)} collective-permute-done((bf16[128,512]{1,0:T(8,128)(2,1)}, bf16[128,512]{1,0:T(8,128)(2,1)S(1)}, u32[]{:S(2)}, u32[]{:S(2)}) %collective-permute-start.1) | collective-permute-done | bytes 131104 | tf_op jit(solution)/shard_map/ppermute | solution.py:40
  12.7 0.3 collective-permute-start.2
  13.0 1.0 %collective-permute-done.seen.second_value = bf16[128,512]{1,0:T(8,128)(2,1)S(1)} collective-permute-done((bf16[128,512]{1,0:T(8,128)(2,1)}, bf16[128,512]{1,0:T(8,128)(2,1)S(1)}, u32[]{:S(2)}, u32[]{:S(2)}) %collective-permute-start) | collective-permute-done | bytes 131104 | tf_op jit(solution)/shard_map/ppermute | solution.py:40
  14.1 1.6 %collective-permute-start.3 = (bf16[128,512]{1,0:T(8,128)(2,1)S(1)}, bf16[128,512]{1,0:T(8,128)(2,1)S(1)}, u32[]{:S(2)}, u32[]{:S(2)}) collective-permute-start(bf16[128,512]{1,0:T(8,128)(2,1)S(1)} %collective-permute-done.seen.second_value), channel_id=1, source_target_pairs={{0,4},{4,0},{8,12},{12,8},{16,20},{20,16},{24,28},{28,24},{1,5},{5... | collective-permute-start | bytes 393224 | tf_op jit(solution)/shard_map/ppermute | solution.py:29
  15.7 1.5 %collective-permute-start.7 = (bf16[128,512]{1,0:T(8,128)(2,1)}, bf16[128,512]{1,0:T(8,128)(2,1)S(1)}, u32[]{:S(2)}, u32[]{:S(2)}) collective-permute-start(bf16[128,512]{1,0:T(8,128)(2,1)} %param.13), channel_id=1, source_target_pairs={{0,2},{1,3},{2,0},{3,1},{4,6},{5,7},{6,4},{7,5},{8,10},{9,11},{10,... | collective-permute-start | bytes 393224 | tf_op jit(solution)/shard_map/ppermute | solution.py:29
  17.3 0.0 collective-permute-done.4.near
  17.3 0.4 collective-permute-start.6
  17.7 0.0 collective-permute-done.5.first
  17.7 0.0 copy-done.1
  17.7 0.5 collective-permute-start.8
  18.2 0.6 %forward.1 = (f32[128,512]{1,0:T(8,128)S(1)}, f32[128,512]{1,0:T(8,128)S(1)}, f32[128,512]{1,0:T(8,128)S(1)}) custom-call(bf16[128,512]{1,0:T(8,128)(2,1)S(1)} %get-tuple-element.38.q, bf16[256,512]{1,0:T(8,128)(2,1)S(1)} %pad_add_fusion.1.own, bf16[256,512]{1,0:T(8,128)(2,1)S(1)} %collective-permute-done.4.near, ...), custom_call_target="tpu_custom_call" | custom-call | bytes 3690000 | tf_op jit(solution)/shard_map/forward/pallas_call | solution.py:75
  18.8 0.0 collective-permute-done.2.relay_key
  18.8 0.4 collective-permute-done.3.relay_value
  19.2 0.0 copy-done
  19.2 0.7 %project.1 = (bf16[128,512]{1,0:T(8,128)(2,1)S(1)}, f32[128,512]{1,0:T(8,128)S(1)}, bf16[128,1024]{1,0:T(8,128)(2,1)S(1)}) custom-call(bf16[128,512]{1,0:T(8,128)(2,1)S(1)} %get-tuple-element.38.q, bf16[128,512]{1,0:T(8,128)(2,1)S(1)} %collective-permute-done.2.relay_key, bf16[128,512]{1,0:T(8,128)(2,1)S(1)} %collective-permute-done.3.relay_value, ...), custom_call_target="tpu_custom_call" | custom-call | bytes 3690000 | tf_op jit(solution)/shard_map/project/pallas_call | solution.py:75
  19.9 2.0 %collective-permute-done.8.seen_b.taps_other = f32[31,512]{1,0:T(8,128)S(1)} collective-permute-done((f32[31,512]{1,0:T(8,128)S(1)}, f32[31,512]{1,0:T(8,128)S(1)}, u32[]{:S(2)}, u32[]{:S(2)}) %collective-permute-start.8) | collective-permute-done | bytes 63520 | tf_op jit(solution)/shard_map/ppermute | solution.py:29
  22.0 0.0 collective-permute-done.7.seen_a.cot_other
  22.0 0.3 collective-permute-done.6.q_second
  22.3 0.1 collective-permute-start.9
  22.4 0.3 project_own.1.keep
  22.7 1.2 %collective-permute-done.9.core = bf16[128,1024]{1,0:T(8,128)(2,1)S(1)} collective-permute-done((bf16[128,1024]{1,0:T(8,128)(2,1)S(1)}, bf16[128,1024]{1,0:T(8,128)(2,1)S(1)}, u32[]{:S(2)}, u32[]{:S(2)}) %collective-permute-start.9) | collective-permute-done | bytes 262176 | tf_op jit(solution)/shard_map/ppermute | solution.py:29
  23.9 0.1 join.1
  24.0 0.9 %collective-permute-start.13 = (bf16[128,1024]{1,0:T(8,128)(2,1)S(1)}, bf16[128,1024]{1,0:T(8,128)(2,1)S(1)}, u32[]{:S(2)}, u32[]{:S(2)}) collective-permute-start(bf16[128,1024]{1,0:T(8,128)(2,1)S(1)} %get-tuple-element.52.chip), channel_id=1, source_target_pairs={{0,2},{1,3},{2,0},{3,1},{4,6},{5,7},{6,4},{7,5},{8,10},{9,11},{10,... | collective-permute-start | bytes 786440 | tf_op jit(solution)/shard_map/ppermute | solution.py:29
  24.9 1.2 %collective-permute-start.10 = (bf16[48,1024]{1,0:T(8,128)(2,1)S(1)}, bf16[48,1024]{1,0:T(8,128)(2,1)S(1)}, u32[]{:S(2)}, u32[]{:S(2)}) collective-permute-start(bf16[48,1024]{1,0:T(8,128)(2,1)S(1)} %get-tuple-element.48), channel_id=1, source_target_pairs={{0,4},{4,0},{8,12},{12,8},{16,20},{20,16},{24,28},{28,24},{1,5},{5... | collective-permute-start | bytes 294920 | tf_op jit(solution)/shard_map/ppermute | solution.py:29
  26.1 0.0 collective-permute-start.11
  26.1 2.3 %collective-permute-start.14 = (bf16[128,512]{1,0:T(8,128)(2,1)S(1)}, bf16[128,512]{1,0:T(8,128)(2,1)S(1)}, u32[]{:S(2)}, u32[]{:S(2)}) collective-permute-start(bf16[128,512]{1,0:T(8,128)(2,1)S(1)} %get-tuple-element.47.q.refs_0_), channel_id=1, source_target_pairs={{0,8},{8,16},{16,24},{24,28},{28,20},{20,12},{12,4},{4,0},{1,9},{9... | collective-permute-start | bytes 393224 | tf_op jit(solution)/shard_map/ppermute | solution.py:40
  28.4 0.0 collective-permute-start.15
  28.4 2.0 %collective-permute-done.10.rim_near = bf16[48,1024]{1,0:T(8,128)(2,1)S(1)} collective-permute-done((bf16[48,1024]{1,0:T(8,128)(2,1)S(1)}, bf16[48,1024]{1,0:T(8,128)(2,1)S(1)}, u32[]{:S(2)}, u32[]{:S(2)}) %collective-permute-start.10) | collective-permute-done | bytes 98336 | tf_op jit(solution)/shard_map/ppermute | solution.py:29
  30.4 0.0 collective-permute-done.11.rim_far
  30.4 1.4 %collective-permute-start.12 = (bf16[64,1024]{1,0:T(8,128)(2,1)S(1)}, bf16[64,1024]{1,0:T(8,128)(2,1)S(1)}, u32[]{:S(2)}, u32[]{:S(2)}) collective-permute-start(bf16[64,1024]{1,0:T(8,128)(2,1)S(1)} %get-tuple-element.51.ends), channel_id=1, source_target_pairs={{0,2},{1,3},{2,0},{3,1},{4,6},{5,7},{6,4},{7,5},{8,10},{9,11},{10,... | collective-permute-start | bytes 393224 | tf_op jit(solution)/shard_map/ppermute | solution.py:29
  31.8 2.4 %collective-permute-start.16 = (bf16[128,512]{1,0:T(8,128)(2,1)S(1)}, bf16[128,512]{1,0:T(8,128)(2,1)S(1)}, u32[]{:S(2)}, u32[]{:S(2)}) collective-permute-start(bf16[128,512]{1,0:T(8,128)(2,1)S(1)} %get-tuple-element.57), channel_id=1, source_target_pairs={{0,4},{4,0},{8,12},{12,8},{16,20},{20,16},{24,28},{28,24},{1,5},{5... | collective-permute-start | bytes 393224 | tf_op jit(solution)/shard_map/ppermute | solution.py:29
  34.2 0.0 collective-permute-done.14.seen.refs_2_
  34.2 0.0 collective-permute-done.13.across
  34.2 2.8 %conv_inner.1 = (bf16[128,512]{1,0:T(8,128)(2,1)S(1)}, f32[32,512]{1,0:T(8,128)S(1)}, f32[64,1024]{1,0:T(8,128)S(1)}, f32[128,1024]{1,0:T(8,128)S(1)}) custom-call(bf16[128,1024]{1,0:T(8,128)(2,1)S(1)} %get-tuple-element.52.chip, bf16[128,1024]{1,0:T(8,128)(2,1)S(1)} %collective-permute-done.13.across, bf16[128,512]{1,0:T(8,128)(2,1)S(1)} %get-tuple-element.46.cot, ...), custom_call_target="tpu_custom_call" | custom-call | bytes 11439000 | tf_op jit(solution)/shard_map/conv_inner/pallas_call | solution.py:75
  37.0 0.0 collective-permute-done.15.seen_a.refs_1_
  37.1 0.0 collective-permute-done.12.ends_across
  37.1 0.1 collective-permute-done.16.seen_b.refs_4_.query
  37.2 1.1 %conv_edge.1 = (bf16[128,512]{1,0:T(8,128)(2,1)S(1)}, bf16[128,1024]{1,0:T(8,128)(2,1)S(1)}) custom-call(bf16[64,1024]{1,0:T(8,128)(2,1)S(1)} %get-tuple-element.51.ends, bf16[64,1024]{1,0:T(8,128)(2,1)S(1)} %collective-permute-done.12.ends_across, bf16[48,1024]{1,0:T(8,128)(2,1)S(1)} %collective-permute-done.10.rim_near, ...), custom_call_target="tpu_custom_call" | custom-call | bytes 5166000 | tf_op jit(solution)/shard_map/conv_edge/pallas_call | solution.py:75
  38.3 0.1 collective-permute-start.17
  38.4 0.5 upstream_own.1.partial
  38.9 1.0 %collective-permute-done.17.core = bf16[128,1024]{1,0:T(8,128)(2,1)S(1)} collective-permute-done((bf16[128,1024]{1,0:T(8,128)(2,1)S(1)}, bf16[128,1024]{1,0:T(8,128)(2,1)S(1)}, u32[]{:S(2)}, u32[]{:S(2)}) %collective-permute-start.17) | collective-permute-done | bytes 262176 | tf_op jit(solution)/shard_map/ppermute | solution.py:29
  39.9 0.7 %upstream.1 = (bf16[144,512]{1,0:T(8,128)(2,1)S(1)}, f32[128,512]{1,0:T(8,128)S(1)}) custom-call(bf16[128,1024]{1,0:T(8,128)(2,1)S(1)} %collective-permute-done.17.core, bf16[512,2048]{1,0:T(8,128)(2,1)S(1)} %copy-done, bf16[128,512]{1,0:T(8,128)(2,1)S(1)} %get-tuple-element.42.att, f32[128,512]{1,0:T(8,128)S(1)} %get-tuple-element.59.lse, ...), custom_call_target="tpu_custom_call" | custom-call | bytes 2214000 | tf_op jit(solution)/shard_map/upstream/pallas_call | solution.py:75
  40.6 2.1 %collective-permute-start.18 = (bf16[144,512]{1,0:T(8,128)(2,1)S(1)}, bf16[144,512]{1,0:T(8,128)(2,1)S(1)}, u32[]{:S(2)}, u32[]{:S(2)}) collective-permute-start(bf16[144,512]{1,0:T(8,128)(2,1)S(1)} %get-tuple-element.60.message.refs_5_), channel_id=1, source_target_pairs={{8,0},{16,8},{24,16},{28,24},{20,28},{12,20},{4,12},{0,4},{9,1},{1... | collective-permute-start | bytes 442376 | tf_op jit(solution)/shard_map/ppermute | solution.py:40
  42.6 0.0 collective-permute-start.20
  42.6 4.3 %collective-permute-start.21 = (bf16[144,512]{1,0:T(8,128)(2,1)S(1)}, bf16[144,512]{1,0:T(8,128)(2,1)S(1)}, u32[]{:S(2)}, u32[]{:S(2)}) collective-permute-start(bf16[144,512]{1,0:T(8,128)(2,1)S(1)} %get-tuple-element.60.message.refs_5_), channel_id=1, source_target_pairs={{0,8},{8,16},{16,24},{24,28},{28,20},{20,12},{12,4},{4,0},{1,9},{9... | collective-permute-start | bytes 442376 | tf_op jit(solution)/shard_map/ppermute | solution.py:40
  46.9 0.4 collective-permute-done.18.refs_8_
  47.2 1.3 %collective-permute-start.19 = (bf16[144,512]{1,0:T(8,128)(2,1)S(1)}, bf16[144,512]{1,0:T(8,128)(2,1)S(1)}, u32[]{:S(2)}, u32[]{:S(2)}) collective-permute-start(bf16[144,512]{1,0:T(8,128)(2,1)S(1)} %collective-permute-done.18.refs_8_), channel_id=1, source_target_pairs={{0,4},{4,0},{8,12},{12,8},{16,20},{20,16},{24,28},{28,24},{1,5},{5... | collective-permute-start | bytes 442376 | tf_op jit(solution)/shard_map/ppermute | solution.py:29
  48.5 1.5 %query_grad.1 = (bf16[128,512]{1,0:T(8,128)(2,1)}, bf16[128,512]{1,0:T(8,128)(2,1)}, bf16[128,512]{1,0:T(8,128)(2,1)}) custom-call(bf16[128,512]{1,0:T(8,128)(2,1)S(1)} %get-tuple-element.47.q.refs_0_, bf16[256,512]{1,0:T(8,128)(2,1)S(1)} %pad_add_fusion.1.own, bf16[256,512]{1,0:T(8,128)(2,1)S(1)} %collective-permute-done.4.near, ...), custom_call_target="tpu_custom_call" | custom-call | bytes 6642000 | tf_op jit(solution)/shard_map/query_grad/pallas_call | solution.py:75
  50.1 0.0 collective-permute-done.20.refs_6_
  50.1 0.0 collective-permute-done.21.refs_7_
  50.1 0.9 %key_part.1 = (f32[128,512]{1,0:T(8,128)S(1)}, f32[128,512]{1,0:T(8,128)S(1)}, f32[128,512]{1,0:T(8,128)S(1)}) custom-call(bf16[256,512]{1,0:T(8,128)(2,1)S(1)} %pad_add_fusion.1.own, bf16[128,512]{1,0:T(8,128)(2,1)S(1)} %get-tuple-element.47.q.refs_0_, bf16[128,512]{1,0:T(8,128)(2,1)S(1)} %collective-permute-done.15.seen_a.refs_1_, ...), custom_call_target="tpu_custom_call" | custom-call | bytes 5535000 | tf_op jit(solution)/shard_map/key_part/pallas_call | solution.py:75
  50.9 1.7 %collective-permute-done.19.message = bf16[144,512]{1,0:T(8,128)(2,1)S(1)} collective-permute-done((bf16[144,512]{1,0:T(8,128)(2,1)S(1)}, bf16[144,512]{1,0:T(8,128)(2,1)S(1)}, u32[]{:S(2)}, u32[]{:S(2)}) %collective-permute-start.19) | collective-permute-done | bytes 147488 | tf_op jit(solution)/shard_map/ppermute | solution.py:29
  52.6 1.0 %key_grad.1 = (bf16[128,512]{1,0:T(8,128)(2,1)}, bf16[128,512]{1,0:T(8,128)(2,1)}) custom-call(bf16[256,512]{1,0:T(8,128)(2,1)S(1)} %pad_add_fusion.1.own, bf16[128,512]{1,0:T(8,128)(2,1)S(1)} %collective-permute-done.16.seen_b.refs_4_.query, bf16[144,512]{1,0:T(8,128)(2,1)S(1)} %collective-permute-done.19.message, f32[128,512]{1,0:T(8,128)S(1)} %get-tuple-element.66.late, ...), custom_call_target="tpu_custom_call" | custom-call | bytes 3690000 | tf_op jit(solution)/shard_map/key_grad/pallas_call | solution.py:75
  (4 shorter events, 0.1 us)
Async XLA Ops:
  0.6 17.1 %copy-start.1 = (f32[31,512]{1,0:T(8,128)S(1)}, f32[31,512]{1,0:T(8,128)}, u32[]{:S(2)}) copy-start(f32[31,512]{1,0:T(8,128)} %taps.3) | copy-start | bytes 190468
  0.6 18.6 %copy-start = (bf16[512,2048]{1,0:T(8,128)(2,1)S(1)}, bf16[512,2048]{1,0:T(8,128)(2,1)}, u32[]{:S(2)}) copy-start(bf16[512,2048]{1,0:T(8,128)(2,1)} %weight.7) | copy-start | bytes 6291460
  1.8 15.5 %collective-permute-start.4 = (bf16[256,512]{1,0:T(8,128)(2,1)S(1)}, bf16[256,512]{1,0:T(8,128)(2,1)S(1)}, u32[]{:S(2)}, u32[]{:S(2)}) collective-permute-start(bf16[256,512]{1,0:T(8,128)(2,1)S(1)} %pad_add_fusion.1.own), channel_id=1, source_target_pairs={{0,1},{1,0},{2,3},{3,2},{4,5},{5,4},{6,7},{7,6},{8,12},{9,13},{10,... | collective-permute-start | bytes 786440 | tf_op jit(solution)/shard_map/ppermute | solution.py:51
  2.3 15.4 %collective-permute-start.5 = (bf16[256,512]{1,0:T(8,128)(2,1)S(1)}, bf16[256,512]{1,0:T(8,128)(2,1)S(1)}, u32[]{:S(2)}, u32[]{:S(2)}) collective-permute-start(bf16[256,512]{1,0:T(8,128)(2,1)S(1)} %pad_add_fusion.1.own), channel_id=1, source_target_pairs={{0,8},{8,16},{16,24},{24,28},{28,20},{20,12},{12,4},{4,0},{1,9},{9... | collective-permute-start | bytes 786440 | tf_op jit(solution)/shard_map/ppermute | solution.py:40
  6.4 6.3 %collective-permute-start.1 = (bf16[128,512]{1,0:T(8,128)(2,1)}, bf16[128,512]{1,0:T(8,128)(2,1)S(1)}, u32[]{:S(2)}, u32[]{:S(2)}) collective-permute-start(bf16[128,512]{1,0:T(8,128)(2,1)} %param.8), channel_id=1, source_target_pairs={{8,0},{16,8},{24,16},{28,24},{20,28},{12,20},{4,12},{0,4},{9,1},{1... | collective-permute-start | bytes 393224 | tf_op jit(solution)/shard_map/ppermute | solution.py:40
  6.4 7.7 %collective-permute-start = (bf16[128,512]{1,0:T(8,128)(2,1)}, bf16[128,512]{1,0:T(8,128)(2,1)S(1)}, u32[]{:S(2)}, u32[]{:S(2)}) collective-permute-start(bf16[128,512]{1,0:T(8,128)(2,1)} %param.9), channel_id=1, source_target_pairs={{8,0},{16,8},{24,16},{28,24},{20,28},{12,20},{4,12},{0,4},{9,1},{1... | collective-permute-start | bytes 393224 | tf_op jit(solution)/shard_map/ppermute | solution.py:40
  12.7 6.2 %collective-permute-start.2 = (bf16[128,512]{1,0:T(8,128)(2,1)S(1)}, bf16[128,512]{1,0:T(8,128)(2,1)S(1)}, u32[]{:S(2)}, u32[]{:S(2)}) collective-permute-start(bf16[128,512]{1,0:T(8,128)(2,1)S(1)} %turn.1.second_key), channel_id=1, source_target_pairs={{0,4},{4,0},{8,12},{12,8},{16,20},{20,16},{24,28},{28,24},{1,5},{5... | collective-permute-start | bytes 393224 | tf_op jit(solution)/shard_map/ppermute | solution.py:29
  14.1 5.2 %collective-permute-start.3 = (bf16[128,512]{1,0:T(8,128)(2,1)S(1)}, bf16[128,512]{1,0:T(8,128)(2,1)S(1)}, u32[]{:S(2)}, u32[]{:S(2)}) collective-permute-start(bf16[128,512]{1,0:T(8,128)(2,1)S(1)} %collective-permute-done.seen.second_value), channel_id=1, source_target_pairs={{0,4},{4,0},{8,12},{12,8},{16,20},{20,16},{24,28},{28,24},{1,5},{5... | collective-permute-start | bytes 393224 | tf_op jit(solution)/shard_map/ppermute | solution.py:29
  15.7 6.3 %collective-permute-start.7 = (bf16[128,512]{1,0:T(8,128)(2,1)}, bf16[128,512]{1,0:T(8,128)(2,1)S(1)}, u32[]{:S(2)}, u32[]{:S(2)}) collective-permute-start(bf16[128,512]{1,0:T(8,128)(2,1)} %param.13), channel_id=1, source_target_pairs={{0,2},{1,3},{2,0},{3,1},{4,6},{5,7},{6,4},{7,5},{8,10},{9,11},{10,... | collective-permute-start | bytes 393224 | tf_op jit(solution)/shard_map/ppermute | solution.py:29
  17.3 5.0 %collective-permute-start.6 = (bf16[128,512]{1,0:T(8,128)(2,1)S(1)}, bf16[128,512]{1,0:T(8,128)(2,1)S(1)}, u32[]{:S(2)}, u32[]{:S(2)}) collective-permute-start(bf16[128,512]{1,0:T(8,128)(2,1)S(1)} %get-tuple-element.38.q), channel_id=1, source_target_pairs={{8,0},{16,8},{24,16},{28,24},{20,28},{12,20},{4,12},{0,4},{9,1},{1... | collective-permute-start | bytes 393224 | tf_op jit(solution)/shard_map/ppermute | solution.py:40
  17.7 4.3 %collective-permute-start.8 = (f32[31,512]{1,0:T(8,128)S(1)}, f32[31,512]{1,0:T(8,128)S(1)}, u32[]{:S(2)}, u32[]{:S(2)}) collective-permute-start(f32[31,512]{1,0:T(8,128)S(1)} %copy-done.1), channel_id=1, source_target_pairs={{0,2},{1,3},{2,0},{3,1},{4,6},{5,7},{6,4},{7,5},{8,10},{9,11},{10,... | collective-permute-start | bytes 190472 | tf_op jit(solution)/shard_map/ppermute | solution.py:29
  22.3 1.6 %collective-permute-start.9 = (bf16[128,1024]{1,0:T(8,128)(2,1)S(1)}, bf16[128,1024]{1,0:T(8,128)(2,1)S(1)}, u32[]{:S(2)}, u32[]{:S(2)}) collective-permute-start(bf16[128,1024]{1,0:T(8,128)(2,1)S(1)} %get-tuple-element.44), channel_id=1, source_target_pairs={{0,1},{1,0},{2,3},{3,2},{4,5},{5,4},{6,7},{7,6},{8,9},{9,8},{10,11... | collective-permute-start | bytes 786440 | tf_op jit(solution)/shard_map/ppermute | solution.py:29
  24.0 10.2 %collective-permute-start.13 = (bf16[128,1024]{1,0:T(8,128)(2,1)S(1)}, bf16[128,1024]{1,0:T(8,128)(2,1)S(1)}, u32[]{:S(2)}, u32[]{:S(2)}) collective-permute-start(bf16[128,1024]{1,0:T(8,128)(2,1)S(1)} %get-tuple-element.52.chip), channel_id=1, source_target_pairs={{0,2},{1,3},{2,0},{3,1},{4,6},{5,7},{6,4},{7,5},{8,10},{9,11},{10,... | collective-permute-start | bytes 786440 | tf_op jit(solution)/shard_map/ppermute | solution.py:29
  24.9 5.5 %collective-permute-start.10 = (bf16[48,1024]{1,0:T(8,128)(2,1)S(1)}, bf16[48,1024]{1,0:T(8,128)(2,1)S(1)}, u32[]{:S(2)}, u32[]{:S(2)}) collective-permute-start(bf16[48,1024]{1,0:T(8,128)(2,1)S(1)} %get-tuple-element.48), channel_id=1, source_target_pairs={{0,4},{4,0},{8,12},{12,8},{16,20},{20,16},{24,28},{28,24},{1,5},{5... | collective-permute-start | bytes 294920 | tf_op jit(solution)/shard_map/ppermute | solution.py:29
  26.1 4.3 %collective-permute-start.11 = (bf16[48,1024]{1,0:T(8,128)(2,1)S(1)}, bf16[48,1024]{1,0:T(8,128)(2,1)S(1)}, u32[]{:S(2)}, u32[]{:S(2)}) collective-permute-start(bf16[48,1024]{1,0:T(8,128)(2,1)S(1)} %get-tuple-element.49), channel_id=1, source_target_pairs={{0,1},{1,0},{2,3},{3,2},{4,8},{5,9},{6,10},{7,11},{8,4},{9,5},{10,... | collective-permute-start | bytes 294920 | tf_op jit(solution)/shard_map/ppermute | solution.py:51
  26.1 8.1 %collective-permute-start.14 = (bf16[128,512]{1,0:T(8,128)(2,1)S(1)}, bf16[128,512]{1,0:T(8,128)(2,1)S(1)}, u32[]{:S(2)}, u32[]{:S(2)}) collective-permute-start(bf16[128,512]{1,0:T(8,128)(2,1)S(1)} %get-tuple-element.47.q.refs_0_), channel_id=1, source_target_pairs={{0,8},{8,16},{16,24},{24,28},{28,20},{20,12},{12,4},{4,0},{1,9},{9... | collective-permute-start | bytes 393224 | tf_op jit(solution)/shard_map/ppermute | solution.py:40
  28.4 8.6 %collective-permute-start.15 = (bf16[128,512]{1,0:T(8,128)(2,1)S(1)}, bf16[128,512]{1,0:T(8,128)(2,1)S(1)}, u32[]{:S(2)}, u32[]{:S(2)}) collective-permute-start(bf16[128,512]{1,0:T(8,128)(2,1)S(1)} %get-tuple-element.47.q.refs_0_), channel_id=1, source_target_pairs={{0,1},{1,0},{2,3},{3,2},{4,5},{5,4},{6,7},{7,6},{8,12},{9,13},{10,... | collective-permute-start | bytes 393224 | tf_op jit(solution)/shard_map/ppermute | solution.py:51
  30.4 6.7 %collective-permute-start.12 = (bf16[64,1024]{1,0:T(8,128)(2,1)S(1)}, bf16[64,1024]{1,0:T(8,128)(2,1)S(1)}, u32[]{:S(2)}, u32[]{:S(2)}) collective-permute-start(bf16[64,1024]{1,0:T(8,128)(2,1)S(1)} %get-tuple-element.51.ends), channel_id=1, source_target_pairs={{0,2},{1,3},{2,0},{3,1},{4,6},{5,7},{6,4},{7,5},{8,10},{9,11},{10,... | collective-permute-start | bytes 393224 | tf_op jit(solution)/shard_map/ppermute | solution.py:29
  31.8 5.4 %collective-permute-start.16 = (bf16[128,512]{1,0:T(8,128)(2,1)S(1)}, bf16[128,512]{1,0:T(8,128)(2,1)S(1)}, u32[]{:S(2)}, u32[]{:S(2)}) collective-permute-start(bf16[128,512]{1,0:T(8,128)(2,1)S(1)} %get-tuple-element.57), channel_id=1, source_target_pairs={{0,4},{4,0},{8,12},{12,8},{16,20},{20,16},{24,28},{28,24},{1,5},{5... | collective-permute-start | bytes 393224 | tf_op jit(solution)/shard_map/ppermute | solution.py:29
  38.3 1.6 %collective-permute-start.17 = (bf16[128,1024]{1,0:T(8,128)(2,1)S(1)}, bf16[128,1024]{1,0:T(8,128)(2,1)S(1)}, u32[]{:S(2)}, u32[]{:S(2)}) collective-permute-start(bf16[128,1024]{1,0:T(8,128)(2,1)S(1)} %get-tuple-element.58.own.grad_here), channel_id=1, source_target_pairs={{0,1},{1,0},{2,3},{3,2},{4,5},{5,4},{6,7},{7,6},{8,9},{9,8},{10,11... | collective-permute-start | bytes 786440 | tf_op jit(solution)/shard_map/ppermute | solution.py:29
  40.6 6.7 %collective-permute-start.18 = (bf16[144,512]{1,0:T(8,128)(2,1)S(1)}, bf16[144,512]{1,0:T(8,128)(2,1)S(1)}, u32[]{:S(2)}, u32[]{:S(2)}) collective-permute-start(bf16[144,512]{1,0:T(8,128)(2,1)S(1)} %get-tuple-element.60.message.refs_5_), channel_id=1, source_target_pairs={{8,0},{16,8},{24,16},{28,24},{20,28},{12,20},{4,12},{0,4},{9,1},{1... | collective-permute-start | bytes 442376 | tf_op jit(solution)/shard_map/ppermute | solution.py:40
  42.6 7.4 %collective-permute-start.20 = (bf16[144,512]{1,0:T(8,128)(2,1)S(1)}, bf16[144,512]{1,0:T(8,128)(2,1)S(1)}, u32[]{:S(2)}, u32[]{:S(2)}) collective-permute-start(bf16[144,512]{1,0:T(8,128)(2,1)S(1)} %get-tuple-element.60.message.refs_5_), channel_id=1, source_target_pairs={{0,1},{1,0},{2,3},{3,2},{4,5},{5,4},{6,7},{7,6},{8,12},{9,13},{10,... | collective-permute-start | bytes 442376 | tf_op jit(solution)/shard_map/ppermute | solution.py:51
  42.6 7.4 %collective-permute-start.21 = (bf16[144,512]{1,0:T(8,128)(2,1)S(1)}, bf16[144,512]{1,0:T(8,128)(2,1)S(1)}, u32[]{:S(2)}, u32[]{:S(2)}) collective-permute-start(bf16[144,512]{1,0:T(8,128)(2,1)S(1)} %get-tuple-element.60.message.refs_5_), channel_id=1, source_target_pairs={{0,8},{8,16},{16,24},{24,28},{28,20},{20,12},{12,4},{4,0},{1,9},{9... | collective-permute-start | bytes 442376 | tf_op jit(solution)/shard_map/ppermute | solution.py:40
  47.2 5.4 %collective-permute-start.19 = (bf16[144,512]{1,0:T(8,128)(2,1)S(1)}, bf16[144,512]{1,0:T(8,128)(2,1)S(1)}, u32[]{:S(2)}, u32[]{:S(2)}) collective-permute-start(bf16[144,512]{1,0:T(8,128)(2,1)S(1)} %collective-permute-done.18.refs_8_), channel_id=1, source_target_pairs={{0,4},{4,0},{8,12},{12,8},{16,20},{20,16},{24,28},{28,24},{1,5},{5... | collective-permute-start | bytes 442376 | tf_op jit(solution)/shard_map/ppermute | solution.py:29

commit v14 on v12

--- a/solution.py
+++ b/solution.py
@@ -139,15 +139,19 @@
     return tile
 
 
-def term_rows(rows):
-    at = lax.broadcasted_iota(jnp.int32, (16, rows[0].shape[1]), 0)
-    block = jnp.zeros((16, rows[0].shape[1]), F32)
-    for r, rest in enumerate(rows):
-        for k in range(3):
-            term = rest.astype(BF16).astype(F32)
-            rest = rest - term
-            block = jnp.where(at == 3 * r + k, term, block)
-    return block.astype(BF16)
+def term_rows(row, first):
+    at = lax.broadcasted_iota(jnp.int32, (16, row.shape[1]), 0)
+    block = jnp.zeros((16, row.shape[1]), F32)
+    for k in range(3):
+        term = row.astype(BF16).astype(F32)
+        row = row - term
+        block = jnp.where(at == first + k, term, block)
+    return block
+
+
+def stat_terms(wide, first):
+    rows = tile_of(wide).T
+    return jnp.concatenate([term_rows(rows[h : h + 1], first) for h in range(len(wide))], axis=1)
 
 
 def stat_rows(message, frames, which, cols):
@@ -336,7 +340,7 @@
 
 def conv_edge_body(
     ends, ends_across, rim_near, rim_far, cot, cot_other, taps, taps_other,
-    rows_in, edge_rows, edge_conv, part_grad, seen_a, seen_b, output, grad_input,
+    rows_in, edge_rows, edge_conv, part_grad, seen, output, grad_input,
 ):
     frames, width = cot.shape
     wide, count = 2 * HALO, taps.shape[0]
@@ -383,21 +387,19 @@
     )
 
 
-def upstream_own_body(own, weight, partial):
+def upstream_own_body(own, weight, lse, partial, terms):
     partial[...] = upstream_part(own, weight, (0, 2))
-
-
-def upstream_body(core, weight, att, lse, partial, message, delta):
+    terms[...] = stat_terms([lse[:, c] for c in columns(lse.shape[1])], 0)
+
+
+def upstream_body(core, weight, att, partial, terms, message, delta):
     frames, width = att.shape
     heads = columns(width)
     up = (partial[...] + upstream_part(core, weight, (1, 3))).astype(BF16)
     products = [up[:, c].astype(F32) * att[:, c].astype(F32) for c in heads]
     deltas = [jnp.broadcast_to(jnp.sum(p, axis=1, keepdims=True), (frames, HDIM)) for p in products]
-    lse_rows = tile_of([lse[:, c] for c in heads]).T
-    delta_rows = tile_of(deltas).T
-    terms = [term_rows([lse_rows[h : h + 1], delta_rows[h : h + 1]]) for h in range(len(heads))]
     message[0:frames, :] = up
-    message[frames : frames + 16, :] = jnp.concatenate(terms, axis=1)
+    message[frames : frames + 16, :] = (terms[...] + stat_terms(deltas, 3)).astype(BF16)
     for c, part in zip(heads, deltas):
         delta[:, c] = part
 
@@ -556,14 +558,18 @@
         conv_edge_body,
         (tile, both),
         (ends, ends_across, rim_near, rim_far, cotangent, cot_other, kernel, taps_other)
-        + (rows_out, edge_rows, edge_conv, part_grad, q_near, q_relay),
-        1.4, "conv_edge", 2,
-    )
-
+        + (rows_out, edge_rows, edge_conv, part_grad, q_near),
+        1.4, "conv_edge", 1,
+    )
+
+    (grad_here,) = kernel_call(turn_body, (both,), (grad_here, q_relay), 0.1, "hand", 1)
     gi_core = pair_swap(grad_here, "mp", 1)
-    (partial,) = kernel_call(upstream_own_body, (tile32,), (grad_here, out_weight), 0.5, "upstream_own")
+    partial, terms = kernel_call(
+        upstream_own_body, (tile32, shaped((16, width), F32)), (grad_here, out_weight, lse), 0.5,
+        "upstream_own",
+    )
     message, delta = kernel_call(
-        upstream_body, (noted, tile32), (gi_core, out_weight, att, lse, partial), 0.6, "upstream"
+        upstream_body, (noted, tile32), (gi_core, out_weight, att, partial, terms), 0.6, "upstream"
     )
 
     m_near, m_first, m_second, m_relay = window_of(message)

time: 52.5 us -> 52.1 us (level)
  starting transfers between devices: 24.7 us -> 23.9 us
    pallas_call x14 -> x15, Pallas kernels: 10.1 us -> 10.2 us  [kernel_call(): pl.pallas_call(body, out_shape=outs, in_specs=[VMEM] * (len(args) - unrea...]
  transfers between devices with their start and end apart: 20 -> 20, of which waited for: 9 -> 8; matrix products, arithmetic and copies ran while one was open for 2% -> 2% of each run, Pallas kernels for 14% -> 16%
where the time goes in v14:
time: 52.1 us; the launch traced here: 51.9 us
  starting transfers between devices  23.9 us (46%)
  waiting for transfers between devices  14.8 us (28%)
  Pallas kernels  10.2 us (20%)
  other arithmetic  2.19 us (4%)
  between operations  0.83 us (2%)
    ppermute x10, starting transfers between devices, pair_swap(): lax.ppermute(block, axis, [(i, i ^ bit) for i in range(lax.axis_size(axis...  12.4 us
    ppermute x6, starting transfers between devices, ring(): return lax.ppermute(block, 'ctx', ring_routes(lax.axis_size('ctx'))[way])  11.4 us
    pallas_call x15, Pallas kernels, kernel_call(): pl.pallas_call(body, out_shape=outs, in_specs=[VMEM] * (len(args) - unrea...  10.2 us
    ppermute x10, waiting for transfers between devices, pair_swap(): lax.ppermute(block, axis, [(i, i ^ bit) for i in range(lax.axis_size(axis...  9.5 us
    ppermute x6, waiting for transfers between devices, ring(): return lax.ppermute(block, 'ctx', ring_routes(lax.axis_size('ctx'))[way])  5.3 us
    add x1, other arithmetic, per_device(): lax.pad(key_rows, zero, ((0, frames, 0), (0, 0, 0)))  1.14 us
    add x1, other arithmetic, per_device(): sum((lax.pad(rows, zero, ((k * frames, (2 - k) * frames, 0), (0, 0, 0)))...  1.06 us
  transfers between devices with their start and end apart: 20, of which 8 were waited for; matrix products, arithmetic and copies ran while one was open for 2% of the time, Pallas kernels for 16%

profile of v14, /device:TPU:0, one launch (start us, length us, event | category | flops | bytes accessed | tf_op | source)
XLA Modules:
  0.0 51.9 jit_solution(12541809699177030682)
XLA Ops:
  0.6 0.0 copy-start.2
  0.6 0.0 copy-start.1
  0.7 0.0 copy-start
  0.7 1.1 %pad_add_fusion.1.own = bf16[256,512]{1,0:T(8,128)(2,1)S(1)} fusion(bf16[128,512]{1,0:T(8,128)(2,1)} %param.9, bf16[128,512]{1,0:T(8,128)(2,1)} %param.8), kind=kLoop, calls=%fused_computation.1 | loop fusion | flops 524288 | bytes 524288 | tf_op jit(solution)/shard_map/add | solution.py:493
  1.8 3.0 %collective-permute-start = (bf16[256,512]{1,0:T(8,128)(2,1)S(1)}, bf16[256,512]{1,0:T(8,128)(2,1)S(1)}, u32[]{:S(2)}, u32[]{:S(2)}) collective-permute-start(bf16[256,512]{1,0:T(8,128)(2,1)S(1)} %pad_add_fusion.1.own), channel_id=1, source_target_pairs={{8,0},{16,8},{24,16},{28,24},{20,28},{12,20},{4,12},{0,4},{9,1},{1... | collective-permute-start | bytes 786440 | tf_op jit(solution)/shard_map/ppermute | solution.py:40
  4.8 0.0 collective-permute-start.2
  4.8 3.2 %collective-permute-start.3 = (bf16[256,512]{1,0:T(8,128)(2,1)S(1)}, bf16[256,512]{1,0:T(8,128)(2,1)S(1)}, u32[]{:S(2)}, u32[]{:S(2)}) collective-permute-start(bf16[256,512]{1,0:T(8,128)(2,1)S(1)} %pad_add_fusion.1.own), channel_id=1, source_target_pairs={{0,8},{8,16},{16,24},{24,28},{28,20},{20,12},{12,4},{4,0},{1,9},{9... | collective-permute-start | bytes 786440 | tf_op jit(solution)/shard_map/ppermute | solution.py:40
  7.9 1.1 %pad_add_fusion.seen.joined = bf16[384,512]{1,0:T(8,128)(2,1)S(1)} fusion(bf16[128,512]{1,0:T(8,128)(2,1)} %param.13, bf16[128,512]{1,0:T(8,128)(2,1)} %param.10, bf16[128,512]{1,0:T(8,128)(2,1)} %param.7), kind=kLoop, calls=%fused_computation | loop fusion | flops 1179648 | bytes 786432 | tf_op jit(solution)/shard_map/add | solution.py:496
  9.0 2.2 %collective-permute-done.block = bf16[256,512]{1,0:T(8,128)(2,1)S(1)} collective-permute-done((bf16[256,512]{1,0:T(8,128)(2,1)S(1)}, bf16[256,512]{1,0:T(8,128)(2,1)S(1)}, u32[]{:S(2)}, u32[]{:S(2)}) %collective-permute-start) | collective-permute-done | bytes 262176 | tf_op jit(solution)/shard_map/ppermute | solution.py:40
  11.2 1.7 %collective-permute-start.1 = (bf16[256,512]{1,0:T(8,128)(2,1)S(1)}, bf16[256,512]{1,0:T(8,128)(2,1)S(1)}, u32[]{:S(2)}, u32[]{:S(2)}) collective-permute-start(bf16[256,512]{1,0:T(8,128)(2,1)S(1)} %turn.1.seen.second), channel_id=1, source_target_pairs={{0,4},{4,0},{8,12},{12,8},{16,20},{20,16},{24,28},{28,24},{1,5},{5... | collective-permute-start | bytes 786440 | tf_op jit(solution)/shard_map/ppermute | solution.py:29
  12.9 0.0 copy-done.2
  12.9 1.5 %collective-permute-start.5 = (bf16[128,512]{1,0:T(8,128)(2,1)S(1)}, bf16[128,512]{1,0:T(8,128)(2,1)S(1)}, u32[]{:S(2)}, u32[]{:S(2)}) collective-permute-start(bf16[128,512]{1,0:T(8,128)(2,1)S(1)} %copy-done.2), channel_id=1, source_target_pairs={{0,2},{1,3},{2,0},{3,1},{4,6},{5,7},{6,4},{7,5},{8,10},{9,11},{10,... | collective-permute-start | bytes 393224 | tf_op jit(solution)/shard_map/ppermute | solution.py:29
  14.5 0.6 %collective-permute-start.4 = (bf16[128,512]{1,0:T(8,128)(2,1)S(1)}, bf16[128,512]{1,0:T(8,128)(2,1)S(1)}, u32[]{:S(2)}, u32[]{:S(2)}) collective-permute-start(bf16[128,512]{1,0:T(8,128)(2,1)S(1)} %get-tuple-element.41.q), channel_id=1, source_target_pairs={{8,0},{16,8},{24,16},{28,24},{20,28},{12,20},{4,12},{0,4},{9,1},{1... | collective-permute-start | bytes 393224 | tf_op jit(solution)/shard_map/ppermute | solution.py:40
  15.1 0.0 collective-permute-done.2.near
  15.1 0.0 copy-done.1
  15.1 0.3 collective-permute-start.6
  15.4 0.0 collective-permute-done.3.first
  15.4 0.6 %forward.1 = (f32[128,512]{1,0:T(8,128)S(1)}, f32[128,512]{1,0:T(8,128)S(1)}, f32[128,512]{1,0:T(8,128)S(1)}) custom-call(bf16[128,512]{1,0:T(8,128)(2,1)S(1)} %get-tuple-element.41.q, bf16[256,512]{1,0:T(8,128)(2,1)S(1)} %pad_add_fusion.1.own, bf16[256,512]{1,0:T(8,128)(2,1)S(1)} %collective-permute-done.2.near, ...), custom_call_target="tpu_custom_call" | custom-call | bytes 3690000 | tf_op jit(solution)/shard_map/forward/pallas_call | solution.py:76
  16.0 3.1 %collective-permute-done.1.relay = bf16[256,512]{1,0:T(8,128)(2,1)S(1)} collective-permute-done((bf16[256,512]{1,0:T(8,128)(2,1)S(1)}, bf16[256,512]{1,0:T(8,128)(2,1)S(1)}, u32[]{:S(2)}, u32[]{:S(2)}) %collective-permute-start.1) | collective-permute-done | bytes 262176 | tf_op jit(solution)/shard_map/ppermute | solution.py:29
  19.1 0.0 copy-done
  19.1 0.9 %project.1 = (bf16[128,512]{1,0:T(8,128)(2,1)S(1)}, f32[128,512]{1,0:T(8,128)S(1)}, bf16[128,1024]{1,0:T(8,128)(2,1)S(1)}, bf16[128,1024]{1,0:T(8,128)(2,1)S(1)}) custom-call(bf16[128,512]{1,0:T(8,128)(2,1)S(1)} %get-tuple-element.41.q, bf16[256,512]{1,0:T(8,128)(2,1)S(1)} %collective-permute-done.1.relay, f32[128,512]{1,0:T(8,128)S(1)} %get-tuple-element.42.sums, ...), custom_call_target="tpu_custom_call" | custom-call | bytes 3690000 | tf_op jit(solution)/shard_map/project/pallas_call | solution.py:76
  20.0 0.0 collective-permute-done.6.seen_b.taps_other
  20.0 0.0 collective-permute-done.5.seen_a.cot_other
  20.0 0.4 collective-permute-done.4.q_second
  20.5 0.1 collective-permute-start.7
  20.5 1.5 %collective-permute-done.7.core = bf16[128,1024]{1,0:T(8,128)(2,1)S(1)} collective-permute-done((bf16[128,1024]{1,0:T(8,128)(2,1)S(1)}, bf16[128,1024]{1,0:T(8,128)(2,1)S(1)}, u32[]{:S(2)}, u32[]{:S(2)}) %collective-permute-start.7) | collective-permute-done | bytes 262176 | tf_op jit(solution)/shard_map/ppermute | solution.py:29
  22.1 0.1 join.1
  22.2 1.6 %collective-permute-start.11 = (bf16[128,1024]{1,0:T(8,128)(2,1)S(1)}, bf16[128,1024]{1,0:T(8,128)(2,1)S(1)}, u32[]{:S(2)}, u32[]{:S(2)}) collective-permute-start(bf16[128,1024]{1,0:T(8,128)(2,1)S(1)} %get-tuple-element.55.chip), channel_id=1, source_target_pairs={{0,2},{1,3},{2,0},{3,1},{4,6},{5,7},{6,4},{7,5},{8,10},{9,11},{10,... | collective-permute-start | bytes 786440 | tf_op jit(solution)/shard_map/ppermute | solution.py:29
  23.8 2.5 %collective-permute-start.8 = (bf16[48,1024]{1,0:T(8,128)(2,1)S(1)}, bf16[48,1024]{1,0:T(8,128)(2,1)S(1)}, u32[]{:S(2)}, u32[]{:S(2)}) collective-permute-start(bf16[48,1024]{1,0:T(8,128)(2,1)S(1)} %get-tuple-element.51), channel_id=1, source_target_pairs={{0,4},{4,0},{8,12},{12,8},{16,20},{20,16},{24,28},{28,24},{1,5},{5... | collective-permute-start | bytes 294920 | tf_op jit(solution)/shard_map/ppermute | solution.py:29
  26.2 0.0 collective-permute-start.9
  26.2 1.5 %collective-permute-start.12 = (bf16[128,512]{1,0:T(8,128)(2,1)S(1)}, bf16[128,512]{1,0:T(8,128)(2,1)S(1)}, u32[]{:S(2)}, u32[]{:S(2)}) collective-permute-start(bf16[128,512]{1,0:T(8,128)(2,1)S(1)} %get-tuple-element.50.q.refs_0_), channel_id=1, source_target_pairs={{0,8},{8,16},{16,24},{24,28},{28,20},{20,12},{12,4},{4,0},{1,9},{9... | collective-permute-start | bytes 393224 | tf_op jit(solution)/shard_map/ppermute | solution.py:40
  27.7 0.0 collective-permute-start.13
  27.7 2.7 %collective-permute-done.8.rim_near = bf16[48,1024]{1,0:T(8,128)(2,1)S(1)} collective-permute-done((bf16[48,1024]{1,0:T(8,128)(2,1)S(1)}, bf16[48,1024]{1,0:T(8,128)(2,1)S(1)}, u32[]{:S(2)}, u32[]{:S(2)}) %collective-permute-start.8) | collective-permute-done | bytes 98336 | tf_op jit(solution)/shard_map/ppermute | solution.py:29
  30.4 0.0 collective-permute-done.9.rim_far
  30.4 0.6 %collective-permute-start.10 = (bf16[64,1024]{1,0:T(8,128)(2,1)S(1)}, bf16[64,1024]{1,0:T(8,128)(2,1)S(1)}, u32[]{:S(2)}, u32[]{:S(2)}) collective-permute-start(bf16[64,1024]{1,0:T(8,128)(2,1)S(1)} %get-tuple-element.54.ends), channel_id=1, source_target_pairs={{0,2},{1,3},{2,0},{3,1},{4,6},{5,7},{6,4},{7,5},{8,10},{9,11},{10,... | collective-permute-start | bytes 393224 | tf_op jit(solution)/shard_map/ppermute | solution.py:29
  31.0 2.5 %collective-permute-start.14 = (bf16[128,512]{1,0:T(8,128)(2,1)S(1)}, bf16[128,512]{1,0:T(8,128)(2,1)S(1)}, u32[]{:S(2)}, u32[]{:S(2)}) collective-permute-start(bf16[128,512]{1,0:T(8,128)(2,1)S(1)} %get-tuple-element.61), channel_id=1, source_target_pairs={{0,4},{4,0},{8,12},{12,8},{16,20},{20,16},{24,28},{28,24},{1,5},{5... | collective-permute-start | bytes 393224 | tf_op jit(solution)/shard_map/ppermute | solution.py:29
  33.5 0.0 collective-permute-done.12.seen.refs_2_
  33.5 0.0 collective-permute-done.11.across
  33.5 2.8 %conv_inner.1 = (bf16[128,512]{1,0:T(8,128)(2,1)S(1)}, f32[32,512]{1,0:T(8,128)S(1)}, f32[64,1024]{1,0:T(8,128)S(1)}, f32[128,1024]{1,0:T(8,128)S(1)}) custom-call(bf16[128,1024]{1,0:T(8,128)(2,1)S(1)} %get-tuple-element.55.chip, bf16[128,1024]{1,0:T(8,128)(2,1)S(1)} %collective-permute-done.11.across, bf16[128,512]{1,0:T(8,128)(2,1)S(1)} %get-tuple-element.49.cot, ...), custom_call_target="tpu_custom_call" | custom-call | bytes 11439000 | tf_op jit(solution)/shard_map/conv_inner/pallas_call | solution.py:76
  36.3 0.0 collective-permute-done.13.seen.refs_1_
  36.3 0.0 collective-permute-done.10.ends_across
  36.4 1.1 %conv_edge.1 = (bf16[128,512]{1,0:T(8,128)(2,1)S(1)}, bf16[128,1024]{1,0:T(8,128)(2,1)S(1)}) custom-call(bf16[64,1024]{1,0:T(8,128)(2,1)S(1)} %get-tuple-element.54.ends, bf16[64,1024]{1,0:T(8,128)(2,1)S(1)} %collective-permute-done.10.ends_across, bf16[48,1024]{1,0:T(8,128)(2,1)S(1)} %collective-permute-done.8.rim_near, ...), custom_call_target="tpu_custom_call" | custom-call | bytes 5166000 | tf_op jit(solution)/shard_map/conv_edge/pallas_call | solution.py:76
  37.5 0.0 collective-permute-done.14.seen.refs_4_.query
  37.5 0.1 collective-permute-start.15
  37.6 0.5 upstream_own.1
  38.1 1.0 %collective-permute-done.15.core = bf16[128,1024]{1,0:T(8,128)(2,1)S(1)} collective-permute-done((bf16[128,1024]{1,0:T(8,128)(2,1)S(1)}, bf16[128,1024]{1,0:T(8,128)(2,1)S(1)}, u32[]{:S(2)}, u32[]{:S(2)}) %collective-permute-start.15) | collective-permute-done | bytes 262176 | tf_op jit(solution)/shard_map/ppermute | solution.py:29
  39.1 0.7 %upstream.1 = (bf16[144,512]{1,0:T(8,128)(2,1)S(1)}, f32[128,512]{1,0:T(8,128)S(1)}) custom-call(bf16[128,1024]{1,0:T(8,128)(2,1)S(1)} %collective-permute-done.15.core, bf16[512,2048]{1,0:T(8,128)(2,1)S(1)} %copy-done, bf16[128,512]{1,0:T(8,128)(2,1)S(1)} %get-tuple-element.62.att, f32[128,512]{1,0:T(8,128)S(1)} %get-tuple-element.64.partial, ...), custom_call_target="tpu_custom_call" | custom-call | bytes 2214000 | tf_op jit(solution)/shard_map/upstream/pallas_call | solution.py:76
  39.8 1.7 %collective-permute-start.16 = (bf16[144,512]{1,0:T(8,128)(2,1)S(1)}, bf16[144,512]{1,0:T(8,128)(2,1)S(1)}, u32[]{:S(2)}, u32[]{:S(2)}) collective-permute-start(bf16[144,512]{1,0:T(8,128)(2,1)S(1)} %get-tuple-element.66.message.refs_5_), channel_id=1, source_target_pairs={{8,0},{16,8},{24,16},{28,24},{20,28},{12,20},{4,12},{0,4},{9,1},{1... | collective-permute-start | bytes 442376 | tf_op jit(solution)/shard_map/ppermute | solution.py:40
  41.5 0.0 collective-permute-start.18
  41.5 1.6 %collective-permute-start.19 = (bf16[144,512]{1,0:T(8,128)(2,1)S(1)}, bf16[144,512]{1,0:T(8,128)(2,1)S(1)}, u32[]{:S(2)}, u32[]{:S(2)}) collective-permute-start(bf16[144,512]{1,0:T(8,128)(2,1)S(1)} %get-tuple-element.66.message.refs_5_), channel_id=1, source_target_pairs={{0,8},{8,16},{16,24},{24,28},{28,20},{20,12},{12,4},{4,0},{1,9},{9... | collective-permute-start | bytes 442376 | tf_op jit(solution)/shard_map/ppermute | solution.py:40
  43.0 2.7 %collective-permute-done.16.refs_8_ = bf16[144,512]{1,0:T(8,128)(2,1)S(1)} collective-permute-done((bf16[144,512]{1,0:T(8,128)(2,1)S(1)}, bf16[144,512]{1,0:T(8,128)(2,1)S(1)}, u32[]{:S(2)}, u32[]{:S(2)}) %collective-permute-start.16) | collective-permute-done | bytes 147488 | tf_op jit(solution)/shard_map/ppermute | solution.py:40
  45.7 1.6 %collective-permute-start.17 = (bf16[144,512]{1,0:T(8,128)(2,1)S(1)}, bf16[144,512]{1,0:T(8,128)(2,1)S(1)}, u32[]{:S(2)}, u32[]{:S(2)}) collective-permute-start(bf16[144,512]{1,0:T(8,128)(2,1)S(1)} %collective-permute-done.16.refs_8_), channel_id=1, source_target_pairs={{0,4},{4,0},{8,12},{12,8},{16,20},{20,16},{24,28},{28,24},{1,5},{5... | collective-permute-start | bytes 442376 | tf_op jit(solution)/shard_map/ppermute | solution.py:29
  47.3 1.5 %query_grad.1 = (bf16[128,512]{1,0:T(8,128)(2,1)}, bf16[128,512]{1,0:T(8,128)(2,1)}, bf16[128,512]{1,0:T(8,128)(2,1)}) custom-call(bf16[128,512]{1,0:T(8,128)(2,1)S(1)} %get-tuple-element.50.q.refs_0_, bf16[256,512]{1,0:T(8,128)(2,1)S(1)} %pad_add_fusion.1.own, bf16[256,512]{1,0:T(8,128)(2,1)S(1)} %collective-permute-done.2.near, ...), custom_call_target="tpu_custom_call" | custom-call | bytes 6642000 | tf_op jit(solution)/shard_map/query_grad/pallas_call | solution.py:76
  48.9 0.0 collective-permute-done.18.refs_6_
  48.9 0.0 collective-permute-done.19.refs_7_
  48.9 0.9 %key_part.1 = (f32[128,512]{1,0:T(8,128)S(1)}, f32[128,512]{1,0:T(8,128)S(1)}, f32[128,512]{1,0:T(8,128)S(1)}) custom-call(bf16[256,512]{1,0:T(8,128)(2,1)S(1)} %pad_add_fusion.1.own, bf16[128,512]{1,0:T(8,128)(2,1)S(1)} %get-tuple-element.50.q.refs_0_, bf16[128,512]{1,0:T(8,128)(2,1)S(1)} %collective-permute-done.13.seen.refs_1_, ...), custom_call_target="tpu_custom_call" | custom-call | bytes 5535000 | tf_op jit(solution)/shard_map/key_part/pallas_call | solution.py:76
  49.8 1.1 %collective-permute-done.17.message = bf16[144,512]{1,0:T(8,128)(2,1)S(1)} collective-permute-done((bf16[144,512]{1,0:T(8,128)(2,1)S(1)}, bf16[144,512]{1,0:T(8,128)(2,1)S(1)}, u32[]{:S(2)}, u32[]{:S(2)}) %collective-permute-start.17) | collective-permute-done | bytes 147488 | tf_op jit(solution)/shard_map/ppermute | solution.py:29
  50.9 1.0 %key_grad.1 = (bf16[128,512]{1,0:T(8,128)(2,1)}, bf16[128,512]{1,0:T(8,128)(2,1)}) custom-call(bf16[256,512]{1,0:T(8,128)(2,1)S(1)} %pad_add_fusion.1.own, bf16[128,512]{1,0:T(8,128)(2,1)S(1)} %collective-permute-done.14.seen.refs_4_.query, bf16[144,512]{1,0:T(8,128)(2,1)S(1)} %collective-permute-done.17.message, f32[128,512]{1,0:T(8,128)S(1)} %get-tuple-element.72.late, ...), custom_call_target="tpu_custom_call" | custom-call | bytes 3690000 | tf_op jit(solution)/shard_map/key_grad/pallas_call | solution.py:76
  (5 shorter events, 0.1 us)
Async XLA Ops:
  0.6 12.3 %copy-start.2 = (bf16[128,512]{1,0:T(8,128)(2,1)S(1)}, bf16[128,512]{1,0:T(8,128)(2,1)}, u32[]{:S(2)}) copy-start(bf16[128,512]{1,0:T(8,128)(2,1)} %param.13) | copy-start | bytes 393220
  0.6 14.4 %copy-start.1 = (f32[31,512]{1,0:T(8,128)S(1)}, f32[31,512]{1,0:T(8,128)}, u32[]{:S(2)}) copy-start(f32[31,512]{1,0:T(8,128)} %taps.3) | copy-start | bytes 190468
  0.7 18.5 %copy-start = (bf16[512,2048]{1,0:T(8,128)(2,1)S(1)}, bf16[512,2048]{1,0:T(8,128)(2,1)}, u32[]{:S(2)}) copy-start(bf16[512,2048]{1,0:T(8,128)(2,1)} %weight.5) | copy-start | bytes 6291460
  1.8 9.4 %collective-permute-start = (bf16[256,512]{1,0:T(8,128)(2,1)S(1)}, bf16[256,512]{1,0:T(8,128)(2,1)S(1)}, u32[]{:S(2)}, u32[]{:S(2)}) collective-permute-start(bf16[256,512]{1,0:T(8,128)(2,1)S(1)} %pad_add_fusion.1.own), channel_id=1, source_target_pairs={{8,0},{16,8},{24,16},{28,24},{20,28},{12,20},{4,12},{0,4},{9,1},{1... | collective-permute-start | bytes 786440 | tf_op jit(solution)/shard_map/ppermute | solution.py:40
  4.8 10.3 %collective-permute-start.2 = (bf16[256,512]{1,0:T(8,128)(2,1)S(1)}, bf16[256,512]{1,0:T(8,128)(2,1)S(1)}, u32[]{:S(2)}, u32[]{:S(2)}) collective-permute-start(bf16[256,512]{1,0:T(8,128)(2,1)S(1)} %pad_add_fusion.1.own), channel_id=1, source_target_pairs={{0,1},{1,0},{2,3},{3,2},{4,5},{5,4},{6,7},{7,6},{8,12},{9,13},{10,... | collective-permute-start | bytes 786440 | tf_op jit(solution)/shard_map/ppermute | solution.py:51
  4.8 10.6 %collective-permute-start.3 = (bf16[256,512]{1,0:T(8,128)(2,1)S(1)}, bf16[256,512]{1,0:T(8,128)(2,1)S(1)}, u32[]{:S(2)}, u32[]{:S(2)}) collective-permute-start(bf16[256,512]{1,0:T(8,128)(2,1)S(1)} %pad_add_fusion.1.own), channel_id=1, source_target_pairs={{0,8},{8,16},{16,24},{24,28},{28,20},{20,12},{12,4},{4,0},{1,9},{9... | collective-permute-start | bytes 786440 | tf_op jit(solution)/shard_map/ppermute | solution.py:40
  11.2 7.9 %collective-permute-start.1 = (bf16[256,512]{1,0:T(8,128)(2,1)S(1)}, bf16[256,512]{1,0:T(8,128)(2,1)S(1)}, u32[]{:S(2)}, u32[]{:S(2)}) collective-permute-start(bf16[256,512]{1,0:T(8,128)(2,1)S(1)} %turn.1.seen.second), channel_id=1, source_target_pairs={{0,4},{4,0},{8,12},{12,8},{16,20},{20,16},{24,28},{28,24},{1,5},{5... | collective-permute-start | bytes 786440 | tf_op jit(solution)/shard_map/ppermute | solution.py:29
  12.9 7.1 %collective-permute-start.5 = (bf16[128,512]{1,0:T(8,128)(2,1)S(1)}, bf16[128,512]{1,0:T(8,128)(2,1)S(1)}, u32[]{:S(2)}, u32[]{:S(2)}) collective-permute-start(bf16[128,512]{1,0:T(8,128)(2,1)S(1)} %copy-done.2), channel_id=1, source_target_pairs={{0,2},{1,3},{2,0},{3,1},{4,6},{5,7},{6,4},{7,5},{8,10},{9,11},{10,... | collective-permute-start | bytes 393224 | tf_op jit(solution)/shard_map/ppermute | solution.py:29
  14.5 5.9 %collective-permute-start.4 = (bf16[128,512]{1,0:T(8,128)(2,1)S(1)}, bf16[128,512]{1,0:T(8,128)(2,1)S(1)}, u32[]{:S(2)}, u32[]{:S(2)}) collective-permute-start(bf16[128,512]{1,0:T(8,128)(2,1)S(1)} %get-tuple-element.41.q), channel_id=1, source_target_pairs={{8,0},{16,8},{24,16},{28,24},{20,28},{12,20},{4,12},{0,4},{9,1},{1... | collective-permute-start | bytes 393224 | tf_op jit(solution)/shard_map/ppermute | solution.py:40
  15.1 4.9 %collective-permute-start.6 = (f32[31,512]{1,0:T(8,128)S(1)}, f32[31,512]{1,0:T(8,128)S(1)}, u32[]{:S(2)}, u32[]{:S(2)}) collective-permute-start(f32[31,512]{1,0:T(8,128)S(1)} %copy-done.1), channel_id=1, source_target_pairs={{0,2},{1,3},{2,0},{3,1},{4,6},{5,7},{6,4},{7,5},{8,10},{9,11},{10,... | collective-permute-start | bytes 190472 | tf_op jit(solution)/shard_map/ppermute | solution.py:29
  20.5 1.6 %collective-permute-start.7 = (bf16[128,1024]{1,0:T(8,128)(2,1)S(1)}, bf16[128,1024]{1,0:T(8,128)(2,1)S(1)}, u32[]{:S(2)}, u32[]{:S(2)}) collective-permute-start(bf16[128,1024]{1,0:T(8,128)(2,1)S(1)} %get-tuple-element.47), channel_id=1, source_target_pairs={{0,1},{1,0},{2,3},{3,2},{4,5},{5,4},{6,7},{7,6},{8,9},{9,8},{10,11... | collective-permute-start | bytes 786440 | tf_op jit(solution)/shard_map/ppermute | solution.py:29
  22.2 11.3 %collective-permute-start.11 = (bf16[128,1024]{1,0:T(8,128)(2,1)S(1)}, bf16[128,1024]{1,0:T(8,128)(2,1)S(1)}, u32[]{:S(2)}, u32[]{:S(2)}) collective-permute-start(bf16[128,1024]{1,0:T(8,128)(2,1)S(1)} %get-tuple-element.55.chip), channel_id=1, source_target_pairs={{0,2},{1,3},{2,0},{3,1},{4,6},{5,7},{6,4},{7,5},{8,10},{9,11},{10,... | collective-permute-start | bytes 786440 | tf_op jit(solution)/shard_map/ppermute | solution.py:29
  23.8 6.7 %collective-permute-start.8 = (bf16[48,1024]{1,0:T(8,128)(2,1)S(1)}, bf16[48,1024]{1,0:T(8,128)(2,1)S(1)}, u32[]{:S(2)}, u32[]{:S(2)}) collective-permute-start(bf16[48,1024]{1,0:T(8,128)(2,1)S(1)} %get-tuple-element.51), channel_id=1, source_target_pairs={{0,4},{4,0},{8,12},{12,8},{16,20},{20,16},{24,28},{28,24},{1,5},{5... | collective-permute-start | bytes 294920 | tf_op jit(solution)/shard_map/ppermute | solution.py:29
  26.2 4.2 %collective-permute-start.9 = (bf16[48,1024]{1,0:T(8,128)(2,1)S(1)}, bf16[48,1024]{1,0:T(8,128)(2,1)S(1)}, u32[]{:S(2)}, u32[]{:S(2)}) collective-permute-start(bf16[48,1024]{1,0:T(8,128)(2,1)S(1)} %get-tuple-element.52), channel_id=1, source_target_pairs={{0,1},{1,0},{2,3},{3,2},{4,8},{5,9},{6,10},{7,11},{8,4},{9,5},{10,... | collective-permute-start | bytes 294920 | tf_op jit(solution)/shard_map/ppermute | solution.py:51
  26.2 7.3 %collective-permute-start.12 = (bf16[128,512]{1,0:T(8,128)(2,1)S(1)}, bf16[128,512]{1,0:T(8,128)(2,1)S(1)}, u32[]{:S(2)}, u32[]{:S(2)}) collective-permute-start(bf16[128,512]{1,0:T(8,128)(2,1)S(1)} %get-tuple-element.50.q.refs_0_), channel_id=1, source_target_pairs={{0,8},{8,16},{16,24},{24,28},{28,20},{20,12},{12,4},{4,0},{1,9},{9... | collective-permute-start | bytes 393224 | tf_op jit(solution)/shard_map/ppermute | solution.py:40
  27.7 8.6 %collective-permute-start.13 = (bf16[128,512]{1,0:T(8,128)(2,1)S(1)}, bf16[128,512]{1,0:T(8,128)(2,1)S(1)}, u32[]{:S(2)}, u32[]{:S(2)}) collective-permute-start(bf16[128,512]{1,0:T(8,128)(2,1)S(1)} %get-tuple-element.50.q.refs_0_), channel_id=1, source_target_pairs={{0,1},{1,0},{2,3},{3,2},{4,5},{5,4},{6,7},{7,6},{8,12},{9,13},{10,... | collective-permute-start | bytes 393224 | tf_op jit(solution)/shard_map/ppermute | solution.py:51
  30.4 5.9 %collective-permute-start.10 = (bf16[64,1024]{1,0:T(8,128)(2,1)S(1)}, bf16[64,1024]{1,0:T(8,128)(2,1)S(1)}, u32[]{:S(2)}, u32[]{:S(2)}) collective-permute-start(bf16[64,1024]{1,0:T(8,128)(2,1)S(1)} %get-tuple-element.54.ends), channel_id=1, source_target_pairs={{0,2},{1,3},{2,0},{3,1},{4,6},{5,7},{6,4},{7,5},{8,10},{9,11},{10,... | collective-permute-start | bytes 393224 | tf_op jit(solution)/shard_map/ppermute | solution.py:29
  31.0 6.5 %collective-permute-start.14 = (bf16[128,512]{1,0:T(8,128)(2,1)S(1)}, bf16[128,512]{1,0:T(8,128)(2,1)S(1)}, u32[]{:S(2)}, u32[]{:S(2)}) collective-permute-start(bf16[128,512]{1,0:T(8,128)(2,1)S(1)} %get-tuple-element.61), channel_id=1, source_target_pairs={{0,4},{4,0},{8,12},{12,8},{16,20},{20,16},{24,28},{28,24},{1,5},{5... | collective-permute-start | bytes 393224 | tf_op jit(solution)/shard_map/ppermute | solution.py:29
  37.5 1.6 %collective-permute-start.15 = (bf16[128,1024]{1,0:T(8,128)(2,1)S(1)}, bf16[128,1024]{1,0:T(8,128)(2,1)S(1)}, u32[]{:S(2)}, u32[]{:S(2)}) collective-permute-start(bf16[128,1024]{1,0:T(8,128)(2,1)S(1)} %hand.1.own.grad_here), channel_id=1, source_target_pairs={{0,1},{1,0},{2,3},{3,2},{4,5},{5,4},{6,7},{7,6},{8,9},{9,8},{10,11... | collective-permute-start | bytes 786440 | tf_op jit(solution)/shard_map/ppermute | solution.py:29
  39.8 5.9 %collective-permute-start.16 = (bf16[144,512]{1,0:T(8,128)(2,1)S(1)}, bf16[144,512]{1,0:T(8,128)(2,1)S(1)}, u32[]{:S(2)}, u32[]{:S(2)}) collective-permute-start(bf16[144,512]{1,0:T(8,128)(2,1)S(1)} %get-tuple-element.66.message.refs_5_), channel_id=1, source_target_pairs={{8,0},{16,8},{24,16},{28,24},{20,28},{12,20},{4,12},{0,4},{9,1},{1... | collective-permute-start | bytes 442376 | tf_op jit(solution)/shard_map/ppermute | solution.py:40
  41.5 7.4 %collective-permute-start.18 = (bf16[144,512]{1,0:T(8,128)(2,1)S(1)}, bf16[144,512]{1,0:T(8,128)(2,1)S(1)}, u32[]{:S(2)}, u32[]{:S(2)}) collective-permute-start(bf16[144,512]{1,0:T(8,128)(2,1)S(1)} %get-tuple-element.66.message.refs_5_), channel_id=1, source_target_pairs={{0,1},{1,0},{2,3},{3,2},{4,5},{5,4},{6,7},{7,6},{8,12},{9,13},{10,... | collective-permute-start | bytes 442376 | tf_op jit(solution)/shard_map/ppermute | solution.py:51
  41.5 7.4 %collective-permute-start.19 = (bf16[144,512]{1,0:T(8,128)(2,1)S(1)}, bf16[144,512]{1,0:T(8,128)(2,1)S(1)}, u32[]{:S(2)}, u32[]{:S(2)}) collective-permute-start(bf16[144,512]{1,0:T(8,128)(2,1)S(1)} %get-tuple-element.66.message.refs_5_), channel_id=1, source_target_pairs={{0,8},{8,16},{16,24},{24,28},{28,20},{20,12},{12,4},{4,0},{1,9},{9... | collective-permute-start | bytes 442376 | tf_op jit(solution)/shard_map/ppermute | solution.py:40
  45.7 5.1 %collective-permute-start.17 = (bf16[144,512]{1,0:T(8,128)(2,1)S(1)}, bf16[144,512]{1,0:T(8,128)(2,1)S(1)}, u32[]{:S(2)}, u32[]{:S(2)}) collective-permute-start(bf16[144,512]{1,0:T(8,128)(2,1)S(1)} %collective-permute-done.16.refs_8_), channel_id=1, source_target_pairs={{0,4},{4,0},{8,12},{12,8},{16,20},{20,16},{24,28},{28,24},{1,5},{5... | collective-permute-start | bytes 442376 | tf_op jit(solution)/shard_map/ppermute | solution.py:29

commit v15 on v14

--- a/solution.py
+++ b/solution.py
@@ -572,7 +572,8 @@
         upstream_body, (noted, tile32), (gi_core, out_weight, att, partial, terms), 0.6, "upstream"
     )
 
-    m_near, m_first, m_second, m_relay = window_of(message)
+    m_near, m_first, m_second = inner_swap(message), ring(message, 0), ring(message, 1)
+    m_relay = outer_swap(message)
     output, grad_input, grad_query = kernel_call(
         functools.partial(query_grad_body, scale),
         (tile, tile, tile),

time: 52.1 us -> 50.6 us (0.971)
  starting transfers between devices: 23.9 us -> 21.3 us
  waiting for transfers between devices: 14.8 us -> 16 us
    ppermute x6, waiting for transfers between devices: 5.3 us -> 7.57 us  [ring(): return lax.ppermute(block, 'ctx', ring_routes(lax.axis_size('ctx'))[way])]
    ppermute x10 -> x9, starting transfers between devices: 12.4 us -> 10.8 us  [pair_swap(): lax.ppermute(block, axis, [(i, i ^ bit) for i in range(lax.axis_size(axis...]
    ppermute x6, starting transfers between devices: 11.4 us -> 10.2 us  [ring(): return lax.ppermute(block, 'ctx', ring_routes(lax.axis_size('ctx'))[way])]
    ppermute x10 -> x9, waiting for transfers between devices: 9.5 us -> 8.38 us  [pair_swap(): lax.ppermute(block, axis, [(i, i ^ bit) for i in range(lax.axis_size(axis...]
  transfers between devices with their start and end apart: 20 -> 20, of which waited for: 8 -> 8; matrix products, arithmetic and copies ran while one was open for 2% -> 2% of each run, Pallas kernels for 16% -> 17%
where the time goes in v15:
time: 50.6 us; the launch traced here: 50.4 us
  starting transfers between devices  21.3 us (42%)
  waiting for transfers between devices  16 us (32%)
  Pallas kernels  10.2 us (20%)
  other arithmetic  2.19 us (4%)
  between operations  0.83 us (2%)
    ppermute x9, starting transfers between devices, pair_swap(): lax.ppermute(block, axis, [(i, i ^ bit) for i in range(lax.axis_size(axis...  10.8 us
    ppermute x6, starting transfers between devices, ring(): return lax.ppermute(block, 'ctx', ring_routes(lax.axis_size('ctx'))[way])  10.2 us
    pallas_call x15, Pallas kernels, kernel_call(): pl.pallas_call(body, out_shape=outs, in_specs=[VMEM] * (len(args) - unrea...  10.2 us
    ppermute x9, waiting for transfers between devices, pair_swap(): lax.ppermute(block, axis, [(i, i ^ bit) for i in range(lax.axis_size(axis...  8.38 us
    ppermute x6, waiting for transfers between devices, ring(): return lax.ppermute(block, 'ctx', ring_routes(lax.axis_size('ctx'))[way])  7.57 us
    add x1, other arithmetic, per_device(): lax.pad(key_rows, zero, ((0, frames, 0), (0, 0, 0)))  1.14 us
    add x1, other arithmetic, per_device(): sum((lax.pad(rows, zero, ((k * frames, (2 - k) * frames, 0), (0, 0, 0)))...  1.06 us
  transfers between devices with their start and end apart: 20, of which 8 were waited for; matrix products, arithmetic and copies ran while one was open for 2% of the time, Pallas kernels for 17%

profile of v15, /device:TPU:0, one launch (start us, length us, event | category | flops | bytes accessed | tf_op | source)
XLA Modules:
  0.0 50.4 jit_solution(17087321571118902681)
XLA Ops:
  0.6 0.0 copy-start.2
  0.6 0.0 copy-start.1
  0.7 0.0 copy-start
  0.7 1.1 %pad_add_fusion.1.own = bf16[256,512]{1,0:T(8,128)(2,1)S(1)} fusion(bf16[128,512]{1,0:T(8,128)(2,1)} %param.9, bf16[128,512]{1,0:T(8,128)(2,1)} %param.8), kind=kLoop, calls=%fused_computation.1 | loop fusion | flops 524288 | bytes 524288 | tf_op jit(solution)/shard_map/add | solution.py:493
  1.8 3.0 %collective-permute-start = (bf16[256,512]{1,0:T(8,128)(2,1)S(1)}, bf16[256,512]{1,0:T(8,128)(2,1)S(1)}, u32[]{:S(2)}, u32[]{:S(2)}) collective-permute-start(bf16[256,512]{1,0:T(8,128)(2,1)S(1)} %pad_add_fusion.1.own), channel_id=1, source_target_pairs={{8,0},{16,8},{24,16},{28,24},{20,28},{12,20},{4,12},{0,4},{9,1},{1... | collective-permute-start | bytes 786440 | tf_op jit(solution)/shard_map/ppermute | solution.py:40
  4.8 0.0 collective-permute-start.2
  4.8 3.2 %collective-permute-start.3 = (bf16[256,512]{1,0:T(8,128)(2,1)S(1)}, bf16[256,512]{1,0:T(8,128)(2,1)S(1)}, u32[]{:S(2)}, u32[]{:S(2)}) collective-permute-start(bf16[256,512]{1,0:T(8,128)(2,1)S(1)} %pad_add_fusion.1.own), channel_id=1, source_target_pairs={{0,8},{8,16},{16,24},{24,28},{28,20},{20,12},{12,4},{4,0},{1,9},{9... | collective-permute-start | bytes 786440 | tf_op jit(solution)/shard_map/ppermute | solution.py:40
  7.9 1.1 %pad_add_fusion.seen.joined = bf16[384,512]{1,0:T(8,128)(2,1)S(1)} fusion(bf16[128,512]{1,0:T(8,128)(2,1)} %param.13, bf16[128,512]{1,0:T(8,128)(2,1)} %param.10, bf16[128,512]{1,0:T(8,128)(2,1)} %param.7), kind=kLoop, calls=%fused_computation | loop fusion | flops 1179648 | bytes 786432 | tf_op jit(solution)/shard_map/add | solution.py:496
  9.0 2.2 %collective-permute-done.block = bf16[256,512]{1,0:T(8,128)(2,1)S(1)} collective-permute-done((bf16[256,512]{1,0:T(8,128)(2,1)S(1)}, bf16[256,512]{1,0:T(8,128)(2,1)S(1)}, u32[]{:S(2)}, u32[]{:S(2)}) %collective-permute-start) | collective-permute-done | bytes 262176 | tf_op jit(solution)/shard_map/ppermute | solution.py:40
  11.2 1.7 %collective-permute-start.1 = (bf16[256,512]{1,0:T(8,128)(2,1)S(1)}, bf16[256,512]{1,0:T(8,128)(2,1)S(1)}, u32[]{:S(2)}, u32[]{:S(2)}) collective-permute-start(bf16[256,512]{1,0:T(8,128)(2,1)S(1)} %turn.1.seen.second), channel_id=1, source_target_pairs={{0,4},{4,0},{8,12},{12,8},{16,20},{20,16},{24,28},{28,24},{1,5},{5... | collective-permute-start | bytes 786440 | tf_op jit(solution)/shard_map/ppermute | solution.py:29
  12.9 0.0 copy-done.2
  12.9 1.5 %collective-permute-start.5 = (bf16[128,512]{1,0:T(8,128)(2,1)S(1)}, bf16[128,512]{1,0:T(8,128)(2,1)S(1)}, u32[]{:S(2)}, u32[]{:S(2)}) collective-permute-start(bf16[128,512]{1,0:T(8,128)(2,1)S(1)} %copy-done.2), channel_id=1, source_target_pairs={{0,2},{1,3},{2,0},{3,1},{4,6},{5,7},{6,4},{7,5},{8,10},{9,11},{10,... | collective-permute-start | bytes 393224 | tf_op jit(solution)/shard_map/ppermute | solution.py:29
  14.5 0.6 %collective-permute-start.4 = (bf16[128,512]{1,0:T(8,128)(2,1)S(1)}, bf16[128,512]{1,0:T(8,128)(2,1)S(1)}, u32[]{:S(2)}, u32[]{:S(2)}) collective-permute-start(bf16[128,512]{1,0:T(8,128)(2,1)S(1)} %get-tuple-element.41.q), channel_id=1, source_target_pairs={{8,0},{16,8},{24,16},{28,24},{20,28},{12,20},{4,12},{0,4},{9,1},{1... | collective-permute-start | bytes 393224 | tf_op jit(solution)/shard_map/ppermute | solution.py:40
  15.1 0.0 collective-permute-done.2.near
  15.1 0.0 copy-done.1
  15.1 0.3 collective-permute-start.6
  15.4 0.0 collective-permute-done.3.first
  15.4 0.6 %forward.1 = (f32[128,512]{1,0:T(8,128)S(1)}, f32[128,512]{1,0:T(8,128)S(1)}, f32[128,512]{1,0:T(8,128)S(1)}) custom-call(bf16[128,512]{1,0:T(8,128)(2,1)S(1)} %get-tuple-element.41.q, bf16[256,512]{1,0:T(8,128)(2,1)S(1)} %pad_add_fusion.1.own, bf16[256,512]{1,0:T(8,128)(2,1)S(1)} %collective-permute-done.2.near, ...), custom_call_target="tpu_custom_call" | custom-call | bytes 3690000 | tf_op jit(solution)/shard_map/forward/pallas_call | solution.py:76
  16.0 3.1 %collective-permute-done.1.relay = bf16[256,512]{1,0:T(8,128)(2,1)S(1)} collective-permute-done((bf16[256,512]{1,0:T(8,128)(2,1)S(1)}, bf16[256,512]{1,0:T(8,128)(2,1)S(1)}, u32[]{:S(2)}, u32[]{:S(2)}) %collective-permute-start.1) | collective-permute-done | bytes 262176 | tf_op jit(solution)/shard_map/ppermute | solution.py:29
  19.1 0.0 copy-done
  19.1 0.9 %project.1 = (bf16[128,512]{1,0:T(8,128)(2,1)S(1)}, f32[128,512]{1,0:T(8,128)S(1)}, bf16[128,1024]{1,0:T(8,128)(2,1)S(1)}, bf16[128,1024]{1,0:T(8,128)(2,1)S(1)}) custom-call(bf16[128,512]{1,0:T(8,128)(2,1)S(1)} %get-tuple-element.41.q, bf16[256,512]{1,0:T(8,128)(2,1)S(1)} %collective-permute-done.1.relay, f32[128,512]{1,0:T(8,128)S(1)} %get-tuple-element.42.sums, ...), custom_call_target="tpu_custom_call" | custom-call | bytes 3690000 | tf_op jit(solution)/shard_map/project/pallas_call | solution.py:76
  20.0 0.0 collective-permute-done.6.seen_b.taps_other
  20.0 0.0 collective-permute-done.5.seen_a.cot_other
  20.0 0.4 collective-permute-done.4.q_second
  20.5 0.1 collective-permute-start.7
  20.5 1.5 %collective-permute-done.7.core = bf16[128,1024]{1,0:T(8,128)(2,1)S(1)} collective-permute-done((bf16[128,1024]{1,0:T(8,128)(2,1)S(1)}, bf16[128,1024]{1,0:T(8,128)(2,1)S(1)}, u32[]{:S(2)}, u32[]{:S(2)}) %collective-permute-start.7) | collective-permute-done | bytes 262176 | tf_op jit(solution)/shard_map/ppermute | solution.py:29
  22.1 0.1 join.1
  22.2 1.6 %collective-permute-start.11 = (bf16[128,1024]{1,0:T(8,128)(2,1)S(1)}, bf16[128,1024]{1,0:T(8,128)(2,1)S(1)}, u32[]{:S(2)}, u32[]{:S(2)}) collective-permute-start(bf16[128,1024]{1,0:T(8,128)(2,1)S(1)} %get-tuple-element.55.chip), channel_id=1, source_target_pairs={{0,2},{1,3},{2,0},{3,1},{4,6},{5,7},{6,4},{7,5},{8,10},{9,11},{10,... | collective-permute-start | bytes 786440 | tf_op jit(solution)/shard_map/ppermute | solution.py:29
  23.8 2.5 %collective-permute-start.8 = (bf16[48,1024]{1,0:T(8,128)(2,1)S(1)}, bf16[48,1024]{1,0:T(8,128)(2,1)S(1)}, u32[]{:S(2)}, u32[]{:S(2)}) collective-permute-start(bf16[48,1024]{1,0:T(8,128)(2,1)S(1)} %get-tuple-element.51), channel_id=1, source_target_pairs={{0,4},{4,0},{8,12},{12,8},{16,20},{20,16},{24,28},{28,24},{1,5},{5... | collective-permute-start | bytes 294920 | tf_op jit(solution)/shard_map/ppermute | solution.py:29
  26.2 0.0 collective-permute-start.9
  26.2 1.5 %collective-permute-start.12 = (bf16[128,512]{1,0:T(8,128)(2,1)S(1)}, bf16[128,512]{1,0:T(8,128)(2,1)S(1)}, u32[]{:S(2)}, u32[]{:S(2)}) collective-permute-start(bf16[128,512]{1,0:T(8,128)(2,1)S(1)} %get-tuple-element.50.q.refs_0_), channel_id=1, source_target_pairs={{0,8},{8,16},{16,24},{24,28},{28,20},{20,12},{12,4},{4,0},{1,9},{9... | collective-permute-start | bytes 393224 | tf_op jit(solution)/shard_map/ppermute | solution.py:40
  27.7 0.0 collective-permute-start.13
  27.7 2.7 %collective-permute-done.8.rim_near = bf16[48,1024]{1,0:T(8,128)(2,1)S(1)} collective-permute-done((bf16[48,1024]{1,0:T(8,128)(2,1)S(1)}, bf16[48,1024]{1,0:T(8,128)(2,1)S(1)}, u32[]{:S(2)}, u32[]{:S(2)}) %collective-permute-start.8) | collective-permute-done | bytes 98336 | tf_op jit(solution)/shard_map/ppermute | solution.py:29
  30.4 0.0 collective-permute-done.9.rim_far
  30.4 0.6 %collective-permute-start.10 = (bf16[64,1024]{1,0:T(8,128)(2,1)S(1)}, bf16[64,1024]{1,0:T(8,128)(2,1)S(1)}, u32[]{:S(2)}, u32[]{:S(2)}) collective-permute-start(bf16[64,1024]{1,0:T(8,128)(2,1)S(1)} %get-tuple-element.54.ends), channel_id=1, source_target_pairs={{0,2},{1,3},{2,0},{3,1},{4,6},{5,7},{6,4},{7,5},{8,10},{9,11},{10,... | collective-permute-start | bytes 393224 | tf_op jit(solution)/shard_map/ppermute | solution.py:29
  31.0 2.5 %collective-permute-start.14 = (bf16[128,512]{1,0:T(8,128)(2,1)S(1)}, bf16[128,512]{1,0:T(8,128)(2,1)S(1)}, u32[]{:S(2)}, u32[]{:S(2)}) collective-permute-start(bf16[128,512]{1,0:T(8,128)(2,1)S(1)} %get-tuple-element.61), channel_id=1, source_target_pairs={{0,4},{4,0},{8,12},{12,8},{16,20},{20,16},{24,28},{28,24},{1,5},{5... | collective-permute-start | bytes 393224 | tf_op jit(solution)/shard_map/ppermute | solution.py:29
  33.5 0.0 collective-permute-done.12.seen.refs_2_
  33.5 0.0 collective-permute-done.11.across
  33.5 2.8 %conv_inner.1 = (bf16[128,512]{1,0:T(8,128)(2,1)S(1)}, f32[32,512]{1,0:T(8,128)S(1)}, f32[64,1024]{1,0:T(8,128)S(1)}, f32[128,1024]{1,0:T(8,128)S(1)}) custom-call(bf16[128,1024]{1,0:T(8,128)(2,1)S(1)} %get-tuple-element.55.chip, bf16[128,1024]{1,0:T(8,128)(2,1)S(1)} %collective-permute-done.11.across, bf16[128,512]{1,0:T(8,128)(2,1)S(1)} %get-tuple-element.49.cot, ...), custom_call_target="tpu_custom_call" | custom-call | bytes 11439000 | tf_op jit(solution)/shard_map/conv_inner/pallas_call | solution.py:76
  36.3 0.0 collective-permute-done.13.seen.refs_1_
  36.3 0.0 collective-permute-done.10.ends_across
  36.4 1.1 %conv_edge.1 = (bf16[128,512]{1,0:T(8,128)(2,1)S(1)}, bf16[128,1024]{1,0:T(8,128)(2,1)S(1)}) custom-call(bf16[64,1024]{1,0:T(8,128)(2,1)S(1)} %get-tuple-element.54.ends, bf16[64,1024]{1,0:T(8,128)(2,1)S(1)} %collective-permute-done.10.ends_across, bf16[48,1024]{1,0:T(8,128)(2,1)S(1)} %collective-permute-done.8.rim_near, ...), custom_call_target="tpu_custom_call" | custom-call | bytes 5166000 | tf_op jit(solution)/shard_map/conv_edge/pallas_call | solution.py:76
  37.5 0.0 collective-permute-done.14.seen.refs_4_.query
  37.5 0.1 collective-permute-start.15
  37.6 0.5 upstream_own.1
  38.1 1.0 %collective-permute-done.15.core = bf16[128,1024]{1,0:T(8,128)(2,1)S(1)} collective-permute-done((bf16[128,1024]{1,0:T(8,128)(2,1)S(1)}, bf16[128,1024]{1,0:T(8,128)(2,1)S(1)}, u32[]{:S(2)}, u32[]{:S(2)}) %collective-permute-start.15) | collective-permute-done | bytes 262176 | tf_op jit(solution)/shard_map/ppermute | solution.py:29
  39.1 0.7 %upstream.1 = (bf16[144,512]{1,0:T(8,128)(2,1)S(1)}, f32[128,512]{1,0:T(8,128)S(1)}) custom-call(bf16[128,1024]{1,0:T(8,128)(2,1)S(1)} %collective-permute-done.15.core, bf16[512,2048]{1,0:T(8,128)(2,1)S(1)} %copy-done, bf16[128,512]{1,0:T(8,128)(2,1)S(1)} %get-tuple-element.62.att, f32[128,512]{1,0:T(8,128)S(1)} %get-tuple-element.64.partial, ...), custom_call_target="tpu_custom_call" | custom-call | bytes 2214000 | tf_op jit(solution)/shard_map/upstream/pallas_call | solution.py:76
  39.8 0.2 collective-permute-start.17
  40.0 1.8 %collective-permute-start.18 = (bf16[144,512]{1,0:T(8,128)(2,1)S(1)}, bf16[144,512]{1,0:T(8,128)(2,1)S(1)}, u32[]{:S(2)}, u32[]{:S(2)}) collective-permute-start(bf16[144,512]{1,0:T(8,128)(2,1)S(1)} %get-tuple-element.66.message.refs_5_), channel_id=1, source_target_pairs={{0,8},{8,16},{16,24},{24,28},{28,20},{20,12},{12,4},{4,0},{1,9},{9... | collective-permute-start | bytes 442376 | tf_op jit(solution)/shard_map/ppermute | solution.py:40
  41.8 0.3 collective-permute-start.19
  42.0 0.0 collective-permute-start.16
  42.0 1.5 %query_grad.1 = (bf16[128,512]{1,0:T(8,128)(2,1)}, bf16[128,512]{1,0:T(8,128)(2,1)}, bf16[128,512]{1,0:T(8,128)(2,1)}) custom-call(bf16[128,512]{1,0:T(8,128)(2,1)S(1)} %get-tuple-element.50.q.refs_0_, bf16[256,512]{1,0:T(8,128)(2,1)S(1)} %pad_add_fusion.1.own, bf16[256,512]{1,0:T(8,128)(2,1)S(1)} %collective-permute-done.2.near, ...), custom_call_target="tpu_custom_call" | custom-call | bytes 6642000 | tf_op jit(solution)/shard_map/query_grad/pallas_call | solution.py:76
  43.6 0.0 collective-permute-done.17.refs_6_
  43.6 2.5 %collective-permute-done.18.refs_7_ = bf16[144,512]{1,0:T(8,128)(2,1)S(1)} collective-permute-done((bf16[144,512]{1,0:T(8,128)(2,1)S(1)}, bf16[144,512]{1,0:T(8,128)(2,1)S(1)}, u32[]{:S(2)}, u32[]{:S(2)}) %collective-permute-start.18) | collective-permute-done | bytes 147488 | tf_op jit(solution)/shard_map/ppermute | solution.py:40
  46.1 2.4 %collective-permute-done.19.refs_8_ = bf16[144,512]{1,0:T(8,128)(2,1)S(1)} collective-permute-done((bf16[144,512]{1,0:T(8,128)(2,1)S(1)}, bf16[144,512]{1,0:T(8,128)(2,1)S(1)}, u32[]{:S(2)}, u32[]{:S(2)}) %collective-permute-start.19) | collective-permute-done | bytes 147488 | tf_op jit(solution)/shard_map/ppermute | solution.py:40
  48.6 0.9 %key_part.1 = (f32[128,512]{1,0:T(8,128)S(1)}, f32[128,512]{1,0:T(8,128)S(1)}, f32[128,512]{1,0:T(8,128)S(1)}) custom-call(bf16[256,512]{1,0:T(8,128)(2,1)S(1)} %pad_add_fusion.1.own, bf16[128,512]{1,0:T(8,128)(2,1)S(1)} %get-tuple-element.50.q.refs_0_, bf16[128,512]{1,0:T(8,128)(2,1)S(1)} %collective-permute-done.13.seen.refs_1_, ...), custom_call_target="tpu_custom_call" | custom-call | bytes 5535000 | tf_op jit(solution)/shard_map/key_part/pallas_call | solution.py:76
  49.4 0.0 collective-permute-done.16.message
  49.4 1.0 %key_grad.1 = (bf16[128,512]{1,0:T(8,128)(2,1)}, bf16[128,512]{1,0:T(8,128)(2,1)}) custom-call(bf16[256,512]{1,0:T(8,128)(2,1)S(1)} %pad_add_fusion.1.own, bf16[128,512]{1,0:T(8,128)(2,1)S(1)} %collective-permute-done.14.seen.refs_4_.query, bf16[144,512]{1,0:T(8,128)(2,1)S(1)} %collective-permute-done.16.message, f32[128,512]{1,0:T(8,128)S(1)} %get-tuple-element.72.late, ...), custom_call_target="tpu_custom_call" | custom-call | bytes 3690000 | tf_op jit(solution)/shard_map/key_grad/pallas_call | solution.py:76
  (5 shorter events, 0.1 us)
Async XLA Ops:
  0.6 12.3 %copy-start.2 = (bf16[128,512]{1,0:T(8,128)(2,1)S(1)}, bf16[128,512]{1,0:T(8,128)(2,1)}, u32[]{:S(2)}) copy-start(bf16[128,512]{1,0:T(8,128)(2,1)} %param.13) | copy-start | bytes 393220
  0.6 14.4 %copy-start.1 = (f32[31,512]{1,0:T(8,128)S(1)}, f32[31,512]{1,0:T(8,128)}, u32[]{:S(2)}) copy-start(f32[31,512]{1,0:T(8,128)} %taps.3) | copy-start | bytes 190468
  0.7 18.5 %copy-start = (bf16[512,2048]{1,0:T(8,128)(2,1)S(1)}, bf16[512,2048]{1,0:T(8,128)(2,1)}, u32[]{:S(2)}) copy-start(bf16[512,2048]{1,0:T(8,128)(2,1)} %weight.5) | copy-start | bytes 6291460
  1.8 9.4 %collective-permute-start = (bf16[256,512]{1,0:T(8,128)(2,1)S(1)}, bf16[256,512]{1,0:T(8,128)(2,1)S(1)}, u32[]{:S(2)}, u32[]{:S(2)}) collective-permute-start(bf16[256,512]{1,0:T(8,128)(2,1)S(1)} %pad_add_fusion.1.own), channel_id=1, source_target_pairs={{8,0},{16,8},{24,16},{28,24},{20,28},{12,20},{4,12},{0,4},{9,1},{1... | collective-permute-start | bytes 786440 | tf_op jit(solution)/shard_map/ppermute | solution.py:40
  4.8 10.3 %collective-permute-start.2 = (bf16[256,512]{1,0:T(8,128)(2,1)S(1)}, bf16[256,512]{1,0:T(8,128)(2,1)S(1)}, u32[]{:S(2)}, u32[]{:S(2)}) collective-permute-start(bf16[256,512]{1,0:T(8,128)(2,1)S(1)} %pad_add_fusion.1.own), channel_id=1, source_target_pairs={{0,1},{1,0},{2,3},{3,2},{4,5},{5,4},{6,7},{7,6},{8,12},{9,13},{10,... | collective-permute-start | bytes 786440 | tf_op jit(solution)/shard_map/ppermute | solution.py:51
  4.8 10.6 %collective-permute-start.3 = (bf16[256,512]{1,0:T(8,128)(2,1)S(1)}, bf16[256,512]{1,0:T(8,128)(2,1)S(1)}, u32[]{:S(2)}, u32[]{:S(2)}) collective-permute-start(bf16[256,512]{1,0:T(8,128)(2,1)S(1)} %pad_add_fusion.1.own), channel_id=1, source_target_pairs={{0,8},{8,16},{16,24},{24,28},{28,20},{20,12},{12,4},{4,0},{1,9},{9... | collective-permute-start | bytes 786440 | tf_op jit(solution)/shard_map/ppermute | solution.py:40
  11.2 7.9 %collective-permute-start.1 = (bf16[256,512]{1,0:T(8,128)(2,1)S(1)}, bf16[256,512]{1,0:T(8,128)(2,1)S(1)}, u32[]{:S(2)}, u32[]{:S(2)}) collective-permute-start(bf16[256,512]{1,0:T(8,128)(2,1)S(1)} %turn.1.seen.second), channel_id=1, source_target_pairs={{0,4},{4,0},{8,12},{12,8},{16,20},{20,16},{24,28},{28,24},{1,5},{5... | collective-permute-start | bytes 786440 | tf_op jit(solution)/shard_map/ppermute | solution.py:29
  12.9 7.1 %collective-permute-start.5 = (bf16[128,512]{1,0:T(8,128)(2,1)S(1)}, bf16[128,512]{1,0:T(8,128)(2,1)S(1)}, u32[]{:S(2)}, u32[]{:S(2)}) collective-permute-start(bf16[128,512]{1,0:T(8,128)(2,1)S(1)} %copy-done.2), channel_id=1, source_target_pairs={{0,2},{1,3},{2,0},{3,1},{4,6},{5,7},{6,4},{7,5},{8,10},{9,11},{10,... | collective-permute-start | bytes 393224 | tf_op jit(solution)/shard_map/ppermute | solution.py:29
  14.5 5.9 %collective-permute-start.4 = (bf16[128,512]{1,0:T(8,128)(2,1)S(1)}, bf16[128,512]{1,0:T(8,128)(2,1)S(1)}, u32[]{:S(2)}, u32[]{:S(2)}) collective-permute-start(bf16[128,512]{1,0:T(8,128)(2,1)S(1)} %get-tuple-element.41.q), channel_id=1, source_target_pairs={{8,0},{16,8},{24,16},{28,24},{20,28},{12,20},{4,12},{0,4},{9,1},{1... | collective-permute-start | bytes 393224 | tf_op jit(solution)/shard_map/ppermute | solution.py:40
  15.1 4.9 %collective-permute-start.6 = (f32[31,512]{1,0:T(8,128)S(1)}, f32[31,512]{1,0:T(8,128)S(1)}, u32[]{:S(2)}, u32[]{:S(2)}) collective-permute-start(f32[31,512]{1,0:T(8,128)S(1)} %copy-done.1), channel_id=1, source_target_pairs={{0,2},{1,3},{2,0},{3,1},{4,6},{5,7},{6,4},{7,5},{8,10},{9,11},{10,... | collective-permute-start | bytes 190472 | tf_op jit(solution)/shard_map/ppermute | solution.py:29
  20.5 1.6 %collective-permute-start.7 = (bf16[128,1024]{1,0:T(8,128)(2,1)S(1)}, bf16[128,1024]{1,0:T(8,128)(2,1)S(1)}, u32[]{:S(2)}, u32[]{:S(2)}) collective-permute-start(bf16[128,1024]{1,0:T(8,128)(2,1)S(1)} %get-tuple-element.47), channel_id=1, source_target_pairs={{0,1},{1,0},{2,3},{3,2},{4,5},{5,4},{6,7},{7,6},{8,9},{9,8},{10,11... | collective-permute-start | bytes 786440 | tf_op jit(solution)/shard_map/ppermute | solution.py:29
  22.2 11.3 %collective-permute-start.11 = (bf16[128,1024]{1,0:T(8,128)(2,1)S(1)}, bf16[128,1024]{1,0:T(8,128)(2,1)S(1)}, u32[]{:S(2)}, u32[]{:S(2)}) collective-permute-start(bf16[128,1024]{1,0:T(8,128)(2,1)S(1)} %get-tuple-element.55.chip), channel_id=1, source_target_pairs={{0,2},{1,3},{2,0},{3,1},{4,6},{5,7},{6,4},{7,5},{8,10},{9,11},{10,... | collective-permute-start | bytes 786440 | tf_op jit(solution)/shard_map/ppermute | solution.py:29
  23.8 6.7 %collective-permute-start.8 = (bf16[48,1024]{1,0:T(8,128)(2,1)S(1)}, bf16[48,1024]{1,0:T(8,128)(2,1)S(1)}, u32[]{:S(2)}, u32[]{:S(2)}) collective-permute-start(bf16[48,1024]{1,0:T(8,128)(2,1)S(1)} %get-tuple-element.51), channel_id=1, source_target_pairs={{0,4},{4,0},{8,12},{12,8},{16,20},{20,16},{24,28},{28,24},{1,5},{5... | collective-permute-start | bytes 294920 | tf_op jit(solution)/shard_map/ppermute | solution.py:29
  26.2 4.2 %collective-permute-start.9 = (bf16[48,1024]{1,0:T(8,128)(2,1)S(1)}, bf16[48,1024]{1,0:T(8,128)(2,1)S(1)}, u32[]{:S(2)}, u32[]{:S(2)}) collective-permute-start(bf16[48,1024]{1,0:T(8,128)(2,1)S(1)} %get-tuple-element.52), channel_id=1, source_target_pairs={{0,1},{1,0},{2,3},{3,2},{4,8},{5,9},{6,10},{7,11},{8,4},{9,5},{10,... | collective-permute-start | bytes 294920 | tf_op jit(solution)/shard_map/ppermute | solution.py:51
  26.2 7.3 %collective-permute-start.12 = (bf16[128,512]{1,0:T(8,128)(2,1)S(1)}, bf16[128,512]{1,0:T(8,128)(2,1)S(1)}, u32[]{:S(2)}, u32[]{:S(2)}) collective-permute-start(bf16[128,512]{1,0:T(8,128)(2,1)S(1)} %get-tuple-element.50.q.refs_0_), channel_id=1, source_target_pairs={{0,8},{8,16},{16,24},{24,28},{28,20},{20,12},{12,4},{4,0},{1,9},{9... | collective-permute-start | bytes 393224 | tf_op jit(solution)/shard_map/ppermute | solution.py:40
  27.7 8.6 %collective-permute-start.13 = (bf16[128,512]{1,0:T(8,128)(2,1)S(1)}, bf16[128,512]{1,0:T(8,128)(2,1)S(1)}, u32[]{:S(2)}, u32[]{:S(2)}) collective-permute-start(bf16[128,512]{1,0:T(8,128)(2,1)S(1)} %get-tuple-element.50.q.refs_0_), channel_id=1, source_target_pairs={{0,1},{1,0},{2,3},{3,2},{4,5},{5,4},{6,7},{7,6},{8,12},{9,13},{10,... | collective-permute-start | bytes 393224 | tf_op jit(solution)/shard_map/ppermute | solution.py:51
  30.4 5.9 %collective-permute-start.10 = (bf16[64,1024]{1,0:T(8,128)(2,1)S(1)}, bf16[64,1024]{1,0:T(8,128)(2,1)S(1)}, u32[]{:S(2)}, u32[]{:S(2)}) collective-permute-start(bf16[64,1024]{1,0:T(8,128)(2,1)S(1)} %get-tuple-element.54.ends), channel_id=1, source_target_pairs={{0,2},{1,3},{2,0},{3,1},{4,6},{5,7},{6,4},{7,5},{8,10},{9,11},{10,... | collective-permute-start | bytes 393224 | tf_op jit(solution)/shard_map/ppermute | solution.py:29
  31.0 6.5 %collective-permute-start.14 = (bf16[128,512]{1,0:T(8,128)(2,1)S(1)}, bf16[128,512]{1,0:T(8,128)(2,1)S(1)}, u32[]{:S(2)}, u32[]{:S(2)}) collective-permute-start(bf16[128,512]{1,0:T(8,128)(2,1)S(1)} %get-tuple-element.61), channel_id=1, source_target_pairs={{0,4},{4,0},{8,12},{12,8},{16,20},{20,16},{24,28},{28,24},{1,5},{5... | collective-permute-start | bytes 393224 | tf_op jit(solution)/shard_map/ppermute | solution.py:29
  37.5 1.6 %collective-permute-start.15 = (bf16[128,1024]{1,0:T(8,128)(2,1)S(1)}, bf16[128,1024]{1,0:T(8,128)(2,1)S(1)}, u32[]{:S(2)}, u32[]{:S(2)}) collective-permute-start(bf16[128,1024]{1,0:T(8,128)(2,1)S(1)} %hand.1.own.grad_here), channel_id=1, source_target_pairs={{0,1},{1,0},{2,3},{3,2},{4,5},{5,4},{6,7},{7,6},{8,9},{9,8},{10,11... | collective-permute-start | bytes 786440 | tf_op jit(solution)/shard_map/ppermute | solution.py:29
  39.8 3.8 %collective-permute-start.17 = (bf16[144,512]{1,0:T(8,128)(2,1)S(1)}, bf16[144,512]{1,0:T(8,128)(2,1)S(1)}, u32[]{:S(2)}, u32[]{:S(2)}) collective-permute-start(bf16[144,512]{1,0:T(8,128)(2,1)S(1)} %get-tuple-element.66.message.refs_5_), channel_id=1, source_target_pairs={{0,1},{1,0},{2,3},{3,2},{4,5},{5,4},{6,7},{7,6},{8,12},{9,13},{10,... | collective-permute-start | bytes 442376 | tf_op jit(solution)/shard_map/ppermute | solution.py:51
  40.0 6.1 %collective-permute-start.18 = (bf16[144,512]{1,0:T(8,128)(2,1)S(1)}, bf16[144,512]{1,0:T(8,128)(2,1)S(1)}, u32[]{:S(2)}, u32[]{:S(2)}) collective-permute-start(bf16[144,512]{1,0:T(8,128)(2,1)S(1)} %get-tuple-element.66.message.refs_5_), channel_id=1, source_target_pairs={{0,8},{8,16},{16,24},{24,28},{28,20},{20,12},{12,4},{4,0},{1,9},{9... | collective-permute-start | bytes 442376 | tf_op jit(solution)/shard_map/ppermute | solution.py:40
  41.8 6.8 %collective-permute-start.19 = (bf16[144,512]{1,0:T(8,128)(2,1)S(1)}, bf16[144,512]{1,0:T(8,128)(2,1)S(1)}, u32[]{:S(2)}, u32[]{:S(2)}) collective-permute-start(bf16[144,512]{1,0:T(8,128)(2,1)S(1)} %get-tuple-element.66.message.refs_5_), channel_id=1, source_target_pairs={{8,0},{16,8},{24,16},{28,24},{20,28},{12,20},{4,12},{0,4},{9,1},{1... | collective-permute-start | bytes 442376 | tf_op jit(solution)/shard_map/ppermute | solution.py:40
  42.0 7.4 %collective-permute-start.16 = (bf16[144,512]{1,0:T(8,128)(2,1)S(1)}, bf16[144,512]{1,0:T(8,128)(2,1)S(1)}, u32[]{:S(2)}, u32[]{:S(2)}) collective-permute-start(bf16[144,512]{1,0:T(8,128)(2,1)S(1)} %get-tuple-element.66.message.refs_5_), channel_id=1, source_target_pairs={{0,1},{1,0},{2,3},{3,2},{4,8},{5,9},{6,10},{7,11},{8,4},{9,5},{10,... | collective-permute-start | bytes 442376 | tf_op jit(solution)/shard_map/ppermute | solution.py:51

commit v16 on v15

--- a/solution.py
+++ b/solution.py
@@ -57,14 +57,6 @@
 
 def outer_swap(block):
     return total_swap(block, lambda i, count: ((i + 1) ^ 1) - 1 if 0 < i < count - 1 else None)
-
-
-def window_of(block, before_relay=lambda second: second):
-    second = ring(block, 1)
-    first = ring(block, 0)
-    near = inner_swap(block)
-    second = before_relay(second)
-    return near, first, second, pair_swap(second, "ctx", 1)
 
 
 VMEM = pl.BlockSpec(memory_space=pltpu.VMEM)
@@ -497,12 +489,8 @@
         lax.pad(rows, zero, ((k * frames, (2 - k) * frames, 0), (0, 0, 0)))
         for k, rows in enumerate((query_rows, inputs, cotangent))
     )
-    near, first, second, relay = window_of(
-        kv,
-        lambda second: kernel_call(
-            turn_body, (shaped(kv.shape, BF16),), (second, joined), 0.1, "turn", 1
-        )[0],
-    )
+    near, first, second = inner_swap(kv), ring(kv, 0), ring(kv, 1)
+    relay = outer_swap(kv)
     cot_other = pair_swap(cotangent, "mp", 2)
     taps_other = pair_swap(kernel, "mp", 2)
     query, inputs, cotangent = kernel_call(

time: 50.6 us -> 54.1 us (1.069)
  starting transfers between devices: 21.3 us -> 28.3 us
  waiting for transfers between devices: 16 us -> 12.5 us
    ppermute x6, starting transfers between devices: 10.2 us -> 21.2 us  [ring(): return lax.ppermute(block, 'ctx', ring_routes(lax.axis_size('ctx'))[way])]
    ppermute x9 -> x8, starting transfers between devices: 10.8 us -> 6.95 us  [pair_swap(): lax.ppermute(block, axis, [(i, i ^ bit) for i in range(lax.axis_size(axis...]
    ppermute x9 -> x8, waiting for transfers between devices: 8.38 us -> 5.52 us  [pair_swap(): lax.ppermute(block, axis, [(i, i ^ bit) for i in range(lax.axis_size(axis...]
    ppermute x6, waiting for transfers between devices: 7.57 us -> 6.91 us  [ring(): return lax.ppermute(block, 'ctx', ring_routes(lax.axis_size('ctx'))[way])]
    pallas_call x15 -> x14, Pallas kernels: 10.2 us -> 10.2 us  [kernel_call(): pl.pallas_call(body, out_shape=outs, in_specs=[VMEM] * (len(args) - unrea...]
  transfers between devices with their start and end apart: 20 -> 20, of which waited for: 8 -> 7; matrix products, arithmetic and copies ran while one was open for 2% -> 2% of each run, Pallas kernels for 17% -> 15%
where the time goes in v16:
time: 54.1 us; the launch traced here: 54 us
  starting transfers between devices  28.3 us (52%)
  waiting for transfers between devices  12.5 us (23%)
  Pallas kernels  10.2 us (19%)
  other arithmetic  2.19 us (4%)
  between operations  0.84 us (2%)
    ppermute x6, starting transfers between devices, ring(): return lax.ppermute(block, 'ctx', ring_routes(lax.axis_size('ctx'))[way])  21.2 us
    pallas_call x14, Pallas kernels, kernel_call(): pl.pallas_call(body, out_shape=outs, in_specs=[VMEM] * (len(args) - unrea...  10.2 us
    ppermute x8, starting transfers between devices, pair_swap(): lax.ppermute(block, axis, [(i, i ^ bit) for i in range(lax.axis_size(axis...  6.95 us
    ppermute x6, waiting for transfers between devices, ring(): return lax.ppermute(block, 'ctx', ring_routes(lax.axis_size('ctx'))[way])  6.91 us
    ppermute x8, waiting for transfers between devices, pair_swap(): lax.ppermute(block, axis, [(i, i ^ bit) for i in range(lax.axis_size(axis...  5.52 us
    add x1, other arithmetic, per_device(): lax.pad(key_rows, zero, ((0, frames, 0), (0, 0, 0)))  1.13 us
  transfers between devices with their start and end apart: 20, of which 7 were waited for; matrix products, arithmetic and copies ran while one was open for 2% of the time, Pallas kernels for 15%

profile of v16, /device:TPU:0, one launch (start us, length us, event | category | flops | bytes accessed | tf_op | source)
XLA Modules:
  0.0 54.0 jit_solution(3184658993435578485)
XLA Ops:
  0.6 0.0 copy-start
  0.6 1.1 %pad_add_fusion.1.own = bf16[256,512]{1,0:T(8,128)(2,1)S(1)} fusion(bf16[128,512]{1,0:T(8,128)(2,1)} %param.9, bf16[128,512]{1,0:T(8,128)(2,1)} %param.8), kind=kLoop, calls=%fused_computation.1 | loop fusion | flops 524288 | bytes 524288 | tf_op jit(solution)/shard_map/add | solution.py:485
  1.8 3.0 %collective-permute-start = (bf16[256,512]{1,0:T(8,128)(2,1)S(1)}, bf16[256,512]{1,0:T(8,128)(2,1)S(1)}, u32[]{:S(2)}, u32[]{:S(2)}) collective-permute-start(bf16[256,512]{1,0:T(8,128)(2,1)S(1)} %pad_add_fusion.1.own), channel_id=1, source_target_pairs={{8,0},{16,8},{24,16},{28,24},{20,28},{12,20},{4,12},{0,4},{9,1},{1... | collective-permute-start | bytes 786440 | tf_op jit(solution)/shard_map/ppermute | solution.py:40
  4.8 0.0 collective-permute-start.2
  4.8 3.2 %collective-permute-start.3 = (bf16[256,512]{1,0:T(8,128)(2,1)S(1)}, bf16[256,512]{1,0:T(8,128)(2,1)S(1)}, u32[]{:S(2)}, u32[]{:S(2)}) collective-permute-start(bf16[256,512]{1,0:T(8,128)(2,1)S(1)} %pad_add_fusion.1.own), channel_id=1, source_target_pairs={{0,8},{8,16},{16,24},{24,28},{28,20},{20,12},{12,4},{4,0},{1,9},{9... | collective-permute-start | bytes 786440 | tf_op jit(solution)/shard_map/ppermute | solution.py:40
  7.9 0.0 collective-permute-start.1
  7.9 1.5 %collective-permute-start.5 = (bf16[128,512]{1,0:T(8,128)(2,1)}, bf16[128,512]{1,0:T(8,128)(2,1)S(1)}, u32[]{:S(2)}, u32[]{:S(2)}) collective-permute-start(bf16[128,512]{1,0:T(8,128)(2,1)} %param.13), channel_id=1, source_target_pairs={{0,2},{1,3},{2,0},{3,1},{4,6},{5,7},{6,4},{7,5},{8,10},{9,11},{10,... | collective-permute-start | bytes 393224 | tf_op jit(solution)/shard_map/ppermute | solution.py:29
  9.4 1.1 %pad_add_fusion.joined = bf16[384,512]{1,0:T(8,128)(2,1)S(1)} fusion(bf16[128,512]{1,0:T(8,128)(2,1)} %param.13, bf16[128,512]{1,0:T(8,128)(2,1)} %param.10, bf16[128,512]{1,0:T(8,128)(2,1)} %param.7), kind=kLoop, calls=%fused_computation | loop fusion | flops 1179648 | bytes 786432 | tf_op jit(solution)/shard_map/add | solution.py:488
  10.5 1.5 %collective-permute-done.seen.second = bf16[256,512]{1,0:T(8,128)(2,1)S(1)} collective-permute-done((bf16[256,512]{1,0:T(8,128)(2,1)S(1)}, bf16[256,512]{1,0:T(8,128)(2,1)S(1)}, u32[]{:S(2)}, u32[]{:S(2)}) %collective-permute-start) | collective-permute-done | bytes 262176 | tf_op jit(solution)/shard_map/ppermute | solution.py:40
  12.0 5.9 %collective-permute-start.4 = (bf16[128,512]{1,0:T(8,128)(2,1)S(1)}, bf16[128,512]{1,0:T(8,128)(2,1)S(1)}, u32[]{:S(2)}, u32[]{:S(2)}) collective-permute-start(bf16[128,512]{1,0:T(8,128)(2,1)S(1)} %get-tuple-element.41.q), channel_id=1, source_target_pairs={{8,0},{16,8},{24,16},{28,24},{20,28},{12,20},{4,12},{0,4},{9,1},{1... | collective-permute-start | bytes 393224 | tf_op jit(solution)/shard_map/ppermute | solution.py:40
  17.9 0.0 collective-permute-done.2.near
  17.9 0.0 collective-permute-start.6
  17.9 0.0 collective-permute-done.3.first
  17.9 0.6 %forward.1 = (f32[128,512]{1,0:T(8,128)S(1)}, f32[128,512]{1,0:T(8,128)S(1)}, f32[128,512]{1,0:T(8,128)S(1)}) custom-call(bf16[128,512]{1,0:T(8,128)(2,1)S(1)} %get-tuple-element.41.q, bf16[256,512]{1,0:T(8,128)(2,1)S(1)} %pad_add_fusion.1.own, bf16[256,512]{1,0:T(8,128)(2,1)S(1)} %collective-permute-done.2.near, ...), custom_call_target="tpu_custom_call" | custom-call | bytes 3690000 | tf_op jit(solution)/shard_map/forward/pallas_call | solution.py:68
  18.5 0.0 collective-permute-done.1.relay
  18.5 0.0 copy-done
  18.5 0.0 copy-start.1
  18.5 0.9 %project.1 = (bf16[128,512]{1,0:T(8,128)(2,1)S(1)}, f32[128,512]{1,0:T(8,128)S(1)}, bf16[128,1024]{1,0:T(8,128)(2,1)S(1)}, bf16[128,1024]{1,0:T(8,128)(2,1)S(1)}) custom-call(bf16[128,512]{1,0:T(8,128)(2,1)S(1)} %get-tuple-element.41.q, bf16[256,512]{1,0:T(8,128)(2,1)S(1)} %collective-permute-done.1.relay, f32[128,512]{1,0:T(8,128)S(1)} %get-tuple-element.42.sums, ...), custom_call_target="tpu_custom_call" | custom-call | bytes 3690000 | tf_op jit(solution)/shard_map/project/pallas_call | solution.py:68
  19.4 3.0 %collective-permute-done.6.seen_b.taps_other = f32[31,512]{1,0:T(8,128)S(1)} collective-permute-done((f32[31,512]{1,0:T(8,128)}, f32[31,512]{1,0:T(8,128)S(1)}, u32[]{:S(2)}, u32[]{:S(2)}) %collective-permute-start.6) | collective-permute-done | bytes 63520 | tf_op jit(solution)/shard_map/ppermute | solution.py:29
  22.4 0.0 collective-permute-done.5.seen_a.cot_other
  22.4 0.0 collective-permute-done.4.q_second
  22.4 0.1 collective-permute-start.7
  22.5 1.5 %collective-permute-done.7.core = bf16[128,1024]{1,0:T(8,128)(2,1)S(1)} collective-permute-done((bf16[128,1024]{1,0:T(8,128)(2,1)S(1)}, bf16[128,1024]{1,0:T(8,128)(2,1)S(1)}, u32[]{:S(2)}, u32[]{:S(2)}) %collective-permute-start.7) | collective-permute-done | bytes 262176 | tf_op jit(solution)/shard_map/ppermute | solution.py:29
  24.0 0.1 join.1
  24.1 0.1 collective-permute-start.11
  24.2 0.5 %collective-permute-start.8 = (bf16[48,1024]{1,0:T(8,128)(2,1)S(1)}, bf16[48,1024]{1,0:T(8,128)(2,1)S(1)}, u32[]{:S(2)}, u32[]{:S(2)}) collective-permute-start(bf16[48,1024]{1,0:T(8,128)(2,1)S(1)} %get-tuple-element.51), channel_id=1, source_target_pairs={{0,4},{4,0},{8,12},{12,8},{16,20},{20,16},{24,28},{28,24},{1,5},{5... | collective-permute-start | bytes 294920 | tf_op jit(solution)/shard_map/ppermute | solution.py:29
  24.7 0.0 collective-permute-start.9
  24.7 4.4 %collective-permute-start.12 = (bf16[128,512]{1,0:T(8,128)(2,1)S(1)}, bf16[128,512]{1,0:T(8,128)(2,1)S(1)}, u32[]{:S(2)}, u32[]{:S(2)}) collective-permute-start(bf16[128,512]{1,0:T(8,128)(2,1)S(1)} %get-tuple-element.50.q.refs_0_), channel_id=1, source_target_pairs={{0,8},{8,16},{16,24},{24,28},{28,20},{20,12},{12,4},{4,0},{1,9},{9... | collective-permute-start | bytes 393224 | tf_op jit(solution)/shard_map/ppermute | solution.py:40
  29.1 0.0 collective-permute-start.13
  29.1 0.0 collective-permute-done.8.rim_near
  29.1 0.0 collective-permute-done.9.rim_far
  29.2 1.8 %collective-permute-start.10 = (bf16[64,1024]{1,0:T(8,128)(2,1)S(1)}, bf16[64,1024]{1,0:T(8,128)(2,1)S(1)}, u32[]{:S(2)}, u32[]{:S(2)}) collective-permute-start(bf16[64,1024]{1,0:T(8,128)(2,1)S(1)} %get-tuple-element.54.ends), channel_id=1, source_target_pairs={{0,2},{1,3},{2,0},{3,1},{4,6},{5,7},{6,4},{7,5},{8,10},{9,11},{10,... | collective-permute-start | bytes 393224 | tf_op jit(solution)/shard_map/ppermute | solution.py:29
  30.9 2.9 %collective-permute-start.14 = (bf16[128,512]{1,0:T(8,128)(2,1)S(1)}, bf16[128,512]{1,0:T(8,128)(2,1)S(1)}, u32[]{:S(2)}, u32[]{:S(2)}) collective-permute-start(bf16[128,512]{1,0:T(8,128)(2,1)S(1)} %get-tuple-element.61), channel_id=1, source_target_pairs={{0,4},{4,0},{8,12},{12,8},{16,20},{20,16},{24,28},{28,24},{1,5},{5... | collective-permute-start | bytes 393224 | tf_op jit(solution)/shard_map/ppermute | solution.py:29
  33.8 0.2 collective-permute-done.12.seen.refs_2_
  34.0 0.0 collective-permute-done.11.across
  34.0 0.0 copy-done.1
  34.0 2.8 %conv_inner.1 = (bf16[128,512]{1,0:T(8,128)(2,1)S(1)}, f32[32,512]{1,0:T(8,128)S(1)}, f32[64,1024]{1,0:T(8,128)S(1)}, f32[128,1024]{1,0:T(8,128)S(1)}) custom-call(bf16[128,1024]{1,0:T(8,128)(2,1)S(1)} %get-tuple-element.55.chip, bf16[128,1024]{1,0:T(8,128)(2,1)S(1)} %collective-permute-done.11.across, bf16[128,512]{1,0:T(8,128)(2,1)S(1)} %get-tuple-element.49.cot, ...), custom_call_target="tpu_custom_call" | custom-call | bytes 11439000 | tf_op jit(solution)/shard_map/conv_inner/pallas_call | solution.py:68
  36.9 0.0 collective-permute-done.13.seen.refs_1_
  36.9 0.0 collective-permute-done.10.ends_across
  36.9 1.1 %conv_edge.1 = (bf16[128,512]{1,0:T(8,128)(2,1)S(1)}, bf16[128,1024]{1,0:T(8,128)(2,1)S(1)}) custom-call(bf16[64,1024]{1,0:T(8,128)(2,1)S(1)} %get-tuple-element.54.ends, bf16[64,1024]{1,0:T(8,128)(2,1)S(1)} %collective-permute-done.10.ends_across, bf16[48,1024]{1,0:T(8,128)(2,1)S(1)} %collective-permute-done.8.rim_near, ...), custom_call_target="tpu_custom_call" | custom-call | bytes 5166000 | tf_op jit(solution)/shard_map/conv_edge/pallas_call | solution.py:68
  38.0 0.0 collective-permute-done.14.seen.refs_4_.query
  38.1 0.1 collective-permute-start.15
  38.1 0.5 upstream_own.1
  38.6 1.0 %collective-permute-done.15.core = bf16[128,1024]{1,0:T(8,128)(2,1)S(1)} collective-permute-done((bf16[128,1024]{1,0:T(8,128)(2,1)S(1)}, bf16[128,1024]{1,0:T(8,128)(2,1)S(1)}, u32[]{:S(2)}, u32[]{:S(2)}) %collective-permute-start.15) | collective-permute-done | bytes 262176 | tf_op jit(solution)/shard_map/ppermute | solution.py:29
  39.7 0.7 %upstream.1 = (bf16[144,512]{1,0:T(8,128)(2,1)S(1)}, f32[128,512]{1,0:T(8,128)S(1)}) custom-call(bf16[128,1024]{1,0:T(8,128)(2,1)S(1)} %collective-permute-done.15.core, bf16[512,2048]{1,0:T(8,128)(2,1)S(1)} %copy-done, bf16[128,512]{1,0:T(8,128)(2,1)S(1)} %get-tuple-element.62.att, f32[128,512]{1,0:T(8,128)S(1)} %get-tuple-element.64.partial, ...), custom_call_target="tpu_custom_call" | custom-call | bytes 2214000 | tf_op jit(solution)/shard_map/upstream/pallas_call | solution.py:68
  40.3 0.2 collective-permute-start.17
  40.5 4.8 %collective-permute-start.18 = (bf16[144,512]{1,0:T(8,128)(2,1)S(1)}, bf16[144,512]{1,0:T(8,128)(2,1)S(1)}, u32[]{:S(2)}, u32[]{:S(2)}) collective-permute-start(bf16[144,512]{1,0:T(8,128)(2,1)S(1)} %get-tuple-element.66.message.refs_5_), channel_id=1, source_target_pairs={{0,8},{8,16},{16,24},{24,28},{28,20},{20,12},{12,4},{4,0},{1,9},{9... | collective-permute-start | bytes 442376 | tf_op jit(solution)/shard_map/ppermute | solution.py:40
  45.3 0.0 collective-permute-start.19
  45.3 0.0 collective-permute-start.16
  45.3 1.5 %query_grad.1 = (bf16[128,512]{1,0:T(8,128)(2,1)}, bf16[128,512]{1,0:T(8,128)(2,1)}, bf16[128,512]{1,0:T(8,128)(2,1)}) custom-call(bf16[128,512]{1,0:T(8,128)(2,1)S(1)} %get-tuple-element.50.q.refs_0_, bf16[256,512]{1,0:T(8,128)(2,1)S(1)} %pad_add_fusion.1.own, bf16[256,512]{1,0:T(8,128)(2,1)S(1)} %collective-permute-done.2.near, ...), custom_call_target="tpu_custom_call" | custom-call | bytes 6642000 | tf_op jit(solution)/shard_map/query_grad/pallas_call | solution.py:68
  46.9 0.0 collective-permute-done.17.refs_6_
  46.9 1.6 %collective-permute-done.18.refs_7_ = bf16[144,512]{1,0:T(8,128)(2,1)S(1)} collective-permute-done((bf16[144,512]{1,0:T(8,128)(2,1)S(1)}, bf16[144,512]{1,0:T(8,128)(2,1)S(1)}, u32[]{:S(2)}, u32[]{:S(2)}) %collective-permute-start.18) | collective-permute-done | bytes 147488 | tf_op jit(solution)/shard_map/ppermute | solution.py:40
  48.4 3.7 %collective-permute-done.19.refs_8_ = bf16[144,512]{1,0:T(8,128)(2,1)S(1)} collective-permute-done((bf16[144,512]{1,0:T(8,128)(2,1)S(1)}, bf16[144,512]{1,0:T(8,128)(2,1)S(1)}, u32[]{:S(2)}, u32[]{:S(2)}) %collective-permute-start.19) | collective-permute-done | bytes 147488 | tf_op jit(solution)/shard_map/ppermute | solution.py:40
  52.1 0.9 %key_part.1 = (f32[128,512]{1,0:T(8,128)S(1)}, f32[128,512]{1,0:T(8,128)S(1)}, f32[128,512]{1,0:T(8,128)S(1)}) custom-call(bf16[256,512]{1,0:T(8,128)(2,1)S(1)} %pad_add_fusion.1.own, bf16[128,512]{1,0:T(8,128)(2,1)S(1)} %get-tuple-element.50.q.refs_0_, bf16[128,512]{1,0:T(8,128)(2,1)S(1)} %collective-permute-done.13.seen.refs_1_, ...), custom_call_target="tpu_custom_call" | custom-call | bytes 5535000 | tf_op jit(solution)/shard_map/key_part/pallas_call | solution.py:68
  53.0 0.0 collective-permute-done.16.message
  53.0 1.0 %key_grad.1 = (bf16[128,512]{1,0:T(8,128)(2,1)}, bf16[128,512]{1,0:T(8,128)(2,1)}) custom-call(bf16[256,512]{1,0:T(8,128)(2,1)S(1)} %pad_add_fusion.1.own, bf16[128,512]{1,0:T(8,128)(2,1)S(1)} %collective-permute-done.14.seen.refs_4_.query, bf16[144,512]{1,0:T(8,128)(2,1)S(1)} %collective-permute-done.16.message, f32[128,512]{1,0:T(8,128)S(1)} %get-tuple-element.72.late, ...), custom_call_target="tpu_custom_call" | custom-call | bytes 3690000 | tf_op jit(solution)/shard_map/key_grad/pallas_call | solution.py:68
  (4 shorter events, 0.1 us)
Async XLA Ops:
  0.6 17.9 %copy-start = (bf16[512,2048]{1,0:T(8,128)(2,1)S(1)}, bf16[512,2048]{1,0:T(8,128)(2,1)}, u32[]{:S(2)}) copy-start(bf16[512,2048]{1,0:T(8,128)(2,1)} %weight.5) | copy-start | bytes 6291460
  1.8 10.2 %collective-permute-start = (bf16[256,512]{1,0:T(8,128)(2,1)S(1)}, bf16[256,512]{1,0:T(8,128)(2,1)S(1)}, u32[]{:S(2)}, u32[]{:S(2)}) collective-permute-start(bf16[256,512]{1,0:T(8,128)(2,1)S(1)} %pad_add_fusion.1.own), channel_id=1, source_target_pairs={{8,0},{16,8},{24,16},{28,24},{20,28},{12,20},{4,12},{0,4},{9,1},{1... | collective-permute-start | bytes 786440 | tf_op jit(solution)/shard_map/ppermute | solution.py:40
  4.8 13.1 %collective-permute-start.2 = (bf16[256,512]{1,0:T(8,128)(2,1)S(1)}, bf16[256,512]{1,0:T(8,128)(2,1)S(1)}, u32[]{:S(2)}, u32[]{:S(2)}) collective-permute-start(bf16[256,512]{1,0:T(8,128)(2,1)S(1)} %pad_add_fusion.1.own), channel_id=1, source_target_pairs={{0,1},{1,0},{2,3},{3,2},{4,5},{5,4},{6,7},{7,6},{8,12},{9,13},{10,... | collective-permute-start | bytes 786440 | tf_op jit(solution)/shard_map/ppermute | solution.py:51
  4.8 13.1 %collective-permute-start.3 = (bf16[256,512]{1,0:T(8,128)(2,1)S(1)}, bf16[256,512]{1,0:T(8,128)(2,1)S(1)}, u32[]{:S(2)}, u32[]{:S(2)}) collective-permute-start(bf16[256,512]{1,0:T(8,128)(2,1)S(1)} %pad_add_fusion.1.own), channel_id=1, source_target_pairs={{0,8},{8,16},{16,24},{24,28},{28,20},{20,12},{12,4},{4,0},{1,9},{9... | collective-permute-start | bytes 786440 | tf_op jit(solution)/shard_map/ppermute | solution.py:40
  7.9 10.6 %collective-permute-start.1 = (bf16[256,512]{1,0:T(8,128)(2,1)S(1)}, bf16[256,512]{1,0:T(8,128)(2,1)S(1)}, u32[]{:S(2)}, u32[]{:S(2)}) collective-permute-start(bf16[256,512]{1,0:T(8,128)(2,1)S(1)} %pad_add_fusion.1.own), channel_id=1, source_target_pairs={{0,1},{1,0},{2,3},{3,2},{4,8},{5,9},{6,10},{7,11},{8,4},{9,5},{10,... | collective-permute-start | bytes 786440 | tf_op jit(solution)/shard_map/ppermute | solution.py:51
  7.9 14.4 %collective-permute-start.5 = (bf16[128,512]{1,0:T(8,128)(2,1)}, bf16[128,512]{1,0:T(8,128)(2,1)S(1)}, u32[]{:S(2)}, u32[]{:S(2)}) collective-permute-start(bf16[128,512]{1,0:T(8,128)(2,1)} %param.13), channel_id=1, source_target_pairs={{0,2},{1,3},{2,0},{3,1},{4,6},{5,7},{6,4},{7,5},{8,10},{9,11},{10,... | collective-permute-start | bytes 393224 | tf_op jit(solution)/shard_map/ppermute | solution.py:29
  12.0 10.4 %collective-permute-start.4 = (bf16[128,512]{1,0:T(8,128)(2,1)S(1)}, bf16[128,512]{1,0:T(8,128)(2,1)S(1)}, u32[]{:S(2)}, u32[]{:S(2)}) collective-permute-start(bf16[128,512]{1,0:T(8,128)(2,1)S(1)} %get-tuple-element.41.q), channel_id=1, source_target_pairs={{8,0},{16,8},{24,16},{28,24},{20,28},{12,20},{4,12},{0,4},{9,1},{1... | collective-permute-start | bytes 393224 | tf_op jit(solution)/shard_map/ppermute | solution.py:40
  17.9 4.5 %collective-permute-start.6 = (f32[31,512]{1,0:T(8,128)}, f32[31,512]{1,0:T(8,128)S(1)}, u32[]{:S(2)}, u32[]{:S(2)}) collective-permute-start(f32[31,512]{1,0:T(8,128)} %taps.3), channel_id=1, source_target_pairs={{0,2},{1,3},{2,0},{3,1},{4,6},{5,7},{6,4},{7,5},{8,10},{9,11},{10,... | collective-permute-start | bytes 190472 | tf_op jit(solution)/shard_map/ppermute | solution.py:29
  18.5 15.5 %copy-start.1 = (f32[31,512]{1,0:T(8,128)S(1)}, f32[31,512]{1,0:T(8,128)}, u32[]{:S(2)}) copy-start(f32[31,512]{1,0:T(8,128)} %taps.3) | copy-start | bytes 190468
  22.4 1.6 %collective-permute-start.7 = (bf16[128,1024]{1,0:T(8,128)(2,1)S(1)}, bf16[128,1024]{1,0:T(8,128)(2,1)S(1)}, u32[]{:S(2)}, u32[]{:S(2)}) collective-permute-start(bf16[128,1024]{1,0:T(8,128)(2,1)S(1)} %get-tuple-element.47), channel_id=1, source_target_pairs={{0,1},{1,0},{2,3},{3,2},{4,5},{5,4},{6,7},{7,6},{8,9},{9,8},{10,11... | collective-permute-start | bytes 786440 | tf_op jit(solution)/shard_map/ppermute | solution.py:29
  24.1 9.9 %collective-permute-start.11 = (bf16[128,1024]{1,0:T(8,128)(2,1)S(1)}, bf16[128,1024]{1,0:T(8,128)(2,1)S(1)}, u32[]{:S(2)}, u32[]{:S(2)}) collective-permute-start(bf16[128,1024]{1,0:T(8,128)(2,1)S(1)} %get-tuple-element.55.chip), channel_id=1, source_target_pairs={{0,2},{1,3},{2,0},{3,1},{4,6},{5,7},{6,4},{7,5},{8,10},{9,11},{10,... | collective-permute-start | bytes 786440 | tf_op jit(solution)/shard_map/ppermute | solution.py:29
  24.2 4.9 %collective-permute-start.8 = (bf16[48,1024]{1,0:T(8,128)(2,1)S(1)}, bf16[48,1024]{1,0:T(8,128)(2,1)S(1)}, u32[]{:S(2)}, u32[]{:S(2)}) collective-permute-start(bf16[48,1024]{1,0:T(8,128)(2,1)S(1)} %get-tuple-element.51), channel_id=1, source_target_pairs={{0,4},{4,0},{8,12},{12,8},{16,20},{20,16},{24,28},{28,24},{1,5},{5... | collective-permute-start | bytes 294920 | tf_op jit(solution)/shard_map/ppermute | solution.py:29
  24.7 4.4 %collective-permute-start.9 = (bf16[48,1024]{1,0:T(8,128)(2,1)S(1)}, bf16[48,1024]{1,0:T(8,128)(2,1)S(1)}, u32[]{:S(2)}, u32[]{:S(2)}) collective-permute-start(bf16[48,1024]{1,0:T(8,128)(2,1)S(1)} %get-tuple-element.52), channel_id=1, source_target_pairs={{0,1},{1,0},{2,3},{3,2},{4,8},{5,9},{6,10},{7,11},{8,4},{9,5},{10,... | collective-permute-start | bytes 294920 | tf_op jit(solution)/shard_map/ppermute | solution.py:51
  24.7 9.3 %collective-permute-start.12 = (bf16[128,512]{1,0:T(8,128)(2,1)S(1)}, bf16[128,512]{1,0:T(8,128)(2,1)S(1)}, u32[]{:S(2)}, u32[]{:S(2)}) collective-permute-start(bf16[128,512]{1,0:T(8,128)(2,1)S(1)} %get-tuple-element.50.q.refs_0_), channel_id=1, source_target_pairs={{0,8},{8,16},{16,24},{24,28},{28,20},{20,12},{12,4},{4,0},{1,9},{9... | collective-permute-start | bytes 393224 | tf_op jit(solution)/shard_map/ppermute | solution.py:40
  29.1 7.7 %collective-permute-start.13 = (bf16[128,512]{1,0:T(8,128)(2,1)S(1)}, bf16[128,512]{1,0:T(8,128)(2,1)S(1)}, u32[]{:S(2)}, u32[]{:S(2)}) collective-permute-start(bf16[128,512]{1,0:T(8,128)(2,1)S(1)} %get-tuple-element.50.q.refs_0_), channel_id=1, source_target_pairs={{0,1},{1,0},{2,3},{3,2},{4,5},{5,4},{6,7},{7,6},{8,12},{9,13},{10,... | collective-permute-start | bytes 393224 | tf_op jit(solution)/shard_map/ppermute | solution.py:51
  29.2 7.7 %collective-permute-start.10 = (bf16[64,1024]{1,0:T(8,128)(2,1)S(1)}, bf16[64,1024]{1,0:T(8,128)(2,1)S(1)}, u32[]{:S(2)}, u32[]{:S(2)}) collective-permute-start(bf16[64,1024]{1,0:T(8,128)(2,1)S(1)} %get-tuple-element.54.ends), channel_id=1, source_target_pairs={{0,2},{1,3},{2,0},{3,1},{4,6},{5,7},{6,4},{7,5},{8,10},{9,11},{10,... | collective-permute-start | bytes 393224 | tf_op jit(solution)/shard_map/ppermute | solution.py:29
  30.9 7.1 %collective-permute-start.14 = (bf16[128,512]{1,0:T(8,128)(2,1)S(1)}, bf16[128,512]{1,0:T(8,128)(2,1)S(1)}, u32[]{:S(2)}, u32[]{:S(2)}) collective-permute-start(bf16[128,512]{1,0:T(8,128)(2,1)S(1)} %get-tuple-element.61), channel_id=1, source_target_pairs={{0,4},{4,0},{8,12},{12,8},{16,20},{20,16},{24,28},{28,24},{1,5},{5... | collective-permute-start | bytes 393224 | tf_op jit(solution)/shard_map/ppermute | solution.py:29
  38.1 1.6 %collective-permute-start.15 = (bf16[128,1024]{1,0:T(8,128)(2,1)S(1)}, bf16[128,1024]{1,0:T(8,128)(2,1)S(1)}, u32[]{:S(2)}, u32[]{:S(2)}) collective-permute-start(bf16[128,1024]{1,0:T(8,128)(2,1)S(1)} %hand.1.own.grad_here), channel_id=1, source_target_pairs={{0,1},{1,0},{2,3},{3,2},{4,5},{5,4},{6,7},{7,6},{8,9},{9,8},{10,11... | collective-permute-start | bytes 786440 | tf_op jit(solution)/shard_map/ppermute | solution.py:29
  40.3 6.5 %collective-permute-start.17 = (bf16[144,512]{1,0:T(8,128)(2,1)S(1)}, bf16[144,512]{1,0:T(8,128)(2,1)S(1)}, u32[]{:S(2)}, u32[]{:S(2)}) collective-permute-start(bf16[144,512]{1,0:T(8,128)(2,1)S(1)} %get-tuple-element.66.message.refs_5_), channel_id=1, source_target_pairs={{0,1},{1,0},{2,3},{3,2},{4,5},{5,4},{6,7},{7,6},{8,12},{9,13},{10,... | collective-permute-start | bytes 442376 | tf_op jit(solution)/shard_map/ppermute | solution.py:51
  40.5 7.9 %collective-permute-start.18 = (bf16[144,512]{1,0:T(8,128)(2,1)S(1)}, bf16[144,512]{1,0:T(8,128)(2,1)S(1)}, u32[]{:S(2)}, u32[]{:S(2)}) collective-permute-start(bf16[144,512]{1,0:T(8,128)(2,1)S(1)} %get-tuple-element.66.message.refs_5_), channel_id=1, source_target_pairs={{0,8},{8,16},{16,24},{24,28},{28,20},{20,12},{12,4},{4,0},{1,9},{9... | collective-permute-start | bytes 442376 | tf_op jit(solution)/shard_map/ppermute | solution.py:40
  45.3 6.8 %collective-permute-start.19 = (bf16[144,512]{1,0:T(8,128)(2,1)S(1)}, bf16[144,512]{1,0:T(8,128)(2,1)S(1)}, u32[]{:S(2)}, u32[]{:S(2)}) collective-permute-start(bf16[144,512]{1,0:T(8,128)(2,1)S(1)} %get-tuple-element.66.message.refs_5_), channel_id=1, source_target_pairs={{8,0},{16,8},{24,16},{28,24},{20,28},{12,20},{4,12},{0,4},{9,1},{1... | collective-permute-start | bytes 442376 | tf_op jit(solution)/shard_map/ppermute | solution.py:40
  45.3 7.6 %collective-permute-start.16 = (bf16[144,512]{1,0:T(8,128)(2,1)S(1)}, bf16[144,512]{1,0:T(8,128)(2,1)S(1)}, u32[]{:S(2)}, u32[]{:S(2)}) collective-permute-start(bf16[144,512]{1,0:T(8,128)(2,1)S(1)} %get-tuple-element.66.message.refs_5_), channel_id=1, source_target_pairs={{0,1},{1,0},{2,3},{3,2},{4,8},{5,9},{6,10},{7,11},{8,4},{9,5},{10,... | collective-permute-start | bytes 442376 | tf_op jit(solution)/shard_map/ppermute | solution.py:51

commit v17 on v15

--- a/solution.py
+++ b/solution.py
@@ -437,12 +437,12 @@
     frames = own.shape[0] // 2
     heads = columns(own.shape[1])
     above, below = slice(0, frames), slice(frames, 2 * frames)
-    biases = (None, bias_of(near_swapped()), None, None)
+    biases = (None, bias_of(far_there()), bias_of(near_swapped()), None)
     asks = [stacked(queries, above, c) for c in heads]
     ups = [stacked(messages, above, c) for c in heads]
     scores = [dot_nt(own[above, c], a) * scale for c, a in zip(heads, asks)]
     dots = [dot_nt(own[below, c], u) for c, u in zip(heads, ups)]
-    last = [dot_nt(own[above, c], late_query[:, c]) * scale + bias_of(far_there()) for c in heads]
+    last = [dot_nt(own[above, c], late_query[:, c]) * scale for c in heads]
     logs = [[stat_rows(m, frames, 0, c) for m in messages] for c in heads]
     deltas = [[stat_rows(m, frames, 1, c) for m in messages] for c in heads]
     probs = [jnp.exp(by_block(s, biases, n)) for s, n in zip(scores, logs)]
@@ -573,7 +573,7 @@
     )
 
     m_near, m_first, m_second = inner_swap(message), ring(message, 0), ring(message, 1)
-    m_relay = outer_swap(message)
+    m_far = outer_swap(message)
     output, grad_input, grad_query = kernel_call(
         functools.partial(query_grad_body, scale),
         (tile, tile, tile),
@@ -584,13 +584,13 @@
     key_part, value_part, late = kernel_call(
         functools.partial(key_part_body, scale),
         (tile32, tile32, tile32),
-        (kv, q_own, q_near, q_first, q_second, q_relay, message, m_near, m_first, m_second),
+        (kv, q_own, q_relay, q_near, q_first, q_second, message, m_far, m_near, m_first),
         1.5, "key_part",
     )
     grad_key, grad_value = kernel_call(
         functools.partial(key_grad_body, scale),
         (tile, tile),
-        (kv, q_relay, m_relay, late, key_part, value_part),
+        (kv, q_second, m_second, late, key_part, value_part),
         1.0, "key_grad", 0,
         [pltpu.VMEM((frames, width), BF16)] * 2 + [pltpu.SemaphoreType.DMA((2,))], HBM,
     )

time: 50.6 us -> 51.2 us (1.012)
  starting transfers between devices: 21.3 us -> 22.3 us
    ppermute x6, starting transfers between devices: 10.2 us -> 10.9 us  [ring(): return lax.ppermute(block, 'ctx', ring_routes(lax.axis_size('ctx'))[way])]
  transfers between devices with their start and end apart: 20 -> 20, of which waited for: 8 -> 8; matrix products, arithmetic and copies ran while one was open for 2% -> 2% of each run, Pallas kernels for 17% -> 16%
where the time goes in v17:
time: 51.2 us; the launch traced here: 51 us
  starting transfers between devices  22.3 us (44%)
  waiting for transfers between devices  15.5 us (30%)
  Pallas kernels  10.2 us (20%)
  other arithmetic  2.19 us (4%)
  between operations  0.83 us (2%)
    ppermute x6, starting transfers between devices, ring(): return lax.ppermute(block, 'ctx', ring_routes(lax.axis_size('ctx'))[way])  10.9 us
    ppermute x9, starting transfers between devices, pair_swap(): lax.ppermute(block, axis, [(i, i ^ bit) for i in range(lax.axis_size(axis...  10.8 us
    pallas_call x15, Pallas kernels, kernel_call(): pl.pallas_call(body, out_shape=outs, in_specs=[VMEM] * (len(args) - unrea...  10.2 us
    ppermute x9, waiting for transfers between devices, pair_swap(): lax.ppermute(block, axis, [(i, i ^ bit) for i in range(lax.axis_size(axis...  8.38 us
    ppermute x6, waiting for transfers between devices, ring(): return lax.ppermute(block, 'ctx', ring_routes(lax.axis_size('ctx'))[way])  7.09 us
    add x1, other arithmetic, per_device(): lax.pad(key_rows, zero, ((0, frames, 0), (0, 0, 0)))  1.14 us
    add x1, other arithmetic, per_device(): sum((lax.pad(rows, zero, ((k * frames, (2 - k) * frames, 0), (0, 0, 0)))...  1.06 us
  transfers between devices with their start and end apart: 20, of which 8 were waited for; matrix products, arithmetic and copies ran while one was open for 2% of the time, Pallas kernels for 16%

profile of v17, /device:TPU:0, one launch (start us, length us, event | category | flops | bytes accessed | tf_op | source)
XLA Modules:
  0.0 51.0 jit_solution(15829454072097973443)
XLA Ops:
  0.6 0.0 copy-start.2
  0.6 0.0 copy-start.1
  0.7 0.0 copy-start
  0.7 1.1 %pad_add_fusion.1.own = bf16[256,512]{1,0:T(8,128)(2,1)S(1)} fusion(bf16[128,512]{1,0:T(8,128)(2,1)} %param.9, bf16[128,512]{1,0:T(8,128)(2,1)} %param.8), kind=kLoop, calls=%fused_computation.1 | loop fusion | flops 524288 | bytes 524288 | tf_op jit(solution)/shard_map/add | solution.py:493
  1.8 3.0 %collective-permute-start = (bf16[256,512]{1,0:T(8,128)(2,1)S(1)}, bf16[256,512]{1,0:T(8,128)(2,1)S(1)}, u32[]{:S(2)}, u32[]{:S(2)}) collective-permute-start(bf16[256,512]{1,0:T(8,128)(2,1)S(1)} %pad_add_fusion.1.own), channel_id=1, source_target_pairs={{8,0},{16,8},{24,16},{28,24},{20,28},{12,20},{4,12},{0,4},{9,1},{1... | collective-permute-start | bytes 786440 | tf_op jit(solution)/shard_map/ppermute | solution.py:40
  4.8 0.0 collective-permute-start.2
  4.8 3.2 %collective-permute-start.3 = (bf16[256,512]{1,0:T(8,128)(2,1)S(1)}, bf16[256,512]{1,0:T(8,128)(2,1)S(1)}, u32[]{:S(2)}, u32[]{:S(2)}) collective-permute-start(bf16[256,512]{1,0:T(8,128)(2,1)S(1)} %pad_add_fusion.1.own), channel_id=1, source_target_pairs={{0,8},{8,16},{16,24},{24,28},{28,20},{20,12},{12,4},{4,0},{1,9},{9... | collective-permute-start | bytes 786440 | tf_op jit(solution)/shard_map/ppermute | solution.py:40
  7.9 1.1 %pad_add_fusion.seen.joined = bf16[384,512]{1,0:T(8,128)(2,1)S(1)} fusion(bf16[128,512]{1,0:T(8,128)(2,1)} %param.13, bf16[128,512]{1,0:T(8,128)(2,1)} %param.10, bf16[128,512]{1,0:T(8,128)(2,1)} %param.7), kind=kLoop, calls=%fused_computation | loop fusion | flops 1179648 | bytes 786432 | tf_op jit(solution)/shard_map/add | solution.py:496
  9.0 2.2 %collective-permute-done.block = bf16[256,512]{1,0:T(8,128)(2,1)S(1)} collective-permute-done((bf16[256,512]{1,0:T(8,128)(2,1)S(1)}, bf16[256,512]{1,0:T(8,128)(2,1)S(1)}, u32[]{:S(2)}, u32[]{:S(2)}) %collective-permute-start) | collective-permute-done | bytes 262176 | tf_op jit(solution)/shard_map/ppermute | solution.py:40
  11.2 1.7 %collective-permute-start.1 = (bf16[256,512]{1,0:T(8,128)(2,1)S(1)}, bf16[256,512]{1,0:T(8,128)(2,1)S(1)}, u32[]{:S(2)}, u32[]{:S(2)}) collective-permute-start(bf16[256,512]{1,0:T(8,128)(2,1)S(1)} %turn.1.seen.second), channel_id=1, source_target_pairs={{0,4},{4,0},{8,12},{12,8},{16,20},{20,16},{24,28},{28,24},{1,5},{5... | collective-permute-start | bytes 786440 | tf_op jit(solution)/shard_map/ppermute | solution.py:29
  12.9 0.0 copy-done.2
  12.9 1.5 %collective-permute-start.5 = (bf16[128,512]{1,0:T(8,128)(2,1)S(1)}, bf16[128,512]{1,0:T(8,128)(2,1)S(1)}, u32[]{:S(2)}, u32[]{:S(2)}) collective-permute-start(bf16[128,512]{1,0:T(8,128)(2,1)S(1)} %copy-done.2), channel_id=1, source_target_pairs={{0,2},{1,3},{2,0},{3,1},{4,6},{5,7},{6,4},{7,5},{8,10},{9,11},{10,... | collective-permute-start | bytes 393224 | tf_op jit(solution)/shard_map/ppermute | solution.py:29
  14.5 0.6 %collective-permute-start.4 = (bf16[128,512]{1,0:T(8,128)(2,1)S(1)}, bf16[128,512]{1,0:T(8,128)(2,1)S(1)}, u32[]{:S(2)}, u32[]{:S(2)}) collective-permute-start(bf16[128,512]{1,0:T(8,128)(2,1)S(1)} %get-tuple-element.41.q), channel_id=1, source_target_pairs={{8,0},{16,8},{24,16},{28,24},{20,28},{12,20},{4,12},{0,4},{9,1},{1... | collective-permute-start | bytes 393224 | tf_op jit(solution)/shard_map/ppermute | solution.py:40
  15.1 0.0 collective-permute-done.2.near
  15.1 0.0 copy-done.1
  15.1 0.3 collective-permute-start.6
  15.4 0.0 collective-permute-done.3.first
  15.4 0.6 %forward.1 = (f32[128,512]{1,0:T(8,128)S(1)}, f32[128,512]{1,0:T(8,128)S(1)}, f32[128,512]{1,0:T(8,128)S(1)}) custom-call(bf16[128,512]{1,0:T(8,128)(2,1)S(1)} %get-tuple-element.41.q, bf16[256,512]{1,0:T(8,128)(2,1)S(1)} %pad_add_fusion.1.own, bf16[256,512]{1,0:T(8,128)(2,1)S(1)} %collective-permute-done.2.near, ...), custom_call_target="tpu_custom_call" | custom-call | bytes 3690000 | tf_op jit(solution)/shard_map/forward/pallas_call | solution.py:76
  16.0 3.1 %collective-permute-done.1.relay = bf16[256,512]{1,0:T(8,128)(2,1)S(1)} collective-permute-done((bf16[256,512]{1,0:T(8,128)(2,1)S(1)}, bf16[256,512]{1,0:T(8,128)(2,1)S(1)}, u32[]{:S(2)}, u32[]{:S(2)}) %collective-permute-start.1) | collective-permute-done | bytes 262176 | tf_op jit(solution)/shard_map/ppermute | solution.py:29
  19.1 0.0 copy-done
  19.1 0.9 %project.1 = (bf16[128,512]{1,0:T(8,128)(2,1)S(1)}, f32[128,512]{1,0:T(8,128)S(1)}, bf16[128,1024]{1,0:T(8,128)(2,1)S(1)}, bf16[128,1024]{1,0:T(8,128)(2,1)S(1)}) custom-call(bf16[128,512]{1,0:T(8,128)(2,1)S(1)} %get-tuple-element.41.q, bf16[256,512]{1,0:T(8,128)(2,1)S(1)} %collective-permute-done.1.relay, f32[128,512]{1,0:T(8,128)S(1)} %get-tuple-element.42.sums, ...), custom_call_target="tpu_custom_call" | custom-call | bytes 3690000 | tf_op jit(solution)/shard_map/project/pallas_call | solution.py:76
  20.0 0.0 collective-permute-done.6.seen_b.taps_other
  20.0 0.0 collective-permute-done.5.seen_a.cot_other
  20.0 0.4 collective-permute-done.4.q_second
  20.5 0.1 collective-permute-start.7
  20.5 1.5 %collective-permute-done.7.core = bf16[128,1024]{1,0:T(8,128)(2,1)S(1)} collective-permute-done((bf16[128,1024]{1,0:T(8,128)(2,1)S(1)}, bf16[128,1024]{1,0:T(8,128)(2,1)S(1)}, u32[]{:S(2)}, u32[]{:S(2)}) %collective-permute-start.7) | collective-permute-done | bytes 262176 | tf_op jit(solution)/shard_map/ppermute | solution.py:29
  22.1 0.1 join.1
  22.2 1.6 %collective-permute-start.11 = (bf16[128,1024]{1,0:T(8,128)(2,1)S(1)}, bf16[128,1024]{1,0:T(8,128)(2,1)S(1)}, u32[]{:S(2)}, u32[]{:S(2)}) collective-permute-start(bf16[128,1024]{1,0:T(8,128)(2,1)S(1)} %get-tuple-element.55.chip), channel_id=1, source_target_pairs={{0,2},{1,3},{2,0},{3,1},{4,6},{5,7},{6,4},{7,5},{8,10},{9,11},{10,... | collective-permute-start | bytes 786440 | tf_op jit(solution)/shard_map/ppermute | solution.py:29
  23.8 2.5 %collective-permute-start.8 = (bf16[48,1024]{1,0:T(8,128)(2,1)S(1)}, bf16[48,1024]{1,0:T(8,128)(2,1)S(1)}, u32[]{:S(2)}, u32[]{:S(2)}) collective-permute-start(bf16[48,1024]{1,0:T(8,128)(2,1)S(1)} %get-tuple-element.51), channel_id=1, source_target_pairs={{0,4},{4,0},{8,12},{12,8},{16,20},{20,16},{24,28},{28,24},{1,5},{5... | collective-permute-start | bytes 294920 | tf_op jit(solution)/shard_map/ppermute | solution.py:29
  26.2 0.0 collective-permute-start.9
  26.2 1.5 %collective-permute-start.12 = (bf16[128,512]{1,0:T(8,128)(2,1)S(1)}, bf16[128,512]{1,0:T(8,128)(2,1)S(1)}, u32[]{:S(2)}, u32[]{:S(2)}) collective-permute-start(bf16[128,512]{1,0:T(8,128)(2,1)S(1)} %get-tuple-element.50.q.refs_0_), channel_id=1, source_target_pairs={{0,8},{8,16},{16,24},{24,28},{28,20},{20,12},{12,4},{4,0},{1,9},{9... | collective-permute-start | bytes 393224 | tf_op jit(solution)/shard_map/ppermute | solution.py:40
  27.7 0.0 collective-permute-start.13
  27.7 2.7 %collective-permute-done.8.rim_near = bf16[48,1024]{1,0:T(8,128)(2,1)S(1)} collective-permute-done((bf16[48,1024]{1,0:T(8,128)(2,1)S(1)}, bf16[48,1024]{1,0:T(8,128)(2,1)S(1)}, u32[]{:S(2)}, u32[]{:S(2)}) %collective-permute-start.8) | collective-permute-done | bytes 98336 | tf_op jit(solution)/shard_map/ppermute | solution.py:29
  30.4 0.0 collective-permute-done.9.rim_far
  30.4 0.6 %collective-permute-start.10 = (bf16[64,1024]{1,0:T(8,128)(2,1)S(1)}, bf16[64,1024]{1,0:T(8,128)(2,1)S(1)}, u32[]{:S(2)}, u32[]{:S(2)}) collective-permute-start(bf16[64,1024]{1,0:T(8,128)(2,1)S(1)} %get-tuple-element.54.ends), channel_id=1, source_target_pairs={{0,2},{1,3},{2,0},{3,1},{4,6},{5,7},{6,4},{7,5},{8,10},{9,11},{10,... | collective-permute-start | bytes 393224 | tf_op jit(solution)/shard_map/ppermute | solution.py:29
  31.0 2.5 %collective-permute-start.14 = (bf16[128,512]{1,0:T(8,128)(2,1)S(1)}, bf16[128,512]{1,0:T(8,128)(2,1)S(1)}, u32[]{:S(2)}, u32[]{:S(2)}) collective-permute-start(bf16[128,512]{1,0:T(8,128)(2,1)S(1)} %get-tuple-element.61), channel_id=1, source_target_pairs={{0,4},{4,0},{8,12},{12,8},{16,20},{20,16},{24,28},{28,24},{1,5},{5... | collective-permute-start | bytes 393224 | tf_op jit(solution)/shard_map/ppermute | solution.py:29
  33.5 0.0 collective-permute-done.12.seen.refs_3_
  33.5 0.0 collective-permute-done.11.across
  33.5 2.8 %conv_inner.1 = (bf16[128,512]{1,0:T(8,128)(2,1)S(1)}, f32[32,512]{1,0:T(8,128)S(1)}, f32[64,1024]{1,0:T(8,128)S(1)}, f32[128,1024]{1,0:T(8,128)S(1)}) custom-call(bf16[128,1024]{1,0:T(8,128)(2,1)S(1)} %get-tuple-element.55.chip, bf16[128,1024]{1,0:T(8,128)(2,1)S(1)} %collective-permute-done.11.across, bf16[128,512]{1,0:T(8,128)(2,1)S(1)} %get-tuple-element.49.cot, ...), custom_call_target="tpu_custom_call" | custom-call | bytes 11439000 | tf_op jit(solution)/shard_map/conv_inner/pallas_call | solution.py:76
  36.3 0.0 collective-permute-done.13.seen.refs_2_
  36.3 0.0 collective-permute-done.10.ends_across
  36.4 1.1 %conv_edge.1 = (bf16[128,512]{1,0:T(8,128)(2,1)S(1)}, bf16[128,1024]{1,0:T(8,128)(2,1)S(1)}) custom-call(bf16[64,1024]{1,0:T(8,128)(2,1)S(1)} %get-tuple-element.54.ends, bf16[64,1024]{1,0:T(8,128)(2,1)S(1)} %collective-permute-done.10.ends_across, bf16[48,1024]{1,0:T(8,128)(2,1)S(1)} %collective-permute-done.8.rim_near, ...), custom_call_target="tpu_custom_call" | custom-call | bytes 5166000 | tf_op jit(solution)/shard_map/conv_edge/pallas_call | solution.py:76
  37.5 0.0 collective-permute-done.14.seen.refs_1_
  37.5 0.1 collective-permute-start.15
  37.6 0.5 upstream_own.1
  38.1 1.0 %collective-permute-done.15.core = bf16[128,1024]{1,0:T(8,128)(2,1)S(1)} collective-permute-done((bf16[128,1024]{1,0:T(8,128)(2,1)S(1)}, bf16[128,1024]{1,0:T(8,128)(2,1)S(1)}, u32[]{:S(2)}, u32[]{:S(2)}) %collective-permute-start.15) | collective-permute-done | bytes 262176 | tf_op jit(solution)/shard_map/ppermute | solution.py:29
  39.1 0.7 %upstream.1 = (bf16[144,512]{1,0:T(8,128)(2,1)S(1)}, f32[128,512]{1,0:T(8,128)S(1)}) custom-call(bf16[128,1024]{1,0:T(8,128)(2,1)S(1)} %collective-permute-done.15.core, bf16[512,2048]{1,0:T(8,128)(2,1)S(1)} %copy-done, bf16[128,512]{1,0:T(8,128)(2,1)S(1)} %get-tuple-element.62.att, f32[128,512]{1,0:T(8,128)S(1)} %get-tuple-element.64.partial, ...), custom_call_target="tpu_custom_call" | custom-call | bytes 2214000 | tf_op jit(solution)/shard_map/upstream/pallas_call | solution.py:76
  39.8 0.2 collective-permute-start.17
  40.0 0.4 collective-permute-start.18
  40.4 2.7 %collective-permute-start.19 = (bf16[144,512]{1,0:T(8,128)(2,1)S(1)}, bf16[144,512]{1,0:T(8,128)(2,1)S(1)}, u32[]{:S(2)}, u32[]{:S(2)}) collective-permute-start(bf16[144,512]{1,0:T(8,128)(2,1)S(1)} %get-tuple-element.66.message.refs_5_), channel_id=1, source_target_pairs={{0,8},{8,16},{16,24},{24,28},{28,20},{20,12},{12,4},{4,0},{1,9},{9... | collective-permute-start | bytes 442376 | tf_op jit(solution)/shard_map/ppermute | solution.py:40
  43.1 0.0 collective-permute-start.16
  43.1 1.5 %query_grad.1 = (bf16[128,512]{1,0:T(8,128)(2,1)}, bf16[128,512]{1,0:T(8,128)(2,1)}, bf16[128,512]{1,0:T(8,128)(2,1)}) custom-call(bf16[128,512]{1,0:T(8,128)(2,1)S(1)} %get-tuple-element.50.q.refs_0_, bf16[256,512]{1,0:T(8,128)(2,1)S(1)} %pad_add_fusion.1.own, bf16[256,512]{1,0:T(8,128)(2,1)S(1)} %collective-permute-done.2.near, ...), custom_call_target="tpu_custom_call" | custom-call | bytes 6642000 | tf_op jit(solution)/shard_map/query_grad/pallas_call | solution.py:76
  44.6 0.0 collective-permute-done.17.refs_6_
  44.6 0.0 collective-permute-done.18.refs_7_
  44.6 1.6 %collective-permute-done.19.refs_8_ = bf16[144,512]{1,0:T(8,128)(2,1)S(1)} collective-permute-done((bf16[144,512]{1,0:T(8,128)(2,1)S(1)}, bf16[144,512]{1,0:T(8,128)(2,1)S(1)}, u32[]{:S(2)}, u32[]{:S(2)}) %collective-permute-start.19) | collective-permute-done | bytes 147488 | tf_op jit(solution)/shard_map/ppermute | solution.py:40
  46.3 0.9 %key_part.1 = (f32[128,512]{1,0:T(8,128)S(1)}, f32[128,512]{1,0:T(8,128)S(1)}, f32[128,512]{1,0:T(8,128)S(1)}) custom-call(bf16[256,512]{1,0:T(8,128)(2,1)S(1)} %pad_add_fusion.1.own, bf16[128,512]{1,0:T(8,128)(2,1)S(1)} %get-tuple-element.50.q.refs_0_, bf16[128,512]{1,0:T(8,128)(2,1)S(1)} %collective-permute-done.14.seen.refs_1_, ...), custom_call_target="tpu_custom_call" | custom-call | bytes 5535000 | tf_op jit(solution)/shard_map/key_part/pallas_call | solution.py:76
  47.1 2.9 %collective-permute-done.16.message = bf16[144,512]{1,0:T(8,128)(2,1)S(1)} collective-permute-done((bf16[144,512]{1,0:T(8,128)(2,1)S(1)}, bf16[144,512]{1,0:T(8,128)(2,1)S(1)}, u32[]{:S(2)}, u32[]{:S(2)}) %collective-permute-start.16) | collective-permute-done | bytes 147488 | tf_op jit(solution)/shard_map/ppermute | solution.py:40
  50.0 1.0 %key_grad.1 = (bf16[128,512]{1,0:T(8,128)(2,1)}, bf16[128,512]{1,0:T(8,128)(2,1)}) custom-call(bf16[256,512]{1,0:T(8,128)(2,1)S(1)} %pad_add_fusion.1.own, bf16[128,512]{1,0:T(8,128)(2,1)S(1)} %get-tuple-element.53.q_second.refs_4_.query, bf16[144,512]{1,0:T(8,128)(2,1)S(1)} %collective-permute-done.16.message, f32[128,512]{1,0:T(8,128)S(1)} %get-tuple-element.72.late, ...), custom_call_target="tpu_custom_call" | custom-call | bytes 3690000 | tf_op jit(solution)/shard_map/key_grad/pallas_call | solution.py:76
  (5 shorter events, 0.1 us)
Async XLA Ops:
  0.6 12.3 %copy-start.2 = (bf16[128,512]{1,0:T(8,128)(2,1)S(1)}, bf16[128,512]{1,0:T(8,128)(2,1)}, u32[]{:S(2)}) copy-start(bf16[128,512]{1,0:T(8,128)(2,1)} %param.13) | copy-start | bytes 393220
  0.6 14.4 %copy-start.1 = (f32[31,512]{1,0:T(8,128)S(1)}, f32[31,512]{1,0:T(8,128)}, u32[]{:S(2)}) copy-start(f32[31,512]{1,0:T(8,128)} %taps.3) | copy-start | bytes 190468
  0.7 18.5 %copy-start = (bf16[512,2048]{1,0:T(8,128)(2,1)S(1)}, bf16[512,2048]{1,0:T(8,128)(2,1)}, u32[]{:S(2)}) copy-start(bf16[512,2048]{1,0:T(8,128)(2,1)} %weight.5) | copy-start | bytes 6291460
  1.8 9.4 %collective-permute-start = (bf16[256,512]{1,0:T(8,128)(2,1)S(1)}, bf16[256,512]{1,0:T(8,128)(2,1)S(1)}, u32[]{:S(2)}, u32[]{:S(2)}) collective-permute-start(bf16[256,512]{1,0:T(8,128)(2,1)S(1)} %pad_add_fusion.1.own), channel_id=1, source_target_pairs={{8,0},{16,8},{24,16},{28,24},{20,28},{12,20},{4,12},{0,4},{9,1},{1... | collective-permute-start | bytes 786440 | tf_op jit(solution)/shard_map/ppermute | solution.py:40
  4.8 10.3 %collective-permute-start.2 = (bf16[256,512]{1,0:T(8,128)(2,1)S(1)}, bf16[256,512]{1,0:T(8,128)(2,1)S(1)}, u32[]{:S(2)}, u32[]{:S(2)}) collective-permute-start(bf16[256,512]{1,0:T(8,128)(2,1)S(1)} %pad_add_fusion.1.own), channel_id=1, source_target_pairs={{0,1},{1,0},{2,3},{3,2},{4,5},{5,4},{6,7},{7,6},{8,12},{9,13},{10,... | collective-permute-start | bytes 786440 | tf_op jit(solution)/shard_map/ppermute | solution.py:51
  4.8 10.6 %collective-permute-start.3 = (bf16[256,512]{1,0:T(8,128)(2,1)S(1)}, bf16[256,512]{1,0:T(8,128)(2,1)S(1)}, u32[]{:S(2)}, u32[]{:S(2)}) collective-permute-start(bf16[256,512]{1,0:T(8,128)(2,1)S(1)} %pad_add_fusion.1.own), channel_id=1, source_target_pairs={{0,8},{8,16},{16,24},{24,28},{28,20},{20,12},{12,4},{4,0},{1,9},{9... | collective-permute-start | bytes 786440 | tf_op jit(solution)/shard_map/ppermute | solution.py:40
  11.2 7.9 %collective-permute-start.1 = (bf16[256,512]{1,0:T(8,128)(2,1)S(1)}, bf16[256,512]{1,0:T(8,128)(2,1)S(1)}, u32[]{:S(2)}, u32[]{:S(2)}) collective-permute-start(bf16[256,512]{1,0:T(8,128)(2,1)S(1)} %turn.1.seen.second), channel_id=1, source_target_pairs={{0,4},{4,0},{8,12},{12,8},{16,20},{20,16},{24,28},{28,24},{1,5},{5... | collective-permute-start | bytes 786440 | tf_op jit(solution)/shard_map/ppermute | solution.py:29
  12.9 7.1 %collective-permute-start.5 = (bf16[128,512]{1,0:T(8,128)(2,1)S(1)}, bf16[128,512]{1,0:T(8,128)(2,1)S(1)}, u32[]{:S(2)}, u32[]{:S(2)}) collective-permute-start(bf16[128,512]{1,0:T(8,128)(2,1)S(1)} %copy-done.2), channel_id=1, source_target_pairs={{0,2},{1,3},{2,0},{3,1},{4,6},{5,7},{6,4},{7,5},{8,10},{9,11},{10,... | collective-permute-start | bytes 393224 | tf_op jit(solution)/shard_map/ppermute | solution.py:29
  14.5 5.9 %collective-permute-start.4 = (bf16[128,512]{1,0:T(8,128)(2,1)S(1)}, bf16[128,512]{1,0:T(8,128)(2,1)S(1)}, u32[]{:S(2)}, u32[]{:S(2)}) collective-permute-start(bf16[128,512]{1,0:T(8,128)(2,1)S(1)} %get-tuple-element.41.q), channel_id=1, source_target_pairs={{8,0},{16,8},{24,16},{28,24},{20,28},{12,20},{4,12},{0,4},{9,1},{1... | collective-permute-start | bytes 393224 | tf_op jit(solution)/shard_map/ppermute | solution.py:40
  15.1 4.9 %collective-permute-start.6 = (f32[31,512]{1,0:T(8,128)S(1)}, f32[31,512]{1,0:T(8,128)S(1)}, u32[]{:S(2)}, u32[]{:S(2)}) collective-permute-start(f32[31,512]{1,0:T(8,128)S(1)} %copy-done.1), channel_id=1, source_target_pairs={{0,2},{1,3},{2,0},{3,1},{4,6},{5,7},{6,4},{7,5},{8,10},{9,11},{10,... | collective-permute-start | bytes 190472 | tf_op jit(solution)/shard_map/ppermute | solution.py:29
  20.5 1.6 %collective-permute-start.7 = (bf16[128,1024]{1,0:T(8,128)(2,1)S(1)}, bf16[128,1024]{1,0:T(8,128)(2,1)S(1)}, u32[]{:S(2)}, u32[]{:S(2)}) collective-permute-start(bf16[128,1024]{1,0:T(8,128)(2,1)S(1)} %get-tuple-element.47), channel_id=1, source_target_pairs={{0,1},{1,0},{2,3},{3,2},{4,5},{5,4},{6,7},{7,6},{8,9},{9,8},{10,11... | collective-permute-start | bytes 786440 | tf_op jit(solution)/shard_map/ppermute | solution.py:29
  22.2 11.3 %collective-permute-start.11 = (bf16[128,1024]{1,0:T(8,128)(2,1)S(1)}, bf16[128,1024]{1,0:T(8,128)(2,1)S(1)}, u32[]{:S(2)}, u32[]{:S(2)}) collective-permute-start(bf16[128,1024]{1,0:T(8,128)(2,1)S(1)} %get-tuple-element.55.chip), channel_id=1, source_target_pairs={{0,2},{1,3},{2,0},{3,1},{4,6},{5,7},{6,4},{7,5},{8,10},{9,11},{10,... | collective-permute-start | bytes 786440 | tf_op jit(solution)/shard_map/ppermute | solution.py:29
  23.8 6.7 %collective-permute-start.8 = (bf16[48,1024]{1,0:T(8,128)(2,1)S(1)}, bf16[48,1024]{1,0:T(8,128)(2,1)S(1)}, u32[]{:S(2)}, u32[]{:S(2)}) collective-permute-start(bf16[48,1024]{1,0:T(8,128)(2,1)S(1)} %get-tuple-element.51), channel_id=1, source_target_pairs={{0,4},{4,0},{8,12},{12,8},{16,20},{20,16},{24,28},{28,24},{1,5},{5... | collective-permute-start | bytes 294920 | tf_op jit(solution)/shard_map/ppermute | solution.py:29
  26.2 4.2 %collective-permute-start.9 = (bf16[48,1024]{1,0:T(8,128)(2,1)S(1)}, bf16[48,1024]{1,0:T(8,128)(2,1)S(1)}, u32[]{:S(2)}, u32[]{:S(2)}) collective-permute-start(bf16[48,1024]{1,0:T(8,128)(2,1)S(1)} %get-tuple-element.52), channel_id=1, source_target_pairs={{0,1},{1,0},{2,3},{3,2},{4,8},{5,9},{6,10},{7,11},{8,4},{9,5},{10,... | collective-permute-start | bytes 294920 | tf_op jit(solution)/shard_map/ppermute | solution.py:51
  26.2 7.3 %collective-permute-start.12 = (bf16[128,512]{1,0:T(8,128)(2,1)S(1)}, bf16[128,512]{1,0:T(8,128)(2,1)S(1)}, u32[]{:S(2)}, u32[]{:S(2)}) collective-permute-start(bf16[128,512]{1,0:T(8,128)(2,1)S(1)} %get-tuple-element.50.q.refs_0_), channel_id=1, source_target_pairs={{0,8},{8,16},{16,24},{24,28},{28,20},{20,12},{12,4},{4,0},{1,9},{9... | collective-permute-start | bytes 393224 | tf_op jit(solution)/shard_map/ppermute | solution.py:40
  27.7 8.6 %collective-permute-start.13 = (bf16[128,512]{1,0:T(8,128)(2,1)S(1)}, bf16[128,512]{1,0:T(8,128)(2,1)S(1)}, u32[]{:S(2)}, u32[]{:S(2)}) collective-permute-start(bf16[128,512]{1,0:T(8,128)(2,1)S(1)} %get-tuple-element.50.q.refs_0_), channel_id=1, source_target_pairs={{0,1},{1,0},{2,3},{3,2},{4,5},{5,4},{6,7},{7,6},{8,12},{9,13},{10,... | collective-permute-start | bytes 393224 | tf_op jit(solution)/shard_map/ppermute | solution.py:51
  30.4 5.9 %collective-permute-start.10 = (bf16[64,1024]{1,0:T(8,128)(2,1)S(1)}, bf16[64,1024]{1,0:T(8,128)(2,1)S(1)}, u32[]{:S(2)}, u32[]{:S(2)}) collective-permute-start(bf16[64,1024]{1,0:T(8,128)(2,1)S(1)} %get-tuple-element.54.ends), channel_id=1, source_target_pairs={{0,2},{1,3},{2,0},{3,1},{4,6},{5,7},{6,4},{7,5},{8,10},{9,11},{10,... | collective-permute-start | bytes 393224 | tf_op jit(solution)/shard_map/ppermute | solution.py:29
  31.0 6.5 %collective-permute-start.14 = (bf16[128,512]{1,0:T(8,128)(2,1)S(1)}, bf16[128,512]{1,0:T(8,128)(2,1)S(1)}, u32[]{:S(2)}, u32[]{:S(2)}) collective-permute-start(bf16[128,512]{1,0:T(8,128)(2,1)S(1)} %get-tuple-element.61), channel_id=1, source_target_pairs={{0,4},{4,0},{8,12},{12,8},{16,20},{20,16},{24,28},{28,24},{1,5},{5... | collective-permute-start | bytes 393224 | tf_op jit(solution)/shard_map/ppermute | solution.py:29
  37.5 1.6 %collective-permute-start.15 = (bf16[128,1024]{1,0:T(8,128)(2,1)S(1)}, bf16[128,1024]{1,0:T(8,128)(2,1)S(1)}, u32[]{:S(2)}, u32[]{:S(2)}) collective-permute-start(bf16[128,1024]{1,0:T(8,128)(2,1)S(1)} %hand.1.own.grad_here), channel_id=1, source_target_pairs={{0,1},{1,0},{2,3},{3,2},{4,5},{5,4},{6,7},{7,6},{8,9},{9,8},{10,11... | collective-permute-start | bytes 786440 | tf_op jit(solution)/shard_map/ppermute | solution.py:29
  39.8 4.8 %collective-permute-start.17 = (bf16[144,512]{1,0:T(8,128)(2,1)S(1)}, bf16[144,512]{1,0:T(8,128)(2,1)S(1)}, u32[]{:S(2)}, u32[]{:S(2)}) collective-permute-start(bf16[144,512]{1,0:T(8,128)(2,1)S(1)} %get-tuple-element.66.message.refs_5_), channel_id=1, source_target_pairs={{0,1},{1,0},{2,3},{3,2},{4,8},{5,9},{6,10},{7,11},{8,4},{9,5},{10,... | collective-permute-start | bytes 442376 | tf_op jit(solution)/shard_map/ppermute | solution.py:51
  40.0 4.6 %collective-permute-start.18 = (bf16[144,512]{1,0:T(8,128)(2,1)S(1)}, bf16[144,512]{1,0:T(8,128)(2,1)S(1)}, u32[]{:S(2)}, u32[]{:S(2)}) collective-permute-start(bf16[144,512]{1,0:T(8,128)(2,1)S(1)} %get-tuple-element.66.message.refs_5_), channel_id=1, source_target_pairs={{0,1},{1,0},{2,3},{3,2},{4,5},{5,4},{6,7},{7,6},{8,12},{9,13},{10,... | collective-permute-start | bytes 442376 | tf_op jit(solution)/shard_map/ppermute | solution.py:51
  40.4 5.9 %collective-permute-start.19 = (bf16[144,512]{1,0:T(8,128)(2,1)S(1)}, bf16[144,512]{1,0:T(8,128)(2,1)S(1)}, u32[]{:S(2)}, u32[]{:S(2)}) collective-permute-start(bf16[144,512]{1,0:T(8,128)(2,1)S(1)} %get-tuple-element.66.message.refs_5_), channel_id=1, source_target_pairs={{0,8},{8,16},{16,24},{24,28},{28,20},{20,12},{12,4},{4,0},{1,9},{9... | collective-permute-start | bytes 442376 | tf_op jit(solution)/shard_map/ppermute | solution.py:40
  43.1 6.9 %collective-permute-start.16 = (bf16[144,512]{1,0:T(8,128)(2,1)S(1)}, bf16[144,512]{1,0:T(8,128)(2,1)S(1)}, u32[]{:S(2)}, u32[]{:S(2)}) collective-permute-start(bf16[144,512]{1,0:T(8,128)(2,1)S(1)} %get-tuple-element.66.message.refs_5_), channel_id=1, source_target_pairs={{8,0},{16,8},{24,16},{28,24},{20,28},{12,20},{4,12},{0,4},{9,1},{1... | collective-permute-start | bytes 442376 | tf_op jit(solution)/shard_map/ppermute | solution.py:40

commit v18 on v16

--- a/solution.py
+++ b/solution.py
@@ -158,8 +158,9 @@
     return weight[:, pl.ds(pl.multiple_of(at, 128), width)]
 
 
-def turn_body(block, seen, copy):
+def hand_body(block, q, seen, copy, q_copy):
     copy[...] = block[...]
+    q_copy[...] = q[...]
 
 
 def split_body(joined, seen, *parts):
@@ -209,9 +210,8 @@
         lse[:, c] = part
 
 
-def pass_body(send, q_second, seen_a, seen_b, send_copy, second_copy):
+def pass_body(send, seen_a, seen_b, send_copy):
     send_copy[...] = send[...]
-    second_copy[...] = q_second[...]
 
 
 def join_body(keep, core, inputs, cot, cot_other, q, chip, rim_near, rim_far, q_copy):
@@ -234,11 +234,11 @@
     q_copy[...] = q[...]
 
 
-def stack_body(rim_near, rim_far, q_second, ends, second_copy):
+def stack_body(rim_near, rim_far, q, ends, q_copy):
     wide = 2 * HALO
     ends[0:wide, :] = rim_near[0:wide, :]
     ends[wide : 2 * wide, :] = rim_far[0:wide, :]
-    second_copy[...] = q_second[...]
+    q_copy[...] = q[...]
 
 
 def summed(share, across, rows, cols, width):
@@ -425,7 +425,7 @@
 
 
 def key_part_body(scale, own, *refs):
-    queries, late_query, messages, (key_part, value_part, late) = refs[0:4], refs[4], refs[5:9], refs[9:12]
+    queries, messages, (key_part, value_part) = refs[0:4], refs[4:8], refs[8:10]
     frames = own.shape[0] // 2
     heads = columns(own.shape[1])
     above, below = slice(0, frames), slice(frames, 2 * frames)
@@ -434,7 +434,6 @@
     ups = [stacked(messages, above, c) for c in heads]
     scores = [dot_nt(own[above, c], a) * scale for c, a in zip(heads, asks)]
     dots = [dot_nt(own[below, c], u) for c, u in zip(heads, ups)]
-    last = [dot_nt(own[above, c], late_query[:, c]) * scale + bias_of(far_there()) for c in heads]
     logs = [[stat_rows(m, frames, 0, c) for m in messages] for c in heads]
     deltas = [[stat_rows(m, frames, 1, c) for m in messages] for c in heads]
     probs = [jnp.exp(by_block(s, biases, n)) for s, n in zip(scores, logs)]
@@ -442,20 +441,21 @@
     grads = [(p * d * scale).astype(BF16) for p, d in zip(probs, drops)]
     value_sums = [dot_nn(p.astype(BF16), u) for p, u in zip(probs, ups)]
     key_sums = [dot_nn(g, a) for g, a in zip(grads, asks)]
-    for c, k, v, s in zip(heads, key_sums, value_sums, last):
+    for c, k, v in zip(heads, key_sums, value_sums):
         key_part[:, c] = k
         value_part[:, c] = v
-        late[:, c] = s
 
 
 def key_grad_body(
-    scale, own, query, message, late, key_part, value_part, grad_key, grad_value, held_key, held_value, sems
+    scale, own, query, message, key_part, value_part, grad_key, grad_value, held_key, held_value, sems
 ):
     frames = own.shape[0] // 2
     heads = columns(own.shape[1])
     above, below = slice(0, frames), slice(frames, 2 * frames)
     ups = [message[above, c] for c in heads]
-    probs = [jnp.exp(late[:, c] - stat_rows(message, frames, 0, c)) for c in heads]
+    bias = bias_of(far_there())
+    scores = [dot_nt(own[above, c], query[:, c]) * scale + bias for c in heads]
+    probs = [jnp.exp(s - stat_rows(message, frames, 0, c)) for s, c in zip(scores, heads)]
     dots = [dot_nt(own[below, c], u) for c, u in zip(heads, ups)]
     values = [value_part[:, c] + dot_nn(p.astype(BF16), u) for c, p, u in zip(heads, probs, ups)]
     held_value[...] = jnp.concatenate([v.astype(BF16) for v in values], axis=1)
@@ -496,7 +496,6 @@
     query, inputs, cotangent = kernel_call(
         split_body, (tile, tile, tile), (joined, second), 0.1, "split", 1
     )
-    q_second = ring(query, 1)
     sums, tops, totals = kernel_call(
         functools.partial(forward_body, scale),
         (tile32, tile32, tile32),
@@ -510,7 +509,7 @@
         1.0, "project",
     )
 
-    send, q_second = kernel_call(pass_body, (both, tile), (send, q_second, cot_other, taps_other), 0.1, "pass", 2)
+    (send,) = kernel_call(pass_body, (both,), (send, cot_other, taps_other), 0.1, "pass", 2)
     core = pair_swap(send, "mp", 1)
     chip, rim_up, rim_down, q_own = kernel_call(
         join_body,
@@ -524,13 +523,13 @@
     ends, q_handed = kernel_call(
         stack_body,
         (shaped((2 * wide, 2 * width), BF16), tile),
-        (rim_near, rim_far, q_second),
+        (rim_near, rim_far, query),
         0.1, "stack",
     )
     ends_across = pair_swap(ends, "mp", 2)
     q_first = ring(q_own, 0)
     q_near = inner_swap(q_own)
-    q_relay = pair_swap(q_handed, "ctx", 1)
+    q_second = ring(q_handed, 1)
     rows_out, edge_rows, edge_conv, part_grad = kernel_call(
         conv_inner_body,
         (
@@ -550,7 +549,10 @@
         1.4, "conv_edge", 1,
     )
 
-    (grad_here,) = kernel_call(turn_body, (both,), (grad_here, q_relay), 0.1, "hand", 1)
+    grad_here, q_late = kernel_call(
+        hand_body, (both, tile), (grad_here, query, q_second), 0.1, "hand", 1
+    )
+    q_relay = outer_swap(q_late)
     gi_core = pair_swap(grad_here, "mp", 1)
     partial, terms = kernel_call(
         upstream_own_body, (tile32, shaped((16, width), F32)), (grad_here, out_weight, lse), 0.5,
@@ -569,16 +571,16 @@
         1.8, "query_grad", 0,
         [pltpu.VMEM((frames, width), BF16), pltpu.SemaphoreType.DMA((3,))], HBM,
     )
-    key_part, value_part, late = kernel_call(
+    key_part, value_part = kernel_call(
         functools.partial(key_part_body, scale),
-        (tile32, tile32, tile32),
-        (kv, q_own, q_near, q_first, q_second, q_relay, message, m_near, m_first, m_second),
+        (tile32, tile32),
+        (kv, q_own, q_near, q_first, q_second, message, m_near, m_first, m_second),
         1.5, "key_part",
     )
     grad_key, grad_value = kernel_call(
         functools.partial(key_grad_body, scale),
         (tile, tile),
-        (kv, q_relay, m_relay, late, key_part, value_part),
+        (kv, q_relay, m_relay, key_part, value_part),
         1.0, "key_grad", 0,
         [pltpu.VMEM((frames, width), BF16)] * 2 + [pltpu.SemaphoreType.DMA((2,))], HBM,
     )

time: 54.1 us -> 53.3 us (0.985)
  the two profiles are of different devices: /device:TPU:0 before, /device:TPU:10 now
where the time goes in v18:
time: 53.3 us; the launch traced here: 53.2 us
  starting transfers between devices  20.5 us (38%)
  waiting for transfers between devices  19.4 us (36%)
  Pallas kernels  10.2 us (19%)
  other arithmetic  2.19 us (4%)
  between operations  0.84 us (2%)
    pallas_call x14, Pallas kernels, kernel_call(): pl.pallas_call(body, out_shape=outs, in_specs=[VMEM] * (len(args) - unrea...  10.2 us
    ppermute x7, waiting for transfers between devices, total_swap(): return lax.ppermute(block, ('ctx', 'mp'), route)  9.22 us
    ppermute x7, starting transfers between devices, total_swap(): return lax.ppermute(block, ('ctx', 'mp'), route)  8.78 us
    ppermute x7, waiting for transfers between devices, pair_swap(): lax.ppermute(block, axis, [(i, i ^ bit) for i in range(lax.axis_size(axis...  6.31 us
    ppermute x6, starting transfers between devices, ring(): return lax.ppermute(block, 'ctx', ring_routes(lax.axis_size('ctx'))[way])  6.11 us
    ppermute x7, starting transfers between devices, pair_swap(): lax.ppermute(block, axis, [(i, i ^ bit) for i in range(lax.axis_size(axis...  5.63 us
    ppermute x6, waiting for transfers between devices, ring(): return lax.ppermute(block, 'ctx', ring_routes(lax.axis_size('ctx'))[way])  3.89 us
    add x1, other arithmetic, per_device(): lax.pad(key_rows, zero, ((0, frames, 0), (0, 0, 0)))  1.13 us
  transfers between devices with their start and end apart: 20, of which 7 were waited for; matrix products, arithmetic and copies ran while one was open for 2% of the time, Pallas kernels for 16%

profile of v18, /device:TPU:10, one launch (start us, length us, event | category | flops | bytes accessed | tf_op | source)
XLA Modules:
  0.0 53.2 jit_solution(3889759358147062187)
XLA Ops:
  0.6 0.0 copy-start
  0.6 1.1 %pad_add_fusion.1.own = bf16[256,512]{1,0:T(8,128)(2,1)S(1)} fusion(bf16[128,512]{1,0:T(8,128)(2,1)} %param.9, bf16[128,512]{1,0:T(8,128)(2,1)} %param.8), kind=kLoop, calls=%fused_computation.1 | loop fusion | flops 524288 | bytes 524288 | tf_op jit(solution)/shard_map/add | solution.py:485
  1.8 1.6 %collective-permute-start = (bf16[256,512]{1,0:T(8,128)(2,1)S(1)}, bf16[256,512]{1,0:T(8,128)(2,1)S(1)}, u32[]{:S(2)}, u32[]{:S(2)}) collective-permute-start(bf16[256,512]{1,0:T(8,128)(2,1)S(1)} %pad_add_fusion.1.own), channel_id=1, source_target_pairs={{8,0},{16,8},{24,16},{28,24},{20,28},{12,20},{4,12},{0,4},{9,1},{1... | collective-permute-start | bytes 786440 | tf_op jit(solution)/shard_map/ppermute | solution.py:40
  3.4 0.0 collective-permute-start.2
  3.4 0.4 collective-permute-start.3
  3.9 2.6 %collective-permute-start.1 = (bf16[256,512]{1,0:T(8,128)(2,1)S(1)}, bf16[256,512]{1,0:T(8,128)(2,1)S(1)}, u32[]{:S(2)}, u32[]{:S(2)}) collective-permute-start(bf16[256,512]{1,0:T(8,128)(2,1)S(1)} %pad_add_fusion.1.own), channel_id=1, source_target_pairs={{0,1},{1,0},{2,3},{3,2},{4,8},{5,9},{6,10},{7,11},{8,4},{9,5},{10,... | collective-permute-start | bytes 786440 | tf_op jit(solution)/shard_map/ppermute | solution.py:51
  6.5 1.5 %collective-permute-start.4 = (bf16[128,512]{1,0:T(8,128)(2,1)}, bf16[128,512]{1,0:T(8,128)(2,1)S(1)}, u32[]{:S(2)}, u32[]{:S(2)}) collective-permute-start(bf16[128,512]{1,0:T(8,128)(2,1)} %param.13), channel_id=1, source_target_pairs={{0,2},{1,3},{2,0},{3,1},{4,6},{5,7},{6,4},{7,5},{8,10},{9,11},{10,... | collective-permute-start | bytes 393224 | tf_op jit(solution)/shard_map/ppermute | solution.py:29
  8.0 3.1 %collective-permute-done.seen.second = bf16[256,512]{1,0:T(8,128)(2,1)S(1)} collective-permute-done((bf16[256,512]{1,0:T(8,128)(2,1)S(1)}, bf16[256,512]{1,0:T(8,128)(2,1)S(1)}, u32[]{:S(2)}, u32[]{:S(2)}) %collective-permute-start) | collective-permute-done | bytes 262176 | tf_op jit(solution)/shard_map/ppermute | solution.py:40
  11.0 1.5 %collective-permute-start.5 = (f32[31,512]{1,0:T(8,128)}, f32[31,512]{1,0:T(8,128)S(1)}, u32[]{:S(2)}, u32[]{:S(2)}) collective-permute-start(f32[31,512]{1,0:T(8,128)} %taps.3), channel_id=1, source_target_pairs={{0,2},{1,3},{2,0},{3,1},{4,6},{5,7},{6,4},{7,5},{8,10},{9,11},{10,... | collective-permute-start | bytes 190472 | tf_op jit(solution)/shard_map/ppermute | solution.py:29
  12.5 1.1 %pad_add_fusion.joined = bf16[384,512]{1,0:T(8,128)(2,1)S(1)} fusion(bf16[128,512]{1,0:T(8,128)(2,1)} %param.13, bf16[128,512]{1,0:T(8,128)(2,1)} %param.10, bf16[128,512]{1,0:T(8,128)(2,1)} %param.7), kind=kLoop, calls=%fused_computation | loop fusion | flops 1179648 | bytes 786432 | tf_op jit(solution)/shard_map/add | solution.py:488
  13.6 3.2 %collective-permute-done.2.near = bf16[256,512]{1,0:T(8,128)(2,1)S(1)} collective-permute-done((bf16[256,512]{1,0:T(8,128)(2,1)S(1)}, bf16[256,512]{1,0:T(8,128)(2,1)S(1)}, u32[]{:S(2)}, u32[]{:S(2)}) %collective-permute-start.2) | collective-permute-done | bytes 262176 | tf_op jit(solution)/shard_map/ppermute | solution.py:51
  16.8 0.0 collective-permute-done.3.first
  16.8 0.6 %forward.1 = (f32[128,512]{1,0:T(8,128)S(1)}, f32[128,512]{1,0:T(8,128)S(1)}, f32[128,512]{1,0:T(8,128)S(1)}) custom-call(bf16[128,512]{1,0:T(8,128)(2,1)S(1)} %get-tuple-element.40.q, bf16[256,512]{1,0:T(8,128)(2,1)S(1)} %pad_add_fusion.1.own, bf16[256,512]{1,0:T(8,128)(2,1)S(1)} %collective-permute-done.2.near, ...), custom_call_target="tpu_custom_call" | custom-call | bytes 3690000 | tf_op jit(solution)/shard_map/forward/pallas_call | solution.py:68
  17.4 0.0 collective-permute-done.1.relay
  17.4 0.0 copy-done
  17.4 0.0 copy-start.1
  17.4 0.9 %project.1 = (bf16[128,512]{1,0:T(8,128)(2,1)S(1)}, f32[128,512]{1,0:T(8,128)S(1)}, bf16[128,1024]{1,0:T(8,128)(2,1)S(1)}, bf16[128,1024]{1,0:T(8,128)(2,1)S(1)}) custom-call(bf16[128,512]{1,0:T(8,128)(2,1)S(1)} %get-tuple-element.40.q, bf16[256,512]{1,0:T(8,128)(2,1)S(1)} %collective-permute-done.1.relay, f32[128,512]{1,0:T(8,128)S(1)} %get-tuple-element.41.sums, ...), custom_call_target="tpu_custom_call" | custom-call | bytes 3690000 | tf_op jit(solution)/shard_map/project/pallas_call | solution.py:68
  18.3 0.0 collective-permute-done.5.seen_b.taps_other
  18.3 0.0 collective-permute-done.4.seen_a.cot_other
  18.3 0.1 collective-permute-start.6
  18.4 1.5 %collective-permute-done.6.core = bf16[128,1024]{1,0:T(8,128)(2,1)S(1)} collective-permute-done((bf16[128,1024]{1,0:T(8,128)(2,1)S(1)}, bf16[128,1024]{1,0:T(8,128)(2,1)S(1)}, u32[]{:S(2)}, u32[]{:S(2)}) %collective-permute-start.6) | collective-permute-done | bytes 262176 | tf_op jit(solution)/shard_map/ppermute | solution.py:29
  19.9 0.1 join.1
  20.1 1.6 %collective-permute-start.10 = (bf16[128,1024]{1,0:T(8,128)(2,1)S(1)}, bf16[128,1024]{1,0:T(8,128)(2,1)S(1)}, u32[]{:S(2)}, u32[]{:S(2)}) collective-permute-start(bf16[128,1024]{1,0:T(8,128)(2,1)S(1)} %get-tuple-element.52.chip), channel_id=1, source_target_pairs={{0,2},{1,3},{2,0},{3,1},{4,6},{5,7},{6,4},{7,5},{8,10},{9,11},{10,... | collective-permute-start | bytes 786440 | tf_op jit(solution)/shard_map/ppermute | solution.py:29
  21.6 0.3 collective-permute-start.7
  21.9 2.8 %collective-permute-start.8 = (bf16[48,1024]{1,0:T(8,128)(2,1)S(1)}, bf16[48,1024]{1,0:T(8,128)(2,1)S(1)}, u32[]{:S(2)}, u32[]{:S(2)}) collective-permute-start(bf16[48,1024]{1,0:T(8,128)(2,1)S(1)} %get-tuple-element.50), channel_id=1, source_target_pairs={{0,1},{1,0},{2,3},{3,2},{4,8},{5,9},{6,10},{7,11},{8,4},{9,5},{10,... | collective-permute-start | bytes 294920 | tf_op jit(solution)/shard_map/ppermute | solution.py:51
  24.7 0.4 collective-permute-start.11
  25.1 0.3 collective-permute-start.12
  25.4 3.7 %collective-permute-done.7.rim_near = bf16[48,1024]{1,0:T(8,128)(2,1)S(1)} collective-permute-done((bf16[48,1024]{1,0:T(8,128)(2,1)S(1)}, bf16[48,1024]{1,0:T(8,128)(2,1)S(1)}, u32[]{:S(2)}, u32[]{:S(2)}) %collective-permute-start.7) | collective-permute-done | bytes 98336 | tf_op jit(solution)/shard_map/ppermute | solution.py:29
  29.1 0.0 collective-permute-done.8.rim_far
  29.2 0.6 %collective-permute-start.9 = (bf16[64,1024]{1,0:T(8,128)(2,1)S(1)}, bf16[64,1024]{1,0:T(8,128)(2,1)S(1)}, u32[]{:S(2)}, u32[]{:S(2)}) collective-permute-start(bf16[64,1024]{1,0:T(8,128)(2,1)S(1)} %get-tuple-element.51.ends), channel_id=1, source_target_pairs={{0,2},{1,3},{2,0},{3,1},{4,6},{5,7},{6,4},{7,5},{8,10},{9,11},{10,... | collective-permute-start | bytes 393224 | tf_op jit(solution)/shard_map/ppermute | solution.py:29
  29.7 1.6 %collective-permute-start.13 = (bf16[128,512]{1,0:T(8,128)(2,1)S(1)}, bf16[128,512]{1,0:T(8,128)(2,1)S(1)}, u32[]{:S(2)}, u32[]{:S(2)}) collective-permute-start(bf16[128,512]{1,0:T(8,128)(2,1)S(1)} %get-tuple-element.58), channel_id=1, source_target_pairs={{8,0},{16,8},{24,16},{28,24},{20,28},{12,20},{4,12},{0,4},{9,1},{1... | collective-permute-start | bytes 393224 | tf_op jit(solution)/shard_map/ppermute | solution.py:40
  31.3 0.0 collective-permute-done.11.seen.refs_2_
  31.3 0.0 collective-permute-done.10.across
  31.3 0.0 copy-done.1
  31.3 2.8 %conv_inner.1 = (bf16[128,512]{1,0:T(8,128)(2,1)S(1)}, f32[32,512]{1,0:T(8,128)S(1)}, f32[64,1024]{1,0:T(8,128)S(1)}, f32[128,1024]{1,0:T(8,128)S(1)}) custom-call(bf16[128,1024]{1,0:T(8,128)(2,1)S(1)} %get-tuple-element.52.chip, bf16[128,1024]{1,0:T(8,128)(2,1)S(1)} %collective-permute-done.10.across, bf16[128,512]{1,0:T(8,128)(2,1)S(1)} %get-tuple-element.47.cot, ...), custom_call_target="tpu_custom_call" | custom-call | bytes 11439000 | tf_op jit(solution)/shard_map/conv_inner/pallas_call | solution.py:68
  34.1 0.0 collective-permute-done.12.seen.refs_1_
  34.1 0.0 collective-permute-done.9.ends_across
  34.2 1.1 %conv_edge.1 = (bf16[128,512]{1,0:T(8,128)(2,1)S(1)}, bf16[128,1024]{1,0:T(8,128)(2,1)S(1)}) custom-call(bf16[64,1024]{1,0:T(8,128)(2,1)S(1)} %get-tuple-element.51.ends, bf16[64,1024]{1,0:T(8,128)(2,1)S(1)} %collective-permute-done.9.ends_across, bf16[48,1024]{1,0:T(8,128)(2,1)S(1)} %collective-permute-done.7.rim_near, ...), custom_call_target="tpu_custom_call" | custom-call | bytes 5166000 | tf_op jit(solution)/shard_map/conv_edge/pallas_call | solution.py:68
  35.3 0.0 collective-permute-done.13.seen.refs_3_
  35.4 0.1 collective-permute-start.14
  35.4 0.5 upstream_own.1
  35.9 1.0 %collective-permute-done.14.core = bf16[128,1024]{1,0:T(8,128)(2,1)S(1)} collective-permute-done((bf16[128,1024]{1,0:T(8,128)(2,1)S(1)}, bf16[128,1024]{1,0:T(8,128)(2,1)S(1)}, u32[]{:S(2)}, u32[]{:S(2)}) %collective-permute-start.14) | collective-permute-done | bytes 262176 | tf_op jit(solution)/shard_map/ppermute | solution.py:29
  37.0 0.7 %upstream.1 = (bf16[144,512]{1,0:T(8,128)(2,1)S(1)}, f32[128,512]{1,0:T(8,128)S(1)}) custom-call(bf16[128,1024]{1,0:T(8,128)(2,1)S(1)} %collective-permute-done.14.core, bf16[512,2048]{1,0:T(8,128)(2,1)S(1)} %copy-done, bf16[128,512]{1,0:T(8,128)(2,1)S(1)} %get-tuple-element.60.att, f32[128,512]{1,0:T(8,128)S(1)} %get-tuple-element.62.partial, ...), custom_call_target="tpu_custom_call" | custom-call | bytes 2214000 | tf_op jit(solution)/shard_map/upstream/pallas_call | solution.py:68
  37.6 0.2 collective-permute-start.17
  37.8 0.7 %collective-permute-start.18 = (bf16[144,512]{1,0:T(8,128)(2,1)S(1)}, bf16[144,512]{1,0:T(8,128)(2,1)S(1)}, u32[]{:S(2)}, u32[]{:S(2)}) collective-permute-start(bf16[144,512]{1,0:T(8,128)(2,1)S(1)} %get-tuple-element.64.message.refs_4_), channel_id=1, source_target_pairs={{0,8},{8,16},{16,24},{24,28},{28,20},{20,12},{12,4},{4,0},{1,9},{9... | collective-permute-start | bytes 442376 | tf_op jit(solution)/shard_map/ppermute | solution.py:40
  38.5 1.3 %collective-permute-start.19 = (bf16[144,512]{1,0:T(8,128)(2,1)S(1)}, bf16[144,512]{1,0:T(8,128)(2,1)S(1)}, u32[]{:S(2)}, u32[]{:S(2)}) collective-permute-start(bf16[144,512]{1,0:T(8,128)(2,1)S(1)} %get-tuple-element.64.message.refs_4_), channel_id=1, source_target_pairs={{8,0},{16,8},{24,16},{28,24},{20,28},{12,20},{4,12},{0,4},{9,1},{1... | collective-permute-start | bytes 442376 | tf_op jit(solution)/shard_map/ppermute | solution.py:40
  39.8 2.9 %collective-permute-start.16 = (bf16[144,512]{1,0:T(8,128)(2,1)S(1)}, bf16[144,512]{1,0:T(8,128)(2,1)S(1)}, u32[]{:S(2)}, u32[]{:S(2)}) collective-permute-start(bf16[144,512]{1,0:T(8,128)(2,1)S(1)} %get-tuple-element.64.message.refs_4_), channel_id=1, source_target_pairs={{0,1},{1,0},{2,3},{3,2},{4,8},{5,9},{6,10},{7,11},{8,4},{9,5},{10,... | collective-permute-start | bytes 442376 | tf_op jit(solution)/shard_map/ppermute | solution.py:51
  42.8 0.0 collective-permute-start.15
  42.8 1.5 %query_grad.1 = (bf16[128,512]{1,0:T(8,128)(2,1)}, bf16[128,512]{1,0:T(8,128)(2,1)}, bf16[128,512]{1,0:T(8,128)(2,1)}) custom-call(bf16[128,512]{1,0:T(8,128)(2,1)S(1)} %get-tuple-element.48.q.refs_0_, bf16[256,512]{1,0:T(8,128)(2,1)S(1)} %pad_add_fusion.1.own, bf16[256,512]{1,0:T(8,128)(2,1)S(1)} %collective-permute-done.2.near, ...), custom_call_target="tpu_custom_call" | custom-call | bytes 6642000 | tf_op jit(solution)/shard_map/query_grad/pallas_call | solution.py:68
  44.3 0.0 collective-permute-done.17.refs_5_
  44.4 0.0 collective-permute-done.18.refs_6_
  44.4 0.8 %collective-permute-done.19.refs_7_ = bf16[144,512]{1,0:T(8,128)(2,1)S(1)} collective-permute-done((bf16[144,512]{1,0:T(8,128)(2,1)S(1)}, bf16[144,512]{1,0:T(8,128)(2,1)S(1)}, u32[]{:S(2)}, u32[]{:S(2)}) %collective-permute-start.19) | collective-permute-done | bytes 147488 | tf_op jit(solution)/shard_map/ppermute | solution.py:40
  45.2 0.8 %key_part.1 = (f32[128,512]{1,0:T(8,128)S(1)}, f32[128,512]{1,0:T(8,128)S(1)}) custom-call(bf16[256,512]{1,0:T(8,128)(2,1)S(1)} %pad_add_fusion.1.own, bf16[128,512]{1,0:T(8,128)(2,1)S(1)} %get-tuple-element.48.q.refs_0_, bf16[128,512]{1,0:T(8,128)(2,1)S(1)} %collective-permute-done.12.seen.refs_1_, ...), custom_call_target="tpu_custom_call" | custom-call | bytes 5535000 | tf_op jit(solution)/shard_map/key_part/pallas_call | solution.py:68
  46.0 6.1 %collective-permute-done.15.query = bf16[128,512]{1,0:T(8,128)(2,1)S(1)} collective-permute-done((bf16[128,512]{1,0:T(8,128)(2,1)S(1)}, bf16[128,512]{1,0:T(8,128)(2,1)S(1)}, u32[]{:S(2)}, u32[]{:S(2)}) %collective-permute-start.15) | collective-permute-done | bytes 131104 | tf_op jit(solution)/shard_map/ppermute | solution.py:51
  52.0 0.0 collective-permute-done.16.message
  52.0 1.1 %key_grad.1 = (bf16[128,512]{1,0:T(8,128)(2,1)}, bf16[128,512]{1,0:T(8,128)(2,1)}) custom-call(bf16[256,512]{1,0:T(8,128)(2,1)S(1)} %pad_add_fusion.1.own, bf16[128,512]{1,0:T(8,128)(2,1)S(1)} %collective-permute-done.15.query, bf16[144,512]{1,0:T(8,128)(2,1)S(1)} %collective-permute-done.16.message, f32[128,512]{1,0:T(8,128)S(1)} %get-tuple-element.71.key_part, ...), custom_call_target="tpu_custom_call" | custom-call | bytes 3690000 | tf_op jit(solution)/shard_map/key_grad/pallas_call | solution.py:68
  (4 shorter events, 0.1 us)
Async XLA Ops:
  0.6 16.8 %copy-start = (bf16[512,2048]{1,0:T(8,128)(2,1)S(1)}, bf16[512,2048]{1,0:T(8,128)(2,1)}, u32[]{:S(2)}) copy-start(bf16[512,2048]{1,0:T(8,128)(2,1)} %weight.5) | copy-start | bytes 6291460
  1.8 9.2 %collective-permute-start = (bf16[256,512]{1,0:T(8,128)(2,1)S(1)}, bf16[256,512]{1,0:T(8,128)(2,1)S(1)}, u32[]{:S(2)}, u32[]{:S(2)}) collective-permute-start(bf16[256,512]{1,0:T(8,128)(2,1)S(1)} %pad_add_fusion.1.own), channel_id=1, source_target_pairs={{8,0},{16,8},{24,16},{28,24},{20,28},{12,20},{4,12},{0,4},{9,1},{1... | collective-permute-start | bytes 786440 | tf_op jit(solution)/shard_map/ppermute | solution.py:40
  3.4 13.4 %collective-permute-start.2 = (bf16[256,512]{1,0:T(8,128)(2,1)S(1)}, bf16[256,512]{1,0:T(8,128)(2,1)S(1)}, u32[]{:S(2)}, u32[]{:S(2)}) collective-permute-start(bf16[256,512]{1,0:T(8,128)(2,1)S(1)} %pad_add_fusion.1.own), channel_id=1, source_target_pairs={{0,1},{1,0},{2,3},{3,2},{4,5},{5,4},{6,7},{7,6},{8,12},{9,13},{10,... | collective-permute-start | bytes 786440 | tf_op jit(solution)/shard_map/ppermute | solution.py:51
  3.4 13.4 %collective-permute-start.3 = (bf16[256,512]{1,0:T(8,128)(2,1)S(1)}, bf16[256,512]{1,0:T(8,128)(2,1)S(1)}, u32[]{:S(2)}, u32[]{:S(2)}) collective-permute-start(bf16[256,512]{1,0:T(8,128)(2,1)S(1)} %pad_add_fusion.1.own), channel_id=1, source_target_pairs={{0,8},{8,16},{16,24},{24,28},{28,20},{20,12},{12,4},{4,0},{1,9},{9... | collective-permute-start | bytes 786440 | tf_op jit(solution)/shard_map/ppermute | solution.py:40
  3.9 13.5 %collective-permute-start.1 = (bf16[256,512]{1,0:T(8,128)(2,1)S(1)}, bf16[256,512]{1,0:T(8,128)(2,1)S(1)}, u32[]{:S(2)}, u32[]{:S(2)}) collective-permute-start(bf16[256,512]{1,0:T(8,128)(2,1)S(1)} %pad_add_fusion.1.own), channel_id=1, source_target_pairs={{0,1},{1,0},{2,3},{3,2},{4,8},{5,9},{6,10},{7,11},{8,4},{9,5},{10,... | collective-permute-start | bytes 786440 | tf_op jit(solution)/shard_map/ppermute | solution.py:51
  6.5 11.9 %collective-permute-start.4 = (bf16[128,512]{1,0:T(8,128)(2,1)}, bf16[128,512]{1,0:T(8,128)(2,1)S(1)}, u32[]{:S(2)}, u32[]{:S(2)}) collective-permute-start(bf16[128,512]{1,0:T(8,128)(2,1)} %param.13), channel_id=1, source_target_pairs={{0,2},{1,3},{2,0},{3,1},{4,6},{5,7},{6,4},{7,5},{8,10},{9,11},{10,... | collective-permute-start | bytes 393224 | tf_op jit(solution)/shard_map/ppermute | solution.py:29
  11.0 7.3 %collective-permute-start.5 = (f32[31,512]{1,0:T(8,128)}, f32[31,512]{1,0:T(8,128)S(1)}, u32[]{:S(2)}, u32[]{:S(2)}) collective-permute-start(f32[31,512]{1,0:T(8,128)} %taps.3), channel_id=1, source_target_pairs={{0,2},{1,3},{2,0},{3,1},{4,6},{5,7},{6,4},{7,5},{8,10},{9,11},{10,... | collective-permute-start | bytes 190472 | tf_op jit(solution)/shard_map/ppermute | solution.py:29
  17.4 13.9 %copy-start.1 = (f32[31,512]{1,0:T(8,128)S(1)}, f32[31,512]{1,0:T(8,128)}, u32[]{:S(2)}) copy-start(f32[31,512]{1,0:T(8,128)} %taps.3) | copy-start | bytes 190468
  18.3 1.6 %collective-permute-start.6 = (bf16[128,1024]{1,0:T(8,128)(2,1)S(1)}, bf16[128,1024]{1,0:T(8,128)(2,1)S(1)}, u32[]{:S(2)}, u32[]{:S(2)}) collective-permute-start(bf16[128,1024]{1,0:T(8,128)(2,1)S(1)} %pass.1), channel_id=1, source_target_pairs={{0,1},{1,0},{2,3},{3,2},{4,5},{5,4},{6,7},{7,6},{8,9},{9,8},{10,11... | collective-permute-start | bytes 786440 | tf_op jit(solution)/shard_map/ppermute | solution.py:29
  20.1 11.2 %collective-permute-start.10 = (bf16[128,1024]{1,0:T(8,128)(2,1)S(1)}, bf16[128,1024]{1,0:T(8,128)(2,1)S(1)}, u32[]{:S(2)}, u32[]{:S(2)}) collective-permute-start(bf16[128,1024]{1,0:T(8,128)(2,1)S(1)} %get-tuple-element.52.chip), channel_id=1, source_target_pairs={{0,2},{1,3},{2,0},{3,1},{4,6},{5,7},{6,4},{7,5},{8,10},{9,11},{10,... | collective-permute-start | bytes 786440 | tf_op jit(solution)/shard_map/ppermute | solution.py:29
  21.6 7.5 %collective-permute-start.7 = (bf16[48,1024]{1,0:T(8,128)(2,1)S(1)}, bf16[48,1024]{1,0:T(8,128)(2,1)S(1)}, u32[]{:S(2)}, u32[]{:S(2)}) collective-permute-start(bf16[48,1024]{1,0:T(8,128)(2,1)S(1)} %get-tuple-element.49), channel_id=1, source_target_pairs={{0,4},{4,0},{8,12},{12,8},{16,20},{20,16},{24,28},{28,24},{1,5},{5... | collective-permute-start | bytes 294920 | tf_op jit(solution)/shard_map/ppermute | solution.py:29
  21.9 7.2 %collective-permute-start.8 = (bf16[48,1024]{1,0:T(8,128)(2,1)S(1)}, bf16[48,1024]{1,0:T(8,128)(2,1)S(1)}, u32[]{:S(2)}, u32[]{:S(2)}) collective-permute-start(bf16[48,1024]{1,0:T(8,128)(2,1)S(1)} %get-tuple-element.50), channel_id=1, source_target_pairs={{0,1},{1,0},{2,3},{3,2},{4,8},{5,9},{6,10},{7,11},{8,4},{9,5},{10,... | collective-permute-start | bytes 294920 | tf_op jit(solution)/shard_map/ppermute | solution.py:51
  24.7 6.6 %collective-permute-start.11 = (bf16[128,512]{1,0:T(8,128)(2,1)S(1)}, bf16[128,512]{1,0:T(8,128)(2,1)S(1)}, u32[]{:S(2)}, u32[]{:S(2)}) collective-permute-start(bf16[128,512]{1,0:T(8,128)(2,1)S(1)} %get-tuple-element.48.q.refs_0_), channel_id=1, source_target_pairs={{0,8},{8,16},{16,24},{24,28},{28,20},{20,12},{12,4},{4,0},{1,9},{9... | collective-permute-start | bytes 393224 | tf_op jit(solution)/shard_map/ppermute | solution.py:40
  25.1 9.0 %collective-permute-start.12 = (bf16[128,512]{1,0:T(8,128)(2,1)S(1)}, bf16[128,512]{1,0:T(8,128)(2,1)S(1)}, u32[]{:S(2)}, u32[]{:S(2)}) collective-permute-start(bf16[128,512]{1,0:T(8,128)(2,1)S(1)} %get-tuple-element.48.q.refs_0_), channel_id=1, source_target_pairs={{0,1},{1,0},{2,3},{3,2},{4,5},{5,4},{6,7},{7,6},{8,12},{9,13},{10,... | collective-permute-start | bytes 393224 | tf_op jit(solution)/shard_map/ppermute | solution.py:51
  29.2 5.0 %collective-permute-start.9 = (bf16[64,1024]{1,0:T(8,128)(2,1)S(1)}, bf16[64,1024]{1,0:T(8,128)(2,1)S(1)}, u32[]{:S(2)}, u32[]{:S(2)}) collective-permute-start(bf16[64,1024]{1,0:T(8,128)(2,1)S(1)} %get-tuple-element.51.ends), channel_id=1, source_target_pairs={{0,2},{1,3},{2,0},{3,1},{4,6},{5,7},{6,4},{7,5},{8,10},{9,11},{10,... | collective-permute-start | bytes 393224 | tf_op jit(solution)/shard_map/ppermute | solution.py:29
  29.7 5.6 %collective-permute-start.13 = (bf16[128,512]{1,0:T(8,128)(2,1)S(1)}, bf16[128,512]{1,0:T(8,128)(2,1)S(1)}, u32[]{:S(2)}, u32[]{:S(2)}) collective-permute-start(bf16[128,512]{1,0:T(8,128)(2,1)S(1)} %get-tuple-element.58), channel_id=1, source_target_pairs={{8,0},{16,8},{24,16},{28,24},{20,28},{12,20},{4,12},{0,4},{9,1},{1... | collective-permute-start | bytes 393224 | tf_op jit(solution)/shard_map/ppermute | solution.py:40
  35.4 1.6 %collective-permute-start.14 = (bf16[128,1024]{1,0:T(8,128)(2,1)S(1)}, bf16[128,1024]{1,0:T(8,128)(2,1)S(1)}, u32[]{:S(2)}, u32[]{:S(2)}) collective-permute-start(bf16[128,1024]{1,0:T(8,128)(2,1)S(1)} %get-tuple-element.59.own.grad_here), channel_id=1, source_target_pairs={{0,1},{1,0},{2,3},{3,2},{4,5},{5,4},{6,7},{7,6},{8,9},{9,8},{10,11... | collective-permute-start | bytes 786440 | tf_op jit(solution)/shard_map/ppermute | solution.py:29
  37.6 6.7 %collective-permute-start.17 = (bf16[144,512]{1,0:T(8,128)(2,1)S(1)}, bf16[144,512]{1,0:T(8,128)(2,1)S(1)}, u32[]{:S(2)}, u32[]{:S(2)}) collective-permute-start(bf16[144,512]{1,0:T(8,128)(2,1)S(1)} %get-tuple-element.64.message.refs_4_), channel_id=1, source_target_pairs={{0,1},{1,0},{2,3},{3,2},{4,5},{5,4},{6,7},{7,6},{8,12},{9,13},{10,... | collective-permute-start | bytes 442376 | tf_op jit(solution)/shard_map/ppermute | solution.py:51
  37.8 6.5 %collective-permute-start.18 = (bf16[144,512]{1,0:T(8,128)(2,1)S(1)}, bf16[144,512]{1,0:T(8,128)(2,1)S(1)}, u32[]{:S(2)}, u32[]{:S(2)}) collective-permute-start(bf16[144,512]{1,0:T(8,128)(2,1)S(1)} %get-tuple-element.64.message.refs_4_), channel_id=1, source_target_pairs={{0,8},{8,16},{16,24},{24,28},{28,20},{20,12},{12,4},{4,0},{1,9},{9... | collective-permute-start | bytes 442376 | tf_op jit(solution)/shard_map/ppermute | solution.py:40
  38.5 6.7 %collective-permute-start.19 = (bf16[144,512]{1,0:T(8,128)(2,1)S(1)}, bf16[144,512]{1,0:T(8,128)(2,1)S(1)}, u32[]{:S(2)}, u32[]{:S(2)}) collective-permute-start(bf16[144,512]{1,0:T(8,128)(2,1)S(1)} %get-tuple-element.64.message.refs_4_), channel_id=1, source_target_pairs={{8,0},{16,8},{24,16},{28,24},{20,28},{12,20},{4,12},{0,4},{9,1},{1... | collective-permute-start | bytes 442376 | tf_op jit(solution)/shard_map/ppermute | solution.py:40
  39.8 12.2 %collective-permute-start.16 = (bf16[144,512]{1,0:T(8,128)(2,1)S(1)}, bf16[144,512]{1,0:T(8,128)(2,1)S(1)}, u32[]{:S(2)}, u32[]{:S(2)}) collective-permute-start(bf16[144,512]{1,0:T(8,128)(2,1)S(1)} %get-tuple-element.64.message.refs_4_), channel_id=1, source_target_pairs={{0,1},{1,0},{2,3},{3,2},{4,8},{5,9},{6,10},{7,11},{8,4},{9,5},{10,... | collective-permute-start | bytes 442376 | tf_op jit(solution)/shard_map/ppermute | solution.py:51
  42.8 9.3 %collective-permute-start.15 = (bf16[128,512]{1,0:T(8,128)(2,1)S(1)}, bf16[128,512]{1,0:T(8,128)(2,1)S(1)}, u32[]{:S(2)}, u32[]{:S(2)}) collective-permute-start(bf16[128,512]{1,0:T(8,128)(2,1)S(1)} %get-tuple-element.70), channel_id=1, source_target_pairs={{0,1},{1,0},{2,3},{3,2},{4,8},{5,9},{6,10},{7,11},{8,4},{9,5},{10,... | collective-permute-start | bytes 393224 | tf_op jit(solution)/shard_map/ppermute | solution.py:51

commit v19 on v15

--- a/solution.py
+++ b/solution.py
@@ -166,8 +166,8 @@
     return weight[:, pl.ds(pl.multiple_of(at, 128), width)]
 
 
-def turn_body(block, seen, copy):
-    copy[...] = block[...]
+def turn_body(block, *refs):
+    refs[-1][...] = block[...]
 
 
 def split_body(joined, seen, *parts):
@@ -194,7 +194,7 @@
         totals[:, c] = s[:, HDIM:]
 
 
-def project_body(scale, q, relay, sums, tops, totals, weight, att, lse, send, keep):
+def project_body(scale, q, relay, sums, tops, totals, weight, att, lse, send):
     frames, width = q.shape
     heads = columns(width)
     bias = bias_of(far_there())
@@ -208,18 +208,20 @@
     summed = [sums[:, c] * k + s[:, 0:HDIM] for c, k, s in zip(heads, shrink, late)]
     attended = jnp.concatenate([(s * (1.0 / t)).astype(BF16) for s, t in zip(summed, total)], axis=1)
     sent = [dot_nn(attended, weight_columns(weight, flip)).astype(BF16) for flip in (1, 3)]
-    kept = [dot_nn(attended, weight_columns(weight, flip)).astype(BF16) for flip in (0, 2)]
     logs = [t + jnp.log(n) for t, n in zip(top, total)]
     att[...] = attended
     send[...] = jnp.concatenate(sent, axis=1)
-    keep[...] = jnp.concatenate(kept, axis=1)
     for c, part in zip(heads, logs):
         lse[:, c] = part
 
 
-def pass_body(send, q_second, seen_a, seen_b, send_copy, second_copy):
+def project_own_body(att, weight, keep):
+    kept = [dot_nn(att[...], weight_columns(weight, flip)).astype(BF16) for flip in (0, 2)]
+    keep[...] = jnp.concatenate(kept, axis=1)
+
+
+def pass_body(send, seen_a, seen_b, send_copy):
     send_copy[...] = send[...]
-    second_copy[...] = q_second[...]
 
 
 def join_body(keep, core, inputs, cot, cot_other, q, chip, rim_near, rim_far, q_copy):
@@ -497,13 +499,13 @@
         lax.pad(rows, zero, ((k * frames, (2 - k) * frames, 0), (0, 0, 0)))
         for k, rows in enumerate((query_rows, inputs, cotangent))
     )
+    cot_other = pair_swap(cotangent, "mp", 2)
     near, first, second, relay = window_of(
         kv,
         lambda second: kernel_call(
-            turn_body, (shaped(kv.shape, BF16),), (second, joined), 0.1, "turn", 1
+            turn_body, (shaped(kv.shape, BF16),), (second, joined, cot_other), 0.1, "turn", 2
         )[0],
     )
-    cot_other = pair_swap(cotangent, "mp", 2)
     taps_other = pair_swap(kernel, "mp", 2)
     query, inputs, cotangent = kernel_call(
         split_body, (tile, tile, tile), (joined, second), 0.1, "split", 1
@@ -515,15 +517,16 @@
         (query, kv, near, first, second),
         1.0, "forward",
     )
-    att, lse, send, keep = kernel_call(
+    att, lse, send = kernel_call(
         functools.partial(project_body, scale),
-        (tile, tile32, both, both),
+        (tile, tile32, both),
         (query, relay, sums, tops, totals, out_weight),
         1.0, "project",
     )
 
-    send, q_second = kernel_call(pass_body, (both, tile), (send, q_second, cot_other, taps_other), 0.1, "pass", 2)
+    (send,) = kernel_call(pass_body, (both,), (send, taps_other, q_second), 0.1, "pass", 2)
     core = pair_swap(send, "mp", 1)
+    (keep,) = kernel_call(project_own_body, (both,), (att, out_weight), 0.4, "project_own")
     chip, rim_up, rim_down, q_own = kernel_call(
         join_body,
         (both, rim, rim, tile),

time: 50.6 us -> 50.9 us (level)
    ppermute x6, waiting for transfers between devices: 7.57 us -> 6.19 us  [ring(): return lax.ppermute(block, 'ctx', ring_routes(lax.axis_size('ctx'))[way])]
    ppermute x9, waiting for transfers between devices: 8.38 us -> 9.57 us  [pair_swap(): lax.ppermute(block, axis, [(i, i ^ bit) for i in range(lax.axis_size(axis...]
    pallas_call x15 -> x16, Pallas kernels: 10.2 us -> 10.3 us  [kernel_call(): pl.pallas_call(body, out_shape=outs, in_specs=[VMEM] * (len(args) - unrea...]
where the time goes in v19:
time: 50.9 us; the launch traced here: 50.7 us
  starting transfers between devices  21.5 us (42%)
  waiting for transfers between devices  15.8 us (31%)
  Pallas kernels  10.3 us (20%)
  other arithmetic  2.19 us (4%)
  between operations  0.85 us (2%)
    ppermute x9, starting transfers between devices, pair_swap(): lax.ppermute(block, axis, [(i, i ^ bit) for i in range(lax.axis_size(axis...  11.3 us
    pallas_call x16, Pallas kernels, kernel_call(): pl.pallas_call(body, out_shape=outs, in_specs=[VMEM] * (len(args) - unrea...  10.3 us
    ppermute x6, starting transfers between devices, ring(): return lax.ppermute(block, 'ctx', ring_routes(lax.axis_size('ctx'))[way])  10.1 us
    ppermute x9, waiting for transfers between devices, pair_swap(): lax.ppermute(block, axis, [(i, i ^ bit) for i in range(lax.axis_size(axis...  9.57 us
    ppermute x6, waiting for transfers between devices, ring(): return lax.ppermute(block, 'ctx', ring_routes(lax.axis_size('ctx'))[way])  6.19 us
    add x1, other arithmetic, per_device(): lax.pad(key_rows, zero, ((0, frames, 0), (0, 0, 0)))  1.14 us
    add x1, other arithmetic, per_device(): sum((lax.pad(rows, zero, ((k * frames, (2 - k) * frames, 0), (0, 0, 0)))...  1.06 us
  transfers between devices with their start and end apart: 20, of which 8 were waited for; matrix products, arithmetic and copies ran while one was open for 2% of the time, Pallas kernels for 17%

profile of v19, /device:TPU:0, one launch (start us, length us, event | category | flops | bytes accessed | tf_op | source)
XLA Modules:
  0.0 50.7 jit_solution(5394180189941792029)
XLA Ops:
  0.6 0.0 copy-start.1
  0.6 0.0 copy-start
  0.7 1.1 %pad_add_fusion.1.own = bf16[256,512]{1,0:T(8,128)(2,1)S(1)} fusion(bf16[128,512]{1,0:T(8,128)(2,1)} %param.9, bf16[128,512]{1,0:T(8,128)(2,1)} %param.8), kind=kLoop, calls=%fused_computation.1 | loop fusion | flops 524288 | bytes 524288 | tf_op jit(solution)/shard_map/add | solution.py:495
  1.8 3.0 %collective-permute-start = (bf16[256,512]{1,0:T(8,128)(2,1)S(1)}, bf16[256,512]{1,0:T(8,128)(2,1)S(1)}, u32[]{:S(2)}, u32[]{:S(2)}) collective-permute-start(bf16[256,512]{1,0:T(8,128)(2,1)S(1)} %pad_add_fusion.1.own), channel_id=1, source_target_pairs={{8,0},{16,8},{24,16},{28,24},{20,28},{12,20},{4,12},{0,4},{9,1},{1... | collective-permute-start | bytes 786440 | tf_op jit(solution)/shard_map/ppermute | solution.py:40
  4.8 1.5 %collective-permute-start.1 = (bf16[128,512]{1,0:T(8,128)(2,1)}, bf16[128,512]{1,0:T(8,128)(2,1)S(1)}, u32[]{:S(2)}, u32[]{:S(2)}) collective-permute-start(bf16[128,512]{1,0:T(8,128)(2,1)} %param.13), channel_id=1, source_target_pairs={{0,2},{1,3},{2,0},{3,1},{4,6},{5,7},{6,4},{7,5},{8,10},{9,11},{10,... | collective-permute-start | bytes 393224 | tf_op jit(solution)/shard_map/ppermute | solution.py:29
  6.3 0.0 collective-permute-start.3
  6.3 3.2 %collective-permute-start.4 = (bf16[256,512]{1,0:T(8,128)(2,1)S(1)}, bf16[256,512]{1,0:T(8,128)(2,1)S(1)}, u32[]{:S(2)}, u32[]{:S(2)}) collective-permute-start(bf16[256,512]{1,0:T(8,128)(2,1)S(1)} %pad_add_fusion.1.own), channel_id=1, source_target_pairs={{0,8},{8,16},{16,24},{24,28},{28,20},{20,12},{12,4},{4,0},{1,9},{9... | collective-permute-start | bytes 786440 | tf_op jit(solution)/shard_map/ppermute | solution.py:40
  9.5 1.1 %pad_add_fusion.refs_0_.joined = bf16[384,512]{1,0:T(8,128)(2,1)S(1)} fusion(bf16[128,512]{1,0:T(8,128)(2,1)} %param.13, bf16[128,512]{1,0:T(8,128)(2,1)} %param.10, bf16[128,512]{1,0:T(8,128)(2,1)} %param.7), kind=kLoop, calls=%fused_computation | loop fusion | flops 1179648 | bytes 786432 | tf_op jit(solution)/shard_map/add | solution.py:498
  10.5 0.0 collective-permute-done.1.refs_1_.cot_other
  10.5 0.6 %collective-permute-done.block = bf16[256,512]{1,0:T(8,128)(2,1)S(1)} collective-permute-done((bf16[256,512]{1,0:T(8,128)(2,1)S(1)}, bf16[256,512]{1,0:T(8,128)(2,1)S(1)}, u32[]{:S(2)}, u32[]{:S(2)}) %collective-permute-start) | collective-permute-done | bytes 262176 | tf_op jit(solution)/shard_map/ppermute | solution.py:40
  11.2 1.7 %collective-permute-start.2 = (bf16[256,512]{1,0:T(8,128)(2,1)S(1)}, bf16[256,512]{1,0:T(8,128)(2,1)S(1)}, u32[]{:S(2)}, u32[]{:S(2)}) collective-permute-start(bf16[256,512]{1,0:T(8,128)(2,1)S(1)} %turn.1.seen.second), channel_id=1, source_target_pairs={{0,4},{4,0},{8,12},{12,8},{16,20},{20,16},{24,28},{28,24},{1,5},{5... | collective-permute-start | bytes 786440 | tf_op jit(solution)/shard_map/ppermute | solution.py:29
  12.9 0.4 collective-permute-start.6
  13.4 0.0 copy-done.1
  13.4 1.7 %collective-permute-start.5 = (f32[31,512]{1,0:T(8,128)S(1)}, f32[31,512]{1,0:T(8,128)S(1)}, u32[]{:S(2)}, u32[]{:S(2)}) collective-permute-start(f32[31,512]{1,0:T(8,128)S(1)} %copy-done.1), channel_id=1, source_target_pairs={{0,2},{1,3},{2,0},{3,1},{4,6},{5,7},{6,4},{7,5},{8,10},{9,11},{10,... | collective-permute-start | bytes 190472 | tf_op jit(solution)/shard_map/ppermute | solution.py:29
  15.1 0.0 collective-permute-done.3.near
  15.1 0.3 collective-permute-done.4.first
  15.4 0.6 %forward.1 = (f32[128,512]{1,0:T(8,128)S(1)}, f32[128,512]{1,0:T(8,128)S(1)}, f32[128,512]{1,0:T(8,128)S(1)}) custom-call(bf16[128,512]{1,0:T(8,128)(2,1)S(1)} %get-tuple-element.38.q, bf16[256,512]{1,0:T(8,128)(2,1)S(1)} %pad_add_fusion.1.own, bf16[256,512]{1,0:T(8,128)(2,1)S(1)} %collective-permute-done.3.near, ...), custom_call_target="tpu_custom_call" | custom-call | bytes 3690000 | tf_op jit(solution)/shard_map/forward/pallas_call | solution.py:76
  16.0 4.6 %collective-permute-done.2.relay = bf16[256,512]{1,0:T(8,128)(2,1)S(1)} collective-permute-done((bf16[256,512]{1,0:T(8,128)(2,1)S(1)}, bf16[256,512]{1,0:T(8,128)(2,1)S(1)}, u32[]{:S(2)}, u32[]{:S(2)}) %collective-permute-start.2) | collective-permute-done | bytes 262176 | tf_op jit(solution)/shard_map/ppermute | solution.py:29
  20.6 0.0 copy-done
  20.6 0.7 %project.1 = (bf16[128,512]{1,0:T(8,128)(2,1)S(1)}, f32[128,512]{1,0:T(8,128)S(1)}, bf16[128,1024]{1,0:T(8,128)(2,1)S(1)}) custom-call(bf16[128,512]{1,0:T(8,128)(2,1)S(1)} %get-tuple-element.38.q, bf16[256,512]{1,0:T(8,128)(2,1)S(1)} %collective-permute-done.2.relay, f32[128,512]{1,0:T(8,128)S(1)} %get-tuple-element.39.sums, ...), custom_call_target="tpu_custom_call" | custom-call | bytes 3690000 | tf_op jit(solution)/shard_map/project/pallas_call | solution.py:76
  21.4 0.0 collective-permute-done.5.seen_a.taps_other
  21.4 0.0 collective-permute-done.6.seen_b.q_second.refs_3_
  21.4 0.1 collective-permute-start.7
  21.5 0.3 project_own.1.keep
  21.8 1.2 %collective-permute-done.7.core = bf16[128,1024]{1,0:T(8,128)(2,1)S(1)} collective-permute-done((bf16[128,1024]{1,0:T(8,128)(2,1)S(1)}, bf16[128,1024]{1,0:T(8,128)(2,1)S(1)}, u32[]{:S(2)}, u32[]{:S(2)}) %collective-permute-start.7) | collective-permute-done | bytes 262176 | tf_op jit(solution)/shard_map/ppermute | solution.py:29
  23.0 0.1 join.1
  23.1 0.6 %collective-permute-start.11 = (bf16[128,1024]{1,0:T(8,128)(2,1)S(1)}, bf16[128,1024]{1,0:T(8,128)(2,1)S(1)}, u32[]{:S(2)}, u32[]{:S(2)}) collective-permute-start(bf16[128,1024]{1,0:T(8,128)(2,1)S(1)} %get-tuple-element.50.chip), channel_id=1, source_target_pairs={{0,2},{1,3},{2,0},{3,1},{4,6},{5,7},{6,4},{7,5},{8,10},{9,11},{10,... | collective-permute-start | bytes 786440 | tf_op jit(solution)/shard_map/ppermute | solution.py:29
  23.7 2.5 %collective-permute-start.8 = (bf16[48,1024]{1,0:T(8,128)(2,1)S(1)}, bf16[48,1024]{1,0:T(8,128)(2,1)S(1)}, u32[]{:S(2)}, u32[]{:S(2)}) collective-permute-start(bf16[48,1024]{1,0:T(8,128)(2,1)S(1)} %get-tuple-element.47), channel_id=1, source_target_pairs={{0,4},{4,0},{8,12},{12,8},{16,20},{20,16},{24,28},{28,24},{1,5},{5... | collective-permute-start | bytes 294920 | tf_op jit(solution)/shard_map/ppermute | solution.py:29
  26.2 0.0 collective-permute-start.9
  26.2 1.5 %collective-permute-start.12 = (bf16[128,512]{1,0:T(8,128)(2,1)S(1)}, bf16[128,512]{1,0:T(8,128)(2,1)S(1)}, u32[]{:S(2)}, u32[]{:S(2)}) collective-permute-start(bf16[128,512]{1,0:T(8,128)(2,1)S(1)} %get-tuple-element.46.q.refs_0_), channel_id=1, source_target_pairs={{0,8},{8,16},{16,24},{24,28},{28,20},{20,12},{12,4},{4,0},{1,9},{9... | collective-permute-start | bytes 393224 | tf_op jit(solution)/shard_map/ppermute | solution.py:40
  27.7 0.0 collective-permute-start.13
  27.7 2.7 %collective-permute-done.8.rim_near = bf16[48,1024]{1,0:T(8,128)(2,1)S(1)} collective-permute-done((bf16[48,1024]{1,0:T(8,128)(2,1)S(1)}, bf16[48,1024]{1,0:T(8,128)(2,1)S(1)}, u32[]{:S(2)}, u32[]{:S(2)}) %collective-permute-start.8) | collective-permute-done | bytes 98336 | tf_op jit(solution)/shard_map/ppermute | solution.py:29
  30.4 0.0 collective-permute-done.9.rim_far
  30.4 0.6 %collective-permute-start.10 = (bf16[64,1024]{1,0:T(8,128)(2,1)S(1)}, bf16[64,1024]{1,0:T(8,128)(2,1)S(1)}, u32[]{:S(2)}, u32[]{:S(2)}) collective-permute-start(bf16[64,1024]{1,0:T(8,128)(2,1)S(1)} %get-tuple-element.49.ends), channel_id=1, source_target_pairs={{0,2},{1,3},{2,0},{3,1},{4,6},{5,7},{6,4},{7,5},{8,10},{9,11},{10,... | collective-permute-start | bytes 393224 | tf_op jit(solution)/shard_map/ppermute | solution.py:29
  31.1 2.5 %collective-permute-start.14 = (bf16[128,512]{1,0:T(8,128)(2,1)S(1)}, bf16[128,512]{1,0:T(8,128)(2,1)S(1)}, u32[]{:S(2)}, u32[]{:S(2)}) collective-permute-start(bf16[128,512]{1,0:T(8,128)(2,1)S(1)} %get-tuple-element.56), channel_id=1, source_target_pairs={{0,4},{4,0},{8,12},{12,8},{16,20},{20,16},{24,28},{28,24},{1,5},{5... | collective-permute-start | bytes 393224 | tf_op jit(solution)/shard_map/ppermute | solution.py:29
  33.5 0.0 collective-permute-done.12.seen.refs_2_
  33.5 0.0 collective-permute-done.11.across
  33.5 2.8 %conv_inner.1 = (bf16[128,512]{1,0:T(8,128)(2,1)S(1)}, f32[32,512]{1,0:T(8,128)S(1)}, f32[64,1024]{1,0:T(8,128)S(1)}, f32[128,1024]{1,0:T(8,128)S(1)}) custom-call(bf16[128,1024]{1,0:T(8,128)(2,1)S(1)} %get-tuple-element.50.chip, bf16[128,1024]{1,0:T(8,128)(2,1)S(1)} %collective-permute-done.11.across, bf16[128,512]{1,0:T(8,128)(2,1)S(1)} %get-tuple-element.45.cot, ...), custom_call_target="tpu_custom_call" | custom-call | bytes 11439000 | tf_op jit(solution)/shard_map/conv_inner/pallas_call | solution.py:76
  36.4 0.0 collective-permute-done.13.seen.refs_1_
  36.4 0.0 collective-permute-done.10.ends_across
  36.4 1.1 %conv_edge.1 = (bf16[128,512]{1,0:T(8,128)(2,1)S(1)}, bf16[128,1024]{1,0:T(8,128)(2,1)S(1)}) custom-call(bf16[64,1024]{1,0:T(8,128)(2,1)S(1)} %get-tuple-element.49.ends, bf16[64,1024]{1,0:T(8,128)(2,1)S(1)} %collective-permute-done.10.ends_across, bf16[48,1024]{1,0:T(8,128)(2,1)S(1)} %collective-permute-done.8.rim_near, ...), custom_call_target="tpu_custom_call" | custom-call | bytes 5166000 | tf_op jit(solution)/shard_map/conv_edge/pallas_call | solution.py:76
  37.5 0.0 collective-permute-done.14.refs_0_.refs_4_.query
  37.6 0.1 collective-permute-start.15
  37.6 0.5 upstream_own.1
  38.1 1.0 %collective-permute-done.15.core = bf16[128,1024]{1,0:T(8,128)(2,1)S(1)} collective-permute-done((bf16[128,1024]{1,0:T(8,128)(2,1)S(1)}, bf16[128,1024]{1,0:T(8,128)(2,1)S(1)}, u32[]{:S(2)}, u32[]{:S(2)}) %collective-permute-start.15) | collective-permute-done | bytes 262176 | tf_op jit(solution)/shard_map/ppermute | solution.py:29
  39.2 0.7 %upstream.1 = (bf16[144,512]{1,0:T(8,128)(2,1)S(1)}, f32[128,512]{1,0:T(8,128)S(1)}) custom-call(bf16[128,1024]{1,0:T(8,128)(2,1)S(1)} %collective-permute-done.15.core, bf16[512,2048]{1,0:T(8,128)(2,1)S(1)} %copy-done, bf16[128,512]{1,0:T(8,128)(2,1)S(1)} %get-tuple-element.42.att, f32[128,512]{1,0:T(8,128)S(1)} %get-tuple-element.58.partial, ...), custom_call_target="tpu_custom_call" | custom-call | bytes 2214000 | tf_op jit(solution)/shard_map/upstream/pallas_call | solution.py:76
  39.8 0.2 collective-permute-start.17
  40.0 2.0 %collective-permute-start.18 = (bf16[144,512]{1,0:T(8,128)(2,1)S(1)}, bf16[144,512]{1,0:T(8,128)(2,1)S(1)}, u32[]{:S(2)}, u32[]{:S(2)}) collective-permute-start(bf16[144,512]{1,0:T(8,128)(2,1)S(1)} %get-tuple-element.60.message.refs_5_), channel_id=1, source_target_pairs={{0,8},{8,16},{16,24},{24,28},{28,20},{20,12},{12,4},{4,0},{1,9},{9... | collective-permute-start | bytes 442376 | tf_op jit(solution)/shard_map/ppermute | solution.py:40
  42.0 0.0 collective-permute-start.19
  42.1 0.0 collective-permute-start.16
  42.1 1.5 %query_grad.1 = (bf16[128,512]{1,0:T(8,128)(2,1)}, bf16[128,512]{1,0:T(8,128)(2,1)}, bf16[128,512]{1,0:T(8,128)(2,1)}) custom-call(bf16[128,512]{1,0:T(8,128)(2,1)S(1)} %get-tuple-element.46.q.refs_0_, bf16[256,512]{1,0:T(8,128)(2,1)S(1)} %pad_add_fusion.1.own, bf16[256,512]{1,0:T(8,128)(2,1)S(1)} %collective-permute-done.3.near, ...), custom_call_target="tpu_custom_call" | custom-call | bytes 6642000 | tf_op jit(solution)/shard_map/query_grad/pallas_call | solution.py:76
  43.6 0.0 collective-permute-done.17.refs_6_
  43.6 2.5 %collective-permute-done.18.refs_7_ = bf16[144,512]{1,0:T(8,128)(2,1)S(1)} collective-permute-done((bf16[144,512]{1,0:T(8,128)(2,1)S(1)}, bf16[144,512]{1,0:T(8,128)(2,1)S(1)}, u32[]{:S(2)}, u32[]{:S(2)}) %collective-permute-start.18) | collective-permute-done | bytes 147488 | tf_op jit(solution)/shard_map/ppermute | solution.py:40
  46.2 2.7 %collective-permute-done.19.refs_8_ = bf16[144,512]{1,0:T(8,128)(2,1)S(1)} collective-permute-done((bf16[144,512]{1,0:T(8,128)(2,1)S(1)}, bf16[144,512]{1,0:T(8,128)(2,1)S(1)}, u32[]{:S(2)}, u32[]{:S(2)}) %collective-permute-start.19) | collective-permute-done | bytes 147488 | tf_op jit(solution)/shard_map/ppermute | solution.py:40
  48.8 0.9 %key_part.1 = (f32[128,512]{1,0:T(8,128)S(1)}, f32[128,512]{1,0:T(8,128)S(1)}, f32[128,512]{1,0:T(8,128)S(1)}) custom-call(bf16[256,512]{1,0:T(8,128)(2,1)S(1)} %pad_add_fusion.1.own, bf16[128,512]{1,0:T(8,128)(2,1)S(1)} %get-tuple-element.46.q.refs_0_, bf16[128,512]{1,0:T(8,128)(2,1)S(1)} %collective-permute-done.13.seen.refs_1_, ...), custom_call_target="tpu_custom_call" | custom-call | bytes 5535000 | tf_op jit(solution)/shard_map/key_part/pallas_call | solution.py:76
  49.7 0.0 collective-permute-done.16.message
  49.7 1.0 %key_grad.1 = (bf16[128,512]{1,0:T(8,128)(2,1)}, bf16[128,512]{1,0:T(8,128)(2,1)}) custom-call(bf16[256,512]{1,0:T(8,128)(2,1)S(1)} %pad_add_fusion.1.own, bf16[128,512]{1,0:T(8,128)(2,1)S(1)} %collective-permute-done.14.refs_0_.refs_4_.query, bf16[144,512]{1,0:T(8,128)(2,1)S(1)} %collective-permute-done.16.message, f32[128,512]{1,0:T(8,128)S(1)} %get-tuple-element.66.late, ...), custom_call_target="tpu_custom_call" | custom-call | bytes 3690000 | tf_op jit(solution)/shard_map/key_grad/pallas_call | solution.py:76
  (5 shorter events, 0.1 us)
Async XLA Ops:
  0.6 12.7 %copy-start.1 = (f32[31,512]{1,0:T(8,128)S(1)}, f32[31,512]{1,0:T(8,128)}, u32[]{:S(2)}) copy-start(f32[31,512]{1,0:T(8,128)} %taps.3) | copy-start | bytes 190468
  0.6 20.0 %copy-start = (bf16[512,2048]{1,0:T(8,128)(2,1)S(1)}, bf16[512,2048]{1,0:T(8,128)(2,1)}, u32[]{:S(2)}) copy-start(bf16[512,2048]{1,0:T(8,128)(2,1)} %weight.7) | copy-start | bytes 6291460
  1.8 9.4 %collective-permute-start = (bf16[256,512]{1,0:T(8,128)(2,1)S(1)}, bf16[256,512]{1,0:T(8,128)(2,1)S(1)}, u32[]{:S(2)}, u32[]{:S(2)}) collective-permute-start(bf16[256,512]{1,0:T(8,128)(2,1)S(1)} %pad_add_fusion.1.own), channel_id=1, source_target_pairs={{8,0},{16,8},{24,16},{28,24},{20,28},{12,20},{4,12},{0,4},{9,1},{1... | collective-permute-start | bytes 786440 | tf_op jit(solution)/shard_map/ppermute | solution.py:40
  4.8 5.7 %collective-permute-start.1 = (bf16[128,512]{1,0:T(8,128)(2,1)}, bf16[128,512]{1,0:T(8,128)(2,1)S(1)}, u32[]{:S(2)}, u32[]{:S(2)}) collective-permute-start(bf16[128,512]{1,0:T(8,128)(2,1)} %param.13), channel_id=1, source_target_pairs={{0,2},{1,3},{2,0},{3,1},{4,6},{5,7},{6,4},{7,5},{8,10},{9,11},{10,... | collective-permute-start | bytes 393224 | tf_op jit(solution)/shard_map/ppermute | solution.py:29
  6.3 8.8 %collective-permute-start.3 = (bf16[256,512]{1,0:T(8,128)(2,1)S(1)}, bf16[256,512]{1,0:T(8,128)(2,1)S(1)}, u32[]{:S(2)}, u32[]{:S(2)}) collective-permute-start(bf16[256,512]{1,0:T(8,128)(2,1)S(1)} %pad_add_fusion.1.own), channel_id=1, source_target_pairs={{0,1},{1,0},{2,3},{3,2},{4,5},{5,4},{6,7},{7,6},{8,12},{9,13},{10,... | collective-permute-start | bytes 786440 | tf_op jit(solution)/shard_map/ppermute | solution.py:51
  6.3 9.1 %collective-permute-start.4 = (bf16[256,512]{1,0:T(8,128)(2,1)S(1)}, bf16[256,512]{1,0:T(8,128)(2,1)S(1)}, u32[]{:S(2)}, u32[]{:S(2)}) collective-permute-start(bf16[256,512]{1,0:T(8,128)(2,1)S(1)} %pad_add_fusion.1.own), channel_id=1, source_target_pairs={{0,8},{8,16},{16,24},{24,28},{28,20},{20,12},{12,4},{4,0},{1,9},{9... | collective-permute-start | bytes 786440 | tf_op jit(solution)/shard_map/ppermute | solution.py:40
  11.2 9.4 %collective-permute-start.2 = (bf16[256,512]{1,0:T(8,128)(2,1)S(1)}, bf16[256,512]{1,0:T(8,128)(2,1)S(1)}, u32[]{:S(2)}, u32[]{:S(2)}) collective-permute-start(bf16[256,512]{1,0:T(8,128)(2,1)S(1)} %turn.1.seen.second), channel_id=1, source_target_pairs={{0,4},{4,0},{8,12},{12,8},{16,20},{20,16},{24,28},{28,24},{1,5},{5... | collective-permute-start | bytes 786440 | tf_op jit(solution)/shard_map/ppermute | solution.py:29
  12.9 8.4 %collective-permute-start.6 = (bf16[128,512]{1,0:T(8,128)(2,1)S(1)}, bf16[128,512]{1,0:T(8,128)(2,1)S(1)}, u32[]{:S(2)}, u32[]{:S(2)}) collective-permute-start(bf16[128,512]{1,0:T(8,128)(2,1)S(1)} %get-tuple-element.38.q), channel_id=1, source_target_pairs={{8,0},{16,8},{24,16},{28,24},{20,28},{12,20},{4,12},{0,4},{9,1},{1... | collective-permute-start | bytes 393224 | tf_op jit(solution)/shard_map/ppermute | solution.py:40
  13.4 8.0 %collective-permute-start.5 = (f32[31,512]{1,0:T(8,128)S(1)}, f32[31,512]{1,0:T(8,128)S(1)}, u32[]{:S(2)}, u32[]{:S(2)}) collective-permute-start(f32[31,512]{1,0:T(8,128)S(1)} %copy-done.1), channel_id=1, source_target_pairs={{0,2},{1,3},{2,0},{3,1},{4,6},{5,7},{6,4},{7,5},{8,10},{9,11},{10,... | collective-permute-start | bytes 190472 | tf_op jit(solution)/shard_map/ppermute | solution.py:29
  21.4 1.6 %collective-permute-start.7 = (bf16[128,1024]{1,0:T(8,128)(2,1)S(1)}, bf16[128,1024]{1,0:T(8,128)(2,1)S(1)}, u32[]{:S(2)}, u32[]{:S(2)}) collective-permute-start(bf16[128,1024]{1,0:T(8,128)(2,1)S(1)} %pass.1), channel_id=1, source_target_pairs={{0,1},{1,0},{2,3},{3,2},{4,5},{5,4},{6,7},{7,6},{8,9},{9,8},{10,11... | collective-permute-start | bytes 786440 | tf_op jit(solution)/shard_map/ppermute | solution.py:29
  23.1 10.4 %collective-permute-start.11 = (bf16[128,1024]{1,0:T(8,128)(2,1)S(1)}, bf16[128,1024]{1,0:T(8,128)(2,1)S(1)}, u32[]{:S(2)}, u32[]{:S(2)}) collective-permute-start(bf16[128,1024]{1,0:T(8,128)(2,1)S(1)} %get-tuple-element.50.chip), channel_id=1, source_target_pairs={{0,2},{1,3},{2,0},{3,1},{4,6},{5,7},{6,4},{7,5},{8,10},{9,11},{10,... | collective-permute-start | bytes 786440 | tf_op jit(solution)/shard_map/ppermute | solution.py:29
  23.7 6.7 %collective-permute-start.8 = (bf16[48,1024]{1,0:T(8,128)(2,1)S(1)}, bf16[48,1024]{1,0:T(8,128)(2,1)S(1)}, u32[]{:S(2)}, u32[]{:S(2)}) collective-permute-start(bf16[48,1024]{1,0:T(8,128)(2,1)S(1)} %get-tuple-element.47), channel_id=1, source_target_pairs={{0,4},{4,0},{8,12},{12,8},{16,20},{20,16},{24,28},{28,24},{1,5},{5... | collective-permute-start | bytes 294920 | tf_op jit(solution)/shard_map/ppermute | solution.py:29
  26.2 4.2 %collective-permute-start.9 = (bf16[48,1024]{1,0:T(8,128)(2,1)S(1)}, bf16[48,1024]{1,0:T(8,128)(2,1)S(1)}, u32[]{:S(2)}, u32[]{:S(2)}) collective-permute-start(bf16[48,1024]{1,0:T(8,128)(2,1)S(1)} %get-tuple-element.48), channel_id=1, source_target_pairs={{0,1},{1,0},{2,3},{3,2},{4,8},{5,9},{6,10},{7,11},{8,4},{9,5},{10,... | collective-permute-start | bytes 294920 | tf_op jit(solution)/shard_map/ppermute | solution.py:51
  26.2 7.3 %collective-permute-start.12 = (bf16[128,512]{1,0:T(8,128)(2,1)S(1)}, bf16[128,512]{1,0:T(8,128)(2,1)S(1)}, u32[]{:S(2)}, u32[]{:S(2)}) collective-permute-start(bf16[128,512]{1,0:T(8,128)(2,1)S(1)} %get-tuple-element.46.q.refs_0_), channel_id=1, source_target_pairs={{0,8},{8,16},{16,24},{24,28},{28,20},{20,12},{12,4},{4,0},{1,9},{9... | collective-permute-start | bytes 393224 | tf_op jit(solution)/shard_map/ppermute | solution.py:40
  27.7 8.7 %collective-permute-start.13 = (bf16[128,512]{1,0:T(8,128)(2,1)S(1)}, bf16[128,512]{1,0:T(8,128)(2,1)S(1)}, u32[]{:S(2)}, u32[]{:S(2)}) collective-permute-start(bf16[128,512]{1,0:T(8,128)(2,1)S(1)} %get-tuple-element.46.q.refs_0_), channel_id=1, source_target_pairs={{0,1},{1,0},{2,3},{3,2},{4,5},{5,4},{6,7},{7,6},{8,12},{9,13},{10,... | collective-permute-start | bytes 393224 | tf_op jit(solution)/shard_map/ppermute | solution.py:51
  30.4 6.0 %collective-permute-start.10 = (bf16[64,1024]{1,0:T(8,128)(2,1)S(1)}, bf16[64,1024]{1,0:T(8,128)(2,1)S(1)}, u32[]{:S(2)}, u32[]{:S(2)}) collective-permute-start(bf16[64,1024]{1,0:T(8,128)(2,1)S(1)} %get-tuple-element.49.ends), channel_id=1, source_target_pairs={{0,2},{1,3},{2,0},{3,1},{4,6},{5,7},{6,4},{7,5},{8,10},{9,11},{10,... | collective-permute-start | bytes 393224 | tf_op jit(solution)/shard_map/ppermute | solution.py:29
  31.1 6.5 %collective-permute-start.14 = (bf16[128,512]{1,0:T(8,128)(2,1)S(1)}, bf16[128,512]{1,0:T(8,128)(2,1)S(1)}, u32[]{:S(2)}, u32[]{:S(2)}) collective-permute-start(bf16[128,512]{1,0:T(8,128)(2,1)S(1)} %get-tuple-element.56), channel_id=1, source_target_pairs={{0,4},{4,0},{8,12},{12,8},{16,20},{20,16},{24,28},{28,24},{1,5},{5... | collective-permute-start | bytes 393224 | tf_op jit(solution)/shard_map/ppermute | solution.py:29
  37.6 1.6 %collective-permute-start.15 = (bf16[128,1024]{1,0:T(8,128)(2,1)S(1)}, bf16[128,1024]{1,0:T(8,128)(2,1)S(1)}, u32[]{:S(2)}, u32[]{:S(2)}) collective-permute-start(bf16[128,1024]{1,0:T(8,128)(2,1)S(1)} %hand.1.own.grad_here), channel_id=1, source_target_pairs={{0,1},{1,0},{2,3},{3,2},{4,5},{5,4},{6,7},{7,6},{8,9},{9,8},{10,11... | collective-permute-start | bytes 786440 | tf_op jit(solution)/shard_map/ppermute | solution.py:29
  39.8 3.8 %collective-permute-start.17 = (bf16[144,512]{1,0:T(8,128)(2,1)S(1)}, bf16[144,512]{1,0:T(8,128)(2,1)S(1)}, u32[]{:S(2)}, u32[]{:S(2)}) collective-permute-start(bf16[144,512]{1,0:T(8,128)(2,1)S(1)} %get-tuple-element.60.message.refs_5_), channel_id=1, source_target_pairs={{0,1},{1,0},{2,3},{3,2},{4,5},{5,4},{6,7},{7,6},{8,12},{9,13},{10,... | collective-permute-start | bytes 442376 | tf_op jit(solution)/shard_map/ppermute | solution.py:51
  40.0 6.1 %collective-permute-start.18 = (bf16[144,512]{1,0:T(8,128)(2,1)S(1)}, bf16[144,512]{1,0:T(8,128)(2,1)S(1)}, u32[]{:S(2)}, u32[]{:S(2)}) collective-permute-start(bf16[144,512]{1,0:T(8,128)(2,1)S(1)} %get-tuple-element.60.message.refs_5_), channel_id=1, source_target_pairs={{0,8},{8,16},{16,24},{24,28},{28,20},{20,12},{12,4},{4,0},{1,9},{9... | collective-permute-start | bytes 442376 | tf_op jit(solution)/shard_map/ppermute | solution.py:40
  42.0 6.8 %collective-permute-start.19 = (bf16[144,512]{1,0:T(8,128)(2,1)S(1)}, bf16[144,512]{1,0:T(8,128)(2,1)S(1)}, u32[]{:S(2)}, u32[]{:S(2)}) collective-permute-start(bf16[144,512]{1,0:T(8,128)(2,1)S(1)} %get-tuple-element.60.message.refs_5_), channel_id=1, source_target_pairs={{8,0},{16,8},{24,16},{28,24},{20,28},{12,20},{4,12},{0,4},{9,1},{1... | collective-permute-start | bytes 442376 | tf_op jit(solution)/shard_map/ppermute | solution.py:40
  42.1 7.6 %collective-permute-start.16 = (bf16[144,512]{1,0:T(8,128)(2,1)S(1)}, bf16[144,512]{1,0:T(8,128)(2,1)S(1)}, u32[]{:S(2)}, u32[]{:S(2)}) collective-permute-start(bf16[144,512]{1,0:T(8,128)(2,1)S(1)} %get-tuple-element.60.message.refs_5_), channel_id=1, source_target_pairs={{0,1},{1,0},{2,3},{3,2},{4,8},{5,9},{6,10},{7,11},{8,4},{9,5},{10,... | collective-permute-start | bytes 442376 | tf_op jit(solution)/shard_map/ppermute | solution.py:51

commit v20 on v15

--- a/solution.py
+++ b/solution.py
@@ -194,7 +194,7 @@
         totals[:, c] = s[:, HDIM:]
 
 
-def project_body(scale, q, relay, sums, tops, totals, weight, att, lse, send, keep):
+def project_body(scale, q, relay, sums, tops, totals, weight, att, lse, send):
     frames, width = q.shape
     heads = columns(width)
     bias = bias_of(far_there())
@@ -208,13 +208,16 @@
     summed = [sums[:, c] * k + s[:, 0:HDIM] for c, k, s in zip(heads, shrink, late)]
     attended = jnp.concatenate([(s * (1.0 / t)).astype(BF16) for s, t in zip(summed, total)], axis=1)
     sent = [dot_nn(attended, weight_columns(weight, flip)).astype(BF16) for flip in (1, 3)]
-    kept = [dot_nn(attended, weight_columns(weight, flip)).astype(BF16) for flip in (0, 2)]
     logs = [t + jnp.log(n) for t, n in zip(top, total)]
     att[...] = attended
     send[...] = jnp.concatenate(sent, axis=1)
-    keep[...] = jnp.concatenate(kept, axis=1)
     for c, part in zip(heads, logs):
         lse[:, c] = part
+
+
+def project_own_body(att, weight, keep):
+    kept = [dot_nn(att[...], weight_columns(weight, flip)).astype(BF16) for flip in (0, 2)]
+    keep[...] = jnp.concatenate(kept, axis=1)
 
 
 def pass_body(send, q_second, seen_a, seen_b, send_copy, second_copy):
@@ -515,15 +518,16 @@
         (query, kv, near, first, second),
         1.0, "forward",
     )
-    att, lse, send, keep = kernel_call(
+    att, lse, send = kernel_call(
         functools.partial(project_body, scale),
-        (tile, tile32, both, both),
+        (tile, tile32, both),
         (query, relay, sums, tops, totals, out_weight),
         1.0, "project",
     )
 
     send, q_second = kernel_call(pass_body, (both, tile), (send, q_second, cot_other, taps_other), 0.1, "pass", 2)
     core = pair_swap(send, "mp", 1)
+    (keep,) = kernel_call(project_own_body, (both,), (att, out_weight), 0.4, "project_own")
     chip, rim_up, rim_down, q_own = kernel_call(
         join_body,
         (both, rim, rim, tile),

time: 50.6 us -> 50.5 us (level)
    pallas_call x15 -> x16, Pallas kernels: 10.2 us -> 10.3 us  [kernel_call(): pl.pallas_call(body, out_shape=outs, in_specs=[VMEM] * (len(args) - unrea...]
where the time goes in v20:
time: 50.5 us; the launch traced here: 50.3 us
  starting transfers between devices  21.3 us (42%)
  waiting for transfers between devices  15.6 us (31%)
  Pallas kernels  10.3 us (20%)
  other arithmetic  2.19 us (4%)
  between operations  0.84 us (2%)
    ppermute x9, starting transfers between devices, pair_swap(): lax.ppermute(block, axis, [(i, i ^ bit) for i in range(lax.axis_size(axis...  10.8 us
    pallas_call x16, Pallas kernels, kernel_call(): pl.pallas_call(body, out_shape=outs, in_specs=[VMEM] * (len(args) - unrea...  10.3 us
    ppermute x6, starting transfers between devices, ring(): return lax.ppermute(block, 'ctx', ring_routes(lax.axis_size('ctx'))[way])  10.2 us
    ppermute x9, waiting for transfers between devices, pair_swap(): lax.ppermute(block, axis, [(i, i ^ bit) for i in range(lax.axis_size(axis...  8.05 us
    ppermute x6, waiting for transfers between devices, ring(): return lax.ppermute(block, 'ctx', ring_routes(lax.axis_size('ctx'))[way])  7.57 us
    add x1, other arithmetic, per_device(): lax.pad(key_rows, zero, ((0, frames, 0), (0, 0, 0)))  1.14 us
    add x1, other arithmetic, per_device(): sum((lax.pad(rows, zero, ((k * frames, (2 - k) * frames, 0), (0, 0, 0)))...  1.06 us
  transfers between devices with their start and end apart: 20, of which 8 were waited for; matrix products, arithmetic and copies ran while one was open for 2% of the time, Pallas kernels for 17%

profile of v20, /device:TPU:0, one launch (start us, length us, event | category | flops | bytes accessed | tf_op | source)
XLA Modules:
  0.0 50.3 jit_solution(14997326659653779674)
XLA Ops:
  0.6 0.0 copy-start.2
  0.6 0.0 copy-start.1
  0.7 0.0 copy-start
  0.7 1.1 %pad_add_fusion.1.own = bf16[256,512]{1,0:T(8,128)(2,1)S(1)} fusion(bf16[128,512]{1,0:T(8,128)(2,1)} %param.9, bf16[128,512]{1,0:T(8,128)(2,1)} %param.8), kind=kLoop, calls=%fused_computation.1 | loop fusion | flops 524288 | bytes 524288 | tf_op jit(solution)/shard_map/add | solution.py:496
  1.8 3.0 %collective-permute-start = (bf16[256,512]{1,0:T(8,128)(2,1)S(1)}, bf16[256,512]{1,0:T(8,128)(2,1)S(1)}, u32[]{:S(2)}, u32[]{:S(2)}) collective-permute-start(bf16[256,512]{1,0:T(8,128)(2,1)S(1)} %pad_add_fusion.1.own), channel_id=1, source_target_pairs={{8,0},{16,8},{24,16},{28,24},{20,28},{12,20},{4,12},{0,4},{9,1},{1... | collective-permute-start | bytes 786440 | tf_op jit(solution)/shard_map/ppermute | solution.py:40
  4.8 0.0 collective-permute-start.2
  4.8 3.2 %collective-permute-start.3 = (bf16[256,512]{1,0:T(8,128)(2,1)S(1)}, bf16[256,512]{1,0:T(8,128)(2,1)S(1)}, u32[]{:S(2)}, u32[]{:S(2)}) collective-permute-start(bf16[256,512]{1,0:T(8,128)(2,1)S(1)} %pad_add_fusion.1.own), channel_id=1, source_target_pairs={{0,8},{8,16},{16,24},{24,28},{28,20},{20,12},{12,4},{4,0},{1,9},{9... | collective-permute-start | bytes 786440 | tf_op jit(solution)/shard_map/ppermute | solution.py:40
  7.9 1.1 %pad_add_fusion.seen.joined = bf16[384,512]{1,0:T(8,128)(2,1)S(1)} fusion(bf16[128,512]{1,0:T(8,128)(2,1)} %param.13, bf16[128,512]{1,0:T(8,128)(2,1)} %param.10, bf16[128,512]{1,0:T(8,128)(2,1)} %param.7), kind=kLoop, calls=%fused_computation | loop fusion | flops 1179648 | bytes 786432 | tf_op jit(solution)/shard_map/add | solution.py:499
  9.0 2.2 %collective-permute-done.block = bf16[256,512]{1,0:T(8,128)(2,1)S(1)} collective-permute-done((bf16[256,512]{1,0:T(8,128)(2,1)S(1)}, bf16[256,512]{1,0:T(8,128)(2,1)S(1)}, u32[]{:S(2)}, u32[]{:S(2)}) %collective-permute-start) | collective-permute-done | bytes 262176 | tf_op jit(solution)/shard_map/ppermute | solution.py:40
  11.2 1.7 %collective-permute-start.1 = (bf16[256,512]{1,0:T(8,128)(2,1)S(1)}, bf16[256,512]{1,0:T(8,128)(2,1)S(1)}, u32[]{:S(2)}, u32[]{:S(2)}) collective-permute-start(bf16[256,512]{1,0:T(8,128)(2,1)S(1)} %turn.1.seen.second), channel_id=1, source_target_pairs={{0,4},{4,0},{8,12},{12,8},{16,20},{20,16},{24,28},{28,24},{1,5},{5... | collective-permute-start | bytes 786440 | tf_op jit(solution)/shard_map/ppermute | solution.py:29
  12.9 0.0 copy-done.2
  12.9 1.5 %collective-permute-start.5 = (bf16[128,512]{1,0:T(8,128)(2,1)S(1)}, bf16[128,512]{1,0:T(8,128)(2,1)S(1)}, u32[]{:S(2)}, u32[]{:S(2)}) collective-permute-start(bf16[128,512]{1,0:T(8,128)(2,1)S(1)} %copy-done.2), channel_id=1, source_target_pairs={{0,2},{1,3},{2,0},{3,1},{4,6},{5,7},{6,4},{7,5},{8,10},{9,11},{10,... | collective-permute-start | bytes 393224 | tf_op jit(solution)/shard_map/ppermute | solution.py:29
  14.5 0.6 %collective-permute-start.4 = (bf16[128,512]{1,0:T(8,128)(2,1)S(1)}, bf16[128,512]{1,0:T(8,128)(2,1)S(1)}, u32[]{:S(2)}, u32[]{:S(2)}) collective-permute-start(bf16[128,512]{1,0:T(8,128)(2,1)S(1)} %get-tuple-element.40.q), channel_id=1, source_target_pairs={{8,0},{16,8},{24,16},{28,24},{20,28},{12,20},{4,12},{0,4},{9,1},{1... | collective-permute-start | bytes 393224 | tf_op jit(solution)/shard_map/ppermute | solution.py:40
  15.1 0.0 collective-permute-done.2.near
  15.1 0.0 copy-done.1
  15.1 0.3 collective-permute-start.6
  15.4 0.0 collective-permute-done.3.first
  15.4 0.6 %forward.1 = (f32[128,512]{1,0:T(8,128)S(1)}, f32[128,512]{1,0:T(8,128)S(1)}, f32[128,512]{1,0:T(8,128)S(1)}) custom-call(bf16[128,512]{1,0:T(8,128)(2,1)S(1)} %get-tuple-element.40.q, bf16[256,512]{1,0:T(8,128)(2,1)S(1)} %pad_add_fusion.1.own, bf16[256,512]{1,0:T(8,128)(2,1)S(1)} %collective-permute-done.2.near, ...), custom_call_target="tpu_custom_call" | custom-call | bytes 3690000 | tf_op jit(solution)/shard_map/forward/pallas_call | solution.py:76
  16.0 3.1 %collective-permute-done.1.relay = bf16[256,512]{1,0:T(8,128)(2,1)S(1)} collective-permute-done((bf16[256,512]{1,0:T(8,128)(2,1)S(1)}, bf16[256,512]{1,0:T(8,128)(2,1)S(1)}, u32[]{:S(2)}, u32[]{:S(2)}) %collective-permute-start.1) | collective-permute-done | bytes 262176 | tf_op jit(solution)/shard_map/ppermute | solution.py:29
  19.1 0.0 copy-done
  19.1 0.7 %project.1 = (bf16[128,512]{1,0:T(8,128)(2,1)S(1)}, f32[128,512]{1,0:T(8,128)S(1)}, bf16[128,1024]{1,0:T(8,128)(2,1)S(1)}) custom-call(bf16[128,512]{1,0:T(8,128)(2,1)S(1)} %get-tuple-element.40.q, bf16[256,512]{1,0:T(8,128)(2,1)S(1)} %collective-permute-done.1.relay, f32[128,512]{1,0:T(8,128)S(1)} %get-tuple-element.41.sums, ...), custom_call_target="tpu_custom_call" | custom-call | bytes 3690000 | tf_op jit(solution)/shard_map/project/pallas_call | solution.py:76
  19.9 0.0 collective-permute-done.6.seen_b.taps_other
  19.9 0.0 collective-permute-done.5.seen_a.cot_other
  19.9 0.6 %collective-permute-done.4.q_second = bf16[128,512]{1,0:T(8,128)(2,1)S(1)} collective-permute-done((bf16[128,512]{1,0:T(8,128)(2,1)S(1)}, bf16[128,512]{1,0:T(8,128)(2,1)S(1)}, u32[]{:S(2)}, u32[]{:S(2)}) %collective-permute-start.4) | collective-permute-done | bytes 131104 | tf_op jit(solution)/shard_map/ppermute | solution.py:40
  20.5 0.1 collective-permute-start.7
  20.5 0.3 project_own.1.keep
  20.9 1.2 %collective-permute-done.7.core = bf16[128,1024]{1,0:T(8,128)(2,1)S(1)} collective-permute-done((bf16[128,1024]{1,0:T(8,128)(2,1)S(1)}, bf16[128,1024]{1,0:T(8,128)(2,1)S(1)}, u32[]{:S(2)}, u32[]{:S(2)}) %collective-permute-start.7) | collective-permute-done | bytes 262176 | tf_op jit(solution)/shard_map/ppermute | solution.py:29
  22.1 0.1 join.1
  22.2 1.6 %collective-permute-start.11 = (bf16[128,1024]{1,0:T(8,128)(2,1)S(1)}, bf16[128,1024]{1,0:T(8,128)(2,1)S(1)}, u32[]{:S(2)}, u32[]{:S(2)}) collective-permute-start(bf16[128,1024]{1,0:T(8,128)(2,1)S(1)} %get-tuple-element.54.chip), channel_id=1, source_target_pairs={{0,2},{1,3},{2,0},{3,1},{4,6},{5,7},{6,4},{7,5},{8,10},{9,11},{10,... | collective-permute-start | bytes 786440 | tf_op jit(solution)/shard_map/ppermute | solution.py:29
  23.8 2.5 %collective-permute-start.8 = (bf16[48,1024]{1,0:T(8,128)(2,1)S(1)}, bf16[48,1024]{1,0:T(8,128)(2,1)S(1)}, u32[]{:S(2)}, u32[]{:S(2)}) collective-permute-start(bf16[48,1024]{1,0:T(8,128)(2,1)S(1)} %get-tuple-element.50), channel_id=1, source_target_pairs={{0,4},{4,0},{8,12},{12,8},{16,20},{20,16},{24,28},{28,24},{1,5},{5... | collective-permute-start | bytes 294920 | tf_op jit(solution)/shard_map/ppermute | solution.py:29
  26.2 0.0 collective-permute-start.9
  26.2 1.5 %collective-permute-start.12 = (bf16[128,512]{1,0:T(8,128)(2,1)S(1)}, bf16[128,512]{1,0:T(8,128)(2,1)S(1)}, u32[]{:S(2)}, u32[]{:S(2)}) collective-permute-start(bf16[128,512]{1,0:T(8,128)(2,1)S(1)} %get-tuple-element.49.q.refs_0_), channel_id=1, source_target_pairs={{0,8},{8,16},{16,24},{24,28},{28,20},{20,12},{12,4},{4,0},{1,9},{9... | collective-permute-start | bytes 393224 | tf_op jit(solution)/shard_map/ppermute | solution.py:40
  27.7 0.0 collective-permute-start.13
  27.7 2.7 %collective-permute-done.8.rim_near = bf16[48,1024]{1,0:T(8,128)(2,1)S(1)} collective-permute-done((bf16[48,1024]{1,0:T(8,128)(2,1)S(1)}, bf16[48,1024]{1,0:T(8,128)(2,1)S(1)}, u32[]{:S(2)}, u32[]{:S(2)}) %collective-permute-start.8) | collective-permute-done | bytes 98336 | tf_op jit(solution)/shard_map/ppermute | solution.py:29
  30.4 0.0 collective-permute-done.9.rim_far
  30.4 0.6 %collective-permute-start.10 = (bf16[64,1024]{1,0:T(8,128)(2,1)S(1)}, bf16[64,1024]{1,0:T(8,128)(2,1)S(1)}, u32[]{:S(2)}, u32[]{:S(2)}) collective-permute-start(bf16[64,1024]{1,0:T(8,128)(2,1)S(1)} %get-tuple-element.53.ends), channel_id=1, source_target_pairs={{0,2},{1,3},{2,0},{3,1},{4,6},{5,7},{6,4},{7,5},{8,10},{9,11},{10,... | collective-permute-start | bytes 393224 | tf_op jit(solution)/shard_map/ppermute | solution.py:29
  31.0 2.5 %collective-permute-start.14 = (bf16[128,512]{1,0:T(8,128)(2,1)S(1)}, bf16[128,512]{1,0:T(8,128)(2,1)S(1)}, u32[]{:S(2)}, u32[]{:S(2)}) collective-permute-start(bf16[128,512]{1,0:T(8,128)(2,1)S(1)} %get-tuple-element.60), channel_id=1, source_target_pairs={{0,4},{4,0},{8,12},{12,8},{16,20},{20,16},{24,28},{28,24},{1,5},{5... | collective-permute-start | bytes 393224 | tf_op jit(solution)/shard_map/ppermute | solution.py:29
  33.5 0.0 collective-permute-done.12.seen.refs_2_
  33.5 0.0 collective-permute-done.11.across
  33.5 2.8 %conv_inner.1 = (bf16[128,512]{1,0:T(8,128)(2,1)S(1)}, f32[32,512]{1,0:T(8,128)S(1)}, f32[64,1024]{1,0:T(8,128)S(1)}, f32[128,1024]{1,0:T(8,128)S(1)}) custom-call(bf16[128,1024]{1,0:T(8,128)(2,1)S(1)} %get-tuple-element.54.chip, bf16[128,1024]{1,0:T(8,128)(2,1)S(1)} %collective-permute-done.11.across, bf16[128,512]{1,0:T(8,128)(2,1)S(1)} %get-tuple-element.48.cot, ...), custom_call_target="tpu_custom_call" | custom-call | bytes 11439000 | tf_op jit(solution)/shard_map/conv_inner/pallas_call | solution.py:76
  36.3 0.0 collective-permute-done.13.seen.refs_1_
  36.3 0.0 collective-permute-done.10.ends_across
  36.4 1.1 %conv_edge.1 = (bf16[128,512]{1,0:T(8,128)(2,1)S(1)}, bf16[128,1024]{1,0:T(8,128)(2,1)S(1)}) custom-call(bf16[64,1024]{1,0:T(8,128)(2,1)S(1)} %get-tuple-element.53.ends, bf16[64,1024]{1,0:T(8,128)(2,1)S(1)} %collective-permute-done.10.ends_across, bf16[48,1024]{1,0:T(8,128)(2,1)S(1)} %collective-permute-done.8.rim_near, ...), custom_call_target="tpu_custom_call" | custom-call | bytes 5166000 | tf_op jit(solution)/shard_map/conv_edge/pallas_call | solution.py:76
  37.5 0.0 collective-permute-done.14.seen.refs_4_.query
  37.5 0.1 collective-permute-start.15
  37.6 0.5 upstream_own.1
  38.1 1.0 %collective-permute-done.15.core = bf16[128,1024]{1,0:T(8,128)(2,1)S(1)} collective-permute-done((bf16[128,1024]{1,0:T(8,128)(2,1)S(1)}, bf16[128,1024]{1,0:T(8,128)(2,1)S(1)}, u32[]{:S(2)}, u32[]{:S(2)}) %collective-permute-start.15) | collective-permute-done | bytes 262176 | tf_op jit(solution)/shard_map/ppermute | solution.py:29
  39.1 0.7 %upstream.1 = (bf16[144,512]{1,0:T(8,128)(2,1)S(1)}, f32[128,512]{1,0:T(8,128)S(1)}) custom-call(bf16[128,1024]{1,0:T(8,128)(2,1)S(1)} %collective-permute-done.15.core, bf16[512,2048]{1,0:T(8,128)(2,1)S(1)} %copy-done, bf16[128,512]{1,0:T(8,128)(2,1)S(1)} %get-tuple-element.44.att, f32[128,512]{1,0:T(8,128)S(1)} %get-tuple-element.62.partial, ...), custom_call_target="tpu_custom_call" | custom-call | bytes 2214000 | tf_op jit(solution)/shard_map/upstream/pallas_call | solution.py:76
  39.8 0.2 collective-permute-start.17
  40.0 1.7 %collective-permute-start.18 = (bf16[144,512]{1,0:T(8,128)(2,1)S(1)}, bf16[144,512]{1,0:T(8,128)(2,1)S(1)}, u32[]{:S(2)}, u32[]{:S(2)}) collective-permute-start(bf16[144,512]{1,0:T(8,128)(2,1)S(1)} %get-tuple-element.64.message.refs_5_), channel_id=1, source_target_pairs={{0,8},{8,16},{16,24},{24,28},{28,20},{20,12},{12,4},{4,0},{1,9},{9... | collective-permute-start | bytes 442376 | tf_op jit(solution)/shard_map/ppermute | solution.py:40
  41.6 0.4 collective-permute-start.19
  42.0 0.0 collective-permute-start.16
  42.0 1.5 %query_grad.1 = (bf16[128,512]{1,0:T(8,128)(2,1)}, bf16[128,512]{1,0:T(8,128)(2,1)}, bf16[128,512]{1,0:T(8,128)(2,1)}) custom-call(bf16[128,512]{1,0:T(8,128)(2,1)S(1)} %get-tuple-element.49.q.refs_0_, bf16[256,512]{1,0:T(8,128)(2,1)S(1)} %pad_add_fusion.1.own, bf16[256,512]{1,0:T(8,128)(2,1)S(1)} %collective-permute-done.2.near, ...), custom_call_target="tpu_custom_call" | custom-call | bytes 6642000 | tf_op jit(solution)/shard_map/query_grad/pallas_call | solution.py:76
  43.6 0.0 collective-permute-done.17.refs_6_
  43.6 2.5 %collective-permute-done.18.refs_7_ = bf16[144,512]{1,0:T(8,128)(2,1)S(1)} collective-permute-done((bf16[144,512]{1,0:T(8,128)(2,1)S(1)}, bf16[144,512]{1,0:T(8,128)(2,1)S(1)}, u32[]{:S(2)}, u32[]{:S(2)}) %collective-permute-start.18) | collective-permute-done | bytes 147488 | tf_op jit(solution)/shard_map/ppermute | solution.py:40
  46.1 2.3 %collective-permute-done.19.refs_8_ = bf16[144,512]{1,0:T(8,128)(2,1)S(1)} collective-permute-done((bf16[144,512]{1,0:T(8,128)(2,1)S(1)}, bf16[144,512]{1,0:T(8,128)(2,1)S(1)}, u32[]{:S(2)}, u32[]{:S(2)}) %collective-permute-start.19) | collective-permute-done | bytes 147488 | tf_op jit(solution)/shard_map/ppermute | solution.py:40
  48.4 0.9 %key_part.1 = (f32[128,512]{1,0:T(8,128)S(1)}, f32[128,512]{1,0:T(8,128)S(1)}, f32[128,512]{1,0:T(8,128)S(1)}) custom-call(bf16[256,512]{1,0:T(8,128)(2,1)S(1)} %pad_add_fusion.1.own, bf16[128,512]{1,0:T(8,128)(2,1)S(1)} %get-tuple-element.49.q.refs_0_, bf16[128,512]{1,0:T(8,128)(2,1)S(1)} %collective-permute-done.13.seen.refs_1_, ...), custom_call_target="tpu_custom_call" | custom-call | bytes 5535000 | tf_op jit(solution)/shard_map/key_part/pallas_call | solution.py:76
  49.3 0.0 collective-permute-done.16.message
  49.3 1.0 %key_grad.1 = (bf16[128,512]{1,0:T(8,128)(2,1)}, bf16[128,512]{1,0:T(8,128)(2,1)}) custom-call(bf16[256,512]{1,0:T(8,128)(2,1)S(1)} %pad_add_fusion.1.own, bf16[128,512]{1,0:T(8,128)(2,1)S(1)} %collective-permute-done.14.seen.refs_4_.query, bf16[144,512]{1,0:T(8,128)(2,1)S(1)} %collective-permute-done.16.message, f32[128,512]{1,0:T(8,128)S(1)} %get-tuple-element.70.late, ...), custom_call_target="tpu_custom_call" | custom-call | bytes 3690000 | tf_op jit(solution)/shard_map/key_grad/pallas_call | solution.py:76
  (5 shorter events, 0.1 us)
Async XLA Ops:
  0.6 12.3 %copy-start.2 = (bf16[128,512]{1,0:T(8,128)(2,1)S(1)}, bf16[128,512]{1,0:T(8,128)(2,1)}, u32[]{:S(2)}) copy-start(bf16[128,512]{1,0:T(8,128)(2,1)} %param.13) | copy-start | bytes 393220
  0.6 14.4 %copy-start.1 = (f32[31,512]{1,0:T(8,128)S(1)}, f32[31,512]{1,0:T(8,128)}, u32[]{:S(2)}) copy-start(f32[31,512]{1,0:T(8,128)} %taps.3) | copy-start | bytes 190468
  0.7 18.5 %copy-start = (bf16[512,2048]{1,0:T(8,128)(2,1)S(1)}, bf16[512,2048]{1,0:T(8,128)(2,1)}, u32[]{:S(2)}) copy-start(bf16[512,2048]{1,0:T(8,128)(2,1)} %weight.7) | copy-start | bytes 6291460
  1.8 9.4 %collective-permute-start = (bf16[256,512]{1,0:T(8,128)(2,1)S(1)}, bf16[256,512]{1,0:T(8,128)(2,1)S(1)}, u32[]{:S(2)}, u32[]{:S(2)}) collective-permute-start(bf16[256,512]{1,0:T(8,128)(2,1)S(1)} %pad_add_fusion.1.own), channel_id=1, source_target_pairs={{8,0},{16,8},{24,16},{28,24},{20,28},{12,20},{4,12},{0,4},{9,1},{1... | collective-permute-start | bytes 786440 | tf_op jit(solution)/shard_map/ppermute | solution.py:40
  4.8 10.3 %collective-permute-start.2 = (bf16[256,512]{1,0:T(8,128)(2,1)S(1)}, bf16[256,512]{1,0:T(8,128)(2,1)S(1)}, u32[]{:S(2)}, u32[]{:S(2)}) collective-permute-start(bf16[256,512]{1,0:T(8,128)(2,1)S(1)} %pad_add_fusion.1.own), channel_id=1, source_target_pairs={{0,1},{1,0},{2,3},{3,2},{4,5},{5,4},{6,7},{7,6},{8,12},{9,13},{10,... | collective-permute-start | bytes 786440 | tf_op jit(solution)/shard_map/ppermute | solution.py:51
  4.8 10.6 %collective-permute-start.3 = (bf16[256,512]{1,0:T(8,128)(2,1)S(1)}, bf16[256,512]{1,0:T(8,128)(2,1)S(1)}, u32[]{:S(2)}, u32[]{:S(2)}) collective-permute-start(bf16[256,512]{1,0:T(8,128)(2,1)S(1)} %pad_add_fusion.1.own), channel_id=1, source_target_pairs={{0,8},{8,16},{16,24},{24,28},{28,20},{20,12},{12,4},{4,0},{1,9},{9... | collective-permute-start | bytes 786440 | tf_op jit(solution)/shard_map/ppermute | solution.py:40
  11.2 7.9 %collective-permute-start.1 = (bf16[256,512]{1,0:T(8,128)(2,1)S(1)}, bf16[256,512]{1,0:T(8,128)(2,1)S(1)}, u32[]{:S(2)}, u32[]{:S(2)}) collective-permute-start(bf16[256,512]{1,0:T(8,128)(2,1)S(1)} %turn.1.seen.second), channel_id=1, source_target_pairs={{0,4},{4,0},{8,12},{12,8},{16,20},{20,16},{24,28},{28,24},{1,5},{5... | collective-permute-start | bytes 786440 | tf_op jit(solution)/shard_map/ppermute | solution.py:29
  12.9 6.9 %collective-permute-start.5 = (bf16[128,512]{1,0:T(8,128)(2,1)S(1)}, bf16[128,512]{1,0:T(8,128)(2,1)S(1)}, u32[]{:S(2)}, u32[]{:S(2)}) collective-permute-start(bf16[128,512]{1,0:T(8,128)(2,1)S(1)} %copy-done.2), channel_id=1, source_target_pairs={{0,2},{1,3},{2,0},{3,1},{4,6},{5,7},{6,4},{7,5},{8,10},{9,11},{10,... | collective-permute-start | bytes 393224 | tf_op jit(solution)/shard_map/ppermute | solution.py:29
  14.5 5.9 %collective-permute-start.4 = (bf16[128,512]{1,0:T(8,128)(2,1)S(1)}, bf16[128,512]{1,0:T(8,128)(2,1)S(1)}, u32[]{:S(2)}, u32[]{:S(2)}) collective-permute-start(bf16[128,512]{1,0:T(8,128)(2,1)S(1)} %get-tuple-element.40.q), channel_id=1, source_target_pairs={{8,0},{16,8},{24,16},{28,24},{20,28},{12,20},{4,12},{0,4},{9,1},{1... | collective-permute-start | bytes 393224 | tf_op jit(solution)/shard_map/ppermute | solution.py:40
  15.1 4.8 %collective-permute-start.6 = (f32[31,512]{1,0:T(8,128)S(1)}, f32[31,512]{1,0:T(8,128)S(1)}, u32[]{:S(2)}, u32[]{:S(2)}) collective-permute-start(f32[31,512]{1,0:T(8,128)S(1)} %copy-done.1), channel_id=1, source_target_pairs={{0,2},{1,3},{2,0},{3,1},{4,6},{5,7},{6,4},{7,5},{8,10},{9,11},{10,... | collective-permute-start | bytes 190472 | tf_op jit(solution)/shard_map/ppermute | solution.py:29
  20.5 1.6 %collective-permute-start.7 = (bf16[128,1024]{1,0:T(8,128)(2,1)S(1)}, bf16[128,1024]{1,0:T(8,128)(2,1)S(1)}, u32[]{:S(2)}, u32[]{:S(2)}) collective-permute-start(bf16[128,1024]{1,0:T(8,128)(2,1)S(1)} %get-tuple-element.46), channel_id=1, source_target_pairs={{0,1},{1,0},{2,3},{3,2},{4,5},{5,4},{6,7},{7,6},{8,9},{9,8},{10,11... | collective-permute-start | bytes 786440 | tf_op jit(solution)/shard_map/ppermute | solution.py:29
  22.2 11.3 %collective-permute-start.11 = (bf16[128,1024]{1,0:T(8,128)(2,1)S(1)}, bf16[128,1024]{1,0:T(8,128)(2,1)S(1)}, u32[]{:S(2)}, u32[]{:S(2)}) collective-permute-start(bf16[128,1024]{1,0:T(8,128)(2,1)S(1)} %get-tuple-element.54.chip), channel_id=1, source_target_pairs={{0,2},{1,3},{2,0},{3,1},{4,6},{5,7},{6,4},{7,5},{8,10},{9,11},{10,... | collective-permute-start | bytes 786440 | tf_op jit(solution)/shard_map/ppermute | solution.py:29
  23.8 6.7 %collective-permute-start.8 = (bf16[48,1024]{1,0:T(8,128)(2,1)S(1)}, bf16[48,1024]{1,0:T(8,128)(2,1)S(1)}, u32[]{:S(2)}, u32[]{:S(2)}) collective-permute-start(bf16[48,1024]{1,0:T(8,128)(2,1)S(1)} %get-tuple-element.50), channel_id=1, source_target_pairs={{0,4},{4,0},{8,12},{12,8},{16,20},{20,16},{24,28},{28,24},{1,5},{5... | collective-permute-start | bytes 294920 | tf_op jit(solution)/shard_map/ppermute | solution.py:29
  26.2 4.2 %collective-permute-start.9 = (bf16[48,1024]{1,0:T(8,128)(2,1)S(1)}, bf16[48,1024]{1,0:T(8,128)(2,1)S(1)}, u32[]{:S(2)}, u32[]{:S(2)}) collective-permute-start(bf16[48,1024]{1,0:T(8,128)(2,1)S(1)} %get-tuple-element.51), channel_id=1, source_target_pairs={{0,1},{1,0},{2,3},{3,2},{4,8},{5,9},{6,10},{7,11},{8,4},{9,5},{10,... | collective-permute-start | bytes 294920 | tf_op jit(solution)/shard_map/ppermute | solution.py:51
  26.2 7.3 %collective-permute-start.12 = (bf16[128,512]{1,0:T(8,128)(2,1)S(1)}, bf16[128,512]{1,0:T(8,128)(2,1)S(1)}, u32[]{:S(2)}, u32[]{:S(2)}) collective-permute-start(bf16[128,512]{1,0:T(8,128)(2,1)S(1)} %get-tuple-element.49.q.refs_0_), channel_id=1, source_target_pairs={{0,8},{8,16},{16,24},{24,28},{28,20},{20,12},{12,4},{4,0},{1,9},{9... | collective-permute-start | bytes 393224 | tf_op jit(solution)/shard_map/ppermute | solution.py:40
  27.7 8.6 %collective-permute-start.13 = (bf16[128,512]{1,0:T(8,128)(2,1)S(1)}, bf16[128,512]{1,0:T(8,128)(2,1)S(1)}, u32[]{:S(2)}, u32[]{:S(2)}) collective-permute-start(bf16[128,512]{1,0:T(8,128)(2,1)S(1)} %get-tuple-element.49.q.refs_0_), channel_id=1, source_target_pairs={{0,1},{1,0},{2,3},{3,2},{4,5},{5,4},{6,7},{7,6},{8,12},{9,13},{10,... | collective-permute-start | bytes 393224 | tf_op jit(solution)/shard_map/ppermute | solution.py:51
  30.4 5.9 %collective-permute-start.10 = (bf16[64,1024]{1,0:T(8,128)(2,1)S(1)}, bf16[64,1024]{1,0:T(8,128)(2,1)S(1)}, u32[]{:S(2)}, u32[]{:S(2)}) collective-permute-start(bf16[64,1024]{1,0:T(8,128)(2,1)S(1)} %get-tuple-element.53.ends), channel_id=1, source_target_pairs={{0,2},{1,3},{2,0},{3,1},{4,6},{5,7},{6,4},{7,5},{8,10},{9,11},{10,... | collective-permute-start | bytes 393224 | tf_op jit(solution)/shard_map/ppermute | solution.py:29
  31.0 6.5 %collective-permute-start.14 = (bf16[128,512]{1,0:T(8,128)(2,1)S(1)}, bf16[128,512]{1,0:T(8,128)(2,1)S(1)}, u32[]{:S(2)}, u32[]{:S(2)}) collective-permute-start(bf16[128,512]{1,0:T(8,128)(2,1)S(1)} %get-tuple-element.60), channel_id=1, source_target_pairs={{0,4},{4,0},{8,12},{12,8},{16,20},{20,16},{24,28},{28,24},{1,5},{5... | collective-permute-start | bytes 393224 | tf_op jit(solution)/shard_map/ppermute | solution.py:29
  37.5 1.6 %collective-permute-start.15 = (bf16[128,1024]{1,0:T(8,128)(2,1)S(1)}, bf16[128,1024]{1,0:T(8,128)(2,1)S(1)}, u32[]{:S(2)}, u32[]{:S(2)}) collective-permute-start(bf16[128,1024]{1,0:T(8,128)(2,1)S(1)} %hand.1.own.grad_here), channel_id=1, source_target_pairs={{0,1},{1,0},{2,3},{3,2},{4,5},{5,4},{6,7},{7,6},{8,9},{9,8},{10,11... | collective-permute-start | bytes 786440 | tf_op jit(solution)/shard_map/ppermute | solution.py:29
  39.8 3.8 %collective-permute-start.17 = (bf16[144,512]{1,0:T(8,128)(2,1)S(1)}, bf16[144,512]{1,0:T(8,128)(2,1)S(1)}, u32[]{:S(2)}, u32[]{:S(2)}) collective-permute-start(bf16[144,512]{1,0:T(8,128)(2,1)S(1)} %get-tuple-element.64.message.refs_5_), channel_id=1, source_target_pairs={{0,1},{1,0},{2,3},{3,2},{4,5},{5,4},{6,7},{7,6},{8,12},{9,13},{10,... | collective-permute-start | bytes 442376 | tf_op jit(solution)/shard_map/ppermute | solution.py:51
  40.0 6.1 %collective-permute-start.18 = (bf16[144,512]{1,0:T(8,128)(2,1)S(1)}, bf16[144,512]{1,0:T(8,128)(2,1)S(1)}, u32[]{:S(2)}, u32[]{:S(2)}) collective-permute-start(bf16[144,512]{1,0:T(8,128)(2,1)S(1)} %get-tuple-element.64.message.refs_5_), channel_id=1, source_target_pairs={{0,8},{8,16},{16,24},{24,28},{28,20},{20,12},{12,4},{4,0},{1,9},{9... | collective-permute-start | bytes 442376 | tf_op jit(solution)/shard_map/ppermute | solution.py:40
  41.6 6.8 %collective-permute-start.19 = (bf16[144,512]{1,0:T(8,128)(2,1)S(1)}, bf16[144,512]{1,0:T(8,128)(2,1)S(1)}, u32[]{:S(2)}, u32[]{:S(2)}) collective-permute-start(bf16[144,512]{1,0:T(8,128)(2,1)S(1)} %get-tuple-element.64.message.refs_5_), channel_id=1, source_target_pairs={{8,0},{16,8},{24,16},{28,24},{20,28},{12,20},{4,12},{0,4},{9,1},{1... | collective-permute-start | bytes 442376 | tf_op jit(solution)/shard_map/ppermute | solution.py:40
  42.0 7.3 %collective-permute-start.16 = (bf16[144,512]{1,0:T(8,128)(2,1)S(1)}, bf16[144,512]{1,0:T(8,128)(2,1)S(1)}, u32[]{:S(2)}, u32[]{:S(2)}) collective-permute-start(bf16[144,512]{1,0:T(8,128)(2,1)S(1)} %get-tuple-element.64.message.refs_5_), channel_id=1, source_target_pairs={{0,1},{1,0},{2,3},{3,2},{4,8},{5,9},{6,10},{7,11},{8,4},{9,5},{10,... | collective-permute-start | bytes 442376 | tf_op jit(solution)/shard_map/ppermute | solution.py:51

commit v21 on v20

--- a/solution.py
+++ b/solution.py
@@ -440,7 +440,7 @@
     frames = own.shape[0] // 2
     heads = columns(own.shape[1])
     above, below = slice(0, frames), slice(frames, 2 * frames)
-    biases = (None, bias_of(near_swapped()), None, None)
+    biases = (None, None, None, bias_of(near_swapped()))
     asks = [stacked(queries, above, c) for c in heads]
     ups = [stacked(messages, above, c) for c in heads]
     scores = [dot_nt(own[above, c], a) * scale for c, a in zip(heads, asks)]
@@ -588,7 +588,7 @@
     key_part, value_part, late = kernel_call(
         functools.partial(key_part_body, scale),
         (tile32, tile32, tile32),
-        (kv, q_own, q_near, q_first, q_second, q_relay, message, m_near, m_first, m_second),
+        (kv, q_own, q_first, q_second, q_near, q_relay, message, m_first, m_second, m_near),
         1.5, "key_part",
     )
     grad_key, grad_value = kernel_call(

time: 50.5 us -> 50.9 us (level)
  the two profiles are of different devices: /device:TPU:0 before, /device:TPU:16 now
where the time goes in v21:
time: 50.9 us; the launch traced here: 50.7 us
  starting transfers between devices  20 us (39%)
  waiting for transfers between devices  17.3 us (34%)
  Pallas kernels  10.3 us (20%)
  other arithmetic  2.19 us (4%)
  between operations  0.83 us (2%)
    pallas_call x16, Pallas kernels, kernel_call(): pl.pallas_call(body, out_shape=outs, in_specs=[VMEM] * (len(args) - unrea...  10.3 us
    ppermute x9, starting transfers between devices, pair_swap(): lax.ppermute(block, axis, [(i, i ^ bit) for i in range(lax.axis_size(axis...  8.67 us
    ppermute x6, waiting for transfers between devices, ring(): return lax.ppermute(block, 'ctx', ring_routes(lax.axis_size('ctx'))[way])  8.4 us
    ppermute x6, starting transfers between devices, ring(): return lax.ppermute(block, 'ctx', ring_routes(lax.axis_size('ctx'))[way])  6.01 us
    ppermute x9, waiting for transfers between devices, pair_swap(): lax.ppermute(block, axis, [(i, i ^ bit) for i in range(lax.axis_size(axis...  5.6 us
    ppermute x5, starting transfers between devices, total_swap(): return lax.ppermute(block, ('ctx', 'mp'), route)  5.36 us
    ppermute x5, waiting for transfers between devices, total_swap(): return lax.ppermute(block, ('ctx', 'mp'), route)  3.33 us
    add x1, other arithmetic, per_device(): lax.pad(key_rows, zero, ((0, frames, 0), (0, 0, 0)))  1.14 us
  transfers between devices with their start and end apart: 20, of which 11 were waited for; matrix products, arithmetic and copies ran while one was open for 2% of the time, Pallas kernels for 17%

profile of v21, /device:TPU:16, one launch (start us, length us, event | category | flops | bytes accessed | tf_op | source)
XLA Modules:
  0.0 50.7 jit_solution(9909532030762442454)
XLA Ops:
  0.6 0.0 copy-start.2
  0.6 0.0 copy-start.1
  0.7 0.0 copy-start
  0.7 1.1 %pad_add_fusion.1.own = bf16[256,512]{1,0:T(8,128)(2,1)S(1)} fusion(bf16[128,512]{1,0:T(8,128)(2,1)} %param.9, bf16[128,512]{1,0:T(8,128)(2,1)} %param.8), kind=kLoop, calls=%fused_computation.1 | loop fusion | flops 524288 | bytes 524288 | tf_op jit(solution)/shard_map/add | solution.py:496
  1.8 0.5 collective-permute-start
  2.3 2.6 %collective-permute-start.2 = (bf16[256,512]{1,0:T(8,128)(2,1)S(1)}, bf16[256,512]{1,0:T(8,128)(2,1)S(1)}, u32[]{:S(2)}, u32[]{:S(2)}) collective-permute-start(bf16[256,512]{1,0:T(8,128)(2,1)S(1)} %pad_add_fusion.1.own), channel_id=1, source_target_pairs={{0,1},{1,0},{2,3},{3,2},{4,5},{5,4},{6,7},{7,6},{8,12},{9,13},{10,... | collective-permute-start | bytes 786440 | tf_op jit(solution)/shard_map/ppermute | solution.py:51
  4.9 0.0 collective-permute-start.3
  4.9 1.1 %pad_add_fusion.seen.joined = bf16[384,512]{1,0:T(8,128)(2,1)S(1)} fusion(bf16[128,512]{1,0:T(8,128)(2,1)} %param.13, bf16[128,512]{1,0:T(8,128)(2,1)} %param.10, bf16[128,512]{1,0:T(8,128)(2,1)} %param.7), kind=kLoop, calls=%fused_computation | loop fusion | flops 1179648 | bytes 786432 | tf_op jit(solution)/shard_map/add | solution.py:499
  6.0 3.9 %collective-permute-done.block = bf16[256,512]{1,0:T(8,128)(2,1)S(1)} collective-permute-done((bf16[256,512]{1,0:T(8,128)(2,1)S(1)}, bf16[256,512]{1,0:T(8,128)(2,1)S(1)}, u32[]{:S(2)}, u32[]{:S(2)}) %collective-permute-start) | collective-permute-done | bytes 262176 | tf_op jit(solution)/shard_map/ppermute | solution.py:40
  9.9 1.6 %collective-permute-start.1 = (bf16[256,512]{1,0:T(8,128)(2,1)S(1)}, bf16[256,512]{1,0:T(8,128)(2,1)S(1)}, u32[]{:S(2)}, u32[]{:S(2)}) collective-permute-start(bf16[256,512]{1,0:T(8,128)(2,1)S(1)} %turn.1.seen.second), channel_id=1, source_target_pairs={{0,4},{4,0},{8,12},{12,8},{16,20},{20,16},{24,28},{28,24},{1,5},{5... | collective-permute-start | bytes 786440 | tf_op jit(solution)/shard_map/ppermute | solution.py:29
  11.5 0.0 copy-done.2
  11.5 1.5 %collective-permute-start.5 = (bf16[128,512]{1,0:T(8,128)(2,1)S(1)}, bf16[128,512]{1,0:T(8,128)(2,1)S(1)}, u32[]{:S(2)}, u32[]{:S(2)}) collective-permute-start(bf16[128,512]{1,0:T(8,128)(2,1)S(1)} %copy-done.2), channel_id=1, source_target_pairs={{0,2},{1,3},{2,0},{3,1},{4,6},{5,7},{6,4},{7,5},{8,10},{9,11},{10,... | collective-permute-start | bytes 393224 | tf_op jit(solution)/shard_map/ppermute | solution.py:29
  13.0 0.5 collective-permute-start.4
  13.5 0.0 collective-permute-done.2.near
  13.5 0.0 copy-done.1
  13.5 0.5 collective-permute-start.6
  14.0 0.0 collective-permute-done.3.first
  14.1 0.6 %forward.1 = (f32[128,512]{1,0:T(8,128)S(1)}, f32[128,512]{1,0:T(8,128)S(1)}, f32[128,512]{1,0:T(8,128)S(1)}) custom-call(bf16[128,512]{1,0:T(8,128)(2,1)S(1)} %get-tuple-element.40.q, bf16[256,512]{1,0:T(8,128)(2,1)S(1)} %pad_add_fusion.1.own, bf16[256,512]{1,0:T(8,128)(2,1)S(1)} %collective-permute-done.2.near, ...), custom_call_target="tpu_custom_call" | custom-call | bytes 3690000 | tf_op jit(solution)/shard_map/forward/pallas_call | solution.py:76
  14.7 2.5 %collective-permute-done.1.relay = bf16[256,512]{1,0:T(8,128)(2,1)S(1)} collective-permute-done((bf16[256,512]{1,0:T(8,128)(2,1)S(1)}, bf16[256,512]{1,0:T(8,128)(2,1)S(1)}, u32[]{:S(2)}, u32[]{:S(2)}) %collective-permute-start.1) | collective-permute-done | bytes 262176 | tf_op jit(solution)/shard_map/ppermute | solution.py:29
  17.2 0.0 copy-done
  17.2 0.7 %project.1 = (bf16[128,512]{1,0:T(8,128)(2,1)S(1)}, f32[128,512]{1,0:T(8,128)S(1)}, bf16[128,1024]{1,0:T(8,128)(2,1)S(1)}) custom-call(bf16[128,512]{1,0:T(8,128)(2,1)S(1)} %get-tuple-element.40.q, bf16[256,512]{1,0:T(8,128)(2,1)S(1)} %collective-permute-done.1.relay, f32[128,512]{1,0:T(8,128)S(1)} %get-tuple-element.41.sums, ...), custom_call_target="tpu_custom_call" | custom-call | bytes 3690000 | tf_op jit(solution)/shard_map/project/pallas_call | solution.py:76
  17.9 0.0 collective-permute-done.6.seen_b.taps_other
  17.9 0.0 collective-permute-done.5.seen_a.cot_other
  17.9 0.1 collective-permute-done.4.q_second
  18.1 0.1 collective-permute-start.7
  18.2 0.3 project_own.1.keep
  18.5 1.2 %collective-permute-done.7.core = bf16[128,1024]{1,0:T(8,128)(2,1)S(1)} collective-permute-done((bf16[128,1024]{1,0:T(8,128)(2,1)S(1)}, bf16[128,1024]{1,0:T(8,128)(2,1)S(1)}, u32[]{:S(2)}, u32[]{:S(2)}) %collective-permute-start.7) | collective-permute-done | bytes 262176 | tf_op jit(solution)/shard_map/ppermute | solution.py:29
  19.7 0.1 join.1
  19.8 1.5 %collective-permute-start.11 = (bf16[128,1024]{1,0:T(8,128)(2,1)S(1)}, bf16[128,1024]{1,0:T(8,128)(2,1)S(1)}, u32[]{:S(2)}, u32[]{:S(2)}) collective-permute-start(bf16[128,1024]{1,0:T(8,128)(2,1)S(1)} %get-tuple-element.54.chip), channel_id=1, source_target_pairs={{0,2},{1,3},{2,0},{3,1},{4,6},{5,7},{6,4},{7,5},{8,10},{9,11},{10,... | collective-permute-start | bytes 786440 | tf_op jit(solution)/shard_map/ppermute | solution.py:29
  21.3 1.5 %collective-permute-start.8 = (bf16[48,1024]{1,0:T(8,128)(2,1)S(1)}, bf16[48,1024]{1,0:T(8,128)(2,1)S(1)}, u32[]{:S(2)}, u32[]{:S(2)}) collective-permute-start(bf16[48,1024]{1,0:T(8,128)(2,1)S(1)} %get-tuple-element.50), channel_id=1, source_target_pairs={{0,4},{4,0},{8,12},{12,8},{16,20},{20,16},{24,28},{28,24},{1,5},{5... | collective-permute-start | bytes 294920 | tf_op jit(solution)/shard_map/ppermute | solution.py:29
  22.7 0.4 collective-permute-start.9
  23.2 1.7 %collective-permute-start.12 = (bf16[128,512]{1,0:T(8,128)(2,1)S(1)}, bf16[128,512]{1,0:T(8,128)(2,1)S(1)}, u32[]{:S(2)}, u32[]{:S(2)}) collective-permute-start(bf16[128,512]{1,0:T(8,128)(2,1)S(1)} %get-tuple-element.49.q.refs_0_), channel_id=1, source_target_pairs={{0,8},{8,16},{16,24},{24,28},{28,20},{20,12},{12,4},{4,0},{1,9},{9... | collective-permute-start | bytes 393224 | tf_op jit(solution)/shard_map/ppermute | solution.py:40
  24.9 1.5 %collective-permute-start.13 = (bf16[128,512]{1,0:T(8,128)(2,1)S(1)}, bf16[128,512]{1,0:T(8,128)(2,1)S(1)}, u32[]{:S(2)}, u32[]{:S(2)}) collective-permute-start(bf16[128,512]{1,0:T(8,128)(2,1)S(1)} %get-tuple-element.49.q.refs_0_), channel_id=1, source_target_pairs={{0,1},{1,0},{2,3},{3,2},{4,5},{5,4},{6,7},{7,6},{8,12},{9,13},{10,... | collective-permute-start | bytes 393224 | tf_op jit(solution)/shard_map/ppermute | solution.py:51
  26.3 0.7 %collective-permute-done.8.rim_near = bf16[48,1024]{1,0:T(8,128)(2,1)S(1)} collective-permute-done((bf16[48,1024]{1,0:T(8,128)(2,1)S(1)}, bf16[48,1024]{1,0:T(8,128)(2,1)S(1)}, u32[]{:S(2)}, u32[]{:S(2)}) %collective-permute-start.8) | collective-permute-done | bytes 98336 | tf_op jit(solution)/shard_map/ppermute | solution.py:29
  27.0 1.3 %collective-permute-done.9.rim_far = bf16[48,1024]{1,0:T(8,128)(2,1)S(1)} collective-permute-done((bf16[48,1024]{1,0:T(8,128)(2,1)S(1)}, bf16[48,1024]{1,0:T(8,128)(2,1)S(1)}, u32[]{:S(2)}, u32[]{:S(2)}) %collective-permute-start.9) | collective-permute-done | bytes 98336 | tf_op jit(solution)/shard_map/ppermute | solution.py:51
  28.3 0.6 %collective-permute-start.10 = (bf16[64,1024]{1,0:T(8,128)(2,1)S(1)}, bf16[64,1024]{1,0:T(8,128)(2,1)S(1)}, u32[]{:S(2)}, u32[]{:S(2)}) collective-permute-start(bf16[64,1024]{1,0:T(8,128)(2,1)S(1)} %get-tuple-element.53.ends), channel_id=1, source_target_pairs={{0,2},{1,3},{2,0},{3,1},{4,6},{5,7},{6,4},{7,5},{8,10},{9,11},{10,... | collective-permute-start | bytes 393224 | tf_op jit(solution)/shard_map/ppermute | solution.py:29
  29.0 1.4 %collective-permute-start.14 = (bf16[128,512]{1,0:T(8,128)(2,1)S(1)}, bf16[128,512]{1,0:T(8,128)(2,1)S(1)}, u32[]{:S(2)}, u32[]{:S(2)}) collective-permute-start(bf16[128,512]{1,0:T(8,128)(2,1)S(1)} %get-tuple-element.60), channel_id=1, source_target_pairs={{0,4},{4,0},{8,12},{12,8},{16,20},{20,16},{24,28},{28,24},{1,5},{5... | collective-permute-start | bytes 393224 | tf_op jit(solution)/shard_map/ppermute | solution.py:29
  30.3 0.0 collective-permute-done.12.seen.refs_1_
  30.3 0.0 collective-permute-done.11.across
  30.3 2.8 %conv_inner.1 = (bf16[128,512]{1,0:T(8,128)(2,1)S(1)}, f32[32,512]{1,0:T(8,128)S(1)}, f32[64,1024]{1,0:T(8,128)S(1)}, f32[128,1024]{1,0:T(8,128)S(1)}) custom-call(bf16[128,1024]{1,0:T(8,128)(2,1)S(1)} %get-tuple-element.54.chip, bf16[128,1024]{1,0:T(8,128)(2,1)S(1)} %collective-permute-done.11.across, bf16[128,512]{1,0:T(8,128)(2,1)S(1)} %get-tuple-element.48.cot, ...), custom_call_target="tpu_custom_call" | custom-call | bytes 11439000 | tf_op jit(solution)/shard_map/conv_inner/pallas_call | solution.py:76
  33.2 0.0 collective-permute-done.13.seen.refs_3_
  33.2 0.2 collective-permute-done.10.ends_across
  33.4 1.1 %conv_edge.1 = (bf16[128,512]{1,0:T(8,128)(2,1)S(1)}, bf16[128,1024]{1,0:T(8,128)(2,1)S(1)}) custom-call(bf16[64,1024]{1,0:T(8,128)(2,1)S(1)} %get-tuple-element.53.ends, bf16[64,1024]{1,0:T(8,128)(2,1)S(1)} %collective-permute-done.10.ends_across, bf16[48,1024]{1,0:T(8,128)(2,1)S(1)} %collective-permute-done.8.rim_near, ...), custom_call_target="tpu_custom_call" | custom-call | bytes 5166000 | tf_op jit(solution)/shard_map/conv_edge/pallas_call | solution.py:76
  34.5 0.0 collective-permute-done.14.seen.refs_4_.query
  34.5 0.1 collective-permute-start.15
  34.6 0.5 upstream_own.1
  35.1 1.0 %collective-permute-done.15.core = bf16[128,1024]{1,0:T(8,128)(2,1)S(1)} collective-permute-done((bf16[128,1024]{1,0:T(8,128)(2,1)S(1)}, bf16[128,1024]{1,0:T(8,128)(2,1)S(1)}, u32[]{:S(2)}, u32[]{:S(2)}) %collective-permute-start.15) | collective-permute-done | bytes 262176 | tf_op jit(solution)/shard_map/ppermute | solution.py:29
  36.1 0.7 %upstream.1 = (bf16[144,512]{1,0:T(8,128)(2,1)S(1)}, f32[128,512]{1,0:T(8,128)S(1)}) custom-call(bf16[128,1024]{1,0:T(8,128)(2,1)S(1)} %collective-permute-done.15.core, bf16[512,2048]{1,0:T(8,128)(2,1)S(1)} %copy-done, bf16[128,512]{1,0:T(8,128)(2,1)S(1)} %get-tuple-element.44.att, f32[128,512]{1,0:T(8,128)S(1)} %get-tuple-element.62.partial, ...), custom_call_target="tpu_custom_call" | custom-call | bytes 2214000 | tf_op jit(solution)/shard_map/upstream/pallas_call | solution.py:76
  36.8 3.3 %collective-permute-start.17 = (bf16[144,512]{1,0:T(8,128)(2,1)S(1)}, bf16[144,512]{1,0:T(8,128)(2,1)S(1)}, u32[]{:S(2)}, u32[]{:S(2)}) collective-permute-start(bf16[144,512]{1,0:T(8,128)(2,1)S(1)} %get-tuple-element.64.message.refs_5_), channel_id=1, source_target_pairs={{0,8},{8,16},{16,24},{24,28},{28,20},{20,12},{12,4},{4,0},{1,9},{9... | collective-permute-start | bytes 442376 | tf_op jit(solution)/shard_map/ppermute | solution.py:40
  40.1 0.0 collective-permute-start.18
  40.1 0.5 collective-permute-start.19
  40.6 0.4 collective-permute-start.16
  41.0 1.5 %query_grad.1 = (bf16[128,512]{1,0:T(8,128)(2,1)}, bf16[128,512]{1,0:T(8,128)(2,1)}, bf16[128,512]{1,0:T(8,128)(2,1)}) custom-call(bf16[128,512]{1,0:T(8,128)(2,1)S(1)} %get-tuple-element.49.q.refs_0_, bf16[256,512]{1,0:T(8,128)(2,1)S(1)} %pad_add_fusion.1.own, bf16[256,512]{1,0:T(8,128)(2,1)S(1)} %collective-permute-done.2.near, ...), custom_call_target="tpu_custom_call" | custom-call | bytes 6642000 | tf_op jit(solution)/shard_map/query_grad/pallas_call | solution.py:76
  42.5 1.0 %collective-permute-done.17.refs_6_ = bf16[144,512]{1,0:T(8,128)(2,1)S(1)} collective-permute-done((bf16[144,512]{1,0:T(8,128)(2,1)S(1)}, bf16[144,512]{1,0:T(8,128)(2,1)S(1)}, u32[]{:S(2)}, u32[]{:S(2)}) %collective-permute-start.17) | collective-permute-done | bytes 147488 | tf_op jit(solution)/shard_map/ppermute | solution.py:40
  43.5 3.3 %collective-permute-done.18.refs_7_ = bf16[144,512]{1,0:T(8,128)(2,1)S(1)} collective-permute-done((bf16[144,512]{1,0:T(8,128)(2,1)S(1)}, bf16[144,512]{1,0:T(8,128)(2,1)S(1)}, u32[]{:S(2)}, u32[]{:S(2)}) %collective-permute-start.18) | collective-permute-done | bytes 147488 | tf_op jit(solution)/shard_map/ppermute | solution.py:40
  46.8 2.0 %collective-permute-done.19.refs_8_ = bf16[144,512]{1,0:T(8,128)(2,1)S(1)} collective-permute-done((bf16[144,512]{1,0:T(8,128)(2,1)S(1)}, bf16[144,512]{1,0:T(8,128)(2,1)S(1)}, u32[]{:S(2)}, u32[]{:S(2)}) %collective-permute-start.19) | collective-permute-done | bytes 147488 | tf_op jit(solution)/shard_map/ppermute | solution.py:51
  48.9 0.8 %key_part.1 = (f32[128,512]{1,0:T(8,128)S(1)}, f32[128,512]{1,0:T(8,128)S(1)}, f32[128,512]{1,0:T(8,128)S(1)}) custom-call(bf16[256,512]{1,0:T(8,128)(2,1)S(1)} %pad_add_fusion.1.own, bf16[128,512]{1,0:T(8,128)(2,1)S(1)} %get-tuple-element.49.q.refs_0_, bf16[128,512]{1,0:T(8,128)(2,1)S(1)} %collective-permute-done.12.seen.refs_1_, ...), custom_call_target="tpu_custom_call" | custom-call | bytes 5535000 | tf_op jit(solution)/shard_map/key_part/pallas_call | solution.py:76
  49.7 0.0 collective-permute-done.16.message
  49.7 1.0 %key_grad.1 = (bf16[128,512]{1,0:T(8,128)(2,1)}, bf16[128,512]{1,0:T(8,128)(2,1)}) custom-call(bf16[256,512]{1,0:T(8,128)(2,1)S(1)} %pad_add_fusion.1.own, bf16[128,512]{1,0:T(8,128)(2,1)S(1)} %collective-permute-done.14.seen.refs_4_.query, bf16[144,512]{1,0:T(8,128)(2,1)S(1)} %collective-permute-done.16.message, f32[128,512]{1,0:T(8,128)S(1)} %get-tuple-element.70.late, ...), custom_call_target="tpu_custom_call" | custom-call | bytes 3690000 | tf_op jit(solution)/shard_map/key_grad/pallas_call | solution.py:76
  (5 shorter events, 0.1 us)
Async XLA Ops:
  0.6 10.9 %copy-start.2 = (bf16[128,512]{1,0:T(8,128)(2,1)S(1)}, bf16[128,512]{1,0:T(8,128)(2,1)}, u32[]{:S(2)}) copy-start(bf16[128,512]{1,0:T(8,128)(2,1)} %param.13) | copy-start | bytes 393220
  0.6 12.9 %copy-start.1 = (f32[31,512]{1,0:T(8,128)S(1)}, f32[31,512]{1,0:T(8,128)}, u32[]{:S(2)}) copy-start(f32[31,512]{1,0:T(8,128)} %taps.3) | copy-start | bytes 190468
  0.7 16.5 %copy-start = (bf16[512,2048]{1,0:T(8,128)(2,1)S(1)}, bf16[512,2048]{1,0:T(8,128)(2,1)}, u32[]{:S(2)}) copy-start(bf16[512,2048]{1,0:T(8,128)(2,1)} %weight.7) | copy-start | bytes 6291460
  1.8 8.1 %collective-permute-start = (bf16[256,512]{1,0:T(8,128)(2,1)S(1)}, bf16[256,512]{1,0:T(8,128)(2,1)S(1)}, u32[]{:S(2)}, u32[]{:S(2)}) collective-permute-start(bf16[256,512]{1,0:T(8,128)(2,1)S(1)} %pad_add_fusion.1.own), channel_id=1, source_target_pairs={{8,0},{16,8},{24,16},{28,24},{20,28},{12,20},{4,12},{0,4},{9,1},{1... | collective-permute-start | bytes 786440 | tf_op jit(solution)/shard_map/ppermute | solution.py:40
  2.3 11.2 %collective-permute-start.2 = (bf16[256,512]{1,0:T(8,128)(2,1)S(1)}, bf16[256,512]{1,0:T(8,128)(2,1)S(1)}, u32[]{:S(2)}, u32[]{:S(2)}) collective-permute-start(bf16[256,512]{1,0:T(8,128)(2,1)S(1)} %pad_add_fusion.1.own), channel_id=1, source_target_pairs={{0,1},{1,0},{2,3},{3,2},{4,5},{5,4},{6,7},{7,6},{8,12},{9,13},{10,... | collective-permute-start | bytes 786440 | tf_op jit(solution)/shard_map/ppermute | solution.py:51
  4.9 9.1 %collective-permute-start.3 = (bf16[256,512]{1,0:T(8,128)(2,1)S(1)}, bf16[256,512]{1,0:T(8,128)(2,1)S(1)}, u32[]{:S(2)}, u32[]{:S(2)}) collective-permute-start(bf16[256,512]{1,0:T(8,128)(2,1)S(1)} %pad_add_fusion.1.own), channel_id=1, source_target_pairs={{0,8},{8,16},{16,24},{24,28},{28,20},{20,12},{12,4},{4,0},{1,9},{9... | collective-permute-start | bytes 786440 | tf_op jit(solution)/shard_map/ppermute | solution.py:40
  9.9 7.2 %collective-permute-start.1 = (bf16[256,512]{1,0:T(8,128)(2,1)S(1)}, bf16[256,512]{1,0:T(8,128)(2,1)S(1)}, u32[]{:S(2)}, u32[]{:S(2)}) collective-permute-start(bf16[256,512]{1,0:T(8,128)(2,1)S(1)} %turn.1.seen.second), channel_id=1, source_target_pairs={{0,4},{4,0},{8,12},{12,8},{16,20},{20,16},{24,28},{28,24},{1,5},{5... | collective-permute-start | bytes 786440 | tf_op jit(solution)/shard_map/ppermute | solution.py:29
  11.5 6.4 %collective-permute-start.5 = (bf16[128,512]{1,0:T(8,128)(2,1)S(1)}, bf16[128,512]{1,0:T(8,128)(2,1)S(1)}, u32[]{:S(2)}, u32[]{:S(2)}) collective-permute-start(bf16[128,512]{1,0:T(8,128)(2,1)S(1)} %copy-done.2), channel_id=1, source_target_pairs={{0,2},{1,3},{2,0},{3,1},{4,6},{5,7},{6,4},{7,5},{8,10},{9,11},{10,... | collective-permute-start | bytes 393224 | tf_op jit(solution)/shard_map/ppermute | solution.py:29
  13.0 5.0 %collective-permute-start.4 = (bf16[128,512]{1,0:T(8,128)(2,1)S(1)}, bf16[128,512]{1,0:T(8,128)(2,1)S(1)}, u32[]{:S(2)}, u32[]{:S(2)}) collective-permute-start(bf16[128,512]{1,0:T(8,128)(2,1)S(1)} %get-tuple-element.40.q), channel_id=1, source_target_pairs={{8,0},{16,8},{24,16},{28,24},{20,28},{12,20},{4,12},{0,4},{9,1},{1... | collective-permute-start | bytes 393224 | tf_op jit(solution)/shard_map/ppermute | solution.py:40
  13.5 4.4 %collective-permute-start.6 = (f32[31,512]{1,0:T(8,128)S(1)}, f32[31,512]{1,0:T(8,128)S(1)}, u32[]{:S(2)}, u32[]{:S(2)}) collective-permute-start(f32[31,512]{1,0:T(8,128)S(1)} %copy-done.1), channel_id=1, source_target_pairs={{0,2},{1,3},{2,0},{3,1},{4,6},{5,7},{6,4},{7,5},{8,10},{9,11},{10,... | collective-permute-start | bytes 190472 | tf_op jit(solution)/shard_map/ppermute | solution.py:29
  18.1 1.6 %collective-permute-start.7 = (bf16[128,1024]{1,0:T(8,128)(2,1)S(1)}, bf16[128,1024]{1,0:T(8,128)(2,1)S(1)}, u32[]{:S(2)}, u32[]{:S(2)}) collective-permute-start(bf16[128,1024]{1,0:T(8,128)(2,1)S(1)} %get-tuple-element.46), channel_id=1, source_target_pairs={{0,1},{1,0},{2,3},{3,2},{4,5},{5,4},{6,7},{7,6},{8,9},{9,8},{10,11... | collective-permute-start | bytes 786440 | tf_op jit(solution)/shard_map/ppermute | solution.py:29
  19.8 10.5 %collective-permute-start.11 = (bf16[128,1024]{1,0:T(8,128)(2,1)S(1)}, bf16[128,1024]{1,0:T(8,128)(2,1)S(1)}, u32[]{:S(2)}, u32[]{:S(2)}) collective-permute-start(bf16[128,1024]{1,0:T(8,128)(2,1)S(1)} %get-tuple-element.54.chip), channel_id=1, source_target_pairs={{0,2},{1,3},{2,0},{3,1},{4,6},{5,7},{6,4},{7,5},{8,10},{9,11},{10,... | collective-permute-start | bytes 786440 | tf_op jit(solution)/shard_map/ppermute | solution.py:29
  21.3 5.8 %collective-permute-start.8 = (bf16[48,1024]{1,0:T(8,128)(2,1)S(1)}, bf16[48,1024]{1,0:T(8,128)(2,1)S(1)}, u32[]{:S(2)}, u32[]{:S(2)}) collective-permute-start(bf16[48,1024]{1,0:T(8,128)(2,1)S(1)} %get-tuple-element.50), channel_id=1, source_target_pairs={{0,4},{4,0},{8,12},{12,8},{16,20},{20,16},{24,28},{28,24},{1,5},{5... | collective-permute-start | bytes 294920 | tf_op jit(solution)/shard_map/ppermute | solution.py:29
  22.7 5.6 %collective-permute-start.9 = (bf16[48,1024]{1,0:T(8,128)(2,1)S(1)}, bf16[48,1024]{1,0:T(8,128)(2,1)S(1)}, u32[]{:S(2)}, u32[]{:S(2)}) collective-permute-start(bf16[48,1024]{1,0:T(8,128)(2,1)S(1)} %get-tuple-element.51), channel_id=1, source_target_pairs={{0,1},{1,0},{2,3},{3,2},{4,8},{5,9},{6,10},{7,11},{8,4},{9,5},{10,... | collective-permute-start | bytes 294920 | tf_op jit(solution)/shard_map/ppermute | solution.py:51
  23.2 7.2 %collective-permute-start.12 = (bf16[128,512]{1,0:T(8,128)(2,1)S(1)}, bf16[128,512]{1,0:T(8,128)(2,1)S(1)}, u32[]{:S(2)}, u32[]{:S(2)}) collective-permute-start(bf16[128,512]{1,0:T(8,128)(2,1)S(1)} %get-tuple-element.49.q.refs_0_), channel_id=1, source_target_pairs={{0,8},{8,16},{16,24},{24,28},{28,20},{20,12},{12,4},{4,0},{1,9},{9... | collective-permute-start | bytes 393224 | tf_op jit(solution)/shard_map/ppermute | solution.py:40
  24.9 8.3 %collective-permute-start.13 = (bf16[128,512]{1,0:T(8,128)(2,1)S(1)}, bf16[128,512]{1,0:T(8,128)(2,1)S(1)}, u32[]{:S(2)}, u32[]{:S(2)}) collective-permute-start(bf16[128,512]{1,0:T(8,128)(2,1)S(1)} %get-tuple-element.49.q.refs_0_), channel_id=1, source_target_pairs={{0,1},{1,0},{2,3},{3,2},{4,5},{5,4},{6,7},{7,6},{8,12},{9,13},{10,... | collective-permute-start | bytes 393224 | tf_op jit(solution)/shard_map/ppermute | solution.py:51
  28.3 5.0 %collective-permute-start.10 = (bf16[64,1024]{1,0:T(8,128)(2,1)S(1)}, bf16[64,1024]{1,0:T(8,128)(2,1)S(1)}, u32[]{:S(2)}, u32[]{:S(2)}) collective-permute-start(bf16[64,1024]{1,0:T(8,128)(2,1)S(1)} %get-tuple-element.53.ends), channel_id=1, source_target_pairs={{0,2},{1,3},{2,0},{3,1},{4,6},{5,7},{6,4},{7,5},{8,10},{9,11},{10,... | collective-permute-start | bytes 393224 | tf_op jit(solution)/shard_map/ppermute | solution.py:29
  29.0 5.5 %collective-permute-start.14 = (bf16[128,512]{1,0:T(8,128)(2,1)S(1)}, bf16[128,512]{1,0:T(8,128)(2,1)S(1)}, u32[]{:S(2)}, u32[]{:S(2)}) collective-permute-start(bf16[128,512]{1,0:T(8,128)(2,1)S(1)} %get-tuple-element.60), channel_id=1, source_target_pairs={{0,4},{4,0},{8,12},{12,8},{16,20},{20,16},{24,28},{28,24},{1,5},{5... | collective-permute-start | bytes 393224 | tf_op jit(solution)/shard_map/ppermute | solution.py:29
  34.5 1.6 %collective-permute-start.15 = (bf16[128,1024]{1,0:T(8,128)(2,1)S(1)}, bf16[128,1024]{1,0:T(8,128)(2,1)S(1)}, u32[]{:S(2)}, u32[]{:S(2)}) collective-permute-start(bf16[128,1024]{1,0:T(8,128)(2,1)S(1)} %hand.1.own.grad_here), channel_id=1, source_target_pairs={{0,1},{1,0},{2,3},{3,2},{4,5},{5,4},{6,7},{7,6},{8,9},{9,8},{10,11... | collective-permute-start | bytes 786440 | tf_op jit(solution)/shard_map/ppermute | solution.py:29
  36.8 6.7 %collective-permute-start.17 = (bf16[144,512]{1,0:T(8,128)(2,1)S(1)}, bf16[144,512]{1,0:T(8,128)(2,1)S(1)}, u32[]{:S(2)}, u32[]{:S(2)}) collective-permute-start(bf16[144,512]{1,0:T(8,128)(2,1)S(1)} %get-tuple-element.64.message.refs_5_), channel_id=1, source_target_pairs={{0,8},{8,16},{16,24},{24,28},{28,20},{20,12},{12,4},{4,0},{1,9},{9... | collective-permute-start | bytes 442376 | tf_op jit(solution)/shard_map/ppermute | solution.py:40
  40.1 6.7 %collective-permute-start.18 = (bf16[144,512]{1,0:T(8,128)(2,1)S(1)}, bf16[144,512]{1,0:T(8,128)(2,1)S(1)}, u32[]{:S(2)}, u32[]{:S(2)}) collective-permute-start(bf16[144,512]{1,0:T(8,128)(2,1)S(1)} %get-tuple-element.64.message.refs_5_), channel_id=1, source_target_pairs={{8,0},{16,8},{24,16},{28,24},{20,28},{12,20},{4,12},{0,4},{9,1},{1... | collective-permute-start | bytes 442376 | tf_op jit(solution)/shard_map/ppermute | solution.py:40
  40.1 8.8 %collective-permute-start.19 = (bf16[144,512]{1,0:T(8,128)(2,1)S(1)}, bf16[144,512]{1,0:T(8,128)(2,1)S(1)}, u32[]{:S(2)}, u32[]{:S(2)}) collective-permute-start(bf16[144,512]{1,0:T(8,128)(2,1)S(1)} %get-tuple-element.64.message.refs_5_), channel_id=1, source_target_pairs={{0,1},{1,0},{2,3},{3,2},{4,5},{5,4},{6,7},{7,6},{8,12},{9,13},{10,... | collective-permute-start | bytes 442376 | tf_op jit(solution)/shard_map/ppermute | solution.py:51
  40.6 9.1 %collective-permute-start.16 = (bf16[144,512]{1,0:T(8,128)(2,1)S(1)}, bf16[144,512]{1,0:T(8,128)(2,1)S(1)}, u32[]{:S(2)}, u32[]{:S(2)}) collective-permute-start(bf16[144,512]{1,0:T(8,128)(2,1)S(1)} %get-tuple-element.64.message.refs_5_), channel_id=1, source_target_pairs={{0,1},{1,0},{2,3},{3,2},{4,8},{5,9},{6,10},{7,11},{8,4},{9,5},{10,... | collective-permute-start | bytes 442376 | tf_op jit(solution)/shard_map/ppermute | solution.py:51
